TPU v7x, 128 devices: a whole 4x4x4 slice. The times are simulated.
128 devices in a mesh: rep: 4 (over x_hi, core), grid: 32 (over x_lo, z, y).
Axes of the slice: x: 4 (x_hi: 2, x_lo: 2; x = x_hi * 2 + x_lo), y: 4, z: 4, core: 2. Of those that a mesh axis runs over, the one named last changes fastest.
Arguments:
- panel_left: float32 [2048, 16384], P('grid', 'rep'), may hold values from -6 to 6
- panel_right: float32 [16384, 8192], P('rep', 'grid'), may hold values from -0.046875 to 0.046875
Outputs:
- product: float32 [2048, 8192], P('rep', 'grid')
All inputs are finite; a program needn't handle non-finite values.
Results may differ from a plain program's by a relative error of at most 0.0001.
Values sent between devices are 32-bit elements; how exact they have to be, the bound alone decides.
No kernel may reach another device: no remote copies, remote signals or barrier semaphores. Data moves between devices by JAX's collectives and lax.ppermute only.
A program may use at most 128 MiB of HBM per device.

v0:
```python
import jax
import jax.numpy as jnp
from jax import lax
from jax.sharding import PartitionSpec as P


def per_device(panel_left, panel_right):
    partial_value = jnp.dot(
        lax.all_gather(panel_left, "grid", axis=0, tiled=True),
        panel_right,
        precision=lax.Precision.HIGHEST,
        preferred_element_type=jnp.float32,
    )
    return lax.psum_scatter(partial_value, "rep", scatter_dimension=0, tiled=True)


def solution(mesh):
    return jax.shard_map(
        per_device,
        mesh=mesh,
        in_specs=(P("grid", "rep"), P("rep", "grid")),
        out_specs=P("rep", "grid"),
        check_vma=False,
    )
```

profile of v0, /device:TPU:0, one launch (start us, length us, event | category | flops | bytes accessed | tf_op | source)
XLA Modules:
  0.0 449.6 jit_solution(4483976155065748928)
XLA Ops:
  6.5 0.0 all-gather.2.cloned.1.call-start
  6.5 0.7 all-gather.2.cloned.1.call-update
  7.3 0.0 reduce-scatter.2.cloned.1.call-start
  7.3 369.1 %all-gather.2.cloned.1.call-done = f32[2048,4096]{1,0:T(8,128)} async-done(((f32[64,4096]{1,0:T(8,128)}), f32[2048,4096]{1,0:T(8,128)}) %all-gather.2.cloned.1.call-update) | async-done | bytes 33554448 | tf_op jit(solution)/shard_map/all_gather | solution.py:9
  376.4 31.4 %fusion = f32[2048,256]{1,0:T(8,128)} fusion(f32[2048,4096]{1,0:T(8,128)} %all-gather.2.cloned.1.call-done, f32[4096,256]{1,0:T(8,128)} %param.3), kind=kOutput, calls=%fused_computation | convolution fusion | flops 25769803776 | bytes 39845888 | tf_op jit(solution)/shard_map/dot_general | solution.py:8
  407.9 0.0 reduce-scatter.2.cloned.1.call-update
  407.9 34.9 %reduce-scatter.2.cloned.1.call-done = f32[512,256]{1,0:T(8,128)} async-done(((f32[2048,256]{1,0:T(8,128)}), f32[512,256]{1,0:T(8,128)}) %reduce-scatter.2.cloned.1.call-update) | async-done | bytes 524304 | tf_op jit(solution)/shard_map/reduce_scatter | solution.py:14
Async XLA Ops:
  6.5 369.9 %all-gather.2.cloned.1.call-start = ((), (), s32[]{:S(2)}) async-start(), calls=%async_computation.1 | async-start | bytes 34603008 | tf_op jit(solution)/shard_map/all_gather | solution.py:9
  7.3 435.5 %reduce-scatter.2.cloned.1.call-start = ((), (), s32[]{:S(2)}) async-start(), calls=%async_computation.2 | async-start | bytes 2621440 | tf_op jit(solution)/shard_map/reduce_scatter | solution.py:14
Sparse Core Ops, SparseCore 0:
  9.0 367.3 all-gather.1
  408.0 34.6 reduce-scatter.1
where the time goes:
time: 450 us
  waiting for transfers between devices  405 us (90%)
  matrix products  31.4 us (7%)
  between operations  13.4 us (3%)
    all_gather x1, waiting for transfers between devices, per_device(): lax.all_gather(panel_left, 'grid', axis=0, tiled=True)  369 us
    reduce_scatter x1, waiting for transfers between devices, per_device(): lax.psum_scatter(partial_value, 'rep', scatter_dimension=0, tiled=True)  34.9 us
    dot_general x1, matrix products, per_device(): jnp.dot(lax.all_gather(panel_left, 'grid', axis=0, tiled=True), panel_rig...  31.4 us
  transfers between devices with their start and end apart: 2, of which 2 were waited for; matrix products, arithmetic and copies ran while one was open for 0% of the time, Pallas kernels for 0%

commit v1 on v0

v1 whole, which is shorter than its diff:
```python
import jax
import jax.numpy as jnp
from jax import lax
from jax.sharding import PartitionSpec as P

AXES = ("rep", "grid")


def moved(dx=0, dz=0, dy=0, dhi=0, core=0, chosen=lambda rep, grid: True):
    pairs = []
    for rep in range(4):
        for grid in range(32):
            if chosen(rep, grid):
                pairs.append((rep * 32 + grid, (rep ^ (2 * dhi) ^ core) * 32 + (grid ^ (16 * dx) ^ (4 * dz) ^ dy)))
    return pairs


def owns(side):
    return lambda rep, grid: ((rep & 1) ^ ((grid >> 3) & 1)) == side


def send(value, **where):
    return lax.ppermute(value, AXES, moved(**where))


NEAR = (dict(), dict(dy=1), dict(dy=3), dict(dx=1))


def flip_if(bit, value, axis):
    return jnp.where(bit == 1, jnp.flip(value, axis), value)


def reordered(value, dx=0, dy=0):
    split = value.reshape(2, 2, 2, -1, value.shape[1])
    axes = [axis for axis, bit in enumerate((dx, dy >> 1, dy & 1)) if bit]
    return jnp.flip(split, axes).reshape(value.shape) if axes else value


def per_device(left, right):
    rows, depth = left.shape
    columns = right.shape[1]
    part = depth // 4
    rep, grid = lax.axis_index("rep"), lax.axis_index("grid")
    core, x_hi = rep & 1, rep >> 1
    x_lo, z, y = grid >> 4, (grid >> 2) & 3, grid & 3
    quarter = 2 * (x_lo ^ (y >> 1)) + (x_lo ^ (y >> 1) ^ (y & 1))

    left_of = [lax.dynamic_slice_in_dim(left, (quarter ^ d) * part, part, 1) for d in range(4)]
    right_of = [lax.dynamic_slice_in_dim(right, (quarter ^ d) * part, part, 0) for d in range(4)]

    blocks = {(0, 0): left_of[0]}
    for dx, dy in ((0, 1), (0, 3), (1, 0), (1, 1), (1, 3), (0, 2), (1, 2)):
        flips = (dy & 1) ^ (dy >> 1), dy >> 1
        d = (3 * dx) ^ (2 * flips[1] + flips[0])
        blocks[dx, dy] = send(left_of[d], dx=dx, dy=dy)
    groups = [
        [(0, 0)],
        [(0, 1), (0, 3), (1, 0)],
        [(1, 1), (1, 3), (0, 2), (1, 2)],
    ]
    panel = jnp.concatenate([right_of[0]] + [send(right_of[d], **NEAR[d]) for d in range(1, 4)], axis=1)

    by_dz = {dz: {} for dz in range(4)}
    for group in groups:
        own = jnp.concatenate([blocks[name] for name in group], axis=0) if len(group) > 1 else blocks[group[0]]
        half = own.shape[0] // 2
        one, three = send(own, dz=1), send(own, dz=3)
        two = jnp.concatenate([send(one[:half], dz=3), send(three[half:], dz=1)], axis=0)
        for dz, value in enumerate((own, one, two, three)):
            for at, name in enumerate(group):
                by_dz[dz][name] = value[at * rows:(at + 1) * rows]

    finals = {}
    order = [(dx, dy) for dx in range(2) for dy in range(4)]
    for dz in (0, 1, 3, 2):
        side = dz >> 1
        stack = jnp.concatenate([by_dz[dz][name] for name in order], axis=0)
        partial = jnp.dot(stack, panel, precision=lax.Precision.HIGH, preferred_element_type=jnp.float32)
        partial = partial.reshape(stack.shape[0], 4, columns).transpose(1, 0, 2)
        other = send(partial, core=1, chosen=owns(1 - side))
        both = [reordered(partial[d] + other[d], **NEAR[d]) for d in range(4)]
        total = both[0]
        for d in range(1, 4):
            total = total + send(both[d], chosen=owns(side), **NEAR[d])
        total = total.reshape(2, stack.shape[0] // 2, columns)
        keep = x_hi ^ x_lo
        mine = lax.dynamic_index_in_dim(total, keep, 0, False)
        theirs = lax.dynamic_index_in_dim(total, 1 - keep, 0, False)
        finals[dz] = mine + send(theirs, dhi=1, chosen=owns(side))

    early = core == (z >> 1)
    first = jnp.where(early, finals[0], finals[2])
    second = jnp.where(early, finals[1], finals[3])
    out = jnp.stack([first, second]).reshape(2, 2, 2, rows, columns)
    out = flip_if(z & 1, out, 0)
    out = flip_if(y >> 1, out, 1)
    out = flip_if(y & 1, out, 2)
    return out.reshape(8 * rows, columns)


def solution(mesh):
    return jax.shard_map(
        per_device,
        mesh=mesh,
        in_specs=(P("grid", "rep"), P("rep", "grid")),
        out_specs=P("rep", "grid"),
        check_vma=False,
    )
```

time: 450 us -> 254 us (0.56)
  waiting for transfers between devices: 405 us -> 25.8 us
  starting transfers between devices: 0.04 us -> 85.4 us
  local copies, waits for them, and re-layouts: 0 us -> 72.7 us
  other arithmetic: 0 us -> 48.8 us
  between operations: 13.4 us -> 0.69 us
  matrix products: 31.4 us -> 18.9 us
    all_gather x1 -> x0, waiting for transfers between devices: 369 us -> none  [per_device(): lax.all_gather(panel_left, 'grid', axis=0, tiled=True)]
    ppermute x0 -> x42, starting transfers between devices: none -> 85.4 us  [send(): return lax.ppermute(value, AXES, moved(**where))]
    add x0 -> x8, other arithmetic: none -> 44.7 us  [the longest x4 39.3 us: per_device(): both = [reordered(partial[d] + other[d], **NEAR[d]) for d in range(4)]]
    reduce_scatter x1 -> x0, waiting for transfers between devices: 34.9 us -> none  [per_device(): lax.psum_scatter(partial_value, 'rep', scatter_dimension=0, tiled=True)]
    unnamed x0 -> x88, local copies, waits for them, and re-layouts: none -> 29.5 us
    ppermute x0 -> x42, waiting for transfers between devices: none -> 25.8 us  [send(): return lax.ppermute(value, AXES, moved(**where))]
    rev x0 -> x12, local copies, waits for them, and re-layouts: none -> 19.5 us  [reordered(): return jnp.flip(split, axes).reshape(value.shape) if axes else value]
    dot_general x1 -> x4, matrix products: 31.4 us -> 18.9 us  [per_device(): jnp.dot(stack, panel, precision=lax.Precision.HIGH, preferred_element_typ...]
  transfers between devices with their start and end apart: 2 -> 42, of which waited for: 2 -> 5; matrix products, arithmetic and copies ran while one was open for 0% -> 53% of each run, Pallas kernels for 0% -> 0%
where the time goes in v1:
time: 254 us; the launch traced here: 252 us
  starting transfers between devices  85.4 us (34%)
  local copies, waits for them, and re-layouts  72.7 us (29%)
  other arithmetic  48.8 us (19%)
  waiting for transfers between devices  25.8 us (10%)
  matrix products  18.9 us (7%)
    ppermute x42, starting transfers between devices, send(): return lax.ppermute(value, AXES, moved(**where))  85.4 us
    add x4, other arithmetic, per_device(): both = [reordered(partial[d] + other[d], **NEAR[d]) for d in range(4)]  39.3 us
    unnamed x88, local copies, waits for them, and re-layouts  29.5 us
    ppermute x42, waiting for transfers between devices, send(): return lax.ppermute(value, AXES, moved(**where))  25.8 us
    rev x12, local copies, waits for them, and re-layouts, reordered(): return jnp.flip(split, axes).reshape(value.shape) if axes else value  19.5 us
    dot_general x4, matrix products, per_device(): jnp.dot(stack, panel, precision=lax.Precision.HIGH, preferred_element_typ...  18.9 us
    reshape x4, local copies, waits for them, and re-layouts, per_device(): partial = partial.reshape(stack.shape[0], 4, columns).transpose(1, 0, 2)  10.8 us
    add x4, other arithmetic, per_device(): total = total + send(both[d], chosen=owns(side), **NEAR[d])  5.41 us
  transfers between devices with their start and end apart: 42, of which 5 were waited for; matrix products, arithmetic and copies ran while one was open for 53% of the time, Pallas kernels for 0%

profile of v1, /device:TPU:0, one launch (start us, length us, event | category | flops | bytes accessed | tf_op | source)
XLA Modules:
  0.0 252.3 jit_solution(5099890933458207644)
XLA Ops:
  0.0 2.0 constant_dynamic-slice_fusion.5
  2.0 1.7 collective-permute-start
  3.7 1.5 collective-permute-start.3
  5.2 2.9 %collective-permute-start.1 = (f32[64,1024]{1,0:T(8,128)S(1)}, f32[64,1024]{1,0:T(8,128)S(1)}, u32[]{:S(2)}, u32[]{:S(2)}) collective-permute-start(f32[64,1024]{1,0:T(8,128)S(1)} %get-tuple-element.27), channel_id=1, source_target_pairs={{0,2},{1,3},{2,0},{3,1},{4,6},{5,7},{6,4},{7,5},{8,10},{9,11},{10,... | collective-permute-start | bytes 786440 | tf_op jit(solution)/shard_map/ppermute | solution.py:23
  8.1 4.0 %collective-permute-start.17 = (f32[64,1024]{1,0:T(8,128)S(1)}, f32[64,1024]{1,0:T(8,128)S(1)}, u32[]{:S(2)}, u32[]{:S(2)}) collective-permute-start(f32[64,1024]{1,0:T(8,128)S(1)} %get-tuple-element.30), channel_id=1, source_target_pairs={{0,12},{1,13},{2,14},{3,15},{4,8},{5,9},{6,10},{7,11},{8,4},{9,5},... | collective-permute-start | bytes 786440 | tf_op jit(solution)/shard_map/ppermute | solution.py:23
  12.1 2.2 collective-permute-start.2
  14.3 4.3 %constant_dynamic-slice_fusion.3 = (f32[1024,256]{1,0:T(8,128)}, f32[1024,256]{1,0:T(8,128)}, f32[1024,256]{1,0:T(8,128)}, f32[1024,256]{1,0:T(8,128)}) fusion(f32[4096,256]{1,0:T(8,128)} %param.3, s32[]{:T(128)S(6)} %select_n.65, s32[]{:T(128)S(6)} %select_n.66, s32[]{:T(128)S(6)} %select_n.67, s32[]{:T(128)S(6)} %select_n.68), kind=kLoop, calls=%fused_computation.85 | loop fusion | bytes 8388624 | tf_op jit(solution)/shard_map/dynamic_slice | solution.py:49
  20.9 5.0 %collective-permute-start.5 = (f32[64,1024]{1,0:T(8,128)S(1)}, f32[64,1024]{1,0:T(8,128)S(1)}, u32[]{:S(2)}, u32[]{:S(2)}) collective-permute-start(f32[64,1024]{1,0:T(8,128)S(1)} %get-tuple-element.30), channel_id=1, source_target_pairs={{0,18},{1,19},{2,16},{3,17},{4,22},{5,23},{6,20},{7,21},{8,26},{9,... | collective-permute-start | bytes 786440 | tf_op jit(solution)/shard_map/ppermute | solution.py:23
  26.7 2.0 collective-permute-start.18
  28.7 2.8 %collective-permute-start.16 = (f32[32,1024]{1,0:T(8,128)S(1)}, f32[32,1024]{1,0:T(8,128)S(1)}, u32[]{:S(2)}, u32[]{:S(2)}) collective-permute-start(f32[32,1024]{1,0:T(8,128)S(1)} %slice.240), channel_id=1, source_target_pairs={{0,12},{1,13},{2,14},{3,15},{4,8},{5,9},{6,10},{7,11},{8,4},{9,5},... | collective-permute-start | bytes 393224 | tf_op jit(solution)/shard_map/ppermute | solution.py:23
  33.0 1.6 collective-permute-start.7
  34.7 1.4 collective-permute-start.9
  36.0 2.4 collective-permute-done.5
  39.5 6.6 %collective-permute-start.23 = (f32[192,1024]{1,0:T(8,128)S(1)}, f32[192,1024]{1,0:T(8,128)S(1)}, u32[]{:S(2)}, u32[]{:S(2)}) collective-permute-start(f32[192,1024]{1,0:T(8,128)S(1)} %get-tuple-element.37), channel_id=1, source_target_pairs={{0,12},{1,13},{2,14},{3,15},{4,8},{5,9},{6,10},{7,11},{8,4},{9,5},... | collective-permute-start | bytes 2359304 | tf_op jit(solution)/shard_map/ppermute | solution.py:23
  51.4 8.4 %collective-permute-done.23 = f32[192,1024]{1,0:T(8,128)S(1)} collective-permute-done((f32[192,1024]{1,0:T(8,128)S(1)}, f32[192,1024]{1,0:T(8,128)S(1)}, u32[]{:S(2)}, u32[]{:S(2)}) %collective-permute-start.23) | collective-permute-done | bytes 786464 | tf_op jit(solution)/shard_map/ppermute | solution.py:23
  59.8 4.7 %collective-permute-done.19 = f32[192,1024]{1,0:T(8,128)S(1)} collective-permute-done((f32[192,1024]{1,0:T(8,128)S(1)}, f32[192,1024]{1,0:T(8,128)S(1)}, u32[]{:S(2)}, u32[]{:S(2)}) %collective-permute-start.19) | collective-permute-done | bytes 786464 | tf_op jit(solution)/shard_map/ppermute | solution.py:23
  67.9 2.7 %collective-permute-start.20 = (f32[96,1024]{1,0:T(8,128)}, f32[96,1024]{1,0:T(8,128)}, u32[]{:S(2)}, u32[]{:S(2)}) collective-permute-start(f32[96,1024]{1,0:T(8,128)} %slice.242), channel_id=1, source_target_pairs={{0,12},{1,13},{2,14},{3,15},{4,8},{5,9},{6,10},{7,11},{8,4},{9,5},... | collective-permute-start | bytes 1179656 | tf_op jit(solution)/shard_map/ppermute | solution.py:23
  71.6 5.1 %fusion.14 = f32[512,1024]{1,0:T(8,128)} fusion(f32[512,1024]{1,0:T(8,128)S(1)} %copy-done.14, f32[1024,256]{1,0:T(8,128)S(1)} %collective-permute-done.9, f32[1024,256]{1,0:T(8,128)S(1)} %collective-permute-done.8, f32[1024,256]{1,0:T(8,128)S(1)} %collective-permute-done.7, f32[1024,256]{1,0:T(8,128)S(1)} %copy-done.8), kind=kOutput, calls=%fused_computation.93 | convolution fusion | flops 3224371200 | bytes 8388608 | tf_op jit(solution)/shard_map/dot_general | solution.py:78
  76.7 3.3 %reshape.120 = f32[512,4,256]{2,1,0:T(4,128)} reshape(f32[512,1024]{1,0:T(8,128)} %fusion.14) | data formatting | bytes 4194304 | tf_op jit(solution)/shard_map/reshape | solution.py:79
  80.0 1.4 collective-permute-start.10
  81.4 1.7 slice_dynamic-update-slice_fusion.11
  83.8 1.6 collective-permute-done.25
  90.8 3.7 %fusion.12 = f32[512,1024]{1,0:T(8,128)S(1)} fusion(f32[512,1024]{1,0:T(8,128)S(1)} %slice_dynamic-update-slice_fusion.7, f32[1024,256]{1,0:T(8,128)S(1)} %copy-done.20, f32[1024,256]{1,0:T(8,128)S(1)} %copy-done.23, f32[1024,256]{1,0:T(8,128)S(1)} %copy-done.17, f32[1024,256]{1,0:T(8,128)S(1)} %copy-done.9), kind=kOutput, calls=%fused_computation.91 | convolution fusion | flops 3224371200 | bytes 8388608 | tf_op jit(solution)/shard_map/dot_general | solution.py:78
  94.5 5.1 %fusion.11 = f32[512,1024]{1,0:T(8,128)} fusion(f32[512,1024]{1,0:T(8,128)S(1)} %slice_dynamic-update-slice_fusion.2, f32[1024,256]{1,0:T(8,128)S(1)} %copy-done.20, f32[1024,256]{1,0:T(8,128)S(1)} %copy-done.23, f32[1024,256]{1,0:T(8,128)S(1)} %copy-done.17, f32[1024,256]{1,0:T(8,128)S(1)} %copy-done.9), kind=kOutput, calls=%fused_computation.90 | convolution fusion | flops 3224371200 | bytes 8388608 | tf_op jit(solution)/shard_map/dot_general | solution.py:78
  99.5 2.0 reshape.130
  101.5 3.4 %reshape.135 = f32[512,4,256]{2,1,0:T(4,128)} reshape(f32[512,1024]{1,0:T(8,128)} %fusion.11) | data formatting | bytes 4194304 | tf_op jit(solution)/shard_map/reshape | solution.py:79
  104.9 3.9 %collective-permute-start.37 = (f32[4,512,256]{2,0,1:T(4,128)}, f32[4,512,256]{2,0,1:T(4,128)}, u32[]{:S(2)}, u32[]{:S(2)}) collective-permute-start(f32[4,512,256]{2,0,1:T(4,128)} %bitcast.22), channel_id=1, source_target_pairs={{0,32},{1,33},{2,34},{3,35},{4,36},{5,37},{6,38},{7,39},{16,48},{1... | collective-permute-start | bytes 6291464 | tf_op jit(solution)/shard_map/ppermute | solution.py:23
  109.8 1.3 collective-permute-start.32
  116.1 5.1 %fusion.13 = f32[512,1024]{1,0:T(8,128)} fusion(f32[512,1024]{1,0:T(8,128)S(1)} %slice_dynamic-update-slice_fusion.12, f32[1024,256]{1,0:T(8,128)S(1)} %copy-done.21, f32[1024,256]{1,0:T(8,128)S(1)} %copy-done.24, f32[1024,256]{1,0:T(8,128)S(1)} %copy-done.18, f32[1024,256]{1,0:T(8,128)S(1)} %copy-done.10), kind=kOutput, calls=%fused_computation.92 | convolution fusion | flops 3224371200 | bytes 8388608 | tf_op jit(solution)/shard_map/dot_general | solution.py:78
  121.1 2.2 reshape.125
  123.3 5.7 %collective-permute-start.27 = (f32[4,512,256]{2,0,1:T(4,128)S(1)}, f32[4,512,256]{2,0,1:T(4,128)}, u32[]{:S(2)}, u32[]{:S(2)}) collective-permute-start(f32[4,512,256]{2,0,1:T(4,128)S(1)} %bitcast.87), channel_id=1, source_target_pairs={{0,32},{1,33},{2,34},{3,35},{4,36},{5,37},{6,38},{7,39},{16,48},{1... | collective-permute-start | bytes 6291464 | tf_op jit(solution)/shard_map/ppermute | solution.py:23
  129.0 10.4 %slice_add_fusion.15 = (f32[1,512,256]{2,0,1:T(1,128)S(1)}, f32[1,512,256]{2,0,1:T(1,128)S(1)}, f32[1,512,256]{2,0,1:T(1,128)}, f32[1,512,256]{2,0,1:T(1,128)S(1)}) fusion(f32[4,512,256]{2,0,1:T(4,128)} %collective-permute-done.10, f32[4,512,256]{2,0,1:T(4,128)} %bitcast), kind=kLoop, calls=%fused_computation.21 | loop fusion | flops 524288 | bytes 6291456 | tf_op jit(solution)/shard_map/add | solution.py:81
  140.3 1.9 rev.53
  142.2 1.9 copy.5
  144.1 1.9 rev.52
  146.8 1.9 rev.51
  148.7 2.1 collective-permute-start.11
  150.8 5.2 %collective-permute-start.12 = (f32[512,256]{1,0:T(8,128)}, f32[512,256]{1,0:T(8,128)}, u32[]{:S(2)}, u32[]{:S(2)}) collective-permute-start(f32[512,256]{1,0:T(8,128)} %bitcast.116), channel_id=1, source_target_pairs={{0,3},{1,2},{2,1},{3,0},{4,7},{5,6},{6,5},{7,4},{16,19},{17,18},{1... | collective-permute-start | bytes 1572872 | tf_op jit(solution)/shard_map/ppermute | solution.py:23
  156.0 3.4 %collective-permute-start.13 = (f32[512,256]{1,0:T(8,128)}, f32[512,256]{1,0:T(8,128)}, u32[]{:S(2)}, u32[]{:S(2)}) collective-permute-start(f32[512,256]{1,0:T(8,128)} %bitcast.111), channel_id=1, source_target_pairs={{0,16},{1,17},{2,18},{3,19},{4,20},{5,21},{6,22},{7,23},{16,0},{17... | collective-permute-start | bytes 1572872 | tf_op jit(solution)/shard_map/ppermute | solution.py:23
  159.4 10.9 %slice_add_fusion.3 = (f32[1,512,256]{2,0,1:T(1,128)}, f32[1,512,256]{2,0,1:T(1,128)S(1)}, f32[1,512,256]{2,0,1:T(1,128)}, f32[1,512,256]{2,0,1:T(1,128)S(1)}) fusion(f32[4,512,256]{2,0,1:T(4,128)} %collective-permute-done.37, f32[4,512,256]{2,0,1:T(4,128)} %bitcast.22), kind=kLoop, calls=%fused_computation.7 | loop fusion | flops 524288 | bytes 6291456 | tf_op jit(solution)/shard_map/add | solution.py:81
  171.1 1.9 rev.62
  173.1 1.9 copy.17
  174.9 1.9 rev.61
  177.6 1.9 rev.60
  179.5 1.5 collective-permute-start.38
  181.0 1.4 collective-permute-start.39
  182.4 1.5 collective-permute-start.40
  183.9 10.6 %slice_add_fusion.7 = (f32[1,512,256]{2,0,1:T(1,128)S(1)}, f32[1,512,256]{2,0,1:T(1,128)S(1)}, f32[1,512,256]{2,0,1:T(1,128)}, f32[1,512,256]{2,0,1:T(1,128)}) fusion(f32[4,512,256]{2,0,1:T(4,128)} %collective-permute-done.32, f32[4,512,256]{2,0,1:T(4,128)} %bitcast.15), kind=kLoop, calls=%fused_computation.12 | loop fusion | flops 524288 | bytes 6291456 | tf_op jit(solution)/shard_map/add | solution.py:81
  195.4 1.9 rev.59
  197.3 1.9 copy.13
  199.1 1.9 rev.58
  201.0 1.9 copy.12
  202.8 1.9 rev.57
  204.7 2.2 collective-permute-start.33
  206.9 1.5 fusion.7
  208.4 3.0 %collective-permute-start.34 = (f32[512,256]{1,0:T(8,128)}, f32[512,256]{1,0:T(8,128)}, u32[]{:S(2)}, u32[]{:S(2)}) collective-permute-start(f32[512,256]{1,0:T(8,128)} %bitcast.17), channel_id=1, source_target_pairs={{0,3},{1,2},{2,1},{3,0},{4,7},{5,6},{6,5},{7,4},{16,19},{17,18},{1... | collective-permute-start | bytes 1572872 | tf_op jit(solution)/shard_map/ppermute | solution.py:23
  211.4 2.4 collective-permute-start.35
  213.9 2.3 fusion.1
  216.2 7.4 %slice_add_fusion.11 = (f32[1,512,256]{2,0,1:T(1,128)S(1)}, f32[1,512,256]{2,0,1:T(1,128)S(1)}, f32[1,512,256]{2,0,1:T(1,128)}, f32[1,512,256]{2,0,1:T(1,128)}) fusion(f32[4,512,256]{2,0,1:T(4,128)} %collective-permute-done.27, f32[4,512,256]{2,0,1:T(4,128)S(1)} %bitcast.88), kind=kLoop, calls=%fused_computation.17 | loop fusion | flops 524288 | bytes 6291456 | tf_op jit(solution)/shard_map/add | solution.py:81
  229.3 4.9 %collective-permute-start.14 = (f32[256,256]{1,0:T(8,128)S(1)}, f32[256,256]{1,0:T(8,128)}, u32[]{:S(2)}, u32[]{:S(2)}) collective-permute-start(f32[256,256]{1,0:T(8,128)S(1)} %dynamic-slice_bitcast_fusion.3), channel_id=1, source_target_pairs={{0,64},{1,65},{2,66},{3,67},{4,68},{5,69},{6,70},{7,71},{16,80},{1... | collective-permute-start | bytes 786440 | tf_op jit(solution)/shard_map/ppermute | solution.py:23
  234.3 1.4 collective-permute-start.41
  235.6 1.5 fusion.3
  237.2 2.4 collective-permute-start.36
  240.5 8.6 %collective-permute-done.36 = f32[256,256]{1,0:T(8,128)} collective-permute-done((f32[256,256]{1,0:T(8,128)S(1)}, f32[256,256]{1,0:T(8,128)}, u32[]{:S(2)}, u32[]{:S(2)}) %collective-permute-start.36) | collective-permute-done | bytes 262176 | tf_op jit(solution)/shard_map/ppermute | solution.py:23
  (160 shorter events, 41.1 us)
Async XLA Ops:
  2.0 10.1 %collective-permute-start = (f32[64,1024]{1,0:T(8,128)S(1)}, f32[64,1024]{1,0:T(8,128)S(1)}, u32[]{:S(2)}, u32[]{:S(2)}) collective-permute-start(f32[64,1024]{1,0:T(8,128)S(1)} %get-tuple-element.28), channel_id=1, source_target_pairs={{0,1},{1,0},{2,3},{3,2},{4,5},{5,4},{6,7},{7,6},{8,9},{9,8},{10,11... | collective-permute-start | bytes 786440 | tf_op jit(solution)/shard_map/ppermute | solution.py:23
  3.7 23.0 %collective-permute-start.3 = (f32[64,1024]{1,0:T(8,128)S(1)}, f32[64,1024]{1,0:T(8,128)S(1)}, u32[]{:S(2)}, u32[]{:S(2)}) collective-permute-start(f32[64,1024]{1,0:T(8,128)S(1)} %get-tuple-element.27), channel_id=1, source_target_pairs={{0,16},{1,17},{2,18},{3,19},{4,20},{5,21},{6,22},{7,23},{8,24},{9,... | collective-permute-start | bytes 786440 | tf_op jit(solution)/shard_map/ppermute | solution.py:23
  5.2 14.2 %collective-permute-start.1 = (f32[64,1024]{1,0:T(8,128)S(1)}, f32[64,1024]{1,0:T(8,128)S(1)}, u32[]{:S(2)}, u32[]{:S(2)}) collective-permute-start(f32[64,1024]{1,0:T(8,128)S(1)} %get-tuple-element.27), channel_id=1, source_target_pairs={{0,2},{1,3},{2,0},{3,1},{4,6},{5,7},{6,4},{7,5},{8,10},{9,11},{10,... | collective-permute-start | bytes 786440 | tf_op jit(solution)/shard_map/ppermute | solution.py:23
  8.1 12.4 %collective-permute-start.17 = (f32[64,1024]{1,0:T(8,128)S(1)}, f32[64,1024]{1,0:T(8,128)S(1)}, u32[]{:S(2)}, u32[]{:S(2)}) collective-permute-start(f32[64,1024]{1,0:T(8,128)S(1)} %get-tuple-element.30), channel_id=1, source_target_pairs={{0,12},{1,13},{2,14},{3,15},{4,8},{5,9},{6,10},{7,11},{8,4},{9,5},... | collective-permute-start | bytes 786440 | tf_op jit(solution)/shard_map/ppermute | solution.py:23
  12.1 8.7 %collective-permute-start.15 = (f32[64,1024]{1,0:T(8,128)S(1)}, f32[64,1024]{1,0:T(8,128)S(1)}, u32[]{:S(2)}, u32[]{:S(2)}) collective-permute-start(f32[64,1024]{1,0:T(8,128)S(1)} %get-tuple-element.30), channel_id=1, source_target_pairs={{0,4},{1,5},{2,6},{3,7},{4,0},{5,1},{6,2},{7,3},{8,12},{9,13},{10,... | collective-permute-start | bytes 786440 | tf_op jit(solution)/shard_map/ppermute | solution.py:23
  12.1 16.5 %collective-permute-start.2 = (f32[64,1024]{1,0:T(8,128)S(1)}, f32[64,1024]{1,0:T(8,128)S(1)}, u32[]{:S(2)}, u32[]{:S(2)}) collective-permute-start(f32[64,1024]{1,0:T(8,128)S(1)} %get-tuple-element.31), channel_id=1, source_target_pairs={{0,3},{1,2},{2,1},{3,0},{4,7},{5,6},{6,5},{7,4},{8,11},{9,10},{10,... | collective-permute-start | bytes 786440 | tf_op jit(solution)/shard_map/ppermute | solution.py:23
  19.4 13.6 %collective-permute-start.6 = (f32[64,1024]{1,0:T(8,128)S(1)}, f32[64,1024]{1,0:T(8,128)S(1)}, u32[]{:S(2)}, u32[]{:S(2)}) collective-permute-start(f32[64,1024]{1,0:T(8,128)S(1)} %get-tuple-element.28), channel_id=1, source_target_pairs={{0,19},{1,18},{2,17},{3,16},{4,23},{5,22},{6,21},{7,20},{8,27},{9,... | collective-permute-start | bytes 786440 | tf_op jit(solution)/shard_map/ppermute | solution.py:23
  20.5 14.1 %collective-permute-start.4 = (f32[64,1024]{1,0:T(8,128)S(1)}, f32[64,1024]{1,0:T(8,128)S(1)}, u32[]{:S(2)}, u32[]{:S(2)}) collective-permute-start(f32[64,1024]{1,0:T(8,128)S(1)} %get-tuple-element.31), channel_id=1, source_target_pairs={{0,17},{1,16},{2,19},{3,18},{4,21},{5,20},{6,23},{7,22},{8,25},{9,... | collective-permute-start | bytes 786440 | tf_op jit(solution)/shard_map/ppermute | solution.py:23
  20.9 17.6 %collective-permute-start.5 = (f32[64,1024]{1,0:T(8,128)S(1)}, f32[64,1024]{1,0:T(8,128)S(1)}, u32[]{:S(2)}, u32[]{:S(2)}) collective-permute-start(f32[64,1024]{1,0:T(8,128)S(1)} %get-tuple-element.30), channel_id=1, source_target_pairs={{0,18},{1,19},{2,16},{3,17},{4,22},{5,23},{6,20},{7,21},{8,26},{9,... | collective-permute-start | bytes 786440 | tf_op jit(solution)/shard_map/ppermute | solution.py:23
  26.7 12.8 %collective-permute-start.18 = (f32[32,1024]{1,0:T(8,128)S(1)}, f32[32,1024]{1,0:T(8,128)S(1)}, u32[]{:S(2)}, u32[]{:S(2)}) collective-permute-start(f32[32,1024]{1,0:T(8,128)S(1)} %slice.241), channel_id=1, source_target_pairs={{0,4},{1,5},{2,6},{3,7},{4,0},{5,1},{6,2},{7,3},{8,12},{9,13},{10,... | collective-permute-start | bytes 393224 | tf_op jit(solution)/shard_map/ppermute | solution.py:23
  28.7 17.4 %collective-permute-start.16 = (f32[32,1024]{1,0:T(8,128)S(1)}, f32[32,1024]{1,0:T(8,128)S(1)}, u32[]{:S(2)}, u32[]{:S(2)}) collective-permute-start(f32[32,1024]{1,0:T(8,128)S(1)} %slice.240), channel_id=1, source_target_pairs={{0,12},{1,13},{2,14},{3,15},{4,8},{5,9},{6,10},{7,11},{8,4},{9,5},... | collective-permute-start | bytes 393224 | tf_op jit(solution)/shard_map/ppermute | solution.py:23
  33.0 34.4 %collective-permute-start.7 = (f32[1024,256]{1,0:T(8,128)}, f32[1024,256]{1,0:T(8,128)S(1)}, u32[]{:S(2)}, u32[]{:S(2)}) collective-permute-start(f32[1024,256]{1,0:T(8,128)} %get-tuple-element.24), channel_id=1, source_target_pairs={{0,1},{1,0},{2,3},{3,2},{4,5},{5,4},{6,7},{7,6},{8,9},{9,8},{10,11... | collective-permute-start | bytes 3145736 | tf_op jit(solution)/shard_map/ppermute | solution.py:23
  34.7 33.3 %collective-permute-start.9 = (f32[1024,256]{1,0:T(8,128)}, f32[1024,256]{1,0:T(8,128)S(1)}, u32[]{:S(2)}, u32[]{:S(2)}) collective-permute-start(f32[1024,256]{1,0:T(8,128)} %get-tuple-element.25), channel_id=1, source_target_pairs={{0,16},{1,17},{2,18},{3,19},{4,20},{5,21},{6,22},{7,23},{8,24},{9,... | collective-permute-start | bytes 3145736 | tf_op jit(solution)/shard_map/ppermute | solution.py:23
  38.4 32.2 %collective-permute-start.8 = (f32[1024,256]{1,0:T(8,128)}, f32[1024,256]{1,0:T(8,128)S(1)}, u32[]{:S(2)}, u32[]{:S(2)}) collective-permute-start(f32[1024,256]{1,0:T(8,128)} %get-tuple-element.26), channel_id=1, source_target_pairs={{0,3},{1,2},{2,1},{3,0},{4,7},{5,6},{6,5},{7,4},{8,11},{9,10},{10,... | collective-permute-start | bytes 3145736 | tf_op jit(solution)/shard_map/ppermute | solution.py:23
  39.5 20.3 %collective-permute-start.23 = (f32[192,1024]{1,0:T(8,128)S(1)}, f32[192,1024]{1,0:T(8,128)S(1)}, u32[]{:S(2)}, u32[]{:S(2)}) collective-permute-start(f32[192,1024]{1,0:T(8,128)S(1)} %get-tuple-element.37), channel_id=1, source_target_pairs={{0,12},{1,13},{2,14},{3,15},{4,8},{5,9},{6,10},{7,11},{8,4},{9,5},... | collective-permute-start | bytes 2359304 | tf_op jit(solution)/shard_map/ppermute | solution.py:23
  46.0 18.4 %collective-permute-start.19 = (f32[192,1024]{1,0:T(8,128)S(1)}, f32[192,1024]{1,0:T(8,128)S(1)}, u32[]{:S(2)}, u32[]{:S(2)}) collective-permute-start(f32[192,1024]{1,0:T(8,128)S(1)} %get-tuple-element.37), channel_id=1, source_target_pairs={{0,4},{1,5},{2,6},{3,7},{4,0},{5,1},{6,2},{7,3},{8,12},{9,13},{10,... | collective-permute-start | bytes 2359304 | tf_op jit(solution)/shard_map/ppermute | solution.py:23
  49.1 22.6 %copy-start.8 = (f32[1024,256]{1,0:T(8,128)S(1)}, f32[1024,256]{1,0:T(8,128)}, u32[]{:S(2)}) copy-start(f32[1024,256]{1,0:T(8,128)} %get-tuple-element.23) | copy-start | bytes 3145732
  50.0 21.7 %copy-start.14 = (f32[512,1024]{1,0:T(8,128)S(1)}, f32[512,1024]{1,0:T(8,128)}, u32[]{:S(2)}) copy-start(f32[512,1024]{1,0:T(8,128)} %get-tuple-element.32) | copy-start | bytes 6291460
  59.8 25.6 %collective-permute-start.25 = (f32[256,1024]{1,0:T(8,128)}, f32[256,1024]{1,0:T(8,128)S(1)}, u32[]{:S(2)}, u32[]{:S(2)}) collective-permute-start(f32[256,1024]{1,0:T(8,128)} %constant_dynamic-update-slice_fusion.11), channel_id=1, source_target_pairs={{0,4},{1,5},{2,6},{3,7},{4,0},{5,1},{6,2},{7,3},{8,12},{9,13},{10,... | collective-permute-start | bytes 3145736 | tf_op jit(solution)/shard_map/ppermute | solution.py:23
  64.5 2.1 copy-start.6
  64.5 22.1 %collective-permute-start.21 = (f32[256,1024]{1,0:T(8,128)}, f32[256,1024]{1,0:T(8,128)S(1)}, u32[]{:S(2)}, u32[]{:S(2)}) collective-permute-start(f32[256,1024]{1,0:T(8,128)} %constant_dynamic-update-slice_fusion.11), channel_id=1, source_target_pairs={{0,12},{1,13},{2,14},{3,15},{4,8},{5,9},{6,10},{7,11},{8,4},{9,5},... | collective-permute-start | bytes 3145736 | tf_op jit(solution)/shard_map/ppermute | solution.py:23
  67.4 3.3 %copy-start.16 = (f32[1024,256]{1,0:T(8,128)}, f32[1024,256]{1,0:T(8,128)S(1)}, u32[]{:S(2)}) copy-start(f32[1024,256]{1,0:T(8,128)S(1)} %collective-permute-done.7) | copy-start | bytes 3145732
  67.4 44.8 %collective-permute-start.24 = (f32[96,1024]{1,0:T(8,128)}, f32[96,1024]{1,0:T(8,128)S(1)}, u32[]{:S(2)}, u32[]{:S(2)}) collective-permute-start(f32[96,1024]{1,0:T(8,128)} %slice.246), channel_id=1, source_target_pairs={{0,4},{1,5},{2,6},{3,7},{4,0},{5,1},{6,2},{7,3},{8,12},{9,13},{10,... | collective-permute-start | bytes 1179656 | tf_op jit(solution)/shard_map/ppermute | solution.py:23
  67.9 2.7 %copy-start.19 = (f32[1024,256]{1,0:T(8,128)}, f32[1024,256]{1,0:T(8,128)S(1)}, u32[]{:S(2)}) copy-start(f32[1024,256]{1,0:T(8,128)S(1)} %collective-permute-done.9) | copy-start | bytes 3145732
  67.9 37.0 %collective-permute-start.20 = (f32[96,1024]{1,0:T(8,128)}, f32[96,1024]{1,0:T(8,128)}, u32[]{:S(2)}, u32[]{:S(2)}) collective-permute-start(f32[96,1024]{1,0:T(8,128)} %slice.242), channel_id=1, source_target_pairs={{0,12},{1,13},{2,14},{3,15},{4,8},{5,9},{6,10},{7,11},{8,4},{9,5},... | collective-permute-start | bytes 1179656 | tf_op jit(solution)/shard_map/ppermute | solution.py:23
  80.0 8.5 %copy-start.7 = (f32[192,1024]{1,0:T(8,128)S(1)}, f32[192,1024]{1,0:T(8,128)}, u32[]{:S(2)}) copy-start(f32[192,1024]{1,0:T(8,128)} %copy-done.6) | copy-start | bytes 2359300
  80.0 49.0 %collective-permute-start.10 = (f32[4,512,256]{2,0,1:T(4,128)}, f32[4,512,256]{2,0,1:T(4,128)}, u32[]{:S(2)}, u32[]{:S(2)}) collective-permute-start(f32[4,512,256]{2,0,1:T(4,128)} %bitcast), channel_id=1, source_target_pairs={{8,40},{9,41},{10,42},{11,43},{12,44},{13,45},{14,46},{15,47},{24,... | collective-permute-start | bytes 6291464 | tf_op jit(solution)/shard_map/ppermute | solution.py:23
  83.1 5.4 %copy-start.12 = (f32[512,1024]{1,0:T(8,128)S(1)}, f32[512,1024]{1,0:T(8,128)}, u32[]{:S(2)}) copy-start(f32[512,1024]{1,0:T(8,128)} %slice_dynamic-update-slice_fusion.11) | copy-start | bytes 6291460
  86.2 2.5 copy-start.13
  86.2 26.9 %collective-permute-start.26 = (f32[128,1024]{1,0:T(8,128)}, f32[128,1024]{1,0:T(8,128)}, u32[]{:S(2)}, u32[]{:S(2)}) collective-permute-start(f32[128,1024]{1,0:T(8,128)} %slice.248), channel_id=1, source_target_pairs={{0,12},{1,13},{2,14},{3,15},{4,8},{5,9},{6,10},{7,11},{8,4},{9,5},... | collective-permute-start | bytes 1572872 | tf_op jit(solution)/shard_map/ppermute | solution.py:23
  87.4 22.4 %collective-permute-start.22 = (f32[128,1024]{1,0:T(8,128)}, f32[128,1024]{1,0:T(8,128)}, u32[]{:S(2)}, u32[]{:S(2)}) collective-permute-start(f32[128,1024]{1,0:T(8,128)} %slice.244), channel_id=1, source_target_pairs={{0,4},{1,5},{2,6},{3,7},{4,0},{5,1},{6,2},{7,3},{8,12},{9,13},{10,... | collective-permute-start | bytes 1572872 | tf_op jit(solution)/shard_map/ppermute | solution.py:23
  88.6 1.5 copy-start.9
  88.6 1.8 copy-start.17
  88.6 2.1 copy-start.20
  101.5 7.4 %copy-start.15 = (f32[512,1024]{1,0:T(8,128)S(1)}, f32[512,1024]{1,0:T(8,128)}, u32[]{:S(2)}) copy-start(f32[512,1024]{1,0:T(8,128)} %constant_dynamic-update-slice_fusion.15) | copy-start | bytes 6291460
  104.9 11.1 %copy-start.10 = (f32[1024,256]{1,0:T(8,128)S(1)}, f32[1024,256]{1,0:T(8,128)}, u32[]{:S(2)}) copy-start(f32[1024,256]{1,0:T(8,128)} %get-tuple-element.23) | copy-start | bytes 3145732
  104.9 11.1 %copy-start.18 = (f32[1024,256]{1,0:T(8,128)S(1)}, f32[1024,256]{1,0:T(8,128)}, u32[]{:S(2)}) copy-start(f32[1024,256]{1,0:T(8,128)} %copy-done.16) | copy-start | bytes 3145732
  104.9 11.1 %copy-start.21 = (f32[1024,256]{1,0:T(8,128)S(1)}, f32[1024,256]{1,0:T(8,128)}, u32[]{:S(2)}) copy-start(f32[1024,256]{1,0:T(8,128)} %copy-done.19) | copy-start | bytes 3145732
  104.9 11.1 %copy-start.24 = (f32[1024,256]{1,0:T(8,128)S(1)}, f32[1024,256]{1,0:T(8,128)}, u32[]{:S(2)}) copy-start(f32[1024,256]{1,0:T(8,128)} %copy-done.22) | copy-start | bytes 3145732
  104.9 51.0 %collective-permute-start.37 = (f32[4,512,256]{2,0,1:T(4,128)}, f32[4,512,256]{2,0,1:T(4,128)}, u32[]{:S(2)}, u32[]{:S(2)}) collective-permute-start(f32[4,512,256]{2,0,1:T(4,128)} %bitcast.22), channel_id=1, source_target_pairs={{0,32},{1,33},{2,34},{3,35},{4,36},{5,37},{6,38},{7,39},{16,48},{1... | collective-permute-start | bytes 6291464 | tf_op jit(solution)/shard_map/ppermute | solution.py:23
  109.8 69.7 %collective-permute-start.32 = (f32[4,512,256]{2,0,1:T(4,128)}, f32[4,512,256]{2,0,1:T(4,128)}, u32[]{:S(2)}, u32[]{:S(2)}) collective-permute-start(f32[4,512,256]{2,0,1:T(4,128)} %bitcast.15), channel_id=1, source_target_pairs={{8,40},{9,41},{10,42},{11,43},{12,44},{13,45},{14,46},{15,47},{24,... | collective-permute-start | bytes 6291464 | tf_op jit(solution)/shard_map/ppermute | solution.py:23
  123.3 92.9 %collective-permute-start.27 = (f32[4,512,256]{2,0,1:T(4,128)S(1)}, f32[4,512,256]{2,0,1:T(4,128)}, u32[]{:S(2)}, u32[]{:S(2)}) collective-permute-start(f32[4,512,256]{2,0,1:T(4,128)S(1)} %bitcast.87), channel_id=1, source_target_pairs={{0,32},{1,33},{2,34},{3,35},{4,36},{5,37},{6,38},{7,39},{16,48},{1... | collective-permute-start | bytes 6291464 | tf_op jit(solution)/shard_map/ppermute | solution.py:23
  148.7 32.3 %collective-permute-start.11 = (f32[512,256]{1,0:T(8,128)}, f32[512,256]{1,0:T(8,128)}, u32[]{:S(2)}, u32[]{:S(2)}) collective-permute-start(f32[512,256]{1,0:T(8,128)} %bitcast.1), channel_id=1, source_target_pairs={{0,1},{1,0},{2,3},{3,2},{4,5},{5,4},{6,7},{7,6},{16,17},{17,16},{1... | collective-permute-start | bytes 1572872 | tf_op jit(solution)/shard_map/ppermute | solution.py:23
  150.8 31.7 %collective-permute-start.12 = (f32[512,256]{1,0:T(8,128)}, f32[512,256]{1,0:T(8,128)}, u32[]{:S(2)}, u32[]{:S(2)}) collective-permute-start(f32[512,256]{1,0:T(8,128)} %bitcast.116), channel_id=1, source_target_pairs={{0,3},{1,2},{2,1},{3,0},{4,7},{5,6},{6,5},{7,4},{16,19},{17,18},{1... | collective-permute-start | bytes 1572872 | tf_op jit(solution)/shard_map/ppermute | solution.py:23
  156.0 48.7 %collective-permute-start.13 = (f32[512,256]{1,0:T(8,128)}, f32[512,256]{1,0:T(8,128)}, u32[]{:S(2)}, u32[]{:S(2)}) collective-permute-start(f32[512,256]{1,0:T(8,128)} %bitcast.111), channel_id=1, source_target_pairs={{0,16},{1,17},{2,18},{3,19},{4,20},{5,21},{6,22},{7,23},{16,0},{17... | collective-permute-start | bytes 1572872 | tf_op jit(solution)/shard_map/ppermute | solution.py:23
  179.5 28.9 %collective-permute-start.38 = (f32[512,256]{1,0:T(8,128)}, f32[512,256]{1,0:T(8,128)}, u32[]{:S(2)}, u32[]{:S(2)}) collective-permute-start(f32[512,256]{1,0:T(8,128)} %bitcast.23), channel_id=1, source_target_pairs={{8,9},{9,8},{10,11},{11,10},{12,13},{13,12},{14,15},{15,14},{24,25... | collective-permute-start | bytes 1572872 | tf_op jit(solution)/shard_map/ppermute | solution.py:23
  181.0 30.4 %collective-permute-start.39 = (f32[512,256]{1,0:T(8,128)}, f32[512,256]{1,0:T(8,128)}, u32[]{:S(2)}, u32[]{:S(2)}) collective-permute-start(f32[512,256]{1,0:T(8,128)} %bitcast.114), channel_id=1, source_target_pairs={{8,11},{9,10},{10,9},{11,8},{12,15},{13,14},{14,13},{15,12},{24,27... | collective-permute-start | bytes 1572872 | tf_op jit(solution)/shard_map/ppermute | solution.py:23
  182.4 31.4 %collective-permute-start.40 = (f32[512,256]{1,0:T(8,128)}, f32[512,256]{1,0:T(8,128)}, u32[]{:S(2)}, u32[]{:S(2)}) collective-permute-start(f32[512,256]{1,0:T(8,128)} %bitcast.112), channel_id=1, source_target_pairs={{8,24},{9,25},{10,26},{11,27},{12,28},{13,29},{14,30},{15,31},{24,... | collective-permute-start | bytes 1572872 | tf_op jit(solution)/shard_map/ppermute | solution.py:23
  204.7 9.2 %copy-start = (f32[1,512,256]{2,0,1:T(1,128)S(1)}, f32[1,512,256]{2,0,1:T(1,128)}, u32[]{:S(2)}) copy-start(f32[1,512,256]{2,0,1:T(1,128)} %get-tuple-element.19) | copy-start | bytes 1572868
  204.7 23.2 %collective-permute-start.33 = (f32[512,256]{1,0:T(8,128)}, f32[512,256]{1,0:T(8,128)}, u32[]{:S(2)}, u32[]{:S(2)}) collective-permute-start(f32[512,256]{1,0:T(8,128)} %bitcast.113), channel_id=1, source_target_pairs={{0,1},{1,0},{2,3},{3,2},{4,5},{5,4},{6,7},{7,6},{16,17},{17,16},{1... | collective-permute-start | bytes 1572872 | tf_op jit(solution)/shard_map/ppermute | solution.py:23
  208.4 7.8 %copy-start.1 = (f32[512,256]{1,0:T(8,128)}, f32[512,256]{1,0:T(8,128)S(1)}, u32[]{:S(2)}) copy-start(f32[512,256]{1,0:T(8,128)S(1)} %fusion.7) | copy-start | bytes 1572868
  208.4 20.9 %collective-permute-start.34 = (f32[512,256]{1,0:T(8,128)}, f32[512,256]{1,0:T(8,128)}, u32[]{:S(2)}, u32[]{:S(2)}) collective-permute-start(f32[512,256]{1,0:T(8,128)} %bitcast.17), channel_id=1, source_target_pairs={{0,3},{1,2},{2,1},{3,0},{4,7},{5,6},{6,5},{7,4},{16,19},{17,18},{1... | collective-permute-start | bytes 1572872 | tf_op jit(solution)/shard_map/ppermute | solution.py:23
  211.4 22.9 %collective-permute-start.35 = (f32[512,256]{1,0:T(8,128)}, f32[512,256]{1,0:T(8,128)}, u32[]{:S(2)}, u32[]{:S(2)}) collective-permute-start(f32[512,256]{1,0:T(8,128)} %bitcast.18), channel_id=1, source_target_pairs={{0,16},{1,17},{2,18},{3,19},{4,20},{5,21},{6,22},{7,23},{16,0},{17... | collective-permute-start | bytes 1572872 | tf_op jit(solution)/shard_map/ppermute | solution.py:23
  223.6 2.0 copy-start.4
  224.7 3.9 %copy-start.3 = (f32[512,256]{1,0:T(8,128)S(1)}, f32[512,256]{1,0:T(8,128)}, u32[]{:S(2)}) copy-start(f32[512,256]{1,0:T(8,128)} %fusion.1) | copy-start | bytes 1572868
  225.6 1.6 copy-start.11
  226.5 10.7 %collective-permute-start.28 = (f32[512,256]{1,0:T(8,128)}, f32[512,256]{1,0:T(8,128)S(1)}, u32[]{:S(2)}, u32[]{:S(2)}) collective-permute-start(f32[512,256]{1,0:T(8,128)} %bitcast.8), channel_id=1, source_target_pairs={{8,9},{9,8},{10,11},{11,10},{12,13},{13,12},{14,15},{15,14},{24,25... | collective-permute-start | bytes 1572872 | tf_op jit(solution)/shard_map/ppermute | solution.py:23
  227.2 12.4 %collective-permute-start.29 = (f32[512,256]{1,0:T(8,128)S(1)}, f32[512,256]{1,0:T(8,128)S(1)}, u32[]{:S(2)}, u32[]{:S(2)}) collective-permute-start(f32[512,256]{1,0:T(8,128)S(1)} %bitcast.117), channel_id=1, source_target_pairs={{8,11},{9,10},{10,9},{11,8},{12,15},{13,14},{14,13},{15,12},{24,27... | collective-permute-start | bytes 1572872 | tf_op jit(solution)/shard_map/ppermute | solution.py:23
  227.9 11.7 %collective-permute-start.30 = (f32[512,256]{1,0:T(8,128)}, f32[512,256]{1,0:T(8,128)S(1)}, u32[]{:S(2)}, u32[]{:S(2)}) collective-permute-start(f32[512,256]{1,0:T(8,128)} %bitcast.115), channel_id=1, source_target_pairs={{8,24},{9,25},{10,26},{11,27},{12,28},{13,29},{14,30},{15,31},{24,... | collective-permute-start | bytes 1572872 | tf_op jit(solution)/shard_map/ppermute | solution.py:23
  229.3 20.9 %collective-permute-start.14 = (f32[256,256]{1,0:T(8,128)S(1)}, f32[256,256]{1,0:T(8,128)}, u32[]{:S(2)}, u32[]{:S(2)}) collective-permute-start(f32[256,256]{1,0:T(8,128)S(1)} %dynamic-slice_bitcast_fusion.3), channel_id=1, source_target_pairs={{0,64},{1,65},{2,66},{3,67},{4,68},{5,69},{6,70},{7,71},{16,80},{1... | collective-permute-start | bytes 786440 | tf_op jit(solution)/shard_map/ppermute | solution.py:23
  234.3 6.2 %collective-permute-start.41 = (f32[256,256]{1,0:T(8,128)}, f32[256,256]{1,0:T(8,128)}, u32[]{:S(2)}, u32[]{:S(2)}) collective-permute-start(f32[256,256]{1,0:T(8,128)} %dynamic-slice_bitcast_fusion), channel_id=1, source_target_pairs={{8,72},{9,73},{10,74},{11,75},{12,76},{13,77},{14,78},{15,79},{24,... | collective-permute-start | bytes 786440 | tf_op jit(solution)/shard_map/ppermute | solution.py:23
  237.2 12.0 %collective-permute-start.36 = (f32[256,256]{1,0:T(8,128)S(1)}, f32[256,256]{1,0:T(8,128)}, u32[]{:S(2)}, u32[]{:S(2)}) collective-permute-start(f32[256,256]{1,0:T(8,128)S(1)} %dynamic-slice_bitcast_fusion.1), channel_id=1, source_target_pairs={{0,64},{1,65},{2,66},{3,67},{4,68},{5,69},{6,70},{7,71},{16,80},{1... | collective-permute-start | bytes 786440 | tf_op jit(solution)/shard_map/ppermute | solution.py:23
  239.6 10.7 %copy-start.2 = (f32[512,256]{1,0:T(8,128)S(1)}, f32[512,256]{1,0:T(8,128)}, u32[]{:S(2)}) copy-start(f32[512,256]{1,0:T(8,128)} %copy-done.1) | copy-start | bytes 1572868
  239.8 10.5 %collective-permute-start.31 = (f32[256,256]{1,0:T(8,128)S(1)}, f32[256,256]{1,0:T(8,128)S(1)}, u32[]{:S(2)}, u32[]{:S(2)}) collective-permute-start(f32[256,256]{1,0:T(8,128)S(1)} %dynamic-slice_bitcast_fusion.2), channel_id=1, source_target_pairs={{8,72},{9,73},{10,74},{11,75},{12,76},{13,77},{14,78},{15,79},{24,... | collective-permute-start | bytes 786440 | tf_op jit(solution)/shard_map/ppermute | solution.py:23
  (3 other events, 3.3 us)

commit v2 on v0

v2 whole, which is shorter than its diff:
```python
import functools

import jax
import jax.numpy as jnp
from jax import lax
from jax.experimental import pallas as pl
from jax.experimental.pallas import tpu as pltpu
from jax.sharding import PartitionSpec as P

AXES = ("rep", "grid")
VMEM_LIMIT = 48 * 1024 * 1024


def number(x_hi, core, x_lo, z, y):
    return (2 * x_hi + core) * 32 + 16 * x_lo + 4 * z + y


def every(pick):
    return [
        pick(x_hi, core, x_lo, z, y)
        for x_hi in range(2) for core in range(2) for x_lo in range(2) for z in range(4) for y in range(4)
    ]


def moved(dx=0, dz=0, dy=0, core=0):
    return every(lambda h, c, x, z, y: (number(h, c, x, z, y), number(h, c ^ core, x ^ dx, z ^ dz, y ^ dy)))


def send(value, **where):
    return lax.ppermute(value, AXES, moved(**where))


PLANES = [
    [number(h, c, x, z, y) for z in range(4) for y in range(4)]
    for h in range(2) for c in range(2) for x in range(2)
]
LINES = [
    [number(h, c, x, z, y) for h in range(2) for c in range(2) for x in range(2)]
    for z in range(4) for y in range(4)
]


def halves(value):
    high = value.astype(jnp.bfloat16)
    return high, (value - high.astype(jnp.float32)).astype(jnp.bfloat16)


def split_kernel(own_0, own_1, far_0, far_1, high, low):
    for piece, refs in enumerate(((own_0, far_0), (own_1, far_1))):
        for group, ref in enumerate(refs):
            columns = ref.shape[1]
            at = slice(group * columns, (group + 1) * columns)
            high[piece, :, at], low[piece, :, at] = halves(ref[...])


def split_right(own_0, own_1, far_0, far_1, steps=8):
    depth, columns = own_0.shape
    shape = jax.ShapeDtypeStruct((2, depth, 2 * columns), jnp.bfloat16)
    out = pl.BlockSpec((2, depth // steps, 2 * columns), lambda i: (0, i, 0))
    return pl.pallas_call(
        split_kernel,
        grid=(steps,),
        in_specs=[pl.BlockSpec((depth // steps, columns), lambda i: (i, 0))] * 4,
        out_specs=[out, out],
        out_shape=[shape, shape],
        compiler_params=pltpu.CompilerParams(vmem_limit_bytes=VMEM_LIMIT),
        cost_estimate=pl.CostEstimate(flops=0, bytes_accessed=depth * columns * 32, transcendentals=0),
    )(own_0, own_1, far_0, far_1)


def multiply_kernel(place, left, high, low, *rest):
    out = rest[-1]
    own = place[1]
    total = None
    for piece in range(2):
        block = left[:, piece]
        left_high, left_low = halves(block.reshape(block.shape[0] * block.shape[1], block.shape[2]))
        for one, two in ((left_high, high), (left_high, low), (left_low, high)):
            term = jnp.dot(one, two[piece], preferred_element_type=jnp.float32)
            total = term if total is None else total + term
    columns = total.shape[1] // 2
    out[0, 0, own] = total[:, :columns]
    out[0, 0, 1 - own] = total[:, columns:]


def multiply(place, left, high, low, earlier=None):
    positions, _, rows, depth = left.shape
    columns = high.shape[2] // 2
    group = positions // 2
    whole = pl.BlockSpec(high.shape, lambda i, place: (0, 0, 0), pipeline_mode=pl.Buffered(1))
    chained = () if earlier is None else (earlier,)
    return pl.pallas_call(
        multiply_kernel,
        grid_spec=pltpu.PrefetchScalarGridSpec(
            num_scalar_prefetch=1,
            grid=(2,),
            in_specs=[
                pl.BlockSpec((group, 2, rows, depth), lambda i, place: (i, 0, 0, 0)),
                whole,
                whole,
            ] + [pl.BlockSpec(memory_space=pl.ANY)] * len(chained),
            out_specs=pl.BlockSpec(
                (1, 1, 2, group * rows, columns), lambda i, place: (place[0], i, 0, 0, 0)
            ),
        ),
        out_shape=jax.ShapeDtypeStruct((2, 2, 2, group * rows, columns), jnp.float32),
        input_output_aliases={4: 0} if chained else {},
        compiler_params=pltpu.CompilerParams(vmem_limit_bytes=VMEM_LIMIT),
        cost_estimate=pl.CostEstimate(
            flops=12 * positions * rows * depth * 2 * columns, bytes_accessed=32 << 20, transcendentals=0
        ),
    )(place, left, high, low, *chained)


def per_device(left, right):
    rows, depth = left.shape[0] // 2, left.shape[1] // 2
    columns = right.shape[1]
    rep, grid = lax.axis_index("rep"), lax.axis_index("grid")
    core, x_lo = rep & 1, grid >> 4

    def left_part(value, at, half):
        return lax.dynamic_slice(value, (at * rows, half * depth), (rows, depth))

    swapped = send(lax.dynamic_slice(left, ((1 - core) * rows, 0), (rows, 2 * depth)), core=1)
    mine = jnp.stack([left_part(left, core, x_lo), left_part(swapped, 0, x_lo)])
    theirs = jnp.stack([left_part(left, core, 1 - x_lo), left_part(swapped, 0, 1 - x_lo)])

    near = lax.all_gather(mine, AXES, axis=0, axis_index_groups=PLANES)
    far = lax.all_gather(send(theirs, dx=1), AXES, axis=0, axis_index_groups=PLANES)

    own = lax.dynamic_slice(right, (x_lo * depth, 0), (depth, columns))
    other = send(lax.dynamic_slice(right, ((1 - x_lo) * depth, 0), (depth, columns)), dx=1)
    high, low = split_right(own, send(own, core=1), other, send(other, core=1))

    parts = multiply(jnp.stack([x_lo, x_lo]), near, high, low)
    parts = multiply(jnp.stack([1 - x_lo, x_lo]), far, high, low, parts)

    parts = lax.all_to_all(
        parts.reshape(-1, columns), AXES, 0, 0, tiled=True, axis_index_groups=LINES
    )
    parts = parts.reshape(2, 2, 2, 8, rows, columns)
    total = (parts[0, :, 0] + parts[0, :, 1]) + (parts[1, :, 0] + parts[1, :, 1])
    return total.transpose(1, 0, 2, 3).reshape(16 * rows, columns)


def solution(mesh):
    return jax.shard_map(
        per_device,
        mesh=mesh,
        in_specs=(P("grid", "rep"), P("rep", "grid")),
        out_specs=P("rep", "grid"),
        check_vma=False,
    )
```

time: 450 us -> 209 us (0.46)
  waiting for transfers between devices: 405 us -> 119 us
  Pallas kernels: 0 us -> 31.8 us
  matrix products: 31.4 us -> 0 us
  blocking collectives: 0 us -> 31.3 us
  local copies, waits for them, and re-layouts: 0 us -> 7.06 us
    all_gather x1 -> x2, waiting for transfers between devices: 369 us -> 56.5 us  [the longest x1 56.5 us: per_device(): lax.all_gather(send(theirs, dx=1), AXES, axis=0, axis_index_groups=PLANES)]
    ppermute x0 -> x5, waiting for transfers between devices: none -> 62.5 us  [send(): return lax.ppermute(value, AXES, moved(**where))]
    reduce_scatter x1 -> x0, waiting for transfers between devices: 34.9 us -> none  [per_device(): lax.psum_scatter(partial_value, 'rep', scatter_dimension=0, tiled=True)]
    pallas_call x0 -> x3, Pallas kernels: none -> 31.8 us  [the longest x2 24.2 us: multiply(): pl.pallas_call(multiply_kernel, grid_spec=pltpu.PrefetchScalarGridSpec(nu...]
    dot_general x1 -> x0, matrix products: 31.4 us -> none  [per_device(): jnp.dot(lax.all_gather(panel_left, 'grid', axis=0, tiled=True), panel_rig...]
    all_to_all x0 -> x1, blocking collectives: none -> 31.3 us  [per_device(): lax.all_to_all(parts.reshape(-1, columns), AXES, 0, 0, tiled=True, axis_i...]
  transfers between devices with their start and end apart: 2 -> 7, of which waited for: 2 -> 5; matrix products, arithmetic and copies ran while one was open for 0% -> 2% of each run, Pallas kernels for 0% -> 9%
where the time goes in v2:
time: 209 us; the launch traced here: 208 us
  waiting for transfers between devices  119 us (57%)
  Pallas kernels  31.8 us (15%)
  blocking collectives  31.3 us (15%)
  between operations  13.5 us (6%)
  local copies, waits for them, and re-layouts  7.06 us (3%)
  starting transfers between devices  3.44 us (2%)
    ppermute x5, waiting for transfers between devices, send(): return lax.ppermute(value, AXES, moved(**where))  62.5 us
    all_gather x1, waiting for transfers between devices, per_device(): lax.all_gather(send(theirs, dx=1), AXES, axis=0, axis_index_groups=PLANES)  56.5 us
    all_to_all x1, blocking collectives, per_device(): lax.all_to_all(parts.reshape(-1, columns), AXES, 0, 0, tiled=True, axis_i...  31.3 us
    pallas_call x2, Pallas kernels, multiply(): pl.pallas_call(multiply_kernel, grid_spec=pltpu.PrefetchScalarGridSpec(nu...  24.2 us
    pallas_call x1, Pallas kernels, split_right(): pl.pallas_call(split_kernel, grid=(steps,), in_specs=[pl.BlockSpec((depth...  7.63 us
  transfers between devices with their start and end apart: 7, of which 5 were waited for; matrix products, arithmetic and copies ran while one was open for 2% of the time, Pallas kernels for 9%

profile of v2, /device:TPU:0, one launch (start us, length us, event | category | flops | bytes accessed | tf_op | source)
XLA Modules:
  0.0 208.1 jit_solution(2366123242807573034)
XLA Ops:
  6.5 0.0 all-gather.7.cloned.1.call-start
  6.5 1.1 constant_dynamic-slice_fusion.2
  7.6 0.1 collective-permute-start
  7.7 1.1 dynamic-slice_bitcast_fusion.1
  8.8 0.8 collective-permute-done
  9.6 0.9 pad_maximum_fusion.1
  10.5 0.0 all-gather.7.cloned.1.call-update
  10.6 0.0 all-gather.5.cloned.1.call-start
  10.7 1.7 collective-permute-start.1
  12.3 12.4 %collective-permute-done.1 = f32[2,32,2048]{2,1,0:T(8,128)S(1)} collective-permute-done((f32[2,32,2048]{2,1,0:T(8,128)S(1)}, f32[2,32,2048]{2,1,0:T(8,128)S(1)}, u32[]{:S(2)}, u32[]{:S(2)}) %collective-permute-start.1) | collective-permute-done | bytes 524320 | tf_op jit(solution)/shard_map/ppermute | solution.py:30
  24.7 0.0 copy-start.2
  24.7 0.8 copy-done.2
  25.5 0.0 all-gather.5.cloned.1.call-update
  25.5 2.5 %constant_dynamic-slice_fusion = (f32[2048,256]{1,0:T(8,128)S(1)}, f32[2048,256]{1,0:T(8,128)S(1)}) fusion(f32[4096,256]{1,0:T(8,128)} %param.3, s32[]{:T(128)S(6)} %select_n.18, s32[]{:T(128)S(6)} %select_n.20), kind=kLoop, calls=%fused_computation.9 | loop fusion | bytes 8388616 | tf_op jit(solution)/shard_map/dynamic_slice | solution.py:132
  28.0 1.7 collective-permute-start.3
  29.7 0.0 collective-permute-start.2
  29.7 45.3 %collective-permute-done.3.far_0 = f32[2048,256]{1,0:T(8,128)S(1)} collective-permute-done((f32[2048,256]{1,0:T(8,128)S(1)}, f32[2048,256]{1,0:T(8,128)S(1)}, u32[]{:S(2)}, u32[]{:S(2)}) %collective-permute-start.3) | collective-permute-done | bytes 2097184 | tf_op jit(solution)/shard_map/ppermute | solution.py:30
  74.9 0.0 copy-start
  74.9 0.0 collective-permute-start.4
  75.0 0.1 pad_add_fusion
  75.0 0.0 collective-permute-done.2.own_1
  75.0 4.1 %collective-permute-done.4.far_1 = f32[2048,256]{1,0:T(8,128)S(1)} collective-permute-done((f32[2048,256]{1,0:T(8,128)S(1)}, f32[2048,256]{1,0:T(8,128)S(1)}, u32[]{:S(2)}, u32[]{:S(2)}) %collective-permute-start.4) | collective-permute-done | bytes 2097184 | tf_op jit(solution)/shard_map/ppermute | solution.py:30
  79.1 0.0 copy-done
  79.1 0.0 copy-start.1
  79.1 1.3 copy-done.1
  80.5 7.6 %shard_map.28 = (bf16[2,2048,512]{2,1,0:T(8,128)(2,1)}, bf16[2,2048,512]{2,1,0:T(8,128)(2,1)}) custom-call(f32[2048,256]{1,0:T(8,128)S(1)} %get-tuple-element.10.own_0, f32[2048,256]{1,0:T(8,128)S(1)} %collective-permute-done.2.own_1, f32[2048,256]{1,0:T(8,128)} %copy-done, f32[2048,256]{1,0:T(8,128)} %copy-done.1), custom_call_target="tpu_custom_call" | custom-call | bytes 16777216 | tf_op jit(solution)/shard_map/pallas_call | solution.py:60
  88.1 0.0 all-gather.7.cloned.1.call-done
  88.1 12.1 %shard_map.29.rest_0_ = f32[2,2,2,256,256]{4,3,2,1,0:T(8,128)S(1)} custom-call(s32[2]{0:T(128)S(1)} %get-tuple-element.20.place, f32[16,2,32,2048]{3,2,1,0:T(8,128)} %bitcast.21, bf16[2,2048,512]{2,1,0:T(8,128)(2,1)} %get-tuple-element.7.high, bf16[2,2048,512]{2,1,0:T(8,128)(2,1)} %get-tuple-element.8.low), custom_call_target="tpu_custom_call" | custom-call | flops 6442450944 | bytes 33554432 | tf_op jit(solution)/shard_map/pallas_call | solution.py:92
  100.2 56.5 %all-gather.5.cloned.1.call-done = f32[32,32,2048]{2,1,0:T(8,128)} async-done(((f32[2,32,2048]{2,1,0:T(8,128)}), f32[32,32,2048]{2,1,0:T(8,128)}) %all-gather.5.cloned.1.call-update) | async-done | bytes 8388624 | tf_op jit(solution)/shard_map/all_gather | solution.py:129
  156.7 12.1 %shard_map.30 = f32[2,2,2,256,256]{4,3,2,1,0:T(8,128)S(1)} custom-call(s32[2]{0:T(128)S(1)} %get-tuple-element.19.place, f32[16,2,32,2048]{3,2,1,0:T(8,128)} %bitcast.22, bf16[2,2048,512]{2,1,0:T(8,128)(2,1)} %get-tuple-element.7.high, bf16[2,2048,512]{2,1,0:T(8,128)(2,1)} %get-tuple-element.8.low, ...), custom_call_target="tpu_custom_call", output_to_operand_aliasing={{}: (4, {})} | custom-call | flops 6442450944 | bytes 33554432 | tf_op jit(solution)/shard_map/pallas_call | solution.py:92
  168.8 31.3 %all_to_all.9 = f32[8,256,256]{2,1,0:T(8,128)S(1)} all-to-all(f32[8,256,256]{2,1,0:T(8,128)S(1)} %bitcast.19), channel_id=1, replica_groups={{0,16,32,48,64,80,96,112},{1,17,33,49,65,81,97,113},{2,18,34,50,66,82,9..., dimensions={0} | all-to-all | bytes 4194304 | tf_op jit(solution)/shard_map/all_to_all | solution.py:138
  200.0 0.2 fusion.1
  200.3 1.0 fusion
  (2 shorter events, 0.1 us)
Async XLA Ops:
  6.5 81.6 %all-gather.7.cloned.1.call-start = ((), (), s32[]{:S(2)}) async-start(), calls=%async_computation.2 | async-start | bytes 8912896 | tf_op jit(solution)/shard_map/all_gather | solution.py:128
  7.6 2.0 collective-permute-start
  10.6 146.1 %all-gather.5.cloned.1.call-start = ((), (), s32[]{:S(2)}) async-start(), calls=%async_computation.1 | async-start | bytes 8912896 | tf_op jit(solution)/shard_map/all_gather | solution.py:129
  10.7 14.0 %collective-permute-start.1 = (f32[2,32,2048]{2,1,0:T(8,128)S(1)}, f32[2,32,2048]{2,1,0:T(8,128)S(1)}, u32[]{:S(2)}, u32[]{:S(2)}) collective-permute-start(f32[2,32,2048]{2,1,0:T(8,128)S(1)} %pad_maximum_fusion), channel_id=1, source_target_pairs={{0,16},{1,17},{2,18},{3,19},{4,20},{5,21},{6,22},{7,23},{8,24},{9,... | collective-permute-start | bytes 1572872 | tf_op jit(solution)/shard_map/ppermute | solution.py:30
  24.7 0.8 copy-start.2
  28.0 46.9 %collective-permute-start.3 = (f32[2048,256]{1,0:T(8,128)S(1)}, f32[2048,256]{1,0:T(8,128)S(1)}, u32[]{:S(2)}, u32[]{:S(2)}) collective-permute-start(f32[2048,256]{1,0:T(8,128)S(1)} %get-tuple-element.9), channel_id=1, source_target_pairs={{0,16},{1,17},{2,18},{3,19},{4,20},{5,21},{6,22},{7,23},{8,24},{9,... | collective-permute-start | bytes 6291464 | tf_op jit(solution)/shard_map/ppermute | solution.py:30
  29.7 45.4 %collective-permute-start.2 = (f32[2048,256]{1,0:T(8,128)S(1)}, f32[2048,256]{1,0:T(8,128)S(1)}, u32[]{:S(2)}, u32[]{:S(2)}) collective-permute-start(f32[2048,256]{1,0:T(8,128)S(1)} %get-tuple-element.10.own_0), channel_id=1, source_target_pairs={{0,32},{1,33},{2,34},{3,35},{4,36},{5,37},{6,38},{7,39},{8,40},{9,... | collective-permute-start | bytes 6291464 | tf_op jit(solution)/shard_map/ppermute | solution.py:30
  74.9 4.2 %copy-start = (f32[2048,256]{1,0:T(8,128)}, f32[2048,256]{1,0:T(8,128)S(1)}, u32[]{:S(2)}) copy-start(f32[2048,256]{1,0:T(8,128)S(1)} %collective-permute-done.3.far_0) | copy-start | bytes 6291460
  74.9 4.2 %collective-permute-start.4 = (f32[2048,256]{1,0:T(8,128)S(1)}, f32[2048,256]{1,0:T(8,128)S(1)}, u32[]{:S(2)}, u32[]{:S(2)}) collective-permute-start(f32[2048,256]{1,0:T(8,128)S(1)} %collective-permute-done.3.far_0), channel_id=1, source_target_pairs={{0,32},{1,33},{2,34},{3,35},{4,36},{5,37},{6,38},{7,39},{8,40},{9,... | collective-permute-start | bytes 6291464 | tf_op jit(solution)/shard_map/ppermute | solution.py:30
  79.1 1.3 copy-start.1
Sparse Core Ops, SparseCore 0:
  10.7 73.3 all-gather.6
  86.2 70.4 all-gather.4

commit v3 on v0

v3 whole, which is shorter than its diff:
```python
import jax
import jax.numpy as jnp
from jax import lax
from jax.experimental import pallas as pl
from jax.experimental.pallas import tpu as pltpu
from jax.sharding import PartitionSpec as P

AXES = ("rep", "grid")
VMEM_LIMIT = 40 * 1024 * 1024
PARAMS = pltpu.CompilerParams(vmem_limit_bytes=VMEM_LIMIT)


def number(x_hi, core, x_lo, z, y):
    return (2 * x_hi + core) * 32 + 16 * x_lo + 4 * z + y


def pairs(target):
    found = []
    for x_hi in range(2):
        for core in range(2):
            for x_lo in range(2):
                for z in range(4):
                    for y in range(4):
                        there = target(x_hi, core, x_lo, z, y)
                        if there is not None:
                            found.append((number(x_hi, core, x_lo, z, y), number(*there)))
    return found


def send(value, dx=0, dz=0, dy=0, core=0):
    return lax.ppermute(
        value, AXES, pairs(lambda h, c, x, z, y: (h, c ^ core, x ^ dx, z ^ dz, y ^ dy))
    )


def send_if(value, same, other):
    def target(h, c, x, z, y):
        flips = same if h == x else other
        return None if flips is None else (h ^ flips[0], c, x ^ flips[1], z, y)

    return lax.ppermute(value, AXES, pairs(target))


PLANES = [
    [number(h, c, x, z, y) for z in range(4) for y in range(4)]
    for h in range(2) for c in range(2) for x in range(2)
]
POSITIONS = [(dz, dy) for dz in range(4) for dy in range(4)]
EARLY = [(dz, dy) for dz, dy in POSITIONS if dz != 2 and dy != 2]
LATE = [(dz, dy) for dz, dy in POSITIONS if dz == 2 or dy == 2]


def halves(value):
    high = value.astype(jnp.bfloat16)
    return high, (value - high.astype(jnp.float32)).astype(jnp.bfloat16)


def split_kernel(first, second, high, low):
    for piece, ref in enumerate((first, second)):
        high[piece], low[piece] = halves(ref[...])


def split_right(first, second, steps=4):
    depth, columns = first.shape
    shape = jax.ShapeDtypeStruct((2, depth, columns), jnp.bfloat16)
    out = pl.BlockSpec((2, depth // steps, columns), lambda i: (0, i, 0))
    return pl.pallas_call(
        split_kernel,
        grid=(steps,),
        in_specs=[pl.BlockSpec((depth // steps, columns), lambda i: (i, 0))] * 2,
        out_specs=[out, out],
        out_shape=[shape, shape],
        compiler_params=PARAMS,
        cost_estimate=pl.CostEstimate(flops=0, bytes_accessed=depth * columns * 16, transcendentals=0),
    )(first, second)


def products(lefts, rights):
    found = []
    for high, low in rights:
        total = None
        for piece, (left_high, left_low) in enumerate(lefts):
            for one, two in ((left_high, high), (left_high, low), (left_low, high)):
                term = jnp.dot(one, two[piece], preferred_element_type=jnp.float32)
                total = term if total is None else total + term
        found.append(total)
    return found


def near_kernel(same, left, own_high, own_low, far_high, far_low, first, second):
    lefts = []
    for piece in range(2):
        block = left[:, piece]
        lefts.append(halves(block.reshape(block.shape[0] * block.shape[1], block.shape[2])))
    own, far = products(lefts, ((own_high, own_low), (far_high, far_low)))
    swap = same[0] == 1
    first[...] = jnp.where(swap, far, own).reshape(first.shape)
    second[...] = jnp.where(swap, own, far).reshape(second.shape)


def whole(value):
    return pl.BlockSpec(value.shape, lambda *_: (0,) * value.ndim, pipeline_mode=pl.Buffered(1))


def near_products(same, left, rights):
    positions, _, rows, depth = left.shape
    columns = rights[0].shape[2]
    group = positions // 2
    shape = jax.ShapeDtypeStruct((positions, rows, columns), jnp.float32)
    out = pl.BlockSpec((group, rows, columns), lambda i, same: (i, 0, 0))
    return pl.pallas_call(
        near_kernel,
        grid_spec=pltpu.PrefetchScalarGridSpec(
            num_scalar_prefetch=1,
            grid=(2,),
            in_specs=[pl.BlockSpec((group, 2, rows, depth), lambda i, same: (i, 0, 0, 0))]
            + [whole(right) for right in rights],
            out_specs=[out, out],
        ),
        out_shape=[shape, shape],
        compiler_params=PARAMS,
        cost_estimate=pl.CostEstimate(
            flops=24 * positions * rows * depth * columns, bytes_accessed=20 << 20, transcendentals=0
        ),
    )(same, left, *rights)


def far_products(same, sources, rights):
    positions = len(sources[0])
    columns = rights[0].shape[2]
    rows, depth = sources[0][0][0].shape[1:]
    arrays, uses = [], {}
    for piece in sources:
        for array, at in piece:
            if id(array) not in uses:
                uses[id(array)] = (len(arrays), set())
                arrays.append(array)
            uses[id(array)][1].add(at)
    specs, places = [], {}
    for array in arrays:
        slot, used = uses[id(array)]
        if len(used) == 1:
            (only,) = used
            specs.append(pl.BlockSpec((1, rows, depth), lambda i, same, only=only: (only, 0, 0)))
            places[slot, only] = 0
        else:
            specs.append(whole(array))
            places.update({(slot, at): at for at in used})
    plan = [[(uses[id(array)][0], places[uses[id(array)][0], at]) for array, at in piece] for piece in sources]

    def kernel(same, *refs):
        blocks, rest = refs[: len(arrays)], refs[len(arrays):]
        own_high, own_low, far_high, far_low, first, second, high, low = rest
        for piece in range(2):
            for place, (slot, at) in enumerate(plan[piece]):
                span = slice(place * rows, (place + 1) * rows)
                high[piece, span], low[piece, span] = halves(blocks[slot][at])
        lefts = [(high[piece], low[piece]) for piece in range(2)]
        own, far = products(lefts, ((own_high, own_low), (far_high, far_low)))
        swap = same[0] == 1
        first[...] = jnp.where(swap, own, far).reshape(first.shape)
        second[...] = jnp.where(swap, far, own).reshape(second.shape)

    shape = jax.ShapeDtypeStruct((positions, rows, columns), jnp.float32)
    scratch = pltpu.VMEM((2, positions * rows, depth), jnp.bfloat16)
    return pl.pallas_call(
        kernel,
        grid_spec=pltpu.PrefetchScalarGridSpec(
            num_scalar_prefetch=1,
            grid=(1,),
            in_specs=specs + [whole(right) for right in rights],
            out_specs=[pl.BlockSpec(shape.shape, lambda i, same: (0, 0, 0))] * 2,
            scratch_shapes=[scratch, scratch],
        ),
        out_shape=[shape, shape],
        compiler_params=PARAMS,
        cost_estimate=pl.CostEstimate(
            flops=24 * positions * rows * depth * columns, bytes_accessed=12 << 20, transcendentals=0
        ),
    )(same, *arrays, *rights)


def total_kernel(place, near_a, near_b, near_own, early_a, early_b, early_own, late_a, late_b, late_own, keep, give):
    same, core, z, y = place[0] == 1, place[1], place[2], place[3]
    groups = ((EARLY, early_a, early_b, early_own), (LATE, late_a, late_b, late_own))
    for positions, one, two, own in groups:
        for place_in, (dz, dy) in enumerate(positions):
            plane, line = z ^ dz, y ^ dy
            at = plane * 4 + line
            mine = jnp.where(same, near_own[at], own[place_in])
            value = near_a[at] + near_b[at] + one[place_in] + two[place_in] + mine
            into = (plane & 1) * 4 + line

            @pl.when((plane >> 1) == core)
            def _():
                keep[into] = value

            @pl.when((plane >> 1) != core)
            def _():
                give[into] = value


def total_of(place, near, early, late):
    _, rows, columns = near[0].shape
    shape = jax.ShapeDtypeStruct((8, rows, columns), jnp.float32)
    values = [*near, *early, *late]
    return pl.pallas_call(
        total_kernel,
        grid_spec=pltpu.PrefetchScalarGridSpec(
            num_scalar_prefetch=1,
            grid=(1,),
            in_specs=[whole(value) for value in values],
            out_specs=[pl.BlockSpec(shape.shape, lambda i, place: (0, 0, 0))] * 2,
        ),
        out_shape=[shape, shape],
        compiler_params=PARAMS,
        cost_estimate=pl.CostEstimate(flops=1 << 20, bytes_accessed=4 << 20, transcendentals=0),
    )(place, *values)


def join_kernel(core, kept, given, out):
    rows = kept.shape[1]
    mine = core[0]
    out[:, pl.ds(pl.multiple_of(mine * rows, rows), rows)] = kept[...]
    out[:, pl.ds(pl.multiple_of((1 - mine) * rows, rows), rows)] = given[...]


def join(core, kept, given):
    blocks, rows, columns = kept.shape
    shape = jax.ShapeDtypeStruct((blocks, 2 * rows, columns), jnp.float32)
    return pl.pallas_call(
        join_kernel,
        grid_spec=pltpu.PrefetchScalarGridSpec(
            num_scalar_prefetch=1,
            grid=(1,),
            in_specs=[whole(kept), whole(given)],
            out_specs=pl.BlockSpec(shape.shape, lambda i, core: (0, 0, 0)),
        ),
        out_shape=shape,
        compiler_params=PARAMS,
        cost_estimate=pl.CostEstimate(flops=0, bytes_accessed=1 << 20, transcendentals=0),
    )(core, kept, given)


def gathered(block, small, big):
    ring = [block] + [send(block, **{small: step}) for step in (1, 2, 3)]
    line = jnp.stack(ring)
    one, three = send(line, **{big: 1}), send(line, **{big: 3})
    two = send(one[:2], **{big: 3}), send(three[2:], **{big: 1})

    def source(far, near):
        if far == 2:
            return two[near >> 1], near & 1
        return {0: line, 1: one, 3: three}[far], near

    return source


def per_device(left, right):
    rows, depth = left.shape[0] // 2, left.shape[1] // 2
    columns = right.shape[1]
    rep, grid = lax.axis_index("rep"), lax.axis_index("grid")
    core, x_hi = rep & 1, rep >> 1
    x_lo, z, y = grid >> 4, (grid >> 2) & 3, grid & 3
    same = (x_hi == x_lo).astype(jnp.int32)

    def left_part(value, at, half):
        return lax.dynamic_slice(value, (at * rows, half * depth), (rows, depth))

    swapped = send(lax.dynamic_slice(left, ((1 - core) * rows, 0), (rows, 2 * depth)), core=1)
    mine = jnp.stack([left_part(left, core, x_lo), left_part(swapped, 0, x_lo)])
    near = lax.all_gather(mine, AXES, axis=0, axis_index_groups=PLANES)

    by_y = gathered(send(left_part(left, core, 1 - x_lo), dx=1), "dy", "dz")
    by_z = gathered(send(left_part(swapped, 0, 1 - x_lo), dx=1), "dz", "dy")

    own = lax.dynamic_slice(right, (x_lo * depth, 0), (depth, columns))
    other = send(lax.dynamic_slice(right, ((1 - x_lo) * depth, 0), (depth, columns)), dx=1)
    rights = (*split_right(own, send(own, core=1)), *split_right(other, send(other, core=1)))

    flag = same.reshape(1)
    first, second = near_products(flag, near, rights)
    near_sums = send_if(first, (0, 1), (1, 0)), send_if(second, None, (1, 1)), second

    far_sums = []
    for positions in (EARLY, LATE):
        sources = (
            [by_y(dz, dy) for dz, dy in positions],
            [by_z(dy, dz) for dz, dy in positions],
        )
        first, second = far_products(flag, sources, rights)
        far_sums.append((send_if(first, (1, 0), (0, 1)), send_if(second, (1, 1), None), second))

    keep, give = total_of(jnp.stack([same, core, z, y]), near_sums, *far_sums)
    return join(core.reshape(1), keep, send(give, core=1)).reshape(16 * rows, columns)


def solution(mesh):
    return jax.shard_map(
        per_device,
        mesh=mesh,
        in_specs=(P("grid", "rep"), P("rep", "grid")),
        out_specs=P("rep", "grid"),
        check_vma=False,
    )
```

time: 450 us -> 237 us (0.53)
  waiting for transfers between devices: 405 us -> 130 us
  starting transfers between devices: 0.04 us -> 37.5 us
  Pallas kernels: 0 us -> 31.7 us
  matrix products: 31.4 us -> 0 us
  local copies, waits for them, and re-layouts: 0 us -> 21.6 us
    all_gather x1, waiting for transfers between devices: 369 us -> 0.01 us  [per_device(): near = lax.all_gather(mine, AXES, axis=0, axis_index_groups=PLANES)]
    ppermute x0 -> x27, waiting for transfers between devices: none -> 130 us  [the longest x21 124 us: send(): lax.ppermute(value, AXES, pairs(lambda h, c, x, z, y: (h, c ^ core, x ^ d...]
    ppermute x0 -> x27, starting transfers between devices: none -> 37.5 us  [the longest x21 21.5 us: send(): lax.ppermute(value, AXES, pairs(lambda h, c, x, z, y: (h, c ^ core, x ^ d...]
    reduce_scatter x1 -> x0, waiting for transfers between devices: 34.9 us -> none  [per_device(): lax.psum_scatter(partial_value, 'rep', scatter_dimension=0, tiled=True)]
    pallas_call x0 -> x7, Pallas kernels: none -> 31.7 us  [the longest x2 12.8 us: far_products(): pl.pallas_call(kernel, grid_spec=pltpu.PrefetchScalarGridSpec(num_scalar_...]
    dot_general x1 -> x0, matrix products: 31.4 us -> none  [per_device(): jnp.dot(lax.all_gather(panel_left, 'grid', axis=0, tiled=True), panel_rig...]
    unnamed x0 -> x42, local copies, waits for them, and re-layouts: none -> 13.6 us
    dynamic_slice x0 -> x4, local copies, waits for them, and re-layouts: none -> 4.69 us  [the longest x1 2.5 us: per_device(): lax.dynamic_slice(right, ((1 - x_lo) * depth, 0), (depth, columns))]
  transfers between devices with their start and end apart: 2 -> 28, of which waited for: 2 -> 12; matrix products, arithmetic and copies ran while one was open for 0% -> 3% of each run, Pallas kernels for 0% -> 12%
where the time goes in v3:
time: 237 us; the launch traced here: 236 us
  waiting for transfers between devices  130 us (55%)
  starting transfers between devices  37.5 us (16%)
  Pallas kernels  31.7 us (13%)
  local copies, waits for them, and re-layouts  21.6 us (9%)
  between operations  13.7 us (6%)
    ppermute x21, waiting for transfers between devices, send(): lax.ppermute(value, AXES, pairs(lambda h, c, x, z, y: (h, c ^ core, x ^ d...  124 us
    ppermute x21, starting transfers between devices, send(): lax.ppermute(value, AXES, pairs(lambda h, c, x, z, y: (h, c ^ core, x ^ d...  21.5 us
    ppermute x6, starting transfers between devices, send_if(): return lax.ppermute(value, AXES, pairs(target))  16 us
    unnamed x42, local copies, waits for them, and re-layouts  13.6 us
    pallas_call x2, Pallas kernels, far_products(): pl.pallas_call(kernel, grid_spec=pltpu.PrefetchScalarGridSpec(num_scalar_...  12.8 us
    pallas_call x1, Pallas kernels, near_products(): pl.pallas_call(near_kernel, grid_spec=pltpu.PrefetchScalarGridSpec(num_sc...  9.96 us
    ppermute x6, waiting for transfers between devices, send_if(): return lax.ppermute(value, AXES, pairs(target))  6.41 us
    pallas_call x2, Pallas kernels, split_right(): pl.pallas_call(split_kernel, grid=(steps,), in_specs=[pl.BlockSpec((depth...  5.93 us
  transfers between devices with their start and end apart: 28, of which 12 were waited for; matrix products, arithmetic and copies ran while one was open for 3% of the time, Pallas kernels for 12%

profile of v3, /device:TPU:0, one launch (start us, length us, event | category | flops | bytes accessed | tf_op | source)
XLA Modules:
  0.0 235.7 jit_solution(9945416545763479965)
XLA Ops:
  6.5 1.1 constant_dynamic-slice_fusion.3
  7.6 0.1 collective-permute-start
  7.7 1.1 fusion
  8.8 0.8 collective-permute-done
  9.6 0.8 pad_maximum_fusion.2
  10.5 0.0 all-gather.3.cloned.1.call-update
  10.5 2.5 %constant_dynamic-slice_fusion.1 = (f32[2048,256]{1,0:T(8,128)S(1)}, f32[2048,256]{1,0:T(8,128)S(1)}) fusion(f32[4096,256]{1,0:T(8,128)} %param.3, s32[]{:T(128)S(6)} %select_n.20, s32[]{:T(128)S(6)} %select_n.18), kind=kLoop, calls=%fused_computation.6 | loop fusion | bytes 8388616 | tf_op jit(solution)/shard_map/dynamic_slice | solution.py:278
  13.0 1.7 collective-permute-start.2
  14.7 0.5 collective-permute-start.6
  15.1 51.3 %collective-permute-done.6 = f32[32,2048]{1,0:T(8,128)S(1)} collective-permute-done((f32[32,2048]{1,0:T(8,128)S(1)}, f32[32,2048]{1,0:T(8,128)S(1)}, u32[]{:S(2)}, u32[]{:S(2)}) %collective-permute-start.6) | collective-permute-done | bytes 262176 | tf_op jit(solution)/shard_map/ppermute | solution.py:31
  66.4 3.1 %collective-permute-start.9 = (f32[32,2048]{1,0:T(8,128)S(1)}, f32[32,2048]{1,0:T(8,128)S(1)}, u32[]{:S(2)}, u32[]{:S(2)}) collective-permute-start(f32[32,2048]{1,0:T(8,128)S(1)} %collective-permute-done.6), channel_id=1, source_target_pairs={{0,3},{1,2},{2,1},{3,0},{4,7},{5,6},{6,5},{7,4},{8,11},{9,10},{10,... | collective-permute-start | bytes 786440 | tf_op jit(solution)/shard_map/ppermute | solution.py:31
  69.5 0.6 collective-permute-start.8
  70.1 0.4 collective-permute-start.7
  70.5 17.0 %collective-permute-done.9 = f32[32,2048]{1,0:T(8,128)S(1)} collective-permute-done((f32[32,2048]{1,0:T(8,128)S(1)}, f32[32,2048]{1,0:T(8,128)S(1)}, u32[]{:S(2)}, u32[]{:S(2)}) %collective-permute-start.9) | collective-permute-done | bytes 262176 | tf_op jit(solution)/shard_map/ppermute | solution.py:31
  87.5 5.8 %collective-permute-done.7 = f32[32,2048]{1,0:T(8,128)S(1)} collective-permute-done((f32[32,2048]{1,0:T(8,128)S(1)}, f32[32,2048]{1,0:T(8,128)S(1)}, u32[]{:S(2)}, u32[]{:S(2)}) %collective-permute-start.7) | collective-permute-done | bytes 262176 | tf_op jit(solution)/shard_map/ppermute | solution.py:31
  93.3 0.1 pad_maximum_fusion.refs_0_
  93.4 1.6 collective-permute-start.10
  95.0 1.5 collective-permute-start.12
  96.5 7.2 %collective-permute-done.12 = f32[32,2048]{1,0:T(8,128)S(1)} collective-permute-done((f32[32,2048]{1,0:T(8,128)S(1)}, f32[32,2048]{1,0:T(8,128)S(1)}, u32[]{:S(2)}, u32[]{:S(2)}) %collective-permute-start.12) | collective-permute-done | bytes 262176 | tf_op jit(solution)/shard_map/ppermute | solution.py:31
  103.7 2.2 collective-permute-start.15
  105.9 0.0 collective-permute-done.2.first
  105.9 0.8 collective-permute-start.14
  106.7 6.2 %collective-permute-done.15 = f32[32,2048]{1,0:T(8,128)S(1)} collective-permute-done((f32[32,2048]{1,0:T(8,128)S(1)}, f32[32,2048]{1,0:T(8,128)S(1)}, u32[]{:S(2)}, u32[]{:S(2)}) %collective-permute-start.15) | collective-permute-done | bytes 262176 | tf_op jit(solution)/shard_map/ppermute | solution.py:31
  112.9 14.6 %collective-permute-done.14 = f32[32,2048]{1,0:T(8,128)S(1)} collective-permute-done((f32[32,2048]{1,0:T(8,128)S(1)}, f32[32,2048]{1,0:T(8,128)S(1)}, u32[]{:S(2)}, u32[]{:S(2)}) %collective-permute-start.14) | collective-permute-done | bytes 262176 | tf_op jit(solution)/shard_map/ppermute | solution.py:31
  127.5 0.3 collective-permute-start.11
  127.8 1.2 collective-permute-done.13
  129.0 0.1 pad_maximum_fusion.1.refs_3_.refs_6_
  129.1 0.8 collective-permute-start.16
  129.9 2.8 %collective-permute-start.17 = (f32[4,32,2048]{2,1,0:T(8,128)S(1)}, f32[4,32,2048]{2,1,0:T(8,128)S(1)}, u32[]{:S(2)}, u32[]{:S(2)}) collective-permute-start(f32[4,32,2048]{2,1,0:T(8,128)S(1)} %pad_maximum_fusion.1.refs_3_.refs_6_), channel_id=1, source_target_pairs={{0,3},{1,2},{2,1},{3,0},{4,7},{5,6},{6,5},{7,4},{8,11},{9,10},{10,... | collective-permute-start | bytes 3145736 | tf_op jit(solution)/shard_map/ppermute | solution.py:31
  132.7 0.8 slice.16
  133.5 17.7 %collective-permute-done.11.refs_2_.refs_4_ = f32[4,32,2048]{2,1,0:T(8,128)S(1)} collective-permute-done((f32[4,32,2048]{2,1,0:T(8,128)S(1)}, f32[4,32,2048]{2,1,0:T(8,128)S(1)}, u32[]{:S(2)}, u32[]{:S(2)}) %collective-permute-start.11) | collective-permute-done | bytes 1048608 | tf_op jit(solution)/shard_map/ppermute | solution.py:31
  151.2 0.3 collective-permute-start.20
  151.4 0.9 slice.17
  152.3 0.3 collective-permute-done.16.refs_4_.refs_7_
  152.6 1.9 collective-permute-start.21
  154.5 0.8 slice.18
  155.3 2.4 %collective-permute-start.22 = (f32[2,32,2048]{2,1,0:T(8,128)}, f32[2,32,2048]{2,1,0:T(8,128)}, u32[]{:S(2)}, u32[]{:S(2)}) collective-permute-start(f32[2,32,2048]{2,1,0:T(8,128)} %slice.18), channel_id=1, source_target_pairs={{0,3},{1,2},{2,1},{3,0},{4,7},{5,6},{6,5},{7,4},{8,11},{9,10},{10,... | collective-permute-start | bytes 1572872 | tf_op jit(solution)/shard_map/ppermute | solution.py:31
  157.8 0.8 slice.19
  158.6 1.3 copy-done.19
  159.9 0.6 collective-permute-start.23
  160.5 1.6 copy-done.1
  162.1 1.6 copy-done.20
  163.7 1.0 shard_map.28
  164.8 4.9 %shard_map.29 = (bf16[2,2048,256]{2,1,0:T(8,128)(2,1)S(1)}, bf16[2,2048,256]{2,1,0:T(8,128)(2,1)S(1)}) custom-call(f32[2048,256]{1,0:T(8,128)} %collective-permute-done.2.first, f32[2048,256]{1,0:T(8,128)} %collective-permute-done.3.second), custom_call_target="tpu_custom_call" | custom-call | bytes 8388608 | tf_op jit(solution)/shard_map/pallas_call | solution.py:67
  169.7 1.4 copy-done.6
  171.1 1.3 copy-done.8
  172.5 6.6 %shard_map.32 = (f32[7,32,256]{2,1,0:T(8,128)}, f32[7,32,256]{2,1,0:T(8,128)}) custom-call(s32[1]{0:T(128)} %bitcast.1.same, f32[4,32,2048]{2,1,0:T(8,128)S(1)} %pad_maximum_fusion.refs_0_, f32[4,32,2048]{2,1,0:T(8,128)S(1)} %collective-permute-done.10.refs_1_, f32[2,32,2048]{2,1,0:T(8,128)} %collective-permute-done.20.refs_2_, ...), custom_call_target="tpu_custom_call" | custom-call | flops 2818572288 | bytes 12582912 | tf_op jit(solution)/shard_map/pallas_call | solution.py:166
  179.1 3.0 %collective-permute-start.24 = (f32[7,32,256]{2,1,0:T(8,128)}, f32[7,32,256]{2,1,0:T(8,128)}, u32[]{:S(2)}, u32[]{:S(2)}) collective-permute-start(f32[7,32,256]{2,1,0:T(8,128)} %get-tuple-element.25), channel_id=1, source_target_pairs={{0,64},{1,65},{2,66},{3,67},{4,68},{5,69},{6,70},{7,71},{8,72},{9,... | collective-permute-start | bytes 688136 | tf_op jit(solution)/shard_map/ppermute | solution.py:41
  182.1 1.6 copy-done.3
  183.7 1.6 copy-done.5
  185.3 1.6 copy-done.7
  186.9 1.6 copy-done.9
  188.5 10.0 %shard_map.30 = (f32[16,32,256]{2,1,0:T(8,128)}, f32[16,32,256]{2,1,0:T(8,128)}) custom-call(s32[1]{0:T(128)} %bitcast.1.same, f32[16,2,32,2048]{3,2,1,0:T(8,128)} %bitcast.26, bf16[2,2048,256]{2,1,0:T(8,128)(2,1)S(1)} %copy-done.3, bf16[2,2048,256]{2,1,0:T(8,128)(2,1)S(1)} %copy-done.5, bf16[2,2048,256]{2,1,0:T(8,128)(2,1)S(1)} %copy-done.7, ...), custom_call_target="tpu_custom_call" | custom-call | flops 6442450944 | bytes 20971520 | tf_op jit(solution)/shard_map/pallas_call | solution.py:111
  198.4 1.5 collective-permute-start.5
  199.9 6.1 %shard_map.31 = (f32[9,32,256]{2,1,0:T(8,128)}, f32[9,32,256]{2,1,0:T(8,128)S(1)}) custom-call(s32[1]{0:T(128)} %bitcast.1.same, f32[4,32,2048]{2,1,0:T(8,128)S(1)} %pad_maximum_fusion.refs_0_, f32[4,32,2048]{2,1,0:T(8,128)S(1)} %collective-permute-done.10.refs_1_, f32[4,32,2048]{2,1,0:T(8,128)S(1)} %copy-done.12, ...), custom_call_target="tpu_custom_call" | custom-call | flops 3623878656 | bytes 12582912 | tf_op jit(solution)/shard_map/pallas_call | solution.py:166
  206.1 4.5 %collective-permute-start.18 = (f32[9,32,256]{2,1,0:T(8,128)}, f32[9,32,256]{2,1,0:T(8,128)S(1)}, u32[]{:S(2)}, u32[]{:S(2)}) collective-permute-start(f32[9,32,256]{2,1,0:T(8,128)} %get-tuple-element.23), channel_id=1, source_target_pairs={{0,64},{1,65},{2,66},{3,67},{4,68},{5,69},{6,70},{7,71},{8,72},{9,... | collective-permute-start | bytes 884744 | tf_op jit(solution)/shard_map/ppermute | solution.py:41
  210.6 4.0 %collective-permute-start.19 = (f32[9,32,256]{2,1,0:T(8,128)S(1)}, f32[9,32,256]{2,1,0:T(8,128)S(1)}, u32[]{:S(2)}, u32[]{:S(2)}) collective-permute-start(f32[9,32,256]{2,1,0:T(8,128)S(1)} %get-tuple-element.24.early_own), channel_id=1, source_target_pairs={{0,80},{1,81},{2,82},{3,83},{4,84},{5,85},{6,86},{7,87},{8,88},{9,... | collective-permute-start | bytes 884744 | tf_op jit(solution)/shard_map/ppermute | solution.py:41
  214.6 3.0 %collective-permute-start.25 = (f32[7,32,256]{2,1,0:T(8,128)}, f32[7,32,256]{2,1,0:T(8,128)S(1)}, u32[]{:S(2)}, u32[]{:S(2)}) collective-permute-start(f32[7,32,256]{2,1,0:T(8,128)} %get-tuple-element.26.late_own), channel_id=1, source_target_pairs={{0,80},{1,81},{2,82},{3,83},{4,84},{5,85},{6,86},{7,87},{8,88},{9,... | collective-permute-start | bytes 688136 | tf_op jit(solution)/shard_map/ppermute | solution.py:41
  217.6 0.1 pad_add_fusion.place
  217.7 6.4 %collective-permute-done.25.late_b = f32[7,32,256]{2,1,0:T(8,128)S(1)} collective-permute-done((f32[7,32,256]{2,1,0:T(8,128)}, f32[7,32,256]{2,1,0:T(8,128)S(1)}, u32[]{:S(2)}, u32[]{:S(2)}) %collective-permute-start.25) | collective-permute-done | bytes 229408 | tf_op jit(solution)/shard_map/ppermute | solution.py:41
  224.1 2.3 shard_map.33
  226.4 0.1 collective-permute-start.26
  226.5 1.5 collective-permute-done.26.given
  228.0 0.8 shard_map.34
  (54 shorter events, 0.1 us)
Async XLA Ops:
  6.5 175.6 %all-gather.3.cloned.1.call-start = ((), (), s32[]{:S(2)}) async-start(), calls=%async_computation | async-start | bytes 8912896 | tf_op jit(solution)/shard_map/all_gather | solution.py:272
  7.6 2.0 collective-permute-start
  13.0 116.1 %copy-start = (f32[2048,256]{1,0:T(8,128)}, f32[2048,256]{1,0:T(8,128)S(1)}, u32[]{:S(2)}) copy-start(f32[2048,256]{1,0:T(8,128)S(1)} %get-tuple-element.30.first) | copy-start | bytes 6291460
  13.0 92.9 %collective-permute-start.2 = (f32[2048,256]{1,0:T(8,128)S(1)}, f32[2048,256]{1,0:T(8,128)}, u32[]{:S(2)}, u32[]{:S(2)}) collective-permute-start(f32[2048,256]{1,0:T(8,128)S(1)} %get-tuple-element.29), channel_id=1, source_target_pairs={{0,16},{1,17},{2,18},{3,19},{4,20},{5,21},{6,22},{7,23},{8,24},{9,... | collective-permute-start | bytes 6291464 | tf_op jit(solution)/shard_map/ppermute | solution.py:31
  14.7 51.7 %collective-permute-start.6 = (f32[32,2048]{1,0:T(8,128)S(1)}, f32[32,2048]{1,0:T(8,128)S(1)}, u32[]{:S(2)}, u32[]{:S(2)}) collective-permute-start(f32[32,2048]{1,0:T(8,128)S(1)} %get-tuple-element.31), channel_id=1, source_target_pairs={{0,16},{1,17},{2,18},{3,19},{4,20},{5,21},{6,22},{7,23},{8,24},{9,... | collective-permute-start | bytes 786440 | tf_op jit(solution)/shard_map/ppermute | solution.py:31
  66.4 21.1 %collective-permute-start.9 = (f32[32,2048]{1,0:T(8,128)S(1)}, f32[32,2048]{1,0:T(8,128)S(1)}, u32[]{:S(2)}, u32[]{:S(2)}) collective-permute-start(f32[32,2048]{1,0:T(8,128)S(1)} %collective-permute-done.6), channel_id=1, source_target_pairs={{0,3},{1,2},{2,1},{3,0},{4,7},{5,6},{6,5},{7,4},{8,11},{9,10},{10,... | collective-permute-start | bytes 786440 | tf_op jit(solution)/shard_map/ppermute | solution.py:31
  69.5 18.0 %collective-permute-start.8 = (f32[32,2048]{1,0:T(8,128)S(1)}, f32[32,2048]{1,0:T(8,128)S(1)}, u32[]{:S(2)}, u32[]{:S(2)}) collective-permute-start(f32[32,2048]{1,0:T(8,128)S(1)} %collective-permute-done.6), channel_id=1, source_target_pairs={{0,2},{1,3},{2,0},{3,1},{4,6},{5,7},{6,4},{7,5},{8,10},{9,11},{10,... | collective-permute-start | bytes 786440 | tf_op jit(solution)/shard_map/ppermute | solution.py:31
  70.1 23.2 %collective-permute-start.7 = (f32[32,2048]{1,0:T(8,128)S(1)}, f32[32,2048]{1,0:T(8,128)S(1)}, u32[]{:S(2)}, u32[]{:S(2)}) collective-permute-start(f32[32,2048]{1,0:T(8,128)S(1)} %collective-permute-done.6), channel_id=1, source_target_pairs={{0,1},{1,0},{2,3},{3,2},{4,5},{5,4},{6,7},{7,6},{8,9},{9,8},{10,11... | collective-permute-start | bytes 786440 | tf_op jit(solution)/shard_map/ppermute | solution.py:31
  93.4 36.5 %collective-permute-start.10 = (f32[4,32,2048]{2,1,0:T(8,128)S(1)}, f32[4,32,2048]{2,1,0:T(8,128)S(1)}, u32[]{:S(2)}, u32[]{:S(2)}) collective-permute-start(f32[4,32,2048]{2,1,0:T(8,128)S(1)} %pad_maximum_fusion.refs_0_), channel_id=1, source_target_pairs={{0,4},{1,5},{2,6},{3,7},{4,0},{5,1},{6,2},{7,3},{8,12},{9,13},{10,... | collective-permute-start | bytes 3145736 | tf_op jit(solution)/shard_map/ppermute | solution.py:31
  95.0 63.6 %collective-permute-start.1 = (f32[2048,256]{1,0:T(8,128)S(1)}, f32[2048,256]{1,0:T(8,128)S(1)}, u32[]{:S(2)}, u32[]{:S(2)}) collective-permute-start(f32[2048,256]{1,0:T(8,128)S(1)} %get-tuple-element.30.first), channel_id=1, source_target_pairs={{0,32},{1,33},{2,34},{3,35},{4,36},{5,37},{6,38},{7,39},{8,40},{9,... | collective-permute-start | bytes 6291464 | tf_op jit(solution)/shard_map/ppermute | solution.py:31
  95.0 8.7 %collective-permute-start.12 = (f32[32,2048]{1,0:T(8,128)S(1)}, f32[32,2048]{1,0:T(8,128)S(1)}, u32[]{:S(2)}, u32[]{:S(2)}) collective-permute-start(f32[32,2048]{1,0:T(8,128)S(1)} %get-tuple-element.33), channel_id=1, source_target_pairs={{0,16},{1,17},{2,18},{3,19},{4,20},{5,21},{6,22},{7,23},{8,24},{9,... | collective-permute-start | bytes 786440 | tf_op jit(solution)/shard_map/ppermute | solution.py:31
  103.7 9.1 %collective-permute-start.15 = (f32[32,2048]{1,0:T(8,128)S(1)}, f32[32,2048]{1,0:T(8,128)S(1)}, u32[]{:S(2)}, u32[]{:S(2)}) collective-permute-start(f32[32,2048]{1,0:T(8,128)S(1)} %collective-permute-done.12), channel_id=1, source_target_pairs={{0,12},{1,13},{2,14},{3,15},{4,8},{5,9},{6,10},{7,11},{8,4},{9,5},... | collective-permute-start | bytes 786440 | tf_op jit(solution)/shard_map/ppermute | solution.py:31
  105.9 58.9 %collective-permute-start.3 = (f32[2048,256]{1,0:T(8,128)}, f32[2048,256]{1,0:T(8,128)}, u32[]{:S(2)}, u32[]{:S(2)}) collective-permute-start(f32[2048,256]{1,0:T(8,128)} %collective-permute-done.2.first), channel_id=1, source_target_pairs={{0,32},{1,33},{2,34},{3,35},{4,36},{5,37},{6,38},{7,39},{8,40},{9,... | collective-permute-start | bytes 6291464 | tf_op jit(solution)/shard_map/ppermute | solution.py:31
  105.9 21.6 %collective-permute-start.14 = (f32[32,2048]{1,0:T(8,128)S(1)}, f32[32,2048]{1,0:T(8,128)S(1)}, u32[]{:S(2)}, u32[]{:S(2)}) collective-permute-start(f32[32,2048]{1,0:T(8,128)S(1)} %collective-permute-done.12), channel_id=1, source_target_pairs={{0,8},{1,9},{2,10},{3,11},{4,12},{5,13},{6,14},{7,15},{8,0},{9,1},... | collective-permute-start | bytes 786440 | tf_op jit(solution)/shard_map/ppermute | solution.py:31
  112.9 16.1 %collective-permute-start.13 = (f32[32,2048]{1,0:T(8,128)S(1)}, f32[32,2048]{1,0:T(8,128)S(1)}, u32[]{:S(2)}, u32[]{:S(2)}) collective-permute-start(f32[32,2048]{1,0:T(8,128)S(1)} %collective-permute-done.12), channel_id=1, source_target_pairs={{0,4},{1,5},{2,6},{3,7},{4,0},{5,1},{6,2},{7,3},{8,12},{9,13},{10,... | collective-permute-start | bytes 786440 | tf_op jit(solution)/shard_map/ppermute | solution.py:31
  127.5 23.6 %collective-permute-start.11 = (f32[4,32,2048]{2,1,0:T(8,128)S(1)}, f32[4,32,2048]{2,1,0:T(8,128)S(1)}, u32[]{:S(2)}, u32[]{:S(2)}) collective-permute-start(f32[4,32,2048]{2,1,0:T(8,128)S(1)} %pad_maximum_fusion.refs_0_), channel_id=1, source_target_pairs={{0,12},{1,13},{2,14},{3,15},{4,8},{5,9},{6,10},{7,11},{8,4},{9,5},... | collective-permute-start | bytes 3145736 | tf_op jit(solution)/shard_map/ppermute | solution.py:31
  129.1 23.5 %collective-permute-start.16 = (f32[4,32,2048]{2,1,0:T(8,128)S(1)}, f32[4,32,2048]{2,1,0:T(8,128)S(1)}, u32[]{:S(2)}, u32[]{:S(2)}) collective-permute-start(f32[4,32,2048]{2,1,0:T(8,128)S(1)} %pad_maximum_fusion.1.refs_3_.refs_6_), channel_id=1, source_target_pairs={{0,1},{1,0},{2,3},{3,2},{4,5},{5,4},{6,7},{7,6},{8,9},{9,8},{10,11... | collective-permute-start | bytes 3145736 | tf_op jit(solution)/shard_map/ppermute | solution.py:31
  129.9 25.5 %collective-permute-start.17 = (f32[4,32,2048]{2,1,0:T(8,128)S(1)}, f32[4,32,2048]{2,1,0:T(8,128)S(1)}, u32[]{:S(2)}, u32[]{:S(2)}) collective-permute-start(f32[4,32,2048]{2,1,0:T(8,128)S(1)} %pad_maximum_fusion.1.refs_3_.refs_6_), channel_id=1, source_target_pairs={{0,3},{1,2},{2,1},{3,0},{4,7},{5,6},{6,5},{7,4},{8,11},{9,10},{10,... | collective-permute-start | bytes 3145736 | tf_op jit(solution)/shard_map/ppermute | solution.py:31
  151.1 7.5 %copy-start.10 = (f32[4,32,2048]{2,1,0:T(8,128)}, f32[4,32,2048]{2,1,0:T(8,128)S(1)}, u32[]{:S(2)}) copy-start(f32[4,32,2048]{2,1,0:T(8,128)S(1)} %collective-permute-done.11.refs_2_.refs_4_) | copy-start | bytes 3145732
  151.2 21.3 %collective-permute-start.20 = (f32[2,32,2048]{2,1,0:T(8,128)}, f32[2,32,2048]{2,1,0:T(8,128)}, u32[]{:S(2)}, u32[]{:S(2)}) collective-permute-start(f32[2,32,2048]{2,1,0:T(8,128)} %slice.16), channel_id=1, source_target_pairs={{0,12},{1,13},{2,14},{3,15},{4,8},{5,9},{6,10},{7,11},{8,4},{9,5},... | collective-permute-start | bytes 1572872 | tf_op jit(solution)/shard_map/ppermute | solution.py:31
  152.6 6.0 %copy-start.13 = (f32[4,32,2048]{2,1,0:T(8,128)}, f32[4,32,2048]{2,1,0:T(8,128)S(1)}, u32[]{:S(2)}) copy-start(f32[4,32,2048]{2,1,0:T(8,128)S(1)} %collective-permute-done.16.refs_4_.refs_7_) | copy-start | bytes 3145732
  152.6 19.8 %collective-permute-start.21 = (f32[2,32,2048]{2,1,0:T(8,128)}, f32[2,32,2048]{2,1,0:T(8,128)}, u32[]{:S(2)}, u32[]{:S(2)}) collective-permute-start(f32[2,32,2048]{2,1,0:T(8,128)} %slice.17), channel_id=1, source_target_pairs={{0,4},{1,5},{2,6},{3,7},{4,0},{5,1},{6,2},{7,3},{8,12},{9,13},{10,... | collective-permute-start | bytes 1572872 | tf_op jit(solution)/shard_map/ppermute | solution.py:31
  155.3 3.3 %copy-start.16 = (f32[4,32,2048]{2,1,0:T(8,128)}, f32[4,32,2048]{2,1,0:T(8,128)S(1)}, u32[]{:S(2)}) copy-start(f32[4,32,2048]{2,1,0:T(8,128)S(1)} %collective-permute-done.17.refs_5_.refs_9_) | copy-start | bytes 3145732
  155.3 17.1 %collective-permute-start.22 = (f32[2,32,2048]{2,1,0:T(8,128)}, f32[2,32,2048]{2,1,0:T(8,128)}, u32[]{:S(2)}, u32[]{:S(2)}) collective-permute-start(f32[2,32,2048]{2,1,0:T(8,128)} %slice.18), channel_id=1, source_target_pairs={{0,3},{1,2},{2,1},{3,0},{4,7},{5,6},{6,5},{7,4},{8,11},{9,10},{10,... | collective-permute-start | bytes 1572872 | tf_op jit(solution)/shard_map/ppermute | solution.py:31
  158.6 1.3 copy-start.19
  159.9 12.5 %collective-permute-start.23 = (f32[2,32,2048]{2,1,0:T(8,128)}, f32[2,32,2048]{2,1,0:T(8,128)}, u32[]{:S(2)}, u32[]{:S(2)}) collective-permute-start(f32[2,32,2048]{2,1,0:T(8,128)} %slice.19), channel_id=1, source_target_pairs={{0,1},{1,0},{2,3},{3,2},{4,5},{5,4},{6,7},{7,6},{8,9},{9,8},{10,11... | collective-permute-start | bytes 1572872 | tf_op jit(solution)/shard_map/ppermute | solution.py:31
  160.5 1.6 copy-start.1
  162.1 1.6 copy-start.20
  164.7 7.7 %copy-start.2 = (bf16[2,2048,256]{2,1,0:T(8,128)(2,1)}, bf16[2,2048,256]{2,1,0:T(8,128)(2,1)S(1)}, u32[]{:S(2)}) copy-start(bf16[2,2048,256]{2,1,0:T(8,128)(2,1)S(1)} %get-tuple-element.17.own_high.refs_6_.refs_10_) | copy-start | bytes 6291460
  164.7 7.7 %copy-start.4 = (bf16[2,2048,256]{2,1,0:T(8,128)(2,1)}, bf16[2,2048,256]{2,1,0:T(8,128)(2,1)S(1)}, u32[]{:S(2)}) copy-start(bf16[2,2048,256]{2,1,0:T(8,128)(2,1)S(1)} %get-tuple-element.18.own_low.refs_7_.refs_11_) | copy-start | bytes 6291460
  164.8 7.7 %copy-start.11 = (f32[4,32,2048]{2,1,0:T(8,128)S(1)}, f32[4,32,2048]{2,1,0:T(8,128)}, u32[]{:S(2)}) copy-start(f32[4,32,2048]{2,1,0:T(8,128)} %copy-done.10) | copy-start | bytes 3145732
  164.8 7.7 %copy-start.14 = (f32[4,32,2048]{2,1,0:T(8,128)S(1)}, f32[4,32,2048]{2,1,0:T(8,128)}, u32[]{:S(2)}) copy-start(f32[4,32,2048]{2,1,0:T(8,128)} %copy-done.13) | copy-start | bytes 3145732
  164.8 7.7 %copy-start.17 = (f32[4,32,2048]{2,1,0:T(8,128)S(1)}, f32[4,32,2048]{2,1,0:T(8,128)}, u32[]{:S(2)}) copy-start(f32[4,32,2048]{2,1,0:T(8,128)} %copy-done.16) | copy-start | bytes 3145732
  169.7 1.4 copy-start.6
  171.1 1.3 copy-start.8
  179.1 35.4 %collective-permute-start.24 = (f32[7,32,256]{2,1,0:T(8,128)}, f32[7,32,256]{2,1,0:T(8,128)}, u32[]{:S(2)}, u32[]{:S(2)}) collective-permute-start(f32[7,32,256]{2,1,0:T(8,128)} %get-tuple-element.25), channel_id=1, source_target_pairs={{0,64},{1,65},{2,66},{3,67},{4,68},{5,69},{6,70},{7,71},{8,72},{9,... | collective-permute-start | bytes 688136 | tf_op jit(solution)/shard_map/ppermute | solution.py:41
  182.1 1.6 copy-start.3
  183.7 1.6 copy-start.5
  185.3 1.6 copy-start.7
  186.9 1.6 copy-start.9
  188.5 11.4 %copy-start.12 = (f32[4,32,2048]{2,1,0:T(8,128)S(1)}, f32[4,32,2048]{2,1,0:T(8,128)}, u32[]{:S(2)}) copy-start(f32[4,32,2048]{2,1,0:T(8,128)} %copy-done.10) | copy-start | bytes 3145732
  188.5 11.4 %copy-start.15 = (f32[4,32,2048]{2,1,0:T(8,128)S(1)}, f32[4,32,2048]{2,1,0:T(8,128)}, u32[]{:S(2)}) copy-start(f32[4,32,2048]{2,1,0:T(8,128)} %copy-done.13) | copy-start | bytes 3145732
  188.5 11.4 %copy-start.18 = (f32[4,32,2048]{2,1,0:T(8,128)S(1)}, f32[4,32,2048]{2,1,0:T(8,128)}, u32[]{:S(2)}) copy-start(f32[4,32,2048]{2,1,0:T(8,128)} %copy-done.16) | copy-start | bytes 3145732
  198.4 25.7 %collective-permute-start.4 = (f32[16,32,256]{2,1,0:T(8,128)}, f32[16,32,256]{2,1,0:T(8,128)}, u32[]{:S(2)}, u32[]{:S(2)}) collective-permute-start(f32[16,32,256]{2,1,0:T(8,128)} %get-tuple-element.21), channel_id=1, source_target_pairs={{0,16},{1,17},{2,18},{3,19},{4,20},{5,21},{6,22},{7,23},{8,24},{9,... | collective-permute-start | bytes 1572872 | tf_op jit(solution)/shard_map/ppermute | solution.py:41
  198.4 25.7 %collective-permute-start.5 = (f32[16,32,256]{2,1,0:T(8,128)}, f32[16,32,256]{2,1,0:T(8,128)}, u32[]{:S(2)}, u32[]{:S(2)}) collective-permute-start(f32[16,32,256]{2,1,0:T(8,128)} %get-tuple-element.22.near_own), channel_id=1, source_target_pairs={{16,64},{17,65},{18,66},{19,67},{20,68},{21,69},{22,70},{23,71},{2... | collective-permute-start | bytes 1572872 | tf_op jit(solution)/shard_map/ppermute | solution.py:41
  206.1 18.1 %collective-permute-start.18 = (f32[9,32,256]{2,1,0:T(8,128)}, f32[9,32,256]{2,1,0:T(8,128)S(1)}, u32[]{:S(2)}, u32[]{:S(2)}) collective-permute-start(f32[9,32,256]{2,1,0:T(8,128)} %get-tuple-element.23), channel_id=1, source_target_pairs={{0,64},{1,65},{2,66},{3,67},{4,68},{5,69},{6,70},{7,71},{8,72},{9,... | collective-permute-start | bytes 884744 | tf_op jit(solution)/shard_map/ppermute | solution.py:41
  210.6 13.6 %collective-permute-start.19 = (f32[9,32,256]{2,1,0:T(8,128)S(1)}, f32[9,32,256]{2,1,0:T(8,128)S(1)}, u32[]{:S(2)}, u32[]{:S(2)}) collective-permute-start(f32[9,32,256]{2,1,0:T(8,128)S(1)} %get-tuple-element.24.early_own), channel_id=1, source_target_pairs={{0,80},{1,81},{2,82},{3,83},{4,84},{5,85},{6,86},{7,87},{8,88},{9,... | collective-permute-start | bytes 884744 | tf_op jit(solution)/shard_map/ppermute | solution.py:41
  214.6 9.5 %collective-permute-start.25 = (f32[7,32,256]{2,1,0:T(8,128)}, f32[7,32,256]{2,1,0:T(8,128)S(1)}, u32[]{:S(2)}, u32[]{:S(2)}) collective-permute-start(f32[7,32,256]{2,1,0:T(8,128)} %get-tuple-element.26.late_own), channel_id=1, source_target_pairs={{0,80},{1,81},{2,82},{3,83},{4,84},{5,85},{6,86},{7,87},{8,88},{9,... | collective-permute-start | bytes 688136 | tf_op jit(solution)/shard_map/ppermute | solution.py:41
  226.4 1.6 collective-permute-start.26
Sparse Core Ops, SparseCore 0:
  10.6 84.3 all-gather.2

commit v4 on v3

--- a/solution.py
+++ b/solution.py
@@ -242,6 +242,31 @@
     )(core, kept, given)
 
 
+def cut_kernel(place, value, _, out, sem):
+    depth = out.shape[0]
+    at = pl.ds(pl.multiple_of(place[0] * depth, depth), depth)
+    copy = pltpu.make_async_copy(value.at[at], out, sem)
+    copy.start()
+    copy.wait()
+
+
+def cut_after(place, value, earlier, depth):
+    anywhere = pl.BlockSpec(memory_space=pl.ANY)
+    return pl.pallas_call(
+        cut_kernel,
+        grid_spec=pltpu.PrefetchScalarGridSpec(
+            num_scalar_prefetch=1,
+            grid=(1,),
+            in_specs=[anywhere, anywhere],
+            out_specs=anywhere,
+            scratch_shapes=[pltpu.SemaphoreType.DMA(())],
+        ),
+        out_shape=jax.ShapeDtypeStruct((depth, value.shape[1]), value.dtype),
+        compiler_params=PARAMS,
+        cost_estimate=pl.CostEstimate(flops=0, bytes_accessed=4 << 20, transcendentals=0),
+    )(place, value, earlier)
+
+
 def gathered(block, small, big):
     ring = [block] + [send(block, **{small: step}) for step in (1, 2, 3)]
     line = jnp.stack(ring)
@@ -271,11 +296,13 @@
     mine = jnp.stack([left_part(left, core, x_lo), left_part(swapped, 0, x_lo)])
     near = lax.all_gather(mine, AXES, axis=0, axis_index_groups=PLANES)
 
-    by_y = gathered(send(left_part(left, core, 1 - x_lo), dx=1), "dy", "dz")
-    by_z = gathered(send(left_part(swapped, 0, 1 - x_lo), dx=1), "dz", "dy")
+    theirs = jnp.stack([left_part(left, core, 1 - x_lo), left_part(swapped, 0, 1 - x_lo)])
+    arrived = send(theirs, dx=1)
+    by_y = gathered(arrived[0], "dy", "dz")
+    by_z = gathered(arrived[1], "dz", "dy")
 
     own = lax.dynamic_slice(right, (x_lo * depth, 0), (depth, columns))
-    other = send(lax.dynamic_slice(right, ((1 - x_lo) * depth, 0), (depth, columns)), dx=1)
+    other = send(cut_after((1 - x_lo).reshape(1), right, arrived, depth), dx=1)
     rights = (*split_right(own, send(own, core=1)), *split_right(other, send(other, core=1)))
 
     flag = same.reshape(1)

time: 237 us -> 218 us (0.920)
  waiting for transfers between devices: 130 us -> 106 us
  starting transfers between devices: 37.5 us -> 41.6 us
    ppermute x21 -> x20, waiting for transfers between devices: 124 us -> 99.4 us  [send(): lax.ppermute(value, AXES, pairs(lambda h, c, x, z, y: (h, c ^ core, x ^ d...]
    ppermute x21 -> x20, starting transfers between devices: 21.5 us -> 25.8 us  [send(): lax.ppermute(value, AXES, pairs(lambda h, c, x, z, y: (h, c ^ core, x ^ d...]
    dynamic_slice x3 -> x1, local copies, waits for them, and re-layouts: 3.61 us -> 0.14 us  [per_device(): own = lax.dynamic_slice(right, (x_lo * depth, 0), (depth, columns))]
    unnamed x42 -> x44, local copies, waits for them, and re-layouts: 13.6 us -> 15.8 us
  transfers between devices with their start and end apart: 28 -> 27, of which waited for: 12 -> 10; matrix products, arithmetic and copies ran while one was open for 3% -> 2% of each run, Pallas kernels for 12% -> 13%
where the time goes in v4:
time: 218 us; the launch traced here: 216 us
  waiting for transfers between devices  106 us (49%)
  starting transfers between devices  41.6 us (19%)
  Pallas kernels  32.1 us (15%)
  local copies, waits for them, and re-layouts  21.5 us (10%)
  between operations  13.7 us (6%)
    ppermute x20, waiting for transfers between devices, send(): lax.ppermute(value, AXES, pairs(lambda h, c, x, z, y: (h, c ^ core, x ^ d...  99.4 us
    ppermute x20, starting transfers between devices, send(): lax.ppermute(value, AXES, pairs(lambda h, c, x, z, y: (h, c ^ core, x ^ d...  25.8 us
    unnamed x44, local copies, waits for them, and re-layouts  15.8 us
    ppermute x6, starting transfers between devices, send_if(): return lax.ppermute(value, AXES, pairs(target))  15.7 us
    pallas_call x2, Pallas kernels, far_products(): pl.pallas_call(kernel, grid_spec=pltpu.PrefetchScalarGridSpec(num_scalar_...  13 us
    pallas_call x1, Pallas kernels, near_products(): pl.pallas_call(near_kernel, grid_spec=pltpu.PrefetchScalarGridSpec(num_sc...  9.95 us
    ppermute x6, waiting for transfers between devices, send_if(): return lax.ppermute(value, AXES, pairs(target))  6.56 us
    pallas_call x2, Pallas kernels, split_right(): pl.pallas_call(split_kernel, grid=(steps,), in_specs=[pl.BlockSpec((depth...  5.93 us
  transfers between devices with their start and end apart: 27, of which 10 were waited for; matrix products, arithmetic and copies ran while one was open for 2% of the time, Pallas kernels for 13%

profile of v4, /device:TPU:0, one launch (start us, length us, event | category | flops | bytes accessed | tf_op | source)
XLA Modules:
  0.0 216.0 jit_solution(8634084993256218359)
XLA Ops:
  6.5 1.1 constant_dynamic-slice_fusion.1
  7.6 0.1 collective-permute-start
  7.7 1.1 dynamic-slice_bitcast_fusion.1
  8.8 0.8 collective-permute-done
  9.6 0.8 pad_maximum_fusion.2
  10.5 0.0 all-gather.3.cloned.1.call-update
  10.5 1.7 collective-permute-start.2
  12.2 12.4 %collective-permute-done.2._ = f32[2,32,2048]{2,1,0:T(8,128)S(1)} collective-permute-done((f32[2,32,2048]{2,1,0:T(8,128)S(1)}, f32[2,32,2048]{2,1,0:T(8,128)S(1)}, u32[]{:S(2)}, u32[]{:S(2)}) %collective-permute-start.2) | collective-permute-done | bytes 524320 | tf_op jit(solution)/shard_map/ppermute | solution.py:31
  24.6 2.2 %copy-done = f32[4096,256]{1,0:T(8,128)S(1)} copy-done((f32[4096,256]{1,0:T(8,128)S(1)}, f32[4096,256]{1,0:T(8,128)}, u32[]{:S(2)}) %copy-start) | copy-done | bytes 4194328
  26.8 0.1 shard_map.29
  26.9 1.7 collective-permute-start.3
  28.6 0.1 fusion
  28.7 3.1 %collective-permute-start.9 = (f32[32,2048]{1,0:T(8,128)S(1)}, f32[32,2048]{1,0:T(8,128)S(1)}, u32[]{:S(2)}, u32[]{:S(2)}) collective-permute-start(f32[32,2048]{1,0:T(8,128)S(1)} %get-tuple-element.32), channel_id=1, source_target_pairs={{0,3},{1,2},{2,1},{3,0},{4,7},{5,6},{6,5},{7,4},{8,11},{9,10},{10,... | collective-permute-start | bytes 786440 | tf_op jit(solution)/shard_map/ppermute | solution.py:31
  31.8 0.6 collective-permute-start.8
  32.4 0.5 collective-permute-start.7
  32.9 15.0 %collective-permute-done.9 = f32[32,2048]{1,0:T(8,128)S(1)} collective-permute-done((f32[32,2048]{1,0:T(8,128)S(1)}, f32[32,2048]{1,0:T(8,128)S(1)}, u32[]{:S(2)}, u32[]{:S(2)}) %collective-permute-start.9) | collective-permute-done | bytes 262176 | tf_op jit(solution)/shard_map/ppermute | solution.py:31
  47.9 0.1 pad_maximum_fusion.refs_0_
  48.0 1.1 collective-permute-start.10
  49.1 0.1 constant_dynamic-slice_fusion.first
  49.3 0.1 collective-permute-start.1
  49.4 1.9 collective-permute-start.14
  51.3 22.8 %collective-permute-done.3.first = f32[2048,256]{1,0:T(8,128)} collective-permute-done((f32[2048,256]{1,0:T(8,128)S(1)}, f32[2048,256]{1,0:T(8,128)}, u32[]{:S(2)}, u32[]{:S(2)}) %collective-permute-start.3) | collective-permute-done | bytes 2097184 | tf_op jit(solution)/shard_map/ppermute | solution.py:31
  74.1 3.9 %collective-permute-start.13 = (f32[32,2048]{1,0:T(8,128)S(1)}, f32[32,2048]{1,0:T(8,128)S(1)}, u32[]{:S(2)}, u32[]{:S(2)}) collective-permute-start(f32[32,2048]{1,0:T(8,128)S(1)} %get-tuple-element.33), channel_id=1, source_target_pairs={{0,8},{1,9},{2,10},{3,11},{4,12},{5,13},{6,14},{7,15},{8,0},{9,1},... | collective-permute-start | bytes 786440 | tf_op jit(solution)/shard_map/ppermute | solution.py:31
  77.9 1.0 collective-permute-start.12
  79.0 25.6 %collective-permute-done.13 = f32[32,2048]{1,0:T(8,128)S(1)} collective-permute-done((f32[32,2048]{1,0:T(8,128)S(1)}, f32[32,2048]{1,0:T(8,128)S(1)}, u32[]{:S(2)}, u32[]{:S(2)}) %collective-permute-start.13) | collective-permute-done | bytes 262176 | tf_op jit(solution)/shard_map/ppermute | solution.py:31
  104.6 1.2 collective-permute-start.11
  105.8 6.6 %collective-permute-done.12 = f32[32,2048]{1,0:T(8,128)S(1)} collective-permute-done((f32[32,2048]{1,0:T(8,128)S(1)}, f32[32,2048]{1,0:T(8,128)S(1)}, u32[]{:S(2)}, u32[]{:S(2)}) %collective-permute-start.12) | collective-permute-done | bytes 262176 | tf_op jit(solution)/shard_map/ppermute | solution.py:31
  112.4 0.1 pad_maximum_fusion.1.refs_3_.refs_6_
  112.4 0.1 collective-permute-start.15
  112.5 2.4 %collective-permute-start.16 = (f32[4,32,2048]{2,1,0:T(8,128)S(1)}, f32[4,32,2048]{2,1,0:T(8,128)S(1)}, u32[]{:S(2)}, u32[]{:S(2)}) collective-permute-start(f32[4,32,2048]{2,1,0:T(8,128)S(1)} %pad_maximum_fusion.1.refs_3_.refs_6_), channel_id=1, source_target_pairs={{0,3},{1,2},{2,1},{3,0},{4,7},{5,6},{6,5},{7,4},{8,11},{9,10},{10,... | collective-permute-start | bytes 3145736 | tf_op jit(solution)/shard_map/ppermute | solution.py:31
  115.0 0.8 slice.26
  115.8 12.9 %collective-permute-done.11.refs_2_.refs_4_ = f32[4,32,2048]{2,1,0:T(8,128)S(1)} collective-permute-done((f32[4,32,2048]{2,1,0:T(8,128)S(1)}, f32[4,32,2048]{2,1,0:T(8,128)S(1)}, u32[]{:S(2)}, u32[]{:S(2)}) %collective-permute-start.11) | collective-permute-done | bytes 1048608 | tf_op jit(solution)/shard_map/ppermute | solution.py:31
  128.7 1.1 collective-permute-start.19
  129.8 0.8 slice.27
  130.6 1.8 collective-permute-done.15.refs_4_.refs_7_
  132.4 2.6 %collective-permute-start.20 = (f32[2,32,2048]{2,1,0:T(8,128)}, f32[2,32,2048]{2,1,0:T(8,128)}, u32[]{:S(2)}, u32[]{:S(2)}) collective-permute-start(f32[2,32,2048]{2,1,0:T(8,128)} %slice.27), channel_id=1, source_target_pairs={{0,4},{1,5},{2,6},{3,7},{4,0},{5,1},{6,2},{7,3},{8,12},{9,13},{10,... | collective-permute-start | bytes 1572872 | tf_op jit(solution)/shard_map/ppermute | solution.py:31
  135.0 0.8 slice.28
  135.9 2.7 %collective-permute-start.21 = (f32[2,32,2048]{2,1,0:T(8,128)}, f32[2,32,2048]{2,1,0:T(8,128)}, u32[]{:S(2)}, u32[]{:S(2)}) collective-permute-start(f32[2,32,2048]{2,1,0:T(8,128)} %slice.28), channel_id=1, source_target_pairs={{0,3},{1,2},{2,1},{3,0},{4,7},{5,6},{6,5},{7,4},{8,11},{9,10},{10,... | collective-permute-start | bytes 1572872 | tf_op jit(solution)/shard_map/ppermute | solution.py:31
  138.6 0.8 slice.29
  139.5 1.3 copy-done.20
  140.8 1.6 copy-done.2
  142.3 1.6 copy-done.21
  143.9 1.1 shard_map.28
  145.1 4.9 %shard_map.30 = (bf16[2,2048,256]{2,1,0:T(8,128)(2,1)S(1)}, bf16[2,2048,256]{2,1,0:T(8,128)(2,1)S(1)}) custom-call(f32[2048,256]{1,0:T(8,128)} %collective-permute-done.3.first, f32[2048,256]{1,0:T(8,128)} %collective-permute-done.4.second), custom_call_target="tpu_custom_call" | custom-call | bytes 8388608 | tf_op jit(solution)/shard_map/pallas_call | solution.py:67
  149.9 1.4 copy-done.7
  151.3 1.3 copy-done.9
  152.7 6.8 %shard_map.33 = (f32[7,32,256]{2,1,0:T(8,128)}, f32[7,32,256]{2,1,0:T(8,128)}) custom-call(s32[1]{0:T(128)} %bitcast.1.same, f32[4,32,2048]{2,1,0:T(8,128)S(1)} %pad_maximum_fusion.refs_0_, f32[4,32,2048]{2,1,0:T(8,128)S(1)} %collective-permute-done.10.refs_1_, f32[2,32,2048]{2,1,0:T(8,128)} %collective-permute-done.19.refs_2_, ...), custom_call_target="tpu_custom_call" | custom-call | flops 2818572288 | bytes 12582912 | tf_op jit(solution)/shard_map/pallas_call | solution.py:166
  159.5 3.0 %collective-permute-start.23 = (f32[7,32,256]{2,1,0:T(8,128)}, f32[7,32,256]{2,1,0:T(8,128)}, u32[]{:S(2)}, u32[]{:S(2)}) collective-permute-start(f32[7,32,256]{2,1,0:T(8,128)} %get-tuple-element.25), channel_id=1, source_target_pairs={{0,64},{1,65},{2,66},{3,67},{4,68},{5,69},{6,70},{7,71},{8,72},{9,... | collective-permute-start | bytes 688136 | tf_op jit(solution)/shard_map/ppermute | solution.py:41
  162.5 1.6 copy-done.4
  164.1 1.6 copy-done.6
  165.7 1.6 copy-done.8
  167.3 1.6 copy-done.10
  168.9 10.0 %shard_map.31 = (f32[16,32,256]{2,1,0:T(8,128)}, f32[16,32,256]{2,1,0:T(8,128)}) custom-call(s32[1]{0:T(128)} %bitcast.1.same, f32[16,2,32,2048]{3,2,1,0:T(8,128)} %bitcast.31, bf16[2,2048,256]{2,1,0:T(8,128)(2,1)S(1)} %copy-done.4, bf16[2,2048,256]{2,1,0:T(8,128)(2,1)S(1)} %copy-done.6, bf16[2,2048,256]{2,1,0:T(8,128)(2,1)S(1)} %copy-done.8, ...), custom_call_target="tpu_custom_call" | custom-call | flops 6442450944 | bytes 20971520 | tf_op jit(solution)/shard_map/pallas_call | solution.py:111
  178.9 1.5 collective-permute-start.6
  180.3 6.2 %shard_map.32 = (f32[9,32,256]{2,1,0:T(8,128)}, f32[9,32,256]{2,1,0:T(8,128)S(1)}) custom-call(s32[1]{0:T(128)} %bitcast.1.same, f32[4,32,2048]{2,1,0:T(8,128)S(1)} %pad_maximum_fusion.refs_0_, f32[4,32,2048]{2,1,0:T(8,128)S(1)} %collective-permute-done.10.refs_1_, f32[4,32,2048]{2,1,0:T(8,128)S(1)} %copy-done.13, ...), custom_call_target="tpu_custom_call" | custom-call | flops 3623878656 | bytes 12582912 | tf_op jit(solution)/shard_map/pallas_call | solution.py:166
  186.5 4.2 %collective-permute-start.17 = (f32[9,32,256]{2,1,0:T(8,128)}, f32[9,32,256]{2,1,0:T(8,128)S(1)}, u32[]{:S(2)}, u32[]{:S(2)}) collective-permute-start(f32[9,32,256]{2,1,0:T(8,128)} %get-tuple-element.23), channel_id=1, source_target_pairs={{0,64},{1,65},{2,66},{3,67},{4,68},{5,69},{6,70},{7,71},{8,72},{9,... | collective-permute-start | bytes 884744 | tf_op jit(solution)/shard_map/ppermute | solution.py:41
  190.7 4.3 %collective-permute-start.18 = (f32[9,32,256]{2,1,0:T(8,128)S(1)}, f32[9,32,256]{2,1,0:T(8,128)S(1)}, u32[]{:S(2)}, u32[]{:S(2)}) collective-permute-start(f32[9,32,256]{2,1,0:T(8,128)S(1)} %get-tuple-element.24.early_own), channel_id=1, source_target_pairs={{0,80},{1,81},{2,82},{3,83},{4,84},{5,85},{6,86},{7,87},{8,88},{9,... | collective-permute-start | bytes 884744 | tf_op jit(solution)/shard_map/ppermute | solution.py:41
  195.1 2.7 %collective-permute-start.24 = (f32[7,32,256]{2,1,0:T(8,128)}, f32[7,32,256]{2,1,0:T(8,128)S(1)}, u32[]{:S(2)}, u32[]{:S(2)}) collective-permute-start(f32[7,32,256]{2,1,0:T(8,128)} %get-tuple-element.26.late_own), channel_id=1, source_target_pairs={{0,80},{1,81},{2,82},{3,83},{4,84},{5,85},{6,86},{7,87},{8,88},{9,... | collective-permute-start | bytes 688136 | tf_op jit(solution)/shard_map/ppermute | solution.py:41
  197.8 0.1 pad_add_fusion.place
  197.8 6.5 %collective-permute-done.24.late_b = f32[7,32,256]{2,1,0:T(8,128)S(1)} collective-permute-done((f32[7,32,256]{2,1,0:T(8,128)}, f32[7,32,256]{2,1,0:T(8,128)S(1)}, u32[]{:S(2)}, u32[]{:S(2)}) %collective-permute-start.24) | collective-permute-done | bytes 229408 | tf_op jit(solution)/shard_map/ppermute | solution.py:41
  204.4 2.3 %shard_map.34 = (f32[8,32,256]{2,1,0:T(8,128)S(1)}, f32[8,32,256]{2,1,0:T(8,128)S(1)}) custom-call(s32[4]{0:T(128)S(1)} %pad_add_fusion.place, f32[16,32,256]{2,1,0:T(8,128)} %collective-permute-done.5.near_a, f32[16,32,256]{2,1,0:T(8,128)} %collective-permute-done.6.near_b, f32[16,32,256]{2,1,0:T(8,128)} %get-tuple-element.22.near_own, ...), custom_call_target="tpu_custom_call" | custom-call | flops 1048576 | bytes 4194304 | tf_op jit(solution)/shard_map/pallas_call | solution.py:207
  206.7 0.1 collective-permute-start.25
  206.8 1.5 collective-permute-done.25.given
  208.3 0.8 shard_map.35
  (57 shorter events, 0.2 us)
Async XLA Ops:
  6.5 156.0 %all-gather.3.cloned.1.call-start = ((), (), s32[]{:S(2)}) async-start(), calls=%async_computation | async-start | bytes 8912896 | tf_op jit(solution)/shard_map/all_gather | solution.py:297
  7.6 2.0 collective-permute-start
  10.5 14.0 %collective-permute-start.2 = (f32[2,32,2048]{2,1,0:T(8,128)S(1)}, f32[2,32,2048]{2,1,0:T(8,128)S(1)}, u32[]{:S(2)}, u32[]{:S(2)}) collective-permute-start(f32[2,32,2048]{2,1,0:T(8,128)S(1)} %pad_maximum_fusion.3), channel_id=1, source_target_pairs={{0,16},{1,17},{2,18},{3,19},{4,20},{5,21},{6,22},{7,23},{8,24},{9,... | collective-permute-start | bytes 1572872 | tf_op jit(solution)/shard_map/ppermute | solution.py:31
  24.6 2.2 %copy-start = (f32[4096,256]{1,0:T(8,128)S(1)}, f32[4096,256]{1,0:T(8,128)}, u32[]{:S(2)}) copy-start(f32[4096,256]{1,0:T(8,128)} %value.1) | copy-start | bytes 12582916
  26.9 47.1 %collective-permute-start.3 = (f32[2048,256]{1,0:T(8,128)S(1)}, f32[2048,256]{1,0:T(8,128)}, u32[]{:S(2)}, u32[]{:S(2)}) collective-permute-start(f32[2048,256]{1,0:T(8,128)S(1)} %shard_map.29), channel_id=1, source_target_pairs={{0,16},{1,17},{2,18},{3,19},{4,20},{5,21},{6,22},{7,23},{8,24},{9,... | collective-permute-start | bytes 6291464 | tf_op jit(solution)/shard_map/ppermute | solution.py:31
  28.7 19.2 %collective-permute-start.9 = (f32[32,2048]{1,0:T(8,128)S(1)}, f32[32,2048]{1,0:T(8,128)S(1)}, u32[]{:S(2)}, u32[]{:S(2)}) collective-permute-start(f32[32,2048]{1,0:T(8,128)S(1)} %get-tuple-element.32), channel_id=1, source_target_pairs={{0,3},{1,2},{2,1},{3,0},{4,7},{5,6},{6,5},{7,4},{8,11},{9,10},{10,... | collective-permute-start | bytes 786440 | tf_op jit(solution)/shard_map/ppermute | solution.py:31
  31.8 16.1 %collective-permute-start.8 = (f32[32,2048]{1,0:T(8,128)S(1)}, f32[32,2048]{1,0:T(8,128)S(1)}, u32[]{:S(2)}, u32[]{:S(2)}) collective-permute-start(f32[32,2048]{1,0:T(8,128)S(1)} %get-tuple-element.32), channel_id=1, source_target_pairs={{0,2},{1,3},{2,0},{3,1},{4,6},{5,7},{6,4},{7,5},{8,10},{9,11},{10,... | collective-permute-start | bytes 786440 | tf_op jit(solution)/shard_map/ppermute | solution.py:31
  32.4 15.5 %collective-permute-start.7 = (f32[32,2048]{1,0:T(8,128)S(1)}, f32[32,2048]{1,0:T(8,128)S(1)}, u32[]{:S(2)}, u32[]{:S(2)}) collective-permute-start(f32[32,2048]{1,0:T(8,128)S(1)} %get-tuple-element.32), channel_id=1, source_target_pairs={{0,1},{1,0},{2,3},{3,2},{4,5},{5,4},{6,7},{7,6},{8,9},{9,8},{10,11... | collective-permute-start | bytes 786440 | tf_op jit(solution)/shard_map/ppermute | solution.py:31
  48.0 64.5 %collective-permute-start.10 = (f32[4,32,2048]{2,1,0:T(8,128)S(1)}, f32[4,32,2048]{2,1,0:T(8,128)S(1)}, u32[]{:S(2)}, u32[]{:S(2)}) collective-permute-start(f32[4,32,2048]{2,1,0:T(8,128)S(1)} %pad_maximum_fusion.refs_0_), channel_id=1, source_target_pairs={{0,4},{1,5},{2,6},{3,7},{4,0},{5,1},{6,2},{7,3},{8,12},{9,13},{10,... | collective-permute-start | bytes 3145736 | tf_op jit(solution)/shard_map/ppermute | solution.py:31
  49.3 81.4 %copy-start.1 = (f32[2048,256]{1,0:T(8,128)}, f32[2048,256]{1,0:T(8,128)S(1)}, u32[]{:S(2)}) copy-start(f32[2048,256]{1,0:T(8,128)S(1)} %constant_dynamic-slice_fusion.first) | copy-start | bytes 6291460
  49.3 90.2 %collective-permute-start.1 = (f32[2048,256]{1,0:T(8,128)S(1)}, f32[2048,256]{1,0:T(8,128)S(1)}, u32[]{:S(2)}, u32[]{:S(2)}) collective-permute-start(f32[2048,256]{1,0:T(8,128)S(1)} %constant_dynamic-slice_fusion.first), channel_id=1, source_target_pairs={{0,32},{1,33},{2,34},{3,35},{4,36},{5,37},{6,38},{7,39},{8,40},{9,... | collective-permute-start | bytes 6291464 | tf_op jit(solution)/shard_map/ppermute | solution.py:31
  49.4 28.6 %collective-permute-start.14 = (f32[32,2048]{1,0:T(8,128)S(1)}, f32[32,2048]{1,0:T(8,128)S(1)}, u32[]{:S(2)}, u32[]{:S(2)}) collective-permute-start(f32[32,2048]{1,0:T(8,128)S(1)} %get-tuple-element.33), channel_id=1, source_target_pairs={{0,12},{1,13},{2,14},{3,15},{4,8},{5,9},{6,10},{7,11},{8,4},{9,5},... | collective-permute-start | bytes 786440 | tf_op jit(solution)/shard_map/ppermute | solution.py:31
  74.1 71.0 %collective-permute-start.4 = (f32[2048,256]{1,0:T(8,128)}, f32[2048,256]{1,0:T(8,128)}, u32[]{:S(2)}, u32[]{:S(2)}) collective-permute-start(f32[2048,256]{1,0:T(8,128)} %collective-permute-done.3.first), channel_id=1, source_target_pairs={{0,32},{1,33},{2,34},{3,35},{4,36},{5,37},{6,38},{7,39},{8,40},{9,... | collective-permute-start | bytes 6291464 | tf_op jit(solution)/shard_map/ppermute | solution.py:31
  74.1 30.5 %collective-permute-start.13 = (f32[32,2048]{1,0:T(8,128)S(1)}, f32[32,2048]{1,0:T(8,128)S(1)}, u32[]{:S(2)}, u32[]{:S(2)}) collective-permute-start(f32[32,2048]{1,0:T(8,128)S(1)} %get-tuple-element.33), channel_id=1, source_target_pairs={{0,8},{1,9},{2,10},{3,11},{4,12},{5,13},{6,14},{7,15},{8,0},{9,1},... | collective-permute-start | bytes 786440 | tf_op jit(solution)/shard_map/ppermute | solution.py:31
  77.9 34.4 %collective-permute-start.12 = (f32[32,2048]{1,0:T(8,128)S(1)}, f32[32,2048]{1,0:T(8,128)S(1)}, u32[]{:S(2)}, u32[]{:S(2)}) collective-permute-start(f32[32,2048]{1,0:T(8,128)S(1)} %get-tuple-element.33), channel_id=1, source_target_pairs={{0,4},{1,5},{2,6},{3,7},{4,0},{5,1},{6,2},{7,3},{8,12},{9,13},{10,... | collective-permute-start | bytes 786440 | tf_op jit(solution)/shard_map/ppermute | solution.py:31
  104.6 24.1 %collective-permute-start.11 = (f32[4,32,2048]{2,1,0:T(8,128)S(1)}, f32[4,32,2048]{2,1,0:T(8,128)S(1)}, u32[]{:S(2)}, u32[]{:S(2)}) collective-permute-start(f32[4,32,2048]{2,1,0:T(8,128)S(1)} %pad_maximum_fusion.refs_0_), channel_id=1, source_target_pairs={{0,12},{1,13},{2,14},{3,15},{4,8},{5,9},{6,10},{7,11},{8,4},{9,5},... | collective-permute-start | bytes 3145736 | tf_op jit(solution)/shard_map/ppermute | solution.py:31
  112.4 20.0 %collective-permute-start.15 = (f32[4,32,2048]{2,1,0:T(8,128)S(1)}, f32[4,32,2048]{2,1,0:T(8,128)S(1)}, u32[]{:S(2)}, u32[]{:S(2)}) collective-permute-start(f32[4,32,2048]{2,1,0:T(8,128)S(1)} %pad_maximum_fusion.1.refs_3_.refs_6_), channel_id=1, source_target_pairs={{0,1},{1,0},{2,3},{3,2},{4,5},{5,4},{6,7},{7,6},{8,9},{9,8},{10,11... | collective-permute-start | bytes 3145736 | tf_op jit(solution)/shard_map/ppermute | solution.py:31
  112.5 23.3 %collective-permute-start.16 = (f32[4,32,2048]{2,1,0:T(8,128)S(1)}, f32[4,32,2048]{2,1,0:T(8,128)S(1)}, u32[]{:S(2)}, u32[]{:S(2)}) collective-permute-start(f32[4,32,2048]{2,1,0:T(8,128)S(1)} %pad_maximum_fusion.1.refs_3_.refs_6_), channel_id=1, source_target_pairs={{0,3},{1,2},{2,1},{3,0},{4,7},{5,6},{6,5},{7,4},{8,11},{9,10},{10,... | collective-permute-start | bytes 3145736 | tf_op jit(solution)/shard_map/ppermute | solution.py:31
  128.7 10.7 %copy-start.11 = (f32[4,32,2048]{2,1,0:T(8,128)}, f32[4,32,2048]{2,1,0:T(8,128)S(1)}, u32[]{:S(2)}) copy-start(f32[4,32,2048]{2,1,0:T(8,128)S(1)} %collective-permute-done.11.refs_2_.refs_4_) | copy-start | bytes 3145732
  128.7 24.0 %collective-permute-start.19 = (f32[2,32,2048]{2,1,0:T(8,128)}, f32[2,32,2048]{2,1,0:T(8,128)}, u32[]{:S(2)}, u32[]{:S(2)}) collective-permute-start(f32[2,32,2048]{2,1,0:T(8,128)} %slice.26), channel_id=1, source_target_pairs={{0,12},{1,13},{2,14},{3,15},{4,8},{5,9},{6,10},{7,11},{8,4},{9,5},... | collective-permute-start | bytes 1572872 | tf_op jit(solution)/shard_map/ppermute | solution.py:31
  132.4 7.0 %copy-start.14 = (f32[4,32,2048]{2,1,0:T(8,128)}, f32[4,32,2048]{2,1,0:T(8,128)S(1)}, u32[]{:S(2)}) copy-start(f32[4,32,2048]{2,1,0:T(8,128)S(1)} %collective-permute-done.15.refs_4_.refs_7_) | copy-start | bytes 3145732
  132.4 20.2 %collective-permute-start.20 = (f32[2,32,2048]{2,1,0:T(8,128)}, f32[2,32,2048]{2,1,0:T(8,128)}, u32[]{:S(2)}, u32[]{:S(2)}) collective-permute-start(f32[2,32,2048]{2,1,0:T(8,128)} %slice.27), channel_id=1, source_target_pairs={{0,4},{1,5},{2,6},{3,7},{4,0},{5,1},{6,2},{7,3},{8,12},{9,13},{10,... | collective-permute-start | bytes 1572872 | tf_op jit(solution)/shard_map/ppermute | solution.py:31
  135.9 3.6 %copy-start.17 = (f32[4,32,2048]{2,1,0:T(8,128)}, f32[4,32,2048]{2,1,0:T(8,128)S(1)}, u32[]{:S(2)}) copy-start(f32[4,32,2048]{2,1,0:T(8,128)S(1)} %collective-permute-done.16.refs_5_.refs_9_) | copy-start | bytes 3145732
  135.9 16.8 %collective-permute-start.21 = (f32[2,32,2048]{2,1,0:T(8,128)}, f32[2,32,2048]{2,1,0:T(8,128)}, u32[]{:S(2)}, u32[]{:S(2)}) collective-permute-start(f32[2,32,2048]{2,1,0:T(8,128)} %slice.28), channel_id=1, source_target_pairs={{0,3},{1,2},{2,1},{3,0},{4,7},{5,6},{6,5},{7,4},{8,11},{9,10},{10,... | collective-permute-start | bytes 1572872 | tf_op jit(solution)/shard_map/ppermute | solution.py:31
  139.5 1.3 copy-start.20
  140.7 11.9 %collective-permute-start.22 = (f32[2,32,2048]{2,1,0:T(8,128)}, f32[2,32,2048]{2,1,0:T(8,128)}, u32[]{:S(2)}, u32[]{:S(2)}) collective-permute-start(f32[2,32,2048]{2,1,0:T(8,128)} %slice.29), channel_id=1, source_target_pairs={{0,1},{1,0},{2,3},{3,2},{4,5},{5,4},{6,7},{7,6},{8,9},{9,8},{10,11... | collective-permute-start | bytes 1572872 | tf_op jit(solution)/shard_map/ppermute | solution.py:31
  140.7 1.6 copy-start.2
  142.3 1.6 copy-start.21
  145.0 7.7 %copy-start.3 = (bf16[2,2048,256]{2,1,0:T(8,128)(2,1)}, bf16[2,2048,256]{2,1,0:T(8,128)(2,1)S(1)}, u32[]{:S(2)}) copy-start(bf16[2,2048,256]{2,1,0:T(8,128)(2,1)S(1)} %get-tuple-element.17.own_high.refs_6_.refs_10_) | copy-start | bytes 6291460
  145.0 7.7 %copy-start.5 = (bf16[2,2048,256]{2,1,0:T(8,128)(2,1)}, bf16[2,2048,256]{2,1,0:T(8,128)(2,1)S(1)}, u32[]{:S(2)}) copy-start(bf16[2,2048,256]{2,1,0:T(8,128)(2,1)S(1)} %get-tuple-element.18.own_low.refs_7_.refs_11_) | copy-start | bytes 6291460
  145.0 7.7 %copy-start.12 = (f32[4,32,2048]{2,1,0:T(8,128)S(1)}, f32[4,32,2048]{2,1,0:T(8,128)}, u32[]{:S(2)}) copy-start(f32[4,32,2048]{2,1,0:T(8,128)} %copy-done.11) | copy-start | bytes 3145732
  145.0 7.7 %copy-start.15 = (f32[4,32,2048]{2,1,0:T(8,128)S(1)}, f32[4,32,2048]{2,1,0:T(8,128)}, u32[]{:S(2)}) copy-start(f32[4,32,2048]{2,1,0:T(8,128)} %copy-done.14) | copy-start | bytes 3145732
  145.0 7.7 %copy-start.18 = (f32[4,32,2048]{2,1,0:T(8,128)S(1)}, f32[4,32,2048]{2,1,0:T(8,128)}, u32[]{:S(2)}) copy-start(f32[4,32,2048]{2,1,0:T(8,128)} %copy-done.17) | copy-start | bytes 3145732
  149.9 1.4 copy-start.7
  151.3 1.3 copy-start.9
  159.5 35.6 %collective-permute-start.23 = (f32[7,32,256]{2,1,0:T(8,128)}, f32[7,32,256]{2,1,0:T(8,128)}, u32[]{:S(2)}, u32[]{:S(2)}) collective-permute-start(f32[7,32,256]{2,1,0:T(8,128)} %get-tuple-element.25), channel_id=1, source_target_pairs={{0,64},{1,65},{2,66},{3,67},{4,68},{5,69},{6,70},{7,71},{8,72},{9,... | collective-permute-start | bytes 688136 | tf_op jit(solution)/shard_map/ppermute | solution.py:41
  162.5 1.6 copy-start.4
  164.1 1.6 copy-start.6
  165.7 1.6 copy-start.8
  167.3 1.6 copy-start.10
  168.9 11.4 %copy-start.13 = (f32[4,32,2048]{2,1,0:T(8,128)S(1)}, f32[4,32,2048]{2,1,0:T(8,128)}, u32[]{:S(2)}) copy-start(f32[4,32,2048]{2,1,0:T(8,128)} %copy-done.11) | copy-start | bytes 3145732
  168.9 11.4 %copy-start.16 = (f32[4,32,2048]{2,1,0:T(8,128)S(1)}, f32[4,32,2048]{2,1,0:T(8,128)}, u32[]{:S(2)}) copy-start(f32[4,32,2048]{2,1,0:T(8,128)} %copy-done.14) | copy-start | bytes 3145732
  168.9 11.4 %copy-start.19 = (f32[4,32,2048]{2,1,0:T(8,128)S(1)}, f32[4,32,2048]{2,1,0:T(8,128)}, u32[]{:S(2)}) copy-start(f32[4,32,2048]{2,1,0:T(8,128)} %copy-done.17) | copy-start | bytes 3145732
  178.8 25.6 %collective-permute-start.5 = (f32[16,32,256]{2,1,0:T(8,128)}, f32[16,32,256]{2,1,0:T(8,128)}, u32[]{:S(2)}, u32[]{:S(2)}) collective-permute-start(f32[16,32,256]{2,1,0:T(8,128)} %get-tuple-element.21), channel_id=1, source_target_pairs={{0,16},{1,17},{2,18},{3,19},{4,20},{5,21},{6,22},{7,23},{8,24},{9,... | collective-permute-start | bytes 1572872 | tf_op jit(solution)/shard_map/ppermute | solution.py:41
  178.9 25.6 %collective-permute-start.6 = (f32[16,32,256]{2,1,0:T(8,128)}, f32[16,32,256]{2,1,0:T(8,128)}, u32[]{:S(2)}, u32[]{:S(2)}) collective-permute-start(f32[16,32,256]{2,1,0:T(8,128)} %get-tuple-element.22.near_own), channel_id=1, source_target_pairs={{16,64},{17,65},{18,66},{19,67},{20,68},{21,69},{22,70},{23,71},{2... | collective-permute-start | bytes 1572872 | tf_op jit(solution)/shard_map/ppermute | solution.py:41
  186.5 17.9 %collective-permute-start.17 = (f32[9,32,256]{2,1,0:T(8,128)}, f32[9,32,256]{2,1,0:T(8,128)S(1)}, u32[]{:S(2)}, u32[]{:S(2)}) collective-permute-start(f32[9,32,256]{2,1,0:T(8,128)} %get-tuple-element.23), channel_id=1, source_target_pairs={{0,64},{1,65},{2,66},{3,67},{4,68},{5,69},{6,70},{7,71},{8,72},{9,... | collective-permute-start | bytes 884744 | tf_op jit(solution)/shard_map/ppermute | solution.py:41
  190.7 13.7 %collective-permute-start.18 = (f32[9,32,256]{2,1,0:T(8,128)S(1)}, f32[9,32,256]{2,1,0:T(8,128)S(1)}, u32[]{:S(2)}, u32[]{:S(2)}) collective-permute-start(f32[9,32,256]{2,1,0:T(8,128)S(1)} %get-tuple-element.24.early_own), channel_id=1, source_target_pairs={{0,80},{1,81},{2,82},{3,83},{4,84},{5,85},{6,86},{7,87},{8,88},{9,... | collective-permute-start | bytes 884744 | tf_op jit(solution)/shard_map/ppermute | solution.py:41
  195.1 9.3 %collective-permute-start.24 = (f32[7,32,256]{2,1,0:T(8,128)}, f32[7,32,256]{2,1,0:T(8,128)S(1)}, u32[]{:S(2)}, u32[]{:S(2)}) collective-permute-start(f32[7,32,256]{2,1,0:T(8,128)} %get-tuple-element.26.late_own), channel_id=1, source_target_pairs={{0,80},{1,81},{2,82},{3,83},{4,84},{5,85},{6,86},{7,87},{8,88},{9,... | collective-permute-start | bytes 688136 | tf_op jit(solution)/shard_map/ppermute | solution.py:41
  206.7 1.6 collective-permute-start.25
Sparse Core Ops, SparseCore 0:
  10.6 106.9 all-gather.2

commit v5 on v0

v5 whole, which is shorter than its diff:
```python
import jax
import jax.numpy as jnp
from jax import lax
from jax.experimental import pallas as pl
from jax.experimental.pallas import tpu as pltpu
from jax.sharding import PartitionSpec as P

AXES = ("rep", "grid")
VMEM_LIMIT = 40 * 1024 * 1024
PARAMS = pltpu.CompilerParams(vmem_limit_bytes=VMEM_LIMIT)
SHORT = pl.CostEstimate(flops=1, bytes_accessed=1, transcendentals=0)


def number(x_hi, core, x_lo, z, y):
    return (2 * x_hi + core) * 32 + 16 * x_lo + 4 * z + y


def pairs(target):
    found = []
    for x_hi in range(2):
        for core in range(2):
            for x_lo in range(2):
                for z in range(4):
                    for y in range(4):
                        there = target(x_hi, core, x_lo, z, y)
                        if there is not None:
                            found.append((number(x_hi, core, x_lo, z, y), number(*there)))
    return found


def send(value, dx=0, dz=0, dy=0, core=0):
    return lax.ppermute(
        value, AXES, pairs(lambda h, c, x, z, y: (h, c ^ core, x ^ dx, z ^ dz, y ^ dy))
    )


def send_if(value, same, other):
    def target(h, c, x, z, y):
        flips = same if h == x else other
        return None if flips is None else (h ^ flips[0], c, x ^ flips[1], z, y)

    return lax.ppermute(value, AXES, pairs(target))


PLANES = [
    [number(h, c, x, z, y) for z in range(4) for y in range(4)]
    for h in range(2) for c in range(2) for x in range(2)
]
EARLY = (
    [(0, 0, dy) for dy in range(4)] + [(1, dz, dy) for dy in (0, 1, 3) for dz in (0, 1)],
    [(0, 3, dy) for dy in range(4)] + [(1, dz, dy) for dy in (0, 1, 3) for dz in (2, 3)],
)
LATE = (
    [(0, 1, dy) for dy in range(4)] + [(1, dz, 2) for dz in (0, 1)],
    [(0, 2, dy) for dy in range(4)] + [(1, dz, 2) for dz in (2, 3)],
)


def halves(value):
    high = value.astype(jnp.bfloat16)
    return high, (value - high.astype(jnp.float32)).astype(jnp.bfloat16)


def products(left_high, left_low, high, low):
    total = None
    for one, two in ((left_high, high), (left_high, low), (left_low, high)):
        term = jnp.dot(one, two, preferred_element_type=jnp.float32)
        total = term if total is None else total + term
    columns = total.shape[1] // 2
    return total[:, :columns], total[:, columns:]


def near_kernel(flags, left, own, far, *rest):
    keep_first, keep_second, give, high, low = rest[-5:]
    same, core = flags[0] == 1, flags[1]
    columns = own.shape[1]

    @pl.when(pl.program_id(0) == 0)
    def _():
        high[:, :columns], low[:, :columns] = halves(own[...])
        high[:, columns:], low[:, columns:] = halves(far[...])

    block = left[...].reshape(left.shape[0] * left.shape[1], left.shape[2])
    mine, other = products(*halves(block), high[...], low[...])
    first = jnp.where(same, other, mine).reshape(keep_first.shape)
    second = jnp.where(same, mine, other).reshape(keep_first.shape)

    @pl.when(pl.program_id(0) == core)
    def _():
        keep_first[...] = first
        keep_second[...] = second

    @pl.when(pl.program_id(0) != core)
    def _():
        give[0] = first
        give[1] = second


def whole(value):
    return pl.BlockSpec(value.shape, lambda *_: (0,) * value.ndim, pipeline_mode=pl.Buffered(1))


def near_products(flags, left, own, far, earlier):
    positions, rows, depth = left.shape
    columns = own.shape[1]
    group = positions // 2
    kept = jax.ShapeDtypeStruct((group, rows, columns), jnp.float32)
    given = jax.ShapeDtypeStruct((2, group, rows, columns), jnp.float32)
    part = pltpu.VMEM((depth, 2 * columns), jnp.bfloat16)
    vmem = pl.BlockSpec(memory_space=pltpu.VMEM)
    *found, high, low = pl.pallas_call(
        near_kernel,
        grid_spec=pltpu.PrefetchScalarGridSpec(
            num_scalar_prefetch=1,
            grid=(2,),
            in_specs=[pl.BlockSpec((group, rows, depth), lambda i, flags: (i, 0, 0)), whole(own), whole(far)]
            + [pl.BlockSpec(memory_space=pl.ANY)] * len(earlier),
            out_specs=[whole(kept), whole(kept), whole(given), vmem, vmem],
        ),
        out_shape=[kept, kept, given, part, part],
        compiler_params=PARAMS,
        cost_estimate=SHORT,
    )(flags, left, own, far, *earlier)
    return found, [pltpu.with_memory_space_constraint(value, pltpu.VMEM) for value in (high, low)]


def far_products(flags, sources, rights, earlier):
    pieces = sources[0] + sources[1]
    entries = len(sources[0])
    columns = rights[0].shape[1] // 2
    rows, depth = pieces[0][0].shape[1:]
    arrays, uses = [], {}
    for array, at in pieces:
        if id(array) not in uses:
            uses[id(array)] = (len(arrays), set())
            arrays.append(array)
        uses[id(array)][1].add(at)
    specs, places = [], {}
    for array in arrays:
        slot, used = uses[id(array)]
        if len(used) == 1:
            (only,) = used
            specs.append(pl.BlockSpec((1, rows, depth), lambda i, flags, only=only: (only, 0, 0)))
            places[slot, only] = 0
        else:
            specs.append(whole(array))
            places.update({(slot, at): at for at in used})
    plan = [(uses[id(array)][0], places[uses[id(array)][0], at]) for array, at in pieces]

    def kernel(flags, *refs):
        blocks, rest = refs[: len(arrays)], refs[len(arrays) + len(earlier):]
        high, low, keep_first, keep_second, give, left_high, left_low = rest
        for place, (slot, at) in enumerate(plan):
            span = slice(place * rows, (place + 1) * rows)
            left_high[span], left_low[span] = halves(blocks[slot][at])
        mine, other = products(left_high[...], left_low[...], high[...], low[...])
        same, swap = flags[0] == 1, flags[2] == 1
        for at, value in enumerate((jnp.where(same, mine, other), jnp.where(same, other, mine))):
            zero, one = value[: entries * rows], value[entries * rows:]
            keep = keep_second if at else keep_first
            keep[...] = jnp.where(swap, one, zero).reshape(keep.shape)
            give[at] = jnp.where(swap, zero, one).reshape(keep.shape)

    kept = jax.ShapeDtypeStruct((entries, rows, columns), jnp.float32)
    given = jax.ShapeDtypeStruct((2, entries, rows, columns), jnp.float32)
    scratch = pltpu.VMEM((2 * entries * rows, depth), jnp.bfloat16)
    return pl.pallas_call(
        kernel,
        grid_spec=pltpu.PrefetchScalarGridSpec(
            num_scalar_prefetch=1,
            grid=(1,),
            in_specs=specs
            + [pl.BlockSpec(memory_space=pl.ANY)] * len(earlier)
            + [pl.BlockSpec(memory_space=pltpu.VMEM)] * 2,
            out_specs=[whole(kept), whole(kept), whole(given)],
            scratch_shapes=[scratch, scratch],
        ),
        out_shape=[kept, kept, given],
        compiler_params=PARAMS,
        cost_estimate=SHORT,
    )(flags, *arrays, *earlier, *rights)


def added(keep_first, keep_second, give):
    got = send(give, core=1)
    return keep_first + got[0], keep_second + got[1]


def total_kernel(place, near_a, near_b, near_own, early_a, early_b, early_own, late_a, late_b, late_own, out):
    same, swap, z, y = place[0] == 1, place[1] == 1, place[2], place[3]
    out[...] = near_a[...] + near_b[...] + jnp.where(same, near_own[...], 0.0)
    rows = early_a.shape[1]
    groups = ((EARLY, early_a, early_b, early_own), (LATE, late_a, late_b, late_own))
    for (zero, one), first, second, own in groups:
        for entry, ((half, dz, dy), (_, other_dz, _)) in enumerate(zip(zero, one)):
            plane = z ^ jnp.where(swap, other_dz, dz)
            at, span = (plane & 1) * 4 + (y ^ dy), slice(half * rows, (half + 1) * rows)
            out[at, span] += first[entry] + second[entry] + jnp.where(same, 0.0, own[entry])


def total_of(place, near, early, late):
    shape = jax.ShapeDtypeStruct(near[0].shape, jnp.float32)
    values = [*near, *early, *late]
    return pl.pallas_call(
        total_kernel,
        grid_spec=pltpu.PrefetchScalarGridSpec(
            num_scalar_prefetch=1,
            grid=(1,),
            in_specs=[whole(value) for value in values],
            out_specs=whole(shape),
        ),
        out_shape=shape,
        compiler_params=PARAMS,
        cost_estimate=SHORT,
    )(place, *values)


def cut_kernel(place, value, _, out, sem):
    depth = out.shape[0]
    at = pl.ds(pl.multiple_of(place[0] * depth, depth), depth)
    copy = pltpu.make_async_copy(value.at[at], out, sem)
    copy.start()
    copy.wait()


def cut_after(place, value, earlier, depth):
    anywhere = pl.BlockSpec(memory_space=pl.ANY)
    return pl.pallas_call(
        cut_kernel,
        grid_spec=pltpu.PrefetchScalarGridSpec(
            num_scalar_prefetch=1,
            grid=(1,),
            in_specs=[anywhere, anywhere],
            out_specs=anywhere,
            scratch_shapes=[pltpu.SemaphoreType.DMA(())],
        ),
        out_shape=jax.ShapeDtypeStruct((depth, value.shape[1]), value.dtype),
        compiler_params=PARAMS,
        cost_estimate=SHORT,
    )(place, value, earlier)


def rings(by_y, by_z):
    lines = [
        [block] + [send(block, **{axis: step}) for step in (1, 2, 3)]
        for block, axis in ((by_y, "dy"), (by_z, "dz"))
    ]
    first, second = lax.optimization_barrier(lines)
    return jnp.stack(first), jnp.stack(second)


def gathered(line, axis):
    one, three = send(line, **{axis: 1}), send(line, **{axis: 3})
    onward = one[:2], three[2:]
    two = send(onward[0], **{axis: 3}), send(onward[1], **{axis: 1})

    def source(far, near):
        if far == 2:
            return two[near >> 1], near & 1
        return {0: line, 1: one, 3: three}[far], near

    return source, onward


def per_device(left, right):
    rows, depth = left.shape[0], left.shape[1] // 2
    columns = right.shape[1]
    rep, grid = lax.axis_index("rep"), lax.axis_index("grid")
    core, x_hi = rep & 1, rep >> 1
    x_lo, z, y = grid >> 4, (grid >> 2) & 3, grid & 3
    same = (x_hi == x_lo).astype(jnp.int32)
    swap = core ^ (z >> 1)

    near = lax.all_gather(
        lax.dynamic_slice(left, (0, x_lo * depth), (rows, depth)), AXES, axis=0, axis_index_groups=PLANES
    )
    arrived = send(lax.dynamic_slice(left, (0, (1 - x_lo) * depth), (rows, depth)), dx=1)
    line_y, line_z = rings(arrived[: rows // 2], arrived[rows // 2:])
    (by_y, onward_y), (by_z, onward_z) = gathered(line_y, "dz"), gathered(line_z, "dy")

    own = lax.dynamic_slice(right, (x_lo * depth, 0), (depth, columns))
    other = send(cut_after((1 - x_lo).reshape(1), right, arrived, depth), dx=1)

    flags = jnp.stack([same, core, swap])
    products_of_near, rights = near_products(flags, near, own, other, [])
    first, second = added(*products_of_near)
    near_sums = send_if(first, (0, 1), (1, 0)), send_if(second, None, (1, 1)), second

    far_sums, earlier = [], []
    for groups in (EARLY, LATE):
        sources = [
            [by_z(dy, dz) if half else by_y(dz, dy) for half, dz, dy in group] for group in groups
        ]
        found = far_products(flags, sources, rights, earlier)
        first, second = added(*found)
        earlier = [near_sums[0], second]
        far_sums.append((send_if(first, (1, 0), (0, 1)), send_if(second, (1, 1), None), second))

    total = total_of(jnp.stack([same, swap, z, y]), near_sums, *far_sums)
    return total.reshape(8 * rows, columns)


def solution(mesh):
    return jax.shard_map(
        per_device,
        mesh=mesh,
        in_specs=(P("grid", "rep"), P("rep", "grid")),
        out_specs=P("rep", "grid"),
        check_vma=False,
    )
```

time: 450 us -> 194 us (0.43)
  the two profiles are of different devices: /device:TPU:0 before, /device:TPU:4 now
where the time goes in v5:
time: 194 us; the launch traced here: 193 us
  waiting for transfers between devices  110 us (57%)
  starting transfers between devices  33.1 us (17%)
  Pallas kernels  25.6 us (13%)
  between operations  13.6 us (7%)
  local copies, waits for them, and re-layouts  8.91 us (5%)
  other arithmetic  2.25 us (1%)
    ppermute x19, waiting for transfers between devices, send(): lax.ppermute(value, AXES, pairs(lambda h, c, x, z, y: (h, c ^ core, x ^ d...  50.7 us
    all_gather x1, waiting for transfers between devices, per_device(): lax.all_gather(lax.dynamic_slice(left, (0, x_lo * depth), (rows, depth)),...  38.2 us
    ppermute x19, starting transfers between devices, send(): lax.ppermute(value, AXES, pairs(lambda h, c, x, z, y: (h, c ^ core, x ^ d...  24.9 us
    ppermute x6, waiting for transfers between devices, send_if(): return lax.ppermute(value, AXES, pairs(target))  21.1 us
    pallas_call x2, Pallas kernels, far_products(): pl.pallas_call(kernel, grid_spec=pltpu.PrefetchScalarGridSpec(num_scalar_...  11.5 us
    pallas_call x1, Pallas kernels, near_products(): pl.pallas_call(near_kernel, grid_spec=pltpu.PrefetchScalarGridSpec(num_sc...  11.2 us
    ppermute x6, starting transfers between devices, send_if(): return lax.ppermute(value, AXES, pairs(target))  8.2 us
    slice x4, local copies, waits for them, and re-layouts, gathered(): onward = (one[:2], three[2:])  4.3 us
  transfers between devices with their start and end apart: 26, of which 13 were waited for; matrix products, arithmetic and copies ran while one was open for 3% of the time, Pallas kernels for 10%

profile of v5, /device:TPU:4, one launch (start us, length us, event | category | flops | bytes accessed | tf_op | source)
XLA Modules:
  0.0 193.3 jit_solution(16707729701641475666)
XLA Ops:
  6.5 2.1 %constant_dynamic-slice_fusion = (f32[64,2048]{1,0:T(8,128)S(1)}, f32[64,2048]{1,0:T(8,128)}) fusion(f32[64,4096]{1,0:T(8,128)} %param.2, s32[]{:T(128)S(6)} %select_n.8, s32[]{:T(128)S(6)} %select_n.7), kind=kLoop, calls=%fused_computation.14 | loop fusion | bytes 2097160 | tf_op jit(solution)/shard_map/dynamic_slice | solution.py:277
  8.6 0.0 all-gather.3.cloned.1.call-update
  8.6 1.3 collective-permute-start
  9.9 12.5 %collective-permute-done._ = f32[64,2048]{1,0:T(8,128)S(1)} collective-permute-done((f32[64,2048]{1,0:T(8,128)S(1)}, f32[64,2048]{1,0:T(8,128)S(1)}, u32[]{:S(2)}, u32[]{:S(2)}) %collective-permute-start) | collective-permute-done | bytes 524320 | tf_op jit(solution)/shard_map/ppermute | solution.py:32
  22.4 2.3 %copy-done = f32[4096,256]{1,0:T(8,128)S(1)} copy-done((f32[4096,256]{1,0:T(8,128)S(1)}, f32[4096,256]{1,0:T(8,128)}, u32[]{:S(2)}) %copy-start) | copy-done | bytes 4194328
  24.7 1.4 shard_map.28
  26.1 1.3 collective-permute-start.1
  27.4 1.6 collective-permute-start.5
  29.1 2.9 %collective-permute-start.6 = (f32[32,2048]{1,0:T(8,128)S(1)}, f32[32,2048]{1,0:T(8,128)S(1)}, u32[]{:S(2)}, u32[]{:S(2)}) collective-permute-start(f32[32,2048]{1,0:T(8,128)S(1)} %get-tuple-element.27), channel_id=1, source_target_pairs={{0,2},{1,3},{2,0},{3,1},{4,6},{5,7},{6,4},{7,5},{8,10},{9,11},{10,... | collective-permute-start | bytes 786440 | tf_op jit(solution)/shard_map/ppermute | solution.py:32
  31.9 0.3 collective-permute-start.7
  32.2 1.8 collective-permute-start.8
  34.1 6.6 %collective-permute-done.5 = f32[32,2048]{1,0:T(8,128)S(1)} collective-permute-done((f32[32,2048]{1,0:T(8,128)S(1)}, f32[32,2048]{1,0:T(8,128)S(1)}, u32[]{:S(2)}, u32[]{:S(2)}) %collective-permute-start.5) | collective-permute-done | bytes 262176 | tf_op jit(solution)/shard_map/ppermute | solution.py:32
  40.7 2.8 %collective-permute-start.9 = (f32[32,2048]{1,0:T(8,128)S(1)}, f32[32,2048]{1,0:T(8,128)S(1)}, u32[]{:S(2)}, u32[]{:S(2)}) collective-permute-start(f32[32,2048]{1,0:T(8,128)S(1)} %get-tuple-element.31), channel_id=1, source_target_pairs={{0,8},{1,9},{2,10},{3,11},{4,12},{5,13},{6,14},{7,15},{8,0},{9,1},... | collective-permute-start | bytes 786440 | tf_op jit(solution)/shard_map/ppermute | solution.py:32
  43.5 3.8 %collective-permute-done.6 = f32[32,2048]{1,0:T(8,128)S(1)} collective-permute-done((f32[32,2048]{1,0:T(8,128)S(1)}, f32[32,2048]{1,0:T(8,128)S(1)}, u32[]{:S(2)}, u32[]{:S(2)}) %collective-permute-start.6) | collective-permute-done | bytes 262176 | tf_op jit(solution)/shard_map/ppermute | solution.py:32
  47.3 1.8 collective-permute-start.10
  49.1 0.0 collective-permute-done.7
  49.1 13.0 %collective-permute-done.10 = f32[32,2048]{1,0:T(8,128)S(1)} collective-permute-done((f32[32,2048]{1,0:T(8,128)S(1)}, f32[32,2048]{1,0:T(8,128)S(1)}, u32[]{:S(2)}, u32[]{:S(2)}) %collective-permute-start.10) | collective-permute-done | bytes 262176 | tf_op jit(solution)/shard_map/ppermute | solution.py:32
  62.1 0.1 pad_maximum_fusion.1.refs_1_
  62.2 0.1 collective-permute-start.11
  62.3 1.6 collective-permute-start.12
  63.8 1.1 pad_maximum_fusion.refs_0_
  64.9 3.7 %collective-permute-start.13 = (f32[4,32,2048]{2,1,0:T(8,128)}, f32[4,32,2048]{2,1,0:T(8,128)}, u32[]{:S(2)}, u32[]{:S(2)}) collective-permute-start(f32[4,32,2048]{2,1,0:T(8,128)} %pad_maximum_fusion.refs_0_), channel_id=1, source_target_pairs={{0,12},{1,13},{2,14},{3,15},{4,8},{5,9},{6,10},{7,11},{8,4},{9,5},... | collective-permute-start | bytes 3145736 | tf_op jit(solution)/shard_map/ppermute | solution.py:32
  68.6 0.1 pad_add_fusion.1.flags
  68.6 0.1 constant_dynamic-slice_fusion.1.own
  68.8 0.1 collective-permute-start.17
  68.9 4.2 %collective-permute-done.1.far = f32[2048,256]{1,0:T(8,128)} collective-permute-done((f32[2048,256]{1,0:T(8,128)}, f32[2048,256]{1,0:T(8,128)}, u32[]{:S(2)}, u32[]{:S(2)}) %collective-permute-start.1) | collective-permute-done | bytes 2097184 | tf_op jit(solution)/shard_map/ppermute | solution.py:32
  73.1 38.2 %all-gather.3.cloned.1.call-done = f32[1024,2048]{1,0:T(8,128)} async-done(((f32[64,2048]{1,0:T(8,128)}), f32[1024,2048]{1,0:T(8,128)}) %all-gather.3.cloned.1.call-update) | async-done | bytes 8388624 | tf_op jit(solution)/shard_map/all_gather | solution.py:274
  111.3 11.2 %shard_map.29 = (f32[8,64,256]{2,1,0:T(8,128)S(1)}, f32[8,64,256]{2,1,0:T(8,128)S(1)}, f32[2,8,64,256]{3,2,1,0:T(8,128)S(1)}, bf16[2048,512]{1,0:T(8,128)(2,1)S(1)}, bf16[2048,512]{1,0:T(8,128)(2,1)S(1)}) custom-call(s32[3]{0:T(128)S(1)} %pad_add_fusion.1.flags, f32[16,64,2048]{2,1,0:T(8,128)} %bitcast.40, f32[2048,256]{1,0:T(8,128)S(1)} %constant_dynamic-slice_fusion.1.own, ...), custom_call_target="tpu_custom_call" | custom-call | flops 1 | bytes 1 | tf_op jit(solution)/shard_map/pallas_call | solution.py:111
  122.5 0.1 collective-permute-start.2
  122.5 0.0 collective-permute-done.11.refs_2_
  122.6 0.0 collective-permute-done.12.refs_3_
  122.6 7.0 %shard_map.30 = (f32[10,32,256]{2,1,0:T(8,128)S(1)}, f32[10,32,256]{2,1,0:T(8,128)S(1)}, f32[2,10,32,256]{3,2,1,0:T(8,128)S(1)}) custom-call(s32[3]{0:T(128)S(1)} %pad_add_fusion.1.flags, f32[4,32,2048]{2,1,0:T(8,128)} %pad_maximum_fusion.refs_0_, f32[4,32,2048]{2,1,0:T(8,128)S(1)} %pad_maximum_fusion.1.refs_1_, ...), custom_call_target="tpu_custom_call" | custom-call | flops 1 | bytes 1 | tf_op jit(solution)/shard_map/pallas_call | solution.py:167
  129.6 0.6 collective-permute-start.14
  130.2 1.1 slice.54
  131.2 0.1 collective-permute-start.18
  131.4 1.1 slice.55
  132.4 2.4 %collective-permute-start.19 = (f32[2,32,2048]{2,1,0:T(8,128)S(1)}, f32[2,32,2048]{2,1,0:T(8,128)S(1)}, u32[]{:S(2)}, u32[]{:S(2)}) collective-permute-start(f32[2,32,2048]{2,1,0:T(8,128)S(1)} %slice.55), channel_id=1, source_target_pairs={{0,12},{1,13},{2,14},{3,15},{4,8},{5,9},{6,10},{7,11},{8,4},{9,5},... | collective-permute-start | bytes 1572872 | tf_op jit(solution)/shard_map/ppermute | solution.py:32
  134.9 1.1 slice.56
  136.0 0.4 collective-permute-start.20
  136.3 1.1 slice.57
  137.4 0.0 collective-permute-done.2
  137.4 2.1 %collective-permute-start.21 = (f32[2,32,2048]{2,1,0:T(8,128)S(1)}, f32[2,32,2048]{2,1,0:T(8,128)S(1)}, u32[]{:S(2)}, u32[]{:S(2)}) collective-permute-start(f32[2,32,2048]{2,1,0:T(8,128)S(1)} %slice.57), channel_id=1, source_target_pairs={{0,1},{1,0},{2,3},{3,2},{4,5},{5,4},{6,7},{7,6},{8,9},{9,8},{10,11... | collective-permute-start | bytes 1572872 | tf_op jit(solution)/shard_map/ppermute | solution.py:32
  139.5 0.1 fusion
  139.6 0.0 collective-permute-done.14
  139.6 0.8 collective-permute-start.3
  140.4 0.1 fusion.2
  140.5 5.9 %collective-permute-done.18.refs_1_ = f32[2,32,2048]{2,1,0:T(8,128)S(1)} collective-permute-done((f32[2,32,2048]{2,1,0:T(8,128)S(1)}, f32[2,32,2048]{2,1,0:T(8,128)S(1)}, u32[]{:S(2)}, u32[]{:S(2)}) %collective-permute-start.18) | collective-permute-done | bytes 524320 | tf_op jit(solution)/shard_map/ppermute | solution.py:32
  146.4 1.2 collective-permute-done.19.refs_2_
  147.6 1.8 collective-permute-done.20.refs_3_
  149.3 1.7 collective-permute-done.21.refs_4_
  151.1 1.9 collective-permute-done.3.refs_5_.near_a
  152.9 4.5 %shard_map.31 = (f32[6,32,256]{2,1,0:T(8,128)S(1)}, f32[6,32,256]{2,1,0:T(8,128)S(1)}, f32[2,6,32,256]{3,2,1,0:T(8,128)S(1)}) custom-call(s32[3]{0:T(128)S(1)} %pad_add_fusion.1.flags, f32[4,32,2048]{2,1,0:T(8,128)} %collective-permute-done.17.refs_0_, f32[2,32,2048]{2,1,0:T(8,128)S(1)} %collective-permute-done.18.refs_1_, ...), custom_call_target="tpu_custom_call" | custom-call | flops 1 | bytes 1 | tf_op jit(solution)/shard_map/pallas_call | solution.py:167
  157.4 0.1 collective-permute-start.22
  157.5 2.4 %collective-permute-start.4 = (f32[8,64,256]{2,1,0:T(8,128)S(1)}, f32[8,64,256]{2,1,0:T(8,128)S(1)}, u32[]{:S(2)}, u32[]{:S(2)}) collective-permute-start(f32[8,64,256]{2,1,0:T(8,128)S(1)} %get-tuple-element.43.near_own), channel_id=1, source_target_pairs={{16,64},{17,65},{18,66},{19,67},{20,68},{21,69},{22,70},{23,71},{2... | collective-permute-start | bytes 1572872 | tf_op jit(solution)/shard_map/ppermute | solution.py:42
  160.0 0.7 collective-permute-start.16
  160.6 2.7 %collective-permute-start.15 = (f32[10,32,256]{2,1,0:T(8,128)S(1)}, f32[10,32,256]{2,1,0:T(8,128)S(1)}, u32[]{:S(2)}, u32[]{:S(2)}) collective-permute-start(f32[10,32,256]{2,1,0:T(8,128)S(1)} %get-tuple-element.48), channel_id=1, source_target_pairs={{0,64},{1,65},{2,66},{3,67},{4,68},{5,69},{6,70},{7,71},{8,72},{9,... | collective-permute-start | bytes 983048 | tf_op jit(solution)/shard_map/ppermute | solution.py:42
  163.4 0.7 fusion.4
  164.1 0.9 collective-permute-start.23
  165.0 0.7 collective-permute-start.24
  165.7 0.1 pad_add_fusion.place
  165.8 7.8 %collective-permute-done.15.early_a = f32[10,32,256]{2,1,0:T(8,128)S(1)} collective-permute-done((f32[10,32,256]{2,1,0:T(8,128)S(1)}, f32[10,32,256]{2,1,0:T(8,128)S(1)}, u32[]{:S(2)}, u32[]{:S(2)}) %collective-permute-start.15) | collective-permute-done | bytes 327712 | tf_op jit(solution)/shard_map/ppermute | solution.py:42
  173.6 11.4 %collective-permute-done.4.near_b = f32[8,64,256]{2,1,0:T(8,128)S(1)} collective-permute-done((f32[8,64,256]{2,1,0:T(8,128)S(1)}, f32[8,64,256]{2,1,0:T(8,128)S(1)}, u32[]{:S(2)}, u32[]{:S(2)}) %collective-permute-start.4) | collective-permute-done | bytes 524320 | tf_op jit(solution)/shard_map/ppermute | solution.py:42
  185.0 0.0 collective-permute-done.23.late_a
  185.0 1.5 shard_map.32
  (12 shorter events, 0.1 us)
Async XLA Ops:
  6.5 104.7 %all-gather.3.cloned.1.call-start = ((), (), s32[]{:S(2)}) async-start(), calls=%async_computation | async-start | bytes 8912896 | tf_op jit(solution)/shard_map/all_gather | solution.py:274
  8.6 13.7 %collective-permute-start = (f32[64,2048]{1,0:T(8,128)S(1)}, f32[64,2048]{1,0:T(8,128)S(1)}, u32[]{:S(2)}, u32[]{:S(2)}) collective-permute-start(f32[64,2048]{1,0:T(8,128)S(1)} %get-tuple-element.45), channel_id=1, source_target_pairs={{0,16},{1,17},{2,18},{3,19},{4,20},{5,21},{6,22},{7,23},{8,24},{9,... | collective-permute-start | bytes 1572872 | tf_op jit(solution)/shard_map/ppermute | solution.py:32
  22.4 2.3 %copy-start = (f32[4096,256]{1,0:T(8,128)S(1)}, f32[4096,256]{1,0:T(8,128)}, u32[]{:S(2)}) copy-start(f32[4096,256]{1,0:T(8,128)} %value.1) | copy-start | bytes 12582916
  26.1 47.0 %collective-permute-start.1 = (f32[2048,256]{1,0:T(8,128)}, f32[2048,256]{1,0:T(8,128)}, u32[]{:S(2)}, u32[]{:S(2)}) collective-permute-start(f32[2048,256]{1,0:T(8,128)} %shard_map.28), channel_id=1, source_target_pairs={{0,16},{1,17},{2,18},{3,19},{4,20},{5,21},{6,22},{7,23},{8,24},{9,... | collective-permute-start | bytes 6291464 | tf_op jit(solution)/shard_map/ppermute | solution.py:32
  27.4 13.2 %collective-permute-start.5 = (f32[32,2048]{1,0:T(8,128)S(1)}, f32[32,2048]{1,0:T(8,128)S(1)}, u32[]{:S(2)}, u32[]{:S(2)}) collective-permute-start(f32[32,2048]{1,0:T(8,128)S(1)} %get-tuple-element.27), channel_id=1, source_target_pairs={{0,1},{1,0},{2,3},{3,2},{4,5},{5,4},{6,7},{7,6},{8,9},{9,8},{10,11... | collective-permute-start | bytes 786440 | tf_op jit(solution)/shard_map/ppermute | solution.py:32
  29.1 18.2 %collective-permute-start.6 = (f32[32,2048]{1,0:T(8,128)S(1)}, f32[32,2048]{1,0:T(8,128)S(1)}, u32[]{:S(2)}, u32[]{:S(2)}) collective-permute-start(f32[32,2048]{1,0:T(8,128)S(1)} %get-tuple-element.27), channel_id=1, source_target_pairs={{0,2},{1,3},{2,0},{3,1},{4,6},{5,7},{6,4},{7,5},{8,10},{9,11},{10,... | collective-permute-start | bytes 786440 | tf_op jit(solution)/shard_map/ppermute | solution.py:32
  31.9 17.1 %collective-permute-start.7 = (f32[32,2048]{1,0:T(8,128)S(1)}, f32[32,2048]{1,0:T(8,128)S(1)}, u32[]{:S(2)}, u32[]{:S(2)}) collective-permute-start(f32[32,2048]{1,0:T(8,128)S(1)} %get-tuple-element.27), channel_id=1, source_target_pairs={{0,3},{1,2},{2,1},{3,0},{4,7},{5,6},{6,5},{7,4},{8,11},{9,10},{10,... | collective-permute-start | bytes 786440 | tf_op jit(solution)/shard_map/ppermute | solution.py:32
  32.2 16.9 %collective-permute-start.8 = (f32[32,2048]{1,0:T(8,128)S(1)}, f32[32,2048]{1,0:T(8,128)S(1)}, u32[]{:S(2)}, u32[]{:S(2)}) collective-permute-start(f32[32,2048]{1,0:T(8,128)S(1)} %get-tuple-element.31), channel_id=1, source_target_pairs={{0,4},{1,5},{2,6},{3,7},{4,0},{5,1},{6,2},{7,3},{8,12},{9,13},{10,... | collective-permute-start | bytes 786440 | tf_op jit(solution)/shard_map/ppermute | solution.py:32
  40.7 8.4 %collective-permute-start.9 = (f32[32,2048]{1,0:T(8,128)S(1)}, f32[32,2048]{1,0:T(8,128)S(1)}, u32[]{:S(2)}, u32[]{:S(2)}) collective-permute-start(f32[32,2048]{1,0:T(8,128)S(1)} %get-tuple-element.31), channel_id=1, source_target_pairs={{0,8},{1,9},{2,10},{3,11},{4,12},{5,13},{6,14},{7,15},{8,0},{9,1},... | collective-permute-start | bytes 786440 | tf_op jit(solution)/shard_map/ppermute | solution.py:32
  47.3 14.8 %collective-permute-start.10 = (f32[32,2048]{1,0:T(8,128)S(1)}, f32[32,2048]{1,0:T(8,128)S(1)}, u32[]{:S(2)}, u32[]{:S(2)}) collective-permute-start(f32[32,2048]{1,0:T(8,128)S(1)} %get-tuple-element.31), channel_id=1, source_target_pairs={{0,12},{1,13},{2,14},{3,15},{4,8},{5,9},{6,10},{7,11},{8,4},{9,5},... | collective-permute-start | bytes 786440 | tf_op jit(solution)/shard_map/ppermute | solution.py:32
  62.1 6.6 %copy-start.1 = (f32[4096,256]{1,0:T(8,128)S(1)}, f32[4096,256]{1,0:T(8,128)}, u32[]{:S(2)}) copy-start(f32[4096,256]{1,0:T(8,128)} %value.1) | copy-start | bytes 12582916
  62.2 60.4 %collective-permute-start.11 = (f32[4,32,2048]{2,1,0:T(8,128)S(1)}, f32[4,32,2048]{2,1,0:T(8,128)}, u32[]{:S(2)}, u32[]{:S(2)}) collective-permute-start(f32[4,32,2048]{2,1,0:T(8,128)S(1)} %pad_maximum_fusion.1.refs_1_), channel_id=1, source_target_pairs={{0,1},{1,0},{2,3},{3,2},{4,5},{5,4},{6,7},{7,6},{8,9},{9,8},{10,11... | collective-permute-start | bytes 3145736 | tf_op jit(solution)/shard_map/ppermute | solution.py:32
  62.3 60.3 %collective-permute-start.12 = (f32[4,32,2048]{2,1,0:T(8,128)S(1)}, f32[4,32,2048]{2,1,0:T(8,128)}, u32[]{:S(2)}, u32[]{:S(2)}) collective-permute-start(f32[4,32,2048]{2,1,0:T(8,128)S(1)} %pad_maximum_fusion.1.refs_1_), channel_id=1, source_target_pairs={{0,3},{1,2},{2,1},{3,0},{4,7},{5,6},{6,5},{7,4},{8,11},{9,10},{10,... | collective-permute-start | bytes 3145736 | tf_op jit(solution)/shard_map/ppermute | solution.py:32
  64.9 57.7 %collective-permute-start.13 = (f32[4,32,2048]{2,1,0:T(8,128)}, f32[4,32,2048]{2,1,0:T(8,128)}, u32[]{:S(2)}, u32[]{:S(2)}) collective-permute-start(f32[4,32,2048]{2,1,0:T(8,128)} %pad_maximum_fusion.refs_0_), channel_id=1, source_target_pairs={{0,12},{1,13},{2,14},{3,15},{4,8},{5,9},{6,10},{7,11},{8,4},{9,5},... | collective-permute-start | bytes 3145736 | tf_op jit(solution)/shard_map/ppermute | solution.py:32
  68.8 62.6 %collective-permute-start.17 = (f32[4,32,2048]{2,1,0:T(8,128)}, f32[4,32,2048]{2,1,0:T(8,128)}, u32[]{:S(2)}, u32[]{:S(2)}) collective-permute-start(f32[4,32,2048]{2,1,0:T(8,128)} %pad_maximum_fusion.refs_0_), channel_id=1, source_target_pairs={{0,4},{1,5},{2,6},{3,7},{4,0},{5,1},{6,2},{7,3},{8,12},{9,13},{10,... | collective-permute-start | bytes 3145736 | tf_op jit(solution)/shard_map/ppermute | solution.py:32
  122.5 14.9 %collective-permute-start.2 = (f32[2,8,64,256]{3,2,1,0:T(8,128)S(1)}, f32[2,8,64,256]{3,2,1,0:T(8,128)S(1)}, u32[]{:S(2)}, u32[]{:S(2)}) collective-permute-start(f32[2,8,64,256]{3,2,1,0:T(8,128)S(1)} %get-tuple-element.25), channel_id=1, source_target_pairs={{0,32},{1,33},{2,34},{3,35},{4,36},{5,37},{6,38},{7,39},{8,40},{9,... | collective-permute-start | bytes 3145736 | tf_op jit(solution)/shard_map/ppermute | solution.py:32
  129.6 10.0 %collective-permute-start.14 = (f32[2,10,32,256]{3,2,1,0:T(8,128)S(1)}, f32[2,10,32,256]{3,2,1,0:T(8,128)S(1)}, u32[]{:S(2)}, u32[]{:S(2)}) collective-permute-start(f32[2,10,32,256]{3,2,1,0:T(8,128)S(1)} %get-tuple-element.38), channel_id=1, source_target_pairs={{0,32},{1,33},{2,34},{3,35},{4,36},{5,37},{6,38},{7,39},{8,40},{9,... | collective-permute-start | bytes 1966088 | tf_op jit(solution)/shard_map/ppermute | solution.py:32
  131.2 15.2 %collective-permute-start.18 = (f32[2,32,2048]{2,1,0:T(8,128)S(1)}, f32[2,32,2048]{2,1,0:T(8,128)S(1)}, u32[]{:S(2)}, u32[]{:S(2)}) collective-permute-start(f32[2,32,2048]{2,1,0:T(8,128)S(1)} %slice.54), channel_id=1, source_target_pairs={{0,3},{1,2},{2,1},{3,0},{4,7},{5,6},{6,5},{7,4},{8,11},{9,10},{10,... | collective-permute-start | bytes 1572872 | tf_op jit(solution)/shard_map/ppermute | solution.py:32
  132.4 15.1 %collective-permute-start.19 = (f32[2,32,2048]{2,1,0:T(8,128)S(1)}, f32[2,32,2048]{2,1,0:T(8,128)S(1)}, u32[]{:S(2)}, u32[]{:S(2)}) collective-permute-start(f32[2,32,2048]{2,1,0:T(8,128)S(1)} %slice.55), channel_id=1, source_target_pairs={{0,12},{1,13},{2,14},{3,15},{4,8},{5,9},{6,10},{7,11},{8,4},{9,5},... | collective-permute-start | bytes 1572872 | tf_op jit(solution)/shard_map/ppermute | solution.py:32
  136.0 13.4 %collective-permute-start.20 = (f32[2,32,2048]{2,1,0:T(8,128)S(1)}, f32[2,32,2048]{2,1,0:T(8,128)S(1)}, u32[]{:S(2)}, u32[]{:S(2)}) collective-permute-start(f32[2,32,2048]{2,1,0:T(8,128)S(1)} %slice.56), channel_id=1, source_target_pairs={{0,4},{1,5},{2,6},{3,7},{4,0},{5,1},{6,2},{7,3},{8,12},{9,13},{10,... | collective-permute-start | bytes 1572872 | tf_op jit(solution)/shard_map/ppermute | solution.py:32
  137.4 13.7 %collective-permute-start.21 = (f32[2,32,2048]{2,1,0:T(8,128)S(1)}, f32[2,32,2048]{2,1,0:T(8,128)S(1)}, u32[]{:S(2)}, u32[]{:S(2)}) collective-permute-start(f32[2,32,2048]{2,1,0:T(8,128)S(1)} %slice.57), channel_id=1, source_target_pairs={{0,1},{1,0},{2,3},{3,2},{4,5},{5,4},{6,7},{7,6},{8,9},{9,8},{10,11... | collective-permute-start | bytes 1572872 | tf_op jit(solution)/shard_map/ppermute | solution.py:32
  139.6 13.3 %collective-permute-start.3 = (f32[8,64,256]{2,1,0:T(8,128)S(1)}, f32[8,64,256]{2,1,0:T(8,128)S(1)}, u32[]{:S(2)}, u32[]{:S(2)}) collective-permute-start(f32[8,64,256]{2,1,0:T(8,128)S(1)} %get-tuple-element.44), channel_id=1, source_target_pairs={{0,16},{1,17},{2,18},{3,19},{4,20},{5,21},{6,22},{7,23},{8,24},{9,... | collective-permute-start | bytes 1572872 | tf_op jit(solution)/shard_map/ppermute | solution.py:42
  157.4 6.0 %collective-permute-start.22 = (f32[2,6,32,256]{3,2,1,0:T(8,128)S(1)}, f32[2,6,32,256]{3,2,1,0:T(8,128)S(1)}, u32[]{:S(2)}, u32[]{:S(2)}) collective-permute-start(f32[2,6,32,256]{3,2,1,0:T(8,128)S(1)} %get-tuple-element.41), channel_id=1, source_target_pairs={{0,32},{1,33},{2,34},{3,35},{4,36},{5,37},{6,38},{7,39},{8,40},{9,... | collective-permute-start | bytes 1179656 | tf_op jit(solution)/shard_map/ppermute | solution.py:32
  157.5 27.4 %collective-permute-start.4 = (f32[8,64,256]{2,1,0:T(8,128)S(1)}, f32[8,64,256]{2,1,0:T(8,128)S(1)}, u32[]{:S(2)}, u32[]{:S(2)}) collective-permute-start(f32[8,64,256]{2,1,0:T(8,128)S(1)} %get-tuple-element.43.near_own), channel_id=1, source_target_pairs={{16,64},{17,65},{18,66},{19,67},{20,68},{21,69},{22,70},{23,71},{2... | collective-permute-start | bytes 1572872 | tf_op jit(solution)/shard_map/ppermute | solution.py:42
  160.0 13.6 %collective-permute-start.16 = (f32[10,32,256]{2,1,0:T(8,128)S(1)}, f32[10,32,256]{2,1,0:T(8,128)S(1)}, u32[]{:S(2)}, u32[]{:S(2)}) collective-permute-start(f32[10,32,256]{2,1,0:T(8,128)S(1)} %get-tuple-element.47.refs_6_.early_own), channel_id=1, source_target_pairs={{0,80},{1,81},{2,82},{3,83},{4,84},{5,85},{6,86},{7,87},{8,88},{9,... | collective-permute-start | bytes 983048 | tf_op jit(solution)/shard_map/ppermute | solution.py:42
  160.6 12.9 %collective-permute-start.15 = (f32[10,32,256]{2,1,0:T(8,128)S(1)}, f32[10,32,256]{2,1,0:T(8,128)S(1)}, u32[]{:S(2)}, u32[]{:S(2)}) collective-permute-start(f32[10,32,256]{2,1,0:T(8,128)S(1)} %get-tuple-element.48), channel_id=1, source_target_pairs={{0,64},{1,65},{2,66},{3,67},{4,68},{5,69},{6,70},{7,71},{8,72},{9,... | collective-permute-start | bytes 983048 | tf_op jit(solution)/shard_map/ppermute | solution.py:42
  164.1 20.8 %collective-permute-start.23 = (f32[6,32,256]{2,1,0:T(8,128)}, f32[6,32,256]{2,1,0:T(8,128)S(1)}, u32[]{:S(2)}, u32[]{:S(2)}) collective-permute-start(f32[6,32,256]{2,1,0:T(8,128)} %get-tuple-element.52), channel_id=1, source_target_pairs={{0,64},{1,65},{2,66},{3,67},{4,68},{5,69},{6,70},{7,71},{8,72},{9,... | collective-permute-start | bytes 589832 | tf_op jit(solution)/shard_map/ppermute | solution.py:42
  165.0 19.9 %collective-permute-start.24 = (f32[6,32,256]{2,1,0:T(8,128)S(1)}, f32[6,32,256]{2,1,0:T(8,128)S(1)}, u32[]{:S(2)}, u32[]{:S(2)}) collective-permute-start(f32[6,32,256]{2,1,0:T(8,128)S(1)} %get-tuple-element.51.late_own), channel_id=1, source_target_pairs={{0,80},{1,81},{2,82},{3,83},{4,84},{5,85},{6,86},{7,87},{8,88},{9,... | collective-permute-start | bytes 589832 | tf_op jit(solution)/shard_map/ppermute | solution.py:42
Sparse Core Ops, SparseCore 0:
  9.5 101.7 all-gather.2

commit v6 on v0

v6 whole, which is shorter than its diff:
```python
import jax
import jax.numpy as jnp
from jax import lax
from jax.experimental import pallas as pl
from jax.experimental.pallas import tpu as pltpu
from jax.sharding import PartitionSpec as P

AXES = ("rep", "grid")
PARAMS = pltpu.CompilerParams(vmem_limit_bytes=40 * 1024 * 1024)
SHORT = pl.CostEstimate(flops=1, bytes_accessed=1, transcendentals=0)
NEAR = (dict(), dict(dy=1), dict(dy=3), dict(dx=1))


def number(x_hi, core, x_lo, z, y):
    return (2 * x_hi + core) * 32 + 16 * x_lo + 4 * z + y


def send(value, dhi=0, core=0, dx=0, dz=0, dy=0):
    pairs = [
        (number(h, c, x, z, y), number(h ^ dhi, c ^ core, x ^ dx, z ^ dz, y ^ dy))
        for h in range(2) for c in range(2) for x in range(2) for z in range(4) for y in range(4)
    ]
    return lax.ppermute(value, AXES, pairs)


RINGS = [
    [number(h, c, x, z, y) for y in range(4)]
    for h in range(2) for c in range(2) for x in range(2) for z in range(4)
]


def halves(value):
    high = value.astype(jnp.bfloat16)
    return high, (value - high.astype(jnp.float32)).astype(jnp.bfloat16)


def whole(value):
    return pl.BlockSpec(value.shape, lambda *_: (0,) * value.ndim, pipeline_mode=pl.Buffered(1))


ANYWHERE = pl.BlockSpec(memory_space=pl.ANY)
VMEM = pl.BlockSpec(memory_space=pltpu.VMEM)


def call(kernel, scalars, values, in_specs, out_shape, out_specs, scratch=()):
    return pl.pallas_call(
        kernel,
        grid_spec=pltpu.PrefetchScalarGridSpec(
            num_scalar_prefetch=1, grid=(1,), in_specs=in_specs, out_specs=out_specs, scratch_shapes=scratch
        ),
        out_shape=out_shape,
        compiler_params=PARAMS,
        cost_estimate=SHORT,
    )(scalars, *values)


def cut_kernel(quarter, value, _, *rest):
    outs, sems = rest[:-1], rest[-1]
    depth = outs[0].shape[0]
    copies = []
    for d, out in enumerate(outs):
        at = pl.ds(pl.multiple_of((quarter[0] ^ (d + 1)) * depth, depth), depth)
        copies.append(pltpu.make_async_copy(value.at[at], out, sems.at[d]))
    for copy in copies:
        copy.start()
    for copy in copies:
        copy.wait()


def cut_after(quarter, value, earlier):
    shape = jax.ShapeDtypeStruct((value.shape[0] // 4, value.shape[1]), value.dtype)
    return call(
        cut_kernel, quarter, (value, earlier), [ANYWHERE] * 2, [shape] * 3, [ANYWHERE] * 3,
        [pltpu.SemaphoreType.DMA((3,))],
    )


def split_kernel(_, *refs):
    pieces, (high, low) = refs[:4], refs[4:]
    columns = pieces[0].shape[1]
    for d, piece in enumerate(pieces):
        at = slice(d * columns, (d + 1) * columns)
        high[:, at], low[:, at] = halves(piece[...])


def split(scalars, pieces):
    depth, columns = pieces[0].shape
    shape = pltpu.VMEM((depth, 4 * columns), jnp.bfloat16)
    found = call(split_kernel, scalars, pieces, [whole(piece) for piece in pieces], [shape] * 2, [VMEM] * 2)
    return [pltpu.with_memory_space_constraint(value, pltpu.VMEM) for value in found]


def products(swap, groups, rights, earlier):
    arrays = [array for group in groups for array in group]
    depth = arrays[0].shape[2]
    rows = sum(array.shape[0] * array.shape[1] for array in groups[0])
    columns = rights[0].shape[1] // 4

    def kernel(swap, *refs):
        blocks, rest = refs[: len(arrays)], refs[len(arrays) + len(earlier):]
        high, low, keep, give, left_high, left_low = rest
        at = 0
        for block in blocks:
            value = block[...].reshape(block.shape[0] * block.shape[1], depth)
            span = slice(at, at + value.shape[0])
            left_high[span], left_low[span] = halves(value)
            at += value.shape[0]
        swapped = swap[0] == 1
        for d in range(4):
            span = slice(d * columns, (d + 1) * columns)
            total = jnp.dot(left_high[...], high[:, span], preferred_element_type=jnp.float32)
            total += jnp.dot(left_high[...], low[:, span], preferred_element_type=jnp.float32)
            total += jnp.dot(left_low[...], high[:, span], preferred_element_type=jnp.float32)
            total = total.reshape(2, 2, rows // 2, columns)
            for part in range(2):
                zero, one = total[0, part], total[1, part]
                into = part ^ (d == 3)
                keep[d, into] = jnp.where(swapped, one, zero)
                give[d, into] = jnp.where(swapped, zero, one)

    shape = jax.ShapeDtypeStruct((4, 2, rows // 2, columns), jnp.float32)
    scratch = pltpu.VMEM((2 * rows, depth), jnp.bfloat16)
    return call(
        kernel, swap, (*arrays, *earlier, *rights),
        [whole(array) for array in arrays] + [ANYWHERE] * len(earlier) + [VMEM] * 2,
        [shape] * 2, [whole(shape)] * 2, [scratch] * 2,
    )


def sum_kernel(side, *refs):
    terms, (mine, theirs) = refs[:-2], refs[-2:]
    for out, part in ((mine, side[0]), (theirs, 1 - side[0])):
        total = terms[0][part]
        for term in terms[1:]:
            total = total + term[part]
        out[...] = total


def summed(side, terms):
    shape = jax.ShapeDtypeStruct(terms[0].shape[1:], jnp.float32)
    return call(
        sum_kernel, side, terms, [whole(term) for term in terms], [shape] * 2, [whole(shape)] * 2
    )


def join_kernel(place, one, other_one, two, other_two, out):
    out[place[0]] = one[...] + other_one[...]
    out[1 - place[0]] = two[...] + other_two[...]


def join(place, values):
    shape = jax.ShapeDtypeStruct((2, *values[0].shape), jnp.float32)
    return call(join_kernel, place, values, [whole(value) for value in values], shape, whole(shape))


def per_device(left, right):
    rows, depth = left.shape[0], left.shape[1] // 4
    columns = right.shape[1]
    rep, grid = lax.axis_index("rep"), lax.axis_index("grid")
    core, x_hi = rep & 1, rep >> 1
    x_lo, z, y = grid >> 4, (grid >> 2) & 3, grid & 3
    quarter = 2 * (x_lo ^ (y >> 1)) + (x_lo ^ (y >> 1) ^ (y & 1))
    swap = (core ^ (z >> 1)).reshape(1)
    side = (x_hi ^ x_lo).reshape(1)

    blocks = [lax.dynamic_slice(left, (0, (number ^ (3 * x_lo)) * depth), (rows, depth)) for number in (0, 1, 3, 2)]
    mine = lax.all_to_all(jnp.stack(blocks), AXES, 0, 0, tiled=True, axis_index_groups=RINGS)
    other = send(mine, dx=1, dy=2)

    planes = []
    for part in (mine, other):
        one, three = send(part, dz=1), send(part, dz=3)
        two = send(one[:2], dz=3), send(three[2:], dz=1)
        planes.append(((part,), (one,), two, (three,)))

    pieces = [lax.dynamic_slice(right, (quarter * depth, 0), (depth, columns))]
    (ready, *_) = lax.optimization_barrier((other, planes[0][1][0], planes[0][3][0]))
    for d, piece in enumerate(cut_after(quarter.reshape(1), right, ready)):
        pieces.append(send(piece, **NEAR[d + 1]))
    rights = split(swap, pieces)

    late = [*planes[0][2], *planes[1][2]]
    ends, earlier = [], [planes[1][1][0]]
    for kept, given in ((0, 3), (1, 2)):
        groups = [[array for part in planes for array in part[dz]] for dz in (kept, given)]
        keep, give = products(swap, groups, rights, earlier)
        give, *_ = lax.optimization_barrier((give, *late))
        got = send(give, core=1)
        sums = [keep[d] + got[d] for d in range(4)]
        terms = [sums[0]] + [send(sums[d], **NEAR[d]) for d in range(1, 4)]
        earlier = [keep]
        here, there = summed(side, terms)
        ends += [here, send(there, dhi=1)]

    total = join(((z & 1) ^ swap[0]).reshape(1), ends)
    return total.reshape(8 * rows, columns)


def solution(mesh):
    return jax.shard_map(
        per_device,
        mesh=mesh,
        in_specs=(P("grid", "rep"), P("rep", "grid")),
        out_specs=P("rep", "grid"),
        check_vma=False,
    )
```

time: 450 us -> 150 us (0.33)
  waiting for transfers between devices: 405 us -> 60.4 us
  matrix products: 31.4 us -> 0 us
  starting transfers between devices: 0.04 us -> 30.6 us
  Pallas kernels: 0 us -> 22.3 us
  blocking collectives: 0 us -> 19.4 us
  local copies, waits for them, and re-layouts: 0 us -> 14.2 us
  between operations: 13.4 us -> 0.13 us
    all_gather x1 -> x0, waiting for transfers between devices: 369 us -> none  [per_device(): lax.all_gather(panel_left, 'grid', axis=0, tiled=True)]
    ppermute x0 -> x22, waiting for transfers between devices: none -> 60.4 us  [send(): return lax.ppermute(value, AXES, pairs)]
    reduce_scatter x1 -> x0, waiting for transfers between devices: 34.9 us -> none  [per_device(): lax.psum_scatter(partial_value, 'rep', scatter_dimension=0, tiled=True)]
    dot_general x1 -> x0, matrix products: 31.4 us -> none  [per_device(): jnp.dot(lax.all_gather(panel_left, 'grid', axis=0, tiled=True), panel_rig...]
    ppermute x0 -> x22, starting transfers between devices: none -> 30.6 us  [send(): return lax.ppermute(value, AXES, pairs)]
    pallas_call x0 -> x7, Pallas kernels: none -> 22.3 us  [call(): pl.pallas_call(kernel, grid_spec=pltpu.PrefetchScalarGridSpec(num_scalar_...]
    all_to_all x0 -> x1, blocking collectives: none -> 19.4 us  [per_device(): lax.all_to_all(jnp.stack(blocks), AXES, 0, 0, tiled=True, axis_index_grou...]
    unnamed x0 -> x24, local copies, waits for them, and re-layouts: none -> 6.95 us
  transfers between devices with their start and end apart: 2 -> 22, of which waited for: 2 -> 13; matrix products, arithmetic and copies ran while one was open for 0% -> 6% of each run, Pallas kernels for 0% -> 14%
where the time goes in v6:
time: 150 us
  waiting for transfers between devices  60.4 us (40%)
  starting transfers between devices  30.6 us (20%)
  Pallas kernels  22.3 us (15%)
  blocking collectives  19.4 us (13%)
  local copies, waits for them, and re-layouts  14.2 us (9%)
  other arithmetic  2.61 us (2%)
    ppermute x22, waiting for transfers between devices, send(): return lax.ppermute(value, AXES, pairs)  60.4 us
    ppermute x22, starting transfers between devices, send(): return lax.ppermute(value, AXES, pairs)  30.6 us
    pallas_call x7, Pallas kernels, call(): pl.pallas_call(kernel, grid_spec=pltpu.PrefetchScalarGridSpec(num_scalar_...  22.3 us
    all_to_all x1, blocking collectives, per_device(): lax.all_to_all(jnp.stack(blocks), AXES, 0, 0, tiled=True, axis_index_grou...  19.4 us
    unnamed x24, local copies, waits for them, and re-layouts  6.95 us
    slice x4, local copies, waits for them, and re-layouts, per_device(): two = (send(one[:2], dz=3), send(three[2:], dz=1))  4.47 us
  transfers between devices with their start and end apart: 22, of which 13 were waited for; matrix products, arithmetic and copies ran while one was open for 6% of the time, Pallas kernels for 14%

profile of v6, /device:TPU:0, one launch (start us, length us, event | category | flops | bytes accessed | tf_op | source)
XLA Modules:
  0.0 149.7 jit_solution(9932667773503390551)
XLA Ops:
  0.0 1.3 dynamic-slice_bitcast_fusion.3
  1.3 0.1 pad_maximum_fusion
  1.4 19.4 %all_to_all.5.refs_0_ = f32[4,64,1024]{2,1,0:T(8,128)S(1)} all-to-all(f32[4,64,1024]{2,1,0:T(8,128)S(1)} %pad_maximum_fusion), channel_id=1, replica_groups={{0,1,2,3},{4,5,6,7},{8,9,10,11},{12,13,14,15},{16,17,18,19},{20,21,22,2..., dimensions={0} | all-to-all | bytes 2097152 | tf_op jit(solution)/shard_map/all_to_all | solution.py:167
  20.9 1.7 %collective-permute-start = (f32[4,64,1024]{2,1,0:T(8,128)S(1)}, f32[4,64,1024]{2,1,0:T(8,128)S(1)}, u32[]{:S(2)}, u32[]{:S(2)}) collective-permute-start(f32[4,64,1024]{2,1,0:T(8,128)S(1)} %all_to_all.5.refs_0_), channel_id=1, source_target_pairs={{0,18},{1,19},{2,16},{3,17},{4,22},{5,23},{6,20},{7,21},{8,26},{9,... | collective-permute-start | bytes 3145736 | tf_op jit(solution)/shard_map/ppermute | solution.py:23
  22.6 4.0 %collective-permute-start.1 = (f32[4,64,1024]{2,1,0:T(8,128)S(1)}, f32[4,64,1024]{2,1,0:T(8,128)S(1)}, u32[]{:S(2)}, u32[]{:S(2)}) collective-permute-start(f32[4,64,1024]{2,1,0:T(8,128)S(1)} %all_to_all.5.refs_0_), channel_id=1, source_target_pairs={{0,12},{1,13},{2,14},{3,15},{4,8},{5,9},{6,10},{7,11},{8,4},{9,5},... | collective-permute-start | bytes 3145736 | tf_op jit(solution)/shard_map/ppermute | solution.py:23
  26.6 0.0 collective-permute-start.4
  26.6 20.3 %collective-permute-done._.refs_1_ = f32[4,64,1024]{2,1,0:T(8,128)S(1)} collective-permute-done((f32[4,64,1024]{2,1,0:T(8,128)S(1)}, f32[4,64,1024]{2,1,0:T(8,128)S(1)}, u32[]{:S(2)}, u32[]{:S(2)}) %collective-permute-start) | collective-permute-done | bytes 1048608 | tf_op jit(solution)/shard_map/ppermute | solution.py:23
  47.0 1.1 collective-permute-done.1.refs_2_
  48.0 1.6 %collective-permute-done.4.refs_0_ = f32[4,64,1024]{2,1,0:T(8,128)} collective-permute-done((f32[4,64,1024]{2,1,0:T(8,128)S(1)}, f32[4,64,1024]{2,1,0:T(8,128)}, u32[]{:S(2)}, u32[]{:S(2)}) %collective-permute-start.4) | collective-permute-done | bytes 1048608 | tf_op jit(solution)/shard_map/ppermute | solution.py:23
  49.6 2.4 %collective-permute-start.2 = (f32[4,64,1024]{2,1,0:T(8,128)S(1)}, f32[4,64,1024]{2,1,0:T(8,128)S(1)}, u32[]{:S(2)}, u32[]{:S(2)}) collective-permute-start(f32[4,64,1024]{2,1,0:T(8,128)S(1)} %collective-permute-done._.refs_1_), channel_id=1, source_target_pairs={{0,12},{1,13},{2,14},{3,15},{4,8},{5,9},{6,10},{7,11},{8,4},{9,5},... | collective-permute-start | bytes 3145736 | tf_op jit(solution)/shard_map/ppermute | solution.py:23
  52.0 0.0 collective-permute-start.3
  52.0 2.2 %copy-done.2 = f32[4096,256]{1,0:T(8,128)S(1)} copy-done((f32[4096,256]{1,0:T(8,128)S(1)}, f32[4096,256]{1,0:T(8,128)}, u32[]{:S(2)}) %copy-start.2) | copy-done | bytes 4194328
  54.2 1.2 shard_map.28
  55.4 1.6 %collective-permute-start.5 = (f32[1024,256]{1,0:T(8,128)S(1)}, f32[1024,256]{1,0:T(8,128)S(1)}, u32[]{:S(2)}, u32[]{:S(2)}) collective-permute-start(f32[1024,256]{1,0:T(8,128)S(1)} %get-tuple-element.22), channel_id=1, source_target_pairs={{0,1},{1,0},{2,3},{3,2},{4,5},{5,4},{6,7},{7,6},{8,9},{9,8},{10,11... | collective-permute-start | bytes 3145736 | tf_op jit(solution)/shard_map/ppermute | solution.py:23
  56.9 2.1 %collective-permute-start.6 = (f32[1024,256]{1,0:T(8,128)S(1)}, f32[1024,256]{1,0:T(8,128)S(1)}, u32[]{:S(2)}, u32[]{:S(2)}) collective-permute-start(f32[1024,256]{1,0:T(8,128)S(1)} %get-tuple-element.23), channel_id=1, source_target_pairs={{0,3},{1,2},{2,1},{3,0},{4,7},{5,6},{6,5},{7,4},{8,11},{9,10},{10,... | collective-permute-start | bytes 3145736 | tf_op jit(solution)/shard_map/ppermute | solution.py:23
  59.0 0.5 collective-permute-start.7
  59.5 1.9 %slice.80 = f32[2,64,1024]{2,1,0:T(8,128)} slice(f32[4,64,1024]{2,1,0:T(8,128)} %collective-permute-done.4.refs_0_), slice={[0:2], [0:64], [0:1024]} | slice | bytes 1048576 | tf_op jit(solution)/shard_map/slice | solution.py:173
  61.4 0.9 slice.81
  62.3 12.2 %collective-permute-done.3.refs_4_.refs_1_ = f32[4,64,1024]{2,1,0:T(8,128)S(1)} collective-permute-done((f32[4,64,1024]{2,1,0:T(8,128)S(1)}, f32[4,64,1024]{2,1,0:T(8,128)S(1)}, u32[]{:S(2)}, u32[]{:S(2)}) %collective-permute-start.3) | collective-permute-done | bytes 1048608 | tf_op jit(solution)/shard_map/ppermute | solution.py:23
  74.5 0.3 collective-permute-start.8
  74.8 0.8 slice.82
  75.6 0.0 collective-permute-done.2.refs_3_
  75.6 0.0 collective-permute-start.9
  75.6 0.9 slice.83
  76.5 1.0 copy-done.6
  77.5 0.4 collective-permute-done.5.refs_1_
  78.0 1.0 copy-done.8
  79.0 2.5 %collective-permute-start.10 = (f32[2,64,1024]{2,1,0:T(8,128)}, f32[2,64,1024]{2,1,0:T(8,128)}, u32[]{:S(2)}, u32[]{:S(2)}) collective-permute-start(f32[2,64,1024]{2,1,0:T(8,128)} %slice.82), channel_id=1, source_target_pairs={{0,12},{1,13},{2,14},{3,15},{4,8},{5,9},{6,10},{7,11},{8,4},{9,5},... | collective-permute-start | bytes 1572872 | tf_op jit(solution)/shard_map/ppermute | solution.py:23
  81.5 0.0 collective-permute-done.6.refs_2_
  81.5 1.0 copy-done.10
  82.4 1.4 collective-permute-start.11
  83.9 1.4 constant_dynamic-slice_fusion.refs_0_
  85.3 0.1 copy-done.9
  85.4 0.3 copy-done.11
  85.7 2.1 %shard_map.29 = (bf16[1024,1024]{1,0:T(8,128)(2,1)S(1)}, bf16[1024,1024]{1,0:T(8,128)(2,1)S(1)}) custom-call(s32[1]{0:T(128)} %bitcast.2._.swap, f32[1024,256]{1,0:T(8,128)S(1)} %constant_dynamic-slice_fusion.refs_0_, f32[1024,256]{1,0:T(8,128)S(1)} %copy-done.9, f32[1024,256]{1,0:T(8,128)S(1)} %copy-done.11, f32[1024,256]{1,0:T(8,128)} %collective-permute-done.7.refs_3_), custom_call_target="tpu_custom_call" | custom-call | flops 1 | bytes 1 | tf_op jit(solution)/shard_map/pallas_call | solution.py:46
  87.8 6.6 %shard_map.30 = (f32[4,2,256,256]{3,2,1,0:T(8,128)S(1)}, f32[4,2,256,256]{3,2,1,0:T(8,128)S(1)}) custom-call(s32[1]{0:T(128)} %bitcast.2._.swap, f32[4,64,1024]{2,1,0:T(8,128)S(1)} %all_to_all.5.refs_0_, f32[4,64,1024]{2,1,0:T(8,128)S(1)} %collective-permute-done._.refs_1_, f32[4,64,1024]{2,1,0:T(8,128)S(1)} %copy-done.5, f32[4,64,1024]{2,1,0:T(8,128)S(1)} %copy-done.7, ...), custom_call_target="tpu_custom_call" | custom-call | flops 1 | bytes 1 | tf_op jit(solution)/shard_map/pallas_call | solution.py:46
  94.5 1.4 copy-done
  95.9 0.0 collective-permute-done.8.refs_2_
  95.9 1.9 %collective-permute-done.10.refs_4_ = f32[2,64,1024]{2,1,0:T(8,128)} collective-permute-done((f32[2,64,1024]{2,1,0:T(8,128)}, f32[2,64,1024]{2,1,0:T(8,128)}, u32[]{:S(2)}, u32[]{:S(2)}) %collective-permute-start.10) | collective-permute-done | bytes 524320 | tf_op jit(solution)/shard_map/ppermute | solution.py:23
  97.7 0.0 collective-permute-done.11.refs_5_
  97.7 0.0 collective-permute-start.12
  97.7 8.6 %shard_map.32 = (f32[4,2,256,256]{3,2,1,0:T(8,128)S(1)}, f32[4,2,256,256]{3,2,1,0:T(8,128)S(1)}) custom-call(s32[1]{0:T(128)} %bitcast.2._.swap, f32[4,64,1024]{2,1,0:T(8,128)} %collective-permute-done.4.refs_0_, f32[4,64,1024]{2,1,0:T(8,128)S(1)} %collective-permute-done.3.refs_4_.refs_1_, f32[2,64,1024]{2,1,0:T(8,128)} %collective-permute-done.8.refs_2_, ...), custom_call_target="tpu_custom_call" | custom-call | flops 1 | bytes 1 | tf_op jit(solution)/shard_map/pallas_call | solution.py:46
  106.4 0.6 collective-permute-start.17
  107.0 0.0 collective-permute-done.12
  107.0 1.2 fusion.4
  108.2 0.9 collective-permute-start.13
  109.1 2.1 %collective-permute-start.14 = (f32[2,256,256]{2,1,0:T(8,128)}, f32[2,256,256]{2,1,0:T(8,128)S(1)}, u32[]{:S(2)}, u32[]{:S(2)}) collective-permute-start(f32[2,256,256]{2,1,0:T(8,128)} %get-tuple-element.42), channel_id=1, source_target_pairs={{0,3},{1,2},{2,1},{3,0},{4,7},{5,6},{6,5},{7,4},{8,11},{9,10},{10,... | collective-permute-start | bytes 1572872 | tf_op jit(solution)/shard_map/ppermute | solution.py:23
  111.2 0.5 collective-permute-start.15
  111.7 1.3 fusion
  113.0 0.6 collective-permute-start.18
  113.6 2.1 %collective-permute-start.19 = (f32[2,256,256]{2,1,0:T(8,128)}, f32[2,256,256]{2,1,0:T(8,128)S(1)}, u32[]{:S(2)}, u32[]{:S(2)}) collective-permute-start(f32[2,256,256]{2,1,0:T(8,128)} %get-tuple-element.38), channel_id=1, source_target_pairs={{0,3},{1,2},{2,1},{3,0},{4,7},{5,6},{6,5},{7,4},{8,11},{9,10},{10,... | collective-permute-start | bytes 1572872 | tf_op jit(solution)/shard_map/ppermute | solution.py:23
  115.6 7.3 %collective-permute-done.13.refs_1_ = f32[2,256,256]{2,1,0:T(8,128)S(1)} collective-permute-done((f32[2,256,256]{2,1,0:T(8,128)S(1)}, f32[2,256,256]{2,1,0:T(8,128)S(1)}, u32[]{:S(2)}, u32[]{:S(2)}) %collective-permute-start.13) | collective-permute-done | bytes 524320 | tf_op jit(solution)/shard_map/ppermute | solution.py:23
  123.0 1.5 collective-permute-start.20
  124.5 0.9 collective-permute-done.14.refs_2_
  125.4 1.8 %shard_map.31 = (f32[256,256]{1,0:T(8,128)S(1)}, f32[256,256]{1,0:T(8,128)}) custom-call(s32[1]{0:T(128)} %bitcast.1.side, f32[2,256,256]{2,1,0:T(8,128)S(1)} %get-tuple-element.44.refs_0_, f32[2,256,256]{2,1,0:T(8,128)S(1)} %collective-permute-done.13.refs_1_, f32[2,256,256]{2,1,0:T(8,128)S(1)} %collective-permute-done.14.refs_2_, ...), custom_call_target="tpu_custom_call" | custom-call | flops 1 | bytes 1 | tf_op jit(solution)/shard_map/pallas_call | solution.py:46
  127.2 2.7 %collective-permute-start.16 = (f32[256,256]{1,0:T(8,128)}, f32[256,256]{1,0:T(8,128)S(1)}, u32[]{:S(2)}, u32[]{:S(2)}) collective-permute-start(f32[256,256]{1,0:T(8,128)} %get-tuple-element.31), channel_id=1, source_target_pairs={{0,64},{1,65},{2,66},{3,67},{4,68},{5,69},{6,70},{7,71},{8,72},{9,... | collective-permute-start | bytes 786440 | tf_op jit(solution)/shard_map/ppermute | solution.py:23
  129.9 3.4 %collective-permute-done.18.refs_1_ = f32[2,256,256]{2,1,0:T(8,128)S(1)} collective-permute-done((f32[2,256,256]{2,1,0:T(8,128)}, f32[2,256,256]{2,1,0:T(8,128)S(1)}, u32[]{:S(2)}, u32[]{:S(2)}) %collective-permute-start.18) | collective-permute-done | bytes 524320 | tf_op jit(solution)/shard_map/ppermute | solution.py:23
  133.3 2.1 %collective-permute-done.19.refs_2_ = f32[2,256,256]{2,1,0:T(8,128)S(1)} collective-permute-done((f32[2,256,256]{2,1,0:T(8,128)}, f32[2,256,256]{2,1,0:T(8,128)S(1)}, u32[]{:S(2)}, u32[]{:S(2)}) %collective-permute-start.19) | collective-permute-done | bytes 524320 | tf_op jit(solution)/shard_map/ppermute | solution.py:23
  135.3 2.8 %collective-permute-done.20.refs_3_ = f32[2,256,256]{2,1,0:T(8,128)} collective-permute-done((f32[2,256,256]{2,1,0:T(8,128)}, f32[2,256,256]{2,1,0:T(8,128)}, u32[]{:S(2)}, u32[]{:S(2)}) %collective-permute-start.20) | collective-permute-done | bytes 524320 | tf_op jit(solution)/shard_map/ppermute | solution.py:23
  138.2 1.1 shard_map.33
  139.3 3.1 %collective-permute-start.21 = (f32[256,256]{1,0:T(8,128)S(1)}, f32[256,256]{1,0:T(8,128)S(1)}, u32[]{:S(2)}, u32[]{:S(2)}) collective-permute-start(f32[256,256]{1,0:T(8,128)S(1)} %get-tuple-element.36), channel_id=1, source_target_pairs={{0,64},{1,65},{2,66},{3,67},{4,68},{5,69},{6,70},{7,71},{8,72},{9,... | collective-permute-start | bytes 786440 | tf_op jit(solution)/shard_map/ppermute | solution.py:23
  142.4 3.5 %collective-permute-done.16.other_one = f32[256,256]{1,0:T(8,128)S(1)} collective-permute-done((f32[256,256]{1,0:T(8,128)}, f32[256,256]{1,0:T(8,128)S(1)}, u32[]{:S(2)}, u32[]{:S(2)}) %collective-permute-start.16) | collective-permute-done | bytes 262176 | tf_op jit(solution)/shard_map/ppermute | solution.py:23
  145.9 2.9 %collective-permute-done.21.other_two = f32[256,256]{1,0:T(8,128)S(1)} collective-permute-done((f32[256,256]{1,0:T(8,128)S(1)}, f32[256,256]{1,0:T(8,128)S(1)}, u32[]{:S(2)}, u32[]{:S(2)}) %collective-permute-start.21) | collective-permute-done | bytes 262176 | tf_op jit(solution)/shard_map/ppermute | solution.py:23
  148.8 0.8 shard_map.34
  (21 shorter events, 0.0 us)
Async XLA Ops:
  20.9 26.1 %collective-permute-start = (f32[4,64,1024]{2,1,0:T(8,128)S(1)}, f32[4,64,1024]{2,1,0:T(8,128)S(1)}, u32[]{:S(2)}, u32[]{:S(2)}) collective-permute-start(f32[4,64,1024]{2,1,0:T(8,128)S(1)} %all_to_all.5.refs_0_), channel_id=1, source_target_pairs={{0,18},{1,19},{2,16},{3,17},{4,22},{5,23},{6,20},{7,21},{8,26},{9,... | collective-permute-start | bytes 3145736 | tf_op jit(solution)/shard_map/ppermute | solution.py:23
  22.6 25.4 %collective-permute-start.1 = (f32[4,64,1024]{2,1,0:T(8,128)S(1)}, f32[4,64,1024]{2,1,0:T(8,128)S(1)}, u32[]{:S(2)}, u32[]{:S(2)}) collective-permute-start(f32[4,64,1024]{2,1,0:T(8,128)S(1)} %all_to_all.5.refs_0_), channel_id=1, source_target_pairs={{0,12},{1,13},{2,14},{3,15},{4,8},{5,9},{6,10},{7,11},{8,4},{9,5},... | collective-permute-start | bytes 3145736 | tf_op jit(solution)/shard_map/ppermute | solution.py:23
  26.6 23.0 %collective-permute-start.4 = (f32[4,64,1024]{2,1,0:T(8,128)S(1)}, f32[4,64,1024]{2,1,0:T(8,128)}, u32[]{:S(2)}, u32[]{:S(2)}) collective-permute-start(f32[4,64,1024]{2,1,0:T(8,128)S(1)} %all_to_all.5.refs_0_), channel_id=1, source_target_pairs={{0,4},{1,5},{2,6},{3,7},{4,0},{5,1},{6,2},{7,3},{8,12},{9,13},{10,... | collective-permute-start | bytes 3145736 | tf_op jit(solution)/shard_map/ppermute | solution.py:23
  48.0 1.6 %copy-start.3 = (f32[4,64,1024]{2,1,0:T(8,128)}, f32[4,64,1024]{2,1,0:T(8,128)S(1)}, u32[]{:S(2)}) copy-start(f32[4,64,1024]{2,1,0:T(8,128)S(1)} %collective-permute-done.1.refs_2_) | copy-start | bytes 3145732
  49.6 26.0 %collective-permute-start.2 = (f32[4,64,1024]{2,1,0:T(8,128)S(1)}, f32[4,64,1024]{2,1,0:T(8,128)S(1)}, u32[]{:S(2)}, u32[]{:S(2)}) collective-permute-start(f32[4,64,1024]{2,1,0:T(8,128)S(1)} %collective-permute-done._.refs_1_), channel_id=1, source_target_pairs={{0,12},{1,13},{2,14},{3,15},{4,8},{5,9},{6,10},{7,11},{8,4},{9,5},... | collective-permute-start | bytes 3145736 | tf_op jit(solution)/shard_map/ppermute | solution.py:23
  52.0 22.5 %collective-permute-start.3 = (f32[4,64,1024]{2,1,0:T(8,128)S(1)}, f32[4,64,1024]{2,1,0:T(8,128)S(1)}, u32[]{:S(2)}, u32[]{:S(2)}) collective-permute-start(f32[4,64,1024]{2,1,0:T(8,128)S(1)} %collective-permute-done._.refs_1_), channel_id=1, source_target_pairs={{0,4},{1,5},{2,6},{3,7},{4,0},{5,1},{6,2},{7,3},{8,12},{9,13},{10,... | collective-permute-start | bytes 3145736 | tf_op jit(solution)/shard_map/ppermute | solution.py:23
  52.0 2.2 %copy-start.2 = (f32[4096,256]{1,0:T(8,128)S(1)}, f32[4096,256]{1,0:T(8,128)}, u32[]{:S(2)}) copy-start(f32[4096,256]{1,0:T(8,128)} %value.1) | copy-start | bytes 12582916
  54.2 7.2 %copy-start.4 = (f32[4,64,1024]{2,1,0:T(8,128)S(1)}, f32[4,64,1024]{2,1,0:T(8,128)}, u32[]{:S(2)}) copy-start(f32[4,64,1024]{2,1,0:T(8,128)} %copy-done.3) | copy-start | bytes 3145732
  55.4 22.6 %collective-permute-start.5 = (f32[1024,256]{1,0:T(8,128)S(1)}, f32[1024,256]{1,0:T(8,128)S(1)}, u32[]{:S(2)}, u32[]{:S(2)}) collective-permute-start(f32[1024,256]{1,0:T(8,128)S(1)} %get-tuple-element.22), channel_id=1, source_target_pairs={{0,1},{1,0},{2,3},{3,2},{4,5},{5,4},{6,7},{7,6},{8,9},{9,8},{10,11... | collective-permute-start | bytes 3145736 | tf_op jit(solution)/shard_map/ppermute | solution.py:23
  56.9 24.5 %collective-permute-start.6 = (f32[1024,256]{1,0:T(8,128)S(1)}, f32[1024,256]{1,0:T(8,128)S(1)}, u32[]{:S(2)}, u32[]{:S(2)}) collective-permute-start(f32[1024,256]{1,0:T(8,128)S(1)} %get-tuple-element.23), channel_id=1, source_target_pairs={{0,3},{1,2},{2,1},{3,0},{4,7},{5,6},{6,5},{7,4},{8,11},{9,10},{10,... | collective-permute-start | bytes 3145736 | tf_op jit(solution)/shard_map/ppermute | solution.py:23
  59.0 26.3 %collective-permute-start.7 = (f32[1024,256]{1,0:T(8,128)}, f32[1024,256]{1,0:T(8,128)}, u32[]{:S(2)}, u32[]{:S(2)}) collective-permute-start(f32[1024,256]{1,0:T(8,128)} %get-tuple-element.24), channel_id=1, source_target_pairs={{0,16},{1,17},{2,18},{3,19},{4,20},{5,21},{6,22},{7,23},{8,24},{9,... | collective-permute-start | bytes 3145736 | tf_op jit(solution)/shard_map/ppermute | solution.py:23
  74.5 21.3 %collective-permute-start.8 = (f32[2,64,1024]{2,1,0:T(8,128)}, f32[2,64,1024]{2,1,0:T(8,128)}, u32[]{:S(2)}, u32[]{:S(2)}) collective-permute-start(f32[2,64,1024]{2,1,0:T(8,128)} %slice.80), channel_id=1, source_target_pairs={{0,12},{1,13},{2,14},{3,15},{4,8},{5,9},{6,10},{7,11},{8,4},{9,5},... | collective-permute-start | bytes 1572872 | tf_op jit(solution)/shard_map/ppermute | solution.py:23
  75.6 20.2 %collective-permute-start.9 = (f32[2,64,1024]{2,1,0:T(8,128)}, f32[2,64,1024]{2,1,0:T(8,128)}, u32[]{:S(2)}, u32[]{:S(2)}) collective-permute-start(f32[2,64,1024]{2,1,0:T(8,128)} %slice.81), channel_id=1, source_target_pairs={{0,4},{1,5},{2,6},{3,7},{4,0},{5,1},{6,2},{7,3},{8,12},{9,13},{10,... | collective-permute-start | bytes 1572872 | tf_op jit(solution)/shard_map/ppermute | solution.py:23
  76.5 1.0 copy-start.6
  78.0 1.0 copy-start.8
  79.0 18.8 %collective-permute-start.10 = (f32[2,64,1024]{2,1,0:T(8,128)}, f32[2,64,1024]{2,1,0:T(8,128)}, u32[]{:S(2)}, u32[]{:S(2)}) collective-permute-start(f32[2,64,1024]{2,1,0:T(8,128)} %slice.82), channel_id=1, source_target_pairs={{0,12},{1,13},{2,14},{3,15},{4,8},{5,9},{6,10},{7,11},{8,4},{9,5},... | collective-permute-start | bytes 1572872 | tf_op jit(solution)/shard_map/ppermute | solution.py:23
  81.5 1.0 copy-start.10
  82.4 15.3 %collective-permute-start.11 = (f32[2,64,1024]{2,1,0:T(8,128)}, f32[2,64,1024]{2,1,0:T(8,128)}, u32[]{:S(2)}, u32[]{:S(2)}) collective-permute-start(f32[2,64,1024]{2,1,0:T(8,128)} %slice.83), channel_id=1, source_target_pairs={{0,4},{1,5},{2,6},{3,7},{4,0},{5,1},{6,2},{7,3},{8,12},{9,13},{10,... | collective-permute-start | bytes 1572872 | tf_op jit(solution)/shard_map/ppermute | solution.py:23
  83.9 1.5 %copy-start.9 = (f32[1024,256]{1,0:T(8,128)S(1)}, f32[1024,256]{1,0:T(8,128)}, u32[]{:S(2)}) copy-start(f32[1024,256]{1,0:T(8,128)} %copy-done.8) | copy-start | bytes 3145732
  83.9 1.9 %copy-start.11 = (f32[1024,256]{1,0:T(8,128)S(1)}, f32[1024,256]{1,0:T(8,128)}, u32[]{:S(2)}) copy-start(f32[1024,256]{1,0:T(8,128)} %copy-done.10) | copy-start | bytes 3145732
  85.7 2.1 %copy-start.5 = (f32[4,64,1024]{2,1,0:T(8,128)S(1)}, f32[4,64,1024]{2,1,0:T(8,128)}, u32[]{:S(2)}) copy-start(f32[4,64,1024]{2,1,0:T(8,128)} %copy-done.3) | copy-start | bytes 3145732
  85.7 2.1 %copy-start.7 = (f32[4,64,1024]{2,1,0:T(8,128)S(1)}, f32[4,64,1024]{2,1,0:T(8,128)}, u32[]{:S(2)}) copy-start(f32[4,64,1024]{2,1,0:T(8,128)} %copy-done.6) | copy-start | bytes 3145732
  94.5 1.4 copy-start
  97.7 9.2 %collective-permute-start.12 = (f32[4,2,256,256]{3,2,1,0:T(8,128)S(1)}, f32[4,2,256,256]{3,2,1,0:T(8,128)S(1)}, u32[]{:S(2)}, u32[]{:S(2)}) collective-permute-start(f32[4,2,256,256]{3,2,1,0:T(8,128)S(1)} %get-tuple-element.29), channel_id=1, source_target_pairs={{0,32},{1,33},{2,34},{3,35},{4,36},{5,37},{6,38},{7,39},{8,40},{9,... | collective-permute-start | bytes 6291464 | tf_op jit(solution)/shard_map/ppermute | solution.py:23
  97.7 9.2 %copy-start.1 = (f32[4,2,256,256]{3,2,1,0:T(8,128)S(1)}, f32[4,2,256,256]{3,2,1,0:T(8,128)}, u32[]{:S(2)}) copy-start(f32[4,2,256,256]{3,2,1,0:T(8,128)} %copy-done) | copy-start | bytes 6291460
  106.4 5.3 %collective-permute-start.17 = (f32[4,2,256,256]{3,2,1,0:T(8,128)S(1)}, f32[4,2,256,256]{3,2,1,0:T(8,128)S(1)}, u32[]{:S(2)}, u32[]{:S(2)}) collective-permute-start(f32[4,2,256,256]{3,2,1,0:T(8,128)S(1)} %get-tuple-element.34), channel_id=1, source_target_pairs={{0,32},{1,33},{2,34},{3,35},{4,36},{5,37},{6,38},{7,39},{8,40},{9,... | collective-permute-start | bytes 6291464 | tf_op jit(solution)/shard_map/ppermute | solution.py:23
  108.2 14.8 %collective-permute-start.13 = (f32[2,256,256]{2,1,0:T(8,128)S(1)}, f32[2,256,256]{2,1,0:T(8,128)S(1)}, u32[]{:S(2)}, u32[]{:S(2)}) collective-permute-start(f32[2,256,256]{2,1,0:T(8,128)S(1)} %get-tuple-element.43), channel_id=1, source_target_pairs={{0,1},{1,0},{2,3},{3,2},{4,5},{5,4},{6,7},{7,6},{8,9},{9,8},{10,11... | collective-permute-start | bytes 1572872 | tf_op jit(solution)/shard_map/ppermute | solution.py:23
  109.1 16.2 %collective-permute-start.14 = (f32[2,256,256]{2,1,0:T(8,128)}, f32[2,256,256]{2,1,0:T(8,128)S(1)}, u32[]{:S(2)}, u32[]{:S(2)}) collective-permute-start(f32[2,256,256]{2,1,0:T(8,128)} %get-tuple-element.42), channel_id=1, source_target_pairs={{0,3},{1,2},{2,1},{3,0},{4,7},{5,6},{6,5},{7,4},{8,11},{9,10},{10,... | collective-permute-start | bytes 1572872 | tf_op jit(solution)/shard_map/ppermute | solution.py:23
  111.2 14.2 %collective-permute-start.15 = (f32[2,256,256]{2,1,0:T(8,128)}, f32[2,256,256]{2,1,0:T(8,128)}, u32[]{:S(2)}, u32[]{:S(2)}) collective-permute-start(f32[2,256,256]{2,1,0:T(8,128)} %get-tuple-element.41), channel_id=1, source_target_pairs={{0,16},{1,17},{2,18},{3,19},{4,20},{5,21},{6,22},{7,23},{8,24},{9,... | collective-permute-start | bytes 1572872 | tf_op jit(solution)/shard_map/ppermute | solution.py:23
  113.0 20.3 %collective-permute-start.18 = (f32[2,256,256]{2,1,0:T(8,128)}, f32[2,256,256]{2,1,0:T(8,128)S(1)}, u32[]{:S(2)}, u32[]{:S(2)}) collective-permute-start(f32[2,256,256]{2,1,0:T(8,128)} %get-tuple-element.39), channel_id=1, source_target_pairs={{0,1},{1,0},{2,3},{3,2},{4,5},{5,4},{6,7},{7,6},{8,9},{9,8},{10,11... | collective-permute-start | bytes 1572872 | tf_op jit(solution)/shard_map/ppermute | solution.py:23
  113.6 21.8 %collective-permute-start.19 = (f32[2,256,256]{2,1,0:T(8,128)}, f32[2,256,256]{2,1,0:T(8,128)S(1)}, u32[]{:S(2)}, u32[]{:S(2)}) collective-permute-start(f32[2,256,256]{2,1,0:T(8,128)} %get-tuple-element.38), channel_id=1, source_target_pairs={{0,3},{1,2},{2,1},{3,0},{4,7},{5,6},{6,5},{7,4},{8,11},{9,10},{10,... | collective-permute-start | bytes 1572872 | tf_op jit(solution)/shard_map/ppermute | solution.py:23
  123.0 15.2 %collective-permute-start.20 = (f32[2,256,256]{2,1,0:T(8,128)}, f32[2,256,256]{2,1,0:T(8,128)}, u32[]{:S(2)}, u32[]{:S(2)}) collective-permute-start(f32[2,256,256]{2,1,0:T(8,128)} %get-tuple-element.37), channel_id=1, source_target_pairs={{0,16},{1,17},{2,18},{3,19},{4,20},{5,21},{6,22},{7,23},{8,24},{9,... | collective-permute-start | bytes 1572872 | tf_op jit(solution)/shard_map/ppermute | solution.py:23
  127.2 18.7 %collective-permute-start.16 = (f32[256,256]{1,0:T(8,128)}, f32[256,256]{1,0:T(8,128)S(1)}, u32[]{:S(2)}, u32[]{:S(2)}) collective-permute-start(f32[256,256]{1,0:T(8,128)} %get-tuple-element.31), channel_id=1, source_target_pairs={{0,64},{1,65},{2,66},{3,67},{4,68},{5,69},{6,70},{7,71},{8,72},{9,... | collective-permute-start | bytes 786440 | tf_op jit(solution)/shard_map/ppermute | solution.py:23
  139.3 9.5 %collective-permute-start.21 = (f32[256,256]{1,0:T(8,128)S(1)}, f32[256,256]{1,0:T(8,128)S(1)}, u32[]{:S(2)}, u32[]{:S(2)}) collective-permute-start(f32[256,256]{1,0:T(8,128)S(1)} %get-tuple-element.36), channel_id=1, source_target_pairs={{0,64},{1,65},{2,66},{3,67},{4,68},{5,69},{6,70},{7,71},{8,72},{9,... | collective-permute-start | bytes 786440 | tf_op jit(solution)/shard_map/ppermute | solution.py:23

commit v7 on v6

--- a/solution.py
+++ b/solution.py
@@ -21,12 +21,6 @@
         for h in range(2) for c in range(2) for x in range(2) for z in range(4) for y in range(4)
     ]
     return lax.ppermute(value, AXES, pairs)
-
-
-RINGS = [
-    [number(h, c, x, z, y) for y in range(4)]
-    for h in range(2) for c in range(2) for x in range(2) for z in range(4)
-]
 
 
 def halves(value):
@@ -90,39 +84,82 @@
     return [pltpu.with_memory_space_constraint(value, pltpu.VMEM) for value in found]
 
 
-def products(swap, groups, rights, earlier):
-    arrays = [array for group in groups for array in group]
-    depth = arrays[0].shape[2]
-    rows = sum(array.shape[0] * array.shape[1] for array in groups[0])
+def multiplied(blocks, left_high, left_low, high, low, store):
+    depth = left_high.shape[1]
+    at = 0
+    for block in blocks:
+        value = block[...].reshape(block.shape[0] * block.shape[1], depth)
+        span = slice(at, at + value.shape[0])
+        left_high[span], left_low[span] = halves(value)
+        at += value.shape[0]
+    columns = high.shape[1] // 4
+    for d in range(4):
+        span = slice(d * columns, (d + 1) * columns)
+        total = jnp.dot(left_high[...], high[:, span], preferred_element_type=jnp.float32)
+        total += jnp.dot(left_high[...], low[:, span], preferred_element_type=jnp.float32)
+        total += jnp.dot(left_low[...], high[:, span], preferred_element_type=jnp.float32)
+        store(d, total.reshape(-1, 2, 4, blocks[0].shape[1], columns))
+
+
+def places(d):
+    return [(part, block, part ^ (d == 3), block ^ (0, 1, 3, 2)[d]) for part in range(2) for block in range(4)]
+
+
+def flat(planes):
+    return [array for plane in planes for part in plane for array in part]
+
+
+def early_products(swap, pair, ahead, rights, earlier):
+    arrays = flat([*pair, ahead])
+    rows, depth = arrays[0].shape[1:]
     columns = rights[0].shape[1] // 4
 
     def kernel(swap, *refs):
         blocks, rest = refs[: len(arrays)], refs[len(arrays) + len(earlier):]
-        high, low, keep, give, left_high, left_low = rest
-        at = 0
-        for block in blocks:
-            value = block[...].reshape(block.shape[0] * block.shape[1], depth)
-            span = slice(at, at + value.shape[0])
-            left_high[span], left_low[span] = halves(value)
-            at += value.shape[0]
+        high, low, keep, give, third, left_high, left_low = rest
         swapped = swap[0] == 1
-        for d in range(4):
-            span = slice(d * columns, (d + 1) * columns)
-            total = jnp.dot(left_high[...], high[:, span], preferred_element_type=jnp.float32)
-            total += jnp.dot(left_high[...], low[:, span], preferred_element_type=jnp.float32)
-            total += jnp.dot(left_low[...], high[:, span], preferred_element_type=jnp.float32)
-            total = total.reshape(2, 2, rows // 2, columns)
-            for part in range(2):
-                zero, one = total[0, part], total[1, part]
-                into = part ^ (d == 3)
-                keep[d, into] = jnp.where(swapped, one, zero)
-                give[d, into] = jnp.where(swapped, zero, one)
-
-    shape = jax.ShapeDtypeStruct((4, 2, rows // 2, columns), jnp.float32)
-    scratch = pltpu.VMEM((2 * rows, depth), jnp.bfloat16)
+
+        def store(d, total):
+            for part, block, to_part, to_block in places(d):
+                zero, one = total[0, part, block], total[1, part, block]
+                keep[d, to_part, to_block] = jnp.where(swapped, one, zero)
+                give[d, to_part, to_block] = jnp.where(swapped, zero, one)
+                third[d, to_part, to_block] = total[2, part, block]
+
+        multiplied(blocks, left_high, left_low, high, low, store)
+
+    shape = jax.ShapeDtypeStruct((4, 2, 4, rows, columns), jnp.float32)
+    scratch = pltpu.VMEM((24 * rows, depth), jnp.bfloat16)
     return call(
         kernel, swap, (*arrays, *earlier, *rights),
         [whole(array) for array in arrays] + [ANYWHERE] * len(earlier) + [VMEM] * 2,
+        [shape] * 3, [whole(shape)] * 3, [scratch] * 2,
+    )
+
+
+def late_products(swap, plane, third, rights, earlier):
+    arrays = flat([plane])
+    rows, depth = arrays[0].shape[1:]
+    columns = rights[0].shape[1] // 4
+
+    def kernel(swap, *refs):
+        blocks, rest = refs[: len(arrays)], refs[len(arrays) + len(earlier):]
+        high, low, ahead, keep, give, left_high, left_low = rest
+        swapped = swap[0] == 1
+
+        def store(d, total):
+            for part, block, to_part, to_block in places(d):
+                zero, one = ahead[d, to_part, to_block], total[0, part, block]
+                keep[d, to_part, to_block] = jnp.where(swapped, one, zero)
+                give[d, to_part, to_block] = jnp.where(swapped, zero, one)
+
+        multiplied(blocks, left_high, left_low, high, low, store)
+
+    shape = jax.ShapeDtypeStruct((4, 2, 4, rows, columns), jnp.float32)
+    scratch = pltpu.VMEM((8 * rows, depth), jnp.bfloat16)
+    return call(
+        kernel, swap, (*arrays, *earlier, *rights, third),
+        [whole(array) for array in arrays] + [ANYWHERE] * len(earlier) + [VMEM] * 2 + [whole(third)],
         [shape] * 2, [whole(shape)] * 2, [scratch] * 2,
     )
 
@@ -144,8 +181,10 @@
 
 
 def join_kernel(place, one, other_one, two, other_two, out):
-    out[place[0]] = one[...] + other_one[...]
-    out[1 - place[0]] = two[...] + other_two[...]
+    for block in range(4):
+        line = place[1] ^ block
+        out[place[0], line] = one[block] + other_one[block]
+        out[1 - place[0], line] = two[block] + other_two[block]
 
 
 def join(place, values):
@@ -163,8 +202,10 @@
     swap = (core ^ (z >> 1)).reshape(1)
     side = (x_hi ^ x_lo).reshape(1)
 
-    blocks = [lax.dynamic_slice(left, (0, (number ^ (3 * x_lo)) * depth), (rows, depth)) for number in (0, 1, 3, 2)]
-    mine = lax.all_to_all(jnp.stack(blocks), AXES, 0, 0, tiled=True, axis_index_groups=RINGS)
+    def block(d):
+        return lax.dynamic_slice(left, (0, (quarter ^ d) * depth), (rows, depth))
+
+    mine = jnp.stack([block(0), send(block(1), dy=1), send(block(3), dy=2), send(block(2), dy=3)])
     other = send(mine, dx=1, dy=2)
 
     planes = []
@@ -180,19 +221,21 @@
     rights = split(swap, pieces)
 
     late = [*planes[0][2], *planes[1][2]]
-    ends, earlier = [], [planes[1][1][0]]
-    for kept, given in ((0, 3), (1, 2)):
-        groups = [[array for part in planes for array in part[dz]] for dz in (kept, given)]
-        keep, give = products(swap, groups, rights, earlier)
-        give, *_ = lax.optimization_barrier((give, *late))
+    zero, one, two, three = ([part[dz] for part in planes] for dz in range(4))
+    keep, give, third = early_products(swap, (zero, three), one, rights, [planes[1][1][0]])
+    ends = []
+    for last in (False, True):
+        if last:
+            keep, give = late_products(swap, two, third, rights, [])
+        else:
+            give, *_ = lax.optimization_barrier((give, *late))
         got = send(give, core=1)
         sums = [keep[d] + got[d] for d in range(4)]
         terms = [sums[0]] + [send(sums[d], **NEAR[d]) for d in range(1, 4)]
-        earlier = [keep]
         here, there = summed(side, terms)
         ends += [here, send(there, dhi=1)]
 
-    total = join(((z & 1) ^ swap[0]).reshape(1), ends)
+    total = join(jnp.stack([(z & 1) ^ swap[0], y ^ (2 * side[0])]), ends)
     return total.reshape(8 * rows, columns)
 
 

time: 150 us -> 148 us (0.987)
  blocking collectives: 19.4 us -> 0 us
  waiting for transfers between devices: 60.4 us -> 75.9 us
  local copies, waits for them, and re-layouts: 14.2 us -> 11.3 us
  starting transfers between devices: 30.6 us -> 33.1 us
  Pallas kernels: 22.3 us -> 24.4 us
    all_to_all x1 -> x0, blocking collectives: 19.4 us -> none  [per_device(): lax.all_to_all(jnp.stack(blocks), AXES, 0, 0, tiled=True, axis_index_grou...]
    ppermute x22 -> x25, waiting for transfers between devices: 60.4 us -> 75.9 us  [send(): return lax.ppermute(value, AXES, pairs)]
    ppermute x22 -> x25, starting transfers between devices: 30.6 us -> 33.1 us  [send(): return lax.ppermute(value, AXES, pairs)]
    pallas_call x7, Pallas kernels: 22.3 us -> 24.4 us  [call(): pl.pallas_call(kernel, grid_spec=pltpu.PrefetchScalarGridSpec(num_scalar_...]
    unnamed x24, local copies, waits for them, and re-layouts: 6.95 us -> 5.02 us
  transfers between devices with their start and end apart: 22 -> 25, of which waited for: 13 -> 13; matrix products, arithmetic and copies ran while one was open for 6% -> 5% of each run, Pallas kernels for 14% -> 16%
where the time goes in v7:
time: 148 us
  waiting for transfers between devices  75.9 us (51%)
  starting transfers between devices  33.1 us (22%)
  Pallas kernels  24.4 us (16%)
  local copies, waits for them, and re-layouts  11.3 us (8%)
  other arithmetic  2.7 us (2%)
    ppermute x25, waiting for transfers between devices, send(): return lax.ppermute(value, AXES, pairs)  75.9 us
    ppermute x25, starting transfers between devices, send(): return lax.ppermute(value, AXES, pairs)  33.1 us
    pallas_call x7, Pallas kernels, call(): pl.pallas_call(kernel, grid_spec=pltpu.PrefetchScalarGridSpec(num_scalar_...  24.4 us
    unnamed x24, local copies, waits for them, and re-layouts  5.02 us
    slice x4, local copies, waits for them, and re-layouts, per_device(): two = (send(one[:2], dz=3), send(three[2:], dz=1))  3.4 us
  transfers between devices with their start and end apart: 25, of which 13 were waited for; matrix products, arithmetic and copies ran while one was open for 5% of the time, Pallas kernels for 16%

profile of v7, /device:TPU:0, one launch (start us, length us, event | category | flops | bytes accessed | tf_op | source)
XLA Modules:
  0.0 147.5 jit_solution(2678952701959960941)
XLA Ops:
  0.0 1.4 dynamic-slice_bitcast_fusion
  1.4 3.2 %collective-permute-start.2 = (f32[64,1024]{1,0:T(8,128)S(1)}, f32[64,1024]{1,0:T(8,128)S(1)}, u32[]{:S(2)}, u32[]{:S(2)}) collective-permute-start(f32[64,1024]{1,0:T(8,128)S(1)} %get-tuple-element.47), channel_id=1, source_target_pairs={{0,3},{1,2},{2,1},{3,0},{4,7},{5,6},{6,5},{7,4},{8,11},{9,10},{10,... | collective-permute-start | bytes 786440 | tf_op jit(solution)/shard_map/ppermute | solution.py:23
  4.6 0.6 collective-permute-start.1
  5.3 0.4 collective-permute-start
  5.6 10.9 %collective-permute-done.2 = f32[64,1024]{1,0:T(8,128)S(1)} collective-permute-done((f32[64,1024]{1,0:T(8,128)S(1)}, f32[64,1024]{1,0:T(8,128)S(1)}, u32[]{:S(2)}, u32[]{:S(2)}) %collective-permute-start.2) | collective-permute-done | bytes 262176 | tf_op jit(solution)/shard_map/ppermute | solution.py:23
  16.6 0.0 collective-permute-done.1
  16.6 0.7 collective-permute-done
  17.3 0.1 pad_maximum_fusion.refs_0_
  17.3 4.0 %collective-permute-start.3 = (f32[4,64,1024]{2,1,0:T(8,128)S(1)}, f32[4,64,1024]{2,1,0:T(8,128)S(1)}, u32[]{:S(2)}, u32[]{:S(2)}) collective-permute-start(f32[4,64,1024]{2,1,0:T(8,128)S(1)} %pad_maximum_fusion.refs_0_), channel_id=1, source_target_pairs={{0,18},{1,19},{2,16},{3,17},{4,22},{5,23},{6,20},{7,21},{8,26},{9,... | collective-permute-start | bytes 3145736 | tf_op jit(solution)/shard_map/ppermute | solution.py:23
  21.4 4.0 %collective-permute-start.4 = (f32[4,64,1024]{2,1,0:T(8,128)S(1)}, f32[4,64,1024]{2,1,0:T(8,128)S(1)}, u32[]{:S(2)}, u32[]{:S(2)}) collective-permute-start(f32[4,64,1024]{2,1,0:T(8,128)S(1)} %pad_maximum_fusion.refs_0_), channel_id=1, source_target_pairs={{0,12},{1,13},{2,14},{3,15},{4,8},{5,9},{6,10},{7,11},{8,4},{9,5},... | collective-permute-start | bytes 3145736 | tf_op jit(solution)/shard_map/ppermute | solution.py:23
  25.4 18.4 %collective-permute-done.3._.refs_1_ = f32[4,64,1024]{2,1,0:T(8,128)S(1)} collective-permute-done((f32[4,64,1024]{2,1,0:T(8,128)S(1)}, f32[4,64,1024]{2,1,0:T(8,128)S(1)}, u32[]{:S(2)}, u32[]{:S(2)}) %collective-permute-start.3) | collective-permute-done | bytes 1048608 | tf_op jit(solution)/shard_map/ppermute | solution.py:23
  43.8 3.3 %collective-permute-done.4.refs_2_ = f32[4,64,1024]{2,1,0:T(8,128)S(1)} collective-permute-done((f32[4,64,1024]{2,1,0:T(8,128)S(1)}, f32[4,64,1024]{2,1,0:T(8,128)S(1)}, u32[]{:S(2)}, u32[]{:S(2)}) %collective-permute-start.4) | collective-permute-done | bytes 1048608 | tf_op jit(solution)/shard_map/ppermute | solution.py:23
  47.2 1.5 collective-permute-done.6.refs_4_
  48.6 1.6 %collective-permute-start.5 = (f32[4,64,1024]{2,1,0:T(8,128)S(1)}, f32[4,64,1024]{2,1,0:T(8,128)S(1)}, u32[]{:S(2)}, u32[]{:S(2)}) collective-permute-start(f32[4,64,1024]{2,1,0:T(8,128)S(1)} %collective-permute-done.3._.refs_1_), channel_id=1, source_target_pairs={{0,12},{1,13},{2,14},{3,15},{4,8},{5,9},{6,10},{7,11},{8,4},{9,5},... | collective-permute-start | bytes 3145736 | tf_op jit(solution)/shard_map/ppermute | solution.py:23
  50.2 1.1 shard_map.28
  51.3 1.1 collective-permute-start.8
  52.4 0.2 collective-permute-start.9
  52.6 1.4 collective-permute-start.10
  54.0 0.8 slice.80
  54.9 0.9 slice.81
  55.8 16.7 %collective-permute-done.7.refs_5_.refs_6_ = f32[4,64,1024]{2,1,0:T(8,128)S(1)} collective-permute-done((f32[4,64,1024]{2,1,0:T(8,128)S(1)}, f32[4,64,1024]{2,1,0:T(8,128)S(1)}, u32[]{:S(2)}, u32[]{:S(2)}) %collective-permute-start.7) | collective-permute-done | bytes 1048608 | tf_op jit(solution)/shard_map/ppermute | solution.py:23
  72.5 1.4 collective-permute-start.11
  73.8 0.8 slice.82
  74.7 0.8 slice.83
  75.5 1.0 copy-done.5
  76.5 1.0 copy-done.8
  77.5 1.8 %collective-permute-start.13 = (f32[2,64,1024]{2,1,0:T(8,128)}, f32[2,64,1024]{2,1,0:T(8,128)}, u32[]{:S(2)}, u32[]{:S(2)}) collective-permute-start(f32[2,64,1024]{2,1,0:T(8,128)} %slice.82), channel_id=1, source_target_pairs={{0,12},{1,13},{2,14},{3,15},{4,8},{5,9},{6,10},{7,11},{8,4},{9,5},... | collective-permute-start | bytes 1572872 | tf_op jit(solution)/shard_map/ppermute | solution.py:23
  79.4 0.0 collective-permute-done.9.refs_2_
  79.4 1.0 copy-done.10
  80.4 1.4 collective-permute-start.14
  81.8 1.4 constant_dynamic-slice_fusion.refs_0_
  83.2 0.0 collective-permute-done.10.refs_3_
  83.2 0.1 copy-done.9
  83.3 0.3 copy-done.11
  83.6 2.1 %shard_map.29 = (bf16[1024,1024]{1,0:T(8,128)(2,1)S(1)}, bf16[1024,1024]{1,0:T(8,128)(2,1)S(1)}) custom-call(s32[1]{0:T(128)} %bitcast.3._.swap, f32[1024,256]{1,0:T(8,128)S(1)} %constant_dynamic-slice_fusion.refs_0_, f32[1024,256]{1,0:T(8,128)S(1)} %copy-done.9, f32[1024,256]{1,0:T(8,128)S(1)} %copy-done.11, f32[1024,256]{1,0:T(8,128)} %collective-permute-done.10.refs_3_), custom_call_target="tpu_custom_call" | custom-call | flops 1 | bytes 1 | tf_op jit(solution)/shard_map/pallas_call | solution.py:40
  85.8 0.1 copy-done.6
  85.8 11.9 %shard_map.30 = (f32[4,2,4,64,256]{4,3,2,1,0:T(8,128)S(1)}, f32[4,2,4,64,256]{4,3,2,1,0:T(8,128)}, f32[4,2,4,64,256]{4,3,2,1,0:T(8,128)}) custom-call(s32[1]{0:T(128)} %bitcast.3._.swap, f32[4,64,1024]{2,1,0:T(8,128)S(1)} %pad_maximum_fusion.refs_0_, f32[4,64,1024]{2,1,0:T(8,128)S(1)} %collective-permute-done.3._.refs_1_, f32[4,64,1024]{2,1,0:T(8,128)S(1)} %copy-done.2, ...), custom_call_target="tpu_custom_call" | custom-call | flops 1 | bytes 1 | tf_op jit(solution)/shard_map/pallas_call | solution.py:40
  97.7 0.0 collective-permute-done.11.refs_0_
  97.7 0.0 collective-permute-done.12.refs_1_
  97.7 0.1 collective-permute-start.15
  97.8 1.6 %copy-done.7 = f32[4,2,4,64,256]{4,3,2,1,0:T(8,128)S(1)} copy-done((f32[4,2,4,64,256]{4,3,2,1,0:T(8,128)S(1)}, f32[4,2,4,64,256]{4,3,2,1,0:T(8,128)}, u32[]{:S(2)}) %copy-start.7) | copy-done | bytes 2097176
  99.4 4.9 %shard_map.32 = (f32[4,2,4,64,256]{4,3,2,1,0:T(8,128)S(1)}, f32[4,2,4,64,256]{4,3,2,1,0:T(8,128)S(1)}) custom-call(s32[1]{0:T(128)} %bitcast.3._.swap, f32[2,64,1024]{2,1,0:T(8,128)} %collective-permute-done.11.refs_0_, f32[2,64,1024]{2,1,0:T(8,128)} %collective-permute-done.12.refs_1_, f32[2,64,1024]{2,1,0:T(8,128)} %collective-permute-done.13.refs_2_, ...), custom_call_target="tpu_custom_call" | custom-call | flops 1 | bytes 1 | tf_op jit(solution)/shard_map/pallas_call | solution.py:40
  104.4 0.6 collective-permute-start.20
  104.9 1.2 fusion.4
  106.2 1.3 collective-permute-start.16
  107.5 0.1 collective-permute-start.17
  107.6 1.5 %collective-permute-start.18 = (f32[2,4,64,256]{3,2,1,0:T(8,128)}, f32[2,4,64,256]{3,2,1,0:T(8,128)}, u32[]{:S(2)}, u32[]{:S(2)}) collective-permute-start(f32[2,4,64,256]{3,2,1,0:T(8,128)} %get-tuple-element.41), channel_id=1, source_target_pairs={{0,16},{1,17},{2,18},{3,19},{4,20},{5,21},{6,22},{7,23},{8,24},{9,... | collective-permute-start | bytes 1572872 | tf_op jit(solution)/shard_map/ppermute | solution.py:23
  109.1 1.3 fusion
  110.4 1.3 collective-permute-start.21
  111.7 1.0 collective-permute-start.22
  112.7 8.3 %collective-permute-done.16.refs_1_ = f32[2,4,64,256]{3,2,1,0:T(8,128)S(1)} collective-permute-done((f32[2,4,64,256]{3,2,1,0:T(8,128)S(1)}, f32[2,4,64,256]{3,2,1,0:T(8,128)S(1)}, u32[]{:S(2)}, u32[]{:S(2)}) %collective-permute-start.16) | collective-permute-done | bytes 524320 | tf_op jit(solution)/shard_map/ppermute | solution.py:23
  121.0 0.5 collective-permute-start.23
  121.5 2.2 %collective-permute-done.17.refs_2_ = f32[2,4,64,256]{3,2,1,0:T(8,128)S(1)} collective-permute-done((f32[2,4,64,256]{3,2,1,0:T(8,128)}, f32[2,4,64,256]{3,2,1,0:T(8,128)S(1)}, u32[]{:S(2)}, u32[]{:S(2)}) %collective-permute-start.17) | collective-permute-done | bytes 524320 | tf_op jit(solution)/shard_map/ppermute | solution.py:23
  123.7 1.8 %shard_map.31 = (f32[4,64,256]{2,1,0:T(8,128)S(1)}, f32[4,64,256]{2,1,0:T(8,128)}) custom-call(s32[1]{0:T(128)} %bitcast.2.side, f32[2,4,64,256]{3,2,1,0:T(8,128)S(1)} %get-tuple-element.44.refs_0_, f32[2,4,64,256]{3,2,1,0:T(8,128)S(1)} %collective-permute-done.16.refs_1_, f32[2,4,64,256]{3,2,1,0:T(8,128)S(1)} %collective-permute-done.17.refs_2_, ...), custom_call_target="tpu_custom_call" | custom-call | flops 1 | bytes 1 | tf_op jit(solution)/shard_map/pallas_call | solution.py:40
  125.6 2.7 %collective-permute-start.19 = (f32[4,64,256]{2,1,0:T(8,128)}, f32[4,64,256]{2,1,0:T(8,128)S(1)}, u32[]{:S(2)}, u32[]{:S(2)}) collective-permute-start(f32[4,64,256]{2,1,0:T(8,128)} %get-tuple-element.31), channel_id=1, source_target_pairs={{0,64},{1,65},{2,66},{3,67},{4,68},{5,69},{6,70},{7,71},{8,72},{9,... | collective-permute-start | bytes 786440 | tf_op jit(solution)/shard_map/ppermute | solution.py:23
  128.3 3.0 %collective-permute-done.21.refs_1_ = f32[2,4,64,256]{3,2,1,0:T(8,128)S(1)} collective-permute-done((f32[2,4,64,256]{3,2,1,0:T(8,128)}, f32[2,4,64,256]{3,2,1,0:T(8,128)S(1)}, u32[]{:S(2)}, u32[]{:S(2)}) %collective-permute-start.21) | collective-permute-done | bytes 524320 | tf_op jit(solution)/shard_map/ppermute | solution.py:23
  131.3 2.4 %collective-permute-done.22.refs_2_ = f32[2,4,64,256]{3,2,1,0:T(8,128)S(1)} collective-permute-done((f32[2,4,64,256]{3,2,1,0:T(8,128)}, f32[2,4,64,256]{3,2,1,0:T(8,128)S(1)}, u32[]{:S(2)}, u32[]{:S(2)}) %collective-permute-start.22) | collective-permute-done | bytes 524320 | tf_op jit(solution)/shard_map/ppermute | solution.py:23
  133.7 2.4 %collective-permute-done.23.refs_3_ = f32[2,4,64,256]{3,2,1,0:T(8,128)} collective-permute-done((f32[2,4,64,256]{3,2,1,0:T(8,128)}, f32[2,4,64,256]{3,2,1,0:T(8,128)}, u32[]{:S(2)}, u32[]{:S(2)}) %collective-permute-start.23) | collective-permute-done | bytes 524320 | tf_op jit(solution)/shard_map/ppermute | solution.py:23
  136.2 1.1 shard_map.33
  137.3 2.8 %collective-permute-start.24 = (f32[4,64,256]{2,1,0:T(8,128)S(1)}, f32[4,64,256]{2,1,0:T(8,128)S(1)}, u32[]{:S(2)}, u32[]{:S(2)}) collective-permute-start(f32[4,64,256]{2,1,0:T(8,128)S(1)} %get-tuple-element.36), channel_id=1, source_target_pairs={{0,64},{1,65},{2,66},{3,67},{4,68},{5,69},{6,70},{7,71},{8,72},{9,... | collective-permute-start | bytes 786440 | tf_op jit(solution)/shard_map/ppermute | solution.py:23
  140.1 0.1 pad_add_fusion.place
  140.2 2.9 %collective-permute-done.19.other_one = f32[4,64,256]{2,1,0:T(8,128)S(1)} collective-permute-done((f32[4,64,256]{2,1,0:T(8,128)}, f32[4,64,256]{2,1,0:T(8,128)S(1)}, u32[]{:S(2)}, u32[]{:S(2)}) %collective-permute-start.19) | collective-permute-done | bytes 262176 | tf_op jit(solution)/shard_map/ppermute | solution.py:23
  143.1 3.1 %collective-permute-done.24.other_two = f32[4,64,256]{2,1,0:T(8,128)S(1)} collective-permute-done((f32[4,64,256]{2,1,0:T(8,128)S(1)}, f32[4,64,256]{2,1,0:T(8,128)S(1)}, u32[]{:S(2)}, u32[]{:S(2)}) %collective-permute-start.24) | collective-permute-done | bytes 262176 | tf_op jit(solution)/shard_map/ppermute | solution.py:23
  146.1 1.4 shard_map.34
  (27 shorter events, 0.1 us)
Async XLA Ops:
  0.0 50.2 %copy-start = (f32[4096,256]{1,0:T(8,128)S(1)}, f32[4096,256]{1,0:T(8,128)}, u32[]{:S(2)}) copy-start(f32[4096,256]{1,0:T(8,128)} %value.1) | copy-start | bytes 12582916
  1.4 15.1 %collective-permute-start.2 = (f32[64,1024]{1,0:T(8,128)S(1)}, f32[64,1024]{1,0:T(8,128)S(1)}, u32[]{:S(2)}, u32[]{:S(2)}) collective-permute-start(f32[64,1024]{1,0:T(8,128)S(1)} %get-tuple-element.47), channel_id=1, source_target_pairs={{0,3},{1,2},{2,1},{3,0},{4,7},{5,6},{6,5},{7,4},{8,11},{9,10},{10,... | collective-permute-start | bytes 786440 | tf_op jit(solution)/shard_map/ppermute | solution.py:23
  4.6 11.9 %collective-permute-start.1 = (f32[64,1024]{1,0:T(8,128)S(1)}, f32[64,1024]{1,0:T(8,128)S(1)}, u32[]{:S(2)}, u32[]{:S(2)}) collective-permute-start(f32[64,1024]{1,0:T(8,128)S(1)} %get-tuple-element.48), channel_id=1, source_target_pairs={{0,2},{1,3},{2,0},{3,1},{4,6},{5,7},{6,4},{7,5},{8,10},{9,11},{10,... | collective-permute-start | bytes 786440 | tf_op jit(solution)/shard_map/ppermute | solution.py:23
  5.3 12.0 %collective-permute-start = (f32[64,1024]{1,0:T(8,128)S(1)}, f32[64,1024]{1,0:T(8,128)S(1)}, u32[]{:S(2)}, u32[]{:S(2)}) collective-permute-start(f32[64,1024]{1,0:T(8,128)S(1)} %get-tuple-element.46), channel_id=1, source_target_pairs={{0,1},{1,0},{2,3},{3,2},{4,5},{5,4},{6,7},{7,6},{8,9},{9,8},{10,11... | collective-permute-start | bytes 786440 | tf_op jit(solution)/shard_map/ppermute | solution.py:23
  17.3 26.5 %collective-permute-start.3 = (f32[4,64,1024]{2,1,0:T(8,128)S(1)}, f32[4,64,1024]{2,1,0:T(8,128)S(1)}, u32[]{:S(2)}, u32[]{:S(2)}) collective-permute-start(f32[4,64,1024]{2,1,0:T(8,128)S(1)} %pad_maximum_fusion.refs_0_), channel_id=1, source_target_pairs={{0,18},{1,19},{2,16},{3,17},{4,22},{5,23},{6,20},{7,21},{8,26},{9,... | collective-permute-start | bytes 3145736 | tf_op jit(solution)/shard_map/ppermute | solution.py:23
  21.4 25.8 %collective-permute-start.4 = (f32[4,64,1024]{2,1,0:T(8,128)S(1)}, f32[4,64,1024]{2,1,0:T(8,128)S(1)}, u32[]{:S(2)}, u32[]{:S(2)}) collective-permute-start(f32[4,64,1024]{2,1,0:T(8,128)S(1)} %pad_maximum_fusion.refs_0_), channel_id=1, source_target_pairs={{0,12},{1,13},{2,14},{3,15},{4,8},{5,9},{6,10},{7,11},{8,4},{9,5},... | collective-permute-start | bytes 3145736 | tf_op jit(solution)/shard_map/ppermute | solution.py:23
  25.4 23.2 %collective-permute-start.6 = (f32[4,64,1024]{2,1,0:T(8,128)S(1)}, f32[4,64,1024]{2,1,0:T(8,128)S(1)}, u32[]{:S(2)}, u32[]{:S(2)}) collective-permute-start(f32[4,64,1024]{2,1,0:T(8,128)S(1)} %pad_maximum_fusion.refs_0_), channel_id=1, source_target_pairs={{0,4},{1,5},{2,6},{3,7},{4,0},{5,1},{6,2},{7,3},{8,12},{9,13},{10,... | collective-permute-start | bytes 3145736 | tf_op jit(solution)/shard_map/ppermute | solution.py:23
  47.2 7.7 %copy-start.1 = (f32[4,64,1024]{2,1,0:T(8,128)}, f32[4,64,1024]{2,1,0:T(8,128)S(1)}, u32[]{:S(2)}) copy-start(f32[4,64,1024]{2,1,0:T(8,128)S(1)} %collective-permute-done.4.refs_2_) | copy-start | bytes 3145732
  48.6 5.4 %copy-start.3 = (f32[4,64,1024]{2,1,0:T(8,128)}, f32[4,64,1024]{2,1,0:T(8,128)S(1)}, u32[]{:S(2)}) copy-start(f32[4,64,1024]{2,1,0:T(8,128)S(1)} %collective-permute-done.6.refs_4_) | copy-start | bytes 3145732
  48.6 26.1 %collective-permute-start.5 = (f32[4,64,1024]{2,1,0:T(8,128)S(1)}, f32[4,64,1024]{2,1,0:T(8,128)S(1)}, u32[]{:S(2)}, u32[]{:S(2)}) collective-permute-start(f32[4,64,1024]{2,1,0:T(8,128)S(1)} %collective-permute-done.3._.refs_1_), channel_id=1, source_target_pairs={{0,12},{1,13},{2,14},{3,15},{4,8},{5,9},{6,10},{7,11},{8,4},{9,5},... | collective-permute-start | bytes 3145736 | tf_op jit(solution)/shard_map/ppermute | solution.py:23
  50.2 22.3 %collective-permute-start.7 = (f32[4,64,1024]{2,1,0:T(8,128)S(1)}, f32[4,64,1024]{2,1,0:T(8,128)S(1)}, u32[]{:S(2)}, u32[]{:S(2)}) collective-permute-start(f32[4,64,1024]{2,1,0:T(8,128)S(1)} %collective-permute-done.3._.refs_1_), channel_id=1, source_target_pairs={{0,4},{1,5},{2,6},{3,7},{4,0},{5,1},{6,2},{7,3},{8,12},{9,13},{10,... | collective-permute-start | bytes 3145736 | tf_op jit(solution)/shard_map/ppermute | solution.py:23
  51.3 25.2 %collective-permute-start.8 = (f32[1024,256]{1,0:T(8,128)S(1)}, f32[1024,256]{1,0:T(8,128)S(1)}, u32[]{:S(2)}, u32[]{:S(2)}) collective-permute-start(f32[1024,256]{1,0:T(8,128)S(1)} %get-tuple-element.22), channel_id=1, source_target_pairs={{0,1},{1,0},{2,3},{3,2},{4,5},{5,4},{6,7},{7,6},{8,9},{9,8},{10,11... | collective-permute-start | bytes 3145736 | tf_op jit(solution)/shard_map/ppermute | solution.py:23
  52.4 27.0 %collective-permute-start.9 = (f32[1024,256]{1,0:T(8,128)S(1)}, f32[1024,256]{1,0:T(8,128)S(1)}, u32[]{:S(2)}, u32[]{:S(2)}) collective-permute-start(f32[1024,256]{1,0:T(8,128)S(1)} %get-tuple-element.23), channel_id=1, source_target_pairs={{0,3},{1,2},{2,1},{3,0},{4,7},{5,6},{6,5},{7,4},{8,11},{9,10},{10,... | collective-permute-start | bytes 3145736 | tf_op jit(solution)/shard_map/ppermute | solution.py:23
  52.6 30.6 %collective-permute-start.10 = (f32[1024,256]{1,0:T(8,128)}, f32[1024,256]{1,0:T(8,128)}, u32[]{:S(2)}, u32[]{:S(2)}) collective-permute-start(f32[1024,256]{1,0:T(8,128)} %get-tuple-element.24), channel_id=1, source_target_pairs={{0,16},{1,17},{2,18},{3,19},{4,20},{5,21},{6,22},{7,23},{8,24},{9,... | collective-permute-start | bytes 3145736 | tf_op jit(solution)/shard_map/ppermute | solution.py:23
  72.5 25.3 %collective-permute-start.11 = (f32[2,64,1024]{2,1,0:T(8,128)}, f32[2,64,1024]{2,1,0:T(8,128)}, u32[]{:S(2)}, u32[]{:S(2)}) collective-permute-start(f32[2,64,1024]{2,1,0:T(8,128)} %slice.80), channel_id=1, source_target_pairs={{0,12},{1,13},{2,14},{3,15},{4,8},{5,9},{6,10},{7,11},{8,4},{9,5},... | collective-permute-start | bytes 1572872 | tf_op jit(solution)/shard_map/ppermute | solution.py:23
  74.7 23.0 %collective-permute-start.12 = (f32[2,64,1024]{2,1,0:T(8,128)}, f32[2,64,1024]{2,1,0:T(8,128)}, u32[]{:S(2)}, u32[]{:S(2)}) collective-permute-start(f32[2,64,1024]{2,1,0:T(8,128)} %slice.81), channel_id=1, source_target_pairs={{0,4},{1,5},{2,6},{3,7},{4,0},{5,1},{6,2},{7,3},{8,12},{9,13},{10,... | collective-permute-start | bytes 1572872 | tf_op jit(solution)/shard_map/ppermute | solution.py:23
  75.5 1.0 copy-start.5
  76.5 1.0 copy-start.8
  77.5 20.2 %collective-permute-start.13 = (f32[2,64,1024]{2,1,0:T(8,128)}, f32[2,64,1024]{2,1,0:T(8,128)}, u32[]{:S(2)}, u32[]{:S(2)}) collective-permute-start(f32[2,64,1024]{2,1,0:T(8,128)} %slice.82), channel_id=1, source_target_pairs={{0,12},{1,13},{2,14},{3,15},{4,8},{5,9},{6,10},{7,11},{8,4},{9,5},... | collective-permute-start | bytes 1572872 | tf_op jit(solution)/shard_map/ppermute | solution.py:23
  79.4 1.0 copy-start.10
  80.4 17.4 %collective-permute-start.14 = (f32[2,64,1024]{2,1,0:T(8,128)}, f32[2,64,1024]{2,1,0:T(8,128)}, u32[]{:S(2)}, u32[]{:S(2)}) collective-permute-start(f32[2,64,1024]{2,1,0:T(8,128)} %slice.83), channel_id=1, source_target_pairs={{0,4},{1,5},{2,6},{3,7},{4,0},{5,1},{6,2},{7,3},{8,12},{9,13},{10,... | collective-permute-start | bytes 1572872 | tf_op jit(solution)/shard_map/ppermute | solution.py:23
  81.8 1.5 %copy-start.9 = (f32[1024,256]{1,0:T(8,128)S(1)}, f32[1024,256]{1,0:T(8,128)}, u32[]{:S(2)}) copy-start(f32[1024,256]{1,0:T(8,128)} %copy-done.8) | copy-start | bytes 3145732
  81.8 1.9 %copy-start.11 = (f32[1024,256]{1,0:T(8,128)S(1)}, f32[1024,256]{1,0:T(8,128)}, u32[]{:S(2)}) copy-start(f32[1024,256]{1,0:T(8,128)} %copy-done.10) | copy-start | bytes 3145732
  83.6 2.1 %copy-start.2 = (f32[4,64,1024]{2,1,0:T(8,128)S(1)}, f32[4,64,1024]{2,1,0:T(8,128)}, u32[]{:S(2)}) copy-start(f32[4,64,1024]{2,1,0:T(8,128)} %copy-done.1) | copy-start | bytes 3145732
  83.6 2.1 %copy-start.4 = (f32[4,64,1024]{2,1,0:T(8,128)S(1)}, f32[4,64,1024]{2,1,0:T(8,128)}, u32[]{:S(2)}) copy-start(f32[4,64,1024]{2,1,0:T(8,128)} %copy-done.3) | copy-start | bytes 3145732
  83.6 2.2 %copy-start.6 = (f32[4,64,1024]{2,1,0:T(8,128)S(1)}, f32[4,64,1024]{2,1,0:T(8,128)}, u32[]{:S(2)}) copy-start(f32[4,64,1024]{2,1,0:T(8,128)} %copy-done.5) | copy-start | bytes 3145732
  97.7 7.2 %collective-permute-start.15 = (f32[4,2,4,64,256]{4,3,2,1,0:T(8,128)}, f32[4,2,4,64,256]{4,3,2,1,0:T(8,128)S(1)}, u32[]{:S(2)}, u32[]{:S(2)}) collective-permute-start(f32[4,2,4,64,256]{4,3,2,1,0:T(8,128)} %get-tuple-element.29), channel_id=1, source_target_pairs={{0,32},{1,33},{2,34},{3,35},{4,36},{5,37},{6,38},{7,39},{8,40},{9,... | collective-permute-start | bytes 6291464 | tf_op jit(solution)/shard_map/ppermute | solution.py:23
  97.8 1.6 %copy-start.7 = (f32[4,2,4,64,256]{4,3,2,1,0:T(8,128)S(1)}, f32[4,2,4,64,256]{4,3,2,1,0:T(8,128)}, u32[]{:S(2)}) copy-start(f32[4,2,4,64,256]{4,3,2,1,0:T(8,128)} %get-tuple-element.32.refs_6_) | copy-start | bytes 6291460
  104.4 4.7 %collective-permute-start.20 = (f32[4,2,4,64,256]{4,3,2,1,0:T(8,128)S(1)}, f32[4,2,4,64,256]{4,3,2,1,0:T(8,128)S(1)}, u32[]{:S(2)}, u32[]{:S(2)}) collective-permute-start(f32[4,2,4,64,256]{4,3,2,1,0:T(8,128)S(1)} %get-tuple-element.34), channel_id=1, source_target_pairs={{0,32},{1,33},{2,34},{3,35},{4,36},{5,37},{6,38},{7,39},{8,40},{9,... | collective-permute-start | bytes 6291464 | tf_op jit(solution)/shard_map/ppermute | solution.py:23
  106.2 14.8 %collective-permute-start.16 = (f32[2,4,64,256]{3,2,1,0:T(8,128)S(1)}, f32[2,4,64,256]{3,2,1,0:T(8,128)S(1)}, u32[]{:S(2)}, u32[]{:S(2)}) collective-permute-start(f32[2,4,64,256]{3,2,1,0:T(8,128)S(1)} %get-tuple-element.43), channel_id=1, source_target_pairs={{0,1},{1,0},{2,3},{3,2},{4,5},{5,4},{6,7},{7,6},{8,9},{9,8},{10,11... | collective-permute-start | bytes 1572872 | tf_op jit(solution)/shard_map/ppermute | solution.py:23
  107.5 16.2 %collective-permute-start.17 = (f32[2,4,64,256]{3,2,1,0:T(8,128)}, f32[2,4,64,256]{3,2,1,0:T(8,128)S(1)}, u32[]{:S(2)}, u32[]{:S(2)}) collective-permute-start(f32[2,4,64,256]{3,2,1,0:T(8,128)} %get-tuple-element.42), channel_id=1, source_target_pairs={{0,3},{1,2},{2,1},{3,0},{4,7},{5,6},{6,5},{7,4},{8,11},{9,10},{10,... | collective-permute-start | bytes 1572872 | tf_op jit(solution)/shard_map/ppermute | solution.py:23
  107.6 16.1 %collective-permute-start.18 = (f32[2,4,64,256]{3,2,1,0:T(8,128)}, f32[2,4,64,256]{3,2,1,0:T(8,128)}, u32[]{:S(2)}, u32[]{:S(2)}) collective-permute-start(f32[2,4,64,256]{3,2,1,0:T(8,128)} %get-tuple-element.41), channel_id=1, source_target_pairs={{0,16},{1,17},{2,18},{3,19},{4,20},{5,21},{6,22},{7,23},{8,24},{9,... | collective-permute-start | bytes 1572872 | tf_op jit(solution)/shard_map/ppermute | solution.py:23
  110.4 20.9 %collective-permute-start.21 = (f32[2,4,64,256]{3,2,1,0:T(8,128)}, f32[2,4,64,256]{3,2,1,0:T(8,128)S(1)}, u32[]{:S(2)}, u32[]{:S(2)}) collective-permute-start(f32[2,4,64,256]{3,2,1,0:T(8,128)} %get-tuple-element.39), channel_id=1, source_target_pairs={{0,1},{1,0},{2,3},{3,2},{4,5},{5,4},{6,7},{7,6},{8,9},{9,8},{10,11... | collective-permute-start | bytes 1572872 | tf_op jit(solution)/shard_map/ppermute | solution.py:23
  111.7 22.0 %collective-permute-start.22 = (f32[2,4,64,256]{3,2,1,0:T(8,128)}, f32[2,4,64,256]{3,2,1,0:T(8,128)S(1)}, u32[]{:S(2)}, u32[]{:S(2)}) collective-permute-start(f32[2,4,64,256]{3,2,1,0:T(8,128)} %get-tuple-element.38), channel_id=1, source_target_pairs={{0,3},{1,2},{2,1},{3,0},{4,7},{5,6},{6,5},{7,4},{8,11},{9,10},{10,... | collective-permute-start | bytes 1572872 | tf_op jit(solution)/shard_map/ppermute | solution.py:23
  121.0 15.2 %collective-permute-start.23 = (f32[2,4,64,256]{3,2,1,0:T(8,128)}, f32[2,4,64,256]{3,2,1,0:T(8,128)}, u32[]{:S(2)}, u32[]{:S(2)}) collective-permute-start(f32[2,4,64,256]{3,2,1,0:T(8,128)} %get-tuple-element.37), channel_id=1, source_target_pairs={{0,16},{1,17},{2,18},{3,19},{4,20},{5,21},{6,22},{7,23},{8,24},{9,... | collective-permute-start | bytes 1572872 | tf_op jit(solution)/shard_map/ppermute | solution.py:23
  125.6 17.5 %collective-permute-start.19 = (f32[4,64,256]{2,1,0:T(8,128)}, f32[4,64,256]{2,1,0:T(8,128)S(1)}, u32[]{:S(2)}, u32[]{:S(2)}) collective-permute-start(f32[4,64,256]{2,1,0:T(8,128)} %get-tuple-element.31), channel_id=1, source_target_pairs={{0,64},{1,65},{2,66},{3,67},{4,68},{5,69},{6,70},{7,71},{8,72},{9,... | collective-permute-start | bytes 786440 | tf_op jit(solution)/shard_map/ppermute | solution.py:23
  137.3 8.8 %collective-permute-start.24 = (f32[4,64,256]{2,1,0:T(8,128)S(1)}, f32[4,64,256]{2,1,0:T(8,128)S(1)}, u32[]{:S(2)}, u32[]{:S(2)}) collective-permute-start(f32[4,64,256]{2,1,0:T(8,128)S(1)} %get-tuple-element.36), channel_id=1, source_target_pairs={{0,64},{1,65},{2,66},{3,67},{4,68},{5,69},{6,70},{7,71},{8,72},{9,... | collective-permute-start | bytes 786440 | tf_op jit(solution)/shard_map/ppermute | solution.py:23

commit v8 on v7

--- a/solution.py
+++ b/solution.py
@@ -6,7 +6,7 @@
 from jax.sharding import PartitionSpec as P
 
 AXES = ("rep", "grid")
-PARAMS = pltpu.CompilerParams(vmem_limit_bytes=40 * 1024 * 1024)
+PARAMS = pltpu.CompilerParams(vmem_limit_bytes=26 * 1024 * 1024)
 SHORT = pl.CostEstimate(flops=1, bytes_accessed=1, transcendentals=0)
 NEAR = (dict(), dict(dy=1), dict(dy=3), dict(dx=1))
 
@@ -36,13 +36,14 @@
 VMEM = pl.BlockSpec(memory_space=pltpu.VMEM)
 
 
-def call(kernel, scalars, values, in_specs, out_shape, out_specs, scratch=()):
+def call(kernel, scalars, values, in_specs, out_shape, out_specs, scratch=(), aliases=None):
     return pl.pallas_call(
         kernel,
         grid_spec=pltpu.PrefetchScalarGridSpec(
             num_scalar_prefetch=1, grid=(1,), in_specs=in_specs, out_specs=out_specs, scratch_shapes=scratch
         ),
         out_shape=out_shape,
+        input_output_aliases=aliases or {},
         compiler_params=PARAMS,
         cost_estimate=SHORT,
     )(scalars, *values)
@@ -98,68 +99,68 @@
         total = jnp.dot(left_high[...], high[:, span], preferred_element_type=jnp.float32)
         total += jnp.dot(left_high[...], low[:, span], preferred_element_type=jnp.float32)
         total += jnp.dot(left_low[...], high[:, span], preferred_element_type=jnp.float32)
-        store(d, total.reshape(-1, 2, 4, blocks[0].shape[1], columns))
+        store(d, total.reshape(-1, 4, blocks[0].shape[1], columns))
 
 
 def places(d):
-    return [(part, block, part ^ (d == 3), block ^ (0, 1, 3, 2)[d]) for part in range(2) for block in range(4)]
-
-
-def flat(planes):
-    return [array for plane in planes for part in plane for array in part]
-
-
-def early_products(swap, pair, ahead, rights, earlier):
-    arrays = flat([*pair, ahead])
+    return [(block, block ^ (0, 1, 3, 2)[d]) for block in range(4)]
+
+
+def early_products(swap, part, planes, rights, earlier, before=()):
+    arrays = [array for plane in planes for array in plane]
     rows, depth = arrays[0].shape[1:]
     columns = rights[0].shape[1] // 4
+    unread = [*earlier, *before]
 
     def kernel(swap, *refs):
-        blocks, rest = refs[: len(arrays)], refs[len(arrays) + len(earlier):]
+        blocks, rest = refs[: len(arrays)], refs[len(arrays) + len(unread):]
         high, low, keep, give, third, left_high, left_low = rest
         swapped = swap[0] == 1
 
         def store(d, total):
-            for part, block, to_part, to_block in places(d):
-                zero, one = total[0, part, block], total[1, part, block]
-                keep[d, to_part, to_block] = jnp.where(swapped, one, zero)
-                give[d, to_part, to_block] = jnp.where(swapped, zero, one)
-                third[d, to_part, to_block] = total[2, part, block]
+            for block, into in places(d):
+                zero, one = total[0, block], total[1, block]
+                keep[d, 0, into] = jnp.where(swapped, one, zero)
+                give[d, 0, into] = jnp.where(swapped, zero, one)
+                third[d, 0, into] = total[2, block]
 
         multiplied(blocks, left_high, left_low, high, low, store)
 
     shape = jax.ShapeDtypeStruct((4, 2, 4, rows, columns), jnp.float32)
-    scratch = pltpu.VMEM((24 * rows, depth), jnp.bfloat16)
-    return call(
-        kernel, swap, (*arrays, *earlier, *rights),
-        [whole(array) for array in arrays] + [ANYWHERE] * len(earlier) + [VMEM] * 2,
-        [shape] * 3, [whole(shape)] * 3, [scratch] * 2,
-    )
-
-
-def late_products(swap, plane, third, rights, earlier):
-    arrays = flat([plane])
+    out = pl.BlockSpec((4, 1, 4, rows, columns), lambda *_: (0, part, 0, 0, 0), pipeline_mode=pl.Buffered(1))
+    scratch = pltpu.VMEM((12 * rows, depth), jnp.bfloat16)
+    first = 1 + len(arrays) + len(earlier)
+    return call(
+        kernel, swap, (*arrays, *unread, *rights),
+        [whole(array) for array in arrays] + [ANYWHERE] * len(unread) + [VMEM] * 2,
+        [shape] * 3, [out] * 3, [scratch] * 2, {first + at: at for at in range(len(before))},
+    )
+
+
+def late_products(swap, parts, third, rights):
+    arrays = [array for part in parts for array in part]
     rows, depth = arrays[0].shape[1:]
     columns = rights[0].shape[1] // 4
 
     def kernel(swap, *refs):
-        blocks, rest = refs[: len(arrays)], refs[len(arrays) + len(earlier):]
+        blocks, rest = refs[: len(arrays)], refs[len(arrays):]
         high, low, ahead, keep, give, left_high, left_low = rest
         swapped = swap[0] == 1
 
         def store(d, total):
-            for part, block, to_part, to_block in places(d):
-                zero, one = ahead[d, to_part, to_block], total[0, part, block]
-                keep[d, to_part, to_block] = jnp.where(swapped, one, zero)
-                give[d, to_part, to_block] = jnp.where(swapped, zero, one)
+            for part in range(2):
+                for block, into in places(d):
+                    zero, one = ahead[d, part, into], total[part, block]
+                    keep[d, part, into] = jnp.where(swapped, one, zero)
+                    give[d, part, into] = jnp.where(swapped, zero, one)
 
         multiplied(blocks, left_high, left_low, high, low, store)
 
     shape = jax.ShapeDtypeStruct((4, 2, 4, rows, columns), jnp.float32)
     scratch = pltpu.VMEM((8 * rows, depth), jnp.bfloat16)
     return call(
-        kernel, swap, (*arrays, *earlier, *rights, third),
-        [whole(array) for array in arrays] + [ANYWHERE] * len(earlier) + [VMEM] * 2 + [whole(third)],
+        kernel, swap, (*arrays, *rights, third),
+        [whole(array) for array in arrays] + [VMEM] * 2 + [whole(third)],
         [shape] * 2, [whole(shape)] * 2, [scratch] * 2,
     )
 
@@ -167,10 +168,8 @@
 def sum_kernel(side, *refs):
     terms, (mine, theirs) = refs[:-2], refs[-2:]
     for out, part in ((mine, side[0]), (theirs, 1 - side[0])):
-        total = terms[0][part]
-        for term in terms[1:]:
-            total = total + term[part]
-        out[...] = total
+        across = terms[3][1 - part]
+        out[...] = (terms[0][part] + terms[1][part]) + (terms[2][part] + across)
 
 
 def summed(side, terms):
@@ -208,27 +207,25 @@
     mine = jnp.stack([block(0), send(block(1), dy=1), send(block(3), dy=2), send(block(2), dy=3)])
     other = send(mine, dx=1, dy=2)
 
-    planes = []
-    for part in (mine, other):
-        one, three = send(part, dz=1), send(part, dz=3)
-        two = send(one[:2], dz=3), send(three[2:], dz=1)
-        planes.append(((part,), (one,), two, (three,)))
+    own_one, own_three = send(mine, dz=1), send(mine, dz=3)
+    far, *_ = lax.optimization_barrier((other, own_one, own_three))
+    far_one, far_three = lax.optimization_barrier((send(far, dz=1), send(far, dz=3)))
+
+    own_two, far_two = send(own_three, dz=1), send(far_one, dz=3)
 
     pieces = [lax.dynamic_slice(right, (quarter * depth, 0), (depth, columns))]
-    (ready, *_) = lax.optimization_barrier((other, planes[0][1][0], planes[0][3][0]))
-    for d, piece in enumerate(cut_after(quarter.reshape(1), right, ready)):
+    for d, piece in enumerate(cut_after(quarter.reshape(1), right, other)):
         pieces.append(send(piece, **NEAR[d + 1]))
     rights = split(swap, pieces)
 
-    late = [*planes[0][2], *planes[1][2]]
-    zero, one, two, three = ([part[dz] for part in planes] for dz in range(4))
-    keep, give, third = early_products(swap, (zero, three), one, rights, [planes[1][1][0]])
+    before = early_products(swap, 0, ((mine,), (own_three,), (own_one,)), rights, [])
+    keep, give, third = early_products(swap, 1, ((far,), (far_three,), (far_one,)), rights, [], before)
     ends = []
     for last in (False, True):
         if last:
-            keep, give = late_products(swap, two, third, rights, [])
+            keep, give = late_products(swap, ((own_two,), (far_two,)), third, rights)
         else:
-            give, *_ = lax.optimization_barrier((give, *late))
+            give, *_ = lax.optimization_barrier((give, own_two, far_two))
         got = send(give, core=1)
         sums = [keep[d] + got[d] for d in range(4)]
         terms = [sums[0]] + [send(sums[d], **NEAR[d]) for d in range(1, 4)]

time: 148 us -> 145 us (0.980)
  local copies, waits for them, and re-layouts: 11.3 us -> 4.76 us
  Pallas kernels: 24.4 us -> 26 us
    slice x4 -> x0, local copies, waits for them, and re-layouts: 3.4 us -> none  [per_device(): two = (send(one[:2], dz=3), send(three[2:], dz=1))]
    unnamed x24 -> x10, local copies, waits for them, and re-layouts: 5.02 us -> 2.03 us
    pallas_call x7 -> x8, Pallas kernels: 24.4 us -> 26 us  [call(): pl.pallas_call(kernel, grid_spec=pltpu.PrefetchScalarGridSpec(num_scalar_...]
    ppermute x25 -> x23, starting transfers between devices: 33.1 us -> 34.3 us  [send(): return lax.ppermute(value, AXES, pairs)]
    ppermute x25 -> x23, waiting for transfers between devices: 75.9 us -> 76.8 us  [send(): return lax.ppermute(value, AXES, pairs)]
  transfers between devices with their start and end apart: 25 -> 23, of which waited for: 13 -> 17; matrix products, arithmetic and copies ran while one was open for 5% -> 3% of each run, Pallas kernels for 16% -> 17%
where the time goes in v8:
time: 145 us
  waiting for transfers between devices  76.8 us (53%)
  starting transfers between devices  34.3 us (24%)
  Pallas kernels  26 us (18%)
  local copies, waits for them, and re-layouts  4.76 us (3%)
  other arithmetic  2.69 us (2%)
    ppermute x23, waiting for transfers between devices, send(): return lax.ppermute(value, AXES, pairs)  76.8 us
    ppermute x23, starting transfers between devices, send(): return lax.ppermute(value, AXES, pairs)  34.3 us
    pallas_call x8, Pallas kernels, call(): pl.pallas_call(kernel, grid_spec=pltpu.PrefetchScalarGridSpec(num_scalar_...  26 us
  transfers between devices with their start and end apart: 23, of which 17 were waited for; matrix products, arithmetic and copies ran while one was open for 3% of the time, Pallas kernels for 17%

profile of v8, /device:TPU:0, one launch (start us, length us, event | category | flops | bytes accessed | tf_op | source)
XLA Modules:
  0.0 144.7 jit_solution(15238146571947478063)
XLA Ops:
  0.0 1.4 dynamic-slice_bitcast_fusion
  1.4 3.2 %collective-permute-start.2 = (f32[64,1024]{1,0:T(8,128)S(1)}, f32[64,1024]{1,0:T(8,128)S(1)}, u32[]{:S(2)}, u32[]{:S(2)}) collective-permute-start(f32[64,1024]{1,0:T(8,128)S(1)} %get-tuple-element.57), channel_id=1, source_target_pairs={{0,3},{1,2},{2,1},{3,0},{4,7},{5,6},{6,5},{7,4},{8,11},{9,10},{10,... | collective-permute-start | bytes 786440 | tf_op jit(solution)/shard_map/ppermute | solution.py:23
  4.6 0.6 collective-permute-start.1
  5.3 0.4 collective-permute-start
  5.6 10.9 %collective-permute-done.2 = f32[64,1024]{1,0:T(8,128)S(1)} collective-permute-done((f32[64,1024]{1,0:T(8,128)S(1)}, f32[64,1024]{1,0:T(8,128)S(1)}, u32[]{:S(2)}, u32[]{:S(2)}) %collective-permute-start.2) | collective-permute-done | bytes 262176 | tf_op jit(solution)/shard_map/ppermute | solution.py:23
  16.6 0.0 collective-permute-done.1
  16.6 0.7 collective-permute-done
  17.3 0.1 pad_maximum_fusion.refs_0_
  17.3 4.0 %collective-permute-start.3 = (f32[4,64,1024]{2,1,0:T(8,128)S(1)}, f32[4,64,1024]{2,1,0:T(8,128)S(1)}, u32[]{:S(2)}, u32[]{:S(2)}) collective-permute-start(f32[4,64,1024]{2,1,0:T(8,128)S(1)} %pad_maximum_fusion.refs_0_), channel_id=1, source_target_pairs={{0,18},{1,19},{2,16},{3,17},{4,22},{5,23},{6,20},{7,21},{8,26},{9,... | collective-permute-start | bytes 3145736 | tf_op jit(solution)/shard_map/ppermute | solution.py:23
  21.4 1.9 %collective-permute-start.4 = (f32[4,64,1024]{2,1,0:T(8,128)S(1)}, f32[4,64,1024]{2,1,0:T(8,128)S(1)}, u32[]{:S(2)}, u32[]{:S(2)}) collective-permute-start(f32[4,64,1024]{2,1,0:T(8,128)S(1)} %pad_maximum_fusion.refs_0_), channel_id=1, source_target_pairs={{0,4},{1,5},{2,6},{3,7},{4,0},{5,1},{6,2},{7,3},{8,12},{9,13},{10,... | collective-permute-start | bytes 3145736 | tf_op jit(solution)/shard_map/ppermute | solution.py:23
  23.3 2.5 %collective-permute-start.5 = (f32[4,64,1024]{2,1,0:T(8,128)S(1)}, f32[4,64,1024]{2,1,0:T(8,128)}, u32[]{:S(2)}, u32[]{:S(2)}) collective-permute-start(f32[4,64,1024]{2,1,0:T(8,128)S(1)} %pad_maximum_fusion.refs_0_), channel_id=1, source_target_pairs={{0,12},{1,13},{2,14},{3,15},{4,8},{5,9},{6,10},{7,11},{8,4},{9,5},... | collective-permute-start | bytes 3145736 | tf_op jit(solution)/shard_map/ppermute | solution.py:23
  25.8 18.0 %collective-permute-done.3._.refs_0_ = f32[4,64,1024]{2,1,0:T(8,128)S(1)} collective-permute-done((f32[4,64,1024]{2,1,0:T(8,128)S(1)}, f32[4,64,1024]{2,1,0:T(8,128)S(1)}, u32[]{:S(2)}, u32[]{:S(2)}) %collective-permute-start.3) | collective-permute-done | bytes 1048608 | tf_op jit(solution)/shard_map/ppermute | solution.py:23
  43.8 1.2 collective-permute-done.4.refs_2_
  45.0 1.0 copy-done.1
  46.0 1.8 %collective-permute-done.5.refs_1_ = f32[4,64,1024]{2,1,0:T(8,128)} collective-permute-done((f32[4,64,1024]{2,1,0:T(8,128)S(1)}, f32[4,64,1024]{2,1,0:T(8,128)}, u32[]{:S(2)}, u32[]{:S(2)}) %collective-permute-start.5) | collective-permute-done | bytes 1048608 | tf_op jit(solution)/shard_map/ppermute | solution.py:23
  47.8 0.6 collective-permute-start.6
  48.4 2.3 %collective-permute-start.7 = (f32[4,64,1024]{2,1,0:T(8,128)S(1)}, f32[4,64,1024]{2,1,0:T(8,128)S(1)}, u32[]{:S(2)}, u32[]{:S(2)}) collective-permute-start(f32[4,64,1024]{2,1,0:T(8,128)S(1)} %collective-permute-done.3._.refs_0_), channel_id=1, source_target_pairs={{0,12},{1,13},{2,14},{3,15},{4,8},{5,9},{6,10},{7,11},{8,4},{9,5},... | collective-permute-start | bytes 3145736 | tf_op jit(solution)/shard_map/ppermute | solution.py:23
  50.7 0.0 copy-done
  50.8 1.7 %shard_map.28 = (f32[1024,256]{1,0:T(8,128)}, f32[1024,256]{1,0:T(8,128)}, f32[1024,256]{1,0:T(8,128)}) custom-call(s32[1]{0:T(128)} %bitcast.8.quarter, f32[4096,256]{1,0:T(8,128)S(1)} %copy-done, f32[4,64,1024]{2,1,0:T(8,128)S(1)} %collective-permute-done.3._.refs_0_), custom_call_target="tpu_custom_call" | custom-call | flops 1 | bytes 1 | tf_op jit(solution)/shard_map/pallas_call | solution.py:40
  52.5 1.1 collective-permute-start.8
  53.6 0.9 collective-permute-start.9
  54.5 1.5 %collective-permute-start.10 = (f32[1024,256]{1,0:T(8,128)}, f32[1024,256]{1,0:T(8,128)}, u32[]{:S(2)}, u32[]{:S(2)}) collective-permute-start(f32[1024,256]{1,0:T(8,128)} %get-tuple-element.31), channel_id=1, source_target_pairs={{0,16},{1,17},{2,18},{3,19},{4,20},{5,21},{6,22},{7,23},{8,24},{9,... | collective-permute-start | bytes 3145736 | tf_op jit(solution)/shard_map/ppermute | solution.py:23
  55.9 15.0 %collective-permute-done.6.refs_2_ = f32[4,64,1024]{2,1,0:T(8,128)} collective-permute-done((f32[4,64,1024]{2,1,0:T(8,128)S(1)}, f32[4,64,1024]{2,1,0:T(8,128)}, u32[]{:S(2)}, u32[]{:S(2)}) %collective-permute-start.6) | collective-permute-done | bytes 1048608 | tf_op jit(solution)/shard_map/ppermute | solution.py:23
  70.9 0.6 collective-permute-start.11
  71.5 0.4 collective-permute-done.7.refs_1_
  71.9 1.0 copy-done.3
  72.9 2.1 %collective-permute-start.12 = (f32[4,64,1024]{2,1,0:T(8,128)}, f32[4,64,1024]{2,1,0:T(8,128)}, u32[]{:S(2)}, u32[]{:S(2)}) collective-permute-start(f32[4,64,1024]{2,1,0:T(8,128)} %collective-permute-done.6.refs_2_), channel_id=1, source_target_pairs={{0,12},{1,13},{2,14},{3,15},{4,8},{5,9},{6,10},{7,11},{8,4},{9,5},... | collective-permute-start | bytes 3145736 | tf_op jit(solution)/shard_map/ppermute | solution.py:23
  75.0 1.3 constant_dynamic-slice_fusion.refs_0_
  76.3 0.0 collective-permute-done.8.refs_1_
  76.3 0.5 collective-permute-done.9.refs_2_
  76.8 0.0 collective-permute-done.10.refs_3_
  76.8 2.7 %shard_map.29 = (bf16[1024,1024]{1,0:T(8,128)(2,1)S(1)}, bf16[1024,1024]{1,0:T(8,128)(2,1)S(1)}) custom-call(s32[1]{0:T(128)} %bitcast.3._.swap, f32[1024,256]{1,0:T(8,128)S(1)} %constant_dynamic-slice_fusion.refs_0_, f32[1024,256]{1,0:T(8,128)} %collective-permute-done.8.refs_1_, f32[1024,256]{1,0:T(8,128)} %collective-permute-done.9.refs_2_, ...), custom_call_target="tpu_custom_call" | custom-call | flops 1 | bytes 1 | tf_op jit(solution)/shard_map/pallas_call | solution.py:40
  79.5 0.0 copy-done.2
  79.5 6.3 %shard_map.30 = (f32[4,2,4,64,256]{4,3,2,1,0:T(8,128)S(1)}, f32[4,2,4,64,256]{4,3,2,1,0:T(8,128)S(1)}, f32[4,2,4,64,256]{4,3,2,1,0:T(8,128)S(1)}) custom-call(s32[1]{0:T(128)} %bitcast.3._.swap, f32[4,64,1024]{2,1,0:T(8,128)S(1)} %pad_maximum_fusion.refs_0_, f32[4,64,1024]{2,1,0:T(8,128)} %collective-permute-done.5.refs_1_, f32[4,64,1024]{2,1,0:T(8,128)S(1)} %copy-done.2, ...), custom_call_target="tpu_custom_call" | custom-call | flops 1 | bytes 1 | tf_op jit(solution)/shard_map/pallas_call | solution.py:40
  85.9 6.3 %shard_map.31 = (f32[4,2,4,64,256]{4,3,2,1,0:T(8,128)S(1)}, f32[4,2,4,64,256]{4,3,2,1,0:T(8,128)S(1)}, f32[4,2,4,64,256]{4,3,2,1,0:T(8,128)S(1)}) custom-call(s32[1]{0:T(128)} %bitcast.3._.swap, f32[4,64,1024]{2,1,0:T(8,128)S(1)} %collective-permute-done.3._.refs_0_, ...), custom_call_target="tpu_custom_call", output_to_operand_aliasing={{0}: (4, {}), {1}: (5, {}), {2}: (6, {})} | custom-call | flops 1 | bytes 1 | tf_op jit(solution)/shard_map/pallas_call | solution.py:40
  92.1 0.4 collective-permute-done.11.refs_0_
  92.6 3.3 %collective-permute-done.12.refs_1_ = f32[4,64,1024]{2,1,0:T(8,128)} collective-permute-done((f32[4,64,1024]{2,1,0:T(8,128)}, f32[4,64,1024]{2,1,0:T(8,128)}, u32[]{:S(2)}, u32[]{:S(2)}) %collective-permute-start.12) | collective-permute-done | bytes 1048608 | tf_op jit(solution)/shard_map/ppermute | solution.py:23
  95.9 0.0 collective-permute-start.13
  95.9 4.6 %shard_map.33 = (f32[4,2,4,64,256]{4,3,2,1,0:T(8,128)S(1)}, f32[4,2,4,64,256]{4,3,2,1,0:T(8,128)S(1)}) custom-call(s32[1]{0:T(128)} %bitcast.3._.swap, f32[4,64,1024]{2,1,0:T(8,128)S(1)} %collective-permute-done.11.refs_0_, f32[4,64,1024]{2,1,0:T(8,128)} %collective-permute-done.12.refs_1_, bf16[1024,1024]{1,0:T(8,128)(2,1)S(1)} %get-tuple-element.32.refs_3_.refs_6_.refs_2_, ...), custom_call_target="tpu_custom_call" | custom-call | flops 1 | bytes 1 | tf_op jit(solution)/shard_map/pallas_call | solution.py:40
  100.5 0.6 collective-permute-start.18
  101.1 0.0 collective-permute-done.13
  101.1 1.2 fusion.4
  102.4 1.5 %collective-permute-start.14 = (f32[2,4,64,256]{3,2,1,0:T(8,128)S(1)}, f32[2,4,64,256]{3,2,1,0:T(8,128)S(1)}, u32[]{:S(2)}, u32[]{:S(2)}) collective-permute-start(f32[2,4,64,256]{3,2,1,0:T(8,128)S(1)} %get-tuple-element.53), channel_id=1, source_target_pairs={{0,1},{1,0},{2,3},{3,2},{4,5},{5,4},{6,7},{7,6},{8,9},{9,8},{10,11... | collective-permute-start | bytes 1572872 | tf_op jit(solution)/shard_map/ppermute | solution.py:23
  103.9 0.9 collective-permute-start.15
  104.8 1.5 %collective-permute-start.16 = (f32[2,4,64,256]{3,2,1,0:T(8,128)}, f32[2,4,64,256]{3,2,1,0:T(8,128)}, u32[]{:S(2)}, u32[]{:S(2)}) collective-permute-start(f32[2,4,64,256]{3,2,1,0:T(8,128)} %get-tuple-element.51), channel_id=1, source_target_pairs={{0,16},{1,17},{2,18},{3,19},{4,20},{5,21},{6,22},{7,23},{8,24},{9,... | collective-permute-start | bytes 1572872 | tf_op jit(solution)/shard_map/ppermute | solution.py:23
  106.3 0.0 collective-permute-done.18
  106.3 1.3 fusion
  107.6 1.4 collective-permute-start.19
  109.0 0.6 collective-permute-start.20
  109.6 7.5 %collective-permute-done.14.refs_1_ = f32[2,4,64,256]{3,2,1,0:T(8,128)S(1)} collective-permute-done((f32[2,4,64,256]{3,2,1,0:T(8,128)S(1)}, f32[2,4,64,256]{3,2,1,0:T(8,128)S(1)}, u32[]{:S(2)}, u32[]{:S(2)}) %collective-permute-start.14) | collective-permute-done | bytes 524320 | tf_op jit(solution)/shard_map/ppermute | solution.py:23
  117.2 0.5 collective-permute-start.21
  117.7 2.4 %collective-permute-done.15.refs_2_ = f32[2,4,64,256]{3,2,1,0:T(8,128)S(1)} collective-permute-done((f32[2,4,64,256]{3,2,1,0:T(8,128)}, f32[2,4,64,256]{3,2,1,0:T(8,128)S(1)}, u32[]{:S(2)}, u32[]{:S(2)}) %collective-permute-start.15) | collective-permute-done | bytes 524320 | tf_op jit(solution)/shard_map/ppermute | solution.py:23
  120.1 0.0 collective-permute-done.16.refs_3_
  120.1 1.8 %shard_map.32 = (f32[4,64,256]{2,1,0:T(8,128)S(1)}, f32[4,64,256]{2,1,0:T(8,128)}) custom-call(s32[1]{0:T(128)} %bitcast.2.side, f32[2,4,64,256]{3,2,1,0:T(8,128)S(1)} %get-tuple-element.54.refs_0_, f32[2,4,64,256]{3,2,1,0:T(8,128)S(1)} %collective-permute-done.14.refs_1_, f32[2,4,64,256]{3,2,1,0:T(8,128)S(1)} %collective-permute-done.15.refs_2_, ...), custom_call_target="tpu_custom_call" | custom-call | flops 1 | bytes 1 | tf_op jit(solution)/shard_map/pallas_call | solution.py:40
  122.0 2.7 %collective-permute-start.17 = (f32[4,64,256]{2,1,0:T(8,128)}, f32[4,64,256]{2,1,0:T(8,128)S(1)}, u32[]{:S(2)}, u32[]{:S(2)}) collective-permute-start(f32[4,64,256]{2,1,0:T(8,128)} %get-tuple-element.41), channel_id=1, source_target_pairs={{0,64},{1,65},{2,66},{3,67},{4,68},{5,69},{6,70},{7,71},{8,72},{9,... | collective-permute-start | bytes 786440 | tf_op jit(solution)/shard_map/ppermute | solution.py:23
  124.7 2.8 %collective-permute-done.19.refs_1_ = f32[2,4,64,256]{3,2,1,0:T(8,128)S(1)} collective-permute-done((f32[2,4,64,256]{3,2,1,0:T(8,128)}, f32[2,4,64,256]{3,2,1,0:T(8,128)S(1)}, u32[]{:S(2)}, u32[]{:S(2)}) %collective-permute-start.19) | collective-permute-done | bytes 524320 | tf_op jit(solution)/shard_map/ppermute | solution.py:23
  127.5 2.6 %collective-permute-done.20.refs_2_ = f32[2,4,64,256]{3,2,1,0:T(8,128)S(1)} collective-permute-done((f32[2,4,64,256]{3,2,1,0:T(8,128)}, f32[2,4,64,256]{3,2,1,0:T(8,128)S(1)}, u32[]{:S(2)}, u32[]{:S(2)}) %collective-permute-start.20) | collective-permute-done | bytes 524320 | tf_op jit(solution)/shard_map/ppermute | solution.py:23
  130.1 2.2 %collective-permute-done.21.refs_3_ = f32[2,4,64,256]{3,2,1,0:T(8,128)} collective-permute-done((f32[2,4,64,256]{3,2,1,0:T(8,128)}, f32[2,4,64,256]{3,2,1,0:T(8,128)}, u32[]{:S(2)}, u32[]{:S(2)}) %collective-permute-start.21) | collective-permute-done | bytes 524320 | tf_op jit(solution)/shard_map/ppermute | solution.py:23
  132.3 1.1 shard_map.34
  133.5 2.8 %collective-permute-start.22 = (f32[4,64,256]{2,1,0:T(8,128)S(1)}, f32[4,64,256]{2,1,0:T(8,128)S(1)}, u32[]{:S(2)}, u32[]{:S(2)}) collective-permute-start(f32[4,64,256]{2,1,0:T(8,128)S(1)} %get-tuple-element.46), channel_id=1, source_target_pairs={{0,64},{1,65},{2,66},{3,67},{4,68},{5,69},{6,70},{7,71},{8,72},{9,... | collective-permute-start | bytes 786440 | tf_op jit(solution)/shard_map/ppermute | solution.py:23
  136.3 0.1 pad_add_fusion.place
  136.4 3.0 %collective-permute-done.17.other_one = f32[4,64,256]{2,1,0:T(8,128)S(1)} collective-permute-done((f32[4,64,256]{2,1,0:T(8,128)}, f32[4,64,256]{2,1,0:T(8,128)S(1)}, u32[]{:S(2)}, u32[]{:S(2)}) %collective-permute-start.17) | collective-permute-done | bytes 262176 | tf_op jit(solution)/shard_map/ppermute | solution.py:23
  139.4 3.9 %collective-permute-done.22.other_two = f32[4,64,256]{2,1,0:T(8,128)S(1)} collective-permute-done((f32[4,64,256]{2,1,0:T(8,128)S(1)}, f32[4,64,256]{2,1,0:T(8,128)S(1)}, u32[]{:S(2)}, u32[]{:S(2)}) %collective-permute-start.22) | collective-permute-done | bytes 262176 | tf_op jit(solution)/shard_map/ppermute | solution.py:23
  143.3 1.4 shard_map.35
  (6 shorter events, 0.0 us)
Async XLA Ops:
  0.0 50.8 %copy-start = (f32[4096,256]{1,0:T(8,128)S(1)}, f32[4096,256]{1,0:T(8,128)}, u32[]{:S(2)}) copy-start(f32[4096,256]{1,0:T(8,128)} %value.1) | copy-start | bytes 12582916
  1.4 15.1 %collective-permute-start.2 = (f32[64,1024]{1,0:T(8,128)S(1)}, f32[64,1024]{1,0:T(8,128)S(1)}, u32[]{:S(2)}, u32[]{:S(2)}) collective-permute-start(f32[64,1024]{1,0:T(8,128)S(1)} %get-tuple-element.57), channel_id=1, source_target_pairs={{0,3},{1,2},{2,1},{3,0},{4,7},{5,6},{6,5},{7,4},{8,11},{9,10},{10,... | collective-permute-start | bytes 786440 | tf_op jit(solution)/shard_map/ppermute | solution.py:23
  4.6 11.9 %collective-permute-start.1 = (f32[64,1024]{1,0:T(8,128)S(1)}, f32[64,1024]{1,0:T(8,128)S(1)}, u32[]{:S(2)}, u32[]{:S(2)}) collective-permute-start(f32[64,1024]{1,0:T(8,128)S(1)} %get-tuple-element.58), channel_id=1, source_target_pairs={{0,2},{1,3},{2,0},{3,1},{4,6},{5,7},{6,4},{7,5},{8,10},{9,11},{10,... | collective-permute-start | bytes 786440 | tf_op jit(solution)/shard_map/ppermute | solution.py:23
  5.3 12.0 %collective-permute-start = (f32[64,1024]{1,0:T(8,128)S(1)}, f32[64,1024]{1,0:T(8,128)S(1)}, u32[]{:S(2)}, u32[]{:S(2)}) collective-permute-start(f32[64,1024]{1,0:T(8,128)S(1)} %get-tuple-element.56), channel_id=1, source_target_pairs={{0,1},{1,0},{2,3},{3,2},{4,5},{5,4},{6,7},{7,6},{8,9},{9,8},{10,11... | collective-permute-start | bytes 786440 | tf_op jit(solution)/shard_map/ppermute | solution.py:23
  17.3 26.5 %collective-permute-start.3 = (f32[4,64,1024]{2,1,0:T(8,128)S(1)}, f32[4,64,1024]{2,1,0:T(8,128)S(1)}, u32[]{:S(2)}, u32[]{:S(2)}) collective-permute-start(f32[4,64,1024]{2,1,0:T(8,128)S(1)} %pad_maximum_fusion.refs_0_), channel_id=1, source_target_pairs={{0,18},{1,19},{2,16},{3,17},{4,22},{5,23},{6,20},{7,21},{8,26},{9,... | collective-permute-start | bytes 3145736 | tf_op jit(solution)/shard_map/ppermute | solution.py:23
  21.4 23.6 %collective-permute-start.4 = (f32[4,64,1024]{2,1,0:T(8,128)S(1)}, f32[4,64,1024]{2,1,0:T(8,128)S(1)}, u32[]{:S(2)}, u32[]{:S(2)}) collective-permute-start(f32[4,64,1024]{2,1,0:T(8,128)S(1)} %pad_maximum_fusion.refs_0_), channel_id=1, source_target_pairs={{0,4},{1,5},{2,6},{3,7},{4,0},{5,1},{6,2},{7,3},{8,12},{9,13},{10,... | collective-permute-start | bytes 3145736 | tf_op jit(solution)/shard_map/ppermute | solution.py:23
  23.3 24.5 %collective-permute-start.5 = (f32[4,64,1024]{2,1,0:T(8,128)S(1)}, f32[4,64,1024]{2,1,0:T(8,128)}, u32[]{:S(2)}, u32[]{:S(2)}) collective-permute-start(f32[4,64,1024]{2,1,0:T(8,128)S(1)} %pad_maximum_fusion.refs_0_), channel_id=1, source_target_pairs={{0,12},{1,13},{2,14},{3,15},{4,8},{5,9},{6,10},{7,11},{8,4},{9,5},... | collective-permute-start | bytes 3145736 | tf_op jit(solution)/shard_map/ppermute | solution.py:23
  45.0 1.0 copy-start.1
  47.8 23.1 %collective-permute-start.6 = (f32[4,64,1024]{2,1,0:T(8,128)S(1)}, f32[4,64,1024]{2,1,0:T(8,128)}, u32[]{:S(2)}, u32[]{:S(2)}) collective-permute-start(f32[4,64,1024]{2,1,0:T(8,128)S(1)} %collective-permute-done.3._.refs_0_), channel_id=1, source_target_pairs={{0,4},{1,5},{2,6},{3,7},{4,0},{5,1},{6,2},{7,3},{8,12},{9,13},{10,... | collective-permute-start | bytes 3145736 | tf_op jit(solution)/shard_map/ppermute | solution.py:23
  48.4 23.5 %collective-permute-start.7 = (f32[4,64,1024]{2,1,0:T(8,128)S(1)}, f32[4,64,1024]{2,1,0:T(8,128)S(1)}, u32[]{:S(2)}, u32[]{:S(2)}) collective-permute-start(f32[4,64,1024]{2,1,0:T(8,128)S(1)} %collective-permute-done.3._.refs_0_), channel_id=1, source_target_pairs={{0,12},{1,13},{2,14},{3,15},{4,8},{5,9},{6,10},{7,11},{8,4},{9,5},... | collective-permute-start | bytes 3145736 | tf_op jit(solution)/shard_map/ppermute | solution.py:23
  52.5 23.8 %collective-permute-start.8 = (f32[1024,256]{1,0:T(8,128)}, f32[1024,256]{1,0:T(8,128)}, u32[]{:S(2)}, u32[]{:S(2)}) collective-permute-start(f32[1024,256]{1,0:T(8,128)} %get-tuple-element.29), channel_id=1, source_target_pairs={{0,1},{1,0},{2,3},{3,2},{4,5},{5,4},{6,7},{7,6},{8,9},{9,8},{10,11... | collective-permute-start | bytes 3145736 | tf_op jit(solution)/shard_map/ppermute | solution.py:23
  53.6 23.3 %collective-permute-start.9 = (f32[1024,256]{1,0:T(8,128)}, f32[1024,256]{1,0:T(8,128)}, u32[]{:S(2)}, u32[]{:S(2)}) collective-permute-start(f32[1024,256]{1,0:T(8,128)} %get-tuple-element.30), channel_id=1, source_target_pairs={{0,3},{1,2},{2,1},{3,0},{4,7},{5,6},{6,5},{7,4},{8,11},{9,10},{10,... | collective-permute-start | bytes 3145736 | tf_op jit(solution)/shard_map/ppermute | solution.py:23
  54.5 22.4 %collective-permute-start.10 = (f32[1024,256]{1,0:T(8,128)}, f32[1024,256]{1,0:T(8,128)}, u32[]{:S(2)}, u32[]{:S(2)}) collective-permute-start(f32[1024,256]{1,0:T(8,128)} %get-tuple-element.31), channel_id=1, source_target_pairs={{0,16},{1,17},{2,18},{3,19},{4,20},{5,21},{6,22},{7,23},{8,24},{9,... | collective-permute-start | bytes 3145736 | tf_op jit(solution)/shard_map/ppermute | solution.py:23
  70.9 21.6 %collective-permute-start.11 = (f32[4,64,1024]{2,1,0:T(8,128)}, f32[4,64,1024]{2,1,0:T(8,128)S(1)}, u32[]{:S(2)}, u32[]{:S(2)}) collective-permute-start(f32[4,64,1024]{2,1,0:T(8,128)} %collective-permute-done.5.refs_1_), channel_id=1, source_target_pairs={{0,4},{1,5},{2,6},{3,7},{4,0},{5,1},{6,2},{7,3},{8,12},{9,13},{10,... | collective-permute-start | bytes 3145736 | tf_op jit(solution)/shard_map/ppermute | solution.py:23
  71.9 1.0 copy-start.3
  72.9 23.0 %collective-permute-start.12 = (f32[4,64,1024]{2,1,0:T(8,128)}, f32[4,64,1024]{2,1,0:T(8,128)}, u32[]{:S(2)}, u32[]{:S(2)}) collective-permute-start(f32[4,64,1024]{2,1,0:T(8,128)} %collective-permute-done.6.refs_2_), channel_id=1, source_target_pairs={{0,12},{1,13},{2,14},{3,15},{4,8},{5,9},{6,10},{7,11},{8,4},{9,5},... | collective-permute-start | bytes 3145736 | tf_op jit(solution)/shard_map/ppermute | solution.py:23
  76.8 2.7 %copy-start.2 = (f32[4,64,1024]{2,1,0:T(8,128)S(1)}, f32[4,64,1024]{2,1,0:T(8,128)}, u32[]{:S(2)}) copy-start(f32[4,64,1024]{2,1,0:T(8,128)} %copy-done.1) | copy-start | bytes 3145732
  79.5 6.4 %copy-start.4 = (f32[4,64,1024]{2,1,0:T(8,128)S(1)}, f32[4,64,1024]{2,1,0:T(8,128)}, u32[]{:S(2)}) copy-start(f32[4,64,1024]{2,1,0:T(8,128)} %copy-done.3) | copy-start | bytes 3145732
  95.9 5.2 %collective-permute-start.13 = (f32[4,2,4,64,256]{4,3,2,1,0:T(8,128)S(1)}, f32[4,2,4,64,256]{4,3,2,1,0:T(8,128)S(1)}, u32[]{:S(2)}, u32[]{:S(2)}) collective-permute-start(f32[4,2,4,64,256]{4,3,2,1,0:T(8,128)S(1)} %get-tuple-element.39), channel_id=1, source_target_pairs={{0,32},{1,33},{2,34},{3,35},{4,36},{5,37},{6,38},{7,39},{8,40},{9,... | collective-permute-start | bytes 6291464 | tf_op jit(solution)/shard_map/ppermute | solution.py:23
  100.5 5.8 %collective-permute-start.18 = (f32[4,2,4,64,256]{4,3,2,1,0:T(8,128)S(1)}, f32[4,2,4,64,256]{4,3,2,1,0:T(8,128)S(1)}, u32[]{:S(2)}, u32[]{:S(2)}) collective-permute-start(f32[4,2,4,64,256]{4,3,2,1,0:T(8,128)S(1)} %get-tuple-element.44), channel_id=1, source_target_pairs={{0,32},{1,33},{2,34},{3,35},{4,36},{5,37},{6,38},{7,39},{8,40},{9,... | collective-permute-start | bytes 6291464 | tf_op jit(solution)/shard_map/ppermute | solution.py:23
  102.4 14.8 %collective-permute-start.14 = (f32[2,4,64,256]{3,2,1,0:T(8,128)S(1)}, f32[2,4,64,256]{3,2,1,0:T(8,128)S(1)}, u32[]{:S(2)}, u32[]{:S(2)}) collective-permute-start(f32[2,4,64,256]{3,2,1,0:T(8,128)S(1)} %get-tuple-element.53), channel_id=1, source_target_pairs={{0,1},{1,0},{2,3},{3,2},{4,5},{5,4},{6,7},{7,6},{8,9},{9,8},{10,11... | collective-permute-start | bytes 1572872 | tf_op jit(solution)/shard_map/ppermute | solution.py:23
  103.9 16.2 %collective-permute-start.15 = (f32[2,4,64,256]{3,2,1,0:T(8,128)}, f32[2,4,64,256]{3,2,1,0:T(8,128)S(1)}, u32[]{:S(2)}, u32[]{:S(2)}) collective-permute-start(f32[2,4,64,256]{3,2,1,0:T(8,128)} %get-tuple-element.52), channel_id=1, source_target_pairs={{0,3},{1,2},{2,1},{3,0},{4,7},{5,6},{6,5},{7,4},{8,11},{9,10},{10,... | collective-permute-start | bytes 1572872 | tf_op jit(solution)/shard_map/ppermute | solution.py:23
  104.8 15.3 %collective-permute-start.16 = (f32[2,4,64,256]{3,2,1,0:T(8,128)}, f32[2,4,64,256]{3,2,1,0:T(8,128)}, u32[]{:S(2)}, u32[]{:S(2)}) collective-permute-start(f32[2,4,64,256]{3,2,1,0:T(8,128)} %get-tuple-element.51), channel_id=1, source_target_pairs={{0,16},{1,17},{2,18},{3,19},{4,20},{5,21},{6,22},{7,23},{8,24},{9,... | collective-permute-start | bytes 1572872 | tf_op jit(solution)/shard_map/ppermute | solution.py:23
  107.6 19.9 %collective-permute-start.19 = (f32[2,4,64,256]{3,2,1,0:T(8,128)}, f32[2,4,64,256]{3,2,1,0:T(8,128)S(1)}, u32[]{:S(2)}, u32[]{:S(2)}) collective-permute-start(f32[2,4,64,256]{3,2,1,0:T(8,128)} %get-tuple-element.49), channel_id=1, source_target_pairs={{0,1},{1,0},{2,3},{3,2},{4,5},{5,4},{6,7},{7,6},{8,9},{9,8},{10,11... | collective-permute-start | bytes 1572872 | tf_op jit(solution)/shard_map/ppermute | solution.py:23
  109.0 21.1 %collective-permute-start.20 = (f32[2,4,64,256]{3,2,1,0:T(8,128)}, f32[2,4,64,256]{3,2,1,0:T(8,128)S(1)}, u32[]{:S(2)}, u32[]{:S(2)}) collective-permute-start(f32[2,4,64,256]{3,2,1,0:T(8,128)} %get-tuple-element.48), channel_id=1, source_target_pairs={{0,3},{1,2},{2,1},{3,0},{4,7},{5,6},{6,5},{7,4},{8,11},{9,10},{10,... | collective-permute-start | bytes 1572872 | tf_op jit(solution)/shard_map/ppermute | solution.py:23
  117.2 15.2 %collective-permute-start.21 = (f32[2,4,64,256]{3,2,1,0:T(8,128)}, f32[2,4,64,256]{3,2,1,0:T(8,128)}, u32[]{:S(2)}, u32[]{:S(2)}) collective-permute-start(f32[2,4,64,256]{3,2,1,0:T(8,128)} %get-tuple-element.47), channel_id=1, source_target_pairs={{0,16},{1,17},{2,18},{3,19},{4,20},{5,21},{6,22},{7,23},{8,24},{9,... | collective-permute-start | bytes 1572872 | tf_op jit(solution)/shard_map/ppermute | solution.py:23
  122.0 17.4 %collective-permute-start.17 = (f32[4,64,256]{2,1,0:T(8,128)}, f32[4,64,256]{2,1,0:T(8,128)S(1)}, u32[]{:S(2)}, u32[]{:S(2)}) collective-permute-start(f32[4,64,256]{2,1,0:T(8,128)} %get-tuple-element.41), channel_id=1, source_target_pairs={{0,64},{1,65},{2,66},{3,67},{4,68},{5,69},{6,70},{7,71},{8,72},{9,... | collective-permute-start | bytes 786440 | tf_op jit(solution)/shard_map/ppermute | solution.py:23
  133.5 9.8 %collective-permute-start.22 = (f32[4,64,256]{2,1,0:T(8,128)S(1)}, f32[4,64,256]{2,1,0:T(8,128)S(1)}, u32[]{:S(2)}, u32[]{:S(2)}) collective-permute-start(f32[4,64,256]{2,1,0:T(8,128)S(1)} %get-tuple-element.46), channel_id=1, source_target_pairs={{0,64},{1,65},{2,66},{3,67},{4,68},{5,69},{6,70},{7,71},{8,72},{9,... | collective-permute-start | bytes 786440 | tf_op jit(solution)/shard_map/ppermute | solution.py:23

commit v9 on v8

--- a/solution.py
+++ b/solution.py
@@ -54,7 +54,7 @@
     depth = outs[0].shape[0]
     copies = []
     for d, out in enumerate(outs):
-        at = pl.ds(pl.multiple_of((quarter[0] ^ (d + 1)) * depth, depth), depth)
+        at = pl.ds(pl.multiple_of((quarter[0] ^ d) * depth, depth), depth)
         copies.append(pltpu.make_async_copy(value.at[at], out, sems.at[d]))
     for copy in copies:
         copy.start()
@@ -65,8 +65,8 @@
 def cut_after(quarter, value, earlier):
     shape = jax.ShapeDtypeStruct((value.shape[0] // 4, value.shape[1]), value.dtype)
     return call(
-        cut_kernel, quarter, (value, earlier), [ANYWHERE] * 2, [shape] * 3, [ANYWHERE] * 3,
-        [pltpu.SemaphoreType.DMA((3,))],
+        cut_kernel, quarter, (value, earlier), [ANYWHERE] * 2, [shape] * 4, [ANYWHERE] * 4,
+        [pltpu.SemaphoreType.DMA((4,))],
     )
 
 
@@ -103,54 +103,65 @@
 
 
 def places(d):
-    return [(block, block ^ (0, 1, 3, 2)[d]) for block in range(4)]
-
-
-def early_products(swap, part, planes, rights, earlier, before=()):
+    return [(block, block ^ (0, 1, 3, 0)[d]) for block in range(4)]
+
+
+def early_products(swap, planes, rights):
     arrays = [array for plane in planes for array in plane]
     rows, depth = arrays[0].shape[1:]
     columns = rights[0].shape[1] // 4
-    unread = [*earlier, *before]
 
     def kernel(swap, *refs):
-        blocks, rest = refs[: len(arrays)], refs[len(arrays) + len(unread):]
-        high, low, keep, give, third, left_high, left_low = rest
+        blocks, (high, low, keep, third, give, give_too, left_high, left_low) = refs[: len(arrays)], refs[len(arrays):]
         swapped = swap[0] == 1
 
         def store(d, total):
             for block, into in places(d):
                 zero, one = total[0, block], total[1, block]
-                keep[d, 0, into] = jnp.where(swapped, one, zero)
-                give[d, 0, into] = jnp.where(swapped, zero, one)
-                third[d, 0, into] = total[2, block]
+                keep[d, into] = jnp.where(swapped, one, zero)
+                (give_too if d > 1 else give)[d % 2, into] = jnp.where(swapped, zero, one)
+                third[d, into] = total[2, block]
 
         multiplied(blocks, left_high, left_low, high, low, store)
 
-    shape = jax.ShapeDtypeStruct((4, 2, 4, rows, columns), jnp.float32)
-    out = pl.BlockSpec((4, 1, 4, rows, columns), lambda *_: (0, part, 0, 0, 0), pipeline_mode=pl.Buffered(1))
+    kept, given = (jax.ShapeDtypeStruct((count, 4, rows, columns), jnp.float32) for count in (4, 2))
     scratch = pltpu.VMEM((12 * rows, depth), jnp.bfloat16)
-    first = 1 + len(arrays) + len(earlier)
-    return call(
-        kernel, swap, (*arrays, *unread, *rights),
-        [whole(array) for array in arrays] + [ANYWHERE] * len(unread) + [VMEM] * 2,
-        [shape] * 3, [out] * 3, [scratch] * 2, {first + at: at for at in range(len(before))},
-    )
-
-
-def late_products(swap, parts, third, rights):
+    shapes = [kept, kept, given, given]
+    return call(
+        kernel, swap, (*arrays, *rights), [whole(array) for array in arrays] + [VMEM] * 2,
+        shapes, [whole(shape) for shape in shapes], [scratch] * 2,
+    )
+
+
+def added_kernel(_, *refs):
+    keeps, gots, outs = refs[:2], refs[2:6], refs[-4:]
+    for part, keep in enumerate(keeps):
+        for d, out in enumerate(outs):
+            out[part] = keep[d] + gots[2 * part + d // 2][d % 2]
+
+
+def added(scalars, keeps, gots, after):
+    shape = jax.ShapeDtypeStruct((2, *keeps[0].shape[1:]), jnp.float32)
+    return call(
+        added_kernel, scalars, (*keeps, *gots, *after),
+        [whole(value) for value in (*keeps, *gots)] + [ANYWHERE] * len(after), [shape] * 4, [whole(shape)] * 4,
+    )
+
+
+def late_products(swap, parts, thirds, rights, after):
     arrays = [array for part in parts for array in part]
     rows, depth = arrays[0].shape[1:]
     columns = rights[0].shape[1] // 4
 
     def kernel(swap, *refs):
-        blocks, rest = refs[: len(arrays)], refs[len(arrays):]
-        high, low, ahead, keep, give, left_high, left_low = rest
+        blocks, rest = refs[: len(arrays)], refs[len(arrays) + len(after):]
+        high, low, ahead, ahead_too, keep, give, left_high, left_low = rest
         swapped = swap[0] == 1
 
         def store(d, total):
             for part in range(2):
                 for block, into in places(d):
-                    zero, one = ahead[d, part, into], total[part, block]
+                    zero, one = (ahead, ahead_too)[part][d, into], total[part, block]
                     keep[d, part, into] = jnp.where(swapped, one, zero)
                     give[d, part, into] = jnp.where(swapped, zero, one)
 
@@ -159,8 +170,8 @@
     shape = jax.ShapeDtypeStruct((4, 2, 4, rows, columns), jnp.float32)
     scratch = pltpu.VMEM((8 * rows, depth), jnp.bfloat16)
     return call(
-        kernel, swap, (*arrays, *rights, third),
-        [whole(array) for array in arrays] + [VMEM] * 2 + [whole(third)],
+        kernel, swap, (*arrays, *after, *rights, *thirds),
+        [whole(array) for array in arrays] + [ANYWHERE] * len(after) + [VMEM] * 2 + [whole(third) for third in thirds],
         [shape] * 2, [whole(shape)] * 2, [scratch] * 2,
     )
 
@@ -205,7 +216,7 @@
         return lax.dynamic_slice(left, (0, (quarter ^ d) * depth), (rows, depth))
 
     mine = jnp.stack([block(0), send(block(1), dy=1), send(block(3), dy=2), send(block(2), dy=3)])
-    other = send(mine, dx=1, dy=2)
+    other = jnp.stack([send(block(3), dx=1), send(block(2), dx=1, dy=1), send(block(0), dx=1, dy=2), send(block(1), dx=1, dy=3)])
 
     own_one, own_three = send(mine, dz=1), send(mine, dz=3)
     far, *_ = lax.optimization_barrier((other, own_one, own_three))
@@ -213,26 +224,30 @@
 
     own_two, far_two = send(own_three, dz=1), send(far_one, dz=3)
 
-    pieces = [lax.dynamic_slice(right, (quarter * depth, 0), (depth, columns))]
-    for d, piece in enumerate(cut_after(quarter.reshape(1), right, other)):
-        pieces.append(send(piece, **NEAR[d + 1]))
+    pieces = cut_after(quarter.reshape(1), right, other)
+    pieces = [pieces[0]] + [send(pieces[d], **NEAR[d]) for d in range(1, 4)]
     rights = split(swap, pieces)
 
-    before = early_products(swap, 0, ((mine,), (own_three,), (own_one,)), rights, [])
-    keep, give, third = early_products(swap, 1, ((far,), (far_three,), (far_one,)), rights, [], before)
+    keeps, thirds, gots = [], [], []
+    for part in ((mine, own_one, own_three), (far, far_one, far_three)):
+        keep, third, *gives = early_products(swap, [(part[0],), (part[2],), (part[1],)], rights)
+        keeps.append(keep)
+        thirds.append(third)
+        gots += [send(give, core=1) for give in gives]
+
     ends = []
     for last in (False, True):
         if last:
-            keep, give = late_products(swap, ((own_two,), (far_two,)), third, rights)
+            keep, give = late_products(swap, ((own_two,), (far_two,)), thirds, rights, sums[1:])
+            got = send(give, core=1)
+            sums = [keep[d] + got[d] for d in range(4)]
         else:
-            give, *_ = lax.optimization_barrier((give, own_two, far_two))
-        got = send(give, core=1)
-        sums = [keep[d] + got[d] for d in range(4)]
+            sums = added(swap, keeps, gots, [])
         terms = [sums[0]] + [send(sums[d], **NEAR[d]) for d in range(1, 4)]
         here, there = summed(side, terms)
         ends += [here, send(there, dhi=1)]
 
-    total = join(jnp.stack([(z & 1) ^ swap[0], y ^ (2 * side[0])]), ends)
+    total = join(jnp.stack([(z & 1) ^ swap[0], y]), ends)
     return total.reshape(8 * rows, columns)
 
 

time: 145 us -> 157 us (1.083)
  waiting for transfers between devices: 76.8 us -> 90.5 us
  starting transfers between devices: 34.3 us -> 37.2 us
  Pallas kernels: 26 us -> 23.8 us
    ppermute x23 -> x29, waiting for transfers between devices: 76.8 us -> 90.5 us  [send(): return lax.ppermute(value, AXES, pairs)]
    ppermute x23 -> x29, starting transfers between devices: 34.3 us -> 37.2 us  [send(): return lax.ppermute(value, AXES, pairs)]
    pallas_call x8 -> x9, Pallas kernels: 26 us -> 23.8 us  [call(): pl.pallas_call(kernel, grid_spec=pltpu.PrefetchScalarGridSpec(num_scalar_...]
  transfers between devices with their start and end apart: 23 -> 29, of which waited for: 17 -> 20; matrix products, arithmetic and copies ran while one was open for 3% -> 1% of each run, Pallas kernels for 17% -> 12%
where the time goes in v9:
time: 157 us; the launch traced here: 156 us
  waiting for transfers between devices  90.5 us (58%)
  starting transfers between devices  37.2 us (24%)
  Pallas kernels  23.8 us (15%)
  local copies, waits for them, and re-layouts  3.27 us (2%)
    ppermute x29, waiting for transfers between devices, send(): return lax.ppermute(value, AXES, pairs)  90.5 us
    ppermute x29, starting transfers between devices, send(): return lax.ppermute(value, AXES, pairs)  37.2 us
    pallas_call x9, Pallas kernels, call(): pl.pallas_call(kernel, grid_spec=pltpu.PrefetchScalarGridSpec(num_scalar_...  23.8 us
  transfers between devices with their start and end apart: 29, of which 20 were waited for; matrix products, arithmetic and copies ran while one was open for 1% of the time, Pallas kernels for 12%

profile of v9, /device:TPU:0, one launch (start us, length us, event | category | flops | bytes accessed | tf_op | source)
XLA Modules:
  0.0 156.4 jit_solution(3038859400760041242)
XLA Ops:
  0.0 1.3 constant_dynamic-slice_fusion.3
  1.3 3.2 %collective-permute-start.2 = (f32[64,1024]{1,0:T(8,128)S(1)}, f32[64,1024]{1,0:T(8,128)S(1)}, u32[]{:S(2)}, u32[]{:S(2)}) collective-permute-start(f32[64,1024]{1,0:T(8,128)S(1)} %get-tuple-element.65), channel_id=1, source_target_pairs={{0,3},{1,2},{2,1},{3,0},{4,7},{5,6},{6,5},{7,4},{8,11},{9,10},{10,... | collective-permute-start | bytes 786440 | tf_op jit(solution)/shard_map/ppermute | solution.py:23
  4.5 0.6 collective-permute-start.1
  5.1 0.4 collective-permute-start
  5.5 10.9 %collective-permute-done.2 = f32[64,1024]{1,0:T(8,128)S(1)} collective-permute-done((f32[64,1024]{1,0:T(8,128)S(1)}, f32[64,1024]{1,0:T(8,128)S(1)}, u32[]{:S(2)}, u32[]{:S(2)}) %collective-permute-start.2) | collective-permute-done | bytes 262176 | tf_op jit(solution)/shard_map/ppermute | solution.py:23
  16.4 0.7 collective-permute-done
  17.1 0.1 pad_maximum_fusion.refs_0_
  17.2 4.1 %collective-permute-start.3 = (f32[4,64,1024]{2,1,0:T(8,128)S(1)}, f32[4,64,1024]{2,1,0:T(8,128)S(1)}, u32[]{:S(2)}, u32[]{:S(2)}) collective-permute-start(f32[4,64,1024]{2,1,0:T(8,128)S(1)} %pad_maximum_fusion.refs_0_), channel_id=1, source_target_pairs={{0,12},{1,13},{2,14},{3,15},{4,8},{5,9},{6,10},{7,11},{8,4},{9,5},... | collective-permute-start | bytes 3145736 | tf_op jit(solution)/shard_map/ppermute | solution.py:23
  21.3 3.8 %collective-permute-start.8 = (f32[64,1024]{1,0:T(8,128)S(1)}, f32[64,1024]{1,0:T(8,128)S(1)}, u32[]{:S(2)}, u32[]{:S(2)}) collective-permute-start(f32[64,1024]{1,0:T(8,128)S(1)} %get-tuple-element.64), channel_id=1, source_target_pairs={{0,19},{1,18},{2,17},{3,16},{4,23},{5,22},{6,21},{7,20},{8,27},{9,... | collective-permute-start | bytes 786440 | tf_op jit(solution)/shard_map/ppermute | solution.py:23
  25.1 0.6 collective-permute-start.7
  25.7 1.5 collective-permute-start.6
  27.2 5.8 %collective-permute-done.8 = f32[64,1024]{1,0:T(8,128)S(1)} collective-permute-done((f32[64,1024]{1,0:T(8,128)S(1)}, f32[64,1024]{1,0:T(8,128)S(1)}, u32[]{:S(2)}, u32[]{:S(2)}) %collective-permute-start.8) | collective-permute-done | bytes 262176 | tf_op jit(solution)/shard_map/ppermute | solution.py:23
  33.0 1.2 collective-permute-start.5
  34.2 3.7 %collective-permute-done.7 = f32[64,1024]{1,0:T(8,128)S(1)} collective-permute-done((f32[64,1024]{1,0:T(8,128)S(1)}, f32[64,1024]{1,0:T(8,128)S(1)}, u32[]{:S(2)}, u32[]{:S(2)}) %collective-permute-start.7) | collective-permute-done | bytes 262176 | tf_op jit(solution)/shard_map/ppermute | solution.py:23
  37.9 5.8 %collective-permute-done.6 = f32[64,1024]{1,0:T(8,128)S(1)} collective-permute-done((f32[64,1024]{1,0:T(8,128)S(1)}, f32[64,1024]{1,0:T(8,128)S(1)}, u32[]{:S(2)}, u32[]{:S(2)}) %collective-permute-start.6) | collective-permute-done | bytes 262176 | tf_op jit(solution)/shard_map/ppermute | solution.py:23
  43.7 3.7 %collective-permute-done.5 = f32[64,1024]{1,0:T(8,128)S(1)} collective-permute-done((f32[64,1024]{1,0:T(8,128)S(1)}, f32[64,1024]{1,0:T(8,128)S(1)}, u32[]{:S(2)}, u32[]{:S(2)}) %collective-permute-start.5) | collective-permute-done | bytes 262176 | tf_op jit(solution)/shard_map/ppermute | solution.py:23
  47.4 0.1 pad_maximum_fusion.1._.refs_0_
  47.5 1.8 %shard_map.28 = (f32[1024,256]{1,0:T(8,128)S(1)}, f32[1024,256]{1,0:T(8,128)}, f32[1024,256]{1,0:T(8,128)}, f32[1024,256]{1,0:T(8,128)}) custom-call(s32[1]{0:T(128)} %bitcast.8.quarter, f32[4096,256]{1,0:T(8,128)S(1)} %copy-done, f32[4,64,1024]{2,1,0:T(8,128)S(1)} %pad_maximum_fusion.1._.refs_0_), custom_call_target="tpu_custom_call" | custom-call | flops 1 | bytes 1 | tf_op jit(solution)/shard_map/pallas_call | solution.py:40
  49.3 0.1 collective-permute-start.9
  49.4 1.1 collective-permute-start.10
  50.5 1.3 collective-permute-start.11
  51.8 1.0 copy-done.1
  52.7 1.0 copy-done.3
  53.7 1.8 %collective-permute-start.12 = (f32[4,64,1024]{2,1,0:T(8,128)S(1)}, f32[4,64,1024]{2,1,0:T(8,128)}, u32[]{:S(2)}, u32[]{:S(2)}) collective-permute-start(f32[4,64,1024]{2,1,0:T(8,128)S(1)} %pad_maximum_fusion.1._.refs_0_), channel_id=1, source_target_pairs={{0,4},{1,5},{2,6},{3,7},{4,0},{5,1},{6,2},{7,3},{8,12},{9,13},{10,... | collective-permute-start | bytes 3145736 | tf_op jit(solution)/shard_map/ppermute | solution.py:23
  55.5 0.3 collective-permute-start.13
  55.8 16.7 %collective-permute-done.9.refs_1_ = f32[1024,256]{1,0:T(8,128)} collective-permute-done((f32[1024,256]{1,0:T(8,128)}, f32[1024,256]{1,0:T(8,128)}, u32[]{:S(2)}, u32[]{:S(2)}) %collective-permute-start.9) | collective-permute-done | bytes 1048608 | tf_op jit(solution)/shard_map/ppermute | solution.py:23
  72.6 1.3 collective-permute-done.10.refs_2_
  73.9 2.7 %shard_map.29 = (bf16[1024,1024]{1,0:T(8,128)(2,1)S(1)}, bf16[1024,1024]{1,0:T(8,128)(2,1)S(1)}) custom-call(s32[1]{0:T(128)} %bitcast.3._.swap, f32[1024,256]{1,0:T(8,128)S(1)} %get-tuple-element.32.refs_0_, f32[1024,256]{1,0:T(8,128)} %collective-permute-done.9.refs_1_, f32[1024,256]{1,0:T(8,128)} %collective-permute-done.10.refs_2_, ...), custom_call_target="tpu_custom_call" | custom-call | flops 1 | bytes 1 | tf_op jit(solution)/shard_map/pallas_call | solution.py:40
  76.6 5.1 %shard_map.30 = (f32[4,4,64,256]{3,2,1,0:T(8,128)S(1)}, f32[4,4,64,256]{3,2,1,0:T(8,128)S(1)}, f32[2,4,64,256]{3,2,1,0:T(8,128)S(1)}, f32[2,4,64,256]{3,2,1,0:T(8,128)S(1)}) custom-call(s32[1]{0:T(128)} %bitcast.3._.swap, f32[4,64,1024]{2,1,0:T(8,128)S(1)} %pad_maximum_fusion.refs_0_, f32[4,64,1024]{2,1,0:T(8,128)S(1)} %copy-done.2, ...), custom_call_target="tpu_custom_call" | custom-call | flops 1 | bytes 1 | tf_op jit(solution)/shard_map/pallas_call | solution.py:40
  81.7 0.1 collective-permute-start.14
  81.8 1.7 %collective-permute-start.22 = (f32[4,64,1024]{2,1,0:T(8,128)S(1)}, f32[4,64,1024]{2,1,0:T(8,128)S(1)}, u32[]{:S(2)}, u32[]{:S(2)}) collective-permute-start(f32[4,64,1024]{2,1,0:T(8,128)S(1)} %copy-done.2), channel_id=1, source_target_pairs={{0,4},{1,5},{2,6},{3,7},{4,0},{5,1},{6,2},{7,3},{8,12},{9,13},{10,... | collective-permute-start | bytes 3145736 | tf_op jit(solution)/shard_map/ppermute | solution.py:23
  83.5 0.5 collective-permute-start.23
  84.0 0.0 collective-permute-start.15
  84.0 6.6 %shard_map.31 = (f32[4,4,64,256]{3,2,1,0:T(8,128)S(1)}, f32[4,4,64,256]{3,2,1,0:T(8,128)S(1)}, f32[2,4,64,256]{3,2,1,0:T(8,128)S(1)}, f32[2,4,64,256]{3,2,1,0:T(8,128)S(1)}) custom-call(s32[1]{0:T(128)} %bitcast.3._.swap, f32[4,64,1024]{2,1,0:T(8,128)S(1)} %pad_maximum_fusion.1._.refs_0_, f32[4,64,1024]{2,1,0:T(8,128)} %collective-permute-done.13.refs_1_, ...), custom_call_target="tpu_custom_call" | custom-call | flops 1 | bytes 1 | tf_op jit(solution)/shard_map/pallas_call | solution.py:40
  90.6 0.6 collective-permute-start.16
  91.2 0.1 collective-permute-start.17
  91.3 1.4 collective-permute-done.16.refs_4_
  92.7 0.7 collective-permute-done.17.refs_5_
  93.4 0.2 shard_map.32
  93.7 13.7 %collective-permute-done.22.refs_0_ = f32[4,64,1024]{2,1,0:T(8,128)S(1)} collective-permute-done((f32[4,64,1024]{2,1,0:T(8,128)S(1)}, f32[4,64,1024]{2,1,0:T(8,128)S(1)}, u32[]{:S(2)}, u32[]{:S(2)}) %collective-permute-start.22) | collective-permute-done | bytes 1048608 | tf_op jit(solution)/shard_map/ppermute | solution.py:23
  107.3 2.8 %collective-permute-done.23.refs_1_ = f32[4,64,1024]{2,1,0:T(8,128)S(1)} collective-permute-done((f32[4,64,1024]{2,1,0:T(8,128)}, f32[4,64,1024]{2,1,0:T(8,128)S(1)}, u32[]{:S(2)}, u32[]{:S(2)}) %collective-permute-start.23) | collective-permute-done | bytes 1048608 | tf_op jit(solution)/shard_map/ppermute | solution.py:23
  110.1 3.4 %shard_map.34 = (f32[4,2,4,64,256]{4,3,2,1,0:T(8,128)S(1)}, f32[4,2,4,64,256]{4,3,2,1,0:T(8,128)S(1)}) custom-call(s32[1]{0:T(128)} %bitcast.3._.swap, f32[4,64,1024]{2,1,0:T(8,128)S(1)} %collective-permute-done.22.refs_0_, f32[4,64,1024]{2,1,0:T(8,128)S(1)} %collective-permute-done.23.refs_1_, f32[2,4,64,256]{3,2,1,0:T(8,128)S(1)} %get-tuple-element.48.refs_2_, ...), custom_call_target="tpu_custom_call" | custom-call | flops 1 | bytes 1 | tf_op jit(solution)/shard_map/pallas_call | solution.py:40
  113.6 0.1 collective-permute-start.24
  113.6 0.4 collective-permute-start.18
  114.0 2.3 %collective-permute-start.19 = (f32[2,4,64,256]{3,2,1,0:T(8,128)S(1)}, f32[2,4,64,256]{3,2,1,0:T(8,128)}, u32[]{:S(2)}, u32[]{:S(2)}) collective-permute-start(f32[2,4,64,256]{3,2,1,0:T(8,128)S(1)} %get-tuple-element.49.refs_3_), channel_id=1, source_target_pairs={{0,3},{1,2},{2,1},{3,0},{4,7},{5,6},{6,5},{7,4},{8,11},{9,10},{10,... | collective-permute-start | bytes 1572872 | tf_op jit(solution)/shard_map/ppermute | solution.py:23
  116.4 1.5 collective-permute-start.20
  117.9 1.2 fusion
  119.1 0.4 collective-permute-start.25
  119.5 2.2 %collective-permute-start.26 = (f32[2,4,64,256]{3,2,1,0:T(8,128)}, f32[2,4,64,256]{3,2,1,0:T(8,128)}, u32[]{:S(2)}, u32[]{:S(2)}) collective-permute-start(f32[2,4,64,256]{3,2,1,0:T(8,128)} %get-tuple-element.60), channel_id=1, source_target_pairs={{0,3},{1,2},{2,1},{3,0},{4,7},{5,6},{6,5},{7,4},{8,11},{9,10},{10,... | collective-permute-start | bytes 1572872 | tf_op jit(solution)/shard_map/ppermute | solution.py:23
  121.7 6.8 %collective-permute-done.18.refs_1_ = f32[2,4,64,256]{3,2,1,0:T(8,128)S(1)} collective-permute-done((f32[2,4,64,256]{3,2,1,0:T(8,128)S(1)}, f32[2,4,64,256]{3,2,1,0:T(8,128)S(1)}, u32[]{:S(2)}, u32[]{:S(2)}) %collective-permute-start.18) | collective-permute-done | bytes 524320 | tf_op jit(solution)/shard_map/ppermute | solution.py:23
  128.5 1.3 collective-permute-start.27
  129.8 0.3 collective-permute-done.19.refs_2_
  130.1 0.1 collective-permute-done.20.refs_3_
  130.2 1.3 shard_map.33
  131.5 3.1 %collective-permute-start.21 = (f32[4,64,256]{2,1,0:T(8,128)S(1)}, f32[4,64,256]{2,1,0:T(8,128)S(1)}, u32[]{:S(2)}, u32[]{:S(2)}) collective-permute-start(f32[4,64,256]{2,1,0:T(8,128)S(1)} %get-tuple-element.52), channel_id=1, source_target_pairs={{0,64},{1,65},{2,66},{3,67},{4,68},{5,69},{6,70},{7,71},{8,72},{9,... | collective-permute-start | bytes 786440 | tf_op jit(solution)/shard_map/ppermute | solution.py:23
  134.6 4.6 %collective-permute-done.25.refs_1_ = f32[2,4,64,256]{3,2,1,0:T(8,128)S(1)} collective-permute-done((f32[2,4,64,256]{3,2,1,0:T(8,128)}, f32[2,4,64,256]{3,2,1,0:T(8,128)S(1)}, u32[]{:S(2)}, u32[]{:S(2)}) %collective-permute-start.25) | collective-permute-done | bytes 524320 | tf_op jit(solution)/shard_map/ppermute | solution.py:23
  139.2 1.3 collective-permute-done.26.refs_2_
  140.5 3.1 %collective-permute-done.27.refs_3_ = f32[2,4,64,256]{3,2,1,0:T(8,128)} collective-permute-done((f32[2,4,64,256]{3,2,1,0:T(8,128)}, f32[2,4,64,256]{3,2,1,0:T(8,128)}, u32[]{:S(2)}, u32[]{:S(2)}) %collective-permute-start.27) | collective-permute-done | bytes 524320 | tf_op jit(solution)/shard_map/ppermute | solution.py:23
  143.6 1.3 shard_map.35
  144.9 3.0 %collective-permute-start.28 = (f32[4,64,256]{2,1,0:T(8,128)S(1)}, f32[4,64,256]{2,1,0:T(8,128)S(1)}, u32[]{:S(2)}, u32[]{:S(2)}) collective-permute-start(f32[4,64,256]{2,1,0:T(8,128)S(1)} %get-tuple-element.58), channel_id=1, source_target_pairs={{0,64},{1,65},{2,66},{3,67},{4,68},{5,69},{6,70},{7,71},{8,72},{9,... | collective-permute-start | bytes 786440 | tf_op jit(solution)/shard_map/ppermute | solution.py:23
  147.9 0.1 pad_add_fusion.place
  148.0 3.2 %collective-permute-done.21.other_one = f32[4,64,256]{2,1,0:T(8,128)S(1)} collective-permute-done((f32[4,64,256]{2,1,0:T(8,128)S(1)}, f32[4,64,256]{2,1,0:T(8,128)S(1)}, u32[]{:S(2)}, u32[]{:S(2)}) %collective-permute-start.21) | collective-permute-done | bytes 262176 | tf_op jit(solution)/shard_map/ppermute | solution.py:23
  151.2 3.9 %collective-permute-done.28.other_two = f32[4,64,256]{2,1,0:T(8,128)S(1)} collective-permute-done((f32[4,64,256]{2,1,0:T(8,128)S(1)}, f32[4,64,256]{2,1,0:T(8,128)S(1)}, u32[]{:S(2)}, u32[]{:S(2)}) %collective-permute-start.28) | collective-permute-done | bytes 262176 | tf_op jit(solution)/shard_map/ppermute | solution.py:23
  155.0 1.4 shard_map.36
  (18 shorter events, 0.0 us)
Async XLA Ops:
  1.3 15.1 %collective-permute-start.2 = (f32[64,1024]{1,0:T(8,128)S(1)}, f32[64,1024]{1,0:T(8,128)S(1)}, u32[]{:S(2)}, u32[]{:S(2)}) collective-permute-start(f32[64,1024]{1,0:T(8,128)S(1)} %get-tuple-element.65), channel_id=1, source_target_pairs={{0,3},{1,2},{2,1},{3,0},{4,7},{5,6},{6,5},{7,4},{8,11},{9,10},{10,... | collective-permute-start | bytes 786440 | tf_op jit(solution)/shard_map/ppermute | solution.py:23
  4.5 11.9 %collective-permute-start.1 = (f32[64,1024]{1,0:T(8,128)S(1)}, f32[64,1024]{1,0:T(8,128)S(1)}, u32[]{:S(2)}, u32[]{:S(2)}) collective-permute-start(f32[64,1024]{1,0:T(8,128)S(1)} %get-tuple-element.66), channel_id=1, source_target_pairs={{0,2},{1,3},{2,0},{3,1},{4,6},{5,7},{6,4},{7,5},{8,10},{9,11},{10,... | collective-permute-start | bytes 786440 | tf_op jit(solution)/shard_map/ppermute | solution.py:23
  5.1 12.0 %collective-permute-start = (f32[64,1024]{1,0:T(8,128)S(1)}, f32[64,1024]{1,0:T(8,128)S(1)}, u32[]{:S(2)}, u32[]{:S(2)}) collective-permute-start(f32[64,1024]{1,0:T(8,128)S(1)} %get-tuple-element.64), channel_id=1, source_target_pairs={{0,1},{1,0},{2,3},{3,2},{4,5},{5,4},{6,7},{7,6},{8,9},{9,8},{10,11... | collective-permute-start | bytes 786440 | tf_op jit(solution)/shard_map/ppermute | solution.py:23
  17.1 30.4 %copy-start = (f32[4096,256]{1,0:T(8,128)S(1)}, f32[4096,256]{1,0:T(8,128)}, u32[]{:S(2)}) copy-start(f32[4096,256]{1,0:T(8,128)} %value.1) | copy-start | bytes 12582916
  17.2 34.6 %collective-permute-start.3 = (f32[4,64,1024]{2,1,0:T(8,128)S(1)}, f32[4,64,1024]{2,1,0:T(8,128)S(1)}, u32[]{:S(2)}, u32[]{:S(2)}) collective-permute-start(f32[4,64,1024]{2,1,0:T(8,128)S(1)} %pad_maximum_fusion.refs_0_), channel_id=1, source_target_pairs={{0,12},{1,13},{2,14},{3,15},{4,8},{5,9},{6,10},{7,11},{8,4},{9,5},... | collective-permute-start | bytes 3145736 | tf_op jit(solution)/shard_map/ppermute | solution.py:23
  21.3 31.4 %collective-permute-start.4 = (f32[4,64,1024]{2,1,0:T(8,128)S(1)}, f32[4,64,1024]{2,1,0:T(8,128)S(1)}, u32[]{:S(2)}, u32[]{:S(2)}) collective-permute-start(f32[4,64,1024]{2,1,0:T(8,128)S(1)} %pad_maximum_fusion.refs_0_), channel_id=1, source_target_pairs={{0,4},{1,5},{2,6},{3,7},{4,0},{5,1},{6,2},{7,3},{8,12},{9,13},{10,... | collective-permute-start | bytes 3145736 | tf_op jit(solution)/shard_map/ppermute | solution.py:23
  21.3 11.7 %collective-permute-start.8 = (f32[64,1024]{1,0:T(8,128)S(1)}, f32[64,1024]{1,0:T(8,128)S(1)}, u32[]{:S(2)}, u32[]{:S(2)}) collective-permute-start(f32[64,1024]{1,0:T(8,128)S(1)} %get-tuple-element.64), channel_id=1, source_target_pairs={{0,19},{1,18},{2,17},{3,16},{4,23},{5,22},{6,21},{7,20},{8,27},{9,... | collective-permute-start | bytes 786440 | tf_op jit(solution)/shard_map/ppermute | solution.py:23
  25.1 12.8 %collective-permute-start.7 = (f32[64,1024]{1,0:T(8,128)S(1)}, f32[64,1024]{1,0:T(8,128)S(1)}, u32[]{:S(2)}, u32[]{:S(2)}) collective-permute-start(f32[64,1024]{1,0:T(8,128)S(1)} %get-tuple-element.63), channel_id=1, source_target_pairs={{0,18},{1,19},{2,16},{3,17},{4,22},{5,23},{6,20},{7,21},{8,26},{9,... | collective-permute-start | bytes 786440 | tf_op jit(solution)/shard_map/ppermute | solution.py:23
  25.7 18.0 %collective-permute-start.6 = (f32[64,1024]{1,0:T(8,128)S(1)}, f32[64,1024]{1,0:T(8,128)S(1)}, u32[]{:S(2)}, u32[]{:S(2)}) collective-permute-start(f32[64,1024]{1,0:T(8,128)S(1)} %get-tuple-element.65), channel_id=1, source_target_pairs={{0,17},{1,16},{2,19},{3,18},{4,21},{5,20},{6,23},{7,22},{8,25},{9,... | collective-permute-start | bytes 786440 | tf_op jit(solution)/shard_map/ppermute | solution.py:23
  33.0 14.4 %collective-permute-start.5 = (f32[64,1024]{1,0:T(8,128)S(1)}, f32[64,1024]{1,0:T(8,128)S(1)}, u32[]{:S(2)}, u32[]{:S(2)}) collective-permute-start(f32[64,1024]{1,0:T(8,128)S(1)} %get-tuple-element.66), channel_id=1, source_target_pairs={{0,16},{1,17},{2,18},{3,19},{4,20},{5,21},{6,22},{7,23},{8,24},{9,... | collective-permute-start | bytes 786440 | tf_op jit(solution)/shard_map/ppermute | solution.py:23
  49.3 23.3 %collective-permute-start.9 = (f32[1024,256]{1,0:T(8,128)}, f32[1024,256]{1,0:T(8,128)}, u32[]{:S(2)}, u32[]{:S(2)}) collective-permute-start(f32[1024,256]{1,0:T(8,128)} %get-tuple-element.33), channel_id=1, source_target_pairs={{0,1},{1,0},{2,3},{3,2},{4,5},{5,4},{6,7},{7,6},{8,9},{9,8},{10,11... | collective-permute-start | bytes 3145736 | tf_op jit(solution)/shard_map/ppermute | solution.py:23
  49.4 24.5 %collective-permute-start.10 = (f32[1024,256]{1,0:T(8,128)}, f32[1024,256]{1,0:T(8,128)}, u32[]{:S(2)}, u32[]{:S(2)}) collective-permute-start(f32[1024,256]{1,0:T(8,128)} %get-tuple-element.34), channel_id=1, source_target_pairs={{0,3},{1,2},{2,1},{3,0},{4,7},{5,6},{6,5},{7,4},{8,11},{9,10},{10,... | collective-permute-start | bytes 3145736 | tf_op jit(solution)/shard_map/ppermute | solution.py:23
  50.5 23.4 %collective-permute-start.11 = (f32[1024,256]{1,0:T(8,128)}, f32[1024,256]{1,0:T(8,128)}, u32[]{:S(2)}, u32[]{:S(2)}) collective-permute-start(f32[1024,256]{1,0:T(8,128)} %get-tuple-element.35), channel_id=1, source_target_pairs={{0,16},{1,17},{2,18},{3,19},{4,20},{5,21},{6,22},{7,23},{8,24},{9,... | collective-permute-start | bytes 3145736 | tf_op jit(solution)/shard_map/ppermute | solution.py:23
  51.8 1.0 copy-start.1
  52.7 1.0 copy-start.3
  53.7 29.7 %collective-permute-start.12 = (f32[4,64,1024]{2,1,0:T(8,128)S(1)}, f32[4,64,1024]{2,1,0:T(8,128)}, u32[]{:S(2)}, u32[]{:S(2)}) collective-permute-start(f32[4,64,1024]{2,1,0:T(8,128)S(1)} %pad_maximum_fusion.1._.refs_0_), channel_id=1, source_target_pairs={{0,4},{1,5},{2,6},{3,7},{4,0},{5,1},{6,2},{7,3},{8,12},{9,13},{10,... | collective-permute-start | bytes 3145736 | tf_op jit(solution)/shard_map/ppermute | solution.py:23
  55.5 28.0 %collective-permute-start.13 = (f32[4,64,1024]{2,1,0:T(8,128)S(1)}, f32[4,64,1024]{2,1,0:T(8,128)}, u32[]{:S(2)}, u32[]{:S(2)}) collective-permute-start(f32[4,64,1024]{2,1,0:T(8,128)S(1)} %pad_maximum_fusion.1._.refs_0_), channel_id=1, source_target_pairs={{0,12},{1,13},{2,14},{3,15},{4,8},{5,9},{6,10},{7,11},{8,4},{9,5},... | collective-permute-start | bytes 3145736 | tf_op jit(solution)/shard_map/ppermute | solution.py:23
  73.9 2.7 %copy-start.2 = (f32[4,64,1024]{2,1,0:T(8,128)S(1)}, f32[4,64,1024]{2,1,0:T(8,128)}, u32[]{:S(2)}) copy-start(f32[4,64,1024]{2,1,0:T(8,128)} %copy-done.1) | copy-start | bytes 3145732
  73.9 2.7 %copy-start.4 = (f32[4,64,1024]{2,1,0:T(8,128)S(1)}, f32[4,64,1024]{2,1,0:T(8,128)}, u32[]{:S(2)}) copy-start(f32[4,64,1024]{2,1,0:T(8,128)} %copy-done.3) | copy-start | bytes 3145732
  81.7 9.5 %collective-permute-start.14 = (f32[2,4,64,256]{3,2,1,0:T(8,128)S(1)}, f32[2,4,64,256]{3,2,1,0:T(8,128)S(1)}, u32[]{:S(2)}, u32[]{:S(2)}) collective-permute-start(f32[2,4,64,256]{3,2,1,0:T(8,128)S(1)} %get-tuple-element.43), channel_id=1, source_target_pairs={{0,32},{1,33},{2,34},{3,35},{4,36},{5,37},{6,38},{7,39},{8,40},{9,... | collective-permute-start | bytes 1572872 | tf_op jit(solution)/shard_map/ppermute | solution.py:23
  81.8 25.6 %collective-permute-start.22 = (f32[4,64,1024]{2,1,0:T(8,128)S(1)}, f32[4,64,1024]{2,1,0:T(8,128)S(1)}, u32[]{:S(2)}, u32[]{:S(2)}) collective-permute-start(f32[4,64,1024]{2,1,0:T(8,128)S(1)} %copy-done.2), channel_id=1, source_target_pairs={{0,4},{1,5},{2,6},{3,7},{4,0},{5,1},{6,2},{7,3},{8,12},{9,13},{10,... | collective-permute-start | bytes 3145736 | tf_op jit(solution)/shard_map/ppermute | solution.py:23
  83.5 26.6 %collective-permute-start.23 = (f32[4,64,1024]{2,1,0:T(8,128)}, f32[4,64,1024]{2,1,0:T(8,128)S(1)}, u32[]{:S(2)}, u32[]{:S(2)}) collective-permute-start(f32[4,64,1024]{2,1,0:T(8,128)} %collective-permute-done.12.refs_2_), channel_id=1, source_target_pairs={{0,12},{1,13},{2,14},{3,15},{4,8},{5,9},{6,10},{7,11},{8,4},{9,5},... | collective-permute-start | bytes 3145736 | tf_op jit(solution)/shard_map/ppermute | solution.py:23
  84.0 7.3 %collective-permute-start.15 = (f32[2,4,64,256]{3,2,1,0:T(8,128)S(1)}, f32[2,4,64,256]{3,2,1,0:T(8,128)S(1)}, u32[]{:S(2)}, u32[]{:S(2)}) collective-permute-start(f32[2,4,64,256]{3,2,1,0:T(8,128)S(1)} %get-tuple-element.44), channel_id=1, source_target_pairs={{0,32},{1,33},{2,34},{3,35},{4,36},{5,37},{6,38},{7,39},{8,40},{9,... | collective-permute-start | bytes 1572872 | tf_op jit(solution)/shard_map/ppermute | solution.py:23
  90.6 2.1 %collective-permute-start.16 = (f32[2,4,64,256]{3,2,1,0:T(8,128)S(1)}, f32[2,4,64,256]{3,2,1,0:T(8,128)S(1)}, u32[]{:S(2)}, u32[]{:S(2)}) collective-permute-start(f32[2,4,64,256]{3,2,1,0:T(8,128)S(1)} %get-tuple-element.45), channel_id=1, source_target_pairs={{0,32},{1,33},{2,34},{3,35},{4,36},{5,37},{6,38},{7,39},{8,40},{9,... | collective-permute-start | bytes 1572872 | tf_op jit(solution)/shard_map/ppermute | solution.py:23
  91.2 2.3 %collective-permute-start.17 = (f32[2,4,64,256]{3,2,1,0:T(8,128)S(1)}, f32[2,4,64,256]{3,2,1,0:T(8,128)S(1)}, u32[]{:S(2)}, u32[]{:S(2)}) collective-permute-start(f32[2,4,64,256]{3,2,1,0:T(8,128)S(1)} %get-tuple-element.46), channel_id=1, source_target_pairs={{0,32},{1,33},{2,34},{3,35},{4,36},{5,37},{6,38},{7,39},{8,40},{9,... | collective-permute-start | bytes 1572872 | tf_op jit(solution)/shard_map/ppermute | solution.py:23
  113.6 4.3 %collective-permute-start.24 = (f32[4,2,4,64,256]{4,3,2,1,0:T(8,128)S(1)}, f32[4,2,4,64,256]{4,3,2,1,0:T(8,128)S(1)}, u32[]{:S(2)}, u32[]{:S(2)}) collective-permute-start(f32[4,2,4,64,256]{4,3,2,1,0:T(8,128)S(1)} %get-tuple-element.56), channel_id=1, source_target_pairs={{0,32},{1,33},{2,34},{3,35},{4,36},{5,37},{6,38},{7,39},{8,40},{9,... | collective-permute-start | bytes 6291464 | tf_op jit(solution)/shard_map/ppermute | solution.py:23
  113.6 14.8 %collective-permute-start.18 = (f32[2,4,64,256]{3,2,1,0:T(8,128)S(1)}, f32[2,4,64,256]{3,2,1,0:T(8,128)S(1)}, u32[]{:S(2)}, u32[]{:S(2)}) collective-permute-start(f32[2,4,64,256]{3,2,1,0:T(8,128)S(1)} %get-tuple-element.48.refs_2_), channel_id=1, source_target_pairs={{0,1},{1,0},{2,3},{3,2},{4,5},{5,4},{6,7},{7,6},{8,9},{9,8},{10,11... | collective-permute-start | bytes 1572872 | tf_op jit(solution)/shard_map/ppermute | solution.py:23
  114.0 16.1 %collective-permute-start.19 = (f32[2,4,64,256]{3,2,1,0:T(8,128)S(1)}, f32[2,4,64,256]{3,2,1,0:T(8,128)}, u32[]{:S(2)}, u32[]{:S(2)}) collective-permute-start(f32[2,4,64,256]{3,2,1,0:T(8,128)S(1)} %get-tuple-element.49.refs_3_), channel_id=1, source_target_pairs={{0,3},{1,2},{2,1},{3,0},{4,7},{5,6},{6,5},{7,4},{8,11},{9,10},{10,... | collective-permute-start | bytes 1572872 | tf_op jit(solution)/shard_map/ppermute | solution.py:23
  116.4 13.8 %collective-permute-start.20 = (f32[2,4,64,256]{3,2,1,0:T(8,128)S(1)}, f32[2,4,64,256]{3,2,1,0:T(8,128)}, u32[]{:S(2)}, u32[]{:S(2)}) collective-permute-start(f32[2,4,64,256]{3,2,1,0:T(8,128)S(1)} %get-tuple-element.50.refs_4_), channel_id=1, source_target_pairs={{0,16},{1,17},{2,18},{3,19},{4,20},{5,21},{6,22},{7,23},{8,24},{9,... | collective-permute-start | bytes 1572872 | tf_op jit(solution)/shard_map/ppermute | solution.py:23
  119.1 20.1 %collective-permute-start.25 = (f32[2,4,64,256]{3,2,1,0:T(8,128)}, f32[2,4,64,256]{3,2,1,0:T(8,128)S(1)}, u32[]{:S(2)}, u32[]{:S(2)}) collective-permute-start(f32[2,4,64,256]{3,2,1,0:T(8,128)} %get-tuple-element.61), channel_id=1, source_target_pairs={{0,1},{1,0},{2,3},{3,2},{4,5},{5,4},{6,7},{7,6},{8,9},{9,8},{10,11... | collective-permute-start | bytes 1572872 | tf_op jit(solution)/shard_map/ppermute | solution.py:23
  119.5 21.1 %collective-permute-start.26 = (f32[2,4,64,256]{3,2,1,0:T(8,128)}, f32[2,4,64,256]{3,2,1,0:T(8,128)}, u32[]{:S(2)}, u32[]{:S(2)}) collective-permute-start(f32[2,4,64,256]{3,2,1,0:T(8,128)} %get-tuple-element.60), channel_id=1, source_target_pairs={{0,3},{1,2},{2,1},{3,0},{4,7},{5,6},{6,5},{7,4},{8,11},{9,10},{10,... | collective-permute-start | bytes 1572872 | tf_op jit(solution)/shard_map/ppermute | solution.py:23
  128.5 15.2 %collective-permute-start.27 = (f32[2,4,64,256]{3,2,1,0:T(8,128)}, f32[2,4,64,256]{3,2,1,0:T(8,128)}, u32[]{:S(2)}, u32[]{:S(2)}) collective-permute-start(f32[2,4,64,256]{3,2,1,0:T(8,128)} %get-tuple-element.59), channel_id=1, source_target_pairs={{0,16},{1,17},{2,18},{3,19},{4,20},{5,21},{6,22},{7,23},{8,24},{9,... | collective-permute-start | bytes 1572872 | tf_op jit(solution)/shard_map/ppermute | solution.py:23
  131.5 19.7 %collective-permute-start.21 = (f32[4,64,256]{2,1,0:T(8,128)S(1)}, f32[4,64,256]{2,1,0:T(8,128)S(1)}, u32[]{:S(2)}, u32[]{:S(2)}) collective-permute-start(f32[4,64,256]{2,1,0:T(8,128)S(1)} %get-tuple-element.52), channel_id=1, source_target_pairs={{0,64},{1,65},{2,66},{3,67},{4,68},{5,69},{6,70},{7,71},{8,72},{9,... | collective-permute-start | bytes 786440 | tf_op jit(solution)/shard_map/ppermute | solution.py:23
  144.9 10.1 %collective-permute-start.28 = (f32[4,64,256]{2,1,0:T(8,128)S(1)}, f32[4,64,256]{2,1,0:T(8,128)S(1)}, u32[]{:S(2)}, u32[]{:S(2)}) collective-permute-start(f32[4,64,256]{2,1,0:T(8,128)S(1)} %get-tuple-element.58), channel_id=1, source_target_pairs={{0,64},{1,65},{2,66},{3,67},{4,68},{5,69},{6,70},{7,71},{8,72},{9,... | collective-permute-start | bytes 786440 | tf_op jit(solution)/shard_map/ppermute | solution.py:23

commit v10 on v9

--- a/solution.py
+++ b/solution.py
@@ -106,87 +106,96 @@
     return [(block, block ^ (0, 1, 3, 0)[d]) for block in range(4)]
 
 
-def early_products(swap, planes, rights):
+def early_products(swap, part, planes, rights, before=()):
     arrays = [array for plane in planes for array in plane]
     rows, depth = arrays[0].shape[1:]
     columns = rights[0].shape[1] // 4
 
     def kernel(swap, *refs):
-        blocks, (high, low, keep, third, give, give_too, left_high, left_low) = refs[: len(arrays)], refs[len(arrays):]
+        blocks, rest = refs[: len(arrays)], refs[len(arrays) + len(before):]
+        high, low, keep, third, *gives, left_high, left_low = rest
         swapped = swap[0] == 1
 
         def store(d, total):
             for block, into in places(d):
                 zero, one = total[0, block], total[1, block]
-                keep[d, into] = jnp.where(swapped, one, zero)
-                (give_too if d > 1 else give)[d % 2, into] = jnp.where(swapped, zero, one)
-                third[d, into] = total[2, block]
+                keep[d, 0, into] = jnp.where(swapped, one, zero)
+                gives[d][0, into] = jnp.where(swapped, zero, one)
+                third[d, 0, into] = total[2, block]
 
         multiplied(blocks, left_high, left_low, high, low, store)
 
-    kept, given = (jax.ShapeDtypeStruct((count, 4, rows, columns), jnp.float32) for count in (4, 2))
+    kept = jax.ShapeDtypeStruct((4, 2, 4, rows, columns), jnp.float32)
+    given = jax.ShapeDtypeStruct((2, 4, rows, columns), jnp.float32)
+    once = pl.Buffered(1)
+    kept_out = pl.BlockSpec((4, 1, 4, rows, columns), lambda *_: (0, part, 0, 0, 0), pipeline_mode=once)
+    given_out = pl.BlockSpec((1, 4, rows, columns), lambda *_: (part, 0, 0, 0), pipeline_mode=once)
     scratch = pltpu.VMEM((12 * rows, depth), jnp.bfloat16)
-    shapes = [kept, kept, given, given]
-    return call(
-        kernel, swap, (*arrays, *rights), [whole(array) for array in arrays] + [VMEM] * 2,
-        shapes, [whole(shape) for shape in shapes], [scratch] * 2,
-    )
-
-
-def added_kernel(_, *refs):
-    keeps, gots, outs = refs[:2], refs[2:6], refs[-4:]
-    for part, keep in enumerate(keeps):
-        for d, out in enumerate(outs):
-            out[part] = keep[d] + gots[2 * part + d // 2][d % 2]
-
-
-def added(scalars, keeps, gots, after):
-    shape = jax.ShapeDtypeStruct((2, *keeps[0].shape[1:]), jnp.float32)
-    return call(
-        added_kernel, scalars, (*keeps, *gots, *after),
-        [whole(value) for value in (*keeps, *gots)] + [ANYWHERE] * len(after), [shape] * 4, [whole(shape)] * 4,
-    )
-
-
-def late_products(swap, parts, thirds, rights, after):
+    first = 1 + len(arrays)
+    return call(
+        kernel, swap, (*arrays, *before, *rights),
+        [whole(array) for array in arrays] + [ANYWHERE] * len(before) + [VMEM] * 2,
+        [kept] * 2 + [given] * 4, [kept_out] * 2 + [given_out] * 4, [scratch] * 2,
+        {first + at: at for at in range(len(before))},
+    )
+
+
+def added_kernel(_, keep, *refs):
+    gots, outs = refs[:len(refs) // 2], refs[len(refs) // 2:]
+    for at, (got, out) in enumerate(zip(gots, outs)):
+        out[...] = keep[at + 1] + got[...]
+
+
+def added(scalars, keep, gots):
+    shape = jax.ShapeDtypeStruct(gots[0].shape, jnp.float32)
+    return call(
+        added_kernel, scalars, (keep, *gots), [whole(value) for value in (keep, *gots)], [shape] * 3, [whole(shape)] * 3
+    )
+
+
+def late_products(swap, parts, third, rights, after):
     arrays = [array for part in parts for array in part]
     rows, depth = arrays[0].shape[1:]
     columns = rights[0].shape[1] // 4
 
     def kernel(swap, *refs):
         blocks, rest = refs[: len(arrays)], refs[len(arrays) + len(after):]
-        high, low, ahead, ahead_too, keep, give, left_high, left_low = rest
+        high, low, ahead, keep, *gives, left_high, left_low = rest
         swapped = swap[0] == 1
 
         def store(d, total):
             for part in range(2):
                 for block, into in places(d):
-                    zero, one = (ahead, ahead_too)[part][d, into], total[part, block]
+                    zero, one = ahead[d, part, into], total[part, block]
                     keep[d, part, into] = jnp.where(swapped, one, zero)
-                    give[d, part, into] = jnp.where(swapped, zero, one)
+                    gives[d][part, into] = jnp.where(swapped, zero, one)
 
         multiplied(blocks, left_high, left_low, high, low, store)
 
-    shape = jax.ShapeDtypeStruct((4, 2, 4, rows, columns), jnp.float32)
+    kept = jax.ShapeDtypeStruct((4, 2, 4, rows, columns), jnp.float32)
+    given = jax.ShapeDtypeStruct((2, 4, rows, columns), jnp.float32)
+    shapes = [kept] + [given] * 4
     scratch = pltpu.VMEM((8 * rows, depth), jnp.bfloat16)
     return call(
-        kernel, swap, (*arrays, *after, *rights, *thirds),
-        [whole(array) for array in arrays] + [ANYWHERE] * len(after) + [VMEM] * 2 + [whole(third) for third in thirds],
-        [shape] * 2, [whole(shape)] * 2, [scratch] * 2,
-    )
-
-
-def sum_kernel(side, *refs):
+        kernel, swap, (*arrays, *after, *rights, third),
+        [whole(array) for array in arrays] + [ANYWHERE] * len(after) + [VMEM] * 2 + [whole(third)],
+        shapes, [whole(shape) for shape in shapes], [scratch] * 2,
+    )
+
+
+def sum_kernel(side, keep, got, *refs):
     terms, (mine, theirs) = refs[:-2], refs[-2:]
     for out, part in ((mine, side[0]), (theirs, 1 - side[0])):
-        across = terms[3][1 - part]
-        out[...] = (terms[0][part] + terms[1][part]) + (terms[2][part] + across)
-
-
-def summed(side, terms):
-    shape = jax.ShapeDtypeStruct(terms[0].shape[1:], jnp.float32)
-    return call(
-        sum_kernel, side, terms, [whole(term) for term in terms], [shape] * 2, [whole(shape)] * 2
+        across = terms[2][1 - part]
+        out[...] = (keep[0, part] + got[part]) + (terms[0][part] + (terms[1][part] + across))
+
+
+def summed(side, keep, got, terms):
+    shape = jax.ShapeDtypeStruct(got.shape[1:], jnp.float32)
+    own = pl.BlockSpec((1, *keep.shape[1:]), lambda *_: (0,) * keep.ndim, pipeline_mode=pl.Buffered(1))
+    return call(
+        sum_kernel, side, (keep, got, *terms), [own] + [whole(value) for value in (got, *terms)],
+        [shape] * 2, [whole(shape)] * 2,
     )
 
 
@@ -216,8 +225,10 @@
         return lax.dynamic_slice(left, (0, (quarter ^ d) * depth), (rows, depth))
 
     mine = jnp.stack([block(0), send(block(1), dy=1), send(block(3), dy=2), send(block(2), dy=3)])
-    other = jnp.stack([send(block(3), dx=1), send(block(2), dx=1, dy=1), send(block(0), dx=1, dy=2), send(block(1), dx=1, dy=3)])
-
+    others = [send(block(3), dx=1), send(block(2), dx=1, dy=1)]
+    mine, *others = lax.optimization_barrier((mine, *others))
+    others += [send(block(0), dx=1, dy=2), send(block(1), dx=1, dy=3)]
+    other = jnp.stack(others)
     own_one, own_three = send(mine, dz=1), send(mine, dz=3)
     far, *_ = lax.optimization_barrier((other, own_one, own_three))
     far_one, far_three = lax.optimization_barrier((send(far, dz=1), send(far, dz=3)))
@@ -228,23 +239,18 @@
     pieces = [pieces[0]] + [send(pieces[d], **NEAR[d]) for d in range(1, 4)]
     rights = split(swap, pieces)
 
-    keeps, thirds, gots = [], [], []
-    for part in ((mine, own_one, own_three), (far, far_one, far_three)):
-        keep, third, *gives = early_products(swap, [(part[0],), (part[2],), (part[1],)], rights)
-        keeps.append(keep)
-        thirds.append(third)
-        gots += [send(give, core=1) for give in gives]
-
-    ends = []
+    before = early_products(swap, 0, ((mine,), (own_three,), (own_one,)), rights)
+    early = early_products(swap, 1, ((far,), (far_three,), (far_one,)), rights, before)
+
+    ends, third, after = [], early[1], None
     for last in (False, True):
         if last:
-            keep, give = late_products(swap, ((own_two,), (far_two,)), thirds, rights, sums[1:])
-            got = send(give, core=1)
-            sums = [keep[d] + got[d] for d in range(4)]
+            keep, *gives = late_products(swap, ((own_two,), (far_two,)), third, rights, after)
         else:
-            sums = added(swap, keeps, gots, [])
-        terms = [sums[0]] + [send(sums[d], **NEAR[d]) for d in range(1, 4)]
-        here, there = summed(side, terms)
+            keep, _, *gives = early
+        got = [send(give, core=1) for give in gives]
+        after = added(swap, keep, got[1:])
+        here, there = summed(side, keep, got[0], [send(after[d - 1], **NEAR[d]) for d in range(1, 4)])
         ends += [here, send(there, dhi=1)]
 
     total = join(jnp.stack([(z & 1) ^ swap[0], y]), ends)

time: 157 us -> 151 us (0.962)
  waiting for transfers between devices: 90.5 us -> 70 us
  starting transfers between devices: 37.2 us -> 43.4 us
  local copies, waits for them, and re-layouts: 3.27 us -> 8.26 us
  Pallas kernels: 23.8 us -> 28.6 us
    ppermute x29 -> x32, waiting for transfers between devices: 90.5 us -> 70 us  [send(): return lax.ppermute(value, AXES, pairs)]
    ppermute x29 -> x32, starting transfers between devices: 37.2 us -> 43.4 us  [send(): return lax.ppermute(value, AXES, pairs)]
    unnamed x10 -> x26, local copies, waits for them, and re-layouts: 1.98 us -> 6.97 us
    pallas_call x9 -> x10, Pallas kernels: 23.8 us -> 28.6 us  [call(): pl.pallas_call(kernel, grid_spec=pltpu.PrefetchScalarGridSpec(num_scalar_...]
  transfers between devices with their start and end apart: 29 -> 32, of which waited for: 20 -> 20; matrix products, arithmetic and copies ran while one was open for 1% -> 0% of each run, Pallas kernels for 12% -> 15%
where the time goes in v10:
time: 151 us
  waiting for transfers between devices  70 us (46%)
  starting transfers between devices  43.4 us (29%)
  Pallas kernels  28.6 us (19%)
  local copies, waits for them, and re-layouts  8.26 us (5%)
    ppermute x32, waiting for transfers between devices, send(): return lax.ppermute(value, AXES, pairs)  70 us
    ppermute x32, starting transfers between devices, send(): return lax.ppermute(value, AXES, pairs)  43.4 us
    pallas_call x10, Pallas kernels, call(): pl.pallas_call(kernel, grid_spec=pltpu.PrefetchScalarGridSpec(num_scalar_...  28.6 us
    unnamed x26, local copies, waits for them, and re-layouts  6.97 us
  transfers between devices with their start and end apart: 32, of which 20 were waited for; matrix products, arithmetic and copies ran while one was open for 0% of the time, Pallas kernels for 15%

profile of v10, /device:TPU:0, one launch (start us, length us, event | category | flops | bytes accessed | tf_op | source)
XLA Modules:
  0.0 150.6 jit_solution(12261531417889336317)
XLA Ops:
  0.0 1.3 constant_dynamic-slice_fusion.1
  1.3 3.2 %collective-permute-start.2 = (f32[64,1024]{1,0:T(8,128)S(1)}, f32[64,1024]{1,0:T(8,128)S(1)}, u32[]{:S(2)}, u32[]{:S(2)}) collective-permute-start(f32[64,1024]{1,0:T(8,128)S(1)} %get-tuple-element.86), channel_id=1, source_target_pairs={{0,3},{1,2},{2,1},{3,0},{4,7},{5,6},{6,5},{7,4},{8,11},{9,10},{10,... | collective-permute-start | bytes 786440 | tf_op jit(solution)/shard_map/ppermute | solution.py:23
  4.5 0.6 collective-permute-start.1
  5.1 0.4 collective-permute-start
  5.5 1.6 %collective-permute-start.3 = (f32[64,1024]{1,0:T(8,128)S(1)}, f32[64,1024]{1,0:T(8,128)S(1)}, u32[]{:S(2)}, u32[]{:S(2)}) collective-permute-start(f32[64,1024]{1,0:T(8,128)S(1)} %get-tuple-element.83), channel_id=1, source_target_pairs={{0,16},{1,17},{2,18},{3,19},{4,20},{5,21},{6,22},{7,23},{8,24},{9,... | collective-permute-start | bytes 786440 | tf_op jit(solution)/shard_map/ppermute | solution.py:23
  7.0 1.5 %collective-permute-start.4 = (f32[64,1024]{1,0:T(8,128)S(1)}, f32[64,1024]{1,0:T(8,128)S(1)}, u32[]{:S(2)}, u32[]{:S(2)}) collective-permute-start(f32[64,1024]{1,0:T(8,128)S(1)} %get-tuple-element.86), channel_id=1, source_target_pairs={{0,17},{1,16},{2,19},{3,18},{4,21},{5,20},{6,23},{7,22},{8,25},{9,... | collective-permute-start | bytes 786440 | tf_op jit(solution)/shard_map/ppermute | solution.py:23
  8.6 7.6 %collective-permute-done.2 = f32[64,1024]{1,0:T(8,128)S(1)} collective-permute-done((f32[64,1024]{1,0:T(8,128)S(1)}, f32[64,1024]{1,0:T(8,128)S(1)}, u32[]{:S(2)}, u32[]{:S(2)}) %collective-permute-start.2) | collective-permute-done | bytes 262176 | tf_op jit(solution)/shard_map/ppermute | solution.py:23
  16.2 0.9 collective-permute-done.1
  17.1 5.7 %collective-permute-done = f32[64,1024]{1,0:T(8,128)S(1)} collective-permute-done((f32[64,1024]{1,0:T(8,128)S(1)}, f32[64,1024]{1,0:T(8,128)S(1)}, u32[]{:S(2)}, u32[]{:S(2)}) %collective-permute-start) | collective-permute-done | bytes 262176 | tf_op jit(solution)/shard_map/ppermute | solution.py:23
  22.9 2.0 %collective-permute-start.7 = (f32[4,64,1024]{2,1,0:T(8,128)S(1)}, f32[4,64,1024]{2,1,0:T(8,128)S(1)}, u32[]{:S(2)}, u32[]{:S(2)}) collective-permute-start(f32[4,64,1024]{2,1,0:T(8,128)S(1)} %pad_maximum_fusion.refs_0_), channel_id=1, source_target_pairs={{0,4},{1,5},{2,6},{3,7},{4,0},{5,1},{6,2},{7,3},{8,12},{9,13},{10,... | collective-permute-start | bytes 3145736 | tf_op jit(solution)/shard_map/ppermute | solution.py:23
  24.9 2.5 %collective-permute-start.8 = (f32[4,64,1024]{2,1,0:T(8,128)S(1)}, f32[4,64,1024]{2,1,0:T(8,128)}, u32[]{:S(2)}, u32[]{:S(2)}) collective-permute-start(f32[4,64,1024]{2,1,0:T(8,128)S(1)} %pad_maximum_fusion.refs_0_), channel_id=1, source_target_pairs={{0,12},{1,13},{2,14},{3,15},{4,8},{5,9},{6,10},{7,11},{8,4},{9,5},... | collective-permute-start | bytes 3145736 | tf_op jit(solution)/shard_map/ppermute | solution.py:23
  27.4 3.8 %collective-permute-start.6 = (f32[64,1024]{1,0:T(8,128)S(1)}, f32[64,1024]{1,0:T(8,128)S(1)}, u32[]{:S(2)}, u32[]{:S(2)}) collective-permute-start(f32[64,1024]{1,0:T(8,128)S(1)} %get-tuple-element.84), channel_id=1, source_target_pairs={{0,19},{1,18},{2,17},{3,16},{4,23},{5,22},{6,21},{7,20},{8,27},{9,... | collective-permute-start | bytes 786440 | tf_op jit(solution)/shard_map/ppermute | solution.py:23
  31.2 0.6 collective-permute-start.5
  31.8 7.2 %collective-permute-done.6 = f32[64,1024]{1,0:T(8,128)S(1)} collective-permute-done((f32[64,1024]{1,0:T(8,128)S(1)}, f32[64,1024]{1,0:T(8,128)S(1)}, u32[]{:S(2)}, u32[]{:S(2)}) %collective-permute-start.6) | collective-permute-done | bytes 262176 | tf_op jit(solution)/shard_map/ppermute | solution.py:23
  38.9 3.0 %collective-permute-done.5 = f32[64,1024]{1,0:T(8,128)S(1)} collective-permute-done((f32[64,1024]{1,0:T(8,128)S(1)}, f32[64,1024]{1,0:T(8,128)S(1)}, u32[]{:S(2)}, u32[]{:S(2)}) %collective-permute-start.5) | collective-permute-done | bytes 262176 | tf_op jit(solution)/shard_map/ppermute | solution.py:23
  42.1 5.0 %collective-permute-done.7.refs_2_ = f32[4,64,1024]{2,1,0:T(8,128)S(1)} collective-permute-done((f32[4,64,1024]{2,1,0:T(8,128)S(1)}, f32[4,64,1024]{2,1,0:T(8,128)S(1)}, u32[]{:S(2)}, u32[]{:S(2)}) %collective-permute-start.7) | collective-permute-done | bytes 1048608 | tf_op jit(solution)/shard_map/ppermute | solution.py:23
  47.1 1.0 copy-done.5
  48.0 1.8 %collective-permute-done.8.refs_1_ = f32[4,64,1024]{2,1,0:T(8,128)} collective-permute-done((f32[4,64,1024]{2,1,0:T(8,128)S(1)}, f32[4,64,1024]{2,1,0:T(8,128)}, u32[]{:S(2)}, u32[]{:S(2)}) %collective-permute-start.8) | collective-permute-done | bytes 1048608 | tf_op jit(solution)/shard_map/ppermute | solution.py:23
  49.8 0.6 collective-permute-start.9
  50.4 2.3 %collective-permute-start.10 = (f32[4,64,1024]{2,1,0:T(8,128)S(1)}, f32[4,64,1024]{2,1,0:T(8,128)S(1)}, u32[]{:S(2)}, u32[]{:S(2)}) collective-permute-start(f32[4,64,1024]{2,1,0:T(8,128)S(1)} %pad_maximum_fusion.1._.refs_0_), channel_id=1, source_target_pairs={{0,12},{1,13},{2,14},{3,15},{4,8},{5,9},{6,10},{7,11},{8,4},{9,5},... | collective-permute-start | bytes 3145736 | tf_op jit(solution)/shard_map/ppermute | solution.py:23
  52.8 1.9 %shard_map.28 = (f32[1024,256]{1,0:T(8,128)S(1)}, f32[1024,256]{1,0:T(8,128)}, f32[1024,256]{1,0:T(8,128)}, f32[1024,256]{1,0:T(8,128)}) custom-call(s32[1]{0:T(128)} %bitcast.12.quarter, f32[4096,256]{1,0:T(8,128)S(1)} %copy-done.2, f32[4,64,1024]{2,1,0:T(8,128)S(1)} %pad_maximum_fusion.1._.refs_0_), custom_call_target="tpu_custom_call" | custom-call | flops 1 | bytes 1 | tf_op jit(solution)/shard_map/pallas_call | solution.py:40
  54.6 1.3 collective-permute-start.11
  56.0 2.2 %collective-permute-start.12 = (f32[1024,256]{1,0:T(8,128)}, f32[1024,256]{1,0:T(8,128)}, u32[]{:S(2)}, u32[]{:S(2)}) collective-permute-start(f32[1024,256]{1,0:T(8,128)} %get-tuple-element.52), channel_id=1, source_target_pairs={{0,3},{1,2},{2,1},{3,0},{4,7},{5,6},{6,5},{7,4},{8,11},{9,10},{10,... | collective-permute-start | bytes 3145736 | tf_op jit(solution)/shard_map/ppermute | solution.py:23
  58.2 1.5 collective-permute-start.13
  59.7 13.3 %collective-permute-done.9.refs_2_ = f32[4,64,1024]{2,1,0:T(8,128)} collective-permute-done((f32[4,64,1024]{2,1,0:T(8,128)S(1)}, f32[4,64,1024]{2,1,0:T(8,128)}, u32[]{:S(2)}, u32[]{:S(2)}) %collective-permute-start.9) | collective-permute-done | bytes 1048608 | tf_op jit(solution)/shard_map/ppermute | solution.py:23
  72.9 0.6 collective-permute-start.22
  73.5 0.8 collective-permute-done.10.refs_1_
  74.4 1.0 copy-done.7
  75.3 2.1 %collective-permute-start.23 = (f32[4,64,1024]{2,1,0:T(8,128)}, f32[4,64,1024]{2,1,0:T(8,128)}, u32[]{:S(2)}, u32[]{:S(2)}) collective-permute-start(f32[4,64,1024]{2,1,0:T(8,128)} %collective-permute-done.9.refs_2_), channel_id=1, source_target_pairs={{0,12},{1,13},{2,14},{3,15},{4,8},{5,9},{6,10},{7,11},{8,4},{9,5},... | collective-permute-start | bytes 3145736 | tf_op jit(solution)/shard_map/ppermute | solution.py:23
  77.4 1.8 %collective-permute-done.12.refs_2_ = f32[1024,256]{1,0:T(8,128)} collective-permute-done((f32[1024,256]{1,0:T(8,128)}, f32[1024,256]{1,0:T(8,128)}, u32[]{:S(2)}, u32[]{:S(2)}) %collective-permute-start.12) | collective-permute-done | bytes 1048608 | tf_op jit(solution)/shard_map/ppermute | solution.py:23
  79.2 0.7 collective-permute-done.13.refs_3_
  79.9 2.4 %shard_map.29 = (bf16[1024,1024]{1,0:T(8,128)(2,1)S(1)}, bf16[1024,1024]{1,0:T(8,128)(2,1)S(1)}) custom-call(s32[1]{0:T(128)} %bitcast.3._.swap, f32[1024,256]{1,0:T(8,128)S(1)} %get-tuple-element.50.refs_0_, f32[1024,256]{1,0:T(8,128)S(1)} %collective-permute-done.11.refs_1_, f32[1024,256]{1,0:T(8,128)} %collective-permute-done.12.refs_2_, ...), custom_call_target="tpu_custom_call" | custom-call | flops 1 | bytes 1 | tf_op jit(solution)/shard_map/pallas_call | solution.py:40
  82.3 6.4 %shard_map.30 = (f32[4,2,4,64,256]{4,3,2,1,0:T(8,128)S(1)}, f32[4,2,4,64,256]{4,3,2,1,0:T(8,128)S(1)}, f32[2,4,64,256]{3,2,1,0:T(8,128)S(1)}, f32[2,4,64,256]{3,...) custom-call(s32[1]{0:T(128)} %bitcast.3._.swap, f32[4,64,1024]{2,1,0:T(8,128)S(1)} %copy-done.4, ...), custom_call_target="tpu_custom_call" | custom-call | flops 1 | bytes 1 | tf_op jit(solution)/shard_map/pallas_call | solution.py:40
  88.7 6.3 %shard_map.31 = (f32[4,2,4,64,256]{4,3,2,1,0:T(8,128)S(1)}, f32[4,2,4,64,256]{4,3,2,1,0:T(8,128)S(1)}, f32[2,4,64,256]{3,2,1,0:T(8,128)S(1)}, f32[2,4,64,256]{3,...) custom-call(s32[1]{0:T(128)} %bitcast.3._.swap, ...), custom_call_target="tpu_custom_call", output_to_operand_aliasing={{0}: (4, {}), {1}: (5, {}), {2}: (6, {}), {3}: (7, {}), {4}... | custom-call | flops 1 | bytes 1 | tf_op jit(solution)/shard_map/pallas_call | solution.py:40
  95.1 0.5 collective-permute-start.16
  95.7 1.3 collective-permute-done.15.refs_0_
  97.0 0.7 collective-permute-done.16.refs_1_
  97.8 0.7 collective-permute-done.17.refs_2_
  98.5 0.2 shard_map.32
  98.8 5.0 %shard_map.34 = (f32[4,2,4,64,256]{4,3,2,1,0:T(8,128)S(1)}, f32[2,4,64,256]{3,2,1,0:T(8,128)}, f32[2,4,64,256]{3,2,1,0:T(8,128)S(1)}, f32[2,4,64,256]{3,2,1,0:T(8,128)S(1)}, f32[2,4,64,256]{3,2,1,0:T(8,128)S(1)}) custom-call(s32[1]{0:T(128)} %bitcast.3._.swap, f32[4,64,1024]{2,1,0:T(8,128)} %collective-permute-done.22.refs_0_, ...), custom_call_target="tpu_custom_call" | custom-call | flops 1 | bytes 1 | tf_op jit(solution)/shard_map/pallas_call | solution.py:40
  104.0 0.4 collective-permute-start.26
  104.5 0.4 collective-permute-start.14
  104.9 0.8 collective-permute-start.18
  105.8 2.3 %collective-permute-start.19 = (f32[2,4,64,256]{3,2,1,0:T(8,128)S(1)}, f32[2,4,64,256]{3,2,1,0:T(8,128)S(1)}, u32[]{:S(2)}, u32[]{:S(2)}) collective-permute-start(f32[2,4,64,256]{3,2,1,0:T(8,128)S(1)} %get-tuple-element.68.refs_3_), channel_id=1, source_target_pairs={{0,3},{1,2},{2,1},{3,0},{4,7},{5,6},{6,5},{7,4},{8,11},{9,10},{10,... | collective-permute-start | bytes 1572872 | tf_op jit(solution)/shard_map/ppermute | solution.py:23
  108.1 1.5 collective-permute-start.20
  109.6 1.3 shard_map.35
  110.9 1.3 copy-done
  112.2 0.5 collective-permute-start.28
  112.8 6.8 %collective-permute-done.18.refs_0_ = f32[2,4,64,256]{3,2,1,0:T(8,128)S(1)} collective-permute-done((f32[2,4,64,256]{3,2,1,0:T(8,128)S(1)}, f32[2,4,64,256]{3,2,1,0:T(8,128)S(1)}, u32[]{:S(2)}, u32[]{:S(2)}) %collective-permute-start.18) | collective-permute-done | bytes 524320 | tf_op jit(solution)/shard_map/ppermute | solution.py:23
  119.6 0.8 copy-done.9
  120.4 2.3 %collective-permute-start.29 = (f32[2,4,64,256]{3,2,1,0:T(8,128)}, f32[2,4,64,256]{3,2,1,0:T(8,128)}, u32[]{:S(2)}, u32[]{:S(2)}) collective-permute-start(f32[2,4,64,256]{3,2,1,0:T(8,128)} %get-tuple-element.79), channel_id=1, source_target_pairs={{0,3},{1,2},{2,1},{3,0},{4,7},{5,6},{6,5},{7,4},{8,11},{9,10},{10,... | collective-permute-start | bytes 1572872 | tf_op jit(solution)/shard_map/ppermute | solution.py:23
  122.8 0.8 copy-done.11
  123.6 1.5 collective-permute-start.30
  125.1 1.0 copy-done.10
  126.1 1.0 copy-done.12
  127.1 2.1 %shard_map.33 = (f32[4,64,256]{2,1,0:T(8,128)S(1)}, f32[4,64,256]{2,1,0:T(8,128)}) custom-call(s32[1]{0:T(128)} %bitcast.2.side, f32[4,2,4,64,256]{4,3,2,1,0:T(8,128)S(1)} %get-tuple-element.62.keep, f32[2,4,64,256]{3,2,1,0:T(8,128)S(1)} %collective-permute-done.14.got, f32[2,4,64,256]{3,2,1,0:T(8,128)S(1)} %copy-done.10, f32[2,4,64,256]{3,2,1,0:T(8,128)S(1)} %copy-done.12, ...), custom_call_target="tpu_custom_call" | custom-call | flops 1 | bytes 1 | tf_op jit(solution)/shard_map/pallas_call | solution.py:40
  129.2 2.7 %collective-permute-start.21 = (f32[4,64,256]{2,1,0:T(8,128)}, f32[4,64,256]{2,1,0:T(8,128)S(1)}, u32[]{:S(2)}, u32[]{:S(2)}) collective-permute-start(f32[4,64,256]{2,1,0:T(8,128)} %get-tuple-element.71), channel_id=1, source_target_pairs={{0,64},{1,65},{2,66},{3,67},{4,68},{5,69},{6,70},{7,71},{8,72},{9,... | collective-permute-start | bytes 786440 | tf_op jit(solution)/shard_map/ppermute | solution.py:23
  131.9 2.4 %collective-permute-done.29.refs_1_ = f32[2,4,64,256]{3,2,1,0:T(8,128)} collective-permute-done((f32[2,4,64,256]{3,2,1,0:T(8,128)}, f32[2,4,64,256]{3,2,1,0:T(8,128)}, u32[]{:S(2)}, u32[]{:S(2)}) %collective-permute-start.29) | collective-permute-done | bytes 524320 | tf_op jit(solution)/shard_map/ppermute | solution.py:23
  134.4 4.4 %collective-permute-done.30.refs_2_ = f32[2,4,64,256]{3,2,1,0:T(8,128)} collective-permute-done((f32[2,4,64,256]{3,2,1,0:T(8,128)}, f32[2,4,64,256]{3,2,1,0:T(8,128)}, u32[]{:S(2)}, u32[]{:S(2)}) %collective-permute-start.30) | collective-permute-done | bytes 524320 | tf_op jit(solution)/shard_map/ppermute | solution.py:23
  138.7 1.7 %shard_map.36 = (f32[4,64,256]{2,1,0:T(8,128)S(1)}, f32[4,64,256]{2,1,0:T(8,128)S(1)}) custom-call(s32[1]{0:T(128)} %bitcast.2.side, f32[4,2,4,64,256]{4,3,2,1,0:T(8,128)S(1)} %copy-done.1, f32[2,4,64,256]{3,2,1,0:T(8,128)} %collective-permute-done.24.got, f32[2,4,64,256]{3,2,1,0:T(8,128)} %collective-permute-done.28.refs_0_, ...), custom_call_target="tpu_custom_call" | custom-call | flops 1 | bytes 1 | tf_op jit(solution)/shard_map/pallas_call | solution.py:40
  140.4 3.1 %collective-permute-start.31 = (f32[4,64,256]{2,1,0:T(8,128)S(1)}, f32[4,64,256]{2,1,0:T(8,128)S(1)}, u32[]{:S(2)}, u32[]{:S(2)}) collective-permute-start(f32[4,64,256]{2,1,0:T(8,128)S(1)} %get-tuple-element.82), channel_id=1, source_target_pairs={{0,64},{1,65},{2,66},{3,67},{4,68},{5,69},{6,70},{7,71},{8,72},{9,... | collective-permute-start | bytes 786440 | tf_op jit(solution)/shard_map/ppermute | solution.py:23
  143.6 2.9 %collective-permute-done.21.other_one = f32[4,64,256]{2,1,0:T(8,128)S(1)} collective-permute-done((f32[4,64,256]{2,1,0:T(8,128)}, f32[4,64,256]{2,1,0:T(8,128)S(1)}, u32[]{:S(2)}, u32[]{:S(2)}) %collective-permute-start.21) | collective-permute-done | bytes 262176 | tf_op jit(solution)/shard_map/ppermute | solution.py:23
  146.4 2.8 %collective-permute-done.31.other_two = f32[4,64,256]{2,1,0:T(8,128)S(1)} collective-permute-done((f32[4,64,256]{2,1,0:T(8,128)S(1)}, f32[4,64,256]{2,1,0:T(8,128)S(1)}, u32[]{:S(2)}, u32[]{:S(2)}) %collective-permute-start.31) | collective-permute-done | bytes 262176 | tf_op jit(solution)/shard_map/ppermute | solution.py:23
  149.3 1.4 shard_map.37
  (40 shorter events, 0.9 us)
Async XLA Ops:
  1.3 14.9 %collective-permute-start.2 = (f32[64,1024]{1,0:T(8,128)S(1)}, f32[64,1024]{1,0:T(8,128)S(1)}, u32[]{:S(2)}, u32[]{:S(2)}) collective-permute-start(f32[64,1024]{1,0:T(8,128)S(1)} %get-tuple-element.86), channel_id=1, source_target_pairs={{0,3},{1,2},{2,1},{3,0},{4,7},{5,6},{6,5},{7,4},{8,11},{9,10},{10,... | collective-permute-start | bytes 786440 | tf_op jit(solution)/shard_map/ppermute | solution.py:23
  4.5 12.6 %collective-permute-start.1 = (f32[64,1024]{1,0:T(8,128)S(1)}, f32[64,1024]{1,0:T(8,128)S(1)}, u32[]{:S(2)}, u32[]{:S(2)}) collective-permute-start(f32[64,1024]{1,0:T(8,128)S(1)} %get-tuple-element.83), channel_id=1, source_target_pairs={{0,2},{1,3},{2,0},{3,1},{4,6},{5,7},{6,4},{7,5},{8,10},{9,11},{10,... | collective-permute-start | bytes 786440 | tf_op jit(solution)/shard_map/ppermute | solution.py:23
  5.1 17.6 %collective-permute-start = (f32[64,1024]{1,0:T(8,128)S(1)}, f32[64,1024]{1,0:T(8,128)S(1)}, u32[]{:S(2)}, u32[]{:S(2)}) collective-permute-start(f32[64,1024]{1,0:T(8,128)S(1)} %get-tuple-element.84), channel_id=1, source_target_pairs={{0,1},{1,0},{2,3},{3,2},{4,5},{5,4},{6,7},{7,6},{8,9},{9,8},{10,11... | collective-permute-start | bytes 786440 | tf_op jit(solution)/shard_map/ppermute | solution.py:23
  5.5 17.4 %collective-permute-start.3 = (f32[64,1024]{1,0:T(8,128)S(1)}, f32[64,1024]{1,0:T(8,128)S(1)}, u32[]{:S(2)}, u32[]{:S(2)}) collective-permute-start(f32[64,1024]{1,0:T(8,128)S(1)} %get-tuple-element.83), channel_id=1, source_target_pairs={{0,16},{1,17},{2,18},{3,19},{4,20},{5,21},{6,22},{7,23},{8,24},{9,... | collective-permute-start | bytes 786440 | tf_op jit(solution)/shard_map/ppermute | solution.py:23
  7.0 15.8 %collective-permute-start.4 = (f32[64,1024]{1,0:T(8,128)S(1)}, f32[64,1024]{1,0:T(8,128)S(1)}, u32[]{:S(2)}, u32[]{:S(2)}) collective-permute-start(f32[64,1024]{1,0:T(8,128)S(1)} %get-tuple-element.86), channel_id=1, source_target_pairs={{0,17},{1,16},{2,19},{3,18},{4,21},{5,20},{6,23},{7,22},{8,25},{9,... | collective-permute-start | bytes 786440 | tf_op jit(solution)/shard_map/ppermute | solution.py:23
  22.7 30.0 %copy-start.2 = (f32[4096,256]{1,0:T(8,128)S(1)}, f32[4096,256]{1,0:T(8,128)}, u32[]{:S(2)}) copy-start(f32[4096,256]{1,0:T(8,128)} %value.1) | copy-start | bytes 12582916
  22.8 27.0 %copy-start.3 = (f32[4,64,1024]{2,1,0:T(8,128)}, f32[4,64,1024]{2,1,0:T(8,128)S(1)}, u32[]{:S(2)}) copy-start(f32[4,64,1024]{2,1,0:T(8,128)S(1)} %pad_maximum_fusion.refs_0_) | copy-start | bytes 3145732
  22.9 24.2 %collective-permute-start.7 = (f32[4,64,1024]{2,1,0:T(8,128)S(1)}, f32[4,64,1024]{2,1,0:T(8,128)S(1)}, u32[]{:S(2)}, u32[]{:S(2)}) collective-permute-start(f32[4,64,1024]{2,1,0:T(8,128)S(1)} %pad_maximum_fusion.refs_0_), channel_id=1, source_target_pairs={{0,4},{1,5},{2,6},{3,7},{4,0},{5,1},{6,2},{7,3},{8,12},{9,13},{10,... | collective-permute-start | bytes 3145736 | tf_op jit(solution)/shard_map/ppermute | solution.py:23
  24.9 25.0 %collective-permute-start.8 = (f32[4,64,1024]{2,1,0:T(8,128)S(1)}, f32[4,64,1024]{2,1,0:T(8,128)}, u32[]{:S(2)}, u32[]{:S(2)}) collective-permute-start(f32[4,64,1024]{2,1,0:T(8,128)S(1)} %pad_maximum_fusion.refs_0_), channel_id=1, source_target_pairs={{0,12},{1,13},{2,14},{3,15},{4,8},{5,9},{6,10},{7,11},{8,4},{9,5},... | collective-permute-start | bytes 3145736 | tf_op jit(solution)/shard_map/ppermute | solution.py:23
  27.4 11.6 %collective-permute-start.6 = (f32[64,1024]{1,0:T(8,128)S(1)}, f32[64,1024]{1,0:T(8,128)S(1)}, u32[]{:S(2)}, u32[]{:S(2)}) collective-permute-start(f32[64,1024]{1,0:T(8,128)S(1)} %get-tuple-element.84), channel_id=1, source_target_pairs={{0,19},{1,18},{2,17},{3,16},{4,23},{5,22},{6,21},{7,20},{8,27},{9,... | collective-permute-start | bytes 786440 | tf_op jit(solution)/shard_map/ppermute | solution.py:23
  31.2 10.8 %collective-permute-start.5 = (f32[64,1024]{1,0:T(8,128)S(1)}, f32[64,1024]{1,0:T(8,128)S(1)}, u32[]{:S(2)}, u32[]{:S(2)}) collective-permute-start(f32[64,1024]{1,0:T(8,128)S(1)} %get-tuple-element.85), channel_id=1, source_target_pairs={{0,18},{1,19},{2,16},{3,17},{4,22},{5,23},{6,20},{7,21},{8,26},{9,... | collective-permute-start | bytes 786440 | tf_op jit(solution)/shard_map/ppermute | solution.py:23
  47.0 1.0 copy-start.5
  49.8 23.1 %collective-permute-start.9 = (f32[4,64,1024]{2,1,0:T(8,128)S(1)}, f32[4,64,1024]{2,1,0:T(8,128)}, u32[]{:S(2)}, u32[]{:S(2)}) collective-permute-start(f32[4,64,1024]{2,1,0:T(8,128)S(1)} %pad_maximum_fusion.1._.refs_0_), channel_id=1, source_target_pairs={{0,4},{1,5},{2,6},{3,7},{4,0},{5,1},{6,2},{7,3},{8,12},{9,13},{10,... | collective-permute-start | bytes 3145736 | tf_op jit(solution)/shard_map/ppermute | solution.py:23
  50.4 23.9 %collective-permute-start.10 = (f32[4,64,1024]{2,1,0:T(8,128)S(1)}, f32[4,64,1024]{2,1,0:T(8,128)S(1)}, u32[]{:S(2)}, u32[]{:S(2)}) collective-permute-start(f32[4,64,1024]{2,1,0:T(8,128)S(1)} %pad_maximum_fusion.1._.refs_0_), channel_id=1, source_target_pairs={{0,12},{1,13},{2,14},{3,15},{4,8},{5,9},{6,10},{7,11},{8,4},{9,5},... | collective-permute-start | bytes 3145736 | tf_op jit(solution)/shard_map/ppermute | solution.py:23
  54.6 22.7 %collective-permute-start.11 = (f32[1024,256]{1,0:T(8,128)}, f32[1024,256]{1,0:T(8,128)S(1)}, u32[]{:S(2)}, u32[]{:S(2)}) collective-permute-start(f32[1024,256]{1,0:T(8,128)} %get-tuple-element.51), channel_id=1, source_target_pairs={{0,1},{1,0},{2,3},{3,2},{4,5},{5,4},{6,7},{7,6},{8,9},{9,8},{10,11... | collective-permute-start | bytes 3145736 | tf_op jit(solution)/shard_map/ppermute | solution.py:23
  56.0 23.2 %collective-permute-start.12 = (f32[1024,256]{1,0:T(8,128)}, f32[1024,256]{1,0:T(8,128)}, u32[]{:S(2)}, u32[]{:S(2)}) collective-permute-start(f32[1024,256]{1,0:T(8,128)} %get-tuple-element.52), channel_id=1, source_target_pairs={{0,3},{1,2},{2,1},{3,0},{4,7},{5,6},{6,5},{7,4},{8,11},{9,10},{10,... | collective-permute-start | bytes 3145736 | tf_op jit(solution)/shard_map/ppermute | solution.py:23
  58.2 21.7 %collective-permute-start.13 = (f32[1024,256]{1,0:T(8,128)}, f32[1024,256]{1,0:T(8,128)}, u32[]{:S(2)}, u32[]{:S(2)}) collective-permute-start(f32[1024,256]{1,0:T(8,128)} %get-tuple-element.53), channel_id=1, source_target_pairs={{0,16},{1,17},{2,18},{3,19},{4,20},{5,21},{6,22},{7,23},{8,24},{9,... | collective-permute-start | bytes 3145736 | tf_op jit(solution)/shard_map/ppermute | solution.py:23
  72.9 25.8 %collective-permute-start.22 = (f32[4,64,1024]{2,1,0:T(8,128)}, f32[4,64,1024]{2,1,0:T(8,128)}, u32[]{:S(2)}, u32[]{:S(2)}) collective-permute-start(f32[4,64,1024]{2,1,0:T(8,128)} %collective-permute-done.8.refs_1_), channel_id=1, source_target_pairs={{0,4},{1,5},{2,6},{3,7},{4,0},{5,1},{6,2},{7,3},{8,12},{9,13},{10,... | collective-permute-start | bytes 3145736 | tf_op jit(solution)/shard_map/ppermute | solution.py:23
  74.3 1.0 copy-start.7
  75.3 23.4 %collective-permute-start.23 = (f32[4,64,1024]{2,1,0:T(8,128)}, f32[4,64,1024]{2,1,0:T(8,128)}, u32[]{:S(2)}, u32[]{:S(2)}) collective-permute-start(f32[4,64,1024]{2,1,0:T(8,128)} %collective-permute-done.9.refs_2_), channel_id=1, source_target_pairs={{0,12},{1,13},{2,14},{3,15},{4,8},{5,9},{6,10},{7,11},{8,4},{9,5},... | collective-permute-start | bytes 3145736 | tf_op jit(solution)/shard_map/ppermute | solution.py:23
  79.9 2.4 %copy-start.4 = (f32[4,64,1024]{2,1,0:T(8,128)S(1)}, f32[4,64,1024]{2,1,0:T(8,128)}, u32[]{:S(2)}) copy-start(f32[4,64,1024]{2,1,0:T(8,128)} %copy-done.3) | copy-start | bytes 3145732
  79.9 2.4 %copy-start.6 = (f32[4,64,1024]{2,1,0:T(8,128)S(1)}, f32[4,64,1024]{2,1,0:T(8,128)}, u32[]{:S(2)}) copy-start(f32[4,64,1024]{2,1,0:T(8,128)} %copy-done.5) | copy-start | bytes 3145732
  82.3 6.4 %copy-start.8 = (f32[4,64,1024]{2,1,0:T(8,128)S(1)}, f32[4,64,1024]{2,1,0:T(8,128)}, u32[]{:S(2)}) copy-start(f32[4,64,1024]{2,1,0:T(8,128)} %copy-done.7) | copy-start | bytes 3145732
  95.0 2.0 %collective-permute-start.15 = (f32[2,4,64,256]{3,2,1,0:T(8,128)S(1)}, f32[2,4,64,256]{3,2,1,0:T(8,128)S(1)}, u32[]{:S(2)}, u32[]{:S(2)}) collective-permute-start(f32[2,4,64,256]{3,2,1,0:T(8,128)S(1)} %get-tuple-element.64), channel_id=1, source_target_pairs={{0,32},{1,33},{2,34},{3,35},{4,36},{5,37},{6,38},{7,39},{8,40},{9,... | collective-permute-start | bytes 1572872 | tf_op jit(solution)/shard_map/ppermute | solution.py:23
  95.1 2.6 %collective-permute-start.16 = (f32[2,4,64,256]{3,2,1,0:T(8,128)S(1)}, f32[2,4,64,256]{3,2,1,0:T(8,128)S(1)}, u32[]{:S(2)}, u32[]{:S(2)}) collective-permute-start(f32[2,4,64,256]{3,2,1,0:T(8,128)S(1)} %get-tuple-element.65), channel_id=1, source_target_pairs={{0,32},{1,33},{2,34},{3,35},{4,36},{5,37},{6,38},{7,39},{8,40},{9,... | collective-permute-start | bytes 1572872 | tf_op jit(solution)/shard_map/ppermute | solution.py:23
  95.6 2.9 %collective-permute-start.17 = (f32[2,4,64,256]{3,2,1,0:T(8,128)S(1)}, f32[2,4,64,256]{3,2,1,0:T(8,128)S(1)}, u32[]{:S(2)}, u32[]{:S(2)}) collective-permute-start(f32[2,4,64,256]{3,2,1,0:T(8,128)S(1)} %get-tuple-element.66), channel_id=1, source_target_pairs={{0,32},{1,33},{2,34},{3,35},{4,36},{5,37},{6,38},{7,39},{8,40},{9,... | collective-permute-start | bytes 1572872 | tf_op jit(solution)/shard_map/ppermute | solution.py:23
  103.8 2.0 %collective-permute-start.25 = (f32[2,4,64,256]{3,2,1,0:T(8,128)S(1)}, f32[2,4,64,256]{3,2,1,0:T(8,128)S(1)}, u32[]{:S(2)}, u32[]{:S(2)}) collective-permute-start(f32[2,4,64,256]{3,2,1,0:T(8,128)S(1)} %get-tuple-element.75), channel_id=1, source_target_pairs={{0,32},{1,33},{2,34},{3,35},{4,36},{5,37},{6,38},{7,39},{8,40},{9,... | collective-permute-start | bytes 1572872 | tf_op jit(solution)/shard_map/ppermute | solution.py:23
  104.0 4.1 %collective-permute-start.26 = (f32[2,4,64,256]{3,2,1,0:T(8,128)S(1)}, f32[2,4,64,256]{3,2,1,0:T(8,128)S(1)}, u32[]{:S(2)}, u32[]{:S(2)}) collective-permute-start(f32[2,4,64,256]{3,2,1,0:T(8,128)S(1)} %get-tuple-element.76), channel_id=1, source_target_pairs={{0,32},{1,33},{2,34},{3,35},{4,36},{5,37},{6,38},{7,39},{8,40},{9,... | collective-permute-start | bytes 1572872 | tf_op jit(solution)/shard_map/ppermute | solution.py:23
  104.4 5.2 %collective-permute-start.27 = (f32[2,4,64,256]{3,2,1,0:T(8,128)S(1)}, f32[2,4,64,256]{3,2,1,0:T(8,128)S(1)}, u32[]{:S(2)}, u32[]{:S(2)}) collective-permute-start(f32[2,4,64,256]{3,2,1,0:T(8,128)S(1)} %get-tuple-element.77), channel_id=1, source_target_pairs={{0,32},{1,33},{2,34},{3,35},{4,36},{5,37},{6,38},{7,39},{8,40},{9,... | collective-permute-start | bytes 1572872 | tf_op jit(solution)/shard_map/ppermute | solution.py:23
  104.5 7.8 %collective-permute-start.14 = (f32[2,4,64,256]{3,2,1,0:T(8,128)S(1)}, f32[2,4,64,256]{3,2,1,0:T(8,128)S(1)}, u32[]{:S(2)}, u32[]{:S(2)}) collective-permute-start(f32[2,4,64,256]{3,2,1,0:T(8,128)S(1)} %get-tuple-element.63), channel_id=1, source_target_pairs={{0,32},{1,33},{2,34},{3,35},{4,36},{5,37},{6,38},{7,39},{8,40},{9,... | collective-permute-start | bytes 1572872 | tf_op jit(solution)/shard_map/ppermute | solution.py:23
  104.9 14.8 %collective-permute-start.18 = (f32[2,4,64,256]{3,2,1,0:T(8,128)S(1)}, f32[2,4,64,256]{3,2,1,0:T(8,128)S(1)}, u32[]{:S(2)}, u32[]{:S(2)}) collective-permute-start(f32[2,4,64,256]{3,2,1,0:T(8,128)S(1)} %get-tuple-element.67.refs_2_), channel_id=1, source_target_pairs={{0,1},{1,0},{2,3},{3,2},{4,5},{5,4},{6,7},{7,6},{8,9},{9,8},{10,11... | collective-permute-start | bytes 1572872 | tf_op jit(solution)/shard_map/ppermute | solution.py:23
  105.8 17.0 %collective-permute-start.19 = (f32[2,4,64,256]{3,2,1,0:T(8,128)S(1)}, f32[2,4,64,256]{3,2,1,0:T(8,128)S(1)}, u32[]{:S(2)}, u32[]{:S(2)}) collective-permute-start(f32[2,4,64,256]{3,2,1,0:T(8,128)S(1)} %get-tuple-element.68.refs_3_), channel_id=1, source_target_pairs={{0,3},{1,2},{2,1},{3,0},{4,7},{5,6},{6,5},{7,4},{8,11},{9,10},{10,... | collective-permute-start | bytes 1572872 | tf_op jit(solution)/shard_map/ppermute | solution.py:23
  108.1 17.0 %collective-permute-start.20 = (f32[2,4,64,256]{3,2,1,0:T(8,128)S(1)}, f32[2,4,64,256]{3,2,1,0:T(8,128)}, u32[]{:S(2)}, u32[]{:S(2)}) collective-permute-start(f32[2,4,64,256]{3,2,1,0:T(8,128)S(1)} %get-tuple-element.69.refs_4_), channel_id=1, source_target_pairs={{0,16},{1,17},{2,18},{3,19},{4,20},{5,21},{6,22},{7,23},{8,24},{9,... | collective-permute-start | bytes 1572872 | tf_op jit(solution)/shard_map/ppermute | solution.py:23
  109.6 22.4 %collective-permute-start.24 = (f32[2,4,64,256]{3,2,1,0:T(8,128)}, f32[2,4,64,256]{3,2,1,0:T(8,128)}, u32[]{:S(2)}, u32[]{:S(2)}) collective-permute-start(f32[2,4,64,256]{3,2,1,0:T(8,128)} %get-tuple-element.74), channel_id=1, source_target_pairs={{0,32},{1,33},{2,34},{3,35},{4,36},{5,37},{6,38},{7,39},{8,40},{9,... | collective-permute-start | bytes 1572872 | tf_op jit(solution)/shard_map/ppermute | solution.py:23
  110.9 1.3 copy-start
  112.2 19.7 %collective-permute-start.28 = (f32[2,4,64,256]{3,2,1,0:T(8,128)}, f32[2,4,64,256]{3,2,1,0:T(8,128)}, u32[]{:S(2)}, u32[]{:S(2)}) collective-permute-start(f32[2,4,64,256]{3,2,1,0:T(8,128)} %get-tuple-element.78), channel_id=1, source_target_pairs={{0,1},{1,0},{2,3},{3,2},{4,5},{5,4},{6,7},{7,6},{8,9},{9,8},{10,11... | collective-permute-start | bytes 1572872 | tf_op jit(solution)/shard_map/ppermute | solution.py:23
  119.6 0.8 copy-start.9
  120.4 14.0 %collective-permute-start.29 = (f32[2,4,64,256]{3,2,1,0:T(8,128)}, f32[2,4,64,256]{3,2,1,0:T(8,128)}, u32[]{:S(2)}, u32[]{:S(2)}) collective-permute-start(f32[2,4,64,256]{3,2,1,0:T(8,128)} %get-tuple-element.79), channel_id=1, source_target_pairs={{0,3},{1,2},{2,1},{3,0},{4,7},{5,6},{6,5},{7,4},{8,11},{9,10},{10,... | collective-permute-start | bytes 1572872 | tf_op jit(solution)/shard_map/ppermute | solution.py:23
  122.8 0.8 copy-start.11
  123.6 15.2 %collective-permute-start.30 = (f32[2,4,64,256]{3,2,1,0:T(8,128)}, f32[2,4,64,256]{3,2,1,0:T(8,128)}, u32[]{:S(2)}, u32[]{:S(2)}) collective-permute-start(f32[2,4,64,256]{3,2,1,0:T(8,128)} %get-tuple-element.80), channel_id=1, source_target_pairs={{0,16},{1,17},{2,18},{3,19},{4,20},{5,21},{6,22},{7,23},{8,24},{9,... | collective-permute-start | bytes 1572872 | tf_op jit(solution)/shard_map/ppermute | solution.py:23
  125.1 1.0 copy-start.10
  126.1 1.0 copy-start.12
  127.1 11.6 %copy-start.1 = (f32[4,2,4,64,256]{4,3,2,1,0:T(8,128)S(1)}, f32[4,2,4,64,256]{4,3,2,1,0:T(8,128)}, u32[]{:S(2)}) copy-start(f32[4,2,4,64,256]{4,3,2,1,0:T(8,128)} %copy-done) | copy-start | bytes 6291460
  129.2 17.2 %collective-permute-start.21 = (f32[4,64,256]{2,1,0:T(8,128)}, f32[4,64,256]{2,1,0:T(8,128)S(1)}, u32[]{:S(2)}, u32[]{:S(2)}) collective-permute-start(f32[4,64,256]{2,1,0:T(8,128)} %get-tuple-element.71), channel_id=1, source_target_pairs={{0,64},{1,65},{2,66},{3,67},{4,68},{5,69},{6,70},{7,71},{8,72},{9,... | collective-permute-start | bytes 786440 | tf_op jit(solution)/shard_map/ppermute | solution.py:23
  140.4 8.9 %collective-permute-start.31 = (f32[4,64,256]{2,1,0:T(8,128)S(1)}, f32[4,64,256]{2,1,0:T(8,128)S(1)}, u32[]{:S(2)}, u32[]{:S(2)}) collective-permute-start(f32[4,64,256]{2,1,0:T(8,128)S(1)} %get-tuple-element.82), channel_id=1, source_target_pairs={{0,64},{1,65},{2,66},{3,67},{4,68},{5,69},{6,70},{7,71},{8,72},{9,... | collective-permute-start | bytes 786440 | tf_op jit(solution)/shard_map/ppermute | solution.py:23

commit v11 on v10

--- a/solution.py
+++ b/solution.py
@@ -6,7 +6,7 @@
 from jax.sharding import PartitionSpec as P
 
 AXES = ("rep", "grid")
-PARAMS = pltpu.CompilerParams(vmem_limit_bytes=26 * 1024 * 1024)
+PARAMS = pltpu.CompilerParams(vmem_limit_bytes=20 * 1024 * 1024)
 SHORT = pl.CostEstimate(flops=1, bytes_accessed=1, transcendentals=0)
 NEAR = (dict(), dict(dy=1), dict(dy=3), dict(dx=1))
 
@@ -21,6 +21,12 @@
         for h in range(2) for c in range(2) for x in range(2) for z in range(4) for y in range(4)
     ]
     return lax.ppermute(value, AXES, pairs)
+
+
+CORES = [
+    [number(h, c, x, z, y) for c in range(2)]
+    for h in range(2) for x in range(2) for z in range(4) for y in range(4)
+]
 
 
 def halves(value):
@@ -103,7 +109,7 @@
 
 
 def places(d):
-    return [(block, block ^ (0, 1, 3, 0)[d]) for block in range(4)]
+    return [(block, block ^ (0, 1, 3, 2)[d]) for block in range(4)]
 
 
 def early_products(swap, part, planes, rights, before=()):
@@ -153,34 +159,46 @@
     )
 
 
-def late_products(swap, parts, third, rights, after):
+def late_products(flags, parts, third, rights, after):
     arrays = [array for part in parts for array in part]
     rows, depth = arrays[0].shape[1:]
     columns = rights[0].shape[1] // 4
 
-    def kernel(swap, *refs):
+    def kernel(flags, *refs):
         blocks, rest = refs[: len(arrays)], refs[len(arrays) + len(after):]
-        high, low, ahead, keep, *gives, left_high, left_low = rest
-        swapped = swap[0] == 1
+        high, low, ahead, keep, give, both, left_high, left_low = rest
+        swapped, core = flags[0] == 1, flags[1]
 
         def store(d, total):
             for part in range(2):
                 for block, into in places(d):
                     zero, one = ahead[d, part, into], total[part, block]
-                    keep[d, part, into] = jnp.where(swapped, one, zero)
-                    gives[d][part, into] = jnp.where(swapped, zero, one)
+                    kept, given = jnp.where(swapped, one, zero), jnp.where(swapped, zero, one)
+                    if d == 0:
+                        keep[0, part, into], give[part, into] = kept, given
+                    else:
+                        both[core, d - 1, part, into], both[1 - core, d - 1, part, into] = kept, given
 
         multiplied(blocks, left_high, left_low, high, low, store)
 
-    kept = jax.ShapeDtypeStruct((4, 2, 4, rows, columns), jnp.float32)
-    given = jax.ShapeDtypeStruct((2, 4, rows, columns), jnp.float32)
-    shapes = [kept] + [given] * 4
+    piece = (2, 4, rows, columns)
+    shapes = [jax.ShapeDtypeStruct(shape, jnp.float32) for shape in ((1, *piece), piece, (2, 3, *piece))]
     scratch = pltpu.VMEM((8 * rows, depth), jnp.bfloat16)
     return call(
-        kernel, swap, (*arrays, *after, *rights, third),
+        kernel, flags, (*arrays, *after, *rights, third),
         [whole(array) for array in arrays] + [ANYWHERE] * len(after) + [VMEM] * 2 + [whole(third)],
         shapes, [whole(shape) for shape in shapes], [scratch] * 2,
     )
+
+
+def added_by_core_kernel(_, both, *outs):
+    for d, out in enumerate(outs):
+        out[...] = both[0, d] + both[1, d]
+
+
+def added_by_core(scalars, both):
+    shape = jax.ShapeDtypeStruct(both.shape[2:], jnp.float32)
+    return call(added_by_core_kernel, scalars, (both,), [whole(both)], [shape] * 3, [whole(shape)] * 3)
 
 
 def sum_kernel(side, keep, got, *refs):
@@ -225,10 +243,7 @@
         return lax.dynamic_slice(left, (0, (quarter ^ d) * depth), (rows, depth))
 
     mine = jnp.stack([block(0), send(block(1), dy=1), send(block(3), dy=2), send(block(2), dy=3)])
-    others = [send(block(3), dx=1), send(block(2), dx=1, dy=1)]
-    mine, *others = lax.optimization_barrier((mine, *others))
-    others += [send(block(0), dx=1, dy=2), send(block(1), dx=1, dy=3)]
-    other = jnp.stack(others)
+    other = send(mine, dx=1, dy=2)
     own_one, own_three = send(mine, dz=1), send(mine, dz=3)
     far, *_ = lax.optimization_barrier((other, own_one, own_three))
     far_one, far_three = lax.optimization_barrier((send(far, dz=1), send(far, dz=3)))
@@ -242,18 +257,21 @@
     before = early_products(swap, 0, ((mine,), (own_three,), (own_one,)), rights)
     early = early_products(swap, 1, ((far,), (far_three,), (far_one,)), rights, before)
 
-    ends, third, after = [], early[1], None
-    for last in (False, True):
-        if last:
-            keep, *gives = late_products(swap, ((own_two,), (far_two,)), third, rights, after)
-        else:
-            keep, _, *gives = early
-        got = [send(give, core=1) for give in gives]
-        after = added(swap, keep, got[1:])
-        here, there = summed(side, keep, got[0], [send(after[d - 1], **NEAR[d]) for d in range(1, 4)])
+    keep, third, *gives = early
+    got = [send(give, core=1) for give in gives]
+    sums = added(swap, keep, got[1:])
+    late_keep, late_give, both = late_products(
+        jnp.stack([swap[0], core]), ((own_two,), (far_two,)), third, rights, sums
+    )
+    both = lax.all_to_all(both, AXES, 0, 0, tiled=True, axis_index_groups=CORES)
+
+    ends = []
+    for kept, given, terms in ((keep, got[0], sums), (late_keep, send(late_give, core=1), added_by_core(swap, both))):
+        across = send(terms[2], **NEAR[3])
+        here, there = summed(side, kept, given, [send(terms[0], **NEAR[1]), send(terms[1], **NEAR[2]), across])
         ends += [here, send(there, dhi=1)]
 
-    total = join(jnp.stack([(z & 1) ^ swap[0], y]), ends)
+    total = join(jnp.stack([(z & 1) ^ swap[0], y ^ (2 * side[0])]), ends)
     return total.reshape(8 * rows, columns)
 
 

time: 151 us -> 143 us (0.947)
  starting transfers between devices: 43.4 us -> 35.4 us
  blocking collectives: 0 us -> 6.26 us
  local copies, waits for them, and re-layouts: 8.26 us -> 4.3 us
    ppermute x32 -> x26, starting transfers between devices: 43.4 us -> 35.4 us  [send(): return lax.ppermute(value, AXES, pairs)]
    all_to_all x0 -> x1, blocking collectives: none -> 6.26 us  [per_device(): both = lax.all_to_all(both, AXES, 0, 0, tiled=True, axis_index_groups=CORES)]
    unnamed x26 -> x22, local copies, waits for them, and re-layouts: 6.97 us -> 2.87 us
    ppermute x32 -> x26, waiting for transfers between devices: 70 us -> 68.5 us  [send(): return lax.ppermute(value, AXES, pairs)]
  transfers between devices with their start and end apart: 32 -> 26, of which waited for: 20 -> 17; matrix products, arithmetic and copies ran while one was open for 0% -> 0% of each run, Pallas kernels for 15% -> 18%
where the time goes in v11:
time: 143 us; the launch traced here: 142 us
  waiting for transfers between devices  68.5 us (48%)
  starting transfers between devices  35.4 us (25%)
  Pallas kernels  27.4 us (19%)
  blocking collectives  6.26 us (4%)
  local copies, waits for them, and re-layouts  4.3 us (3%)
    ppermute x26, waiting for transfers between devices, send(): return lax.ppermute(value, AXES, pairs)  68.5 us
    ppermute x26, starting transfers between devices, send(): return lax.ppermute(value, AXES, pairs)  35.4 us
    pallas_call x10, Pallas kernels, call(): pl.pallas_call(kernel, grid_spec=pltpu.PrefetchScalarGridSpec(num_scalar_...  27.4 us
    all_to_all x1, blocking collectives, per_device(): both = lax.all_to_all(both, AXES, 0, 0, tiled=True, axis_index_groups=CORES)  6.26 us
    unnamed x22, local copies, waits for them, and re-layouts  2.87 us
  transfers between devices with their start and end apart: 26, of which 17 were waited for; matrix products, arithmetic and copies ran while one was open for 0% of the time, Pallas kernels for 18%

profile of v11, /device:TPU:0, one launch (start us, length us, event | category | flops | bytes accessed | tf_op | source)
XLA Modules:
  0.0 142.3 jit_solution(12117216210832342610)
XLA Ops:
  0.0 1.4 %dynamic-slice_bitcast_fusion = (f32[1,64,1024]{2,1,0:T(8,128)S(1)}, f32[64,1024]{1,0:T(8,128)S(1)}, f32[64,1024]{1,0:T(8,128)S(1)}, f32[64,1024]{1,0:T(8,128)S(1)}) fusion(f32[64,4096]{1,0:T(8,128)} %param.2, s32[]{:T(128)S(6)} %select_n.12, s32[]{:T(128)S(6)} %select_n.13, s32[]{:T(128)S(6)} %select_n.15, s32[]{:T(128)S(6)} %select_n.14), kind=kLoop, calls=%fused_computation.1 | loop fusion | bytes 2097168 | tf_op jit(solution)/shard_map/stack | solution.py:245
  1.4 3.2 %collective-permute-start.2 = (f32[64,1024]{1,0:T(8,128)S(1)}, f32[64,1024]{1,0:T(8,128)S(1)}, u32[]{:S(2)}, u32[]{:S(2)}) collective-permute-start(f32[64,1024]{1,0:T(8,128)S(1)} %get-tuple-element.75), channel_id=1, source_target_pairs={{0,3},{1,2},{2,1},{3,0},{4,7},{5,6},{6,5},{7,4},{8,11},{9,10},{10,... | collective-permute-start | bytes 786440 | tf_op jit(solution)/shard_map/ppermute | solution.py:23
  4.6 0.6 collective-permute-start.1
  5.3 0.4 collective-permute-start
  5.6 10.9 %collective-permute-done.2 = f32[64,1024]{1,0:T(8,128)S(1)} collective-permute-done((f32[64,1024]{1,0:T(8,128)S(1)}, f32[64,1024]{1,0:T(8,128)S(1)}, u32[]{:S(2)}, u32[]{:S(2)}) %collective-permute-start.2) | collective-permute-done | bytes 262176 | tf_op jit(solution)/shard_map/ppermute | solution.py:23
  16.6 0.7 collective-permute-done
  17.3 0.1 pad_maximum_fusion.refs_0_
  17.3 4.0 %collective-permute-start.3 = (f32[4,64,1024]{2,1,0:T(8,128)S(1)}, f32[4,64,1024]{2,1,0:T(8,128)S(1)}, u32[]{:S(2)}, u32[]{:S(2)}) collective-permute-start(f32[4,64,1024]{2,1,0:T(8,128)S(1)} %pad_maximum_fusion.refs_0_), channel_id=1, source_target_pairs={{0,18},{1,19},{2,16},{3,17},{4,22},{5,23},{6,20},{7,21},{8,26},{9,... | collective-permute-start | bytes 3145736 | tf_op jit(solution)/shard_map/ppermute | solution.py:23
  21.4 1.9 %collective-permute-start.4 = (f32[4,64,1024]{2,1,0:T(8,128)S(1)}, f32[4,64,1024]{2,1,0:T(8,128)S(1)}, u32[]{:S(2)}, u32[]{:S(2)}) collective-permute-start(f32[4,64,1024]{2,1,0:T(8,128)S(1)} %pad_maximum_fusion.refs_0_), channel_id=1, source_target_pairs={{0,4},{1,5},{2,6},{3,7},{4,0},{5,1},{6,2},{7,3},{8,12},{9,13},{10,... | collective-permute-start | bytes 3145736 | tf_op jit(solution)/shard_map/ppermute | solution.py:23
  23.3 2.5 %collective-permute-start.5 = (f32[4,64,1024]{2,1,0:T(8,128)S(1)}, f32[4,64,1024]{2,1,0:T(8,128)S(1)}, u32[]{:S(2)}, u32[]{:S(2)}) collective-permute-start(f32[4,64,1024]{2,1,0:T(8,128)S(1)} %pad_maximum_fusion.refs_0_), channel_id=1, source_target_pairs={{0,12},{1,13},{2,14},{3,15},{4,8},{5,9},{6,10},{7,11},{8,4},{9,5},... | collective-permute-start | bytes 3145736 | tf_op jit(solution)/shard_map/ppermute | solution.py:23
  25.8 18.0 %collective-permute-done.3._.refs_0_ = f32[4,64,1024]{2,1,0:T(8,128)S(1)} collective-permute-done((f32[4,64,1024]{2,1,0:T(8,128)S(1)}, f32[4,64,1024]{2,1,0:T(8,128)S(1)}, u32[]{:S(2)}, u32[]{:S(2)}) %collective-permute-start.3) | collective-permute-done | bytes 1048608 | tf_op jit(solution)/shard_map/ppermute | solution.py:23
  43.8 1.2 collective-permute-done.4.refs_2_
  45.0 1.0 copy-done.5
  46.0 1.7 %collective-permute-done.5.refs_1_ = f32[4,64,1024]{2,1,0:T(8,128)S(1)} collective-permute-done((f32[4,64,1024]{2,1,0:T(8,128)S(1)}, f32[4,64,1024]{2,1,0:T(8,128)S(1)}, u32[]{:S(2)}, u32[]{:S(2)}) %collective-permute-start.5) | collective-permute-done | bytes 1048608 | tf_op jit(solution)/shard_map/ppermute | solution.py:23
  47.7 0.6 collective-permute-start.6
  48.3 2.3 %collective-permute-start.7 = (f32[4,64,1024]{2,1,0:T(8,128)S(1)}, f32[4,64,1024]{2,1,0:T(8,128)}, u32[]{:S(2)}, u32[]{:S(2)}) collective-permute-start(f32[4,64,1024]{2,1,0:T(8,128)S(1)} %collective-permute-done.3._.refs_0_), channel_id=1, source_target_pairs={{0,12},{1,13},{2,14},{3,15},{4,8},{5,9},{6,10},{7,11},{8,4},{9,5},... | collective-permute-start | bytes 3145736 | tf_op jit(solution)/shard_map/ppermute | solution.py:23
  50.7 1.8 %shard_map.28 = (f32[1024,256]{1,0:T(8,128)S(1)}, f32[1024,256]{1,0:T(8,128)}, f32[1024,256]{1,0:T(8,128)}, f32[1024,256]{1,0:T(8,128)}) custom-call(s32[1]{0:T(128)} %bitcast.8.quarter, f32[4096,256]{1,0:T(8,128)S(1)} %copy-done, f32[4,64,1024]{2,1,0:T(8,128)S(1)} %collective-permute-done.3._.refs_0_), custom_call_target="tpu_custom_call" | custom-call | flops 1 | bytes 1 | tf_op jit(solution)/shard_map/pallas_call | solution.py:46
  52.5 1.1 collective-permute-start.8
  53.5 1.0 collective-permute-start.9
  54.6 1.5 %collective-permute-start.10 = (f32[1024,256]{1,0:T(8,128)}, f32[1024,256]{1,0:T(8,128)}, u32[]{:S(2)}, u32[]{:S(2)}) collective-permute-start(f32[1024,256]{1,0:T(8,128)} %get-tuple-element.45), channel_id=1, source_target_pairs={{0,16},{1,17},{2,18},{3,19},{4,20},{5,21},{6,22},{7,23},{8,24},{9,... | collective-permute-start | bytes 3145736 | tf_op jit(solution)/shard_map/ppermute | solution.py:23
  56.0 14.8 %collective-permute-done.6.refs_2_ = f32[4,64,1024]{2,1,0:T(8,128)} collective-permute-done((f32[4,64,1024]{2,1,0:T(8,128)S(1)}, f32[4,64,1024]{2,1,0:T(8,128)}, u32[]{:S(2)}, u32[]{:S(2)}) %collective-permute-start.6) | collective-permute-done | bytes 1048608 | tf_op jit(solution)/shard_map/ppermute | solution.py:23
  70.8 0.6 collective-permute-start.19
  71.4 0.5 collective-permute-done.7.refs_1_
  71.9 2.1 %collective-permute-start.20 = (f32[4,64,1024]{2,1,0:T(8,128)}, f32[4,64,1024]{2,1,0:T(8,128)S(1)}, u32[]{:S(2)}, u32[]{:S(2)}) collective-permute-start(f32[4,64,1024]{2,1,0:T(8,128)} %collective-permute-done.6.refs_2_), channel_id=1, source_target_pairs={{0,12},{1,13},{2,14},{3,15},{4,8},{5,9},{6,10},{7,11},{8,4},{9,5},... | collective-permute-start | bytes 3145736 | tf_op jit(solution)/shard_map/ppermute | solution.py:23
  74.0 0.6 collective-permute-done.8.refs_1_
  74.6 2.2 %collective-permute-done.9.refs_2_ = f32[1024,256]{1,0:T(8,128)} collective-permute-done((f32[1024,256]{1,0:T(8,128)}, f32[1024,256]{1,0:T(8,128)}, u32[]{:S(2)}, u32[]{:S(2)}) %collective-permute-start.9) | collective-permute-done | bytes 1048608 | tf_op jit(solution)/shard_map/ppermute | solution.py:23
  76.8 0.0 collective-permute-done.10.refs_3_
  76.8 2.7 %shard_map.29 = (bf16[1024,1024]{1,0:T(8,128)(2,1)S(1)}, bf16[1024,1024]{1,0:T(8,128)(2,1)S(1)}) custom-call(s32[1]{0:T(128)} %bitcast.3._.swap, f32[1024,256]{1,0:T(8,128)S(1)} %get-tuple-element.42.refs_0_, f32[1024,256]{1,0:T(8,128)} %collective-permute-done.8.refs_1_, f32[1024,256]{1,0:T(8,128)} %collective-permute-done.9.refs_2_, ...), custom_call_target="tpu_custom_call" | custom-call | flops 1 | bytes 1 | tf_op jit(solution)/shard_map/pallas_call | solution.py:46
  79.6 5.0 %shard_map.30 = (f32[4,2,4,64,256]{4,3,2,1,0:T(8,128)S(1)}, f32[4,2,4,64,256]{4,3,2,1,0:T(8,128)S(1)}, f32[2,4,64,256]{3,2,1,0:T(8,128)S(1)}, f32[2,4,64,256]{3,...) custom-call(s32[1]{0:T(128)} %bitcast.3._.swap, ...), custom_call_target="tpu_custom_call" | custom-call | flops 1 | bytes 1 | tf_op jit(solution)/shard_map/pallas_call | solution.py:46
  84.6 6.6 %shard_map.31 = (f32[4,2,4,64,256]{4,3,2,1,0:T(8,128)S(1)}, f32[4,2,4,64,256]{4,3,2,1,0:T(8,128)S(1)}, f32[2,4,64,256]{3,2,1,0:T(8,128)S(1)}, f32[2,4,64,256]{3,...) custom-call(s32[1]{0:T(128)} %bitcast.3._.swap, ...), custom_call_target="tpu_custom_call", output_to_operand_aliasing={{0}: (4, {}), {1}: (5, {}), {2}: (6, {}), {3}: (7, {}), {4}... | custom-call | flops 1 | bytes 1 | tf_op jit(solution)/shard_map/pallas_call | solution.py:46
  91.2 0.1 collective-permute-start.12
  91.3 0.5 collective-permute-start.13
  91.8 0.3 collective-permute-start.14
  92.1 1.1 collective-permute-done.12.refs_0_
  93.2 0.1 collective-permute-start.11
  93.3 0.6 collective-permute-done.13.refs_1_
  94.0 0.7 collective-permute-done.14.refs_2_
  94.7 1.0 shard_map.32
  95.7 1.0 collective-permute-start.15
  96.7 0.9 collective-permute-start.16
  97.6 0.1 pad_add_fusion.1.flags
  97.7 0.0 collective-permute-done.19.refs_0_
  97.7 1.5 %collective-permute-start.17 = (f32[2,4,64,256]{3,2,1,0:T(8,128)}, f32[2,4,64,256]{3,2,1,0:T(8,128)}, u32[]{:S(2)}, u32[]{:S(2)}) collective-permute-start(f32[2,4,64,256]{3,2,1,0:T(8,128)} %get-tuple-element.61.refs_4_), channel_id=1, source_target_pairs={{0,16},{1,17},{2,18},{3,19},{4,20},{5,21},{6,22},{7,23},{8,24},{9,... | collective-permute-start | bytes 1572872 | tf_op jit(solution)/shard_map/ppermute | solution.py:23
  99.2 0.0 collective-permute-done.20.refs_1_
  99.2 4.1 %shard_map.34 = (f32[1,2,4,64,256]{4,3,2,1,0:T(8,128)S(1)}, f32[2,4,64,256]{3,2,1,0:T(8,128)}, f32[2,3,2,4,64,256]{5,4,3,2,1,0:T(8,128)S(1)}) custom-call(s32[2]{0:T(128)S(1)} %pad_add_fusion.1.flags, f32[4,64,1024]{2,1,0:T(8,128)S(1)} %collective-permute-done.19.refs_0_, f32[4,64,1024]{2,1,0:T(8,128)S(1)} %collective-permute-done.20.refs_1_, ...), custom_call_target="tpu_custom_call" | custom-call | flops 1 | bytes 1 | tf_op jit(solution)/shard_map/pallas_call | solution.py:46
  103.3 0.1 collective-permute-start.21
  103.4 6.3 %all_to_all.5.both = f32[2,3,2,4,64,256]{5,4,3,2,1,0:T(8,128)S(1)} all-to-all(f32[2,3,2,4,64,256]{5,4,3,2,1,0:T(8,128)S(1)} %get-tuple-element.67), channel_id=1, replica_groups={{0,32},{1,33},{2,34},{3,35},{4,36},{5,37},{6,38},{7,39},{8,40},{9,41},{..., dimensions={0} | all-to-all | bytes 6291456 | tf_op jit(solution)/shard_map/all_to_all | solution.py:266
  109.6 1.3 shard_map.35
  111.0 1.0 collective-permute-start.22
  111.9 1.7 %collective-permute-start.23 = (f32[2,4,64,256]{3,2,1,0:T(8,128)}, f32[2,4,64,256]{3,2,1,0:T(8,128)}, u32[]{:S(2)}, u32[]{:S(2)}) collective-permute-start(f32[2,4,64,256]{3,2,1,0:T(8,128)} %get-tuple-element.69), channel_id=1, source_target_pairs={{0,3},{1,2},{2,1},{3,0},{4,7},{5,6},{6,5},{7,4},{8,11},{9,10},{10,... | collective-permute-start | bytes 1572872 | tf_op jit(solution)/shard_map/ppermute | solution.py:23
  113.7 0.8 copy-done.7
  114.5 0.5 collective-permute-start.24
  115.0 1.0 copy-done.8
  116.1 1.9 %shard_map.33 = (f32[4,64,256]{2,1,0:T(8,128)S(1)}, f32[4,64,256]{2,1,0:T(8,128)}) custom-call(s32[1]{0:T(128)} %bitcast.2.side, f32[4,2,4,64,256]{4,3,2,1,0:T(8,128)S(1)} %get-tuple-element.54.keep, f32[2,4,64,256]{3,2,1,0:T(8,128)S(1)} %collective-permute-done.11.got, f32[2,4,64,256]{3,2,1,0:T(8,128)S(1)} %collective-permute-done.15.refs_0_, ...), custom_call_target="tpu_custom_call" | custom-call | flops 1 | bytes 1 | tf_op jit(solution)/shard_map/pallas_call | solution.py:46
  118.0 3.0 %collective-permute-start.18 = (f32[4,64,256]{2,1,0:T(8,128)}, f32[4,64,256]{2,1,0:T(8,128)S(1)}, u32[]{:S(2)}, u32[]{:S(2)}) collective-permute-start(f32[4,64,256]{2,1,0:T(8,128)} %get-tuple-element.63), channel_id=1, source_target_pairs={{0,64},{1,65},{2,66},{3,67},{4,68},{5,69},{6,70},{7,71},{8,72},{9,... | collective-permute-start | bytes 786440 | tf_op jit(solution)/shard_map/ppermute | solution.py:23
  121.0 4.2 %collective-permute-done.22.refs_0_ = f32[2,4,64,256]{3,2,1,0:T(8,128)} collective-permute-done((f32[2,4,64,256]{3,2,1,0:T(8,128)}, f32[2,4,64,256]{3,2,1,0:T(8,128)}, u32[]{:S(2)}, u32[]{:S(2)}) %collective-permute-start.22) | collective-permute-done | bytes 524320 | tf_op jit(solution)/shard_map/ppermute | solution.py:23
  125.2 1.9 %collective-permute-done.23.refs_1_ = f32[2,4,64,256]{3,2,1,0:T(8,128)} collective-permute-done((f32[2,4,64,256]{3,2,1,0:T(8,128)}, f32[2,4,64,256]{3,2,1,0:T(8,128)}, u32[]{:S(2)}, u32[]{:S(2)}) %collective-permute-start.23) | collective-permute-done | bytes 524320 | tf_op jit(solution)/shard_map/ppermute | solution.py:23
  127.1 2.5 %collective-permute-done.24.refs_2_ = f32[2,4,64,256]{3,2,1,0:T(8,128)} collective-permute-done((f32[2,4,64,256]{3,2,1,0:T(8,128)}, f32[2,4,64,256]{3,2,1,0:T(8,128)}, u32[]{:S(2)}, u32[]{:S(2)}) %collective-permute-start.24) | collective-permute-done | bytes 524320 | tf_op jit(solution)/shard_map/ppermute | solution.py:23
  129.7 1.7 %shard_map.36 = (f32[4,64,256]{2,1,0:T(8,128)S(1)}, f32[4,64,256]{2,1,0:T(8,128)S(1)}) custom-call(s32[1]{0:T(128)} %bitcast.2.side, f32[1,2,4,64,256]{4,3,2,1,0:T(8,128)S(1)} %copy-done.10, f32[2,4,64,256]{3,2,1,0:T(8,128)} %collective-permute-done.21.got, f32[2,4,64,256]{3,2,1,0:T(8,128)} %collective-permute-done.22.refs_0_, ...), custom_call_target="tpu_custom_call" | custom-call | flops 1 | bytes 1 | tf_op jit(solution)/shard_map/pallas_call | solution.py:46
  131.3 2.8 %collective-permute-start.25 = (f32[4,64,256]{2,1,0:T(8,128)S(1)}, f32[4,64,256]{2,1,0:T(8,128)S(1)}, u32[]{:S(2)}, u32[]{:S(2)}) collective-permute-start(f32[4,64,256]{2,1,0:T(8,128)S(1)} %get-tuple-element.72), channel_id=1, source_target_pairs={{0,64},{1,65},{2,66},{3,67},{4,68},{5,69},{6,70},{7,71},{8,72},{9,... | collective-permute-start | bytes 786440 | tf_op jit(solution)/shard_map/ppermute | solution.py:23
  134.1 0.1 pad_add_fusion.place
  134.2 2.5 %collective-permute-done.18.other_one = f32[4,64,256]{2,1,0:T(8,128)S(1)} collective-permute-done((f32[4,64,256]{2,1,0:T(8,128)}, f32[4,64,256]{2,1,0:T(8,128)S(1)}, u32[]{:S(2)}, u32[]{:S(2)}) %collective-permute-start.18) | collective-permute-done | bytes 262176 | tf_op jit(solution)/shard_map/ppermute | solution.py:23
  136.7 4.2 %collective-permute-done.25.other_two = f32[4,64,256]{2,1,0:T(8,128)S(1)} collective-permute-done((f32[4,64,256]{2,1,0:T(8,128)S(1)}, f32[4,64,256]{2,1,0:T(8,128)S(1)}, u32[]{:S(2)}, u32[]{:S(2)}) %collective-permute-start.25) | collective-permute-done | bytes 262176 | tf_op jit(solution)/shard_map/ppermute | solution.py:23
  140.9 1.4 shard_map.37
  (25 shorter events, 0.1 us)
Async XLA Ops:
  0.0 50.6 %copy-start = (f32[4096,256]{1,0:T(8,128)S(1)}, f32[4096,256]{1,0:T(8,128)}, u32[]{:S(2)}) copy-start(f32[4096,256]{1,0:T(8,128)} %value.1) | copy-start | bytes 12582916
  1.4 15.1 %collective-permute-start.2 = (f32[64,1024]{1,0:T(8,128)S(1)}, f32[64,1024]{1,0:T(8,128)S(1)}, u32[]{:S(2)}, u32[]{:S(2)}) collective-permute-start(f32[64,1024]{1,0:T(8,128)S(1)} %get-tuple-element.75), channel_id=1, source_target_pairs={{0,3},{1,2},{2,1},{3,0},{4,7},{5,6},{6,5},{7,4},{8,11},{9,10},{10,... | collective-permute-start | bytes 786440 | tf_op jit(solution)/shard_map/ppermute | solution.py:23
  4.6 11.9 %collective-permute-start.1 = (f32[64,1024]{1,0:T(8,128)S(1)}, f32[64,1024]{1,0:T(8,128)S(1)}, u32[]{:S(2)}, u32[]{:S(2)}) collective-permute-start(f32[64,1024]{1,0:T(8,128)S(1)} %get-tuple-element.76), channel_id=1, source_target_pairs={{0,2},{1,3},{2,0},{3,1},{4,6},{5,7},{6,4},{7,5},{8,10},{9,11},{10,... | collective-permute-start | bytes 786440 | tf_op jit(solution)/shard_map/ppermute | solution.py:23
  5.3 12.0 %collective-permute-start = (f32[64,1024]{1,0:T(8,128)S(1)}, f32[64,1024]{1,0:T(8,128)S(1)}, u32[]{:S(2)}, u32[]{:S(2)}) collective-permute-start(f32[64,1024]{1,0:T(8,128)S(1)} %get-tuple-element.74), channel_id=1, source_target_pairs={{0,1},{1,0},{2,3},{3,2},{4,5},{5,4},{6,7},{7,6},{8,9},{9,8},{10,11... | collective-permute-start | bytes 786440 | tf_op jit(solution)/shard_map/ppermute | solution.py:23
  17.3 26.5 %collective-permute-start.3 = (f32[4,64,1024]{2,1,0:T(8,128)S(1)}, f32[4,64,1024]{2,1,0:T(8,128)S(1)}, u32[]{:S(2)}, u32[]{:S(2)}) collective-permute-start(f32[4,64,1024]{2,1,0:T(8,128)S(1)} %pad_maximum_fusion.refs_0_), channel_id=1, source_target_pairs={{0,18},{1,19},{2,16},{3,17},{4,22},{5,23},{6,20},{7,21},{8,26},{9,... | collective-permute-start | bytes 3145736 | tf_op jit(solution)/shard_map/ppermute | solution.py:23
  21.4 23.6 %collective-permute-start.4 = (f32[4,64,1024]{2,1,0:T(8,128)S(1)}, f32[4,64,1024]{2,1,0:T(8,128)S(1)}, u32[]{:S(2)}, u32[]{:S(2)}) collective-permute-start(f32[4,64,1024]{2,1,0:T(8,128)S(1)} %pad_maximum_fusion.refs_0_), channel_id=1, source_target_pairs={{0,4},{1,5},{2,6},{3,7},{4,0},{5,1},{6,2},{7,3},{8,12},{9,13},{10,... | collective-permute-start | bytes 3145736 | tf_op jit(solution)/shard_map/ppermute | solution.py:23
  23.3 24.4 %collective-permute-start.5 = (f32[4,64,1024]{2,1,0:T(8,128)S(1)}, f32[4,64,1024]{2,1,0:T(8,128)S(1)}, u32[]{:S(2)}, u32[]{:S(2)}) collective-permute-start(f32[4,64,1024]{2,1,0:T(8,128)S(1)} %pad_maximum_fusion.refs_0_), channel_id=1, source_target_pairs={{0,12},{1,13},{2,14},{3,15},{4,8},{5,9},{6,10},{7,11},{8,4},{9,5},... | collective-permute-start | bytes 3145736 | tf_op jit(solution)/shard_map/ppermute | solution.py:23
  43.8 8.6 %copy-start.1 = (f32[4,64,1024]{2,1,0:T(8,128)}, f32[4,64,1024]{2,1,0:T(8,128)S(1)}, u32[]{:S(2)}) copy-start(f32[4,64,1024]{2,1,0:T(8,128)S(1)} %collective-permute-done.3._.refs_0_) | copy-start | bytes 3145732
  45.0 1.0 copy-start.5
  47.7 2.9 %copy-start.3 = (f32[4,64,1024]{2,1,0:T(8,128)}, f32[4,64,1024]{2,1,0:T(8,128)S(1)}, u32[]{:S(2)}) copy-start(f32[4,64,1024]{2,1,0:T(8,128)S(1)} %collective-permute-done.5.refs_1_) | copy-start | bytes 3145732
  47.7 23.1 %collective-permute-start.6 = (f32[4,64,1024]{2,1,0:T(8,128)S(1)}, f32[4,64,1024]{2,1,0:T(8,128)}, u32[]{:S(2)}, u32[]{:S(2)}) collective-permute-start(f32[4,64,1024]{2,1,0:T(8,128)S(1)} %collective-permute-done.3._.refs_0_), channel_id=1, source_target_pairs={{0,4},{1,5},{2,6},{3,7},{4,0},{5,1},{6,2},{7,3},{8,12},{9,13},{10,... | collective-permute-start | bytes 3145736 | tf_op jit(solution)/shard_map/ppermute | solution.py:23
  48.3 23.6 %collective-permute-start.7 = (f32[4,64,1024]{2,1,0:T(8,128)S(1)}, f32[4,64,1024]{2,1,0:T(8,128)}, u32[]{:S(2)}, u32[]{:S(2)}) collective-permute-start(f32[4,64,1024]{2,1,0:T(8,128)S(1)} %collective-permute-done.3._.refs_0_), channel_id=1, source_target_pairs={{0,12},{1,13},{2,14},{3,15},{4,8},{5,9},{6,10},{7,11},{8,4},{9,5},... | collective-permute-start | bytes 3145736 | tf_op jit(solution)/shard_map/ppermute | solution.py:23
  52.5 22.1 %collective-permute-start.8 = (f32[1024,256]{1,0:T(8,128)}, f32[1024,256]{1,0:T(8,128)}, u32[]{:S(2)}, u32[]{:S(2)}) collective-permute-start(f32[1024,256]{1,0:T(8,128)} %get-tuple-element.43), channel_id=1, source_target_pairs={{0,1},{1,0},{2,3},{3,2},{4,5},{5,4},{6,7},{7,6},{8,9},{9,8},{10,11... | collective-permute-start | bytes 3145736 | tf_op jit(solution)/shard_map/ppermute | solution.py:23
  53.5 23.3 %collective-permute-start.9 = (f32[1024,256]{1,0:T(8,128)}, f32[1024,256]{1,0:T(8,128)}, u32[]{:S(2)}, u32[]{:S(2)}) collective-permute-start(f32[1024,256]{1,0:T(8,128)} %get-tuple-element.44), channel_id=1, source_target_pairs={{0,3},{1,2},{2,1},{3,0},{4,7},{5,6},{6,5},{7,4},{8,11},{9,10},{10,... | collective-permute-start | bytes 3145736 | tf_op jit(solution)/shard_map/ppermute | solution.py:23
  54.6 22.3 %collective-permute-start.10 = (f32[1024,256]{1,0:T(8,128)}, f32[1024,256]{1,0:T(8,128)}, u32[]{:S(2)}, u32[]{:S(2)}) collective-permute-start(f32[1024,256]{1,0:T(8,128)} %get-tuple-element.45), channel_id=1, source_target_pairs={{0,16},{1,17},{2,18},{3,19},{4,20},{5,21},{6,22},{7,23},{8,24},{9,... | collective-permute-start | bytes 3145736 | tf_op jit(solution)/shard_map/ppermute | solution.py:23
  70.8 26.8 %collective-permute-start.19 = (f32[4,64,1024]{2,1,0:T(8,128)}, f32[4,64,1024]{2,1,0:T(8,128)S(1)}, u32[]{:S(2)}, u32[]{:S(2)}) collective-permute-start(f32[4,64,1024]{2,1,0:T(8,128)} %copy-done.3), channel_id=1, source_target_pairs={{0,4},{1,5},{2,6},{3,7},{4,0},{5,1},{6,2},{7,3},{8,12},{9,13},{10,... | collective-permute-start | bytes 3145736 | tf_op jit(solution)/shard_map/ppermute | solution.py:23
  71.9 27.3 %collective-permute-start.20 = (f32[4,64,1024]{2,1,0:T(8,128)}, f32[4,64,1024]{2,1,0:T(8,128)S(1)}, u32[]{:S(2)}, u32[]{:S(2)}) collective-permute-start(f32[4,64,1024]{2,1,0:T(8,128)} %collective-permute-done.6.refs_2_), channel_id=1, source_target_pairs={{0,12},{1,13},{2,14},{3,15},{4,8},{5,9},{6,10},{7,11},{8,4},{9,5},... | collective-permute-start | bytes 3145736 | tf_op jit(solution)/shard_map/ppermute | solution.py:23
  76.8 2.7 %copy-start.4 = (f32[4,64,1024]{2,1,0:T(8,128)S(1)}, f32[4,64,1024]{2,1,0:T(8,128)}, u32[]{:S(2)}) copy-start(f32[4,64,1024]{2,1,0:T(8,128)} %copy-done.3) | copy-start | bytes 3145732
  76.8 2.7 %copy-start.6 = (f32[4,64,1024]{2,1,0:T(8,128)S(1)}, f32[4,64,1024]{2,1,0:T(8,128)}, u32[]{:S(2)}) copy-start(f32[4,64,1024]{2,1,0:T(8,128)} %copy-done.5) | copy-start | bytes 3145732
  79.6 5.1 %copy-start.2 = (f32[4,64,1024]{2,1,0:T(8,128)S(1)}, f32[4,64,1024]{2,1,0:T(8,128)}, u32[]{:S(2)}) copy-start(f32[4,64,1024]{2,1,0:T(8,128)} %copy-done.1) | copy-start | bytes 3145732
  91.2 2.0 %collective-permute-start.12 = (f32[2,4,64,256]{3,2,1,0:T(8,128)S(1)}, f32[2,4,64,256]{3,2,1,0:T(8,128)S(1)}, u32[]{:S(2)}, u32[]{:S(2)}) collective-permute-start(f32[2,4,64,256]{3,2,1,0:T(8,128)S(1)} %get-tuple-element.56), channel_id=1, source_target_pairs={{0,32},{1,33},{2,34},{3,35},{4,36},{5,37},{6,38},{7,39},{8,40},{9,... | collective-permute-start | bytes 1572872 | tf_op jit(solution)/shard_map/ppermute | solution.py:23
  91.3 2.6 %collective-permute-start.13 = (f32[2,4,64,256]{3,2,1,0:T(8,128)S(1)}, f32[2,4,64,256]{3,2,1,0:T(8,128)S(1)}, u32[]{:S(2)}, u32[]{:S(2)}) collective-permute-start(f32[2,4,64,256]{3,2,1,0:T(8,128)S(1)} %get-tuple-element.57), channel_id=1, source_target_pairs={{0,32},{1,33},{2,34},{3,35},{4,36},{5,37},{6,38},{7,39},{8,40},{9,... | collective-permute-start | bytes 1572872 | tf_op jit(solution)/shard_map/ppermute | solution.py:23
  91.8 2.9 %collective-permute-start.14 = (f32[2,4,64,256]{3,2,1,0:T(8,128)S(1)}, f32[2,4,64,256]{3,2,1,0:T(8,128)S(1)}, u32[]{:S(2)}, u32[]{:S(2)}) collective-permute-start(f32[2,4,64,256]{3,2,1,0:T(8,128)S(1)} %get-tuple-element.58), channel_id=1, source_target_pairs={{0,32},{1,33},{2,34},{3,35},{4,36},{5,37},{6,38},{7,39},{8,40},{9,... | collective-permute-start | bytes 1572872 | tf_op jit(solution)/shard_map/ppermute | solution.py:23
  93.2 17.7 %collective-permute-start.11 = (f32[2,4,64,256]{3,2,1,0:T(8,128)S(1)}, f32[2,4,64,256]{3,2,1,0:T(8,128)S(1)}, u32[]{:S(2)}, u32[]{:S(2)}) collective-permute-start(f32[2,4,64,256]{3,2,1,0:T(8,128)S(1)} %get-tuple-element.55), channel_id=1, source_target_pairs={{0,32},{1,33},{2,34},{3,35},{4,36},{5,37},{6,38},{7,39},{8,40},{9,... | collective-permute-start | bytes 1572872 | tf_op jit(solution)/shard_map/ppermute | solution.py:23
  95.7 16.3 %collective-permute-start.15 = (f32[2,4,64,256]{3,2,1,0:T(8,128)S(1)}, f32[2,4,64,256]{3,2,1,0:T(8,128)S(1)}, u32[]{:S(2)}, u32[]{:S(2)}) collective-permute-start(f32[2,4,64,256]{3,2,1,0:T(8,128)S(1)} %get-tuple-element.59.refs_2_), channel_id=1, source_target_pairs={{0,1},{1,0},{2,3},{3,2},{4,5},{5,4},{6,7},{7,6},{8,9},{9,8},{10,11... | collective-permute-start | bytes 1572872 | tf_op jit(solution)/shard_map/ppermute | solution.py:23
  96.7 17.0 %collective-permute-start.16 = (f32[2,4,64,256]{3,2,1,0:T(8,128)S(1)}, f32[2,4,64,256]{3,2,1,0:T(8,128)S(1)}, u32[]{:S(2)}, u32[]{:S(2)}) collective-permute-start(f32[2,4,64,256]{3,2,1,0:T(8,128)S(1)} %get-tuple-element.60.refs_3_), channel_id=1, source_target_pairs={{0,3},{1,2},{2,1},{3,0},{4,7},{5,6},{6,5},{7,4},{8,11},{9,10},{10,... | collective-permute-start | bytes 1572872 | tf_op jit(solution)/shard_map/ppermute | solution.py:23
  97.7 17.4 %collective-permute-start.17 = (f32[2,4,64,256]{3,2,1,0:T(8,128)}, f32[2,4,64,256]{3,2,1,0:T(8,128)}, u32[]{:S(2)}, u32[]{:S(2)}) collective-permute-start(f32[2,4,64,256]{3,2,1,0:T(8,128)} %get-tuple-element.61.refs_4_), channel_id=1, source_target_pairs={{0,16},{1,17},{2,18},{3,19},{4,20},{5,21},{6,22},{7,23},{8,24},{9,... | collective-permute-start | bytes 1572872 | tf_op jit(solution)/shard_map/ppermute | solution.py:23
  103.2 6.4 %copy-start.9 = (f32[1,2,4,64,256]{4,3,2,1,0:T(8,128)}, f32[1,2,4,64,256]{4,3,2,1,0:T(8,128)S(1)}, u32[]{:S(2)}) copy-start(f32[1,2,4,64,256]{4,3,2,1,0:T(8,128)S(1)} %get-tuple-element.65.keep) | copy-start | bytes 1572868
  103.3 17.8 %collective-permute-start.21 = (f32[2,4,64,256]{3,2,1,0:T(8,128)}, f32[2,4,64,256]{3,2,1,0:T(8,128)}, u32[]{:S(2)}, u32[]{:S(2)}) collective-permute-start(f32[2,4,64,256]{3,2,1,0:T(8,128)} %get-tuple-element.66), channel_id=1, source_target_pairs={{0,32},{1,33},{2,34},{3,35},{4,36},{5,37},{6,38},{7,39},{8,40},{9,... | collective-permute-start | bytes 1572872 | tf_op jit(solution)/shard_map/ppermute | solution.py:23
  111.0 14.3 %collective-permute-start.22 = (f32[2,4,64,256]{3,2,1,0:T(8,128)}, f32[2,4,64,256]{3,2,1,0:T(8,128)}, u32[]{:S(2)}, u32[]{:S(2)}) collective-permute-start(f32[2,4,64,256]{3,2,1,0:T(8,128)} %get-tuple-element.68), channel_id=1, source_target_pairs={{0,1},{1,0},{2,3},{3,2},{4,5},{5,4},{6,7},{7,6},{8,9},{9,8},{10,11... | collective-permute-start | bytes 1572872 | tf_op jit(solution)/shard_map/ppermute | solution.py:23
  111.9 15.2 %collective-permute-start.23 = (f32[2,4,64,256]{3,2,1,0:T(8,128)}, f32[2,4,64,256]{3,2,1,0:T(8,128)}, u32[]{:S(2)}, u32[]{:S(2)}) collective-permute-start(f32[2,4,64,256]{3,2,1,0:T(8,128)} %get-tuple-element.69), channel_id=1, source_target_pairs={{0,3},{1,2},{2,1},{3,0},{4,7},{5,6},{6,5},{7,4},{8,11},{9,10},{10,... | collective-permute-start | bytes 1572872 | tf_op jit(solution)/shard_map/ppermute | solution.py:23
  113.7 0.8 copy-start.7
  114.5 15.2 %collective-permute-start.24 = (f32[2,4,64,256]{3,2,1,0:T(8,128)}, f32[2,4,64,256]{3,2,1,0:T(8,128)}, u32[]{:S(2)}, u32[]{:S(2)}) collective-permute-start(f32[2,4,64,256]{3,2,1,0:T(8,128)} %get-tuple-element.70), channel_id=1, source_target_pairs={{0,16},{1,17},{2,18},{3,19},{4,20},{5,21},{6,22},{7,23},{8,24},{9,... | collective-permute-start | bytes 1572872 | tf_op jit(solution)/shard_map/ppermute | solution.py:23
  115.0 1.0 copy-start.8
  116.1 13.6 %copy-start.10 = (f32[1,2,4,64,256]{4,3,2,1,0:T(8,128)S(1)}, f32[1,2,4,64,256]{4,3,2,1,0:T(8,128)}, u32[]{:S(2)}) copy-start(f32[1,2,4,64,256]{4,3,2,1,0:T(8,128)} %copy-done.9) | copy-start | bytes 1572868
  118.0 18.7 %collective-permute-start.18 = (f32[4,64,256]{2,1,0:T(8,128)}, f32[4,64,256]{2,1,0:T(8,128)S(1)}, u32[]{:S(2)}, u32[]{:S(2)}) collective-permute-start(f32[4,64,256]{2,1,0:T(8,128)} %get-tuple-element.63), channel_id=1, source_target_pairs={{0,64},{1,65},{2,66},{3,67},{4,68},{5,69},{6,70},{7,71},{8,72},{9,... | collective-permute-start | bytes 786440 | tf_op jit(solution)/shard_map/ppermute | solution.py:23
  131.3 9.5 %collective-permute-start.25 = (f32[4,64,256]{2,1,0:T(8,128)S(1)}, f32[4,64,256]{2,1,0:T(8,128)S(1)}, u32[]{:S(2)}, u32[]{:S(2)}) collective-permute-start(f32[4,64,256]{2,1,0:T(8,128)S(1)} %get-tuple-element.72), channel_id=1, source_target_pairs={{0,64},{1,65},{2,66},{3,67},{4,68},{5,69},{6,70},{7,71},{8,72},{9,... | collective-permute-start | bytes 786440 | tf_op jit(solution)/shard_map/ppermute | solution.py:23

commit v12 on v11

--- a/solution.py
+++ b/solution.py
@@ -8,7 +8,8 @@
 AXES = ("rep", "grid")
 PARAMS = pltpu.CompilerParams(vmem_limit_bytes=20 * 1024 * 1024)
 SHORT = pl.CostEstimate(flops=1, bytes_accessed=1, transcendentals=0)
-NEAR = (dict(), dict(dy=1), dict(dy=3), dict(dx=1))
+NEAR = (dict(), dict(dx=1), dict(dy=1), dict(dy=3))
+DIFFERS = (0, 3, 1, 2)
 
 
 def number(x_hi, core, x_lo, z, y):
@@ -60,7 +61,7 @@
     depth = outs[0].shape[0]
     copies = []
     for d, out in enumerate(outs):
-        at = pl.ds(pl.multiple_of((quarter[0] ^ d) * depth, depth), depth)
+        at = pl.ds(pl.multiple_of((quarter[0] ^ DIFFERS[d]) * depth, depth), depth)
         copies.append(pltpu.make_async_copy(value.at[at], out, sems.at[d]))
     for copy in copies:
         copy.start()
@@ -109,7 +110,7 @@
 
 
 def places(d):
-    return [(block, block ^ (0, 1, 3, 2)[d]) for block in range(4)]
+    return [(block, block ^ (0, 2, 1, 3)[d]) for block in range(4)]
 
 
 def early_products(swap, part, planes, rights, before=()):
@@ -191,21 +192,34 @@
     )
 
 
-def added_by_core_kernel(_, both, *outs):
-    for d, out in enumerate(outs):
-        out[...] = both[0, d] + both[1, d]
-
-
-def added_by_core(scalars, both):
-    shape = jax.ShapeDtypeStruct(both.shape[2:], jnp.float32)
-    return call(added_by_core_kernel, scalars, (both,), [whole(both)], [shape] * 3, [whole(shape)] * 3)
+def added_by_core_kernel(side, both, *outs):
+    for d, (here, there) in enumerate(zip(outs[:3], outs[3:])):
+        here[...] = both[0, d, side[0]] + both[1, d, side[0]]
+        there[...] = both[0, d, 1 - side[0]] + both[1, d, 1 - side[0]]
+
+
+def added_by_core(side, both):
+    shape = jax.ShapeDtypeStruct(both.shape[3:], jnp.float32)
+    found = call(added_by_core_kernel, side, (both,), [whole(both)], [shape] * 6, [whole(shape)] * 6)
+    return found[:3], found[3:]
+
+
+def onward_kernel(side, keep, got, one, two, three, out):
+    part = 1 - side[0]
+    out[...] = (keep[0, part] + got[part]) + (one[...] + (two[...] + three[...]))
+
+
+def onward(side, keep, got, terms):
+    shape = jax.ShapeDtypeStruct(got.shape[1:], jnp.float32)
+    values = (keep, got, *terms)
+    return call(onward_kernel, side, values, [whole(value) for value in values], shape, whole(shape))
 
 
 def sum_kernel(side, keep, got, *refs):
     terms, (mine, theirs) = refs[:-2], refs[-2:]
     for out, part in ((mine, side[0]), (theirs, 1 - side[0])):
-        across = terms[2][1 - part]
-        out[...] = (keep[0, part] + got[part]) + (terms[0][part] + (terms[1][part] + across))
+        across = terms[0][1 - part]
+        out[...] = (keep[0, part] + got[part]) + (across + (terms[1][part] + terms[2][part]))
 
 
 def summed(side, keep, got, terms):
@@ -217,11 +231,13 @@
     )
 
 
-def join_kernel(place, one, other_one, two, other_two, out):
+def join_kernel(place, one, other_one, keep, got, across, two, three, other_two, out):
+    part = place[2]
     for block in range(4):
         line = place[1] ^ block
         out[place[0], line] = one[block] + other_one[block]
-        out[1 - place[0], line] = two[block] + other_two[block]
+        near = across[block] + (two[block] + three[block])
+        out[1 - place[0], line] = (keep[0, part, block] + got[part, block]) + (near + other_two[block])
 
 
 def join(place, values):
@@ -245,12 +261,12 @@
     mine = jnp.stack([block(0), send(block(1), dy=1), send(block(3), dy=2), send(block(2), dy=3)])
     other = send(mine, dx=1, dy=2)
     own_one, own_three = send(mine, dz=1), send(mine, dz=3)
-    far, *_ = lax.optimization_barrier((other, own_one, own_three))
+    pieces = cut_after(quarter.reshape(1), right, other)
+    far, *_ = lax.optimization_barrier((other, own_one, own_three, *pieces))
     far_one, far_three = lax.optimization_barrier((send(far, dz=1), send(far, dz=3)))
 
     own_two, far_two = send(own_three, dz=1), send(far_one, dz=3)
 
-    pieces = cut_after(quarter.reshape(1), right, other)
     pieces = [pieces[0]] + [send(pieces[d], **NEAR[d]) for d in range(1, 4)]
     rights = split(swap, pieces)
 
@@ -265,13 +281,17 @@
     )
     both = lax.all_to_all(both, AXES, 0, 0, tiled=True, axis_index_groups=CORES)
 
-    ends = []
-    for kept, given, terms in ((keep, got[0], sums), (late_keep, send(late_give, core=1), added_by_core(swap, both))):
-        across = send(terms[2], **NEAR[3])
-        here, there = summed(side, kept, given, [send(terms[0], **NEAR[1]), send(terms[1], **NEAR[2]), across])
-        ends += [here, send(there, dhi=1)]
-
-    total = join(jnp.stack([(z & 1) ^ swap[0], y ^ (2 * side[0])]), ends)
+    here, there = summed(side, keep, got[0], [send(sums[d - 1], **NEAR[d]) for d in range(1, 4)])
+    early_ends = here, send(there, dhi=1)
+
+    late_got = send(late_give, core=1)
+    kept, passed = added_by_core(side, both)
+    passed = [send(passed[d - 1], **NEAR[d]) for d in range(1, 4)]
+    passed = send(onward(side, late_keep, late_got, passed), dhi=1)
+    kept = [send(kept[d - 1], **NEAR[d]) for d in range(1, 4)]
+
+    place = jnp.stack([(z & 1) ^ swap[0], y ^ (2 * side[0]), side[0]])
+    total = join(place, (*early_ends, late_keep, late_got, *kept, passed))
     return total.reshape(8 * rows, columns)
 
 

time: 143 us -> 147 us (1.028)
  waiting for transfers between devices: 68.5 us -> 63 us
  starting transfers between devices: 35.4 us -> 40.4 us
  Pallas kernels: 27.4 us -> 30.1 us
    ppermute x26 -> x29, waiting for transfers between devices: 68.5 us -> 63 us  [send(): return lax.ppermute(value, AXES, pairs)]
    ppermute x26 -> x29, starting transfers between devices: 35.4 us -> 40.4 us  [send(): return lax.ppermute(value, AXES, pairs)]
    pallas_call x10, Pallas kernels: 27.4 us -> 30.1 us  [call(): pl.pallas_call(kernel, grid_spec=pltpu.PrefetchScalarGridSpec(num_scalar_...]
    unnamed x22 -> x16, local copies, waits for them, and re-layouts: 2.87 us -> 3.62 us
  transfers between devices with their start and end apart: 26 -> 29, of which waited for: 17 -> 15; matrix products, arithmetic and copies ran while one was open for 0% -> 0% of each run, Pallas kernels for 18% -> 20%
where the time goes in v12:
time: 147 us; the launch traced here: 146 us
  waiting for transfers between devices  63 us (43%)
  starting transfers between devices  40.4 us (27%)
  Pallas kernels  30.1 us (20%)
  blocking collectives  7.55 us (5%)
  local copies, waits for them, and re-layouts  5.06 us (3%)
    ppermute x29, waiting for transfers between devices, send(): return lax.ppermute(value, AXES, pairs)  63 us
    ppermute x29, starting transfers between devices, send(): return lax.ppermute(value, AXES, pairs)  40.4 us
    pallas_call x10, Pallas kernels, call(): pl.pallas_call(kernel, grid_spec=pltpu.PrefetchScalarGridSpec(num_scalar_...  30.1 us
    all_to_all x1, blocking collectives, per_device(): both = lax.all_to_all(both, AXES, 0, 0, tiled=True, axis_index_groups=CORES)  7.55 us
    unnamed x16, local copies, waits for them, and re-layouts  3.62 us
  transfers between devices with their start and end apart: 29, of which 15 were waited for; matrix products, arithmetic and copies ran while one was open for 0% of the time, Pallas kernels for 20%

profile of v12, /device:TPU:0, one launch (start us, length us, event | category | flops | bytes accessed | tf_op | source)
XLA Modules:
  0.0 146.4 jit_solution(15300915110269633110)
XLA Ops:
  0.0 1.4 dynamic-slice_bitcast_fusion
  1.4 3.2 %collective-permute-start.2 = (f32[64,1024]{1,0:T(8,128)S(1)}, f32[64,1024]{1,0:T(8,128)S(1)}, u32[]{:S(2)}, u32[]{:S(2)}) collective-permute-start(f32[64,1024]{1,0:T(8,128)S(1)} %get-tuple-element.77), channel_id=1, source_target_pairs={{0,3},{1,2},{2,1},{3,0},{4,7},{5,6},{6,5},{7,4},{8,11},{9,10},{10,... | collective-permute-start | bytes 786440 | tf_op jit(solution)/shard_map/ppermute | solution.py:24
  4.6 0.6 collective-permute-start.1
  5.3 0.4 collective-permute-start
  5.6 10.9 %collective-permute-done.2 = f32[64,1024]{1,0:T(8,128)S(1)} collective-permute-done((f32[64,1024]{1,0:T(8,128)S(1)}, f32[64,1024]{1,0:T(8,128)S(1)}, u32[]{:S(2)}, u32[]{:S(2)}) %collective-permute-start.2) | collective-permute-done | bytes 262176 | tf_op jit(solution)/shard_map/ppermute | solution.py:24
  16.6 0.0 collective-permute-done.1
  16.6 0.7 collective-permute-done
  17.3 0.1 pad_maximum_fusion.refs_0_
  17.3 4.0 %collective-permute-start.3 = (f32[4,64,1024]{2,1,0:T(8,128)S(1)}, f32[4,64,1024]{2,1,0:T(8,128)S(1)}, u32[]{:S(2)}, u32[]{:S(2)}) collective-permute-start(f32[4,64,1024]{2,1,0:T(8,128)S(1)} %pad_maximum_fusion.refs_0_), channel_id=1, source_target_pairs={{0,18},{1,19},{2,16},{3,17},{4,22},{5,23},{6,20},{7,21},{8,26},{9,... | collective-permute-start | bytes 3145736 | tf_op jit(solution)/shard_map/ppermute | solution.py:24
  21.4 1.9 %collective-permute-start.4 = (f32[4,64,1024]{2,1,0:T(8,128)S(1)}, f32[4,64,1024]{2,1,0:T(8,128)S(1)}, u32[]{:S(2)}, u32[]{:S(2)}) collective-permute-start(f32[4,64,1024]{2,1,0:T(8,128)S(1)} %pad_maximum_fusion.refs_0_), channel_id=1, source_target_pairs={{0,4},{1,5},{2,6},{3,7},{4,0},{5,1},{6,2},{7,3},{8,12},{9,13},{10,... | collective-permute-start | bytes 3145736 | tf_op jit(solution)/shard_map/ppermute | solution.py:24
  23.3 2.5 %collective-permute-start.5 = (f32[4,64,1024]{2,1,0:T(8,128)S(1)}, f32[4,64,1024]{2,1,0:T(8,128)}, u32[]{:S(2)}, u32[]{:S(2)}) collective-permute-start(f32[4,64,1024]{2,1,0:T(8,128)S(1)} %pad_maximum_fusion.refs_0_), channel_id=1, source_target_pairs={{0,12},{1,13},{2,14},{3,15},{4,8},{5,9},{6,10},{7,11},{8,4},{9,5},... | collective-permute-start | bytes 3145736 | tf_op jit(solution)/shard_map/ppermute | solution.py:24
  25.8 18.0 %collective-permute-done.3._.refs_0_ = f32[4,64,1024]{2,1,0:T(8,128)S(1)} collective-permute-done((f32[4,64,1024]{2,1,0:T(8,128)S(1)}, f32[4,64,1024]{2,1,0:T(8,128)S(1)}, u32[]{:S(2)}, u32[]{:S(2)}) %collective-permute-start.3) | collective-permute-done | bytes 1048608 | tf_op jit(solution)/shard_map/ppermute | solution.py:24
  43.8 1.9 %shard_map.28 = (f32[1024,256]{1,0:T(8,128)S(1)}, f32[1024,256]{1,0:T(8,128)}, f32[1024,256]{1,0:T(8,128)}, f32[1024,256]{1,0:T(8,128)}) custom-call(s32[1]{0:T(128)} %bitcast.8.quarter, f32[4096,256]{1,0:T(8,128)S(1)} %copy-done, f32[4,64,1024]{2,1,0:T(8,128)S(1)} %collective-permute-done.3._.refs_0_), custom_call_target="tpu_custom_call" | custom-call | flops 1 | bytes 1 | tf_op jit(solution)/shard_map/pallas_call | solution.py:47
  45.7 1.0 copy-done.4
  46.7 1.1 collective-permute-done.5.refs_1_
  47.8 0.7 collective-permute-start.6
  48.5 2.5 %collective-permute-start.7 = (f32[4,64,1024]{2,1,0:T(8,128)S(1)}, f32[4,64,1024]{2,1,0:T(8,128)S(1)}, u32[]{:S(2)}, u32[]{:S(2)}) collective-permute-start(f32[4,64,1024]{2,1,0:T(8,128)S(1)} %collective-permute-done.3._.refs_0_), channel_id=1, source_target_pairs={{0,12},{1,13},{2,14},{3,15},{4,8},{5,9},{6,10},{7,11},{8,4},{9,5},... | collective-permute-start | bytes 3145736 | tf_op jit(solution)/shard_map/ppermute | solution.py:24
  51.1 1.5 %collective-permute-start.8 = (f32[1024,256]{1,0:T(8,128)}, f32[1024,256]{1,0:T(8,128)S(1)}, u32[]{:S(2)}, u32[]{:S(2)}) collective-permute-start(f32[1024,256]{1,0:T(8,128)} %get-tuple-element.41), channel_id=1, source_target_pairs={{0,16},{1,17},{2,18},{3,19},{4,20},{5,21},{6,22},{7,23},{8,24},{9,... | collective-permute-start | bytes 3145736 | tf_op jit(solution)/shard_map/ppermute | solution.py:24
  52.6 1.3 collective-permute-start.9
  53.8 2.2 %collective-permute-start.10 = (f32[1024,256]{1,0:T(8,128)}, f32[1024,256]{1,0:T(8,128)}, u32[]{:S(2)}, u32[]{:S(2)}) collective-permute-start(f32[1024,256]{1,0:T(8,128)} %get-tuple-element.43), channel_id=1, source_target_pairs={{0,3},{1,2},{2,1},{3,0},{4,7},{5,6},{6,5},{7,4},{8,11},{9,10},{10,... | collective-permute-start | bytes 3145736 | tf_op jit(solution)/shard_map/ppermute | solution.py:24
  56.0 14.5 %collective-permute-done.6.refs_2_ = f32[4,64,1024]{2,1,0:T(8,128)} collective-permute-done((f32[4,64,1024]{2,1,0:T(8,128)S(1)}, f32[4,64,1024]{2,1,0:T(8,128)}, u32[]{:S(2)}, u32[]{:S(2)}) %collective-permute-start.6) | collective-permute-done | bytes 1048608 | tf_op jit(solution)/shard_map/ppermute | solution.py:24
  70.5 1.2 collective-permute-start.19
  71.6 0.8 collective-permute-done.7.refs_1_
  72.5 1.0 copy-done.6
  73.4 2.5 %collective-permute-start.20 = (f32[4,64,1024]{2,1,0:T(8,128)}, f32[4,64,1024]{2,1,0:T(8,128)}, u32[]{:S(2)}, u32[]{:S(2)}) collective-permute-start(f32[4,64,1024]{2,1,0:T(8,128)} %collective-permute-done.6.refs_2_), channel_id=1, source_target_pairs={{0,12},{1,13},{2,14},{3,15},{4,8},{5,9},{6,10},{7,11},{8,4},{9,5},... | collective-permute-start | bytes 3145736 | tf_op jit(solution)/shard_map/ppermute | solution.py:24
  76.0 1.1 collective-permute-done.10.refs_3_
  77.0 2.3 %shard_map.29 = (bf16[1024,1024]{1,0:T(8,128)(2,1)S(1)}, bf16[1024,1024]{1,0:T(8,128)(2,1)S(1)}) custom-call(s32[1]{0:T(128)} %bitcast.3._.swap, f32[1024,256]{1,0:T(8,128)S(1)} %get-tuple-element.40.refs_0_, f32[1024,256]{1,0:T(8,128)S(1)} %collective-permute-done.8.refs_1_, f32[1024,256]{1,0:T(8,128)} %collective-permute-done.9.refs_2_, ...), custom_call_target="tpu_custom_call" | custom-call | flops 1 | bytes 1 | tf_op jit(solution)/shard_map/pallas_call | solution.py:47
  79.4 7.1 %shard_map.30 = (f32[4,2,4,64,256]{4,3,2,1,0:T(8,128)S(1)}, f32[4,2,4,64,256]{4,3,2,1,0:T(8,128)S(1)}, f32[2,4,64,256]{3,2,1,0:T(8,128)}, f32[2,4,64,256]{3,2,1,...) custom-call(s32[1]{0:T(128)} %bitcast.3._.swap, ...), custom_call_target="tpu_custom_call" | custom-call | flops 1 | bytes 1 | tf_op jit(solution)/shard_map/pallas_call | solution.py:47
  86.5 6.9 %shard_map.31 = (f32[4,2,4,64,256]{4,3,2,1,0:T(8,128)S(1)}, f32[4,2,4,64,256]{4,3,2,1,0:T(8,128)S(1)}, f32[2,4,64,256]{3,2,1,0:T(8,128)}, f32[2,4,64,256]{3,2,1,...) custom-call(s32[1]{0:T(128)} %bitcast.3._.swap, ...), custom_call_target="tpu_custom_call", output_to_operand_aliasing={{0}: (4, {}), {1}: (5, {}), {2}: (6, {}), {3}: (7, {}), {4}... | custom-call | flops 1 | bytes 1 | tf_op jit(solution)/shard_map/pallas_call | solution.py:47
  93.4 0.5 collective-permute-start.13
  93.9 1.4 collective-permute-done.12.refs_0_
  95.3 0.1 collective-permute-start.11
  95.5 0.6 collective-permute-done.13.refs_1_
  96.1 0.7 collective-permute-done.14.refs_2_
  96.8 1.4 shard_map.32
  98.2 0.5 collective-permute-start.15
  98.7 1.0 collective-permute-start.16
  99.7 2.2 %collective-permute-start.17 = (f32[2,4,64,256]{3,2,1,0:T(8,128)}, f32[2,4,64,256]{3,2,1,0:T(8,128)}, u32[]{:S(2)}, u32[]{:S(2)}) collective-permute-start(f32[2,4,64,256]{3,2,1,0:T(8,128)} %get-tuple-element.62.refs_4_), channel_id=1, source_target_pairs={{0,3},{1,2},{2,1},{3,0},{4,7},{5,6},{6,5},{7,4},{8,11},{9,10},{10,... | collective-permute-start | bytes 1572872 | tf_op jit(solution)/shard_map/ppermute | solution.py:24
  101.9 0.1 pad_add_fusion.1.flags
  102.0 0.0 collective-permute-done.20.refs_1_
  102.0 5.6 %shard_map.34 = (f32[1,2,4,64,256]{4,3,2,1,0:T(8,128)S(1)}, f32[2,4,64,256]{3,2,1,0:T(8,128)}, f32[2,3,2,4,64,256]{5,4,3,2,1,0:T(8,128)S(1)}) custom-call(s32[2]{0:T(128)S(1)} %pad_add_fusion.1.flags, f32[4,64,1024]{2,1,0:T(8,128)} %collective-permute-done.19.refs_0_, f32[4,64,1024]{2,1,0:T(8,128)} %collective-permute-done.20.refs_1_, ...), custom_call_target="tpu_custom_call" | custom-call | flops 1 | bytes 1 | tf_op jit(solution)/shard_map/pallas_call | solution.py:47
  107.6 1.6 %copy-done.3 = f32[2,3,2,4,64,256]{5,4,3,2,1,0:T(8,128)} copy-done((f32[2,3,2,4,64,256]{5,4,3,2,1,0:T(8,128)}, f32[2,3,2,4,64,256]{5,4,3,2,1,0:T(8,128)S(1)}, u32[]{:S(2)}) %copy-start.3) | copy-done | bytes 3145752
  109.3 7.6 %all_to_all.5.both = f32[2,3,2,4,64,256]{5,4,3,2,1,0:T(8,128)S(1)} all-to-all(f32[2,3,2,4,64,256]{5,4,3,2,1,0:T(8,128)} %copy-done.3), channel_id=1, replica_groups={{0,32},{1,33},{2,34},{3,35},{4,36},{5,37},{6,38},{7,39},{8,40},{9,41},{..., dimensions={0} | all-to-all | bytes 6291456 | tf_op jit(solution)/shard_map/all_to_all | solution.py:282
  116.8 1.0 shard_map.35
  117.8 1.2 collective-permute-start.25
  119.0 0.0 collective-permute-done.15.refs_0_
  119.0 0.9 collective-permute-start.26
  119.9 0.0 collective-permute-done.16.refs_1_
  119.9 0.9 collective-permute-start.27
  120.8 0.0 collective-permute-done.17.refs_2_
  120.8 2.3 %shard_map.33 = (f32[4,64,256]{2,1,0:T(8,128)S(1)}, f32[4,64,256]{2,1,0:T(8,128)}) custom-call(s32[1]{0:T(128)} %bitcast.2.side, f32[4,2,4,64,256]{4,3,2,1,0:T(8,128)S(1)} %get-tuple-element.55.keep, f32[2,4,64,256]{3,2,1,0:T(8,128)} %collective-permute-done.11.got, f32[2,4,64,256]{3,2,1,0:T(8,128)} %collective-permute-done.15.refs_0_, ...), custom_call_target="tpu_custom_call" | custom-call | flops 1 | bytes 1 | tf_op jit(solution)/shard_map/pallas_call | solution.py:47
  123.2 2.7 %collective-permute-start.18 = (f32[4,64,256]{2,1,0:T(8,128)}, f32[4,64,256]{2,1,0:T(8,128)S(1)}, u32[]{:S(2)}, u32[]{:S(2)}) collective-permute-start(f32[4,64,256]{2,1,0:T(8,128)} %get-tuple-element.64), channel_id=1, source_target_pairs={{0,64},{1,65},{2,66},{3,67},{4,68},{5,69},{6,70},{7,71},{8,72},{9,... | collective-permute-start | bytes 786440 | tf_op jit(solution)/shard_map/ppermute | solution.py:24
  125.9 0.3 collective-permute-done.25.one
  126.2 1.2 collective-permute-start.22
  127.4 0.9 collective-permute-start.23
  128.3 0.7 collective-permute-done.27.three
  128.9 0.9 collective-permute-start.24
  129.8 0.1 shard_map.36
  129.9 2.8 %collective-permute-start.28 = (f32[4,64,256]{2,1,0:T(8,128)S(1)}, f32[4,64,256]{2,1,0:T(8,128)S(1)}, u32[]{:S(2)}, u32[]{:S(2)}) collective-permute-start(f32[4,64,256]{2,1,0:T(8,128)S(1)} %shard_map.36), channel_id=1, source_target_pairs={{0,64},{1,65},{2,66},{3,67},{4,68},{5,69},{6,70},{7,71},{8,72},{9,... | collective-permute-start | bytes 786440 | tf_op jit(solution)/shard_map/ppermute | solution.py:24
  132.7 0.1 pad_add_fusion.place
  132.8 1.7 %collective-permute-done.18.other_one = f32[4,64,256]{2,1,0:T(8,128)S(1)} collective-permute-done((f32[4,64,256]{2,1,0:T(8,128)}, f32[4,64,256]{2,1,0:T(8,128)S(1)}, u32[]{:S(2)}, u32[]{:S(2)}) %collective-permute-start.18) | collective-permute-done | bytes 262176 | tf_op jit(solution)/shard_map/ppermute | solution.py:24
  134.5 4.8 %collective-permute-done.22.across = f32[4,64,256]{2,1,0:T(8,128)S(1)} collective-permute-done((f32[4,64,256]{2,1,0:T(8,128)}, f32[4,64,256]{2,1,0:T(8,128)S(1)}, u32[]{:S(2)}, u32[]{:S(2)}) %collective-permute-start.22) | collective-permute-done | bytes 262176 | tf_op jit(solution)/shard_map/ppermute | solution.py:24
  139.3 5.6 %collective-permute-done.28.other_two = f32[4,64,256]{2,1,0:T(8,128)S(1)} collective-permute-done((f32[4,64,256]{2,1,0:T(8,128)S(1)}, f32[4,64,256]{2,1,0:T(8,128)S(1)}, u32[]{:S(2)}, u32[]{:S(2)}) %collective-permute-start.28) | collective-permute-done | bytes 262176 | tf_op jit(solution)/shard_map/ppermute | solution.py:24
  144.9 1.4 shard_map.37
  (25 shorter events, 0.1 us)
Async XLA Ops:
  0.0 43.8 %copy-start = (f32[4096,256]{1,0:T(8,128)S(1)}, f32[4096,256]{1,0:T(8,128)}, u32[]{:S(2)}) copy-start(f32[4096,256]{1,0:T(8,128)} %value.1) | copy-start | bytes 12582916
  1.4 15.1 %collective-permute-start.2 = (f32[64,1024]{1,0:T(8,128)S(1)}, f32[64,1024]{1,0:T(8,128)S(1)}, u32[]{:S(2)}, u32[]{:S(2)}) collective-permute-start(f32[64,1024]{1,0:T(8,128)S(1)} %get-tuple-element.77), channel_id=1, source_target_pairs={{0,3},{1,2},{2,1},{3,0},{4,7},{5,6},{6,5},{7,4},{8,11},{9,10},{10,... | collective-permute-start | bytes 786440 | tf_op jit(solution)/shard_map/ppermute | solution.py:24
  4.6 11.9 %collective-permute-start.1 = (f32[64,1024]{1,0:T(8,128)S(1)}, f32[64,1024]{1,0:T(8,128)S(1)}, u32[]{:S(2)}, u32[]{:S(2)}) collective-permute-start(f32[64,1024]{1,0:T(8,128)S(1)} %get-tuple-element.78), channel_id=1, source_target_pairs={{0,2},{1,3},{2,0},{3,1},{4,6},{5,7},{6,4},{7,5},{8,10},{9,11},{10,... | collective-permute-start | bytes 786440 | tf_op jit(solution)/shard_map/ppermute | solution.py:24
  5.3 12.0 %collective-permute-start = (f32[64,1024]{1,0:T(8,128)S(1)}, f32[64,1024]{1,0:T(8,128)S(1)}, u32[]{:S(2)}, u32[]{:S(2)}) collective-permute-start(f32[64,1024]{1,0:T(8,128)S(1)} %get-tuple-element.76), channel_id=1, source_target_pairs={{0,1},{1,0},{2,3},{3,2},{4,5},{5,4},{6,7},{7,6},{8,9},{9,8},{10,11... | collective-permute-start | bytes 786440 | tf_op jit(solution)/shard_map/ppermute | solution.py:24
  17.3 26.5 %collective-permute-start.3 = (f32[4,64,1024]{2,1,0:T(8,128)S(1)}, f32[4,64,1024]{2,1,0:T(8,128)S(1)}, u32[]{:S(2)}, u32[]{:S(2)}) collective-permute-start(f32[4,64,1024]{2,1,0:T(8,128)S(1)} %pad_maximum_fusion.refs_0_), channel_id=1, source_target_pairs={{0,18},{1,19},{2,16},{3,17},{4,22},{5,23},{6,20},{7,21},{8,26},{9,... | collective-permute-start | bytes 3145736 | tf_op jit(solution)/shard_map/ppermute | solution.py:24
  21.4 24.3 %collective-permute-start.4 = (f32[4,64,1024]{2,1,0:T(8,128)S(1)}, f32[4,64,1024]{2,1,0:T(8,128)S(1)}, u32[]{:S(2)}, u32[]{:S(2)}) collective-permute-start(f32[4,64,1024]{2,1,0:T(8,128)S(1)} %pad_maximum_fusion.refs_0_), channel_id=1, source_target_pairs={{0,4},{1,5},{2,6},{3,7},{4,0},{5,1},{6,2},{7,3},{8,12},{9,13},{10,... | collective-permute-start | bytes 3145736 | tf_op jit(solution)/shard_map/ppermute | solution.py:24
  23.3 24.5 %collective-permute-start.5 = (f32[4,64,1024]{2,1,0:T(8,128)S(1)}, f32[4,64,1024]{2,1,0:T(8,128)}, u32[]{:S(2)}, u32[]{:S(2)}) collective-permute-start(f32[4,64,1024]{2,1,0:T(8,128)S(1)} %pad_maximum_fusion.refs_0_), channel_id=1, source_target_pairs={{0,12},{1,13},{2,14},{3,15},{4,8},{5,9},{6,10},{7,11},{8,4},{9,5},... | collective-permute-start | bytes 3145736 | tf_op jit(solution)/shard_map/ppermute | solution.py:24
  43.8 4.7 %copy-start.1 = (f32[4,64,1024]{2,1,0:T(8,128)}, f32[4,64,1024]{2,1,0:T(8,128)S(1)}, u32[]{:S(2)}) copy-start(f32[4,64,1024]{2,1,0:T(8,128)S(1)} %collective-permute-done.3._.refs_0_) | copy-start | bytes 3145732
  45.7 1.0 copy-start.4
  47.8 22.7 %collective-permute-start.6 = (f32[4,64,1024]{2,1,0:T(8,128)S(1)}, f32[4,64,1024]{2,1,0:T(8,128)}, u32[]{:S(2)}, u32[]{:S(2)}) collective-permute-start(f32[4,64,1024]{2,1,0:T(8,128)S(1)} %collective-permute-done.3._.refs_0_), channel_id=1, source_target_pairs={{0,4},{1,5},{2,6},{3,7},{4,0},{5,1},{6,2},{7,3},{8,12},{9,13},{10,... | collective-permute-start | bytes 3145736 | tf_op jit(solution)/shard_map/ppermute | solution.py:24
  48.5 23.9 %collective-permute-start.7 = (f32[4,64,1024]{2,1,0:T(8,128)S(1)}, f32[4,64,1024]{2,1,0:T(8,128)S(1)}, u32[]{:S(2)}, u32[]{:S(2)}) collective-permute-start(f32[4,64,1024]{2,1,0:T(8,128)S(1)} %collective-permute-done.3._.refs_0_), channel_id=1, source_target_pairs={{0,12},{1,13},{2,14},{3,15},{4,8},{5,9},{6,10},{7,11},{8,4},{9,5},... | collective-permute-start | bytes 3145736 | tf_op jit(solution)/shard_map/ppermute | solution.py:24
  51.1 24.9 %collective-permute-start.8 = (f32[1024,256]{1,0:T(8,128)}, f32[1024,256]{1,0:T(8,128)S(1)}, u32[]{:S(2)}, u32[]{:S(2)}) collective-permute-start(f32[1024,256]{1,0:T(8,128)} %get-tuple-element.41), channel_id=1, source_target_pairs={{0,16},{1,17},{2,18},{3,19},{4,20},{5,21},{6,22},{7,23},{8,24},{9,... | collective-permute-start | bytes 3145736 | tf_op jit(solution)/shard_map/ppermute | solution.py:24
  52.6 23.4 %collective-permute-start.9 = (f32[1024,256]{1,0:T(8,128)}, f32[1024,256]{1,0:T(8,128)}, u32[]{:S(2)}, u32[]{:S(2)}) collective-permute-start(f32[1024,256]{1,0:T(8,128)} %get-tuple-element.42), channel_id=1, source_target_pairs={{0,1},{1,0},{2,3},{3,2},{4,5},{5,4},{6,7},{7,6},{8,9},{9,8},{10,11... | collective-permute-start | bytes 3145736 | tf_op jit(solution)/shard_map/ppermute | solution.py:24
  53.8 23.2 %collective-permute-start.10 = (f32[1024,256]{1,0:T(8,128)}, f32[1024,256]{1,0:T(8,128)}, u32[]{:S(2)}, u32[]{:S(2)}) collective-permute-start(f32[1024,256]{1,0:T(8,128)} %get-tuple-element.43), channel_id=1, source_target_pairs={{0,3},{1,2},{2,1},{3,0},{4,7},{5,6},{6,5},{7,4},{8,11},{9,10},{10,... | collective-permute-start | bytes 3145736 | tf_op jit(solution)/shard_map/ppermute | solution.py:24
  70.5 29.2 %collective-permute-start.19 = (f32[4,64,1024]{2,1,0:T(8,128)}, f32[4,64,1024]{2,1,0:T(8,128)}, u32[]{:S(2)}, u32[]{:S(2)}) collective-permute-start(f32[4,64,1024]{2,1,0:T(8,128)} %collective-permute-done.5.refs_1_), channel_id=1, source_target_pairs={{0,4},{1,5},{2,6},{3,7},{4,0},{5,1},{6,2},{7,3},{8,12},{9,13},{10,... | collective-permute-start | bytes 3145736 | tf_op jit(solution)/shard_map/ppermute | solution.py:24
  72.5 1.0 copy-start.6
  73.4 28.6 %collective-permute-start.20 = (f32[4,64,1024]{2,1,0:T(8,128)}, f32[4,64,1024]{2,1,0:T(8,128)}, u32[]{:S(2)}, u32[]{:S(2)}) collective-permute-start(f32[4,64,1024]{2,1,0:T(8,128)} %collective-permute-done.6.refs_2_), channel_id=1, source_target_pairs={{0,12},{1,13},{2,14},{3,15},{4,8},{5,9},{6,10},{7,11},{8,4},{9,5},... | collective-permute-start | bytes 3145736 | tf_op jit(solution)/shard_map/ppermute | solution.py:24
  77.0 2.3 %copy-start.5 = (f32[4,64,1024]{2,1,0:T(8,128)S(1)}, f32[4,64,1024]{2,1,0:T(8,128)}, u32[]{:S(2)}) copy-start(f32[4,64,1024]{2,1,0:T(8,128)} %copy-done.4) | copy-start | bytes 3145732
  79.4 7.1 %copy-start.2 = (f32[4,64,1024]{2,1,0:T(8,128)S(1)}, f32[4,64,1024]{2,1,0:T(8,128)}, u32[]{:S(2)}) copy-start(f32[4,64,1024]{2,1,0:T(8,128)} %copy-done.1) | copy-start | bytes 3145732
  79.4 7.1 %copy-start.7 = (f32[4,64,1024]{2,1,0:T(8,128)S(1)}, f32[4,64,1024]{2,1,0:T(8,128)}, u32[]{:S(2)}) copy-start(f32[4,64,1024]{2,1,0:T(8,128)} %copy-done.6) | copy-start | bytes 3145732
  93.4 1.9 %collective-permute-start.12 = (f32[2,4,64,256]{3,2,1,0:T(8,128)S(1)}, f32[2,4,64,256]{3,2,1,0:T(8,128)S(1)}, u32[]{:S(2)}, u32[]{:S(2)}) collective-permute-start(f32[2,4,64,256]{3,2,1,0:T(8,128)S(1)} %get-tuple-element.57), channel_id=1, source_target_pairs={{0,32},{1,33},{2,34},{3,35},{4,36},{5,37},{6,38},{7,39},{8,40},{9,... | collective-permute-start | bytes 1572872 | tf_op jit(solution)/shard_map/ppermute | solution.py:24
  93.4 2.7 %collective-permute-start.13 = (f32[2,4,64,256]{3,2,1,0:T(8,128)S(1)}, f32[2,4,64,256]{3,2,1,0:T(8,128)S(1)}, u32[]{:S(2)}, u32[]{:S(2)}) collective-permute-start(f32[2,4,64,256]{3,2,1,0:T(8,128)S(1)} %get-tuple-element.58), channel_id=1, source_target_pairs={{0,32},{1,33},{2,34},{3,35},{4,36},{5,37},{6,38},{7,39},{8,40},{9,... | collective-permute-start | bytes 1572872 | tf_op jit(solution)/shard_map/ppermute | solution.py:24
  93.9 2.9 %collective-permute-start.14 = (f32[2,4,64,256]{3,2,1,0:T(8,128)S(1)}, f32[2,4,64,256]{3,2,1,0:T(8,128)S(1)}, u32[]{:S(2)}, u32[]{:S(2)}) collective-permute-start(f32[2,4,64,256]{3,2,1,0:T(8,128)S(1)} %get-tuple-element.59), channel_id=1, source_target_pairs={{0,32},{1,33},{2,34},{3,35},{4,36},{5,37},{6,38},{7,39},{8,40},{9,... | collective-permute-start | bytes 1572872 | tf_op jit(solution)/shard_map/ppermute | solution.py:24
  95.3 22.5 %collective-permute-start.11 = (f32[2,4,64,256]{3,2,1,0:T(8,128)}, f32[2,4,64,256]{3,2,1,0:T(8,128)}, u32[]{:S(2)}, u32[]{:S(2)}) collective-permute-start(f32[2,4,64,256]{3,2,1,0:T(8,128)} %get-tuple-element.56), channel_id=1, source_target_pairs={{0,32},{1,33},{2,34},{3,35},{4,36},{5,37},{6,38},{7,39},{8,40},{9,... | collective-permute-start | bytes 1572872 | tf_op jit(solution)/shard_map/ppermute | solution.py:24
  98.2 20.8 %collective-permute-start.15 = (f32[2,4,64,256]{3,2,1,0:T(8,128)}, f32[2,4,64,256]{3,2,1,0:T(8,128)}, u32[]{:S(2)}, u32[]{:S(2)}) collective-permute-start(f32[2,4,64,256]{3,2,1,0:T(8,128)} %get-tuple-element.60.refs_2_), channel_id=1, source_target_pairs={{0,16},{1,17},{2,18},{3,19},{4,20},{5,21},{6,22},{7,23},{8,24},{9,... | collective-permute-start | bytes 1572872 | tf_op jit(solution)/shard_map/ppermute | solution.py:24
  98.7 21.2 %collective-permute-start.16 = (f32[2,4,64,256]{3,2,1,0:T(8,128)}, f32[2,4,64,256]{3,2,1,0:T(8,128)}, u32[]{:S(2)}, u32[]{:S(2)}) collective-permute-start(f32[2,4,64,256]{3,2,1,0:T(8,128)} %get-tuple-element.61.refs_3_), channel_id=1, source_target_pairs={{0,1},{1,0},{2,3},{3,2},{4,5},{5,4},{6,7},{7,6},{8,9},{9,8},{10,11... | collective-permute-start | bytes 1572872 | tf_op jit(solution)/shard_map/ppermute | solution.py:24
  99.7 21.1 %collective-permute-start.17 = (f32[2,4,64,256]{3,2,1,0:T(8,128)}, f32[2,4,64,256]{3,2,1,0:T(8,128)}, u32[]{:S(2)}, u32[]{:S(2)}) collective-permute-start(f32[2,4,64,256]{3,2,1,0:T(8,128)} %get-tuple-element.62.refs_4_), channel_id=1, source_target_pairs={{0,3},{1,2},{2,1},{3,0},{4,7},{5,6},{6,5},{7,4},{8,11},{9,10},{10,... | collective-permute-start | bytes 1572872 | tf_op jit(solution)/shard_map/ppermute | solution.py:24
  107.6 1.7 %copy-start.3 = (f32[2,3,2,4,64,256]{5,4,3,2,1,0:T(8,128)}, f32[2,3,2,4,64,256]{5,4,3,2,1,0:T(8,128)S(1)}, u32[]{:S(2)}) copy-start(f32[2,3,2,4,64,256]{5,4,3,2,1,0:T(8,128)S(1)} %get-tuple-element.68) | copy-start | bytes 9437188
  109.3 20.5 %collective-permute-start.21 = (f32[2,4,64,256]{3,2,1,0:T(8,128)}, f32[2,4,64,256]{3,2,1,0:T(8,128)S(1)}, u32[]{:S(2)}, u32[]{:S(2)}) collective-permute-start(f32[2,4,64,256]{3,2,1,0:T(8,128)} %get-tuple-element.67), channel_id=1, source_target_pairs={{0,32},{1,33},{2,34},{3,35},{4,36},{5,37},{6,38},{7,39},{8,40},{9,... | collective-permute-start | bytes 1572872 | tf_op jit(solution)/shard_map/ppermute | solution.py:24
  117.8 8.3 %collective-permute-start.25 = (f32[4,64,256]{2,1,0:T(8,128)S(1)}, f32[4,64,256]{2,1,0:T(8,128)S(1)}, u32[]{:S(2)}, u32[]{:S(2)}) collective-permute-start(f32[4,64,256]{2,1,0:T(8,128)S(1)} %get-tuple-element.72), channel_id=1, source_target_pairs={{0,16},{1,17},{2,18},{3,19},{4,20},{5,21},{6,22},{7,23},{8,24},{9,... | collective-permute-start | bytes 786440 | tf_op jit(solution)/shard_map/ppermute | solution.py:24
  119.0 8.3 %collective-permute-start.26 = (f32[4,64,256]{2,1,0:T(8,128)S(1)}, f32[4,64,256]{2,1,0:T(8,128)S(1)}, u32[]{:S(2)}, u32[]{:S(2)}) collective-permute-start(f32[4,64,256]{2,1,0:T(8,128)S(1)} %get-tuple-element.73), channel_id=1, source_target_pairs={{0,1},{1,0},{2,3},{3,2},{4,5},{5,4},{6,7},{7,6},{8,9},{9,8},{10,11... | collective-permute-start | bytes 786440 | tf_op jit(solution)/shard_map/ppermute | solution.py:24
  119.9 9.0 %collective-permute-start.27 = (f32[4,64,256]{2,1,0:T(8,128)S(1)}, f32[4,64,256]{2,1,0:T(8,128)S(1)}, u32[]{:S(2)}, u32[]{:S(2)}) collective-permute-start(f32[4,64,256]{2,1,0:T(8,128)S(1)} %get-tuple-element.74), channel_id=1, source_target_pairs={{0,3},{1,2},{2,1},{3,0},{4,7},{5,6},{6,5},{7,4},{8,11},{9,10},{10,... | collective-permute-start | bytes 786440 | tf_op jit(solution)/shard_map/ppermute | solution.py:24
  123.2 11.3 %collective-permute-start.18 = (f32[4,64,256]{2,1,0:T(8,128)}, f32[4,64,256]{2,1,0:T(8,128)S(1)}, u32[]{:S(2)}, u32[]{:S(2)}) collective-permute-start(f32[4,64,256]{2,1,0:T(8,128)} %get-tuple-element.64), channel_id=1, source_target_pairs={{0,64},{1,65},{2,66},{3,67},{4,68},{5,69},{6,70},{7,71},{8,72},{9,... | collective-permute-start | bytes 786440 | tf_op jit(solution)/shard_map/ppermute | solution.py:24
  126.2 13.1 %collective-permute-start.22 = (f32[4,64,256]{2,1,0:T(8,128)}, f32[4,64,256]{2,1,0:T(8,128)S(1)}, u32[]{:S(2)}, u32[]{:S(2)}) collective-permute-start(f32[4,64,256]{2,1,0:T(8,128)} %get-tuple-element.69), channel_id=1, source_target_pairs={{0,16},{1,17},{2,18},{3,19},{4,20},{5,21},{6,22},{7,23},{8,24},{9,... | collective-permute-start | bytes 786440 | tf_op jit(solution)/shard_map/ppermute | solution.py:24
  127.4 11.9 %collective-permute-start.23 = (f32[4,64,256]{2,1,0:T(8,128)}, f32[4,64,256]{2,1,0:T(8,128)S(1)}, u32[]{:S(2)}, u32[]{:S(2)}) collective-permute-start(f32[4,64,256]{2,1,0:T(8,128)} %get-tuple-element.70), channel_id=1, source_target_pairs={{0,1},{1,0},{2,3},{3,2},{4,5},{5,4},{6,7},{7,6},{8,9},{9,8},{10,11... | collective-permute-start | bytes 786440 | tf_op jit(solution)/shard_map/ppermute | solution.py:24
  128.9 10.4 %collective-permute-start.24 = (f32[4,64,256]{2,1,0:T(8,128)}, f32[4,64,256]{2,1,0:T(8,128)S(1)}, u32[]{:S(2)}, u32[]{:S(2)}) collective-permute-start(f32[4,64,256]{2,1,0:T(8,128)} %get-tuple-element.71), channel_id=1, source_target_pairs={{0,3},{1,2},{2,1},{3,0},{4,7},{5,6},{6,5},{7,4},{8,11},{9,10},{10,... | collective-permute-start | bytes 786440 | tf_op jit(solution)/shard_map/ppermute | solution.py:24
  129.9 15.0 %collective-permute-start.28 = (f32[4,64,256]{2,1,0:T(8,128)S(1)}, f32[4,64,256]{2,1,0:T(8,128)S(1)}, u32[]{:S(2)}, u32[]{:S(2)}) collective-permute-start(f32[4,64,256]{2,1,0:T(8,128)S(1)} %shard_map.36), channel_id=1, source_target_pairs={{0,64},{1,65},{2,66},{3,67},{4,68},{5,69},{6,70},{7,71},{8,72},{9,... | collective-permute-start | bytes 786440 | tf_op jit(solution)/shard_map/ppermute | solution.py:24

commit v13 on v12

--- a/solution.py
+++ b/solution.py
@@ -167,23 +167,32 @@
 
     def kernel(flags, *refs):
         blocks, rest = refs[: len(arrays)], refs[len(arrays) + len(after):]
-        high, low, ahead, keep, give, both, left_high, left_low = rest
-        swapped, core = flags[0] == 1, flags[1]
+        high, low, ahead, keep, give, both, here_keep, here_give, left_high, left_low = rest
+        swapped, core, side = flags[0] == 1, flags[1], flags[2] == 1
 
         def store(d, total):
-            for part in range(2):
-                for block, into in places(d):
+            for block, into in places(d):
+                kept, given = [], []
+                for part in range(2):
                     zero, one = ahead[d, part, into], total[part, block]
-                    kept, given = jnp.where(swapped, one, zero), jnp.where(swapped, zero, one)
-                    if d == 0:
-                        keep[0, part, into], give[part, into] = kept, given
-                    else:
-                        both[core, d - 1, part, into], both[1 - core, d - 1, part, into] = kept, given
+                    kept.append(jnp.where(swapped, one, zero))
+                    given.append(jnp.where(swapped, zero, one))
+                if d == 0:
+                    for part in range(2):
+                        keep[0, part, into], give[part, into] = kept[part], given[part]
+                else:
+                    here_keep[d - 1, into] = jnp.where(side, kept[1], kept[0])
+                    here_give[d - 1, into] = jnp.where(side, given[1], given[0])
+                    both[core, d - 1, into] = jnp.where(side, kept[0], kept[1])
+                    both[1 - core, d - 1, into] = jnp.where(side, given[0], given[1])
 
         multiplied(blocks, left_high, left_low, high, low, store)
 
-    piece = (2, 4, rows, columns)
-    shapes = [jax.ShapeDtypeStruct(shape, jnp.float32) for shape in ((1, *piece), piece, (2, 3, *piece))]
+    piece = (4, rows, columns)
+    shapes = [
+        jax.ShapeDtypeStruct(shape, jnp.float32)
+        for shape in ((1, 2, *piece), (2, *piece), (2, 3, *piece), (3, *piece), (3, *piece))
+    ]
     scratch = pltpu.VMEM((8 * rows, depth), jnp.bfloat16)
     return call(
         kernel, flags, (*arrays, *after, *rights, third),
@@ -192,27 +201,37 @@
     )
 
 
-def added_by_core_kernel(side, both, *outs):
-    for d, (here, there) in enumerate(zip(outs[:3], outs[3:])):
-        here[...] = both[0, d, side[0]] + both[1, d, side[0]]
-        there[...] = both[0, d, 1 - side[0]] + both[1, d, 1 - side[0]]
-
-
-def added_by_core(side, both):
-    shape = jax.ShapeDtypeStruct(both.shape[3:], jnp.float32)
-    found = call(added_by_core_kernel, side, (both,), [whole(both)], [shape] * 6, [whole(shape)] * 6)
-    return found[:3], found[3:]
-
-
-def onward_kernel(side, keep, got, one, two, three, out):
+def three_kernel(_, one, two, *outs):
+    for d, out in enumerate(outs):
+        out[...] = one[d] + two[d]
+
+
+def three_sums(scalars, one, two):
+    shape = jax.ShapeDtypeStruct(one.shape[1:], jnp.float32)
+    return call(three_kernel, scalars, (one, two), [whole(one), whole(two)], [shape] * 3, [whole(shape)] * 3)
+
+
+def both_kernel(_, both, *outs):
+    for d, out in enumerate(outs):
+        out[...] = both[0, d] + both[1, d]
+
+
+def both_sums(scalars, both):
+    shape = jax.ShapeDtypeStruct(both.shape[2:], jnp.float32)
+    return call(both_kernel, scalars, (both,), [whole(both)], [shape] * 3, [whole(shape)] * 3)
+
+
+def onward_kernel(side, keep, got, one, two, three, *rest):
+    out = rest[-1]
     part = 1 - side[0]
     out[...] = (keep[0, part] + got[part]) + (one[...] + (two[...] + three[...]))
 
 
-def onward(side, keep, got, terms):
+def onward(side, keep, got, terms, after):
     shape = jax.ShapeDtypeStruct(got.shape[1:], jnp.float32)
     values = (keep, got, *terms)
-    return call(onward_kernel, side, values, [whole(value) for value in values], shape, whole(shape))
+    specs = [whole(value) for value in values] + [ANYWHERE] * len(after)
+    return call(onward_kernel, side, (*values, *after), specs, shape, whole(shape))
 
 
 def sum_kernel(side, keep, got, *refs):
@@ -261,12 +280,12 @@
     mine = jnp.stack([block(0), send(block(1), dy=1), send(block(3), dy=2), send(block(2), dy=3)])
     other = send(mine, dx=1, dy=2)
     own_one, own_three = send(mine, dz=1), send(mine, dz=3)
+    far, *_ = lax.optimization_barrier((other, own_one, own_three))
+    far_one, far_three = lax.optimization_barrier((send(far, dz=1), send(far, dz=3)))
+
+    own_two, far_two = send(own_three, dz=1), send(far_one, dz=3)
+
     pieces = cut_after(quarter.reshape(1), right, other)
-    far, *_ = lax.optimization_barrier((other, own_one, own_three, *pieces))
-    far_one, far_three = lax.optimization_barrier((send(far, dz=1), send(far, dz=3)))
-
-    own_two, far_two = send(own_three, dz=1), send(far_one, dz=3)
-
     pieces = [pieces[0]] + [send(pieces[d], **NEAR[d]) for d in range(1, 4)]
     rights = split(swap, pieces)
 
@@ -276,8 +295,8 @@
     keep, third, *gives = early
     got = [send(give, core=1) for give in gives]
     sums = added(swap, keep, got[1:])
-    late_keep, late_give, both = late_products(
-        jnp.stack([swap[0], core]), ((own_two,), (far_two,)), third, rights, sums
+    late_keep, late_give, both, here_keep, here_give = late_products(
+        jnp.stack([swap[0], core, side[0]]), ((own_two,), (far_two,)), third, rights, sums
     )
     both = lax.all_to_all(both, AXES, 0, 0, tiled=True, axis_index_groups=CORES)
 
@@ -285,9 +304,10 @@
     early_ends = here, send(there, dhi=1)
 
     late_got = send(late_give, core=1)
-    kept, passed = added_by_core(side, both)
+    passed = both_sums(swap, both)
     passed = [send(passed[d - 1], **NEAR[d]) for d in range(1, 4)]
-    passed = send(onward(side, late_keep, late_got, passed), dhi=1)
+    kept = three_sums(swap, here_keep, send(here_give, core=1))
+    passed = send(onward(side, late_keep, late_got, passed, kept), dhi=1)
     kept = [send(kept[d - 1], **NEAR[d]) for d in range(1, 4)]
 
     place = jnp.stack([(z & 1) ^ swap[0], y ^ (2 * side[0]), side[0]])

time: 147 us -> 160 us (1.088)
  local copies, waits for them, and re-layouts: 5.06 us -> 16 us
  waiting for transfers between devices: 63 us -> 70.4 us
  starting transfers between devices: 40.4 us -> 37.8 us
  blocking collectives: 7.55 us -> 5.13 us
    unnamed x16 -> x40, local copies, waits for them, and re-layouts: 3.62 us -> 14.5 us
    ppermute x29 -> x30, waiting for transfers between devices: 63 us -> 70.4 us  [send(): return lax.ppermute(value, AXES, pairs)]
    ppermute x29 -> x30, starting transfers between devices: 40.4 us -> 37.8 us  [send(): return lax.ppermute(value, AXES, pairs)]
    all_to_all x1, blocking collectives: 7.55 us -> 5.13 us  [per_device(): both = lax.all_to_all(both, AXES, 0, 0, tiled=True, axis_index_groups=CORES)]
    pallas_call x10 -> x11, Pallas kernels: 30.1 us -> 29.3 us  [call(): pl.pallas_call(kernel, grid_spec=pltpu.PrefetchScalarGridSpec(num_scalar_...]
  transfers between devices with their start and end apart: 29 -> 30, of which waited for: 15 -> 18; matrix products, arithmetic and copies ran while one was open for 0% -> 0% of each run, Pallas kernels for 20% -> 17%
where the time goes in v13:
time: 160 us; the launch traced here: 159 us
  waiting for transfers between devices  70.4 us (44%)
  starting transfers between devices  37.8 us (24%)
  Pallas kernels  29.3 us (18%)
  local copies, waits for them, and re-layouts  16 us (10%)
  blocking collectives  5.13 us (3%)
    ppermute x30, waiting for transfers between devices, send(): return lax.ppermute(value, AXES, pairs)  70.4 us
    ppermute x30, starting transfers between devices, send(): return lax.ppermute(value, AXES, pairs)  37.8 us
    pallas_call x11, Pallas kernels, call(): pl.pallas_call(kernel, grid_spec=pltpu.PrefetchScalarGridSpec(num_scalar_...  29.3 us
    unnamed x40, local copies, waits for them, and re-layouts  14.5 us
    all_to_all x1, blocking collectives, per_device(): both = lax.all_to_all(both, AXES, 0, 0, tiled=True, axis_index_groups=CORES)  5.13 us
  transfers between devices with their start and end apart: 30, of which 18 were waited for; matrix products, arithmetic and copies ran while one was open for 0% of the time, Pallas kernels for 17%

profile of v13, /device:TPU:0, one launch (start us, length us, event | category | flops | bytes accessed | tf_op | source)
XLA Modules:
  0.0 159.1 jit_solution(10414443210668927711)
XLA Ops:
  0.0 1.4 dynamic-slice_bitcast_fusion
  1.4 3.2 %collective-permute-start.2 = (f32[64,1024]{1,0:T(8,128)S(1)}, f32[64,1024]{1,0:T(8,128)S(1)}, u32[]{:S(2)}, u32[]{:S(2)}) collective-permute-start(f32[64,1024]{1,0:T(8,128)S(1)} %get-tuple-element.81), channel_id=1, source_target_pairs={{0,3},{1,2},{2,1},{3,0},{4,7},{5,6},{6,5},{7,4},{8,11},{9,10},{10,... | collective-permute-start | bytes 786440 | tf_op jit(solution)/shard_map/ppermute | solution.py:24
  4.6 0.6 collective-permute-start.1
  5.3 0.4 collective-permute-start
  5.6 10.9 %collective-permute-done.2 = f32[64,1024]{1,0:T(8,128)S(1)} collective-permute-done((f32[64,1024]{1,0:T(8,128)S(1)}, f32[64,1024]{1,0:T(8,128)S(1)}, u32[]{:S(2)}, u32[]{:S(2)}) %collective-permute-start.2) | collective-permute-done | bytes 262176 | tf_op jit(solution)/shard_map/ppermute | solution.py:24
  16.6 0.7 collective-permute-done
  17.3 4.0 %collective-permute-start.3 = (f32[4,64,1024]{2,1,0:T(8,128)S(1)}, f32[4,64,1024]{2,1,0:T(8,128)S(1)}, u32[]{:S(2)}, u32[]{:S(2)}) collective-permute-start(f32[4,64,1024]{2,1,0:T(8,128)S(1)} %pad_maximum_fusion.refs_0_), channel_id=1, source_target_pairs={{0,18},{1,19},{2,16},{3,17},{4,22},{5,23},{6,20},{7,21},{8,26},{9,... | collective-permute-start | bytes 3145736 | tf_op jit(solution)/shard_map/ppermute | solution.py:24
  21.4 1.9 %collective-permute-start.4 = (f32[4,64,1024]{2,1,0:T(8,128)S(1)}, f32[4,64,1024]{2,1,0:T(8,128)S(1)}, u32[]{:S(2)}, u32[]{:S(2)}) collective-permute-start(f32[4,64,1024]{2,1,0:T(8,128)S(1)} %pad_maximum_fusion.refs_0_), channel_id=1, source_target_pairs={{0,4},{1,5},{2,6},{3,7},{4,0},{5,1},{6,2},{7,3},{8,12},{9,13},{10,... | collective-permute-start | bytes 3145736 | tf_op jit(solution)/shard_map/ppermute | solution.py:24
  23.3 2.5 %collective-permute-start.5 = (f32[4,64,1024]{2,1,0:T(8,128)S(1)}, f32[4,64,1024]{2,1,0:T(8,128)}, u32[]{:S(2)}, u32[]{:S(2)}) collective-permute-start(f32[4,64,1024]{2,1,0:T(8,128)S(1)} %pad_maximum_fusion.refs_0_), channel_id=1, source_target_pairs={{0,12},{1,13},{2,14},{3,15},{4,8},{5,9},{6,10},{7,11},{8,4},{9,5},... | collective-permute-start | bytes 3145736 | tf_op jit(solution)/shard_map/ppermute | solution.py:24
  25.8 18.0 %collective-permute-done.3._.refs_0_ = f32[4,64,1024]{2,1,0:T(8,128)S(1)} collective-permute-done((f32[4,64,1024]{2,1,0:T(8,128)S(1)}, f32[4,64,1024]{2,1,0:T(8,128)S(1)}, u32[]{:S(2)}, u32[]{:S(2)}) %collective-permute-start.3) | collective-permute-done | bytes 1048608 | tf_op jit(solution)/shard_map/ppermute | solution.py:24
  43.8 1.2 collective-permute-done.4.refs_2_
  45.0 1.0 copy-done.16
  46.0 1.8 %collective-permute-done.5.refs_1_ = f32[4,64,1024]{2,1,0:T(8,128)} collective-permute-done((f32[4,64,1024]{2,1,0:T(8,128)S(1)}, f32[4,64,1024]{2,1,0:T(8,128)}, u32[]{:S(2)}, u32[]{:S(2)}) %collective-permute-start.5) | collective-permute-done | bytes 1048608 | tf_op jit(solution)/shard_map/ppermute | solution.py:24
  47.8 0.6 collective-permute-start.6
  48.4 2.3 %collective-permute-start.7 = (f32[4,64,1024]{2,1,0:T(8,128)S(1)}, f32[4,64,1024]{2,1,0:T(8,128)S(1)}, u32[]{:S(2)}, u32[]{:S(2)}) collective-permute-start(f32[4,64,1024]{2,1,0:T(8,128)S(1)} %collective-permute-done.3._.refs_0_), channel_id=1, source_target_pairs={{0,12},{1,13},{2,14},{3,15},{4,8},{5,9},{6,10},{7,11},{8,4},{9,5},... | collective-permute-start | bytes 3145736 | tf_op jit(solution)/shard_map/ppermute | solution.py:24
  50.8 1.8 %shard_map.28 = (f32[1024,256]{1,0:T(8,128)S(1)}, f32[1024,256]{1,0:T(8,128)}, f32[1024,256]{1,0:T(8,128)}, f32[1024,256]{1,0:T(8,128)}) custom-call(s32[1]{0:T(128)} %bitcast.8.quarter, f32[4096,256]{1,0:T(8,128)S(1)} %copy-done.7, f32[4,64,1024]{2,1,0:T(8,128)S(1)} %collective-permute-done.3._.refs_0_), custom_call_target="tpu_custom_call" | custom-call | flops 1 | bytes 1 | tf_op jit(solution)/shard_map/pallas_call | solution.py:47
  52.6 1.0 copy-done.10
  53.6 0.5 collective-permute-start.8
  54.1 1.0 collective-permute-start.9
  55.1 1.9 %collective-permute-start.10 = (f32[1024,256]{1,0:T(8,128)}, f32[1024,256]{1,0:T(8,128)}, u32[]{:S(2)}, u32[]{:S(2)}) collective-permute-start(f32[1024,256]{1,0:T(8,128)} %get-tuple-element.48), channel_id=1, source_target_pairs={{0,3},{1,2},{2,1},{3,0},{4,7},{5,6},{6,5},{7,4},{8,11},{9,10},{10,... | collective-permute-start | bytes 3145736 | tf_op jit(solution)/shard_map/ppermute | solution.py:24
  57.0 13.9 %collective-permute-done.6.refs_2_ = f32[4,64,1024]{2,1,0:T(8,128)} collective-permute-done((f32[4,64,1024]{2,1,0:T(8,128)S(1)}, f32[4,64,1024]{2,1,0:T(8,128)}, u32[]{:S(2)}, u32[]{:S(2)}) %collective-permute-start.6) | collective-permute-done | bytes 1048608 | tf_op jit(solution)/shard_map/ppermute | solution.py:24
  70.9 0.6 collective-permute-start.19
  71.5 0.4 collective-permute-done.7.refs_1_
  71.9 1.0 copy-done.18
  72.9 2.1 %collective-permute-start.20 = (f32[4,64,1024]{2,1,0:T(8,128)}, f32[4,64,1024]{2,1,0:T(8,128)}, u32[]{:S(2)}, u32[]{:S(2)}) collective-permute-start(f32[4,64,1024]{2,1,0:T(8,128)} %collective-permute-done.6.refs_2_), channel_id=1, source_target_pairs={{0,12},{1,13},{2,14},{3,15},{4,8},{5,9},{6,10},{7,11},{8,4},{9,5},... | collective-permute-start | bytes 3145736 | tf_op jit(solution)/shard_map/ppermute | solution.py:24
  75.0 0.6 collective-permute-done.8.refs_1_
  75.5 1.0 copy-done.12
  76.6 1.0 copy-done.14
  77.5 0.6 collective-permute-done.10.refs_3_
  78.1 1.2 copy-done.11
  79.3 1.2 copy-done.13
  80.6 1.2 copy-done.15
  81.8 2.1 %shard_map.29 = (bf16[1024,1024]{1,0:T(8,128)(2,1)S(1)}, bf16[1024,1024]{1,0:T(8,128)(2,1)S(1)}) custom-call(s32[1]{0:T(128)} %bitcast.3._.swap, f32[1024,256]{1,0:T(8,128)S(1)} %copy-done.11, f32[1024,256]{1,0:T(8,128)S(1)} %copy-done.13, f32[1024,256]{1,0:T(8,128)S(1)} %copy-done.15, f32[1024,256]{1,0:T(8,128)} %collective-permute-done.10.refs_3_), custom_call_target="tpu_custom_call" | custom-call | flops 1 | bytes 1 | tf_op jit(solution)/shard_map/pallas_call | solution.py:47
  83.9 7.8 %shard_map.30 = (f32[4,2,4,64,256]{4,3,2,1,0:T(8,128)S(1)}, f32[4,2,4,64,256]{4,3,2,1,0:T(8,128)S(1)}, f32[2,4,64,256]{3,2,1,0:T(8,128)}, f32[2,4,64,256]{3,2,1,...) custom-call(s32[1]{0:T(128)} %bitcast.3._.swap, f32[4,64,1024]{2,1,0:T(8,128)S(1)} %pad_maximum_fusion.refs_0_, ...), custom_call_target="tpu_custom_call" | custom-call | flops 1 | bytes 1 | tf_op jit(solution)/shard_map/pallas_call | solution.py:47
  91.7 7.0 %shard_map.31 = (f32[4,2,4,64,256]{4,3,2,1,0:T(8,128)S(1)}, f32[4,2,4,64,256]{4,3,2,1,0:T(8,128)S(1)}, f32[2,4,64,256]{3,2,1,0:T(8,128)}, f32[2,4,64,256]{3,2,1,...) custom-call(s32[1]{0:T(128)} %bitcast.3._.swap, ...), custom_call_target="tpu_custom_call", output_to_operand_aliasing={{0}: (4, {}), {1}: (5, {}), {2}: (6, {}), {3}: (7, {}), {4}... | custom-call | flops 1 | bytes 1 | tf_op jit(solution)/shard_map/pallas_call | solution.py:47
  98.7 1.4 copy-done.2
  100.1 1.3 copy-done.5
  101.4 0.5 collective-permute-start.13
  101.9 2.1 %collective-permute-done.12.refs_0_ = f32[2,4,64,256]{3,2,1,0:T(8,128)S(1)} collective-permute-done((f32[2,4,64,256]{3,2,1,0:T(8,128)S(1)}, f32[2,4,64,256]{3,2,1,0:T(8,128)S(1)}, u32[]{:S(2)}, u32[]{:S(2)}) %collective-permute-start.12) | collective-permute-done | bytes 524320 | tf_op jit(solution)/shard_map/ppermute | solution.py:24
  104.0 0.1 collective-permute-start.11
  104.2 0.2 collective-permute-done.13.refs_1_
  104.4 0.7 collective-permute-done.14.refs_2_
  105.2 1.6 copy-done.3
  106.7 1.4 shard_map.32
  108.1 1.6 copy-done.6
  109.7 5.7 %shard_map.34 = (f32[1,2,4,64,256]{4,3,2,1,0:T(8,128)S(1)}, f32[2,4,64,256]{3,2,1,0:T(8,128)S(1)}, f32[2,3,4,64,256]{4,3,2,1,0:T(8,128)S(1)}, f32[3,4,64,256]{3,2,1,0:T(8,128)S(1)}, f32[3,4,64,256]{3,2,1,0:T(8,128)S(1)}) custom-call(s32[3]{0:T(128)S(1)} %add_add_fusion.1.flags, f32[4,64,1024]{2,1,0:T(8,128)} %collective-permute-done.19.refs_0_, ...), custom_call_target="tpu_custom_call" | custom-call | flops 1 | bytes 1 | tf_op jit(solution)/shard_map/pallas_call | solution.py:47
  115.4 0.2 collective-permute-start.22
  115.7 1.5 collective-permute-start.15
  117.2 1.9 %collective-permute-start.17 = (f32[2,4,64,256]{3,2,1,0:T(8,128)S(1)}, f32[2,4,64,256]{3,2,1,0:T(8,128)S(1)}, u32[]{:S(2)}, u32[]{:S(2)}) collective-permute-start(f32[2,4,64,256]{3,2,1,0:T(8,128)S(1)} %get-tuple-element.64.refs_4_), channel_id=1, source_target_pairs={{0,3},{1,2},{2,1},{3,0},{4,7},{5,6},{6,5},{7,4},{8,11},{9,10},{10,... | collective-permute-start | bytes 1572872 | tf_op jit(solution)/shard_map/ppermute | solution.py:24
  119.1 5.1 %all_to_all.5.both = f32[2,3,4,64,256]{4,3,2,1,0:T(8,128)S(1)} all-to-all(f32[2,3,4,64,256]{4,3,2,1,0:T(8,128)S(1)} %get-tuple-element.75), channel_id=1, replica_groups={{0,32},{1,33},{2,34},{3,35},{4,36},{5,37},{6,38},{7,39},{8,40},{9,41},{..., dimensions={0} | all-to-all | bytes 3145728 | tf_op jit(solution)/shard_map/all_to_all | solution.py:301
  124.3 5.6 %collective-permute-done.15.refs_0_ = f32[2,4,64,256]{3,2,1,0:T(8,128)S(1)} collective-permute-done((f32[2,4,64,256]{3,2,1,0:T(8,128)S(1)}, f32[2,4,64,256]{3,2,1,0:T(8,128)S(1)}, u32[]{:S(2)}, u32[]{:S(2)}) %collective-permute-start.15) | collective-permute-done | bytes 524320 | tf_op jit(solution)/shard_map/ppermute | solution.py:24
  129.9 1.5 collective-permute-start.26
  131.4 0.9 collective-permute-done.17.refs_2_
  132.3 1.7 %collective-permute-start.28 = (f32[4,64,256]{2,1,0:T(8,128)S(1)}, f32[4,64,256]{2,1,0:T(8,128)S(1)}, u32[]{:S(2)}, u32[]{:S(2)}) collective-permute-start(f32[4,64,256]{2,1,0:T(8,128)S(1)} %get-tuple-element.78), channel_id=1, source_target_pairs={{0,3},{1,2},{2,1},{3,0},{4,7},{5,6},{6,5},{7,4},{8,11},{9,10},{10,... | collective-permute-start | bytes 786440 | tf_op jit(solution)/shard_map/ppermute | solution.py:24
  134.0 0.9 shard_map.33
  134.9 2.8 %collective-permute-start.18 = (f32[4,64,256]{2,1,0:T(8,128)}, f32[4,64,256]{2,1,0:T(8,128)S(1)}, u32[]{:S(2)}, u32[]{:S(2)}) collective-permute-start(f32[4,64,256]{2,1,0:T(8,128)} %get-tuple-element.66), channel_id=1, source_target_pairs={{0,64},{1,65},{2,66},{3,67},{4,68},{5,69},{6,70},{7,71},{8,72},{9,... | collective-permute-start | bytes 786440 | tf_op jit(solution)/shard_map/ppermute | solution.py:24
  137.9 1.3 collective-permute-start.23
  139.1 1.8 %collective-permute-done.28.three = f32[4,64,256]{2,1,0:T(8,128)S(1)} collective-permute-done((f32[4,64,256]{2,1,0:T(8,128)S(1)}, f32[4,64,256]{2,1,0:T(8,128)S(1)}, u32[]{:S(2)}, u32[]{:S(2)}) %collective-permute-start.28) | collective-permute-done | bytes 262176 | tf_op jit(solution)/shard_map/ppermute | solution.py:24
  141.0 1.6 %collective-permute-start.25 = (f32[4,64,256]{2,1,0:T(8,128)S(1)}, f32[4,64,256]{2,1,0:T(8,128)}, u32[]{:S(2)}, u32[]{:S(2)}) collective-permute-start(f32[4,64,256]{2,1,0:T(8,128)S(1)} %get-tuple-element.74.rest_2_), channel_id=1, source_target_pairs={{0,3},{1,2},{2,1},{3,0},{4,7},{5,6},{6,5},{7,4},{8,11},{9,10},{10,... | collective-permute-start | bytes 786440 | tf_op jit(solution)/shard_map/ppermute | solution.py:24
  142.7 3.0 %collective-permute-start.29 = (f32[4,64,256]{2,1,0:T(8,128)S(1)}, f32[4,64,256]{2,1,0:T(8,128)S(1)}, u32[]{:S(2)}, u32[]{:S(2)}) collective-permute-start(f32[4,64,256]{2,1,0:T(8,128)S(1)} %shard_map.37), channel_id=1, source_target_pairs={{0,64},{1,65},{2,66},{3,67},{4,68},{5,69},{6,70},{7,71},{8,72},{9,... | collective-permute-start | bytes 786440 | tf_op jit(solution)/shard_map/ppermute | solution.py:24
  145.7 1.2 collective-permute-done.18.other_one
  146.9 4.5 %collective-permute-done.23.across = f32[4,64,256]{2,1,0:T(8,128)S(1)} collective-permute-done((f32[4,64,256]{2,1,0:T(8,128)S(1)}, f32[4,64,256]{2,1,0:T(8,128)S(1)}, u32[]{:S(2)}, u32[]{:S(2)}) %collective-permute-start.23) | collective-permute-done | bytes 262176 | tf_op jit(solution)/shard_map/ppermute | solution.py:24
  151.4 5.3 %collective-permute-done.29.other_two = f32[4,64,256]{2,1,0:T(8,128)S(1)} collective-permute-done((f32[4,64,256]{2,1,0:T(8,128)S(1)}, f32[4,64,256]{2,1,0:T(8,128)S(1)}, u32[]{:S(2)}, u32[]{:S(2)}) %collective-permute-start.29) | collective-permute-done | bytes 262176 | tf_op jit(solution)/shard_map/ppermute | solution.py:24
  156.7 2.4 %shard_map.38 = f32[2,4,64,256]{3,2,1,0:T(8,128)} custom-call(s32[3]{0:T(128)S(1)} %add_add_fusion.place, f32[4,64,256]{2,1,0:T(8,128)S(1)} %get-tuple-element.65.one, f32[4,64,256]{2,1,0:T(8,128)S(1)} %collective-permute-done.18.other_one, f32[1,2,4,64,256]{4,3,2,1,0:T(8,128)S(1)} %get-tuple-element.68.keep, ...), custom_call_target="tpu_custom_call" | custom-call | flops 1 | bytes 1 | tf_op jit(solution)/shard_map/pallas_call | solution.py:47
  (52 shorter events, 0.6 us)
Async XLA Ops:
  0.0 50.8 %copy-start.7 = (f32[4096,256]{1,0:T(8,128)S(1)}, f32[4096,256]{1,0:T(8,128)}, u32[]{:S(2)}) copy-start(f32[4096,256]{1,0:T(8,128)} %value.1) | copy-start | bytes 12582916
  1.4 15.1 %collective-permute-start.2 = (f32[64,1024]{1,0:T(8,128)S(1)}, f32[64,1024]{1,0:T(8,128)S(1)}, u32[]{:S(2)}, u32[]{:S(2)}) collective-permute-start(f32[64,1024]{1,0:T(8,128)S(1)} %get-tuple-element.81), channel_id=1, source_target_pairs={{0,3},{1,2},{2,1},{3,0},{4,7},{5,6},{6,5},{7,4},{8,11},{9,10},{10,... | collective-permute-start | bytes 786440 | tf_op jit(solution)/shard_map/ppermute | solution.py:24
  4.6 11.9 %collective-permute-start.1 = (f32[64,1024]{1,0:T(8,128)S(1)}, f32[64,1024]{1,0:T(8,128)S(1)}, u32[]{:S(2)}, u32[]{:S(2)}) collective-permute-start(f32[64,1024]{1,0:T(8,128)S(1)} %get-tuple-element.82), channel_id=1, source_target_pairs={{0,2},{1,3},{2,0},{3,1},{4,6},{5,7},{6,4},{7,5},{8,10},{9,11},{10,... | collective-permute-start | bytes 786440 | tf_op jit(solution)/shard_map/ppermute | solution.py:24
  5.3 12.0 %collective-permute-start = (f32[64,1024]{1,0:T(8,128)S(1)}, f32[64,1024]{1,0:T(8,128)S(1)}, u32[]{:S(2)}, u32[]{:S(2)}) collective-permute-start(f32[64,1024]{1,0:T(8,128)S(1)} %get-tuple-element.80), channel_id=1, source_target_pairs={{0,1},{1,0},{2,3},{3,2},{4,5},{5,4},{6,7},{7,6},{8,9},{9,8},{10,11... | collective-permute-start | bytes 786440 | tf_op jit(solution)/shard_map/ppermute | solution.py:24
  17.3 26.5 %collective-permute-start.3 = (f32[4,64,1024]{2,1,0:T(8,128)S(1)}, f32[4,64,1024]{2,1,0:T(8,128)S(1)}, u32[]{:S(2)}, u32[]{:S(2)}) collective-permute-start(f32[4,64,1024]{2,1,0:T(8,128)S(1)} %pad_maximum_fusion.refs_0_), channel_id=1, source_target_pairs={{0,18},{1,19},{2,16},{3,17},{4,22},{5,23},{6,20},{7,21},{8,26},{9,... | collective-permute-start | bytes 3145736 | tf_op jit(solution)/shard_map/ppermute | solution.py:24
  21.4 23.6 %collective-permute-start.4 = (f32[4,64,1024]{2,1,0:T(8,128)S(1)}, f32[4,64,1024]{2,1,0:T(8,128)S(1)}, u32[]{:S(2)}, u32[]{:S(2)}) collective-permute-start(f32[4,64,1024]{2,1,0:T(8,128)S(1)} %pad_maximum_fusion.refs_0_), channel_id=1, source_target_pairs={{0,4},{1,5},{2,6},{3,7},{4,0},{5,1},{6,2},{7,3},{8,12},{9,13},{10,... | collective-permute-start | bytes 3145736 | tf_op jit(solution)/shard_map/ppermute | solution.py:24
  23.3 24.5 %collective-permute-start.5 = (f32[4,64,1024]{2,1,0:T(8,128)S(1)}, f32[4,64,1024]{2,1,0:T(8,128)}, u32[]{:S(2)}, u32[]{:S(2)}) collective-permute-start(f32[4,64,1024]{2,1,0:T(8,128)S(1)} %pad_maximum_fusion.refs_0_), channel_id=1, source_target_pairs={{0,12},{1,13},{2,14},{3,15},{4,8},{5,9},{6,10},{7,11},{8,4},{9,5},... | collective-permute-start | bytes 3145736 | tf_op jit(solution)/shard_map/ppermute | solution.py:24
  43.8 8.8 %copy-start.8 = (f32[4,64,1024]{2,1,0:T(8,128)}, f32[4,64,1024]{2,1,0:T(8,128)S(1)}, u32[]{:S(2)}) copy-start(f32[4,64,1024]{2,1,0:T(8,128)S(1)} %collective-permute-done.3._.refs_0_) | copy-start | bytes 3145732
  45.0 1.0 copy-start.16
  47.8 23.1 %collective-permute-start.6 = (f32[4,64,1024]{2,1,0:T(8,128)S(1)}, f32[4,64,1024]{2,1,0:T(8,128)}, u32[]{:S(2)}, u32[]{:S(2)}) collective-permute-start(f32[4,64,1024]{2,1,0:T(8,128)S(1)} %collective-permute-done.3._.refs_0_), channel_id=1, source_target_pairs={{0,4},{1,5},{2,6},{3,7},{4,0},{5,1},{6,2},{7,3},{8,12},{9,13},{10,... | collective-permute-start | bytes 3145736 | tf_op jit(solution)/shard_map/ppermute | solution.py:24
  48.4 23.5 %collective-permute-start.7 = (f32[4,64,1024]{2,1,0:T(8,128)S(1)}, f32[4,64,1024]{2,1,0:T(8,128)S(1)}, u32[]{:S(2)}, u32[]{:S(2)}) collective-permute-start(f32[4,64,1024]{2,1,0:T(8,128)S(1)} %collective-permute-done.3._.refs_0_), channel_id=1, source_target_pairs={{0,12},{1,13},{2,14},{3,15},{4,8},{5,9},{6,10},{7,11},{8,4},{9,5},... | collective-permute-start | bytes 3145736 | tf_op jit(solution)/shard_map/ppermute | solution.py:24
  52.6 1.0 copy-start.10
  53.6 21.9 %collective-permute-start.8 = (f32[1024,256]{1,0:T(8,128)}, f32[1024,256]{1,0:T(8,128)S(1)}, u32[]{:S(2)}, u32[]{:S(2)}) collective-permute-start(f32[1024,256]{1,0:T(8,128)} %get-tuple-element.46), channel_id=1, source_target_pairs={{0,16},{1,17},{2,18},{3,19},{4,20},{5,21},{6,22},{7,23},{8,24},{9,... | collective-permute-start | bytes 3145736 | tf_op jit(solution)/shard_map/ppermute | solution.py:24
  54.1 22.4 %collective-permute-start.9 = (f32[1024,256]{1,0:T(8,128)}, f32[1024,256]{1,0:T(8,128)S(1)}, u32[]{:S(2)}, u32[]{:S(2)}) collective-permute-start(f32[1024,256]{1,0:T(8,128)} %get-tuple-element.47), channel_id=1, source_target_pairs={{0,1},{1,0},{2,3},{3,2},{4,5},{5,4},{6,7},{7,6},{8,9},{9,8},{10,11... | collective-permute-start | bytes 3145736 | tf_op jit(solution)/shard_map/ppermute | solution.py:24
  55.1 23.0 %collective-permute-start.10 = (f32[1024,256]{1,0:T(8,128)}, f32[1024,256]{1,0:T(8,128)}, u32[]{:S(2)}, u32[]{:S(2)}) collective-permute-start(f32[1024,256]{1,0:T(8,128)} %get-tuple-element.48), channel_id=1, source_target_pairs={{0,3},{1,2},{2,1},{3,0},{4,7},{5,6},{6,5},{7,4},{8,11},{9,10},{10,... | collective-permute-start | bytes 3145736 | tf_op jit(solution)/shard_map/ppermute | solution.py:24
  70.9 37.2 %collective-permute-start.19 = (f32[4,64,1024]{2,1,0:T(8,128)}, f32[4,64,1024]{2,1,0:T(8,128)}, u32[]{:S(2)}, u32[]{:S(2)}) collective-permute-start(f32[4,64,1024]{2,1,0:T(8,128)} %collective-permute-done.5.refs_1_), channel_id=1, source_target_pairs={{0,4},{1,5},{2,6},{3,7},{4,0},{5,1},{6,2},{7,3},{8,12},{9,13},{10,... | collective-permute-start | bytes 3145736 | tf_op jit(solution)/shard_map/ppermute | solution.py:24
  71.9 1.0 copy-start.18
  72.9 35.2 %collective-permute-start.20 = (f32[4,64,1024]{2,1,0:T(8,128)}, f32[4,64,1024]{2,1,0:T(8,128)}, u32[]{:S(2)}, u32[]{:S(2)}) collective-permute-start(f32[4,64,1024]{2,1,0:T(8,128)} %collective-permute-done.6.refs_2_), channel_id=1, source_target_pairs={{0,12},{1,13},{2,14},{3,15},{4,8},{5,9},{6,10},{7,11},{8,4},{9,5},... | collective-permute-start | bytes 3145736 | tf_op jit(solution)/shard_map/ppermute | solution.py:24
  75.5 1.0 copy-start.12
  76.6 1.0 copy-start.14
  78.1 1.2 copy-start.11
  79.3 1.2 copy-start.13
  80.6 1.2 copy-start.15
  81.8 2.1 %copy-start.17 = (f32[4,64,1024]{2,1,0:T(8,128)S(1)}, f32[4,64,1024]{2,1,0:T(8,128)}, u32[]{:S(2)}) copy-start(f32[4,64,1024]{2,1,0:T(8,128)} %copy-done.16) | copy-start | bytes 3145732
  83.8 7.8 %copy-start = (bf16[1024,1024]{1,0:T(8,128)(2,1)}, bf16[1024,1024]{1,0:T(8,128)(2,1)S(1)}, u32[]{:S(2)}) copy-start(bf16[1024,1024]{1,0:T(8,128)(2,1)S(1)} %get-tuple-element.50.refs_4_.refs_10_.refs_6_) | copy-start | bytes 6291460
  83.9 7.8 %copy-start.9 = (f32[4,64,1024]{2,1,0:T(8,128)S(1)}, f32[4,64,1024]{2,1,0:T(8,128)}, u32[]{:S(2)}) copy-start(f32[4,64,1024]{2,1,0:T(8,128)} %copy-done.8) | copy-start | bytes 3145732
  83.9 7.8 %copy-start.19 = (f32[4,64,1024]{2,1,0:T(8,128)S(1)}, f32[4,64,1024]{2,1,0:T(8,128)}, u32[]{:S(2)}) copy-start(f32[4,64,1024]{2,1,0:T(8,128)} %copy-done.18) | copy-start | bytes 3145732
  98.7 1.4 copy-start.2
  100.0 1.3 copy-start.5
  101.4 2.6 %collective-permute-start.12 = (f32[2,4,64,256]{3,2,1,0:T(8,128)S(1)}, f32[2,4,64,256]{3,2,1,0:T(8,128)S(1)}, u32[]{:S(2)}, u32[]{:S(2)}) collective-permute-start(f32[2,4,64,256]{3,2,1,0:T(8,128)S(1)} %get-tuple-element.59), channel_id=1, source_target_pairs={{0,32},{1,33},{2,34},{3,35},{4,36},{5,37},{6,38},{7,39},{8,40},{9,... | collective-permute-start | bytes 1572872 | tf_op jit(solution)/shard_map/ppermute | solution.py:24
  101.4 3.0 %collective-permute-start.13 = (f32[2,4,64,256]{3,2,1,0:T(8,128)}, f32[2,4,64,256]{3,2,1,0:T(8,128)}, u32[]{:S(2)}, u32[]{:S(2)}) collective-permute-start(f32[2,4,64,256]{3,2,1,0:T(8,128)} %get-tuple-element.60), channel_id=1, source_target_pairs={{0,32},{1,33},{2,34},{3,35},{4,36},{5,37},{6,38},{7,39},{8,40},{9,... | collective-permute-start | bytes 1572872 | tf_op jit(solution)/shard_map/ppermute | solution.py:24
  101.9 3.2 %collective-permute-start.14 = (f32[2,4,64,256]{3,2,1,0:T(8,128)}, f32[2,4,64,256]{3,2,1,0:T(8,128)}, u32[]{:S(2)}, u32[]{:S(2)}) collective-permute-start(f32[2,4,64,256]{3,2,1,0:T(8,128)} %get-tuple-element.61), channel_id=1, source_target_pairs={{0,32},{1,33},{2,34},{3,35},{4,36},{5,37},{6,38},{7,39},{8,40},{9,... | collective-permute-start | bytes 1572872 | tf_op jit(solution)/shard_map/ppermute | solution.py:24
  104.0 15.0 %collective-permute-start.11 = (f32[2,4,64,256]{3,2,1,0:T(8,128)}, f32[2,4,64,256]{3,2,1,0:T(8,128)S(1)}, u32[]{:S(2)}, u32[]{:S(2)}) collective-permute-start(f32[2,4,64,256]{3,2,1,0:T(8,128)} %get-tuple-element.58), channel_id=1, source_target_pairs={{0,32},{1,33},{2,34},{3,35},{4,36},{5,37},{6,38},{7,39},{8,40},{9,... | collective-permute-start | bytes 1572872 | tf_op jit(solution)/shard_map/ppermute | solution.py:24
  104.2 4.0 %copy-start.1 = (bf16[1024,1024]{1,0:T(8,128)(2,1)S(1)}, bf16[1024,1024]{1,0:T(8,128)(2,1)}, u32[]{:S(2)}) copy-start(bf16[1024,1024]{1,0:T(8,128)(2,1)} %copy-done) | copy-start | bytes 6291460
  105.2 1.6 %copy-start.3 = (f32[4,2,4,64,256]{4,3,2,1,0:T(8,128)S(1)}, f32[4,2,4,64,256]{4,3,2,1,0:T(8,128)}, u32[]{:S(2)}) copy-start(f32[4,2,4,64,256]{4,3,2,1,0:T(8,128)} %copy-done.2) | copy-start | bytes 6291460
  108.1 1.6 %copy-start.6 = (f32[4,2,4,64,256]{4,3,2,1,0:T(8,128)S(1)}, f32[4,2,4,64,256]{4,3,2,1,0:T(8,128)}, u32[]{:S(2)}) copy-start(f32[4,2,4,64,256]{4,3,2,1,0:T(8,128)} %copy-done.5) | copy-start | bytes 6291460
  115.4 19.5 %collective-permute-start.22 = (f32[3,4,64,256]{3,2,1,0:T(8,128)S(1)}, f32[3,4,64,256]{3,2,1,0:T(8,128)S(1)}, u32[]{:S(2)}, u32[]{:S(2)}) collective-permute-start(f32[3,4,64,256]{3,2,1,0:T(8,128)S(1)} %get-tuple-element.71), channel_id=1, source_target_pairs={{0,32},{1,33},{2,34},{3,35},{4,36},{5,37},{6,38},{7,39},{8,40},{9,... | collective-permute-start | bytes 2359304 | tf_op jit(solution)/shard_map/ppermute | solution.py:24
  115.7 14.2 %collective-permute-start.15 = (f32[2,4,64,256]{3,2,1,0:T(8,128)S(1)}, f32[2,4,64,256]{3,2,1,0:T(8,128)S(1)}, u32[]{:S(2)}, u32[]{:S(2)}) collective-permute-start(f32[2,4,64,256]{3,2,1,0:T(8,128)S(1)} %get-tuple-element.62.refs_2_), channel_id=1, source_target_pairs={{0,16},{1,17},{2,18},{3,19},{4,20},{5,21},{6,22},{7,23},{8,24},{9,... | collective-permute-start | bytes 1572872 | tf_op jit(solution)/shard_map/ppermute | solution.py:24
  117.2 14.2 %collective-permute-start.16 = (f32[2,4,64,256]{3,2,1,0:T(8,128)S(1)}, f32[2,4,64,256]{3,2,1,0:T(8,128)S(1)}, u32[]{:S(2)}, u32[]{:S(2)}) collective-permute-start(f32[2,4,64,256]{3,2,1,0:T(8,128)S(1)} %get-tuple-element.63.refs_3_), channel_id=1, source_target_pairs={{0,1},{1,0},{2,3},{3,2},{4,5},{5,4},{6,7},{7,6},{8,9},{9,8},{10,11... | collective-permute-start | bytes 1572872 | tf_op jit(solution)/shard_map/ppermute | solution.py:24
  117.2 15.1 %collective-permute-start.17 = (f32[2,4,64,256]{3,2,1,0:T(8,128)S(1)}, f32[2,4,64,256]{3,2,1,0:T(8,128)S(1)}, u32[]{:S(2)}, u32[]{:S(2)}) collective-permute-start(f32[2,4,64,256]{3,2,1,0:T(8,128)S(1)} %get-tuple-element.64.refs_4_), channel_id=1, source_target_pairs={{0,3},{1,2},{2,1},{3,0},{4,7},{5,6},{6,5},{7,4},{8,11},{9,10},{10,... | collective-permute-start | bytes 1572872 | tf_op jit(solution)/shard_map/ppermute | solution.py:24
  119.1 23.5 %collective-permute-start.21 = (f32[2,4,64,256]{3,2,1,0:T(8,128)S(1)}, f32[2,4,64,256]{3,2,1,0:T(8,128)S(1)}, u32[]{:S(2)}, u32[]{:S(2)}) collective-permute-start(f32[2,4,64,256]{3,2,1,0:T(8,128)S(1)} %get-tuple-element.69), channel_id=1, source_target_pairs={{0,32},{1,33},{2,34},{3,35},{4,36},{5,37},{6,38},{7,39},{8,40},{9,... | collective-permute-start | bytes 1572872 | tf_op jit(solution)/shard_map/ppermute | solution.py:24
  119.1 15.0 %copy-start.4 = (f32[4,2,4,64,256]{4,3,2,1,0:T(8,128)S(1)}, f32[4,2,4,64,256]{4,3,2,1,0:T(8,128)}, u32[]{:S(2)}) copy-start(f32[4,2,4,64,256]{4,3,2,1,0:T(8,128)} %copy-done.2) | copy-start | bytes 6291460
  129.9 8.0 %collective-permute-start.26 = (f32[4,64,256]{2,1,0:T(8,128)S(1)}, f32[4,64,256]{2,1,0:T(8,128)S(1)}, u32[]{:S(2)}, u32[]{:S(2)}) collective-permute-start(f32[4,64,256]{2,1,0:T(8,128)S(1)} %get-tuple-element.76), channel_id=1, source_target_pairs={{0,16},{1,17},{2,18},{3,19},{4,20},{5,21},{6,22},{7,23},{8,24},{9,... | collective-permute-start | bytes 786440 | tf_op jit(solution)/shard_map/ppermute | solution.py:24
  131.4 7.8 %collective-permute-start.27 = (f32[4,64,256]{2,1,0:T(8,128)S(1)}, f32[4,64,256]{2,1,0:T(8,128)S(1)}, u32[]{:S(2)}, u32[]{:S(2)}) collective-permute-start(f32[4,64,256]{2,1,0:T(8,128)S(1)} %get-tuple-element.77), channel_id=1, source_target_pairs={{0,1},{1,0},{2,3},{3,2},{4,5},{5,4},{6,7},{7,6},{8,9},{9,8},{10,11... | collective-permute-start | bytes 786440 | tf_op jit(solution)/shard_map/ppermute | solution.py:24
  132.3 8.7 %collective-permute-start.28 = (f32[4,64,256]{2,1,0:T(8,128)S(1)}, f32[4,64,256]{2,1,0:T(8,128)S(1)}, u32[]{:S(2)}, u32[]{:S(2)}) collective-permute-start(f32[4,64,256]{2,1,0:T(8,128)S(1)} %get-tuple-element.78), channel_id=1, source_target_pairs={{0,3},{1,2},{2,1},{3,0},{4,7},{5,6},{6,5},{7,4},{8,11},{9,10},{10,... | collective-permute-start | bytes 786440 | tf_op jit(solution)/shard_map/ppermute | solution.py:24
  134.9 12.0 %collective-permute-start.18 = (f32[4,64,256]{2,1,0:T(8,128)}, f32[4,64,256]{2,1,0:T(8,128)S(1)}, u32[]{:S(2)}, u32[]{:S(2)}) collective-permute-start(f32[4,64,256]{2,1,0:T(8,128)} %get-tuple-element.66), channel_id=1, source_target_pairs={{0,64},{1,65},{2,66},{3,67},{4,68},{5,69},{6,70},{7,71},{8,72},{9,... | collective-permute-start | bytes 786440 | tf_op jit(solution)/shard_map/ppermute | solution.py:24
  137.9 13.5 %collective-permute-start.23 = (f32[4,64,256]{2,1,0:T(8,128)S(1)}, f32[4,64,256]{2,1,0:T(8,128)S(1)}, u32[]{:S(2)}, u32[]{:S(2)}) collective-permute-start(f32[4,64,256]{2,1,0:T(8,128)S(1)} %get-tuple-element.72.rest_0_), channel_id=1, source_target_pairs={{0,16},{1,17},{2,18},{3,19},{4,20},{5,21},{6,22},{7,23},{8,24},{9,... | collective-permute-start | bytes 786440 | tf_op jit(solution)/shard_map/ppermute | solution.py:24
  139.1 12.3 %collective-permute-start.24 = (f32[4,64,256]{2,1,0:T(8,128)S(1)}, f32[4,64,256]{2,1,0:T(8,128)S(1)}, u32[]{:S(2)}, u32[]{:S(2)}) collective-permute-start(f32[4,64,256]{2,1,0:T(8,128)S(1)} %get-tuple-element.73.rest_1_), channel_id=1, source_target_pairs={{0,1},{1,0},{2,3},{3,2},{4,5},{5,4},{6,7},{7,6},{8,9},{9,8},{10,11... | collective-permute-start | bytes 786440 | tf_op jit(solution)/shard_map/ppermute | solution.py:24
  141.0 10.5 %collective-permute-start.25 = (f32[4,64,256]{2,1,0:T(8,128)S(1)}, f32[4,64,256]{2,1,0:T(8,128)}, u32[]{:S(2)}, u32[]{:S(2)}) collective-permute-start(f32[4,64,256]{2,1,0:T(8,128)S(1)} %get-tuple-element.74.rest_2_), channel_id=1, source_target_pairs={{0,3},{1,2},{2,1},{3,0},{4,7},{5,6},{6,5},{7,4},{8,11},{9,10},{10,... | collective-permute-start | bytes 786440 | tf_op jit(solution)/shard_map/ppermute | solution.py:24
  142.7 14.0 %collective-permute-start.29 = (f32[4,64,256]{2,1,0:T(8,128)S(1)}, f32[4,64,256]{2,1,0:T(8,128)S(1)}, u32[]{:S(2)}, u32[]{:S(2)}) collective-permute-start(f32[4,64,256]{2,1,0:T(8,128)S(1)} %shard_map.37), channel_id=1, source_target_pairs={{0,64},{1,65},{2,66},{3,67},{4,68},{5,69},{6,70},{7,71},{8,72},{9,... | collective-permute-start | bytes 786440 | tf_op jit(solution)/shard_map/ppermute | solution.py:24

commit v14 on v12

--- a/solution.py
+++ b/solution.py
@@ -44,16 +44,18 @@
 
 
 def call(kernel, scalars, values, in_specs, out_shape, out_specs, scratch=(), aliases=None):
+    scalars = scalars if isinstance(scalars, tuple) else (scalars,)
+    aliases = {at + len(scalars) - 1: out for at, out in (aliases or {}).items()}
     return pl.pallas_call(
         kernel,
         grid_spec=pltpu.PrefetchScalarGridSpec(
-            num_scalar_prefetch=1, grid=(1,), in_specs=in_specs, out_specs=out_specs, scratch_shapes=scratch
+            num_scalar_prefetch=len(scalars), grid=(1,), in_specs=in_specs, out_specs=out_specs, scratch_shapes=scratch
         ),
         out_shape=out_shape,
-        input_output_aliases=aliases or {},
+        input_output_aliases=aliases,
         compiler_params=PARAMS,
         cost_estimate=SHORT,
-    )(scalars, *values)
+    )(*scalars, *values)
 
 
 def cut_kernel(quarter, value, _, *rest):
@@ -165,10 +167,10 @@
     rows, depth = arrays[0].shape[1:]
     columns = rights[0].shape[1] // 4
 
-    def kernel(flags, *refs):
+    def kernel(swap, at_core, *refs):
         blocks, rest = refs[: len(arrays)], refs[len(arrays) + len(after):]
         high, low, ahead, keep, give, both, left_high, left_low = rest
-        swapped, core = flags[0] == 1, flags[1]
+        swapped, core = swap[0] == 1, at_core[0]
 
         def store(d, total):
             for part in range(2):
@@ -231,13 +233,13 @@
     )
 
 
-def join_kernel(place, one, other_one, keep, got, across, two, three, other_two, out):
-    part = place[2]
+def join_kernel(plane, first, side, one, other_one, keep, got, across, two, three, other_two, out):
+    part = side[0]
     for block in range(4):
-        line = place[1] ^ block
-        out[place[0], line] = one[block] + other_one[block]
+        line = first[0] ^ block
+        out[plane[0], line] = one[block] + other_one[block]
         near = across[block] + (two[block] + three[block])
-        out[1 - place[0], line] = (keep[0, part, block] + got[part, block]) + (near + other_two[block])
+        out[1 - plane[0], line] = (keep[0, part, block] + got[part, block]) + (near + other_two[block])
 
 
 def join(place, values):
@@ -261,12 +263,13 @@
     mine = jnp.stack([block(0), send(block(1), dy=1), send(block(3), dy=2), send(block(2), dy=3)])
     other = send(mine, dx=1, dy=2)
     own_one, own_three = send(mine, dz=1), send(mine, dz=3)
+    far, *_ = lax.optimization_barrier((other, own_one, own_three))
+    far_one, far_three = lax.optimization_barrier((send(far, dz=1), send(far, dz=3)))
+
+    own_two, far_two = send(own_three, dz=1), send(far_one, dz=3)
+
+    right = pltpu.with_memory_space_constraint(right, pltpu.HBM)
     pieces = cut_after(quarter.reshape(1), right, other)
-    far, *_ = lax.optimization_barrier((other, own_one, own_three, *pieces))
-    far_one, far_three = lax.optimization_barrier((send(far, dz=1), send(far, dz=3)))
-
-    own_two, far_two = send(own_three, dz=1), send(far_one, dz=3)
-
     pieces = [pieces[0]] + [send(pieces[d], **NEAR[d]) for d in range(1, 4)]
     rights = split(swap, pieces)
 
@@ -277,7 +280,7 @@
     got = [send(give, core=1) for give in gives]
     sums = added(swap, keep, got[1:])
     late_keep, late_give, both = late_products(
-        jnp.stack([swap[0], core]), ((own_two,), (far_two,)), third, rights, sums
+        (swap, core.reshape(1)), ((own_two,), (far_two,)), third, rights, sums
     )
     both = lax.all_to_all(both, AXES, 0, 0, tiled=True, axis_index_groups=CORES)
 
@@ -290,7 +293,7 @@
     passed = send(onward(side, late_keep, late_got, passed), dhi=1)
     kept = [send(kept[d - 1], **NEAR[d]) for d in range(1, 4)]
 
-    place = jnp.stack([(z & 1) ^ swap[0], y ^ (2 * side[0]), side[0]])
+    place = ((z & 1) ^ swap[0]).reshape(1), (y ^ (2 * side[0])).reshape(1), side
     total = join(place, (*early_ends, late_keep, late_got, *kept, passed))
     return total.reshape(8 * rows, columns)
 

time: 147 us -> 240 us (1.63)
  Pallas kernels: 30.1 us -> 124 us
  waiting for transfers between devices: 63 us -> 66.4 us
  starting transfers between devices: 40.4 us -> 37.1 us
    pallas_call x10, Pallas kernels: 30.1 us -> 124 us  [call(): pl.pallas_call(kernel, grid_spec=pltpu.PrefetchScalarGridSpec(num_scalar_...]
    ppermute x29, waiting for transfers between devices: 63 us -> 66.4 us  [send(): return lax.ppermute(value, AXES, pairs)]
    ppermute x29, starting transfers between devices: 40.4 us -> 37.1 us  [send(): return lax.ppermute(value, AXES, pairs)]
  transfers between devices with their start and end apart: 29 -> 29, of which waited for: 15 -> 15; matrix products, arithmetic and copies ran while one was open for 0% -> 0% of each run, Pallas kernels for 20% -> 51%
where the time goes in v14:
time: 240 us
  Pallas kernels  124 us (52%)
  waiting for transfers between devices  66.4 us (28%)
  starting transfers between devices  37.1 us (15%)
  blocking collectives  7.55 us (3%)
  local copies, waits for them, and re-layouts  4.92 us (2%)
    pallas_call x10, Pallas kernels, call(): pl.pallas_call(kernel, grid_spec=pltpu.PrefetchScalarGridSpec(num_scalar_...  124 us
    ppermute x29, waiting for transfers between devices, send(): return lax.ppermute(value, AXES, pairs)  66.4 us
    ppermute x29, starting transfers between devices, send(): return lax.ppermute(value, AXES, pairs)  37.1 us
    all_to_all x1, blocking collectives, per_device(): both = lax.all_to_all(both, AXES, 0, 0, tiled=True, axis_index_groups=CORES)  7.55 us
  transfers between devices with their start and end apart: 29, of which 15 were waited for; matrix products, arithmetic and copies ran while one was open for 0% of the time, Pallas kernels for 51%

profile of v14, /device:TPU:0, one launch (start us, length us, event | category | flops | bytes accessed | tf_op | source)
XLA Modules:
  0.0 239.7 jit_solution(16527036269228166723)
XLA Ops:
  0.0 1.3 dynamic-slice_bitcast_fusion
  1.3 3.2 %collective-permute-start.2 = (f32[64,1024]{1,0:T(8,128)S(1)}, f32[64,1024]{1,0:T(8,128)S(1)}, u32[]{:S(2)}, u32[]{:S(2)}) collective-permute-start(f32[64,1024]{1,0:T(8,128)S(1)} %get-tuple-element.77), channel_id=1, source_target_pairs={{0,3},{1,2},{2,1},{3,0},{4,7},{5,6},{6,5},{7,4},{8,11},{9,10},{10,... | collective-permute-start | bytes 786440 | tf_op jit(solution)/shard_map/ppermute | solution.py:24
  4.5 0.6 collective-permute-start.1
  5.1 0.4 collective-permute-start
  5.5 10.9 %collective-permute-done.2 = f32[64,1024]{1,0:T(8,128)S(1)} collective-permute-done((f32[64,1024]{1,0:T(8,128)S(1)}, f32[64,1024]{1,0:T(8,128)S(1)}, u32[]{:S(2)}, u32[]{:S(2)}) %collective-permute-start.2) | collective-permute-done | bytes 262176 | tf_op jit(solution)/shard_map/ppermute | solution.py:24
  16.4 0.7 collective-permute-done
  17.1 0.1 pad_maximum_fusion.refs_0_
  17.2 4.0 %collective-permute-start.3 = (f32[4,64,1024]{2,1,0:T(8,128)S(1)}, f32[4,64,1024]{2,1,0:T(8,128)S(1)}, u32[]{:S(2)}, u32[]{:S(2)}) collective-permute-start(f32[4,64,1024]{2,1,0:T(8,128)S(1)} %pad_maximum_fusion.refs_0_), channel_id=1, source_target_pairs={{0,18},{1,19},{2,16},{3,17},{4,22},{5,23},{6,20},{7,21},{8,26},{9,... | collective-permute-start | bytes 3145736 | tf_op jit(solution)/shard_map/ppermute | solution.py:24
  21.2 1.9 collective-permute-start.4
  23.2 2.5 %collective-permute-start.5 = (f32[4,64,1024]{2,1,0:T(8,128)S(1)}, f32[4,64,1024]{2,1,0:T(8,128)}, u32[]{:S(2)}, u32[]{:S(2)}) collective-permute-start(f32[4,64,1024]{2,1,0:T(8,128)S(1)} %pad_maximum_fusion.refs_0_), channel_id=1, source_target_pairs={{0,12},{1,13},{2,14},{3,15},{4,8},{5,9},{6,10},{7,11},{8,4},{9,5},... | collective-permute-start | bytes 3145736 | tf_op jit(solution)/shard_map/ppermute | solution.py:24
  25.7 18.0 %collective-permute-done.3._.refs_0_ = f32[4,64,1024]{2,1,0:T(8,128)S(1)} collective-permute-done((f32[4,64,1024]{2,1,0:T(8,128)S(1)}, f32[4,64,1024]{2,1,0:T(8,128)S(1)}, u32[]{:S(2)}, u32[]{:S(2)}) %collective-permute-start.3) | collective-permute-done | bytes 1048608 | tf_op jit(solution)/shard_map/ppermute | solution.py:24
  43.7 1.2 collective-permute-done.4.refs_2_
  44.9 1.0 copy-done.3
  45.9 1.8 collective-permute-done.5.refs_1_
  47.7 0.6 collective-permute-start.6
  48.2 2.3 collective-permute-start.7
  50.6 96.4 %shard_map.28 = (f32[1024,256]{1,0:T(8,128)S(1)}, f32[1024,256]{1,0:T(8,128)}, f32[1024,256]{1,0:T(8,128)}, f32[1024,256]{1,0:T(8,128)}) custom-call(s32[1]{0:T(128)} %bitcast.8.quarter, f32[4096,256]{1,0:T(8,128)} %value.1, f32[4,64,1024]{2,1,0:T(8,128)S(1)} %collective-permute-done.3._.refs_0_), custom_call_target="tpu_custom_call" | custom-call | flops 1 | bytes 1 | tf_op jit(solution)/shard_map/pallas_call | solution.py:49
  147.0 0.6 collective-permute-start.8
  147.7 1.0 collective-permute-start.9
  148.6 1.9 collective-permute-start.10
  150.5 0.0 collective-permute-done.6.refs_2_
  150.5 1.0 collective-permute-start.19
  151.5 0.0 collective-permute-done.7.refs_1_
  151.5 1.0 copy-done.5
  152.5 0.6 collective-permute-start.20
  153.1 15.9 %collective-permute-done.8.refs_1_ = f32[1024,256]{1,0:T(8,128)S(1)} collective-permute-done((f32[1024,256]{1,0:T(8,128)}, f32[1024,256]{1,0:T(8,128)S(1)}, u32[]{:S(2)}, u32[]{:S(2)}) %collective-permute-start.8) | collective-permute-done | bytes 1048608 | tf_op jit(solution)/shard_map/ppermute | solution.py:24
  169.0 0.5 collective-permute-done.9.refs_2_
  169.6 2.1 collective-permute-done.10.refs_3_
  171.6 2.3 shard_map.29
  174.0 7.1 %shard_map.30 = (f32[4,2,4,64,256]{4,3,2,1,0:T(8,128)S(1)}, f32[4,2,4,64,256]{4,3,2,1,0:T(8,128)S(1)}, f32[2,4,64,256]{3,2,1,0:T(8,128)}, f32[2,4,64,256]{3,2,1,...) custom-call(s32[1]{0:T(128)} %bitcast.3._.swap, ...), custom_call_target="tpu_custom_call" | custom-call | flops 1 | bytes 1 | tf_op jit(solution)/shard_map/pallas_call | solution.py:49
  181.1 6.9 %shard_map.31 = (f32[4,2,4,64,256]{4,3,2,1,0:T(8,128)S(1)}, f32[4,2,4,64,256]{4,3,2,1,0:T(8,128)S(1)}, f32[2,4,64,256]{3,2,1,0:T(8,128)}, f32[2,4,64,256]{3,2,1,...) custom-call(s32[1]{0:T(128)} %bitcast.3._.swap, ...), custom_call_target="tpu_custom_call", output_to_operand_aliasing={{0}: (4, {}), {1}: (5, {}), {2}: (6, {}), {3}: (7, {}), {4}... | custom-call | flops 1 | bytes 1 | tf_op jit(solution)/shard_map/pallas_call | solution.py:49
  188.0 0.5 collective-permute-start.13
  188.5 0.0 collective-permute-start.14
  188.5 1.4 collective-permute-done.12.refs_0_
  189.9 0.1 collective-permute-start.11
  190.0 0.6 collective-permute-done.13.refs_1_
  190.7 0.7 collective-permute-done.14.refs_2_
  191.4 1.4 shard_map.32
  192.8 1.5 collective-permute-start.15
  194.3 0.0 collective-permute-start.16
  194.3 0.0 collective-permute-done.19.refs_0_
  194.3 1.9 collective-permute-start.17
  196.1 0.0 collective-permute-done.20.refs_1_
  196.2 5.1 %shard_map.34 = (f32[1,2,4,64,256]{4,3,2,1,0:T(8,128)S(1)}, f32[2,4,64,256]{3,2,1,0:T(8,128)}, f32[2,3,2,4,64,256]{5,4,3,2,1,0:T(8,128)S(1)}) custom-call(s32[1]{0:T(128)} %bitcast.3._.swap, s32[1]{0:T(128)} %bitcast.9.at_core, f32[4,64,1024]{2,1,0:T(8,128)} %collective-permute-done.19.refs_0_, f32[4,64,1024]{2,1,0:T(8,128)} %collective-permute-done.20.refs_1_, ...), custom_call_target="tpu_custom_call" | custom-call | flops 1 | bytes 1 | tf_op jit(solution)/shard_map/pallas_call | solution.py:49
  201.2 1.6 copy-done.2
  202.9 7.6 %all_to_all.5.both = f32[2,3,2,4,64,256]{5,4,3,2,1,0:T(8,128)S(1)} all-to-all(f32[2,3,2,4,64,256]{5,4,3,2,1,0:T(8,128)} %copy-done.2), channel_id=1, replica_groups={{0,32},{1,33},{2,34},{3,35},{4,36},{5,37},{6,38},{7,39},{8,40},{9,41},{..., dimensions={0} | all-to-all | bytes 6291456 | tf_op jit(solution)/shard_map/all_to_all | solution.py:285
  210.4 1.0 shard_map.35
  211.4 1.5 collective-permute-start.25
  212.9 0.0 collective-permute-done.15.refs_0_
  212.9 0.9 collective-permute-start.26
  213.8 1.0 collective-permute-start.27
  214.8 0.0 collective-permute-done.17.refs_2_
  214.8 2.3 shard_map.33
  217.1 3.0 %collective-permute-start.18 = (f32[4,64,256]{2,1,0:T(8,128)}, f32[4,64,256]{2,1,0:T(8,128)S(1)}, u32[]{:S(2)}, u32[]{:S(2)}) collective-permute-start(f32[4,64,256]{2,1,0:T(8,128)} %get-tuple-element.64), channel_id=1, source_target_pairs={{0,64},{1,65},{2,66},{3,67},{4,68},{5,69},{6,70},{7,71},{8,72},{9,... | collective-permute-start | bytes 786440 | tf_op jit(solution)/shard_map/ppermute | solution.py:24
  220.1 1.1 collective-permute-start.22
  221.3 0.9 collective-permute-start.23
  222.1 0.7 collective-permute-done.27.three
  222.8 1.0 collective-permute-start.24
  223.8 0.1 shard_map.36
  223.9 3.1 %collective-permute-start.28 = (f32[4,64,256]{2,1,0:T(8,128)S(1)}, f32[4,64,256]{2,1,0:T(8,128)S(1)}, u32[]{:S(2)}, u32[]{:S(2)}) collective-permute-start(f32[4,64,256]{2,1,0:T(8,128)S(1)} %shard_map.36), channel_id=1, source_target_pairs={{0,64},{1,65},{2,66},{3,67},{4,68},{5,69},{6,70},{7,71},{8,72},{9,... | collective-permute-start | bytes 786440 | tf_op jit(solution)/shard_map/ppermute | solution.py:24
  227.0 1.4 collective-permute-done.18.other_one
  228.4 5.4 %collective-permute-done.22.across = f32[4,64,256]{2,1,0:T(8,128)S(1)} collective-permute-done((f32[4,64,256]{2,1,0:T(8,128)}, f32[4,64,256]{2,1,0:T(8,128)S(1)}, u32[]{:S(2)}, u32[]{:S(2)}) %collective-permute-start.22) | collective-permute-done | bytes 262176 | tf_op jit(solution)/shard_map/ppermute | solution.py:24
  233.8 5.0 %collective-permute-done.28.other_two = f32[4,64,256]{2,1,0:T(8,128)S(1)} collective-permute-done((f32[4,64,256]{2,1,0:T(8,128)S(1)}, f32[4,64,256]{2,1,0:T(8,128)S(1)}, u32[]{:S(2)}, u32[]{:S(2)}) %collective-permute-start.28) | collective-permute-done | bytes 262176 | tf_op jit(solution)/shard_map/ppermute | solution.py:24
  238.8 0.9 shard_map.37
  (21 shorter events, 0.0 us)
Async XLA Ops:
  1.3 15.1 %collective-permute-start.2 = (f32[64,1024]{1,0:T(8,128)S(1)}, f32[64,1024]{1,0:T(8,128)S(1)}, u32[]{:S(2)}, u32[]{:S(2)}) collective-permute-start(f32[64,1024]{1,0:T(8,128)S(1)} %get-tuple-element.77), channel_id=1, source_target_pairs={{0,3},{1,2},{2,1},{3,0},{4,7},{5,6},{6,5},{7,4},{8,11},{9,10},{10,... | collective-permute-start | bytes 786440 | tf_op jit(solution)/shard_map/ppermute | solution.py:24
  4.5 11.9 %collective-permute-start.1 = (f32[64,1024]{1,0:T(8,128)S(1)}, f32[64,1024]{1,0:T(8,128)S(1)}, u32[]{:S(2)}, u32[]{:S(2)}) collective-permute-start(f32[64,1024]{1,0:T(8,128)S(1)} %get-tuple-element.78), channel_id=1, source_target_pairs={{0,2},{1,3},{2,0},{3,1},{4,6},{5,7},{6,4},{7,5},{8,10},{9,11},{10,... | collective-permute-start | bytes 786440 | tf_op jit(solution)/shard_map/ppermute | solution.py:24
  5.1 12.0 %collective-permute-start = (f32[64,1024]{1,0:T(8,128)S(1)}, f32[64,1024]{1,0:T(8,128)S(1)}, u32[]{:S(2)}, u32[]{:S(2)}) collective-permute-start(f32[64,1024]{1,0:T(8,128)S(1)} %get-tuple-element.76), channel_id=1, source_target_pairs={{0,1},{1,0},{2,3},{3,2},{4,5},{5,4},{6,7},{7,6},{8,9},{9,8},{10,11... | collective-permute-start | bytes 786440 | tf_op jit(solution)/shard_map/ppermute | solution.py:24
  17.2 26.5 %collective-permute-start.3 = (f32[4,64,1024]{2,1,0:T(8,128)S(1)}, f32[4,64,1024]{2,1,0:T(8,128)S(1)}, u32[]{:S(2)}, u32[]{:S(2)}) collective-permute-start(f32[4,64,1024]{2,1,0:T(8,128)S(1)} %pad_maximum_fusion.refs_0_), channel_id=1, source_target_pairs={{0,18},{1,19},{2,16},{3,17},{4,22},{5,23},{6,20},{7,21},{8,26},{9,... | collective-permute-start | bytes 3145736 | tf_op jit(solution)/shard_map/ppermute | solution.py:24
  21.2 23.6 %collective-permute-start.4 = (f32[4,64,1024]{2,1,0:T(8,128)S(1)}, f32[4,64,1024]{2,1,0:T(8,128)S(1)}, u32[]{:S(2)}, u32[]{:S(2)}) collective-permute-start(f32[4,64,1024]{2,1,0:T(8,128)S(1)} %pad_maximum_fusion.refs_0_), channel_id=1, source_target_pairs={{0,4},{1,5},{2,6},{3,7},{4,0},{5,1},{6,2},{7,3},{8,12},{9,13},{10,... | collective-permute-start | bytes 3145736 | tf_op jit(solution)/shard_map/ppermute | solution.py:24
  23.2 24.5 %collective-permute-start.5 = (f32[4,64,1024]{2,1,0:T(8,128)S(1)}, f32[4,64,1024]{2,1,0:T(8,128)}, u32[]{:S(2)}, u32[]{:S(2)}) collective-permute-start(f32[4,64,1024]{2,1,0:T(8,128)S(1)} %pad_maximum_fusion.refs_0_), channel_id=1, source_target_pairs={{0,12},{1,13},{2,14},{3,15},{4,8},{5,9},{6,10},{7,11},{8,4},{9,5},... | collective-permute-start | bytes 3145736 | tf_op jit(solution)/shard_map/ppermute | solution.py:24
  43.7 103.4 %copy-start = (f32[4,64,1024]{2,1,0:T(8,128)}, f32[4,64,1024]{2,1,0:T(8,128)S(1)}, u32[]{:S(2)}) copy-start(f32[4,64,1024]{2,1,0:T(8,128)S(1)} %collective-permute-done.3._.refs_0_) | copy-start | bytes 3145732
  44.9 1.0 copy-start.3
  47.7 102.9 %collective-permute-start.6 = (f32[4,64,1024]{2,1,0:T(8,128)S(1)}, f32[4,64,1024]{2,1,0:T(8,128)}, u32[]{:S(2)}, u32[]{:S(2)}) collective-permute-start(f32[4,64,1024]{2,1,0:T(8,128)S(1)} %collective-permute-done.3._.refs_0_), channel_id=1, source_target_pairs={{0,4},{1,5},{2,6},{3,7},{4,0},{5,1},{6,2},{7,3},{8,12},{9,13},{10,... | collective-permute-start | bytes 3145736 | tf_op jit(solution)/shard_map/ppermute | solution.py:24
  48.2 103.3 %collective-permute-start.7 = (f32[4,64,1024]{2,1,0:T(8,128)S(1)}, f32[4,64,1024]{2,1,0:T(8,128)S(1)}, u32[]{:S(2)}, u32[]{:S(2)}) collective-permute-start(f32[4,64,1024]{2,1,0:T(8,128)S(1)} %collective-permute-done.3._.refs_0_), channel_id=1, source_target_pairs={{0,12},{1,13},{2,14},{3,15},{4,8},{5,9},{6,10},{7,11},{8,4},{9,5},... | collective-permute-start | bytes 3145736 | tf_op jit(solution)/shard_map/ppermute | solution.py:24
  147.0 22.0 %collective-permute-start.8 = (f32[1024,256]{1,0:T(8,128)}, f32[1024,256]{1,0:T(8,128)S(1)}, u32[]{:S(2)}, u32[]{:S(2)}) collective-permute-start(f32[1024,256]{1,0:T(8,128)} %get-tuple-element.44), channel_id=1, source_target_pairs={{0,16},{1,17},{2,18},{3,19},{4,20},{5,21},{6,22},{7,23},{8,24},{9,... | collective-permute-start | bytes 3145736 | tf_op jit(solution)/shard_map/ppermute | solution.py:24
  147.7 21.9 %collective-permute-start.9 = (f32[1024,256]{1,0:T(8,128)}, f32[1024,256]{1,0:T(8,128)}, u32[]{:S(2)}, u32[]{:S(2)}) collective-permute-start(f32[1024,256]{1,0:T(8,128)} %get-tuple-element.45), channel_id=1, source_target_pairs={{0,1},{1,0},{2,3},{3,2},{4,5},{5,4},{6,7},{7,6},{8,9},{9,8},{10,11... | collective-permute-start | bytes 3145736 | tf_op jit(solution)/shard_map/ppermute | solution.py:24
  148.6 23.0 %collective-permute-start.10 = (f32[1024,256]{1,0:T(8,128)}, f32[1024,256]{1,0:T(8,128)}, u32[]{:S(2)}, u32[]{:S(2)}) collective-permute-start(f32[1024,256]{1,0:T(8,128)} %get-tuple-element.46), channel_id=1, source_target_pairs={{0,3},{1,2},{2,1},{3,0},{4,7},{5,6},{6,5},{7,4},{8,11},{9,10},{10,... | collective-permute-start | bytes 3145736 | tf_op jit(solution)/shard_map/ppermute | solution.py:24
  150.5 43.8 %collective-permute-start.19 = (f32[4,64,1024]{2,1,0:T(8,128)}, f32[4,64,1024]{2,1,0:T(8,128)}, u32[]{:S(2)}, u32[]{:S(2)}) collective-permute-start(f32[4,64,1024]{2,1,0:T(8,128)} %collective-permute-done.5.refs_1_), channel_id=1, source_target_pairs={{0,4},{1,5},{2,6},{3,7},{4,0},{5,1},{6,2},{7,3},{8,12},{9,13},{10,... | collective-permute-start | bytes 3145736 | tf_op jit(solution)/shard_map/ppermute | solution.py:24
  151.5 1.0 copy-start.5
  152.5 43.6 %collective-permute-start.20 = (f32[4,64,1024]{2,1,0:T(8,128)}, f32[4,64,1024]{2,1,0:T(8,128)}, u32[]{:S(2)}, u32[]{:S(2)}) collective-permute-start(f32[4,64,1024]{2,1,0:T(8,128)} %collective-permute-done.6.refs_2_), channel_id=1, source_target_pairs={{0,12},{1,13},{2,14},{3,15},{4,8},{5,9},{6,10},{7,11},{8,4},{9,5},... | collective-permute-start | bytes 3145736 | tf_op jit(solution)/shard_map/ppermute | solution.py:24
  171.6 2.3 copy-start.4
  174.0 7.1 %copy-start.1 = (f32[4,64,1024]{2,1,0:T(8,128)S(1)}, f32[4,64,1024]{2,1,0:T(8,128)}, u32[]{:S(2)}) copy-start(f32[4,64,1024]{2,1,0:T(8,128)} %copy-done) | copy-start | bytes 3145732
  174.0 7.1 %copy-start.6 = (f32[4,64,1024]{2,1,0:T(8,128)S(1)}, f32[4,64,1024]{2,1,0:T(8,128)}, u32[]{:S(2)}) copy-start(f32[4,64,1024]{2,1,0:T(8,128)} %copy-done.5) | copy-start | bytes 3145732
  188.0 1.9 collective-permute-start.12
  188.0 2.7 %collective-permute-start.13 = (f32[2,4,64,256]{3,2,1,0:T(8,128)S(1)}, f32[2,4,64,256]{3,2,1,0:T(8,128)S(1)}, u32[]{:S(2)}, u32[]{:S(2)}) collective-permute-start(f32[2,4,64,256]{3,2,1,0:T(8,128)S(1)} %get-tuple-element.58), channel_id=1, source_target_pairs={{0,32},{1,33},{2,34},{3,35},{4,36},{5,37},{6,38},{7,39},{8,40},{9,... | collective-permute-start | bytes 1572872 | tf_op jit(solution)/shard_map/ppermute | solution.py:24
  188.5 2.9 %collective-permute-start.14 = (f32[2,4,64,256]{3,2,1,0:T(8,128)S(1)}, f32[2,4,64,256]{3,2,1,0:T(8,128)S(1)}, u32[]{:S(2)}, u32[]{:S(2)}) collective-permute-start(f32[2,4,64,256]{3,2,1,0:T(8,128)S(1)} %get-tuple-element.59), channel_id=1, source_target_pairs={{0,32},{1,33},{2,34},{3,35},{4,36},{5,37},{6,38},{7,39},{8,40},{9,... | collective-permute-start | bytes 1572872 | tf_op jit(solution)/shard_map/ppermute | solution.py:24
  189.9 21.5 %collective-permute-start.11 = (f32[2,4,64,256]{3,2,1,0:T(8,128)}, f32[2,4,64,256]{3,2,1,0:T(8,128)}, u32[]{:S(2)}, u32[]{:S(2)}) collective-permute-start(f32[2,4,64,256]{3,2,1,0:T(8,128)} %get-tuple-element.56), channel_id=1, source_target_pairs={{0,32},{1,33},{2,34},{3,35},{4,36},{5,37},{6,38},{7,39},{8,40},{9,... | collective-permute-start | bytes 1572872 | tf_op jit(solution)/shard_map/ppermute | solution.py:24
  192.8 20.1 %collective-permute-start.15 = (f32[2,4,64,256]{3,2,1,0:T(8,128)}, f32[2,4,64,256]{3,2,1,0:T(8,128)}, u32[]{:S(2)}, u32[]{:S(2)}) collective-permute-start(f32[2,4,64,256]{3,2,1,0:T(8,128)} %get-tuple-element.60.refs_2_), channel_id=1, source_target_pairs={{0,16},{1,17},{2,18},{3,19},{4,20},{5,21},{6,22},{7,23},{8,24},{9,... | collective-permute-start | bytes 1572872 | tf_op jit(solution)/shard_map/ppermute | solution.py:24
  194.3 19.5 %collective-permute-start.16 = (f32[2,4,64,256]{3,2,1,0:T(8,128)}, f32[2,4,64,256]{3,2,1,0:T(8,128)}, u32[]{:S(2)}, u32[]{:S(2)}) collective-permute-start(f32[2,4,64,256]{3,2,1,0:T(8,128)} %get-tuple-element.61.refs_3_), channel_id=1, source_target_pairs={{0,1},{1,0},{2,3},{3,2},{4,5},{5,4},{6,7},{7,6},{8,9},{9,8},{10,11... | collective-permute-start | bytes 1572872 | tf_op jit(solution)/shard_map/ppermute | solution.py:24
  194.3 20.5 %collective-permute-start.17 = (f32[2,4,64,256]{3,2,1,0:T(8,128)}, f32[2,4,64,256]{3,2,1,0:T(8,128)}, u32[]{:S(2)}, u32[]{:S(2)}) collective-permute-start(f32[2,4,64,256]{3,2,1,0:T(8,128)} %get-tuple-element.62.refs_4_), channel_id=1, source_target_pairs={{0,3},{1,2},{2,1},{3,0},{4,7},{5,6},{6,5},{7,4},{8,11},{9,10},{10,... | collective-permute-start | bytes 1572872 | tf_op jit(solution)/shard_map/ppermute | solution.py:24
  201.2 1.6 copy-start.2
  202.9 20.9 %collective-permute-start.21 = (f32[2,4,64,256]{3,2,1,0:T(8,128)}, f32[2,4,64,256]{3,2,1,0:T(8,128)S(1)}, u32[]{:S(2)}, u32[]{:S(2)}) collective-permute-start(f32[2,4,64,256]{3,2,1,0:T(8,128)} %get-tuple-element.67), channel_id=1, source_target_pairs={{0,32},{1,33},{2,34},{3,35},{4,36},{5,37},{6,38},{7,39},{8,40},{9,... | collective-permute-start | bytes 1572872 | tf_op jit(solution)/shard_map/ppermute | solution.py:24
  211.4 8.7 %collective-permute-start.25 = (f32[4,64,256]{2,1,0:T(8,128)S(1)}, f32[4,64,256]{2,1,0:T(8,128)S(1)}, u32[]{:S(2)}, u32[]{:S(2)}) collective-permute-start(f32[4,64,256]{2,1,0:T(8,128)S(1)} %get-tuple-element.72), channel_id=1, source_target_pairs={{0,16},{1,17},{2,18},{3,19},{4,20},{5,21},{6,22},{7,23},{8,24},{9,... | collective-permute-start | bytes 786440 | tf_op jit(solution)/shard_map/ppermute | solution.py:24
  212.9 8.3 %collective-permute-start.26 = (f32[4,64,256]{2,1,0:T(8,128)S(1)}, f32[4,64,256]{2,1,0:T(8,128)S(1)}, u32[]{:S(2)}, u32[]{:S(2)}) collective-permute-start(f32[4,64,256]{2,1,0:T(8,128)S(1)} %get-tuple-element.73), channel_id=1, source_target_pairs={{0,1},{1,0},{2,3},{3,2},{4,5},{5,4},{6,7},{7,6},{8,9},{9,8},{10,11... | collective-permute-start | bytes 786440 | tf_op jit(solution)/shard_map/ppermute | solution.py:24
  213.8 9.0 %collective-permute-start.27 = (f32[4,64,256]{2,1,0:T(8,128)S(1)}, f32[4,64,256]{2,1,0:T(8,128)S(1)}, u32[]{:S(2)}, u32[]{:S(2)}) collective-permute-start(f32[4,64,256]{2,1,0:T(8,128)S(1)} %get-tuple-element.74), channel_id=1, source_target_pairs={{0,3},{1,2},{2,1},{3,0},{4,7},{5,6},{6,5},{7,4},{8,11},{9,10},{10,... | collective-permute-start | bytes 786440 | tf_op jit(solution)/shard_map/ppermute | solution.py:24
  217.1 11.3 %collective-permute-start.18 = (f32[4,64,256]{2,1,0:T(8,128)}, f32[4,64,256]{2,1,0:T(8,128)S(1)}, u32[]{:S(2)}, u32[]{:S(2)}) collective-permute-start(f32[4,64,256]{2,1,0:T(8,128)} %get-tuple-element.64), channel_id=1, source_target_pairs={{0,64},{1,65},{2,66},{3,67},{4,68},{5,69},{6,70},{7,71},{8,72},{9,... | collective-permute-start | bytes 786440 | tf_op jit(solution)/shard_map/ppermute | solution.py:24
  220.1 13.6 %collective-permute-start.22 = (f32[4,64,256]{2,1,0:T(8,128)}, f32[4,64,256]{2,1,0:T(8,128)S(1)}, u32[]{:S(2)}, u32[]{:S(2)}) collective-permute-start(f32[4,64,256]{2,1,0:T(8,128)} %get-tuple-element.69), channel_id=1, source_target_pairs={{0,16},{1,17},{2,18},{3,19},{4,20},{5,21},{6,22},{7,23},{8,24},{9,... | collective-permute-start | bytes 786440 | tf_op jit(solution)/shard_map/ppermute | solution.py:24
  221.3 12.5 %collective-permute-start.23 = (f32[4,64,256]{2,1,0:T(8,128)}, f32[4,64,256]{2,1,0:T(8,128)S(1)}, u32[]{:S(2)}, u32[]{:S(2)}) collective-permute-start(f32[4,64,256]{2,1,0:T(8,128)} %get-tuple-element.70), channel_id=1, source_target_pairs={{0,1},{1,0},{2,3},{3,2},{4,5},{5,4},{6,7},{7,6},{8,9},{9,8},{10,11... | collective-permute-start | bytes 786440 | tf_op jit(solution)/shard_map/ppermute | solution.py:24
  222.8 11.0 %collective-permute-start.24 = (f32[4,64,256]{2,1,0:T(8,128)}, f32[4,64,256]{2,1,0:T(8,128)S(1)}, u32[]{:S(2)}, u32[]{:S(2)}) collective-permute-start(f32[4,64,256]{2,1,0:T(8,128)} %get-tuple-element.71), channel_id=1, source_target_pairs={{0,3},{1,2},{2,1},{3,0},{4,7},{5,6},{6,5},{7,4},{8,11},{9,10},{10,... | collective-permute-start | bytes 786440 | tf_op jit(solution)/shard_map/ppermute | solution.py:24
  223.9 14.9 %collective-permute-start.28 = (f32[4,64,256]{2,1,0:T(8,128)S(1)}, f32[4,64,256]{2,1,0:T(8,128)S(1)}, u32[]{:S(2)}, u32[]{:S(2)}) collective-permute-start(f32[4,64,256]{2,1,0:T(8,128)S(1)} %shard_map.36), channel_id=1, source_target_pairs={{0,64},{1,65},{2,66},{3,67},{4,68},{5,69},{6,70},{7,71},{8,72},{9,... | collective-permute-start | bytes 786440 | tf_op jit(solution)/shard_map/ppermute | solution.py:24

commit v15 on v11

--- a/solution.py
+++ b/solution.py
@@ -8,7 +8,8 @@
 AXES = ("rep", "grid")
 PARAMS = pltpu.CompilerParams(vmem_limit_bytes=20 * 1024 * 1024)
 SHORT = pl.CostEstimate(flops=1, bytes_accessed=1, transcendentals=0)
-NEAR = (dict(), dict(dy=1), dict(dy=3), dict(dx=1))
+NEAR = (dict(), dict(dx=1), dict(dy=1), dict(dy=3))
+DIFFERS = (0, 3, 1, 2)
 
 
 def number(x_hi, core, x_lo, z, y):
@@ -43,16 +44,18 @@
 
 
 def call(kernel, scalars, values, in_specs, out_shape, out_specs, scratch=(), aliases=None):
+    scalars = scalars if isinstance(scalars, tuple) else (scalars,)
+    aliases = {at + len(scalars) - 1: out for at, out in (aliases or {}).items()}
     return pl.pallas_call(
         kernel,
         grid_spec=pltpu.PrefetchScalarGridSpec(
-            num_scalar_prefetch=1, grid=(1,), in_specs=in_specs, out_specs=out_specs, scratch_shapes=scratch
+            num_scalar_prefetch=len(scalars), grid=(1,), in_specs=in_specs, out_specs=out_specs, scratch_shapes=scratch
         ),
         out_shape=out_shape,
-        input_output_aliases=aliases or {},
+        input_output_aliases=aliases,
         compiler_params=PARAMS,
         cost_estimate=SHORT,
-    )(scalars, *values)
+    )(*scalars, *values)
 
 
 def cut_kernel(quarter, value, _, *rest):
@@ -60,7 +63,7 @@
     depth = outs[0].shape[0]
     copies = []
     for d, out in enumerate(outs):
-        at = pl.ds(pl.multiple_of((quarter[0] ^ d) * depth, depth), depth)
+        at = pl.ds(pl.multiple_of((quarter[0] ^ DIFFERS[d]) * depth, depth), depth)
         copies.append(pltpu.make_async_copy(value.at[at], out, sems.at[d]))
     for copy in copies:
         copy.start()
@@ -109,7 +112,7 @@
 
 
 def places(d):
-    return [(block, block ^ (0, 1, 3, 2)[d]) for block in range(4)]
+    return [(block, block ^ (0, 2, 1, 3)[d]) for block in range(4)]
 
 
 def early_products(swap, part, planes, rights, before=()):
@@ -164,10 +167,10 @@
     rows, depth = arrays[0].shape[1:]
     columns = rights[0].shape[1] // 4
 
-    def kernel(flags, *refs):
+    def kernel(swap, at_core, *refs):
         blocks, rest = refs[: len(arrays)], refs[len(arrays) + len(after):]
         high, low, ahead, keep, give, both, left_high, left_low = rest
-        swapped, core = flags[0] == 1, flags[1]
+        swapped, core = swap[0] == 1, at_core[0]
 
         def store(d, total):
             for part in range(2):
@@ -204,8 +207,8 @@
 def sum_kernel(side, keep, got, *refs):
     terms, (mine, theirs) = refs[:-2], refs[-2:]
     for out, part in ((mine, side[0]), (theirs, 1 - side[0])):
-        across = terms[2][1 - part]
-        out[...] = (keep[0, part] + got[part]) + (terms[0][part] + (terms[1][part] + across))
+        across = terms[0][1 - part]
+        out[...] = (keep[0, part] + got[part]) + (across + (terms[1][part] + terms[2][part]))
 
 
 def summed(side, keep, got, terms):
@@ -217,11 +220,11 @@
     )
 
 
-def join_kernel(place, one, other_one, two, other_two, out):
+def join_kernel(plane, first, one, other_one, two, other_two, out):
     for block in range(4):
-        line = place[1] ^ block
-        out[place[0], line] = one[block] + other_one[block]
-        out[1 - place[0], line] = two[block] + other_two[block]
+        line = first[0] ^ block
+        out[plane[0], line] = one[block] + other_one[block]
+        out[1 - plane[0], line] = two[block] + other_two[block]
 
 
 def join(place, values):
@@ -261,17 +264,16 @@
     got = [send(give, core=1) for give in gives]
     sums = added(swap, keep, got[1:])
     late_keep, late_give, both = late_products(
-        jnp.stack([swap[0], core]), ((own_two,), (far_two,)), third, rights, sums
+        (swap, core.reshape(1)), ((own_two,), (far_two,)), third, rights, sums
     )
     both = lax.all_to_all(both, AXES, 0, 0, tiled=True, axis_index_groups=CORES)
 
     ends = []
     for kept, given, terms in ((keep, got[0], sums), (late_keep, send(late_give, core=1), added_by_core(swap, both))):
-        across = send(terms[2], **NEAR[3])
-        here, there = summed(side, kept, given, [send(terms[0], **NEAR[1]), send(terms[1], **NEAR[2]), across])
+        here, there = summed(side, kept, given, [send(terms[d - 1], **NEAR[d]) for d in range(1, 4)])
         ends += [here, send(there, dhi=1)]
 
-    total = join(jnp.stack([(z & 1) ^ swap[0], y ^ (2 * side[0])]), ends)
+    total = join((((z & 1) ^ swap[0]).reshape(1), (y ^ (2 * side[0])).reshape(1)), ends)
     return total.reshape(8 * rows, columns)
 
 

time: 143 us -> 140 us (0.979)
  no operation moved by 1% of the time
where the time goes in v15:
time: 140 us
  waiting for transfers between devices  67.1 us (48%)
  starting transfers between devices  35.5 us (25%)
  Pallas kernels  26.3 us (19%)
  blocking collectives  6.26 us (4%)
  local copies, waits for them, and re-layouts  4.3 us (3%)
    ppermute x26, waiting for transfers between devices, send(): return lax.ppermute(value, AXES, pairs)  67.1 us
    ppermute x26, starting transfers between devices, send(): return lax.ppermute(value, AXES, pairs)  35.5 us
    pallas_call x10, Pallas kernels, call(): pl.pallas_call(kernel, grid_spec=pltpu.PrefetchScalarGridSpec(num_scalar_...  26.3 us
    all_to_all x1, blocking collectives, per_device(): both = lax.all_to_all(both, AXES, 0, 0, tiled=True, axis_index_groups=CORES)  6.26 us
    unnamed x22, local copies, waits for them, and re-layouts  2.87 us
  transfers between devices with their start and end apart: 26, of which 17 were waited for; matrix products, arithmetic and copies ran while one was open for 0% of the time, Pallas kernels for 18%

profile of v15, /device:TPU:0, one launch (start us, length us, event | category | flops | bytes accessed | tf_op | source)
XLA Modules:
  0.0 139.7 jit_solution(1038136411570587482)
XLA Ops:
  0.0 1.4 %dynamic-slice_bitcast_fusion = (f32[1,64,1024]{2,1,0:T(8,128)S(1)}, f32[64,1024]{1,0:T(8,128)S(1)}, f32[64,1024]{1,0:T(8,128)S(1)}, f32[64,1024]{1,0:T(8,128)S(1)}) fusion(f32[64,4096]{1,0:T(8,128)} %param.2, s32[]{:T(128)S(6)} %select_n.12, s32[]{:T(128)S(6)} %select_n.13, s32[]{:T(128)S(6)} %select_n.15, s32[]{:T(128)S(6)} %select_n.14), kind=kLoop, calls=%fused_computation.1 | loop fusion | bytes 2097168 | tf_op jit(solution)/shard_map/stack | solution.py:248
  1.4 3.2 %collective-permute-start.2 = (f32[64,1024]{1,0:T(8,128)S(1)}, f32[64,1024]{1,0:T(8,128)S(1)}, u32[]{:S(2)}, u32[]{:S(2)}) collective-permute-start(f32[64,1024]{1,0:T(8,128)S(1)} %get-tuple-element.75), channel_id=1, source_target_pairs={{0,3},{1,2},{2,1},{3,0},{4,7},{5,6},{6,5},{7,4},{8,11},{9,10},{10,... | collective-permute-start | bytes 786440 | tf_op jit(solution)/shard_map/ppermute | solution.py:24
  4.6 0.6 collective-permute-start.1
  5.3 0.4 collective-permute-start
  5.6 10.9 %collective-permute-done.2 = f32[64,1024]{1,0:T(8,128)S(1)} collective-permute-done((f32[64,1024]{1,0:T(8,128)S(1)}, f32[64,1024]{1,0:T(8,128)S(1)}, u32[]{:S(2)}, u32[]{:S(2)}) %collective-permute-start.2) | collective-permute-done | bytes 262176 | tf_op jit(solution)/shard_map/ppermute | solution.py:24
  16.6 0.0 collective-permute-done.1
  16.6 0.7 collective-permute-done
  17.3 0.1 pad_maximum_fusion.refs_0_
  17.3 4.0 %collective-permute-start.3 = (f32[4,64,1024]{2,1,0:T(8,128)S(1)}, f32[4,64,1024]{2,1,0:T(8,128)S(1)}, u32[]{:S(2)}, u32[]{:S(2)}) collective-permute-start(f32[4,64,1024]{2,1,0:T(8,128)S(1)} %pad_maximum_fusion.refs_0_), channel_id=1, source_target_pairs={{0,18},{1,19},{2,16},{3,17},{4,22},{5,23},{6,20},{7,21},{8,26},{9,... | collective-permute-start | bytes 3145736 | tf_op jit(solution)/shard_map/ppermute | solution.py:24
  21.4 1.9 %collective-permute-start.4 = (f32[4,64,1024]{2,1,0:T(8,128)S(1)}, f32[4,64,1024]{2,1,0:T(8,128)S(1)}, u32[]{:S(2)}, u32[]{:S(2)}) collective-permute-start(f32[4,64,1024]{2,1,0:T(8,128)S(1)} %pad_maximum_fusion.refs_0_), channel_id=1, source_target_pairs={{0,4},{1,5},{2,6},{3,7},{4,0},{5,1},{6,2},{7,3},{8,12},{9,13},{10,... | collective-permute-start | bytes 3145736 | tf_op jit(solution)/shard_map/ppermute | solution.py:24
  23.3 2.5 %collective-permute-start.5 = (f32[4,64,1024]{2,1,0:T(8,128)S(1)}, f32[4,64,1024]{2,1,0:T(8,128)S(1)}, u32[]{:S(2)}, u32[]{:S(2)}) collective-permute-start(f32[4,64,1024]{2,1,0:T(8,128)S(1)} %pad_maximum_fusion.refs_0_), channel_id=1, source_target_pairs={{0,12},{1,13},{2,14},{3,15},{4,8},{5,9},{6,10},{7,11},{8,4},{9,5},... | collective-permute-start | bytes 3145736 | tf_op jit(solution)/shard_map/ppermute | solution.py:24
  25.8 18.0 %collective-permute-done.3._.refs_0_ = f32[4,64,1024]{2,1,0:T(8,128)S(1)} collective-permute-done((f32[4,64,1024]{2,1,0:T(8,128)S(1)}, f32[4,64,1024]{2,1,0:T(8,128)S(1)}, u32[]{:S(2)}, u32[]{:S(2)}) %collective-permute-start.3) | collective-permute-done | bytes 1048608 | tf_op jit(solution)/shard_map/ppermute | solution.py:24
  43.8 1.2 collective-permute-done.4.refs_2_
  45.0 1.0 copy-done.5
  46.0 1.7 %collective-permute-done.5.refs_1_ = f32[4,64,1024]{2,1,0:T(8,128)S(1)} collective-permute-done((f32[4,64,1024]{2,1,0:T(8,128)S(1)}, f32[4,64,1024]{2,1,0:T(8,128)S(1)}, u32[]{:S(2)}, u32[]{:S(2)}) %collective-permute-start.5) | collective-permute-done | bytes 1048608 | tf_op jit(solution)/shard_map/ppermute | solution.py:24
  47.7 0.6 collective-permute-start.6
  48.3 2.3 %collective-permute-start.7 = (f32[4,64,1024]{2,1,0:T(8,128)S(1)}, f32[4,64,1024]{2,1,0:T(8,128)}, u32[]{:S(2)}, u32[]{:S(2)}) collective-permute-start(f32[4,64,1024]{2,1,0:T(8,128)S(1)} %collective-permute-done.3._.refs_0_), channel_id=1, source_target_pairs={{0,12},{1,13},{2,14},{3,15},{4,8},{5,9},{6,10},{7,11},{8,4},{9,5},... | collective-permute-start | bytes 3145736 | tf_op jit(solution)/shard_map/ppermute | solution.py:24
  50.7 1.8 %shard_map.28 = (f32[1024,256]{1,0:T(8,128)S(1)}, f32[1024,256]{1,0:T(8,128)}, f32[1024,256]{1,0:T(8,128)}, f32[1024,256]{1,0:T(8,128)}) custom-call(s32[1]{0:T(128)} %bitcast.8.quarter, f32[4096,256]{1,0:T(8,128)S(1)} %copy-done, f32[4,64,1024]{2,1,0:T(8,128)S(1)} %collective-permute-done.3._.refs_0_), custom_call_target="tpu_custom_call" | custom-call | flops 1 | bytes 1 | tf_op jit(solution)/shard_map/pallas_call | solution.py:49
  52.5 0.6 collective-permute-start.8
  53.1 1.0 collective-permute-start.9
  54.1 2.0 %collective-permute-start.10 = (f32[1024,256]{1,0:T(8,128)}, f32[1024,256]{1,0:T(8,128)}, u32[]{:S(2)}, u32[]{:S(2)}) collective-permute-start(f32[1024,256]{1,0:T(8,128)} %get-tuple-element.45), channel_id=1, source_target_pairs={{0,3},{1,2},{2,1},{3,0},{4,7},{5,6},{6,5},{7,4},{8,11},{9,10},{10,... | collective-permute-start | bytes 3145736 | tf_op jit(solution)/shard_map/ppermute | solution.py:24
  56.1 14.8 %collective-permute-done.6.refs_2_ = f32[4,64,1024]{2,1,0:T(8,128)} collective-permute-done((f32[4,64,1024]{2,1,0:T(8,128)S(1)}, f32[4,64,1024]{2,1,0:T(8,128)}, u32[]{:S(2)}, u32[]{:S(2)}) %collective-permute-start.6) | collective-permute-done | bytes 1048608 | tf_op jit(solution)/shard_map/ppermute | solution.py:24
  70.8 0.6 collective-permute-start.19
  71.4 0.5 collective-permute-done.7.refs_1_
  71.9 2.1 %collective-permute-start.20 = (f32[4,64,1024]{2,1,0:T(8,128)}, f32[4,64,1024]{2,1,0:T(8,128)S(1)}, u32[]{:S(2)}, u32[]{:S(2)}) collective-permute-start(f32[4,64,1024]{2,1,0:T(8,128)} %collective-permute-done.6.refs_2_), channel_id=1, source_target_pairs={{0,12},{1,13},{2,14},{3,15},{4,8},{5,9},{6,10},{7,11},{8,4},{9,5},... | collective-permute-start | bytes 3145736 | tf_op jit(solution)/shard_map/ppermute | solution.py:24
  74.0 0.6 collective-permute-done.8.refs_1_
  74.6 0.5 collective-permute-done.9.refs_2_
  75.1 2.0 %collective-permute-done.10.refs_3_ = f32[1024,256]{1,0:T(8,128)} collective-permute-done((f32[1024,256]{1,0:T(8,128)}, f32[1024,256]{1,0:T(8,128)}, u32[]{:S(2)}, u32[]{:S(2)}) %collective-permute-start.10) | collective-permute-done | bytes 1048608 | tf_op jit(solution)/shard_map/ppermute | solution.py:24
  77.1 2.7 %shard_map.29 = (bf16[1024,1024]{1,0:T(8,128)(2,1)S(1)}, bf16[1024,1024]{1,0:T(8,128)(2,1)S(1)}) custom-call(s32[1]{0:T(128)} %bitcast.3._.swap, f32[1024,256]{1,0:T(8,128)S(1)} %get-tuple-element.42.refs_0_, f32[1024,256]{1,0:T(8,128)} %collective-permute-done.8.refs_1_, f32[1024,256]{1,0:T(8,128)} %collective-permute-done.9.refs_2_, ...), custom_call_target="tpu_custom_call" | custom-call | flops 1 | bytes 1 | tf_op jit(solution)/shard_map/pallas_call | solution.py:49
  79.9 5.0 %shard_map.30 = (f32[4,2,4,64,256]{4,3,2,1,0:T(8,128)S(1)}, f32[4,2,4,64,256]{4,3,2,1,0:T(8,128)S(1)}, f32[2,4,64,256]{3,2,1,0:T(8,128)S(1)}, f32[2,4,64,256]{3,...) custom-call(s32[1]{0:T(128)} %bitcast.3._.swap, ...), custom_call_target="tpu_custom_call" | custom-call | flops 1 | bytes 1 | tf_op jit(solution)/shard_map/pallas_call | solution.py:49
  84.9 6.6 %shard_map.31 = (f32[4,2,4,64,256]{4,3,2,1,0:T(8,128)S(1)}, f32[4,2,4,64,256]{4,3,2,1,0:T(8,128)S(1)}, f32[2,4,64,256]{3,2,1,0:T(8,128)S(1)}, f32[2,4,64,256]{3,...) custom-call(s32[1]{0:T(128)} %bitcast.3._.swap, ...), custom_call_target="tpu_custom_call", output_to_operand_aliasing={{0}: (4, {}), {1}: (5, {}), {2}: (6, {}), {3}: (7, {}), {4}... | custom-call | flops 1 | bytes 1 | tf_op jit(solution)/shard_map/pallas_call | solution.py:49
  91.5 0.1 collective-permute-start.12
  91.6 0.5 collective-permute-start.13
  92.1 0.3 collective-permute-start.14
  92.4 1.1 collective-permute-done.12.refs_0_
  93.5 0.1 collective-permute-start.11
  93.6 0.6 collective-permute-done.13.refs_1_
  94.2 0.7 collective-permute-done.14.refs_2_
  95.0 1.0 shard_map.32
  95.9 1.4 %collective-permute-start.15 = (f32[2,4,64,256]{3,2,1,0:T(8,128)S(1)}, f32[2,4,64,256]{3,2,1,0:T(8,128)S(1)}, u32[]{:S(2)}, u32[]{:S(2)}) collective-permute-start(f32[2,4,64,256]{3,2,1,0:T(8,128)S(1)} %get-tuple-element.59.refs_2_), channel_id=1, source_target_pairs={{0,16},{1,17},{2,18},{3,19},{4,20},{5,21},{6,22},{7,23},{8,24},{9,... | collective-permute-start | bytes 1572872 | tf_op jit(solution)/shard_map/ppermute | solution.py:24
  97.4 0.0 collective-permute-start.16
  97.4 0.0 collective-permute-done.19.refs_0_
  97.4 2.0 %collective-permute-start.17 = (f32[2,4,64,256]{3,2,1,0:T(8,128)}, f32[2,4,64,256]{3,2,1,0:T(8,128)}, u32[]{:S(2)}, u32[]{:S(2)}) collective-permute-start(f32[2,4,64,256]{3,2,1,0:T(8,128)} %get-tuple-element.61.refs_4_), channel_id=1, source_target_pairs={{0,3},{1,2},{2,1},{3,0},{4,7},{5,6},{6,5},{7,4},{8,11},{9,10},{10,... | collective-permute-start | bytes 1572872 | tf_op jit(solution)/shard_map/ppermute | solution.py:24
  99.3 0.0 collective-permute-done.20.refs_1_
  99.4 3.5 %shard_map.34 = (f32[1,2,4,64,256]{4,3,2,1,0:T(8,128)S(1)}, f32[2,4,64,256]{3,2,1,0:T(8,128)}, f32[2,3,2,4,64,256]{5,4,3,2,1,0:T(8,128)S(1)}) custom-call(s32[1]{0:T(128)} %bitcast.3._.swap, s32[1]{0:T(128)} %bitcast.9.at_core, f32[4,64,1024]{2,1,0:T(8,128)S(1)} %collective-permute-done.19.refs_0_, f32[4,64,1024]{2,1,0:T(8,128)S(1)} %collective-permute-done.20.refs_1_, ...), custom_call_target="tpu_custom_call" | custom-call | flops 1 | bytes 1 | tf_op jit(solution)/shard_map/pallas_call | solution.py:49
  102.9 0.1 collective-permute-start.21
  103.0 6.3 %all_to_all.5.both = f32[2,3,2,4,64,256]{5,4,3,2,1,0:T(8,128)S(1)} all-to-all(f32[2,3,2,4,64,256]{5,4,3,2,1,0:T(8,128)S(1)} %get-tuple-element.67), channel_id=1, replica_groups={{0,32},{1,33},{2,34},{3,35},{4,36},{5,37},{6,38},{7,39},{8,40},{9,41},{..., dimensions={0} | all-to-all | bytes 6291456 | tf_op jit(solution)/shard_map/all_to_all | solution.py:269
  109.2 1.3 shard_map.35
  110.6 1.5 %collective-permute-start.22 = (f32[2,4,64,256]{3,2,1,0:T(8,128)}, f32[2,4,64,256]{3,2,1,0:T(8,128)}, u32[]{:S(2)}, u32[]{:S(2)}) collective-permute-start(f32[2,4,64,256]{3,2,1,0:T(8,128)} %get-tuple-element.68), channel_id=1, source_target_pairs={{0,16},{1,17},{2,18},{3,19},{4,20},{5,21},{6,22},{7,23},{8,24},{9,... | collective-permute-start | bytes 1572872 | tf_op jit(solution)/shard_map/ppermute | solution.py:24
  112.1 0.0 collective-permute-done.15.refs_0_
  112.1 0.9 collective-permute-start.23
  113.0 0.8 copy-done.7
  113.8 0.9 collective-permute-start.24
  114.7 1.0 copy-done.8
  115.7 1.9 %shard_map.33 = (f32[4,64,256]{2,1,0:T(8,128)S(1)}, f32[4,64,256]{2,1,0:T(8,128)}) custom-call(s32[1]{0:T(128)} %bitcast.2.side, f32[4,2,4,64,256]{4,3,2,1,0:T(8,128)S(1)} %get-tuple-element.54.keep, f32[2,4,64,256]{3,2,1,0:T(8,128)S(1)} %collective-permute-done.11.got, f32[2,4,64,256]{3,2,1,0:T(8,128)S(1)} %collective-permute-done.15.refs_0_, ...), custom_call_target="tpu_custom_call" | custom-call | flops 1 | bytes 1 | tf_op jit(solution)/shard_map/pallas_call | solution.py:49
  117.6 3.1 %collective-permute-start.18 = (f32[4,64,256]{2,1,0:T(8,128)}, f32[4,64,256]{2,1,0:T(8,128)S(1)}, u32[]{:S(2)}, u32[]{:S(2)}) collective-permute-start(f32[4,64,256]{2,1,0:T(8,128)} %get-tuple-element.63), channel_id=1, source_target_pairs={{0,64},{1,65},{2,66},{3,67},{4,68},{5,69},{6,70},{7,71},{8,72},{9,... | collective-permute-start | bytes 786440 | tf_op jit(solution)/shard_map/ppermute | solution.py:24
  120.7 5.0 %collective-permute-done.22.refs_0_ = f32[2,4,64,256]{3,2,1,0:T(8,128)} collective-permute-done((f32[2,4,64,256]{3,2,1,0:T(8,128)}, f32[2,4,64,256]{3,2,1,0:T(8,128)}, u32[]{:S(2)}, u32[]{:S(2)}) %collective-permute-start.22) | collective-permute-done | bytes 524320 | tf_op jit(solution)/shard_map/ppermute | solution.py:24
  125.6 0.4 collective-permute-done.23.refs_1_
  126.1 2.6 %collective-permute-done.24.refs_2_ = f32[2,4,64,256]{3,2,1,0:T(8,128)} collective-permute-done((f32[2,4,64,256]{3,2,1,0:T(8,128)}, f32[2,4,64,256]{3,2,1,0:T(8,128)}, u32[]{:S(2)}, u32[]{:S(2)}) %collective-permute-start.24) | collective-permute-done | bytes 524320 | tf_op jit(solution)/shard_map/ppermute | solution.py:24
  128.7 1.7 %shard_map.36 = (f32[4,64,256]{2,1,0:T(8,128)S(1)}, f32[4,64,256]{2,1,0:T(8,128)S(1)}) custom-call(s32[1]{0:T(128)} %bitcast.2.side, f32[1,2,4,64,256]{4,3,2,1,0:T(8,128)S(1)} %copy-done.10, f32[2,4,64,256]{3,2,1,0:T(8,128)} %collective-permute-done.21.got, f32[2,4,64,256]{3,2,1,0:T(8,128)} %collective-permute-done.22.refs_0_, ...), custom_call_target="tpu_custom_call" | custom-call | flops 1 | bytes 1 | tf_op jit(solution)/shard_map/pallas_call | solution.py:49
  130.4 2.8 %collective-permute-start.25 = (f32[4,64,256]{2,1,0:T(8,128)S(1)}, f32[4,64,256]{2,1,0:T(8,128)S(1)}, u32[]{:S(2)}, u32[]{:S(2)}) collective-permute-start(f32[4,64,256]{2,1,0:T(8,128)S(1)} %get-tuple-element.72), channel_id=1, source_target_pairs={{0,64},{1,65},{2,66},{3,67},{4,68},{5,69},{6,70},{7,71},{8,72},{9,... | collective-permute-start | bytes 786440 | tf_op jit(solution)/shard_map/ppermute | solution.py:24
  133.2 0.0 collective-permute-done.18.other_one
  133.2 5.7 %collective-permute-done.25.other_two = f32[4,64,256]{2,1,0:T(8,128)S(1)} collective-permute-done((f32[4,64,256]{2,1,0:T(8,128)S(1)}, f32[4,64,256]{2,1,0:T(8,128)S(1)}, u32[]{:S(2)}, u32[]{:S(2)}) %collective-permute-start.25) | collective-permute-done | bytes 262176 | tf_op jit(solution)/shard_map/ppermute | solution.py:24
  138.8 0.8 shard_map.37
  (23 shorter events, 0.0 us)
Async XLA Ops:
  0.0 50.6 %copy-start = (f32[4096,256]{1,0:T(8,128)S(1)}, f32[4096,256]{1,0:T(8,128)}, u32[]{:S(2)}) copy-start(f32[4096,256]{1,0:T(8,128)} %value.1) | copy-start | bytes 12582916
  1.4 15.1 %collective-permute-start.2 = (f32[64,1024]{1,0:T(8,128)S(1)}, f32[64,1024]{1,0:T(8,128)S(1)}, u32[]{:S(2)}, u32[]{:S(2)}) collective-permute-start(f32[64,1024]{1,0:T(8,128)S(1)} %get-tuple-element.75), channel_id=1, source_target_pairs={{0,3},{1,2},{2,1},{3,0},{4,7},{5,6},{6,5},{7,4},{8,11},{9,10},{10,... | collective-permute-start | bytes 786440 | tf_op jit(solution)/shard_map/ppermute | solution.py:24
  4.6 11.9 %collective-permute-start.1 = (f32[64,1024]{1,0:T(8,128)S(1)}, f32[64,1024]{1,0:T(8,128)S(1)}, u32[]{:S(2)}, u32[]{:S(2)}) collective-permute-start(f32[64,1024]{1,0:T(8,128)S(1)} %get-tuple-element.76), channel_id=1, source_target_pairs={{0,2},{1,3},{2,0},{3,1},{4,6},{5,7},{6,4},{7,5},{8,10},{9,11},{10,... | collective-permute-start | bytes 786440 | tf_op jit(solution)/shard_map/ppermute | solution.py:24
  5.3 12.0 %collective-permute-start = (f32[64,1024]{1,0:T(8,128)S(1)}, f32[64,1024]{1,0:T(8,128)S(1)}, u32[]{:S(2)}, u32[]{:S(2)}) collective-permute-start(f32[64,1024]{1,0:T(8,128)S(1)} %get-tuple-element.74), channel_id=1, source_target_pairs={{0,1},{1,0},{2,3},{3,2},{4,5},{5,4},{6,7},{7,6},{8,9},{9,8},{10,11... | collective-permute-start | bytes 786440 | tf_op jit(solution)/shard_map/ppermute | solution.py:24
  17.3 26.5 %collective-permute-start.3 = (f32[4,64,1024]{2,1,0:T(8,128)S(1)}, f32[4,64,1024]{2,1,0:T(8,128)S(1)}, u32[]{:S(2)}, u32[]{:S(2)}) collective-permute-start(f32[4,64,1024]{2,1,0:T(8,128)S(1)} %pad_maximum_fusion.refs_0_), channel_id=1, source_target_pairs={{0,18},{1,19},{2,16},{3,17},{4,22},{5,23},{6,20},{7,21},{8,26},{9,... | collective-permute-start | bytes 3145736 | tf_op jit(solution)/shard_map/ppermute | solution.py:24
  21.4 23.6 %collective-permute-start.4 = (f32[4,64,1024]{2,1,0:T(8,128)S(1)}, f32[4,64,1024]{2,1,0:T(8,128)S(1)}, u32[]{:S(2)}, u32[]{:S(2)}) collective-permute-start(f32[4,64,1024]{2,1,0:T(8,128)S(1)} %pad_maximum_fusion.refs_0_), channel_id=1, source_target_pairs={{0,4},{1,5},{2,6},{3,7},{4,0},{5,1},{6,2},{7,3},{8,12},{9,13},{10,... | collective-permute-start | bytes 3145736 | tf_op jit(solution)/shard_map/ppermute | solution.py:24
  23.3 24.4 %collective-permute-start.5 = (f32[4,64,1024]{2,1,0:T(8,128)S(1)}, f32[4,64,1024]{2,1,0:T(8,128)S(1)}, u32[]{:S(2)}, u32[]{:S(2)}) collective-permute-start(f32[4,64,1024]{2,1,0:T(8,128)S(1)} %pad_maximum_fusion.refs_0_), channel_id=1, source_target_pairs={{0,12},{1,13},{2,14},{3,15},{4,8},{5,9},{6,10},{7,11},{8,4},{9,5},... | collective-permute-start | bytes 3145736 | tf_op jit(solution)/shard_map/ppermute | solution.py:24
  43.8 8.6 %copy-start.1 = (f32[4,64,1024]{2,1,0:T(8,128)}, f32[4,64,1024]{2,1,0:T(8,128)S(1)}, u32[]{:S(2)}) copy-start(f32[4,64,1024]{2,1,0:T(8,128)S(1)} %collective-permute-done.3._.refs_0_) | copy-start | bytes 3145732
  45.0 1.0 copy-start.5
  47.7 2.9 %copy-start.3 = (f32[4,64,1024]{2,1,0:T(8,128)}, f32[4,64,1024]{2,1,0:T(8,128)S(1)}, u32[]{:S(2)}) copy-start(f32[4,64,1024]{2,1,0:T(8,128)S(1)} %collective-permute-done.5.refs_1_) | copy-start | bytes 3145732
  47.7 23.1 %collective-permute-start.6 = (f32[4,64,1024]{2,1,0:T(8,128)S(1)}, f32[4,64,1024]{2,1,0:T(8,128)}, u32[]{:S(2)}, u32[]{:S(2)}) collective-permute-start(f32[4,64,1024]{2,1,0:T(8,128)S(1)} %collective-permute-done.3._.refs_0_), channel_id=1, source_target_pairs={{0,4},{1,5},{2,6},{3,7},{4,0},{5,1},{6,2},{7,3},{8,12},{9,13},{10,... | collective-permute-start | bytes 3145736 | tf_op jit(solution)/shard_map/ppermute | solution.py:24
  48.3 23.6 %collective-permute-start.7 = (f32[4,64,1024]{2,1,0:T(8,128)S(1)}, f32[4,64,1024]{2,1,0:T(8,128)}, u32[]{:S(2)}, u32[]{:S(2)}) collective-permute-start(f32[4,64,1024]{2,1,0:T(8,128)S(1)} %collective-permute-done.3._.refs_0_), channel_id=1, source_target_pairs={{0,12},{1,13},{2,14},{3,15},{4,8},{5,9},{6,10},{7,11},{8,4},{9,5},... | collective-permute-start | bytes 3145736 | tf_op jit(solution)/shard_map/ppermute | solution.py:24
  52.5 22.1 %collective-permute-start.8 = (f32[1024,256]{1,0:T(8,128)}, f32[1024,256]{1,0:T(8,128)}, u32[]{:S(2)}, u32[]{:S(2)}) collective-permute-start(f32[1024,256]{1,0:T(8,128)} %get-tuple-element.43), channel_id=1, source_target_pairs={{0,16},{1,17},{2,18},{3,19},{4,20},{5,21},{6,22},{7,23},{8,24},{9,... | collective-permute-start | bytes 3145736 | tf_op jit(solution)/shard_map/ppermute | solution.py:24
  53.1 22.0 %collective-permute-start.9 = (f32[1024,256]{1,0:T(8,128)}, f32[1024,256]{1,0:T(8,128)}, u32[]{:S(2)}, u32[]{:S(2)}) collective-permute-start(f32[1024,256]{1,0:T(8,128)} %get-tuple-element.44), channel_id=1, source_target_pairs={{0,1},{1,0},{2,3},{3,2},{4,5},{5,4},{6,7},{7,6},{8,9},{9,8},{10,11... | collective-permute-start | bytes 3145736 | tf_op jit(solution)/shard_map/ppermute | solution.py:24
  54.1 23.0 %collective-permute-start.10 = (f32[1024,256]{1,0:T(8,128)}, f32[1024,256]{1,0:T(8,128)}, u32[]{:S(2)}, u32[]{:S(2)}) collective-permute-start(f32[1024,256]{1,0:T(8,128)} %get-tuple-element.45), channel_id=1, source_target_pairs={{0,3},{1,2},{2,1},{3,0},{4,7},{5,6},{6,5},{7,4},{8,11},{9,10},{10,... | collective-permute-start | bytes 3145736 | tf_op jit(solution)/shard_map/ppermute | solution.py:24
  70.8 26.6 %collective-permute-start.19 = (f32[4,64,1024]{2,1,0:T(8,128)}, f32[4,64,1024]{2,1,0:T(8,128)S(1)}, u32[]{:S(2)}, u32[]{:S(2)}) collective-permute-start(f32[4,64,1024]{2,1,0:T(8,128)} %copy-done.3), channel_id=1, source_target_pairs={{0,4},{1,5},{2,6},{3,7},{4,0},{5,1},{6,2},{7,3},{8,12},{9,13},{10,... | collective-permute-start | bytes 3145736 | tf_op jit(solution)/shard_map/ppermute | solution.py:24
  71.9 27.5 %collective-permute-start.20 = (f32[4,64,1024]{2,1,0:T(8,128)}, f32[4,64,1024]{2,1,0:T(8,128)S(1)}, u32[]{:S(2)}, u32[]{:S(2)}) collective-permute-start(f32[4,64,1024]{2,1,0:T(8,128)} %collective-permute-done.6.refs_2_), channel_id=1, source_target_pairs={{0,12},{1,13},{2,14},{3,15},{4,8},{5,9},{6,10},{7,11},{8,4},{9,5},... | collective-permute-start | bytes 3145736 | tf_op jit(solution)/shard_map/ppermute | solution.py:24
  77.1 2.7 %copy-start.4 = (f32[4,64,1024]{2,1,0:T(8,128)S(1)}, f32[4,64,1024]{2,1,0:T(8,128)}, u32[]{:S(2)}) copy-start(f32[4,64,1024]{2,1,0:T(8,128)} %copy-done.3) | copy-start | bytes 3145732
  77.1 2.7 %copy-start.6 = (f32[4,64,1024]{2,1,0:T(8,128)S(1)}, f32[4,64,1024]{2,1,0:T(8,128)}, u32[]{:S(2)}) copy-start(f32[4,64,1024]{2,1,0:T(8,128)} %copy-done.5) | copy-start | bytes 3145732
  79.9 5.1 %copy-start.2 = (f32[4,64,1024]{2,1,0:T(8,128)S(1)}, f32[4,64,1024]{2,1,0:T(8,128)}, u32[]{:S(2)}) copy-start(f32[4,64,1024]{2,1,0:T(8,128)} %copy-done.1) | copy-start | bytes 3145732
  91.5 2.0 %collective-permute-start.12 = (f32[2,4,64,256]{3,2,1,0:T(8,128)S(1)}, f32[2,4,64,256]{3,2,1,0:T(8,128)S(1)}, u32[]{:S(2)}, u32[]{:S(2)}) collective-permute-start(f32[2,4,64,256]{3,2,1,0:T(8,128)S(1)} %get-tuple-element.56), channel_id=1, source_target_pairs={{0,32},{1,33},{2,34},{3,35},{4,36},{5,37},{6,38},{7,39},{8,40},{9,... | collective-permute-start | bytes 1572872 | tf_op jit(solution)/shard_map/ppermute | solution.py:24
  91.6 2.6 %collective-permute-start.13 = (f32[2,4,64,256]{3,2,1,0:T(8,128)S(1)}, f32[2,4,64,256]{3,2,1,0:T(8,128)S(1)}, u32[]{:S(2)}, u32[]{:S(2)}) collective-permute-start(f32[2,4,64,256]{3,2,1,0:T(8,128)S(1)} %get-tuple-element.57), channel_id=1, source_target_pairs={{0,32},{1,33},{2,34},{3,35},{4,36},{5,37},{6,38},{7,39},{8,40},{9,... | collective-permute-start | bytes 1572872 | tf_op jit(solution)/shard_map/ppermute | solution.py:24
  92.1 2.9 %collective-permute-start.14 = (f32[2,4,64,256]{3,2,1,0:T(8,128)S(1)}, f32[2,4,64,256]{3,2,1,0:T(8,128)S(1)}, u32[]{:S(2)}, u32[]{:S(2)}) collective-permute-start(f32[2,4,64,256]{3,2,1,0:T(8,128)S(1)} %get-tuple-element.58), channel_id=1, source_target_pairs={{0,32},{1,33},{2,34},{3,35},{4,36},{5,37},{6,38},{7,39},{8,40},{9,... | collective-permute-start | bytes 1572872 | tf_op jit(solution)/shard_map/ppermute | solution.py:24
  93.5 17.1 %collective-permute-start.11 = (f32[2,4,64,256]{3,2,1,0:T(8,128)S(1)}, f32[2,4,64,256]{3,2,1,0:T(8,128)S(1)}, u32[]{:S(2)}, u32[]{:S(2)}) collective-permute-start(f32[2,4,64,256]{3,2,1,0:T(8,128)S(1)} %get-tuple-element.55), channel_id=1, source_target_pairs={{0,32},{1,33},{2,34},{3,35},{4,36},{5,37},{6,38},{7,39},{8,40},{9,... | collective-permute-start | bytes 1572872 | tf_op jit(solution)/shard_map/ppermute | solution.py:24
  95.9 16.1 %collective-permute-start.15 = (f32[2,4,64,256]{3,2,1,0:T(8,128)S(1)}, f32[2,4,64,256]{3,2,1,0:T(8,128)S(1)}, u32[]{:S(2)}, u32[]{:S(2)}) collective-permute-start(f32[2,4,64,256]{3,2,1,0:T(8,128)S(1)} %get-tuple-element.59.refs_2_), channel_id=1, source_target_pairs={{0,16},{1,17},{2,18},{3,19},{4,20},{5,21},{6,22},{7,23},{8,24},{9,... | collective-permute-start | bytes 1572872 | tf_op jit(solution)/shard_map/ppermute | solution.py:24
  97.4 15.6 %collective-permute-start.16 = (f32[2,4,64,256]{3,2,1,0:T(8,128)S(1)}, f32[2,4,64,256]{3,2,1,0:T(8,128)S(1)}, u32[]{:S(2)}, u32[]{:S(2)}) collective-permute-start(f32[2,4,64,256]{3,2,1,0:T(8,128)S(1)} %get-tuple-element.60.refs_3_), channel_id=1, source_target_pairs={{0,1},{1,0},{2,3},{3,2},{4,5},{5,4},{6,7},{7,6},{8,9},{9,8},{10,11... | collective-permute-start | bytes 1572872 | tf_op jit(solution)/shard_map/ppermute | solution.py:24
  97.4 17.3 %collective-permute-start.17 = (f32[2,4,64,256]{3,2,1,0:T(8,128)}, f32[2,4,64,256]{3,2,1,0:T(8,128)}, u32[]{:S(2)}, u32[]{:S(2)}) collective-permute-start(f32[2,4,64,256]{3,2,1,0:T(8,128)} %get-tuple-element.61.refs_4_), channel_id=1, source_target_pairs={{0,3},{1,2},{2,1},{3,0},{4,7},{5,6},{6,5},{7,4},{8,11},{9,10},{10,... | collective-permute-start | bytes 1572872 | tf_op jit(solution)/shard_map/ppermute | solution.py:24
  102.9 6.4 %copy-start.9 = (f32[1,2,4,64,256]{4,3,2,1,0:T(8,128)}, f32[1,2,4,64,256]{4,3,2,1,0:T(8,128)S(1)}, u32[]{:S(2)}) copy-start(f32[1,2,4,64,256]{4,3,2,1,0:T(8,128)S(1)} %get-tuple-element.65.keep) | copy-start | bytes 1572868
  102.9 17.8 %collective-permute-start.21 = (f32[2,4,64,256]{3,2,1,0:T(8,128)}, f32[2,4,64,256]{3,2,1,0:T(8,128)}, u32[]{:S(2)}, u32[]{:S(2)}) collective-permute-start(f32[2,4,64,256]{3,2,1,0:T(8,128)} %get-tuple-element.66), channel_id=1, source_target_pairs={{0,32},{1,33},{2,34},{3,35},{4,36},{5,37},{6,38},{7,39},{8,40},{9,... | collective-permute-start | bytes 1572872 | tf_op jit(solution)/shard_map/ppermute | solution.py:24
  110.6 15.1 %collective-permute-start.22 = (f32[2,4,64,256]{3,2,1,0:T(8,128)}, f32[2,4,64,256]{3,2,1,0:T(8,128)}, u32[]{:S(2)}, u32[]{:S(2)}) collective-permute-start(f32[2,4,64,256]{3,2,1,0:T(8,128)} %get-tuple-element.68), channel_id=1, source_target_pairs={{0,16},{1,17},{2,18},{3,19},{4,20},{5,21},{6,22},{7,23},{8,24},{9,... | collective-permute-start | bytes 1572872 | tf_op jit(solution)/shard_map/ppermute | solution.py:24
  112.1 14.0 %collective-permute-start.23 = (f32[2,4,64,256]{3,2,1,0:T(8,128)}, f32[2,4,64,256]{3,2,1,0:T(8,128)}, u32[]{:S(2)}, u32[]{:S(2)}) collective-permute-start(f32[2,4,64,256]{3,2,1,0:T(8,128)} %get-tuple-element.69), channel_id=1, source_target_pairs={{0,1},{1,0},{2,3},{3,2},{4,5},{5,4},{6,7},{7,6},{8,9},{9,8},{10,11... | collective-permute-start | bytes 1572872 | tf_op jit(solution)/shard_map/ppermute | solution.py:24
  113.0 0.8 copy-start.7
  113.8 14.9 %collective-permute-start.24 = (f32[2,4,64,256]{3,2,1,0:T(8,128)}, f32[2,4,64,256]{3,2,1,0:T(8,128)}, u32[]{:S(2)}, u32[]{:S(2)}) collective-permute-start(f32[2,4,64,256]{3,2,1,0:T(8,128)} %get-tuple-element.70), channel_id=1, source_target_pairs={{0,3},{1,2},{2,1},{3,0},{4,7},{5,6},{6,5},{7,4},{8,11},{9,10},{10,... | collective-permute-start | bytes 1572872 | tf_op jit(solution)/shard_map/ppermute | solution.py:24
  114.7 1.0 copy-start.8
  115.7 13.0 %copy-start.10 = (f32[1,2,4,64,256]{4,3,2,1,0:T(8,128)S(1)}, f32[1,2,4,64,256]{4,3,2,1,0:T(8,128)}, u32[]{:S(2)}) copy-start(f32[1,2,4,64,256]{4,3,2,1,0:T(8,128)} %copy-done.9) | copy-start | bytes 1572868
  117.6 15.5 %collective-permute-start.18 = (f32[4,64,256]{2,1,0:T(8,128)}, f32[4,64,256]{2,1,0:T(8,128)S(1)}, u32[]{:S(2)}, u32[]{:S(2)}) collective-permute-start(f32[4,64,256]{2,1,0:T(8,128)} %get-tuple-element.63), channel_id=1, source_target_pairs={{0,64},{1,65},{2,66},{3,67},{4,68},{5,69},{6,70},{7,71},{8,72},{9,... | collective-permute-start | bytes 786440 | tf_op jit(solution)/shard_map/ppermute | solution.py:24
  130.4 8.5 %collective-permute-start.25 = (f32[4,64,256]{2,1,0:T(8,128)S(1)}, f32[4,64,256]{2,1,0:T(8,128)S(1)}, u32[]{:S(2)}, u32[]{:S(2)}) collective-permute-start(f32[4,64,256]{2,1,0:T(8,128)S(1)} %get-tuple-element.72), channel_id=1, source_target_pairs={{0,64},{1,65},{2,66},{3,67},{4,68},{5,69},{6,70},{7,71},{8,72},{9,... | collective-permute-start | bytes 786440 | tf_op jit(solution)/shard_map/ppermute | solution.py:24

commit v16 on v15

--- a/solution.py
+++ b/solution.py
@@ -80,7 +80,7 @@
 
 
 def split_kernel(_, *refs):
-    pieces, (high, low) = refs[:4], refs[4:]
+    *pieces, high, low = refs
     columns = pieces[0].shape[1]
     for d, piece in enumerate(pieces):
         at = slice(d * columns, (d + 1) * columns)
@@ -89,12 +89,12 @@
 
 def split(scalars, pieces):
     depth, columns = pieces[0].shape
-    shape = pltpu.VMEM((depth, 4 * columns), jnp.bfloat16)
+    shape = pltpu.VMEM((depth, len(pieces) * columns), jnp.bfloat16)
     found = call(split_kernel, scalars, pieces, [whole(piece) for piece in pieces], [shape] * 2, [VMEM] * 2)
     return [pltpu.with_memory_space_constraint(value, pltpu.VMEM) for value in found]
 
 
-def multiplied(blocks, left_high, left_low, high, low, store):
+def multiplied(blocks, left_high, left_low, rights, store):
     depth = left_high.shape[1]
     at = 0
     for block in blocks:
@@ -102,12 +102,12 @@
         span = slice(at, at + value.shape[0])
         left_high[span], left_low[span] = halves(value)
         at += value.shape[0]
-    columns = high.shape[1] // 4
+    columns = rights[0].shape[1]
     for d in range(4):
-        span = slice(d * columns, (d + 1) * columns)
-        total = jnp.dot(left_high[...], high[:, span], preferred_element_type=jnp.float32)
-        total += jnp.dot(left_high[...], low[:, span], preferred_element_type=jnp.float32)
-        total += jnp.dot(left_low[...], high[:, span], preferred_element_type=jnp.float32)
+        high, low = rights[2 * d][...], rights[2 * d + 1][...]
+        total = jnp.dot(left_high[...], high, preferred_element_type=jnp.float32)
+        total += jnp.dot(left_high[...], low, preferred_element_type=jnp.float32)
+        total += jnp.dot(left_low[...], high, preferred_element_type=jnp.float32)
         store(d, total.reshape(-1, 4, blocks[0].shape[1], columns))
 
 
@@ -118,11 +118,12 @@
 def early_products(swap, part, planes, rights, before=()):
     arrays = [array for plane in planes for array in plane]
     rows, depth = arrays[0].shape[1:]
-    columns = rights[0].shape[1] // 4
+    columns = rights[0].shape[1]
 
     def kernel(swap, *refs):
         blocks, rest = refs[: len(arrays)], refs[len(arrays) + len(before):]
-        high, low, keep, third, *gives, left_high, left_low = rest
+        *rights, keep, third, one_give, two_give, three_give, four_give, left_high, left_low = rest
+        gives = one_give, two_give, three_give, four_give
         swapped = swap[0] == 1
 
         def store(d, total):
@@ -132,7 +133,7 @@
                 gives[d][0, into] = jnp.where(swapped, zero, one)
                 third[d, 0, into] = total[2, block]
 
-        multiplied(blocks, left_high, left_low, high, low, store)
+        multiplied(blocks, left_high, left_low, rights, store)
 
     kept = jax.ShapeDtypeStruct((4, 2, 4, rows, columns), jnp.float32)
     given = jax.ShapeDtypeStruct((2, 4, rows, columns), jnp.float32)
@@ -143,7 +144,7 @@
     first = 1 + len(arrays)
     return call(
         kernel, swap, (*arrays, *before, *rights),
-        [whole(array) for array in arrays] + [ANYWHERE] * len(before) + [VMEM] * 2,
+        [whole(array) for array in arrays] + [ANYWHERE] * len(before) + [VMEM] * 8,
         [kept] * 2 + [given] * 4, [kept_out] * 2 + [given_out] * 4, [scratch] * 2,
         {first + at: at for at in range(len(before))},
     )
@@ -165,11 +166,11 @@
 def late_products(flags, parts, third, rights, after):
     arrays = [array for part in parts for array in part]
     rows, depth = arrays[0].shape[1:]
-    columns = rights[0].shape[1] // 4
+    columns = rights[0].shape[1]
 
     def kernel(swap, at_core, *refs):
         blocks, rest = refs[: len(arrays)], refs[len(arrays) + len(after):]
-        high, low, ahead, keep, give, both, left_high, left_low = rest
+        *rights, ahead, keep, give, both, left_high, left_low = rest
         swapped, core = swap[0] == 1, at_core[0]
 
         def store(d, total):
@@ -182,14 +183,14 @@
                     else:
                         both[core, d - 1, part, into], both[1 - core, d - 1, part, into] = kept, given
 
-        multiplied(blocks, left_high, left_low, high, low, store)
+        multiplied(blocks, left_high, left_low, rights, store)
 
     piece = (2, 4, rows, columns)
     shapes = [jax.ShapeDtypeStruct(shape, jnp.float32) for shape in ((1, *piece), piece, (2, 3, *piece))]
     scratch = pltpu.VMEM((8 * rows, depth), jnp.bfloat16)
     return call(
         kernel, flags, (*arrays, *after, *rights, third),
-        [whole(array) for array in arrays] + [ANYWHERE] * len(after) + [VMEM] * 2 + [whole(third)],
+        [whole(array) for array in arrays] + [ANYWHERE] * len(after) + [VMEM] * 8 + [whole(third)],
         shapes, [whole(shape) for shape in shapes], [scratch] * 2,
     )
 
@@ -255,7 +256,7 @@
 
     pieces = cut_after(quarter.reshape(1), right, other)
     pieces = [pieces[0]] + [send(pieces[d], **NEAR[d]) for d in range(1, 4)]
-    rights = split(swap, pieces)
+    rights = [half for piece in pieces for half in split(swap, [piece])]
 
     before = early_products(swap, 0, ((mine,), (own_three,), (own_one,)), rights)
     early = early_products(swap, 1, ((far,), (far_three,), (far_one,)), rights, before)

time: 140 us -> 139 us (level)
  waiting for transfers between devices: 67.1 us -> 63.4 us
  local copies, waits for them, and re-layouts: 4.3 us -> 6.47 us
    ppermute x26, waiting for transfers between devices: 67.1 us -> 63.4 us  [send(): return lax.ppermute(value, AXES, pairs)]
    unnamed x22 -> x26, local copies, waits for them, and re-layouts: 2.87 us -> 5.03 us
    pallas_call x10 -> x13, Pallas kernels: 26.3 us -> 26.6 us  [call(): pl.pallas_call(kernel, grid_spec=pltpu.PrefetchScalarGridSpec(num_scalar_...]
  transfers between devices with their start and end apart: 26 -> 26, of which waited for: 17 -> 14; matrix products, arithmetic and copies ran while one was open for 0% -> 0% of each run, Pallas kernels for 18% -> 19%
where the time goes in v16:
time: 139 us; the launch traced here: 138 us
  waiting for transfers between devices  63.4 us (46%)
  starting transfers between devices  35.3 us (25%)
  Pallas kernels  26.6 us (19%)
  local copies, waits for them, and re-layouts  6.47 us (5%)
  blocking collectives  6.26 us (5%)
    ppermute x26, waiting for transfers between devices, send(): return lax.ppermute(value, AXES, pairs)  63.4 us
    ppermute x26, starting transfers between devices, send(): return lax.ppermute(value, AXES, pairs)  35.3 us
    pallas_call x13, Pallas kernels, call(): pl.pallas_call(kernel, grid_spec=pltpu.PrefetchScalarGridSpec(num_scalar_...  26.6 us
    all_to_all x1, blocking collectives, per_device(): both = lax.all_to_all(both, AXES, 0, 0, tiled=True, axis_index_groups=CORES)  6.26 us
    unnamed x26, local copies, waits for them, and re-layouts  5.03 us
  transfers between devices with their start and end apart: 26, of which 14 were waited for; matrix products, arithmetic and copies ran while one was open for 0% of the time, Pallas kernels for 19%

profile of v16, /device:TPU:0, one launch (start us, length us, event | category | flops | bytes accessed | tf_op | source)
XLA Modules:
  0.0 138.2 jit_solution(12422442927993204462)
XLA Ops:
  0.0 1.4 %dynamic-slice_bitcast_fusion = (f32[1,64,1024]{2,1,0:T(8,128)S(1)}, f32[64,1024]{1,0:T(8,128)S(1)}, f32[64,1024]{1,0:T(8,128)S(1)}, f32[64,1024]{1,0:T(8,128)S(1)}) fusion(f32[64,4096]{1,0:T(8,128)} %param.2, s32[]{:T(128)S(6)} %select_n.12, s32[]{:T(128)S(6)} %select_n.13, s32[]{:T(128)S(6)} %select_n.15, s32[]{:T(128)S(6)} %select_n.14), kind=kLoop, calls=%fused_computation.1 | loop fusion | bytes 2097168 | tf_op jit(solution)/shard_map/stack | solution.py:249
  1.4 3.2 %collective-permute-start.2 = (f32[64,1024]{1,0:T(8,128)S(1)}, f32[64,1024]{1,0:T(8,128)S(1)}, u32[]{:S(2)}, u32[]{:S(2)}) collective-permute-start(f32[64,1024]{1,0:T(8,128)S(1)} %get-tuple-element.87), channel_id=1, source_target_pairs={{0,3},{1,2},{2,1},{3,0},{4,7},{5,6},{6,5},{7,4},{8,11},{9,10},{10,... | collective-permute-start | bytes 786440 | tf_op jit(solution)/shard_map/ppermute | solution.py:24
  4.6 0.6 collective-permute-start.1
  5.3 0.4 collective-permute-start
  5.6 10.9 %collective-permute-done.2 = f32[64,1024]{1,0:T(8,128)S(1)} collective-permute-done((f32[64,1024]{1,0:T(8,128)S(1)}, f32[64,1024]{1,0:T(8,128)S(1)}, u32[]{:S(2)}, u32[]{:S(2)}) %collective-permute-start.2) | collective-permute-done | bytes 262176 | tf_op jit(solution)/shard_map/ppermute | solution.py:24
  16.6 0.0 collective-permute-done.1
  16.6 0.7 collective-permute-done
  17.3 0.1 pad_maximum_fusion.refs_0_
  17.3 4.0 %collective-permute-start.3 = (f32[4,64,1024]{2,1,0:T(8,128)S(1)}, f32[4,64,1024]{2,1,0:T(8,128)S(1)}, u32[]{:S(2)}, u32[]{:S(2)}) collective-permute-start(f32[4,64,1024]{2,1,0:T(8,128)S(1)} %pad_maximum_fusion.refs_0_), channel_id=1, source_target_pairs={{0,18},{1,19},{2,16},{3,17},{4,22},{5,23},{6,20},{7,21},{8,26},{9,... | collective-permute-start | bytes 3145736 | tf_op jit(solution)/shard_map/ppermute | solution.py:24
  21.4 1.9 %collective-permute-start.4 = (f32[4,64,1024]{2,1,0:T(8,128)S(1)}, f32[4,64,1024]{2,1,0:T(8,128)S(1)}, u32[]{:S(2)}, u32[]{:S(2)}) collective-permute-start(f32[4,64,1024]{2,1,0:T(8,128)S(1)} %pad_maximum_fusion.refs_0_), channel_id=1, source_target_pairs={{0,4},{1,5},{2,6},{3,7},{4,0},{5,1},{6,2},{7,3},{8,12},{9,13},{10,... | collective-permute-start | bytes 3145736 | tf_op jit(solution)/shard_map/ppermute | solution.py:24
  23.3 2.5 %collective-permute-start.5 = (f32[4,64,1024]{2,1,0:T(8,128)S(1)}, f32[4,64,1024]{2,1,0:T(8,128)S(1)}, u32[]{:S(2)}, u32[]{:S(2)}) collective-permute-start(f32[4,64,1024]{2,1,0:T(8,128)S(1)} %pad_maximum_fusion.refs_0_), channel_id=1, source_target_pairs={{0,12},{1,13},{2,14},{3,15},{4,8},{5,9},{6,10},{7,11},{8,4},{9,5},... | collective-permute-start | bytes 3145736 | tf_op jit(solution)/shard_map/ppermute | solution.py:24
  25.8 18.0 %collective-permute-done.3._.refs_0_ = f32[4,64,1024]{2,1,0:T(8,128)S(1)} collective-permute-done((f32[4,64,1024]{2,1,0:T(8,128)S(1)}, f32[4,64,1024]{2,1,0:T(8,128)S(1)}, u32[]{:S(2)}, u32[]{:S(2)}) %collective-permute-start.3) | collective-permute-done | bytes 1048608 | tf_op jit(solution)/shard_map/ppermute | solution.py:24
  43.8 1.2 collective-permute-done.4.refs_2_
  45.0 1.0 copy-done.7
  46.0 1.7 %collective-permute-done.5.refs_1_ = f32[4,64,1024]{2,1,0:T(8,128)S(1)} collective-permute-done((f32[4,64,1024]{2,1,0:T(8,128)S(1)}, f32[4,64,1024]{2,1,0:T(8,128)S(1)}, u32[]{:S(2)}, u32[]{:S(2)}) %collective-permute-start.5) | collective-permute-done | bytes 1048608 | tf_op jit(solution)/shard_map/ppermute | solution.py:24
  47.7 0.6 collective-permute-start.6
  48.3 2.3 %collective-permute-start.7 = (f32[4,64,1024]{2,1,0:T(8,128)S(1)}, f32[4,64,1024]{2,1,0:T(8,128)}, u32[]{:S(2)}, u32[]{:S(2)}) collective-permute-start(f32[4,64,1024]{2,1,0:T(8,128)S(1)} %collective-permute-done.3._.refs_0_), channel_id=1, source_target_pairs={{0,12},{1,13},{2,14},{3,15},{4,8},{5,9},{6,10},{7,11},{8,4},{9,5},... | collective-permute-start | bytes 3145736 | tf_op jit(solution)/shard_map/ppermute | solution.py:24
  50.7 1.8 %shard_map.28 = (f32[1024,256]{1,0:T(8,128)S(1)}, f32[1024,256]{1,0:T(8,128)}, f32[1024,256]{1,0:T(8,128)}, f32[1024,256]{1,0:T(8,128)}) custom-call(s32[1]{0:T(128)} %bitcast.8.quarter, f32[4096,256]{1,0:T(8,128)S(1)} %copy-done, f32[4,64,1024]{2,1,0:T(8,128)S(1)} %collective-permute-done.3._.refs_0_), custom_call_target="tpu_custom_call" | custom-call | flops 1 | bytes 1 | tf_op jit(solution)/shard_map/pallas_call | solution.py:49
  52.4 0.9 copy-done.3
  53.4 0.5 collective-permute-start.8
  53.9 1.0 collective-permute-start.9
  54.9 2.0 %collective-permute-start.10 = (f32[1024,256]{1,0:T(8,128)}, f32[1024,256]{1,0:T(8,128)S(1)}, u32[]{:S(2)}, u32[]{:S(2)}) collective-permute-start(f32[1024,256]{1,0:T(8,128)} %get-tuple-element.57), channel_id=1, source_target_pairs={{0,3},{1,2},{2,1},{3,0},{4,7},{5,6},{6,5},{7,4},{8,11},{9,10},{10,... | collective-permute-start | bytes 3145736 | tf_op jit(solution)/shard_map/ppermute | solution.py:24
  56.9 1.2 copy-done.4
  58.1 0.1 shard_map.29
  58.3 12.6 %collective-permute-done.6.refs_2_ = f32[4,64,1024]{2,1,0:T(8,128)} collective-permute-done((f32[4,64,1024]{2,1,0:T(8,128)S(1)}, f32[4,64,1024]{2,1,0:T(8,128)}, u32[]{:S(2)}, u32[]{:S(2)}) %collective-permute-start.6) | collective-permute-done | bytes 1048608 | tf_op jit(solution)/shard_map/ppermute | solution.py:24
  70.8 0.6 collective-permute-start.19
  71.4 0.5 collective-permute-done.7.refs_1_
  71.9 2.1 %collective-permute-start.20 = (f32[4,64,1024]{2,1,0:T(8,128)}, f32[4,64,1024]{2,1,0:T(8,128)S(1)}, u32[]{:S(2)}, u32[]{:S(2)}) collective-permute-start(f32[4,64,1024]{2,1,0:T(8,128)} %collective-permute-done.6.refs_2_), channel_id=1, source_target_pairs={{0,12},{1,13},{2,14},{3,15},{4,8},{5,9},{6,10},{7,11},{8,4},{9,5},... | collective-permute-start | bytes 3145736 | tf_op jit(solution)/shard_map/ppermute | solution.py:24
  74.0 1.5 %collective-permute-done.8.refs_0_ = f32[1024,256]{1,0:T(8,128)} collective-permute-done((f32[1024,256]{1,0:T(8,128)}, f32[1024,256]{1,0:T(8,128)}, u32[]{:S(2)}, u32[]{:S(2)}) %collective-permute-start.8) | collective-permute-done | bytes 1048608 | tf_op jit(solution)/shard_map/ppermute | solution.py:24
  75.4 1.4 shard_map.30
  76.8 0.0 collective-permute-done.9.refs_0_
  76.8 1.4 shard_map.31
  78.2 0.0 collective-permute-done.10.refs_0_
  78.2 0.1 shard_map.32
  78.3 5.1 %shard_map.33 = (f32[4,2,4,64,256]{4,3,2,1,0:T(8,128)S(1)}, f32[4,2,4,64,256]{4,3,2,1,0:T(8,128)S(1)}, f32[2,4,64,256]{3,2,1,0:T(8,128)S(1)}, f32[2,4,64,256]{3,...) custom-call(s32[1]{0:T(128)} %bitcast.3._.swap, ...), custom_call_target="tpu_custom_call" | custom-call | flops 1 | bytes 1 | tf_op jit(solution)/shard_map/pallas_call | solution.py:49
  83.4 6.6 %shard_map.34 = (f32[4,2,4,64,256]{4,3,2,1,0:T(8,128)S(1)}, f32[4,2,4,64,256]{4,3,2,1,0:T(8,128)S(1)}, f32[2,4,64,256]{3,2,1,0:T(8,128)S(1)}, f32[2,4,64,256]{3,...) custom-call(s32[1]{0:T(128)} %bitcast.3._.swap, ...), custom_call_target="tpu_custom_call", output_to_operand_aliasing={{0}: (4, {}), {1}: (5, {}), {2}: (6, {}), {3}: (7, {}), {4}... | custom-call | flops 1 | bytes 1 | tf_op jit(solution)/shard_map/pallas_call | solution.py:49
  90.0 0.1 collective-permute-start.12
  90.1 0.5 collective-permute-start.13
  90.6 0.1 collective-permute-start.14
  90.7 1.3 collective-permute-done.12.refs_0_
  92.0 0.1 collective-permute-start.11
  92.1 0.6 collective-permute-done.13.refs_1_
  92.7 0.7 collective-permute-done.14.refs_2_
  93.5 1.0 shard_map.35
  94.4 1.1 collective-permute-start.15
  95.5 0.8 collective-permute-start.16
  96.3 2.2 %collective-permute-start.17 = (f32[2,4,64,256]{3,2,1,0:T(8,128)}, f32[2,4,64,256]{3,2,1,0:T(8,128)}, u32[]{:S(2)}, u32[]{:S(2)}) collective-permute-start(f32[2,4,64,256]{3,2,1,0:T(8,128)} %get-tuple-element.73.refs_4_), channel_id=1, source_target_pairs={{0,3},{1,2},{2,1},{3,0},{4,7},{5,6},{6,5},{7,4},{8,11},{9,10},{10,... | collective-permute-start | bytes 1572872 | tf_op jit(solution)/shard_map/ppermute | solution.py:24
  98.5 3.5 %shard_map.37 = (f32[1,2,4,64,256]{4,3,2,1,0:T(8,128)S(1)}, f32[2,4,64,256]{3,2,1,0:T(8,128)}, f32[2,3,2,4,64,256]{5,4,3,2,1,0:T(8,128)S(1)}) custom-call(s32[1]{0:T(128)} %bitcast.3._.swap, s32[1]{0:T(128)} %bitcast.9.at_core, f32[4,64,1024]{2,1,0:T(8,128)S(1)} %collective-permute-done.19.refs_0_, f32[4,64,1024]{2,1,0:T(8,128)S(1)} %collective-permute-done.20.refs_1_, ...), custom_call_target="tpu_custom_call" | custom-call | flops 1 | bytes 1 | tf_op jit(solution)/shard_map/pallas_call | solution.py:49
  102.0 0.1 collective-permute-start.21
  102.1 6.3 %all_to_all.5.both = f32[2,3,2,4,64,256]{5,4,3,2,1,0:T(8,128)S(1)} all-to-all(f32[2,3,2,4,64,256]{5,4,3,2,1,0:T(8,128)S(1)} %get-tuple-element.79), channel_id=1, replica_groups={{0,32},{1,33},{2,34},{3,35},{4,36},{5,37},{6,38},{7,39},{8,40},{9,41},{..., dimensions={0} | all-to-all | bytes 6291456 | tf_op jit(solution)/shard_map/all_to_all | solution.py:270
  108.4 1.3 shard_map.38
  109.7 0.5 collective-permute-start.22
  110.2 1.3 collective-permute-start.23
  111.5 0.8 copy-done.9
  112.4 0.8 collective-permute-start.24
  113.2 1.0 copy-done.10
  114.2 1.9 %shard_map.36 = (f32[4,64,256]{2,1,0:T(8,128)S(1)}, f32[4,64,256]{2,1,0:T(8,128)}) custom-call(s32[1]{0:T(128)} %bitcast.2.side, f32[4,2,4,64,256]{4,3,2,1,0:T(8,128)S(1)} %get-tuple-element.66.keep, f32[2,4,64,256]{3,2,1,0:T(8,128)S(1)} %collective-permute-done.11.got, f32[2,4,64,256]{3,2,1,0:T(8,128)S(1)} %collective-permute-done.15.refs_0_, ...), custom_call_target="tpu_custom_call" | custom-call | flops 1 | bytes 1 | tf_op jit(solution)/shard_map/pallas_call | solution.py:49
  116.1 2.8 %collective-permute-start.18 = (f32[4,64,256]{2,1,0:T(8,128)}, f32[4,64,256]{2,1,0:T(8,128)S(1)}, u32[]{:S(2)}, u32[]{:S(2)}) collective-permute-start(f32[4,64,256]{2,1,0:T(8,128)} %get-tuple-element.75), channel_id=1, source_target_pairs={{0,64},{1,65},{2,66},{3,67},{4,68},{5,69},{6,70},{7,71},{8,72},{9,... | collective-permute-start | bytes 786440 | tf_op jit(solution)/shard_map/ppermute | solution.py:24
  119.0 5.8 %collective-permute-done.22.refs_0_ = f32[2,4,64,256]{3,2,1,0:T(8,128)} collective-permute-done((f32[2,4,64,256]{3,2,1,0:T(8,128)}, f32[2,4,64,256]{3,2,1,0:T(8,128)}, u32[]{:S(2)}, u32[]{:S(2)}) %collective-permute-start.22) | collective-permute-done | bytes 524320 | tf_op jit(solution)/shard_map/ppermute | solution.py:24
  124.8 2.5 %collective-permute-done.24.refs_2_ = f32[2,4,64,256]{3,2,1,0:T(8,128)} collective-permute-done((f32[2,4,64,256]{3,2,1,0:T(8,128)}, f32[2,4,64,256]{3,2,1,0:T(8,128)}, u32[]{:S(2)}, u32[]{:S(2)}) %collective-permute-start.24) | collective-permute-done | bytes 524320 | tf_op jit(solution)/shard_map/ppermute | solution.py:24
  127.3 1.7 %shard_map.39 = (f32[4,64,256]{2,1,0:T(8,128)S(1)}, f32[4,64,256]{2,1,0:T(8,128)S(1)}) custom-call(s32[1]{0:T(128)} %bitcast.2.side, f32[1,2,4,64,256]{4,3,2,1,0:T(8,128)S(1)} %copy-done.12, f32[2,4,64,256]{3,2,1,0:T(8,128)} %collective-permute-done.21.got, f32[2,4,64,256]{3,2,1,0:T(8,128)} %collective-permute-done.22.refs_0_, ...), custom_call_target="tpu_custom_call" | custom-call | flops 1 | bytes 1 | tf_op jit(solution)/shard_map/pallas_call | solution.py:49
  128.9 3.1 %collective-permute-start.25 = (f32[4,64,256]{2,1,0:T(8,128)S(1)}, f32[4,64,256]{2,1,0:T(8,128)S(1)}, u32[]{:S(2)}, u32[]{:S(2)}) collective-permute-start(f32[4,64,256]{2,1,0:T(8,128)S(1)} %get-tuple-element.84), channel_id=1, source_target_pairs={{0,64},{1,65},{2,66},{3,67},{4,68},{5,69},{6,70},{7,71},{8,72},{9,... | collective-permute-start | bytes 786440 | tf_op jit(solution)/shard_map/ppermute | solution.py:24
  132.0 5.4 %collective-permute-done.25.other_two = f32[4,64,256]{2,1,0:T(8,128)S(1)} collective-permute-done((f32[4,64,256]{2,1,0:T(8,128)S(1)}, f32[4,64,256]{2,1,0:T(8,128)S(1)}, u32[]{:S(2)}, u32[]{:S(2)}) %collective-permute-start.25) | collective-permute-done | bytes 262176 | tf_op jit(solution)/shard_map/ppermute | solution.py:24
  137.4 0.8 shard_map.40
  (30 shorter events, 0.1 us)
Async XLA Ops:
  0.0 50.6 %copy-start = (f32[4096,256]{1,0:T(8,128)S(1)}, f32[4096,256]{1,0:T(8,128)}, u32[]{:S(2)}) copy-start(f32[4096,256]{1,0:T(8,128)} %value.1) | copy-start | bytes 12582916
  1.4 15.1 %collective-permute-start.2 = (f32[64,1024]{1,0:T(8,128)S(1)}, f32[64,1024]{1,0:T(8,128)S(1)}, u32[]{:S(2)}, u32[]{:S(2)}) collective-permute-start(f32[64,1024]{1,0:T(8,128)S(1)} %get-tuple-element.87), channel_id=1, source_target_pairs={{0,3},{1,2},{2,1},{3,0},{4,7},{5,6},{6,5},{7,4},{8,11},{9,10},{10,... | collective-permute-start | bytes 786440 | tf_op jit(solution)/shard_map/ppermute | solution.py:24
  4.6 11.9 %collective-permute-start.1 = (f32[64,1024]{1,0:T(8,128)S(1)}, f32[64,1024]{1,0:T(8,128)S(1)}, u32[]{:S(2)}, u32[]{:S(2)}) collective-permute-start(f32[64,1024]{1,0:T(8,128)S(1)} %get-tuple-element.88), channel_id=1, source_target_pairs={{0,2},{1,3},{2,0},{3,1},{4,6},{5,7},{6,4},{7,5},{8,10},{9,11},{10,... | collective-permute-start | bytes 786440 | tf_op jit(solution)/shard_map/ppermute | solution.py:24
  5.3 12.0 %collective-permute-start = (f32[64,1024]{1,0:T(8,128)S(1)}, f32[64,1024]{1,0:T(8,128)S(1)}, u32[]{:S(2)}, u32[]{:S(2)}) collective-permute-start(f32[64,1024]{1,0:T(8,128)S(1)} %get-tuple-element.86), channel_id=1, source_target_pairs={{0,1},{1,0},{2,3},{3,2},{4,5},{5,4},{6,7},{7,6},{8,9},{9,8},{10,11... | collective-permute-start | bytes 786440 | tf_op jit(solution)/shard_map/ppermute | solution.py:24
  17.3 26.5 %collective-permute-start.3 = (f32[4,64,1024]{2,1,0:T(8,128)S(1)}, f32[4,64,1024]{2,1,0:T(8,128)S(1)}, u32[]{:S(2)}, u32[]{:S(2)}) collective-permute-start(f32[4,64,1024]{2,1,0:T(8,128)S(1)} %pad_maximum_fusion.refs_0_), channel_id=1, source_target_pairs={{0,18},{1,19},{2,16},{3,17},{4,22},{5,23},{6,20},{7,21},{8,26},{9,... | collective-permute-start | bytes 3145736 | tf_op jit(solution)/shard_map/ppermute | solution.py:24
  21.4 23.6 %collective-permute-start.4 = (f32[4,64,1024]{2,1,0:T(8,128)S(1)}, f32[4,64,1024]{2,1,0:T(8,128)S(1)}, u32[]{:S(2)}, u32[]{:S(2)}) collective-permute-start(f32[4,64,1024]{2,1,0:T(8,128)S(1)} %pad_maximum_fusion.refs_0_), channel_id=1, source_target_pairs={{0,4},{1,5},{2,6},{3,7},{4,0},{5,1},{6,2},{7,3},{8,12},{9,13},{10,... | collective-permute-start | bytes 3145736 | tf_op jit(solution)/shard_map/ppermute | solution.py:24
  23.3 24.4 %collective-permute-start.5 = (f32[4,64,1024]{2,1,0:T(8,128)S(1)}, f32[4,64,1024]{2,1,0:T(8,128)S(1)}, u32[]{:S(2)}, u32[]{:S(2)}) collective-permute-start(f32[4,64,1024]{2,1,0:T(8,128)S(1)} %pad_maximum_fusion.refs_0_), channel_id=1, source_target_pairs={{0,12},{1,13},{2,14},{3,15},{4,8},{5,9},{6,10},{7,11},{8,4},{9,5},... | collective-permute-start | bytes 3145736 | tf_op jit(solution)/shard_map/ppermute | solution.py:24
  43.8 8.6 %copy-start.1 = (f32[4,64,1024]{2,1,0:T(8,128)}, f32[4,64,1024]{2,1,0:T(8,128)S(1)}, u32[]{:S(2)}) copy-start(f32[4,64,1024]{2,1,0:T(8,128)S(1)} %collective-permute-done.3._.refs_0_) | copy-start | bytes 3145732
  45.0 1.0 copy-start.7
  47.7 2.9 %copy-start.5 = (f32[4,64,1024]{2,1,0:T(8,128)}, f32[4,64,1024]{2,1,0:T(8,128)S(1)}, u32[]{:S(2)}) copy-start(f32[4,64,1024]{2,1,0:T(8,128)S(1)} %collective-permute-done.5.refs_1_) | copy-start | bytes 3145732
  47.7 23.1 %collective-permute-start.6 = (f32[4,64,1024]{2,1,0:T(8,128)S(1)}, f32[4,64,1024]{2,1,0:T(8,128)}, u32[]{:S(2)}, u32[]{:S(2)}) collective-permute-start(f32[4,64,1024]{2,1,0:T(8,128)S(1)} %collective-permute-done.3._.refs_0_), channel_id=1, source_target_pairs={{0,4},{1,5},{2,6},{3,7},{4,0},{5,1},{6,2},{7,3},{8,12},{9,13},{10,... | collective-permute-start | bytes 3145736 | tf_op jit(solution)/shard_map/ppermute | solution.py:24
  48.3 23.6 %collective-permute-start.7 = (f32[4,64,1024]{2,1,0:T(8,128)S(1)}, f32[4,64,1024]{2,1,0:T(8,128)}, u32[]{:S(2)}, u32[]{:S(2)}) collective-permute-start(f32[4,64,1024]{2,1,0:T(8,128)S(1)} %collective-permute-done.3._.refs_0_), channel_id=1, source_target_pairs={{0,12},{1,13},{2,14},{3,15},{4,8},{5,9},{6,10},{7,11},{8,4},{9,5},... | collective-permute-start | bytes 3145736 | tf_op jit(solution)/shard_map/ppermute | solution.py:24
  52.4 1.0 copy-start.3
  53.4 22.0 %collective-permute-start.8 = (f32[1024,256]{1,0:T(8,128)}, f32[1024,256]{1,0:T(8,128)}, u32[]{:S(2)}, u32[]{:S(2)}) collective-permute-start(f32[1024,256]{1,0:T(8,128)} %get-tuple-element.51), channel_id=1, source_target_pairs={{0,16},{1,17},{2,18},{3,19},{4,20},{5,21},{6,22},{7,23},{8,24},{9,... | collective-permute-start | bytes 3145736 | tf_op jit(solution)/shard_map/ppermute | solution.py:24
  53.9 22.9 %collective-permute-start.9 = (f32[1024,256]{1,0:T(8,128)}, f32[1024,256]{1,0:T(8,128)}, u32[]{:S(2)}, u32[]{:S(2)}) collective-permute-start(f32[1024,256]{1,0:T(8,128)} %get-tuple-element.54), channel_id=1, source_target_pairs={{0,1},{1,0},{2,3},{3,2},{4,5},{5,4},{6,7},{7,6},{8,9},{9,8},{10,11... | collective-permute-start | bytes 3145736 | tf_op jit(solution)/shard_map/ppermute | solution.py:24
  54.9 23.3 %collective-permute-start.10 = (f32[1024,256]{1,0:T(8,128)}, f32[1024,256]{1,0:T(8,128)S(1)}, u32[]{:S(2)}, u32[]{:S(2)}) collective-permute-start(f32[1024,256]{1,0:T(8,128)} %get-tuple-element.57), channel_id=1, source_target_pairs={{0,3},{1,2},{2,1},{3,0},{4,7},{5,6},{6,5},{7,4},{8,11},{9,10},{10,... | collective-permute-start | bytes 3145736 | tf_op jit(solution)/shard_map/ppermute | solution.py:24
  56.9 1.2 copy-start.4
  58.1 20.2 %copy-start.6 = (f32[4,64,1024]{2,1,0:T(8,128)S(1)}, f32[4,64,1024]{2,1,0:T(8,128)}, u32[]{:S(2)}) copy-start(f32[4,64,1024]{2,1,0:T(8,128)} %copy-done.5) | copy-start | bytes 3145732
  58.1 20.2 %copy-start.8 = (f32[4,64,1024]{2,1,0:T(8,128)S(1)}, f32[4,64,1024]{2,1,0:T(8,128)}, u32[]{:S(2)}) copy-start(f32[4,64,1024]{2,1,0:T(8,128)} %copy-done.7) | copy-start | bytes 3145732
  70.8 25.5 %collective-permute-start.19 = (f32[4,64,1024]{2,1,0:T(8,128)}, f32[4,64,1024]{2,1,0:T(8,128)S(1)}, u32[]{:S(2)}, u32[]{:S(2)}) collective-permute-start(f32[4,64,1024]{2,1,0:T(8,128)} %copy-done.5), channel_id=1, source_target_pairs={{0,4},{1,5},{2,6},{3,7},{4,0},{5,1},{6,2},{7,3},{8,12},{9,13},{10,... | collective-permute-start | bytes 3145736 | tf_op jit(solution)/shard_map/ppermute | solution.py:24
  71.9 26.6 %collective-permute-start.20 = (f32[4,64,1024]{2,1,0:T(8,128)}, f32[4,64,1024]{2,1,0:T(8,128)S(1)}, u32[]{:S(2)}, u32[]{:S(2)}) collective-permute-start(f32[4,64,1024]{2,1,0:T(8,128)} %collective-permute-done.6.refs_2_), channel_id=1, source_target_pairs={{0,12},{1,13},{2,14},{3,15},{4,8},{5,9},{6,10},{7,11},{8,4},{9,5},... | collective-permute-start | bytes 3145736 | tf_op jit(solution)/shard_map/ppermute | solution.py:24
  78.3 5.1 %copy-start.2 = (f32[4,64,1024]{2,1,0:T(8,128)S(1)}, f32[4,64,1024]{2,1,0:T(8,128)}, u32[]{:S(2)}) copy-start(f32[4,64,1024]{2,1,0:T(8,128)} %copy-done.1) | copy-start | bytes 3145732
  90.0 2.0 %collective-permute-start.12 = (f32[2,4,64,256]{3,2,1,0:T(8,128)S(1)}, f32[2,4,64,256]{3,2,1,0:T(8,128)S(1)}, u32[]{:S(2)}, u32[]{:S(2)}) collective-permute-start(f32[2,4,64,256]{3,2,1,0:T(8,128)S(1)} %get-tuple-element.68), channel_id=1, source_target_pairs={{0,32},{1,33},{2,34},{3,35},{4,36},{5,37},{6,38},{7,39},{8,40},{9,... | collective-permute-start | bytes 1572872 | tf_op jit(solution)/shard_map/ppermute | solution.py:24
  90.1 2.6 %collective-permute-start.13 = (f32[2,4,64,256]{3,2,1,0:T(8,128)S(1)}, f32[2,4,64,256]{3,2,1,0:T(8,128)S(1)}, u32[]{:S(2)}, u32[]{:S(2)}) collective-permute-start(f32[2,4,64,256]{3,2,1,0:T(8,128)S(1)} %get-tuple-element.69), channel_id=1, source_target_pairs={{0,32},{1,33},{2,34},{3,35},{4,36},{5,37},{6,38},{7,39},{8,40},{9,... | collective-permute-start | bytes 1572872 | tf_op jit(solution)/shard_map/ppermute | solution.py:24
  90.6 2.9 %collective-permute-start.14 = (f32[2,4,64,256]{3,2,1,0:T(8,128)S(1)}, f32[2,4,64,256]{3,2,1,0:T(8,128)S(1)}, u32[]{:S(2)}, u32[]{:S(2)}) collective-permute-start(f32[2,4,64,256]{3,2,1,0:T(8,128)S(1)} %get-tuple-element.70), channel_id=1, source_target_pairs={{0,32},{1,33},{2,34},{3,35},{4,36},{5,37},{6,38},{7,39},{8,40},{9,... | collective-permute-start | bytes 1572872 | tf_op jit(solution)/shard_map/ppermute | solution.py:24
  92.0 17.7 %collective-permute-start.11 = (f32[2,4,64,256]{3,2,1,0:T(8,128)S(1)}, f32[2,4,64,256]{3,2,1,0:T(8,128)S(1)}, u32[]{:S(2)}, u32[]{:S(2)}) collective-permute-start(f32[2,4,64,256]{3,2,1,0:T(8,128)S(1)} %get-tuple-element.67), channel_id=1, source_target_pairs={{0,32},{1,33},{2,34},{3,35},{4,36},{5,37},{6,38},{7,39},{8,40},{9,... | collective-permute-start | bytes 1572872 | tf_op jit(solution)/shard_map/ppermute | solution.py:24
  94.4 15.8 %collective-permute-start.15 = (f32[2,4,64,256]{3,2,1,0:T(8,128)S(1)}, f32[2,4,64,256]{3,2,1,0:T(8,128)S(1)}, u32[]{:S(2)}, u32[]{:S(2)}) collective-permute-start(f32[2,4,64,256]{3,2,1,0:T(8,128)S(1)} %get-tuple-element.71.refs_2_), channel_id=1, source_target_pairs={{0,16},{1,17},{2,18},{3,19},{4,20},{5,21},{6,22},{7,23},{8,24},{9,... | collective-permute-start | bytes 1572872 | tf_op jit(solution)/shard_map/ppermute | solution.py:24
  95.5 16.0 %collective-permute-start.16 = (f32[2,4,64,256]{3,2,1,0:T(8,128)S(1)}, f32[2,4,64,256]{3,2,1,0:T(8,128)S(1)}, u32[]{:S(2)}, u32[]{:S(2)}) collective-permute-start(f32[2,4,64,256]{3,2,1,0:T(8,128)S(1)} %get-tuple-element.72.refs_3_), channel_id=1, source_target_pairs={{0,1},{1,0},{2,3},{3,2},{4,5},{5,4},{6,7},{7,6},{8,9},{9,8},{10,11... | collective-permute-start | bytes 1572872 | tf_op jit(solution)/shard_map/ppermute | solution.py:24
  96.3 16.8 %collective-permute-start.17 = (f32[2,4,64,256]{3,2,1,0:T(8,128)}, f32[2,4,64,256]{3,2,1,0:T(8,128)}, u32[]{:S(2)}, u32[]{:S(2)}) collective-permute-start(f32[2,4,64,256]{3,2,1,0:T(8,128)} %get-tuple-element.73.refs_4_), channel_id=1, source_target_pairs={{0,3},{1,2},{2,1},{3,0},{4,7},{5,6},{6,5},{7,4},{8,11},{9,10},{10,... | collective-permute-start | bytes 1572872 | tf_op jit(solution)/shard_map/ppermute | solution.py:24
  102.0 6.4 %copy-start.11 = (f32[1,2,4,64,256]{4,3,2,1,0:T(8,128)}, f32[1,2,4,64,256]{4,3,2,1,0:T(8,128)S(1)}, u32[]{:S(2)}) copy-start(f32[1,2,4,64,256]{4,3,2,1,0:T(8,128)S(1)} %get-tuple-element.77.keep) | copy-start | bytes 1572868
  102.0 17.0 %collective-permute-start.21 = (f32[2,4,64,256]{3,2,1,0:T(8,128)}, f32[2,4,64,256]{3,2,1,0:T(8,128)}, u32[]{:S(2)}, u32[]{:S(2)}) collective-permute-start(f32[2,4,64,256]{3,2,1,0:T(8,128)} %get-tuple-element.78), channel_id=1, source_target_pairs={{0,32},{1,33},{2,34},{3,35},{4,36},{5,37},{6,38},{7,39},{8,40},{9,... | collective-permute-start | bytes 1572872 | tf_op jit(solution)/shard_map/ppermute | solution.py:24
  109.7 15.1 %collective-permute-start.22 = (f32[2,4,64,256]{3,2,1,0:T(8,128)}, f32[2,4,64,256]{3,2,1,0:T(8,128)}, u32[]{:S(2)}, u32[]{:S(2)}) collective-permute-start(f32[2,4,64,256]{3,2,1,0:T(8,128)} %get-tuple-element.80), channel_id=1, source_target_pairs={{0,16},{1,17},{2,18},{3,19},{4,20},{5,21},{6,22},{7,23},{8,24},{9,... | collective-permute-start | bytes 1572872 | tf_op jit(solution)/shard_map/ppermute | solution.py:24
  110.2 14.5 %collective-permute-start.23 = (f32[2,4,64,256]{3,2,1,0:T(8,128)}, f32[2,4,64,256]{3,2,1,0:T(8,128)}, u32[]{:S(2)}, u32[]{:S(2)}) collective-permute-start(f32[2,4,64,256]{3,2,1,0:T(8,128)} %get-tuple-element.81), channel_id=1, source_target_pairs={{0,1},{1,0},{2,3},{3,2},{4,5},{5,4},{6,7},{7,6},{8,9},{9,8},{10,11... | collective-permute-start | bytes 1572872 | tf_op jit(solution)/shard_map/ppermute | solution.py:24
  111.5 0.8 copy-start.9
  112.4 14.9 %collective-permute-start.24 = (f32[2,4,64,256]{3,2,1,0:T(8,128)}, f32[2,4,64,256]{3,2,1,0:T(8,128)}, u32[]{:S(2)}, u32[]{:S(2)}) collective-permute-start(f32[2,4,64,256]{3,2,1,0:T(8,128)} %get-tuple-element.82), channel_id=1, source_target_pairs={{0,3},{1,2},{2,1},{3,0},{4,7},{5,6},{6,5},{7,4},{8,11},{9,10},{10,... | collective-permute-start | bytes 1572872 | tf_op jit(solution)/shard_map/ppermute | solution.py:24
  113.1 1.0 copy-start.10
  114.2 13.1 %copy-start.12 = (f32[1,2,4,64,256]{4,3,2,1,0:T(8,128)S(1)}, f32[1,2,4,64,256]{4,3,2,1,0:T(8,128)}, u32[]{:S(2)}) copy-start(f32[1,2,4,64,256]{4,3,2,1,0:T(8,128)} %copy-done.11) | copy-start | bytes 1572868
  116.1 15.9 %collective-permute-start.18 = (f32[4,64,256]{2,1,0:T(8,128)}, f32[4,64,256]{2,1,0:T(8,128)S(1)}, u32[]{:S(2)}, u32[]{:S(2)}) collective-permute-start(f32[4,64,256]{2,1,0:T(8,128)} %get-tuple-element.75), channel_id=1, source_target_pairs={{0,64},{1,65},{2,66},{3,67},{4,68},{5,69},{6,70},{7,71},{8,72},{9,... | collective-permute-start | bytes 786440 | tf_op jit(solution)/shard_map/ppermute | solution.py:24
  128.9 8.5 %collective-permute-start.25 = (f32[4,64,256]{2,1,0:T(8,128)S(1)}, f32[4,64,256]{2,1,0:T(8,128)S(1)}, u32[]{:S(2)}, u32[]{:S(2)}) collective-permute-start(f32[4,64,256]{2,1,0:T(8,128)S(1)} %get-tuple-element.84), channel_id=1, source_target_pairs={{0,64},{1,65},{2,66},{3,67},{4,68},{5,69},{6,70},{7,71},{8,72},{9,... | collective-permute-start | bytes 786440 | tf_op jit(solution)/shard_map/ppermute | solution.py:24

commit v17 on v16

--- a/solution.py
+++ b/solution.py
@@ -221,16 +221,41 @@
     )
 
 
-def join_kernel(plane, first, one, other_one, two, other_two, out):
+def part_specs(keep, got, terms, which):
+    once = pl.Buffered(1)
+
+    def of(value, flip):
+        return pl.BlockSpec((1, *value.shape[1:]), lambda i, *scalars: (which(*scalars) ^ flip, 0, 0, 0), pipeline_mode=once)
+
+    first = pl.BlockSpec((1, 1, *keep.shape[2:]), lambda i, *scalars: (0, which(*scalars), 0, 0, 0), pipeline_mode=once)
+    return [first, of(got, 0)] + [of(term, at == 0) for at, term in enumerate(terms)]
+
+
+def onward_kernel(_, keep, got, across, two, three, out):
+    out[...] = (keep[0, 0] + got[0]) + (across[0] + (two[0] + three[0]))
+
+
+def onward(side, keep, got, terms):
+    shape = jax.ShapeDtypeStruct(got.shape[1:], jnp.float32)
+    specs = part_specs(keep, got, terms, lambda side: 1 - side[0])
+    return call(onward_kernel, side, (keep, got, *terms), specs, shape, whole(shape))
+
+
+def join_kernel(plane, first, _, one, other_one, keep, got, across, two, three, other_two, out):
     for block in range(4):
         line = first[0] ^ block
         out[plane[0], line] = one[block] + other_one[block]
-        out[1 - plane[0], line] = two[block] + other_two[block]
-
-
-def join(place, values):
-    shape = jax.ShapeDtypeStruct((2, *values[0].shape), jnp.float32)
-    return call(join_kernel, place, values, [whole(value) for value in values], shape, whole(shape))
+        near = across[0, block] + (two[0, block] + three[0, block])
+        out[1 - plane[0], line] = (keep[0, 0, block] + got[0, block]) + (near + other_two[block])
+
+
+def join(scalars, early, keep, got, terms, other):
+    shape = jax.ShapeDtypeStruct((2, *early[0].shape), jnp.float32)
+    specs = part_specs(keep, got, terms, lambda plane, first, side: side[0])
+    return call(
+        join_kernel, scalars, (*early, keep, got, *terms, other),
+        [whole(value) for value in early] + specs + [whole(other)], shape, whole(shape),
+    )
 
 
 def per_device(left, right):
@@ -249,12 +274,12 @@
     mine = jnp.stack([block(0), send(block(1), dy=1), send(block(3), dy=2), send(block(2), dy=3)])
     other = send(mine, dx=1, dy=2)
     own_one, own_three = send(mine, dz=1), send(mine, dz=3)
-    far, *_ = lax.optimization_barrier((other, own_one, own_three))
+    pieces = cut_after(quarter.reshape(1), right, other)
+    far, *_ = lax.optimization_barrier((other, own_one, own_three, *pieces))
     far_one, far_three = lax.optimization_barrier((send(far, dz=1), send(far, dz=3)))
 
     own_two, far_two = send(own_three, dz=1), send(far_one, dz=3)
 
-    pieces = cut_after(quarter.reshape(1), right, other)
     pieces = [pieces[0]] + [send(pieces[d], **NEAR[d]) for d in range(1, 4)]
     rights = [half for piece in pieces for half in split(swap, [piece])]
 
@@ -269,12 +294,15 @@
     )
     both = lax.all_to_all(both, AXES, 0, 0, tiled=True, axis_index_groups=CORES)
 
-    ends = []
-    for kept, given, terms in ((keep, got[0], sums), (late_keep, send(late_give, core=1), added_by_core(swap, both))):
-        here, there = summed(side, kept, given, [send(terms[d - 1], **NEAR[d]) for d in range(1, 4)])
-        ends += [here, send(there, dhi=1)]
-
-    total = join((((z & 1) ^ swap[0]).reshape(1), (y ^ (2 * side[0])).reshape(1)), ends)
+    here, there = summed(side, keep, got[0], [send(sums[d - 1], **NEAR[d]) for d in range(1, 4)])
+    early_ends = here, send(there, dhi=1)
+
+    late_got, late_sums = send(late_give, core=1), added_by_core(swap, both)
+    terms = [send(late_sums[d - 1], **NEAR[d]) for d in range(1, 4)]
+    passed = send(onward(side, late_keep, late_got, terms), dhi=1)
+
+    scalars = ((z & 1) ^ swap[0]).reshape(1), (y ^ (2 * side[0])).reshape(1), side
+    total = join(scalars, early_ends, late_keep, late_got, terms, passed)
     return total.reshape(8 * rows, columns)
 
 

time: 139 us -> 142 us (1.022)
  waiting for transfers between devices: 63.4 us -> 57.5 us
  starting transfers between devices: 35.3 us -> 40.4 us
  local copies, waits for them, and re-layouts: 6.47 us -> 10.2 us
    ppermute x26, waiting for transfers between devices: 63.4 us -> 57.5 us  [send(): return lax.ppermute(value, AXES, pairs)]
    ppermute x26, starting transfers between devices: 35.3 us -> 40.4 us  [send(): return lax.ppermute(value, AXES, pairs)]
    unnamed x26 -> x30, local copies, waits for them, and re-layouts: 5.03 us -> 8.73 us
  transfers between devices with their start and end apart: 26 -> 26, of which waited for: 14 -> 12; matrix products, arithmetic and copies ran while one was open for 0% -> 0% of each run, Pallas kernels for 19% -> 18%
where the time goes in v17:
time: 142 us
  waiting for transfers between devices  57.5 us (40%)
  starting transfers between devices  40.4 us (28%)
  Pallas kernels  27.3 us (19%)
  local copies, waits for them, and re-layouts  10.2 us (7%)
  blocking collectives  6.26 us (4%)
    ppermute x26, waiting for transfers between devices, send(): return lax.ppermute(value, AXES, pairs)  57.5 us
    ppermute x26, starting transfers between devices, send(): return lax.ppermute(value, AXES, pairs)  40.4 us
    pallas_call x13, Pallas kernels, call(): pl.pallas_call(kernel, grid_spec=pltpu.PrefetchScalarGridSpec(num_scalar_...  27.3 us
    unnamed x30, local copies, waits for them, and re-layouts  8.73 us
    all_to_all x1, blocking collectives, per_device(): both = lax.all_to_all(both, AXES, 0, 0, tiled=True, axis_index_groups=CORES)  6.26 us
  transfers between devices with their start and end apart: 26, of which 12 were waited for; matrix products, arithmetic and copies ran while one was open for 0% of the time, Pallas kernels for 18%

profile of v17, /device:TPU:0, one launch (start us, length us, event | category | flops | bytes accessed | tf_op | source)
XLA Modules:
  0.0 141.9 jit_solution(5565073418302660714)
XLA Ops:
  0.0 1.4 %dynamic-slice_bitcast_fusion = (f32[1,64,1024]{2,1,0:T(8,128)S(1)}, f32[64,1024]{1,0:T(8,128)S(1)}, f32[64,1024]{1,0:T(8,128)S(1)}, f32[64,1024]{1,0:T(8,128)S(1)}) fusion(f32[64,4096]{1,0:T(8,128)} %param.2, s32[]{:T(128)S(6)} %select_n.12, s32[]{:T(128)S(6)} %select_n.13, s32[]{:T(128)S(6)} %select_n.15, s32[]{:T(128)S(6)} %select_n.14), kind=kLoop, calls=%fused_computation.1 | loop fusion | bytes 2097168 | tf_op jit(solution)/shard_map/stack | solution.py:274
  1.4 3.2 %collective-permute-start.2 = (f32[64,1024]{1,0:T(8,128)S(1)}, f32[64,1024]{1,0:T(8,128)S(1)}, u32[]{:S(2)}, u32[]{:S(2)}) collective-permute-start(f32[64,1024]{1,0:T(8,128)S(1)} %get-tuple-element.83), channel_id=1, source_target_pairs={{0,3},{1,2},{2,1},{3,0},{4,7},{5,6},{6,5},{7,4},{8,11},{9,10},{10,... | collective-permute-start | bytes 786440 | tf_op jit(solution)/shard_map/ppermute | solution.py:24
  4.6 0.6 collective-permute-start.1
  5.3 0.4 collective-permute-start
  5.6 10.9 %collective-permute-done.2 = f32[64,1024]{1,0:T(8,128)S(1)} collective-permute-done((f32[64,1024]{1,0:T(8,128)S(1)}, f32[64,1024]{1,0:T(8,128)S(1)}, u32[]{:S(2)}, u32[]{:S(2)}) %collective-permute-start.2) | collective-permute-done | bytes 262176 | tf_op jit(solution)/shard_map/ppermute | solution.py:24
  16.6 0.0 collective-permute-done.1
  16.6 0.7 collective-permute-done
  17.3 0.1 pad_maximum_fusion.refs_0_
  17.3 4.0 %collective-permute-start.3 = (f32[4,64,1024]{2,1,0:T(8,128)S(1)}, f32[4,64,1024]{2,1,0:T(8,128)S(1)}, u32[]{:S(2)}, u32[]{:S(2)}) collective-permute-start(f32[4,64,1024]{2,1,0:T(8,128)S(1)} %pad_maximum_fusion.refs_0_), channel_id=1, source_target_pairs={{0,18},{1,19},{2,16},{3,17},{4,22},{5,23},{6,20},{7,21},{8,26},{9,... | collective-permute-start | bytes 3145736 | tf_op jit(solution)/shard_map/ppermute | solution.py:24
  21.4 1.9 %collective-permute-start.4 = (f32[4,64,1024]{2,1,0:T(8,128)S(1)}, f32[4,64,1024]{2,1,0:T(8,128)S(1)}, u32[]{:S(2)}, u32[]{:S(2)}) collective-permute-start(f32[4,64,1024]{2,1,0:T(8,128)S(1)} %pad_maximum_fusion.refs_0_), channel_id=1, source_target_pairs={{0,4},{1,5},{2,6},{3,7},{4,0},{5,1},{6,2},{7,3},{8,12},{9,13},{10,... | collective-permute-start | bytes 3145736 | tf_op jit(solution)/shard_map/ppermute | solution.py:24
  23.3 2.5 %collective-permute-start.5 = (f32[4,64,1024]{2,1,0:T(8,128)S(1)}, f32[4,64,1024]{2,1,0:T(8,128)S(1)}, u32[]{:S(2)}, u32[]{:S(2)}) collective-permute-start(f32[4,64,1024]{2,1,0:T(8,128)S(1)} %pad_maximum_fusion.refs_0_), channel_id=1, source_target_pairs={{0,12},{1,13},{2,14},{3,15},{4,8},{5,9},{6,10},{7,11},{8,4},{9,5},... | collective-permute-start | bytes 3145736 | tf_op jit(solution)/shard_map/ppermute | solution.py:24
  25.8 18.0 %collective-permute-done.3._.refs_0_ = f32[4,64,1024]{2,1,0:T(8,128)S(1)} collective-permute-done((f32[4,64,1024]{2,1,0:T(8,128)S(1)}, f32[4,64,1024]{2,1,0:T(8,128)S(1)}, u32[]{:S(2)}, u32[]{:S(2)}) %collective-permute-start.3) | collective-permute-done | bytes 1048608 | tf_op jit(solution)/shard_map/ppermute | solution.py:24
  43.8 1.9 %shard_map.28 = (f32[1024,256]{1,0:T(8,128)S(1)}, f32[1024,256]{1,0:T(8,128)}, f32[1024,256]{1,0:T(8,128)}, f32[1024,256]{1,0:T(8,128)}) custom-call(s32[1]{0:T(128)} %bitcast.8.quarter, f32[4096,256]{1,0:T(8,128)S(1)} %copy-done, f32[4,64,1024]{2,1,0:T(8,128)S(1)} %collective-permute-done.3._.refs_0_), custom_call_target="tpu_custom_call" | custom-call | flops 1 | bytes 1 | tf_op jit(solution)/shard_map/pallas_call | solution.py:49
  45.8 0.9 copy-done.3
  46.7 1.0 copy-done.7
  47.7 1.8 %collective-permute-start.6 = (f32[4,64,1024]{2,1,0:T(8,128)S(1)}, f32[4,64,1024]{2,1,0:T(8,128)}, u32[]{:S(2)}, u32[]{:S(2)}) collective-permute-start(f32[4,64,1024]{2,1,0:T(8,128)S(1)} %collective-permute-done.3._.refs_0_), channel_id=1, source_target_pairs={{0,4},{1,5},{2,6},{3,7},{4,0},{5,1},{6,2},{7,3},{8,12},{9,13},{10,... | collective-permute-start | bytes 3145736 | tf_op jit(solution)/shard_map/ppermute | solution.py:24
  49.6 2.5 %collective-permute-start.7 = (f32[4,64,1024]{2,1,0:T(8,128)S(1)}, f32[4,64,1024]{2,1,0:T(8,128)}, u32[]{:S(2)}, u32[]{:S(2)}) collective-permute-start(f32[4,64,1024]{2,1,0:T(8,128)S(1)} %collective-permute-done.3._.refs_0_), channel_id=1, source_target_pairs={{0,12},{1,13},{2,14},{3,15},{4,8},{5,9},{6,10},{7,11},{8,4},{9,5},... | collective-permute-start | bytes 3145736 | tf_op jit(solution)/shard_map/ppermute | solution.py:24
  52.1 1.5 %collective-permute-start.8 = (f32[1024,256]{1,0:T(8,128)}, f32[1024,256]{1,0:T(8,128)}, u32[]{:S(2)}, u32[]{:S(2)}) collective-permute-start(f32[1024,256]{1,0:T(8,128)} %get-tuple-element.44), channel_id=1, source_target_pairs={{0,16},{1,17},{2,18},{3,19},{4,20},{5,21},{6,22},{7,23},{8,24},{9,... | collective-permute-start | bytes 3145736 | tf_op jit(solution)/shard_map/ppermute | solution.py:24
  53.6 1.3 collective-permute-start.9
  54.8 2.2 %collective-permute-start.10 = (f32[1024,256]{1,0:T(8,128)}, f32[1024,256]{1,0:T(8,128)S(1)}, u32[]{:S(2)}, u32[]{:S(2)}) collective-permute-start(f32[1024,256]{1,0:T(8,128)} %get-tuple-element.46), channel_id=1, source_target_pairs={{0,3},{1,2},{2,1},{3,0},{4,7},{5,6},{6,5},{7,4},{8,11},{9,10},{10,... | collective-permute-start | bytes 3145736 | tf_op jit(solution)/shard_map/ppermute | solution.py:24
  57.0 1.2 copy-done.4
  58.2 0.1 shard_map.29
  58.4 12.5 %collective-permute-done.6.refs_2_ = f32[4,64,1024]{2,1,0:T(8,128)} collective-permute-done((f32[4,64,1024]{2,1,0:T(8,128)S(1)}, f32[4,64,1024]{2,1,0:T(8,128)}, u32[]{:S(2)}, u32[]{:S(2)}) %collective-permute-start.6) | collective-permute-done | bytes 1048608 | tf_op jit(solution)/shard_map/ppermute | solution.py:24
  70.9 1.7 %collective-permute-start.19 = (f32[4,64,1024]{2,1,0:T(8,128)}, f32[4,64,1024]{2,1,0:T(8,128)S(1)}, u32[]{:S(2)}, u32[]{:S(2)}) collective-permute-start(f32[4,64,1024]{2,1,0:T(8,128)} %copy-done.5), channel_id=1, source_target_pairs={{0,4},{1,5},{2,6},{3,7},{4,0},{5,1},{6,2},{7,3},{8,12},{9,13},{10,... | collective-permute-start | bytes 3145736 | tf_op jit(solution)/shard_map/ppermute | solution.py:24
  72.7 0.9 collective-permute-done.7.refs_1_
  73.6 2.5 %collective-permute-start.20 = (f32[4,64,1024]{2,1,0:T(8,128)}, f32[4,64,1024]{2,1,0:T(8,128)S(1)}, u32[]{:S(2)}, u32[]{:S(2)}) collective-permute-start(f32[4,64,1024]{2,1,0:T(8,128)} %collective-permute-done.6.refs_2_), channel_id=1, source_target_pairs={{0,12},{1,13},{2,14},{3,15},{4,8},{5,9},{6,10},{7,11},{8,4},{9,5},... | collective-permute-start | bytes 3145736 | tf_op jit(solution)/shard_map/ppermute | solution.py:24
  76.1 1.4 shard_map.30
  77.5 1.4 shard_map.31
  78.9 0.1 shard_map.32
  79.1 5.1 %shard_map.33 = (f32[4,2,4,64,256]{4,3,2,1,0:T(8,128)S(1)}, f32[4,2,4,64,256]{4,3,2,1,0:T(8,128)S(1)}, f32[2,4,64,256]{3,2,1,0:T(8,128)S(1)}, f32[2,4,64,256]{3,...) custom-call(s32[1]{0:T(128)} %bitcast.3._.swap, ...), custom_call_target="tpu_custom_call" | custom-call | flops 1 | bytes 1 | tf_op jit(solution)/shard_map/pallas_call | solution.py:49
  84.1 6.6 %shard_map.34 = (f32[4,2,4,64,256]{4,3,2,1,0:T(8,128)S(1)}, f32[4,2,4,64,256]{4,3,2,1,0:T(8,128)S(1)}, f32[2,4,64,256]{3,2,1,0:T(8,128)S(1)}, f32[2,4,64,256]{3,...) custom-call(s32[1]{0:T(128)} %bitcast.3._.swap, ...), custom_call_target="tpu_custom_call", output_to_operand_aliasing={{0}: (4, {}), {1}: (5, {}), {2}: (6, {}), {3}: (7, {}), {4}... | custom-call | flops 1 | bytes 1 | tf_op jit(solution)/shard_map/pallas_call | solution.py:49
  90.7 0.1 collective-permute-start.12
  90.8 0.5 collective-permute-start.13
  91.3 0.1 collective-permute-start.14
  91.4 1.3 collective-permute-done.12.refs_0_
  92.7 0.1 collective-permute-start.11
  92.8 0.6 collective-permute-done.13.refs_1_
  93.4 0.7 collective-permute-done.14.refs_2_
  94.2 0.9 shard_map.35
  95.1 1.5 %collective-permute-start.15 = (f32[2,4,64,256]{3,2,1,0:T(8,128)S(1)}, f32[2,4,64,256]{3,2,1,0:T(8,128)S(1)}, u32[]{:S(2)}, u32[]{:S(2)}) collective-permute-start(f32[2,4,64,256]{3,2,1,0:T(8,128)S(1)} %get-tuple-element.69.refs_2_), channel_id=1, source_target_pairs={{0,16},{1,17},{2,18},{3,19},{4,20},{5,21},{6,22},{7,23},{8,24},{9,... | collective-permute-start | bytes 1572872 | tf_op jit(solution)/shard_map/ppermute | solution.py:24
  96.6 1.1 collective-permute-start.16
  97.7 2.2 %collective-permute-start.17 = (f32[2,4,64,256]{3,2,1,0:T(8,128)}, f32[2,4,64,256]{3,2,1,0:T(8,128)}, u32[]{:S(2)}, u32[]{:S(2)}) collective-permute-start(f32[2,4,64,256]{3,2,1,0:T(8,128)} %get-tuple-element.71.refs_4_), channel_id=1, source_target_pairs={{0,3},{1,2},{2,1},{3,0},{4,7},{5,6},{6,5},{7,4},{8,11},{9,10},{10,... | collective-permute-start | bytes 1572872 | tf_op jit(solution)/shard_map/ppermute | solution.py:24
  99.9 3.5 %shard_map.37 = (f32[1,2,4,64,256]{4,3,2,1,0:T(8,128)S(1)}, f32[2,4,64,256]{3,2,1,0:T(8,128)}, f32[2,3,2,4,64,256]{5,4,3,2,1,0:T(8,128)S(1)}) custom-call(s32[1]{0:T(128)} %bitcast.3._.swap, s32[1]{0:T(128)} %bitcast.9.at_core, f32[4,64,1024]{2,1,0:T(8,128)S(1)} %collective-permute-done.19.refs_0_, f32[4,64,1024]{2,1,0:T(8,128)S(1)} %collective-permute-done.20.refs_1_, ...), custom_call_target="tpu_custom_call" | custom-call | flops 1 | bytes 1 | tf_op jit(solution)/shard_map/pallas_call | solution.py:49
  103.4 0.1 collective-permute-start.21
  103.5 6.3 %all_to_all.5.both = f32[2,3,2,4,64,256]{5,4,3,2,1,0:T(8,128)S(1)} all-to-all(f32[2,3,2,4,64,256]{5,4,3,2,1,0:T(8,128)S(1)} %get-tuple-element.77), channel_id=1, replica_groups={{0,32},{1,33},{2,34},{3,35},{4,36},{5,37},{6,38},{7,39},{8,40},{9,41},{..., dimensions={0} | all-to-all | bytes 6291456 | tf_op jit(solution)/shard_map/all_to_all | solution.py:295
  109.8 1.3 shard_map.38
  111.1 0.8 copy-done.9
  111.9 0.5 collective-permute-start.22
  112.4 0.8 copy-done.11
  113.2 1.3 collective-permute-start.23
  114.5 0.8 copy-done.13
  115.3 0.6 collective-permute-start.24
  116.0 1.0 copy-done.10
  117.0 1.0 copy-done.12
  118.0 1.0 copy-done.14
  119.1 1.9 %shard_map.36 = (f32[4,64,256]{2,1,0:T(8,128)S(1)}, f32[4,64,256]{2,1,0:T(8,128)}) custom-call(s32[1]{0:T(128)} %bitcast.2.side._, f32[4,2,4,64,256]{4,3,2,1,0:T(8,128)S(1)} %get-tuple-element.64.keep, f32[2,4,64,256]{3,2,1,0:T(8,128)S(1)} %copy-done.10, f32[2,4,64,256]{3,2,1,0:T(8,128)S(1)} %copy-done.12, f32[2,4,64,256]{3,2,1,0:T(8,128)S(1)} %copy-done.14, ...), custom_call_target="tpu_custom_call" | custom-call | flops 1 | bytes 1 | tf_op jit(solution)/shard_map/pallas_call | solution.py:49
  120.9 3.0 %collective-permute-start.18 = (f32[4,64,256]{2,1,0:T(8,128)}, f32[4,64,256]{2,1,0:T(8,128)S(1)}, u32[]{:S(2)}, u32[]{:S(2)}) collective-permute-start(f32[4,64,256]{2,1,0:T(8,128)} %get-tuple-element.73), channel_id=1, source_target_pairs={{0,64},{1,65},{2,66},{3,67},{4,68},{5,69},{6,70},{7,71},{8,72},{9,... | collective-permute-start | bytes 786440 | tf_op jit(solution)/shard_map/ppermute | solution.py:24
  124.0 3.0 %collective-permute-done.22.across = f32[2,4,64,256]{3,2,1,0:T(8,128)} collective-permute-done((f32[2,4,64,256]{3,2,1,0:T(8,128)}, f32[2,4,64,256]{3,2,1,0:T(8,128)}, u32[]{:S(2)}, u32[]{:S(2)}) %collective-permute-start.22) | collective-permute-done | bytes 524320 | tf_op jit(solution)/shard_map/ppermute | solution.py:24
  127.0 0.3 collective-permute-done.23.two
  127.2 3.0 %collective-permute-done.24.three = f32[2,4,64,256]{3,2,1,0:T(8,128)} collective-permute-done((f32[2,4,64,256]{3,2,1,0:T(8,128)}, f32[2,4,64,256]{3,2,1,0:T(8,128)}, u32[]{:S(2)}, u32[]{:S(2)}) %collective-permute-start.24) | collective-permute-done | bytes 524320 | tf_op jit(solution)/shard_map/ppermute | solution.py:24
  130.3 1.2 shard_map.39
  131.4 3.1 %collective-permute-start.25 = (f32[4,64,256]{2,1,0:T(8,128)S(1)}, f32[4,64,256]{2,1,0:T(8,128)S(1)}, u32[]{:S(2)}, u32[]{:S(2)}) collective-permute-start(f32[4,64,256]{2,1,0:T(8,128)S(1)} %shard_map.39), channel_id=1, source_target_pairs={{0,64},{1,65},{2,66},{3,67},{4,68},{5,69},{6,70},{7,71},{8,72},{9,... | collective-permute-start | bytes 786440 | tf_op jit(solution)/shard_map/ppermute | solution.py:24
  134.6 5.3 %collective-permute-done.25.other_two = f32[4,64,256]{2,1,0:T(8,128)S(1)} collective-permute-done((f32[4,64,256]{2,1,0:T(8,128)S(1)}, f32[4,64,256]{2,1,0:T(8,128)S(1)}, u32[]{:S(2)}, u32[]{:S(2)}) %collective-permute-start.25) | collective-permute-done | bytes 262176 | tf_op jit(solution)/shard_map/ppermute | solution.py:24
  139.9 2.0 %shard_map.40 = f32[2,4,64,256]{3,2,1,0:T(8,128)} custom-call(s32[1]{0:T(128)} %bitcast.plane, s32[1]{0:T(128)} %bitcast.1.first, s32[1]{0:T(128)} %bitcast.2.side._, f32[4,64,256]{2,1,0:T(8,128)S(1)} %get-tuple-element.72.one, f32[4,64,256]{2,1,0:T(8,128)S(1)} %collective-permute-done.18.other_one, f32[1,2,4,64,256]{4,3,2,1,0:T(8,128)S(1)} %get-tuple-element.75.keep, ...), custom_call_target="tpu_custom_call" | custom-call | flops 1 | bytes 1 | tf_op jit(solution)/shard_map/pallas_call | solution.py:49
  (34 shorter events, 0.1 us)
Async XLA Ops:
  0.0 43.8 %copy-start = (f32[4096,256]{1,0:T(8,128)S(1)}, f32[4096,256]{1,0:T(8,128)}, u32[]{:S(2)}) copy-start(f32[4096,256]{1,0:T(8,128)} %value.1) | copy-start | bytes 12582916
  1.4 15.1 %collective-permute-start.2 = (f32[64,1024]{1,0:T(8,128)S(1)}, f32[64,1024]{1,0:T(8,128)S(1)}, u32[]{:S(2)}, u32[]{:S(2)}) collective-permute-start(f32[64,1024]{1,0:T(8,128)S(1)} %get-tuple-element.83), channel_id=1, source_target_pairs={{0,3},{1,2},{2,1},{3,0},{4,7},{5,6},{6,5},{7,4},{8,11},{9,10},{10,... | collective-permute-start | bytes 786440 | tf_op jit(solution)/shard_map/ppermute | solution.py:24
  4.6 11.9 %collective-permute-start.1 = (f32[64,1024]{1,0:T(8,128)S(1)}, f32[64,1024]{1,0:T(8,128)S(1)}, u32[]{:S(2)}, u32[]{:S(2)}) collective-permute-start(f32[64,1024]{1,0:T(8,128)S(1)} %get-tuple-element.84), channel_id=1, source_target_pairs={{0,2},{1,3},{2,0},{3,1},{4,6},{5,7},{6,4},{7,5},{8,10},{9,11},{10,... | collective-permute-start | bytes 786440 | tf_op jit(solution)/shard_map/ppermute | solution.py:24
  5.3 12.0 %collective-permute-start = (f32[64,1024]{1,0:T(8,128)S(1)}, f32[64,1024]{1,0:T(8,128)S(1)}, u32[]{:S(2)}, u32[]{:S(2)}) collective-permute-start(f32[64,1024]{1,0:T(8,128)S(1)} %get-tuple-element.82), channel_id=1, source_target_pairs={{0,1},{1,0},{2,3},{3,2},{4,5},{5,4},{6,7},{7,6},{8,9},{9,8},{10,11... | collective-permute-start | bytes 786440 | tf_op jit(solution)/shard_map/ppermute | solution.py:24
  17.3 26.5 %collective-permute-start.3 = (f32[4,64,1024]{2,1,0:T(8,128)S(1)}, f32[4,64,1024]{2,1,0:T(8,128)S(1)}, u32[]{:S(2)}, u32[]{:S(2)}) collective-permute-start(f32[4,64,1024]{2,1,0:T(8,128)S(1)} %pad_maximum_fusion.refs_0_), channel_id=1, source_target_pairs={{0,18},{1,19},{2,16},{3,17},{4,22},{5,23},{6,20},{7,21},{8,26},{9,... | collective-permute-start | bytes 3145736 | tf_op jit(solution)/shard_map/ppermute | solution.py:24
  21.4 25.3 %collective-permute-start.4 = (f32[4,64,1024]{2,1,0:T(8,128)S(1)}, f32[4,64,1024]{2,1,0:T(8,128)S(1)}, u32[]{:S(2)}, u32[]{:S(2)}) collective-permute-start(f32[4,64,1024]{2,1,0:T(8,128)S(1)} %pad_maximum_fusion.refs_0_), channel_id=1, source_target_pairs={{0,4},{1,5},{2,6},{3,7},{4,0},{5,1},{6,2},{7,3},{8,12},{9,13},{10,... | collective-permute-start | bytes 3145736 | tf_op jit(solution)/shard_map/ppermute | solution.py:24
  23.3 24.4 %collective-permute-start.5 = (f32[4,64,1024]{2,1,0:T(8,128)S(1)}, f32[4,64,1024]{2,1,0:T(8,128)S(1)}, u32[]{:S(2)}, u32[]{:S(2)}) collective-permute-start(f32[4,64,1024]{2,1,0:T(8,128)S(1)} %pad_maximum_fusion.refs_0_), channel_id=1, source_target_pairs={{0,12},{1,13},{2,14},{3,15},{4,8},{5,9},{6,10},{7,11},{8,4},{9,5},... | collective-permute-start | bytes 3145736 | tf_op jit(solution)/shard_map/ppermute | solution.py:24
  43.8 5.7 %copy-start.1 = (f32[4,64,1024]{2,1,0:T(8,128)}, f32[4,64,1024]{2,1,0:T(8,128)S(1)}, u32[]{:S(2)}) copy-start(f32[4,64,1024]{2,1,0:T(8,128)S(1)} %collective-permute-done.3._.refs_0_) | copy-start | bytes 3145732
  45.8 1.0 copy-start.3
  46.7 1.0 copy-start.7
  47.7 5.8 %copy-start.5 = (f32[4,64,1024]{2,1,0:T(8,128)}, f32[4,64,1024]{2,1,0:T(8,128)S(1)}, u32[]{:S(2)}) copy-start(f32[4,64,1024]{2,1,0:T(8,128)S(1)} %collective-permute-done.5.refs_1_) | copy-start | bytes 3145732
  47.7 23.2 %collective-permute-start.6 = (f32[4,64,1024]{2,1,0:T(8,128)S(1)}, f32[4,64,1024]{2,1,0:T(8,128)}, u32[]{:S(2)}, u32[]{:S(2)}) collective-permute-start(f32[4,64,1024]{2,1,0:T(8,128)S(1)} %collective-permute-done.3._.refs_0_), channel_id=1, source_target_pairs={{0,4},{1,5},{2,6},{3,7},{4,0},{5,1},{6,2},{7,3},{8,12},{9,13},{10,... | collective-permute-start | bytes 3145736 | tf_op jit(solution)/shard_map/ppermute | solution.py:24
  49.6 24.0 %collective-permute-start.7 = (f32[4,64,1024]{2,1,0:T(8,128)S(1)}, f32[4,64,1024]{2,1,0:T(8,128)}, u32[]{:S(2)}, u32[]{:S(2)}) collective-permute-start(f32[4,64,1024]{2,1,0:T(8,128)S(1)} %collective-permute-done.3._.refs_0_), channel_id=1, source_target_pairs={{0,12},{1,13},{2,14},{3,15},{4,8},{5,9},{6,10},{7,11},{8,4},{9,5},... | collective-permute-start | bytes 3145736 | tf_op jit(solution)/shard_map/ppermute | solution.py:24
  52.1 24.0 %collective-permute-start.8 = (f32[1024,256]{1,0:T(8,128)}, f32[1024,256]{1,0:T(8,128)}, u32[]{:S(2)}, u32[]{:S(2)}) collective-permute-start(f32[1024,256]{1,0:T(8,128)} %get-tuple-element.44), channel_id=1, source_target_pairs={{0,16},{1,17},{2,18},{3,19},{4,20},{5,21},{6,22},{7,23},{8,24},{9,... | collective-permute-start | bytes 3145736 | tf_op jit(solution)/shard_map/ppermute | solution.py:24
  53.6 23.9 %collective-permute-start.9 = (f32[1024,256]{1,0:T(8,128)}, f32[1024,256]{1,0:T(8,128)}, u32[]{:S(2)}, u32[]{:S(2)}) collective-permute-start(f32[1024,256]{1,0:T(8,128)} %get-tuple-element.45), channel_id=1, source_target_pairs={{0,1},{1,0},{2,3},{3,2},{4,5},{5,4},{6,7},{7,6},{8,9},{9,8},{10,11... | collective-permute-start | bytes 3145736 | tf_op jit(solution)/shard_map/ppermute | solution.py:24
  54.8 24.0 %collective-permute-start.10 = (f32[1024,256]{1,0:T(8,128)}, f32[1024,256]{1,0:T(8,128)S(1)}, u32[]{:S(2)}, u32[]{:S(2)}) collective-permute-start(f32[1024,256]{1,0:T(8,128)} %get-tuple-element.46), channel_id=1, source_target_pairs={{0,3},{1,2},{2,1},{3,0},{4,7},{5,6},{6,5},{7,4},{8,11},{9,10},{10,... | collective-permute-start | bytes 3145736 | tf_op jit(solution)/shard_map/ppermute | solution.py:24
  57.0 1.2 copy-start.4
  58.2 20.8 %copy-start.6 = (f32[4,64,1024]{2,1,0:T(8,128)S(1)}, f32[4,64,1024]{2,1,0:T(8,128)}, u32[]{:S(2)}) copy-start(f32[4,64,1024]{2,1,0:T(8,128)} %copy-done.5) | copy-start | bytes 3145732
  58.2 20.8 %copy-start.8 = (f32[4,64,1024]{2,1,0:T(8,128)S(1)}, f32[4,64,1024]{2,1,0:T(8,128)}, u32[]{:S(2)}) copy-start(f32[4,64,1024]{2,1,0:T(8,128)} %copy-done.7) | copy-start | bytes 3145732
  70.9 26.8 %collective-permute-start.19 = (f32[4,64,1024]{2,1,0:T(8,128)}, f32[4,64,1024]{2,1,0:T(8,128)S(1)}, u32[]{:S(2)}, u32[]{:S(2)}) collective-permute-start(f32[4,64,1024]{2,1,0:T(8,128)} %copy-done.5), channel_id=1, source_target_pairs={{0,4},{1,5},{2,6},{3,7},{4,0},{5,1},{6,2},{7,3},{8,12},{9,13},{10,... | collective-permute-start | bytes 3145736 | tf_op jit(solution)/shard_map/ppermute | solution.py:24
  73.6 26.3 %collective-permute-start.20 = (f32[4,64,1024]{2,1,0:T(8,128)}, f32[4,64,1024]{2,1,0:T(8,128)S(1)}, u32[]{:S(2)}, u32[]{:S(2)}) collective-permute-start(f32[4,64,1024]{2,1,0:T(8,128)} %collective-permute-done.6.refs_2_), channel_id=1, source_target_pairs={{0,12},{1,13},{2,14},{3,15},{4,8},{5,9},{6,10},{7,11},{8,4},{9,5},... | collective-permute-start | bytes 3145736 | tf_op jit(solution)/shard_map/ppermute | solution.py:24
  79.0 5.1 %copy-start.2 = (f32[4,64,1024]{2,1,0:T(8,128)S(1)}, f32[4,64,1024]{2,1,0:T(8,128)}, u32[]{:S(2)}) copy-start(f32[4,64,1024]{2,1,0:T(8,128)} %copy-done.1) | copy-start | bytes 3145732
  90.7 2.0 %collective-permute-start.12 = (f32[2,4,64,256]{3,2,1,0:T(8,128)S(1)}, f32[2,4,64,256]{3,2,1,0:T(8,128)S(1)}, u32[]{:S(2)}, u32[]{:S(2)}) collective-permute-start(f32[2,4,64,256]{3,2,1,0:T(8,128)S(1)} %get-tuple-element.66), channel_id=1, source_target_pairs={{0,32},{1,33},{2,34},{3,35},{4,36},{5,37},{6,38},{7,39},{8,40},{9,... | collective-permute-start | bytes 1572872 | tf_op jit(solution)/shard_map/ppermute | solution.py:24
  90.8 2.6 %collective-permute-start.13 = (f32[2,4,64,256]{3,2,1,0:T(8,128)S(1)}, f32[2,4,64,256]{3,2,1,0:T(8,128)S(1)}, u32[]{:S(2)}, u32[]{:S(2)}) collective-permute-start(f32[2,4,64,256]{3,2,1,0:T(8,128)S(1)} %get-tuple-element.67), channel_id=1, source_target_pairs={{0,32},{1,33},{2,34},{3,35},{4,36},{5,37},{6,38},{7,39},{8,40},{9,... | collective-permute-start | bytes 1572872 | tf_op jit(solution)/shard_map/ppermute | solution.py:24
  91.3 2.9 %collective-permute-start.14 = (f32[2,4,64,256]{3,2,1,0:T(8,128)S(1)}, f32[2,4,64,256]{3,2,1,0:T(8,128)S(1)}, u32[]{:S(2)}, u32[]{:S(2)}) collective-permute-start(f32[2,4,64,256]{3,2,1,0:T(8,128)S(1)} %get-tuple-element.68), channel_id=1, source_target_pairs={{0,32},{1,33},{2,34},{3,35},{4,36},{5,37},{6,38},{7,39},{8,40},{9,... | collective-permute-start | bytes 1572872 | tf_op jit(solution)/shard_map/ppermute | solution.py:24
  92.7 18.4 %collective-permute-start.11 = (f32[2,4,64,256]{3,2,1,0:T(8,128)S(1)}, f32[2,4,64,256]{3,2,1,0:T(8,128)S(1)}, u32[]{:S(2)}, u32[]{:S(2)}) collective-permute-start(f32[2,4,64,256]{3,2,1,0:T(8,128)S(1)} %get-tuple-element.65), channel_id=1, source_target_pairs={{0,32},{1,33},{2,34},{3,35},{4,36},{5,37},{6,38},{7,39},{8,40},{9,... | collective-permute-start | bytes 1572872 | tf_op jit(solution)/shard_map/ppermute | solution.py:24
  95.1 17.3 %collective-permute-start.15 = (f32[2,4,64,256]{3,2,1,0:T(8,128)S(1)}, f32[2,4,64,256]{3,2,1,0:T(8,128)S(1)}, u32[]{:S(2)}, u32[]{:S(2)}) collective-permute-start(f32[2,4,64,256]{3,2,1,0:T(8,128)S(1)} %get-tuple-element.69.refs_2_), channel_id=1, source_target_pairs={{0,16},{1,17},{2,18},{3,19},{4,20},{5,21},{6,22},{7,23},{8,24},{9,... | collective-permute-start | bytes 1572872 | tf_op jit(solution)/shard_map/ppermute | solution.py:24
  96.6 17.9 %collective-permute-start.16 = (f32[2,4,64,256]{3,2,1,0:T(8,128)S(1)}, f32[2,4,64,256]{3,2,1,0:T(8,128)S(1)}, u32[]{:S(2)}, u32[]{:S(2)}) collective-permute-start(f32[2,4,64,256]{3,2,1,0:T(8,128)S(1)} %get-tuple-element.70.refs_3_), channel_id=1, source_target_pairs={{0,1},{1,0},{2,3},{3,2},{4,5},{5,4},{6,7},{7,6},{8,9},{9,8},{10,11... | collective-permute-start | bytes 1572872 | tf_op jit(solution)/shard_map/ppermute | solution.py:24
  97.7 18.2 %collective-permute-start.17 = (f32[2,4,64,256]{3,2,1,0:T(8,128)}, f32[2,4,64,256]{3,2,1,0:T(8,128)}, u32[]{:S(2)}, u32[]{:S(2)}) collective-permute-start(f32[2,4,64,256]{3,2,1,0:T(8,128)} %get-tuple-element.71.refs_4_), channel_id=1, source_target_pairs={{0,3},{1,2},{2,1},{3,0},{4,7},{5,6},{6,5},{7,4},{8,11},{9,10},{10,... | collective-permute-start | bytes 1572872 | tf_op jit(solution)/shard_map/ppermute | solution.py:24
  103.4 20.6 %collective-permute-start.21 = (f32[2,4,64,256]{3,2,1,0:T(8,128)}, f32[2,4,64,256]{3,2,1,0:T(8,128)S(1)}, u32[]{:S(2)}, u32[]{:S(2)}) collective-permute-start(f32[2,4,64,256]{3,2,1,0:T(8,128)} %get-tuple-element.76), channel_id=1, source_target_pairs={{0,32},{1,33},{2,34},{3,35},{4,36},{5,37},{6,38},{7,39},{8,40},{9,... | collective-permute-start | bytes 1572872 | tf_op jit(solution)/shard_map/ppermute | solution.py:24
  111.1 0.8 copy-start.9
  111.9 15.1 %collective-permute-start.22 = (f32[2,4,64,256]{3,2,1,0:T(8,128)}, f32[2,4,64,256]{3,2,1,0:T(8,128)}, u32[]{:S(2)}, u32[]{:S(2)}) collective-permute-start(f32[2,4,64,256]{3,2,1,0:T(8,128)} %get-tuple-element.78), channel_id=1, source_target_pairs={{0,16},{1,17},{2,18},{3,19},{4,20},{5,21},{6,22},{7,23},{8,24},{9,... | collective-permute-start | bytes 1572872 | tf_op jit(solution)/shard_map/ppermute | solution.py:24
  112.4 0.8 copy-start.11
  113.2 14.0 %collective-permute-start.23 = (f32[2,4,64,256]{3,2,1,0:T(8,128)}, f32[2,4,64,256]{3,2,1,0:T(8,128)}, u32[]{:S(2)}, u32[]{:S(2)}) collective-permute-start(f32[2,4,64,256]{3,2,1,0:T(8,128)} %get-tuple-element.79), channel_id=1, source_target_pairs={{0,1},{1,0},{2,3},{3,2},{4,5},{5,4},{6,7},{7,6},{8,9},{9,8},{10,11... | collective-permute-start | bytes 1572872 | tf_op jit(solution)/shard_map/ppermute | solution.py:24
  114.5 0.8 copy-start.13
  115.3 14.9 %collective-permute-start.24 = (f32[2,4,64,256]{3,2,1,0:T(8,128)}, f32[2,4,64,256]{3,2,1,0:T(8,128)}, u32[]{:S(2)}, u32[]{:S(2)}) collective-permute-start(f32[2,4,64,256]{3,2,1,0:T(8,128)} %get-tuple-element.80), channel_id=1, source_target_pairs={{0,3},{1,2},{2,1},{3,0},{4,7},{5,6},{6,5},{7,4},{8,11},{9,10},{10,... | collective-permute-start | bytes 1572872 | tf_op jit(solution)/shard_map/ppermute | solution.py:24
  116.0 1.0 copy-start.10
  117.0 1.0 copy-start.12
  118.0 1.0 copy-start.14
  120.9 13.6 %collective-permute-start.18 = (f32[4,64,256]{2,1,0:T(8,128)}, f32[4,64,256]{2,1,0:T(8,128)S(1)}, u32[]{:S(2)}, u32[]{:S(2)}) collective-permute-start(f32[4,64,256]{2,1,0:T(8,128)} %get-tuple-element.73), channel_id=1, source_target_pairs={{0,64},{1,65},{2,66},{3,67},{4,68},{5,69},{6,70},{7,71},{8,72},{9,... | collective-permute-start | bytes 786440 | tf_op jit(solution)/shard_map/ppermute | solution.py:24
  131.4 8.5 %collective-permute-start.25 = (f32[4,64,256]{2,1,0:T(8,128)S(1)}, f32[4,64,256]{2,1,0:T(8,128)S(1)}, u32[]{:S(2)}, u32[]{:S(2)}) collective-permute-start(f32[4,64,256]{2,1,0:T(8,128)S(1)} %shard_map.39), channel_id=1, source_target_pairs={{0,64},{1,65},{2,66},{3,67},{4,68},{5,69},{6,70},{7,71},{8,72},{9,... | collective-permute-start | bytes 786440 | tf_op jit(solution)/shard_map/ppermute | solution.py:24

commit v18 on v16

--- a/solution.py
+++ b/solution.py
@@ -6,7 +6,7 @@
 from jax.sharding import PartitionSpec as P
 
 AXES = ("rep", "grid")
-PARAMS = pltpu.CompilerParams(vmem_limit_bytes=20 * 1024 * 1024)
+PARAMS = pltpu.CompilerParams(vmem_limit_bytes=15 * 1024 * 1024)
 SHORT = pl.CostEstimate(flops=1, bytes_accessed=1, transcendentals=0)
 NEAR = (dict(), dict(dx=1), dict(dy=1), dict(dy=3))
 DIFFERS = (0, 3, 1, 2)

time: 139 us -> 139 us (level)
  no operation moved by 1% of the time
where the time goes in v18:
time: 139 us; the launch traced here: 138 us
  waiting for transfers between devices  63.4 us (46%)
  starting transfers between devices  35.3 us (25%)
  Pallas kernels  26.6 us (19%)
  local copies, waits for them, and re-layouts  6.47 us (5%)
  blocking collectives  6.26 us (5%)
    ppermute x26, waiting for transfers between devices, send(): return lax.ppermute(value, AXES, pairs)  63.4 us
    ppermute x26, starting transfers between devices, send(): return lax.ppermute(value, AXES, pairs)  35.3 us
    pallas_call x13, Pallas kernels, call(): pl.pallas_call(kernel, grid_spec=pltpu.PrefetchScalarGridSpec(num_scalar_...  26.6 us
    all_to_all x1, blocking collectives, per_device(): both = lax.all_to_all(both, AXES, 0, 0, tiled=True, axis_index_groups=CORES)  6.26 us
    unnamed x26, local copies, waits for them, and re-layouts  5.03 us
  transfers between devices with their start and end apart: 26, of which 14 were waited for; matrix products, arithmetic and copies ran while one was open for 0% of the time, Pallas kernels for 19%

profile of v18, /device:TPU:0, one launch (start us, length us, event | category | flops | bytes accessed | tf_op | source)
XLA Modules:
  0.0 138.2 jit_solution(17496338933613392636)
XLA Ops:
  0.0 1.4 %dynamic-slice_bitcast_fusion = (f32[1,64,1024]{2,1,0:T(8,128)S(1)}, f32[64,1024]{1,0:T(8,128)S(1)}, f32[64,1024]{1,0:T(8,128)S(1)}, f32[64,1024]{1,0:T(8,128)S(1)}) fusion(f32[64,4096]{1,0:T(8,128)} %param.2, s32[]{:T(128)S(6)} %select_n.12, s32[]{:T(128)S(6)} %select_n.13, s32[]{:T(128)S(6)} %select_n.15, s32[]{:T(128)S(6)} %select_n.14), kind=kLoop, calls=%fused_computation.1 | loop fusion | bytes 2097168 | tf_op jit(solution)/shard_map/stack | solution.py:249
  1.4 3.2 %collective-permute-start.2 = (f32[64,1024]{1,0:T(8,128)S(1)}, f32[64,1024]{1,0:T(8,128)S(1)}, u32[]{:S(2)}, u32[]{:S(2)}) collective-permute-start(f32[64,1024]{1,0:T(8,128)S(1)} %get-tuple-element.87), channel_id=1, source_target_pairs={{0,3},{1,2},{2,1},{3,0},{4,7},{5,6},{6,5},{7,4},{8,11},{9,10},{10,... | collective-permute-start | bytes 786440 | tf_op jit(solution)/shard_map/ppermute | solution.py:24
  4.6 0.6 collective-permute-start.1
  5.3 0.4 collective-permute-start
  5.6 10.9 %collective-permute-done.2 = f32[64,1024]{1,0:T(8,128)S(1)} collective-permute-done((f32[64,1024]{1,0:T(8,128)S(1)}, f32[64,1024]{1,0:T(8,128)S(1)}, u32[]{:S(2)}, u32[]{:S(2)}) %collective-permute-start.2) | collective-permute-done | bytes 262176 | tf_op jit(solution)/shard_map/ppermute | solution.py:24
  16.6 0.0 collective-permute-done.1
  16.6 0.7 collective-permute-done
  17.3 0.1 pad_maximum_fusion.refs_0_
  17.3 4.0 %collective-permute-start.3 = (f32[4,64,1024]{2,1,0:T(8,128)S(1)}, f32[4,64,1024]{2,1,0:T(8,128)S(1)}, u32[]{:S(2)}, u32[]{:S(2)}) collective-permute-start(f32[4,64,1024]{2,1,0:T(8,128)S(1)} %pad_maximum_fusion.refs_0_), channel_id=1, source_target_pairs={{0,18},{1,19},{2,16},{3,17},{4,22},{5,23},{6,20},{7,21},{8,26},{9,... | collective-permute-start | bytes 3145736 | tf_op jit(solution)/shard_map/ppermute | solution.py:24
  21.4 1.9 %collective-permute-start.4 = (f32[4,64,1024]{2,1,0:T(8,128)S(1)}, f32[4,64,1024]{2,1,0:T(8,128)S(1)}, u32[]{:S(2)}, u32[]{:S(2)}) collective-permute-start(f32[4,64,1024]{2,1,0:T(8,128)S(1)} %pad_maximum_fusion.refs_0_), channel_id=1, source_target_pairs={{0,4},{1,5},{2,6},{3,7},{4,0},{5,1},{6,2},{7,3},{8,12},{9,13},{10,... | collective-permute-start | bytes 3145736 | tf_op jit(solution)/shard_map/ppermute | solution.py:24
  23.3 2.5 %collective-permute-start.5 = (f32[4,64,1024]{2,1,0:T(8,128)S(1)}, f32[4,64,1024]{2,1,0:T(8,128)S(1)}, u32[]{:S(2)}, u32[]{:S(2)}) collective-permute-start(f32[4,64,1024]{2,1,0:T(8,128)S(1)} %pad_maximum_fusion.refs_0_), channel_id=1, source_target_pairs={{0,12},{1,13},{2,14},{3,15},{4,8},{5,9},{6,10},{7,11},{8,4},{9,5},... | collective-permute-start | bytes 3145736 | tf_op jit(solution)/shard_map/ppermute | solution.py:24
  25.8 18.0 %collective-permute-done.3._.refs_0_ = f32[4,64,1024]{2,1,0:T(8,128)S(1)} collective-permute-done((f32[4,64,1024]{2,1,0:T(8,128)S(1)}, f32[4,64,1024]{2,1,0:T(8,128)S(1)}, u32[]{:S(2)}, u32[]{:S(2)}) %collective-permute-start.3) | collective-permute-done | bytes 1048608 | tf_op jit(solution)/shard_map/ppermute | solution.py:24
  43.8 1.2 collective-permute-done.4.refs_2_
  45.0 1.0 copy-done.7
  46.0 1.7 %collective-permute-done.5.refs_1_ = f32[4,64,1024]{2,1,0:T(8,128)S(1)} collective-permute-done((f32[4,64,1024]{2,1,0:T(8,128)S(1)}, f32[4,64,1024]{2,1,0:T(8,128)S(1)}, u32[]{:S(2)}, u32[]{:S(2)}) %collective-permute-start.5) | collective-permute-done | bytes 1048608 | tf_op jit(solution)/shard_map/ppermute | solution.py:24
  47.7 0.6 collective-permute-start.6
  48.3 2.3 %collective-permute-start.7 = (f32[4,64,1024]{2,1,0:T(8,128)S(1)}, f32[4,64,1024]{2,1,0:T(8,128)}, u32[]{:S(2)}, u32[]{:S(2)}) collective-permute-start(f32[4,64,1024]{2,1,0:T(8,128)S(1)} %collective-permute-done.3._.refs_0_), channel_id=1, source_target_pairs={{0,12},{1,13},{2,14},{3,15},{4,8},{5,9},{6,10},{7,11},{8,4},{9,5},... | collective-permute-start | bytes 3145736 | tf_op jit(solution)/shard_map/ppermute | solution.py:24
  50.7 1.8 %shard_map.28 = (f32[1024,256]{1,0:T(8,128)S(1)}, f32[1024,256]{1,0:T(8,128)}, f32[1024,256]{1,0:T(8,128)}, f32[1024,256]{1,0:T(8,128)}) custom-call(s32[1]{0:T(128)} %bitcast.8.quarter, f32[4096,256]{1,0:T(8,128)S(1)} %copy-done, f32[4,64,1024]{2,1,0:T(8,128)S(1)} %collective-permute-done.3._.refs_0_), custom_call_target="tpu_custom_call" | custom-call | flops 1 | bytes 1 | tf_op jit(solution)/shard_map/pallas_call | solution.py:49
  52.4 0.9 copy-done.3
  53.4 0.5 collective-permute-start.8
  53.9 1.0 collective-permute-start.9
  54.9 2.0 %collective-permute-start.10 = (f32[1024,256]{1,0:T(8,128)}, f32[1024,256]{1,0:T(8,128)S(1)}, u32[]{:S(2)}, u32[]{:S(2)}) collective-permute-start(f32[1024,256]{1,0:T(8,128)} %get-tuple-element.57), channel_id=1, source_target_pairs={{0,3},{1,2},{2,1},{3,0},{4,7},{5,6},{6,5},{7,4},{8,11},{9,10},{10,... | collective-permute-start | bytes 3145736 | tf_op jit(solution)/shard_map/ppermute | solution.py:24
  56.9 1.2 copy-done.4
  58.1 0.1 shard_map.29
  58.3 12.6 %collective-permute-done.6.refs_2_ = f32[4,64,1024]{2,1,0:T(8,128)} collective-permute-done((f32[4,64,1024]{2,1,0:T(8,128)S(1)}, f32[4,64,1024]{2,1,0:T(8,128)}, u32[]{:S(2)}, u32[]{:S(2)}) %collective-permute-start.6) | collective-permute-done | bytes 1048608 | tf_op jit(solution)/shard_map/ppermute | solution.py:24
  70.8 0.6 collective-permute-start.19
  71.4 0.5 collective-permute-done.7.refs_1_
  71.9 2.1 %collective-permute-start.20 = (f32[4,64,1024]{2,1,0:T(8,128)}, f32[4,64,1024]{2,1,0:T(8,128)S(1)}, u32[]{:S(2)}, u32[]{:S(2)}) collective-permute-start(f32[4,64,1024]{2,1,0:T(8,128)} %collective-permute-done.6.refs_2_), channel_id=1, source_target_pairs={{0,12},{1,13},{2,14},{3,15},{4,8},{5,9},{6,10},{7,11},{8,4},{9,5},... | collective-permute-start | bytes 3145736 | tf_op jit(solution)/shard_map/ppermute | solution.py:24
  74.0 1.5 %collective-permute-done.8.refs_0_ = f32[1024,256]{1,0:T(8,128)} collective-permute-done((f32[1024,256]{1,0:T(8,128)}, f32[1024,256]{1,0:T(8,128)}, u32[]{:S(2)}, u32[]{:S(2)}) %collective-permute-start.8) | collective-permute-done | bytes 1048608 | tf_op jit(solution)/shard_map/ppermute | solution.py:24
  75.4 1.4 shard_map.30
  76.8 0.0 collective-permute-done.9.refs_0_
  76.8 1.4 shard_map.31
  78.2 0.0 collective-permute-done.10.refs_0_
  78.2 0.1 shard_map.32
  78.3 5.1 %shard_map.33 = (f32[4,2,4,64,256]{4,3,2,1,0:T(8,128)S(1)}, f32[4,2,4,64,256]{4,3,2,1,0:T(8,128)S(1)}, f32[2,4,64,256]{3,2,1,0:T(8,128)S(1)}, f32[2,4,64,256]{3,...) custom-call(s32[1]{0:T(128)} %bitcast.3._.swap, ...), custom_call_target="tpu_custom_call" | custom-call | flops 1 | bytes 1 | tf_op jit(solution)/shard_map/pallas_call | solution.py:49
  83.4 6.6 %shard_map.34 = (f32[4,2,4,64,256]{4,3,2,1,0:T(8,128)S(1)}, f32[4,2,4,64,256]{4,3,2,1,0:T(8,128)S(1)}, f32[2,4,64,256]{3,2,1,0:T(8,128)S(1)}, f32[2,4,64,256]{3,...) custom-call(s32[1]{0:T(128)} %bitcast.3._.swap, ...), custom_call_target="tpu_custom_call", output_to_operand_aliasing={{0}: (4, {}), {1}: (5, {}), {2}: (6, {}), {3}: (7, {}), {4}... | custom-call | flops 1 | bytes 1 | tf_op jit(solution)/shard_map/pallas_call | solution.py:49
  90.0 0.1 collective-permute-start.12
  90.1 0.5 collective-permute-start.13
  90.6 0.1 collective-permute-start.14
  90.7 1.3 collective-permute-done.12.refs_0_
  92.0 0.1 collective-permute-start.11
  92.1 0.6 collective-permute-done.13.refs_1_
  92.7 0.7 collective-permute-done.14.refs_2_
  93.5 1.0 shard_map.35
  94.4 1.1 collective-permute-start.15
  95.5 0.8 collective-permute-start.16
  96.3 2.2 %collective-permute-start.17 = (f32[2,4,64,256]{3,2,1,0:T(8,128)}, f32[2,4,64,256]{3,2,1,0:T(8,128)}, u32[]{:S(2)}, u32[]{:S(2)}) collective-permute-start(f32[2,4,64,256]{3,2,1,0:T(8,128)} %get-tuple-element.73.refs_4_), channel_id=1, source_target_pairs={{0,3},{1,2},{2,1},{3,0},{4,7},{5,6},{6,5},{7,4},{8,11},{9,10},{10,... | collective-permute-start | bytes 1572872 | tf_op jit(solution)/shard_map/ppermute | solution.py:24
  98.5 3.5 %shard_map.37 = (f32[1,2,4,64,256]{4,3,2,1,0:T(8,128)S(1)}, f32[2,4,64,256]{3,2,1,0:T(8,128)}, f32[2,3,2,4,64,256]{5,4,3,2,1,0:T(8,128)S(1)}) custom-call(s32[1]{0:T(128)} %bitcast.3._.swap, s32[1]{0:T(128)} %bitcast.9.at_core, f32[4,64,1024]{2,1,0:T(8,128)S(1)} %collective-permute-done.19.refs_0_, f32[4,64,1024]{2,1,0:T(8,128)S(1)} %collective-permute-done.20.refs_1_, ...), custom_call_target="tpu_custom_call" | custom-call | flops 1 | bytes 1 | tf_op jit(solution)/shard_map/pallas_call | solution.py:49
  102.0 0.1 collective-permute-start.21
  102.1 6.3 %all_to_all.5.both = f32[2,3,2,4,64,256]{5,4,3,2,1,0:T(8,128)S(1)} all-to-all(f32[2,3,2,4,64,256]{5,4,3,2,1,0:T(8,128)S(1)} %get-tuple-element.79), channel_id=1, replica_groups={{0,32},{1,33},{2,34},{3,35},{4,36},{5,37},{6,38},{7,39},{8,40},{9,41},{..., dimensions={0} | all-to-all | bytes 6291456 | tf_op jit(solution)/shard_map/all_to_all | solution.py:270
  108.4 1.3 shard_map.38
  109.7 0.5 collective-permute-start.22
  110.2 1.3 collective-permute-start.23
  111.5 0.8 copy-done.9
  112.4 0.8 collective-permute-start.24
  113.2 1.0 copy-done.10
  114.2 1.9 %shard_map.36 = (f32[4,64,256]{2,1,0:T(8,128)S(1)}, f32[4,64,256]{2,1,0:T(8,128)}) custom-call(s32[1]{0:T(128)} %bitcast.2.side, f32[4,2,4,64,256]{4,3,2,1,0:T(8,128)S(1)} %get-tuple-element.66.keep, f32[2,4,64,256]{3,2,1,0:T(8,128)S(1)} %collective-permute-done.11.got, f32[2,4,64,256]{3,2,1,0:T(8,128)S(1)} %collective-permute-done.15.refs_0_, ...), custom_call_target="tpu_custom_call" | custom-call | flops 1 | bytes 1 | tf_op jit(solution)/shard_map/pallas_call | solution.py:49
  116.1 2.8 %collective-permute-start.18 = (f32[4,64,256]{2,1,0:T(8,128)}, f32[4,64,256]{2,1,0:T(8,128)S(1)}, u32[]{:S(2)}, u32[]{:S(2)}) collective-permute-start(f32[4,64,256]{2,1,0:T(8,128)} %get-tuple-element.75), channel_id=1, source_target_pairs={{0,64},{1,65},{2,66},{3,67},{4,68},{5,69},{6,70},{7,71},{8,72},{9,... | collective-permute-start | bytes 786440 | tf_op jit(solution)/shard_map/ppermute | solution.py:24
  119.0 5.8 %collective-permute-done.22.refs_0_ = f32[2,4,64,256]{3,2,1,0:T(8,128)} collective-permute-done((f32[2,4,64,256]{3,2,1,0:T(8,128)}, f32[2,4,64,256]{3,2,1,0:T(8,128)}, u32[]{:S(2)}, u32[]{:S(2)}) %collective-permute-start.22) | collective-permute-done | bytes 524320 | tf_op jit(solution)/shard_map/ppermute | solution.py:24
  124.8 2.5 %collective-permute-done.24.refs_2_ = f32[2,4,64,256]{3,2,1,0:T(8,128)} collective-permute-done((f32[2,4,64,256]{3,2,1,0:T(8,128)}, f32[2,4,64,256]{3,2,1,0:T(8,128)}, u32[]{:S(2)}, u32[]{:S(2)}) %collective-permute-start.24) | collective-permute-done | bytes 524320 | tf_op jit(solution)/shard_map/ppermute | solution.py:24
  127.3 1.7 %shard_map.39 = (f32[4,64,256]{2,1,0:T(8,128)S(1)}, f32[4,64,256]{2,1,0:T(8,128)S(1)}) custom-call(s32[1]{0:T(128)} %bitcast.2.side, f32[1,2,4,64,256]{4,3,2,1,0:T(8,128)S(1)} %copy-done.12, f32[2,4,64,256]{3,2,1,0:T(8,128)} %collective-permute-done.21.got, f32[2,4,64,256]{3,2,1,0:T(8,128)} %collective-permute-done.22.refs_0_, ...), custom_call_target="tpu_custom_call" | custom-call | flops 1 | bytes 1 | tf_op jit(solution)/shard_map/pallas_call | solution.py:49
  128.9 3.1 %collective-permute-start.25 = (f32[4,64,256]{2,1,0:T(8,128)S(1)}, f32[4,64,256]{2,1,0:T(8,128)S(1)}, u32[]{:S(2)}, u32[]{:S(2)}) collective-permute-start(f32[4,64,256]{2,1,0:T(8,128)S(1)} %get-tuple-element.84), channel_id=1, source_target_pairs={{0,64},{1,65},{2,66},{3,67},{4,68},{5,69},{6,70},{7,71},{8,72},{9,... | collective-permute-start | bytes 786440 | tf_op jit(solution)/shard_map/ppermute | solution.py:24
  132.0 5.4 %collective-permute-done.25.other_two = f32[4,64,256]{2,1,0:T(8,128)S(1)} collective-permute-done((f32[4,64,256]{2,1,0:T(8,128)S(1)}, f32[4,64,256]{2,1,0:T(8,128)S(1)}, u32[]{:S(2)}, u32[]{:S(2)}) %collective-permute-start.25) | collective-permute-done | bytes 262176 | tf_op jit(solution)/shard_map/ppermute | solution.py:24
  137.4 0.8 shard_map.40
  (30 shorter events, 0.1 us)
Async XLA Ops:
  0.0 50.6 %copy-start = (f32[4096,256]{1,0:T(8,128)S(1)}, f32[4096,256]{1,0:T(8,128)}, u32[]{:S(2)}) copy-start(f32[4096,256]{1,0:T(8,128)} %value.1) | copy-start | bytes 12582916
  1.4 15.1 %collective-permute-start.2 = (f32[64,1024]{1,0:T(8,128)S(1)}, f32[64,1024]{1,0:T(8,128)S(1)}, u32[]{:S(2)}, u32[]{:S(2)}) collective-permute-start(f32[64,1024]{1,0:T(8,128)S(1)} %get-tuple-element.87), channel_id=1, source_target_pairs={{0,3},{1,2},{2,1},{3,0},{4,7},{5,6},{6,5},{7,4},{8,11},{9,10},{10,... | collective-permute-start | bytes 786440 | tf_op jit(solution)/shard_map/ppermute | solution.py:24
  4.6 11.9 %collective-permute-start.1 = (f32[64,1024]{1,0:T(8,128)S(1)}, f32[64,1024]{1,0:T(8,128)S(1)}, u32[]{:S(2)}, u32[]{:S(2)}) collective-permute-start(f32[64,1024]{1,0:T(8,128)S(1)} %get-tuple-element.88), channel_id=1, source_target_pairs={{0,2},{1,3},{2,0},{3,1},{4,6},{5,7},{6,4},{7,5},{8,10},{9,11},{10,... | collective-permute-start | bytes 786440 | tf_op jit(solution)/shard_map/ppermute | solution.py:24
  5.3 12.0 %collective-permute-start = (f32[64,1024]{1,0:T(8,128)S(1)}, f32[64,1024]{1,0:T(8,128)S(1)}, u32[]{:S(2)}, u32[]{:S(2)}) collective-permute-start(f32[64,1024]{1,0:T(8,128)S(1)} %get-tuple-element.86), channel_id=1, source_target_pairs={{0,1},{1,0},{2,3},{3,2},{4,5},{5,4},{6,7},{7,6},{8,9},{9,8},{10,11... | collective-permute-start | bytes 786440 | tf_op jit(solution)/shard_map/ppermute | solution.py:24
  17.3 26.5 %collective-permute-start.3 = (f32[4,64,1024]{2,1,0:T(8,128)S(1)}, f32[4,64,1024]{2,1,0:T(8,128)S(1)}, u32[]{:S(2)}, u32[]{:S(2)}) collective-permute-start(f32[4,64,1024]{2,1,0:T(8,128)S(1)} %pad_maximum_fusion.refs_0_), channel_id=1, source_target_pairs={{0,18},{1,19},{2,16},{3,17},{4,22},{5,23},{6,20},{7,21},{8,26},{9,... | collective-permute-start | bytes 3145736 | tf_op jit(solution)/shard_map/ppermute | solution.py:24
  21.4 23.6 %collective-permute-start.4 = (f32[4,64,1024]{2,1,0:T(8,128)S(1)}, f32[4,64,1024]{2,1,0:T(8,128)S(1)}, u32[]{:S(2)}, u32[]{:S(2)}) collective-permute-start(f32[4,64,1024]{2,1,0:T(8,128)S(1)} %pad_maximum_fusion.refs_0_), channel_id=1, source_target_pairs={{0,4},{1,5},{2,6},{3,7},{4,0},{5,1},{6,2},{7,3},{8,12},{9,13},{10,... | collective-permute-start | bytes 3145736 | tf_op jit(solution)/shard_map/ppermute | solution.py:24
  23.3 24.4 %collective-permute-start.5 = (f32[4,64,1024]{2,1,0:T(8,128)S(1)}, f32[4,64,1024]{2,1,0:T(8,128)S(1)}, u32[]{:S(2)}, u32[]{:S(2)}) collective-permute-start(f32[4,64,1024]{2,1,0:T(8,128)S(1)} %pad_maximum_fusion.refs_0_), channel_id=1, source_target_pairs={{0,12},{1,13},{2,14},{3,15},{4,8},{5,9},{6,10},{7,11},{8,4},{9,5},... | collective-permute-start | bytes 3145736 | tf_op jit(solution)/shard_map/ppermute | solution.py:24
  43.8 8.6 %copy-start.1 = (f32[4,64,1024]{2,1,0:T(8,128)}, f32[4,64,1024]{2,1,0:T(8,128)S(1)}, u32[]{:S(2)}) copy-start(f32[4,64,1024]{2,1,0:T(8,128)S(1)} %collective-permute-done.3._.refs_0_) | copy-start | bytes 3145732
  45.0 1.0 copy-start.7
  47.7 2.9 %copy-start.5 = (f32[4,64,1024]{2,1,0:T(8,128)}, f32[4,64,1024]{2,1,0:T(8,128)S(1)}, u32[]{:S(2)}) copy-start(f32[4,64,1024]{2,1,0:T(8,128)S(1)} %collective-permute-done.5.refs_1_) | copy-start | bytes 3145732
  47.7 23.1 %collective-permute-start.6 = (f32[4,64,1024]{2,1,0:T(8,128)S(1)}, f32[4,64,1024]{2,1,0:T(8,128)}, u32[]{:S(2)}, u32[]{:S(2)}) collective-permute-start(f32[4,64,1024]{2,1,0:T(8,128)S(1)} %collective-permute-done.3._.refs_0_), channel_id=1, source_target_pairs={{0,4},{1,5},{2,6},{3,7},{4,0},{5,1},{6,2},{7,3},{8,12},{9,13},{10,... | collective-permute-start | bytes 3145736 | tf_op jit(solution)/shard_map/ppermute | solution.py:24
  48.3 23.6 %collective-permute-start.7 = (f32[4,64,1024]{2,1,0:T(8,128)S(1)}, f32[4,64,1024]{2,1,0:T(8,128)}, u32[]{:S(2)}, u32[]{:S(2)}) collective-permute-start(f32[4,64,1024]{2,1,0:T(8,128)S(1)} %collective-permute-done.3._.refs_0_), channel_id=1, source_target_pairs={{0,12},{1,13},{2,14},{3,15},{4,8},{5,9},{6,10},{7,11},{8,4},{9,5},... | collective-permute-start | bytes 3145736 | tf_op jit(solution)/shard_map/ppermute | solution.py:24
  52.4 1.0 copy-start.3
  53.4 22.0 %collective-permute-start.8 = (f32[1024,256]{1,0:T(8,128)}, f32[1024,256]{1,0:T(8,128)}, u32[]{:S(2)}, u32[]{:S(2)}) collective-permute-start(f32[1024,256]{1,0:T(8,128)} %get-tuple-element.51), channel_id=1, source_target_pairs={{0,16},{1,17},{2,18},{3,19},{4,20},{5,21},{6,22},{7,23},{8,24},{9,... | collective-permute-start | bytes 3145736 | tf_op jit(solution)/shard_map/ppermute | solution.py:24
  53.9 22.9 %collective-permute-start.9 = (f32[1024,256]{1,0:T(8,128)}, f32[1024,256]{1,0:T(8,128)}, u32[]{:S(2)}, u32[]{:S(2)}) collective-permute-start(f32[1024,256]{1,0:T(8,128)} %get-tuple-element.54), channel_id=1, source_target_pairs={{0,1},{1,0},{2,3},{3,2},{4,5},{5,4},{6,7},{7,6},{8,9},{9,8},{10,11... | collective-permute-start | bytes 3145736 | tf_op jit(solution)/shard_map/ppermute | solution.py:24
  54.9 23.3 %collective-permute-start.10 = (f32[1024,256]{1,0:T(8,128)}, f32[1024,256]{1,0:T(8,128)S(1)}, u32[]{:S(2)}, u32[]{:S(2)}) collective-permute-start(f32[1024,256]{1,0:T(8,128)} %get-tuple-element.57), channel_id=1, source_target_pairs={{0,3},{1,2},{2,1},{3,0},{4,7},{5,6},{6,5},{7,4},{8,11},{9,10},{10,... | collective-permute-start | bytes 3145736 | tf_op jit(solution)/shard_map/ppermute | solution.py:24
  56.9 1.2 copy-start.4
  58.1 20.2 %copy-start.6 = (f32[4,64,1024]{2,1,0:T(8,128)S(1)}, f32[4,64,1024]{2,1,0:T(8,128)}, u32[]{:S(2)}) copy-start(f32[4,64,1024]{2,1,0:T(8,128)} %copy-done.5) | copy-start | bytes 3145732
  58.1 20.2 %copy-start.8 = (f32[4,64,1024]{2,1,0:T(8,128)S(1)}, f32[4,64,1024]{2,1,0:T(8,128)}, u32[]{:S(2)}) copy-start(f32[4,64,1024]{2,1,0:T(8,128)} %copy-done.7) | copy-start | bytes 3145732
  70.8 25.5 %collective-permute-start.19 = (f32[4,64,1024]{2,1,0:T(8,128)}, f32[4,64,1024]{2,1,0:T(8,128)S(1)}, u32[]{:S(2)}, u32[]{:S(2)}) collective-permute-start(f32[4,64,1024]{2,1,0:T(8,128)} %copy-done.5), channel_id=1, source_target_pairs={{0,4},{1,5},{2,6},{3,7},{4,0},{5,1},{6,2},{7,3},{8,12},{9,13},{10,... | collective-permute-start | bytes 3145736 | tf_op jit(solution)/shard_map/ppermute | solution.py:24
  71.9 26.6 %collective-permute-start.20 = (f32[4,64,1024]{2,1,0:T(8,128)}, f32[4,64,1024]{2,1,0:T(8,128)S(1)}, u32[]{:S(2)}, u32[]{:S(2)}) collective-permute-start(f32[4,64,1024]{2,1,0:T(8,128)} %collective-permute-done.6.refs_2_), channel_id=1, source_target_pairs={{0,12},{1,13},{2,14},{3,15},{4,8},{5,9},{6,10},{7,11},{8,4},{9,5},... | collective-permute-start | bytes 3145736 | tf_op jit(solution)/shard_map/ppermute | solution.py:24
  78.3 5.1 %copy-start.2 = (f32[4,64,1024]{2,1,0:T(8,128)S(1)}, f32[4,64,1024]{2,1,0:T(8,128)}, u32[]{:S(2)}) copy-start(f32[4,64,1024]{2,1,0:T(8,128)} %copy-done.1) | copy-start | bytes 3145732
  90.0 2.0 %collective-permute-start.12 = (f32[2,4,64,256]{3,2,1,0:T(8,128)S(1)}, f32[2,4,64,256]{3,2,1,0:T(8,128)S(1)}, u32[]{:S(2)}, u32[]{:S(2)}) collective-permute-start(f32[2,4,64,256]{3,2,1,0:T(8,128)S(1)} %get-tuple-element.68), channel_id=1, source_target_pairs={{0,32},{1,33},{2,34},{3,35},{4,36},{5,37},{6,38},{7,39},{8,40},{9,... | collective-permute-start | bytes 1572872 | tf_op jit(solution)/shard_map/ppermute | solution.py:24
  90.1 2.6 %collective-permute-start.13 = (f32[2,4,64,256]{3,2,1,0:T(8,128)S(1)}, f32[2,4,64,256]{3,2,1,0:T(8,128)S(1)}, u32[]{:S(2)}, u32[]{:S(2)}) collective-permute-start(f32[2,4,64,256]{3,2,1,0:T(8,128)S(1)} %get-tuple-element.69), channel_id=1, source_target_pairs={{0,32},{1,33},{2,34},{3,35},{4,36},{5,37},{6,38},{7,39},{8,40},{9,... | collective-permute-start | bytes 1572872 | tf_op jit(solution)/shard_map/ppermute | solution.py:24
  90.6 2.9 %collective-permute-start.14 = (f32[2,4,64,256]{3,2,1,0:T(8,128)S(1)}, f32[2,4,64,256]{3,2,1,0:T(8,128)S(1)}, u32[]{:S(2)}, u32[]{:S(2)}) collective-permute-start(f32[2,4,64,256]{3,2,1,0:T(8,128)S(1)} %get-tuple-element.70), channel_id=1, source_target_pairs={{0,32},{1,33},{2,34},{3,35},{4,36},{5,37},{6,38},{7,39},{8,40},{9,... | collective-permute-start | bytes 1572872 | tf_op jit(solution)/shard_map/ppermute | solution.py:24
  92.0 17.7 %collective-permute-start.11 = (f32[2,4,64,256]{3,2,1,0:T(8,128)S(1)}, f32[2,4,64,256]{3,2,1,0:T(8,128)S(1)}, u32[]{:S(2)}, u32[]{:S(2)}) collective-permute-start(f32[2,4,64,256]{3,2,1,0:T(8,128)S(1)} %get-tuple-element.67), channel_id=1, source_target_pairs={{0,32},{1,33},{2,34},{3,35},{4,36},{5,37},{6,38},{7,39},{8,40},{9,... | collective-permute-start | bytes 1572872 | tf_op jit(solution)/shard_map/ppermute | solution.py:24
  94.4 15.8 %collective-permute-start.15 = (f32[2,4,64,256]{3,2,1,0:T(8,128)S(1)}, f32[2,4,64,256]{3,2,1,0:T(8,128)S(1)}, u32[]{:S(2)}, u32[]{:S(2)}) collective-permute-start(f32[2,4,64,256]{3,2,1,0:T(8,128)S(1)} %get-tuple-element.71.refs_2_), channel_id=1, source_target_pairs={{0,16},{1,17},{2,18},{3,19},{4,20},{5,21},{6,22},{7,23},{8,24},{9,... | collective-permute-start | bytes 1572872 | tf_op jit(solution)/shard_map/ppermute | solution.py:24
  95.5 16.0 %collective-permute-start.16 = (f32[2,4,64,256]{3,2,1,0:T(8,128)S(1)}, f32[2,4,64,256]{3,2,1,0:T(8,128)S(1)}, u32[]{:S(2)}, u32[]{:S(2)}) collective-permute-start(f32[2,4,64,256]{3,2,1,0:T(8,128)S(1)} %get-tuple-element.72.refs_3_), channel_id=1, source_target_pairs={{0,1},{1,0},{2,3},{3,2},{4,5},{5,4},{6,7},{7,6},{8,9},{9,8},{10,11... | collective-permute-start | bytes 1572872 | tf_op jit(solution)/shard_map/ppermute | solution.py:24
  96.3 16.8 %collective-permute-start.17 = (f32[2,4,64,256]{3,2,1,0:T(8,128)}, f32[2,4,64,256]{3,2,1,0:T(8,128)}, u32[]{:S(2)}, u32[]{:S(2)}) collective-permute-start(f32[2,4,64,256]{3,2,1,0:T(8,128)} %get-tuple-element.73.refs_4_), channel_id=1, source_target_pairs={{0,3},{1,2},{2,1},{3,0},{4,7},{5,6},{6,5},{7,4},{8,11},{9,10},{10,... | collective-permute-start | bytes 1572872 | tf_op jit(solution)/shard_map/ppermute | solution.py:24
  102.0 6.4 %copy-start.11 = (f32[1,2,4,64,256]{4,3,2,1,0:T(8,128)}, f32[1,2,4,64,256]{4,3,2,1,0:T(8,128)S(1)}, u32[]{:S(2)}) copy-start(f32[1,2,4,64,256]{4,3,2,1,0:T(8,128)S(1)} %get-tuple-element.77.keep) | copy-start | bytes 1572868
  102.0 17.0 %collective-permute-start.21 = (f32[2,4,64,256]{3,2,1,0:T(8,128)}, f32[2,4,64,256]{3,2,1,0:T(8,128)}, u32[]{:S(2)}, u32[]{:S(2)}) collective-permute-start(f32[2,4,64,256]{3,2,1,0:T(8,128)} %get-tuple-element.78), channel_id=1, source_target_pairs={{0,32},{1,33},{2,34},{3,35},{4,36},{5,37},{6,38},{7,39},{8,40},{9,... | collective-permute-start | bytes 1572872 | tf_op jit(solution)/shard_map/ppermute | solution.py:24
  109.7 15.1 %collective-permute-start.22 = (f32[2,4,64,256]{3,2,1,0:T(8,128)}, f32[2,4,64,256]{3,2,1,0:T(8,128)}, u32[]{:S(2)}, u32[]{:S(2)}) collective-permute-start(f32[2,4,64,256]{3,2,1,0:T(8,128)} %get-tuple-element.80), channel_id=1, source_target_pairs={{0,16},{1,17},{2,18},{3,19},{4,20},{5,21},{6,22},{7,23},{8,24},{9,... | collective-permute-start | bytes 1572872 | tf_op jit(solution)/shard_map/ppermute | solution.py:24
  110.2 14.5 %collective-permute-start.23 = (f32[2,4,64,256]{3,2,1,0:T(8,128)}, f32[2,4,64,256]{3,2,1,0:T(8,128)}, u32[]{:S(2)}, u32[]{:S(2)}) collective-permute-start(f32[2,4,64,256]{3,2,1,0:T(8,128)} %get-tuple-element.81), channel_id=1, source_target_pairs={{0,1},{1,0},{2,3},{3,2},{4,5},{5,4},{6,7},{7,6},{8,9},{9,8},{10,11... | collective-permute-start | bytes 1572872 | tf_op jit(solution)/shard_map/ppermute | solution.py:24
  111.5 0.8 copy-start.9
  112.4 14.9 %collective-permute-start.24 = (f32[2,4,64,256]{3,2,1,0:T(8,128)}, f32[2,4,64,256]{3,2,1,0:T(8,128)}, u32[]{:S(2)}, u32[]{:S(2)}) collective-permute-start(f32[2,4,64,256]{3,2,1,0:T(8,128)} %get-tuple-element.82), channel_id=1, source_target_pairs={{0,3},{1,2},{2,1},{3,0},{4,7},{5,6},{6,5},{7,4},{8,11},{9,10},{10,... | collective-permute-start | bytes 1572872 | tf_op jit(solution)/shard_map/ppermute | solution.py:24
  113.1 1.0 copy-start.10
  114.2 13.1 %copy-start.12 = (f32[1,2,4,64,256]{4,3,2,1,0:T(8,128)S(1)}, f32[1,2,4,64,256]{4,3,2,1,0:T(8,128)}, u32[]{:S(2)}) copy-start(f32[1,2,4,64,256]{4,3,2,1,0:T(8,128)} %copy-done.11) | copy-start | bytes 1572868
  116.1 15.9 %collective-permute-start.18 = (f32[4,64,256]{2,1,0:T(8,128)}, f32[4,64,256]{2,1,0:T(8,128)S(1)}, u32[]{:S(2)}, u32[]{:S(2)}) collective-permute-start(f32[4,64,256]{2,1,0:T(8,128)} %get-tuple-element.75), channel_id=1, source_target_pairs={{0,64},{1,65},{2,66},{3,67},{4,68},{5,69},{6,70},{7,71},{8,72},{9,... | collective-permute-start | bytes 786440 | tf_op jit(solution)/shard_map/ppermute | solution.py:24
  128.9 8.5 %collective-permute-start.25 = (f32[4,64,256]{2,1,0:T(8,128)S(1)}, f32[4,64,256]{2,1,0:T(8,128)S(1)}, u32[]{:S(2)}, u32[]{:S(2)}) collective-permute-start(f32[4,64,256]{2,1,0:T(8,128)S(1)} %get-tuple-element.84), channel_id=1, source_target_pairs={{0,64},{1,65},{2,66},{3,67},{4,68},{5,69},{6,70},{7,71},{8,72},{9,... | collective-permute-start | bytes 786440 | tf_op jit(solution)/shard_map/ppermute | solution.py:24

commit v19 on v16

--- a/solution.py
+++ b/solution.py
@@ -122,7 +122,7 @@
 
     def kernel(swap, *refs):
         blocks, rest = refs[: len(arrays)], refs[len(arrays) + len(before):]
-        *rights, keep, third, one_give, two_give, three_give, four_give, left_high, left_low = rest
+        *rights, keep, one_give, two_give, three_give, four_give, left_high, left_low = rest
         gives = one_give, two_give, three_give, four_give
         swapped = swap[0] == 1
 
@@ -131,7 +131,6 @@
                 zero, one = total[0, block], total[1, block]
                 keep[d, 0, into] = jnp.where(swapped, one, zero)
                 gives[d][0, into] = jnp.where(swapped, zero, one)
-                third[d, 0, into] = total[2, block]
 
         multiplied(blocks, left_high, left_low, rights, store)
 
@@ -140,12 +139,12 @@
     once = pl.Buffered(1)
     kept_out = pl.BlockSpec((4, 1, 4, rows, columns), lambda *_: (0, part, 0, 0, 0), pipeline_mode=once)
     given_out = pl.BlockSpec((1, 4, rows, columns), lambda *_: (part, 0, 0, 0), pipeline_mode=once)
-    scratch = pltpu.VMEM((12 * rows, depth), jnp.bfloat16)
+    scratch = pltpu.VMEM((8 * rows, depth), jnp.bfloat16)
     first = 1 + len(arrays)
     return call(
         kernel, swap, (*arrays, *before, *rights),
         [whole(array) for array in arrays] + [ANYWHERE] * len(before) + [VMEM] * 8,
-        [kept] * 2 + [given] * 4, [kept_out] * 2 + [given_out] * 4, [scratch] * 2,
+        [kept] + [given] * 4, [kept_out] + [given_out] * 4, [scratch] * 2,
         {first + at: at for at in range(len(before))},
     )
 
@@ -160,6 +159,27 @@
     shape = jax.ShapeDtypeStruct(gots[0].shape, jnp.float32)
     return call(
         added_kernel, scalars, (keep, *gots), [whole(value) for value in (keep, *gots)], [shape] * 3, [whole(shape)] * 3
+    )
+
+
+def ahead_products(scalars, arrays, rights):
+    rows, depth = arrays[0].shape[1:]
+
+    def kernel(_, *refs):
+        blocks, (*rights, out, left_high, left_low) = refs[: len(arrays)], refs[len(arrays):]
+
+        def store(d, total):
+            for part in range(2):
+                for block, into in places(d):
+                    out[d, part, into] = total[part, block]
+
+        multiplied(blocks, left_high, left_low, rights, store)
+
+    shape = jax.ShapeDtypeStruct((4, 2, 4, rows, rights[0].shape[1]), jnp.float32)
+    scratch = pltpu.VMEM((8 * rows, depth), jnp.bfloat16)
+    return call(
+        kernel, scalars, (*arrays, *rights), [whole(array) for array in arrays] + [VMEM] * 8,
+        shape, whole(shape), [scratch] * 2,
     )
 
 
@@ -258,10 +278,11 @@
     pieces = [pieces[0]] + [send(pieces[d], **NEAR[d]) for d in range(1, 4)]
     rights = [half for piece in pieces for half in split(swap, [piece])]
 
-    before = early_products(swap, 0, ((mine,), (own_three,), (own_one,)), rights)
-    early = early_products(swap, 1, ((far,), (far_three,), (far_one,)), rights, before)
-
-    keep, third, *gives = early
+    before = early_products(swap, 0, ((mine,), (own_three,)), rights)
+    early = early_products(swap, 1, ((far,), (far_three,)), rights, before)
+
+    keep, *gives = early
+    third = ahead_products(swap, (own_one, far_one), rights)
     got = [send(give, core=1) for give in gives]
     sums = added(swap, keep, got[1:])
     late_keep, late_give, both = late_products(

time: 139 us -> 141 us (1.014)
  Pallas kernels: 26.6 us -> 28.9 us
    pallas_call x13 -> x14, Pallas kernels: 26.6 us -> 28.9 us  [call(): pl.pallas_call(kernel, grid_spec=pltpu.PrefetchScalarGridSpec(num_scalar_...]
  transfers between devices with their start and end apart: 26 -> 26, of which waited for: 14 -> 14; matrix products, arithmetic and copies ran while one was open for 0% -> 0% of each run, Pallas kernels for 19% -> 20%
where the time goes in v19:
time: 141 us
  waiting for transfers between devices  64.4 us (46%)
  starting transfers between devices  34.3 us (24%)
  Pallas kernels  28.9 us (20%)
  local copies, waits for them, and re-layouts  6.65 us (5%)
  blocking collectives  6.26 us (4%)
    ppermute x26, waiting for transfers between devices, send(): return lax.ppermute(value, AXES, pairs)  64.4 us
    ppermute x26, starting transfers between devices, send(): return lax.ppermute(value, AXES, pairs)  34.3 us
    pallas_call x14, Pallas kernels, call(): pl.pallas_call(kernel, grid_spec=pltpu.PrefetchScalarGridSpec(num_scalar_...  28.9 us
    all_to_all x1, blocking collectives, per_device(): both = lax.all_to_all(both, AXES, 0, 0, tiled=True, axis_index_groups=CORES)  6.26 us
    unnamed x26, local copies, waits for them, and re-layouts  5.21 us
  transfers between devices with their start and end apart: 26, of which 14 were waited for; matrix products, arithmetic and copies ran while one was open for 0% of the time, Pallas kernels for 20%

profile of v19, /device:TPU:0, one launch (start us, length us, event | category | flops | bytes accessed | tf_op | source)
XLA Modules:
  0.0 140.7 jit_solution(817295540218918849)
XLA Ops:
  0.0 1.4 %dynamic-slice_bitcast_fusion = (f32[1,64,1024]{2,1,0:T(8,128)S(1)}, f32[64,1024]{1,0:T(8,128)S(1)}, f32[64,1024]{1,0:T(8,128)S(1)}, f32[64,1024]{1,0:T(8,128)S(1)}) fusion(f32[64,4096]{1,0:T(8,128)} %param.2, s32[]{:T(128)S(6)} %select_n.12, s32[]{:T(128)S(6)} %select_n.13, s32[]{:T(128)S(6)} %select_n.15, s32[]{:T(128)S(6)} %select_n.14), kind=kLoop, calls=%fused_computation.1 | loop fusion | bytes 2097168 | tf_op jit(solution)/shard_map/stack | solution.py:269
  1.4 3.2 %collective-permute-start.2 = (f32[64,1024]{1,0:T(8,128)S(1)}, f32[64,1024]{1,0:T(8,128)S(1)}, u32[]{:S(2)}, u32[]{:S(2)}) collective-permute-start(f32[64,1024]{1,0:T(8,128)S(1)} %get-tuple-element.83), channel_id=1, source_target_pairs={{0,3},{1,2},{2,1},{3,0},{4,7},{5,6},{6,5},{7,4},{8,11},{9,10},{10,... | collective-permute-start | bytes 786440 | tf_op jit(solution)/shard_map/ppermute | solution.py:24
  4.6 0.6 collective-permute-start.1
  5.3 0.4 collective-permute-start
  5.6 10.9 %collective-permute-done.2 = f32[64,1024]{1,0:T(8,128)S(1)} collective-permute-done((f32[64,1024]{1,0:T(8,128)S(1)}, f32[64,1024]{1,0:T(8,128)S(1)}, u32[]{:S(2)}, u32[]{:S(2)}) %collective-permute-start.2) | collective-permute-done | bytes 262176 | tf_op jit(solution)/shard_map/ppermute | solution.py:24
  16.6 0.0 collective-permute-done.1
  16.6 0.7 collective-permute-done
  17.3 0.1 pad_maximum_fusion.refs_0_
  17.3 4.0 %collective-permute-start.3 = (f32[4,64,1024]{2,1,0:T(8,128)S(1)}, f32[4,64,1024]{2,1,0:T(8,128)S(1)}, u32[]{:S(2)}, u32[]{:S(2)}) collective-permute-start(f32[4,64,1024]{2,1,0:T(8,128)S(1)} %pad_maximum_fusion.refs_0_), channel_id=1, source_target_pairs={{0,18},{1,19},{2,16},{3,17},{4,22},{5,23},{6,20},{7,21},{8,26},{9,... | collective-permute-start | bytes 3145736 | tf_op jit(solution)/shard_map/ppermute | solution.py:24
  21.4 1.9 %collective-permute-start.4 = (f32[4,64,1024]{2,1,0:T(8,128)S(1)}, f32[4,64,1024]{2,1,0:T(8,128)S(1)}, u32[]{:S(2)}, u32[]{:S(2)}) collective-permute-start(f32[4,64,1024]{2,1,0:T(8,128)S(1)} %pad_maximum_fusion.refs_0_), channel_id=1, source_target_pairs={{0,4},{1,5},{2,6},{3,7},{4,0},{5,1},{6,2},{7,3},{8,12},{9,13},{10,... | collective-permute-start | bytes 3145736 | tf_op jit(solution)/shard_map/ppermute | solution.py:24
  23.3 2.5 %collective-permute-start.5 = (f32[4,64,1024]{2,1,0:T(8,128)S(1)}, f32[4,64,1024]{2,1,0:T(8,128)S(1)}, u32[]{:S(2)}, u32[]{:S(2)}) collective-permute-start(f32[4,64,1024]{2,1,0:T(8,128)S(1)} %pad_maximum_fusion.refs_0_), channel_id=1, source_target_pairs={{0,12},{1,13},{2,14},{3,15},{4,8},{5,9},{6,10},{7,11},{8,4},{9,5},... | collective-permute-start | bytes 3145736 | tf_op jit(solution)/shard_map/ppermute | solution.py:24
  25.8 18.0 %collective-permute-done.3._.refs_0_ = f32[4,64,1024]{2,1,0:T(8,128)S(1)} collective-permute-done((f32[4,64,1024]{2,1,0:T(8,128)S(1)}, f32[4,64,1024]{2,1,0:T(8,128)S(1)}, u32[]{:S(2)}, u32[]{:S(2)}) %collective-permute-start.3) | collective-permute-done | bytes 1048608 | tf_op jit(solution)/shard_map/ppermute | solution.py:24
  43.8 1.2 collective-permute-done.4.refs_0_
  45.0 2.7 %collective-permute-done.5.refs_1_ = f32[4,64,1024]{2,1,0:T(8,128)S(1)} collective-permute-done((f32[4,64,1024]{2,1,0:T(8,128)S(1)}, f32[4,64,1024]{2,1,0:T(8,128)S(1)}, u32[]{:S(2)}, u32[]{:S(2)}) %collective-permute-start.5) | collective-permute-done | bytes 1048608 | tf_op jit(solution)/shard_map/ppermute | solution.py:24
  47.7 1.0 copy-done.5
  48.7 0.6 collective-permute-start.6
  49.3 2.3 %collective-permute-start.7 = (f32[4,64,1024]{2,1,0:T(8,128)S(1)}, f32[4,64,1024]{2,1,0:T(8,128)}, u32[]{:S(2)}, u32[]{:S(2)}) collective-permute-start(f32[4,64,1024]{2,1,0:T(8,128)S(1)} %collective-permute-done.3._.refs_0_), channel_id=1, source_target_pairs={{0,12},{1,13},{2,14},{3,15},{4,8},{5,9},{6,10},{7,11},{8,4},{9,5},... | collective-permute-start | bytes 3145736 | tf_op jit(solution)/shard_map/ppermute | solution.py:24
  51.6 1.8 %shard_map.28 = (f32[1024,256]{1,0:T(8,128)S(1)}, f32[1024,256]{1,0:T(8,128)}, f32[1024,256]{1,0:T(8,128)}, f32[1024,256]{1,0:T(8,128)}) custom-call(s32[1]{0:T(128)} %bitcast.8.quarter, f32[4096,256]{1,0:T(8,128)S(1)} %copy-done, f32[4,64,1024]{2,1,0:T(8,128)S(1)} %collective-permute-done.3._.refs_0_), custom_call_target="tpu_custom_call" | custom-call | flops 1 | bytes 1 | tf_op jit(solution)/shard_map/pallas_call | solution.py:49
  53.4 1.0 copy-done.7
  54.4 0.5 collective-permute-start.8
  55.0 1.0 collective-permute-start.9
  56.0 1.0 collective-permute-start.10
  57.0 1.3 copy-done.8
  58.3 0.1 shard_map.29
  58.4 13.4 %collective-permute-done.6.refs_1_ = f32[4,64,1024]{2,1,0:T(8,128)} collective-permute-done((f32[4,64,1024]{2,1,0:T(8,128)S(1)}, f32[4,64,1024]{2,1,0:T(8,128)}, u32[]{:S(2)}, u32[]{:S(2)}) %collective-permute-start.6) | collective-permute-done | bytes 1048608 | tf_op jit(solution)/shard_map/ppermute | solution.py:24
  71.8 0.6 collective-permute-start.19
  72.4 0.5 collective-permute-done.7.refs_1_
  72.9 2.1 %collective-permute-start.20 = (f32[4,64,1024]{2,1,0:T(8,128)}, f32[4,64,1024]{2,1,0:T(8,128)S(1)}, u32[]{:S(2)}, u32[]{:S(2)}) collective-permute-start(f32[4,64,1024]{2,1,0:T(8,128)} %collective-permute-done.6.refs_1_), channel_id=1, source_target_pairs={{0,12},{1,13},{2,14},{3,15},{4,8},{5,9},{6,10},{7,11},{8,4},{9,5},... | collective-permute-start | bytes 3145736 | tf_op jit(solution)/shard_map/ppermute | solution.py:24
  74.9 1.5 %collective-permute-done.8.refs_0_ = f32[1024,256]{1,0:T(8,128)} collective-permute-done((f32[1024,256]{1,0:T(8,128)}, f32[1024,256]{1,0:T(8,128)}, u32[]{:S(2)}, u32[]{:S(2)}) %collective-permute-start.8) | collective-permute-done | bytes 1048608 | tf_op jit(solution)/shard_map/ppermute | solution.py:24
  76.5 1.4 shard_map.30
  77.8 0.0 collective-permute-done.9.refs_0_
  77.8 1.4 shard_map.31
  79.2 1.4 shard_map.32
  80.6 3.4 %shard_map.33 = (f32[4,2,4,64,256]{4,3,2,1,0:T(8,128)S(1)}, f32[2,4,64,256]{3,2,1,0:T(8,128)S(1)}, f32[2,4,64,256]{3,2,1,0:T(8,128)S(1)}, f32[2,4,64,256]{3,2,1,0:T(8,128)S(1)}, f32[2,4,64,256]{3,2,1,0:T(8,128)S(1)}) custom-call(s32[1]{0:T(128)} %bitcast.3._.swap, f32[4,64,1024]{2,1,0:T(8,128)S(1)} %pad_maximum_fusion.refs_0_, f32[4,64,1024]{2,1,0:T(8,128)S(1)} %copy-done.6, ...), custom_call_target="tpu_custom_call" | custom-call | flops 1 | bytes 1 | tf_op jit(solution)/shard_map/pallas_call | solution.py:49
  84.0 4.6 %shard_map.34 = (f32[4,2,4,64,256]{4,3,2,1,0:T(8,128)S(1)}, f32[2,4,64,256]{3,2,1,0:T(8,128)S(1)}, f32[2,4,64,256]{3,2,1,0:T(8,128)S(1)}, f32[2,4,64,256]{3,2,1,0:T(8,128)S(1)}, f32[2,4,64,256]{3,2,1,0:T(8,128)S(1)}) custom-call(s32[1]{0:T(128)} %bitcast.3._.swap, ...), custom_call_target="tpu_custom_call", output_to_operand_aliasing={{0}: (3, {}), {1}: (4, {}), {2}: (5, {}), {3}: (6, {}), {4}... | custom-call | flops 1 | bytes 1 | tf_op jit(solution)/shard_map/pallas_call | solution.py:49
  88.7 0.1 collective-permute-start.12
  88.8 0.5 collective-permute-start.13
  89.3 0.1 collective-permute-start.14
  89.4 1.3 collective-permute-done.12.refs_0_
  90.7 0.1 collective-permute-start.11
  90.8 0.6 collective-permute-done.13.refs_1_
  91.4 0.7 collective-permute-done.14.refs_2_
  92.2 1.0 shard_map.35
  93.1 1.2 collective-permute-start.15
  94.3 0.6 collective-permute-start.16
  95.0 4.6 %shard_map.37.refs_13_ = f32[4,2,4,64,256]{4,3,2,1,0:T(8,128)S(1)} custom-call(s32[1]{0:T(128)} %bitcast.3._.swap, f32[4,64,1024]{2,1,0:T(8,128)S(1)} %copy-done.4, f32[4,64,1024]{2,1,0:T(8,128)} %collective-permute-done.6.refs_1_, bf16[1024,256]{1,0:T(8,128)(2,1)S(1)} %get-tuple-element.46.refs_2_.refs_7_.refs_5_, ...), custom_call_target="tpu_custom_call" | custom-call | flops 1 | bytes 1 | tf_op jit(solution)/shard_map/pallas_call | solution.py:49
  99.6 1.3 collective-permute-start.17
  100.9 3.5 %shard_map.38 = (f32[1,2,4,64,256]{4,3,2,1,0:T(8,128)S(1)}, f32[2,4,64,256]{3,2,1,0:T(8,128)}, f32[2,3,2,4,64,256]{5,4,3,2,1,0:T(8,128)S(1)}) custom-call(s32[1]{0:T(128)} %bitcast.3._.swap, s32[1]{0:T(128)} %bitcast.9.at_core, f32[4,64,1024]{2,1,0:T(8,128)S(1)} %collective-permute-done.19.refs_0_, f32[4,64,1024]{2,1,0:T(8,128)S(1)} %collective-permute-done.20.refs_1_, ...), custom_call_target="tpu_custom_call" | custom-call | flops 1 | bytes 1 | tf_op jit(solution)/shard_map/pallas_call | solution.py:49
  104.5 0.1 collective-permute-start.21
  104.6 6.3 %all_to_all.5.both = f32[2,3,2,4,64,256]{5,4,3,2,1,0:T(8,128)S(1)} all-to-all(f32[2,3,2,4,64,256]{5,4,3,2,1,0:T(8,128)S(1)} %get-tuple-element.75), channel_id=1, replica_groups={{0,32},{1,33},{2,34},{3,35},{4,36},{5,37},{6,38},{7,39},{8,40},{9,41},{..., dimensions={0} | all-to-all | bytes 6291456 | tf_op jit(solution)/shard_map/all_to_all | solution.py:291
  110.9 1.3 shard_map.39
  112.2 0.6 collective-permute-start.22
  112.8 1.2 collective-permute-start.23
  114.0 0.8 copy-done.9
  114.8 1.8 %collective-permute-start.24 = (f32[2,4,64,256]{3,2,1,0:T(8,128)}, f32[2,4,64,256]{3,2,1,0:T(8,128)}, u32[]{:S(2)}, u32[]{:S(2)}) collective-permute-start(f32[2,4,64,256]{3,2,1,0:T(8,128)} %get-tuple-element.78), channel_id=1, source_target_pairs={{0,3},{1,2},{2,1},{3,0},{4,7},{5,6},{6,5},{7,4},{8,11},{9,10},{10,... | collective-permute-start | bytes 1572872 | tf_op jit(solution)/shard_map/ppermute | solution.py:24
  116.6 1.0 copy-done.10
  117.7 1.9 %shard_map.36 = (f32[4,64,256]{2,1,0:T(8,128)S(1)}, f32[4,64,256]{2,1,0:T(8,128)}) custom-call(s32[1]{0:T(128)} %bitcast.2.side, f32[4,2,4,64,256]{4,3,2,1,0:T(8,128)S(1)} %get-tuple-element.62.keep, f32[2,4,64,256]{3,2,1,0:T(8,128)S(1)} %collective-permute-done.11.got, f32[2,4,64,256]{3,2,1,0:T(8,128)S(1)} %collective-permute-done.15.refs_0_, ...), custom_call_target="tpu_custom_call" | custom-call | flops 1 | bytes 1 | tf_op jit(solution)/shard_map/pallas_call | solution.py:49
  119.6 2.7 %collective-permute-start.18 = (f32[4,64,256]{2,1,0:T(8,128)}, f32[4,64,256]{2,1,0:T(8,128)S(1)}, u32[]{:S(2)}, u32[]{:S(2)}) collective-permute-start(f32[4,64,256]{2,1,0:T(8,128)} %get-tuple-element.71), channel_id=1, source_target_pairs={{0,64},{1,65},{2,66},{3,67},{4,68},{5,69},{6,70},{7,71},{8,72},{9,... | collective-permute-start | bytes 786440 | tf_op jit(solution)/shard_map/ppermute | solution.py:24
  122.3 4.9 %collective-permute-done.22.refs_0_ = f32[2,4,64,256]{3,2,1,0:T(8,128)} collective-permute-done((f32[2,4,64,256]{3,2,1,0:T(8,128)}, f32[2,4,64,256]{3,2,1,0:T(8,128)}, u32[]{:S(2)}, u32[]{:S(2)}) %collective-permute-start.22) | collective-permute-done | bytes 524320 | tf_op jit(solution)/shard_map/ppermute | solution.py:24
  127.3 2.5 %collective-permute-done.24.refs_2_ = f32[2,4,64,256]{3,2,1,0:T(8,128)} collective-permute-done((f32[2,4,64,256]{3,2,1,0:T(8,128)}, f32[2,4,64,256]{3,2,1,0:T(8,128)}, u32[]{:S(2)}, u32[]{:S(2)}) %collective-permute-start.24) | collective-permute-done | bytes 524320 | tf_op jit(solution)/shard_map/ppermute | solution.py:24
  129.8 1.7 %shard_map.40 = (f32[4,64,256]{2,1,0:T(8,128)S(1)}, f32[4,64,256]{2,1,0:T(8,128)S(1)}) custom-call(s32[1]{0:T(128)} %bitcast.2.side, f32[1,2,4,64,256]{4,3,2,1,0:T(8,128)S(1)} %copy-done.12, f32[2,4,64,256]{3,2,1,0:T(8,128)} %collective-permute-done.21.got, f32[2,4,64,256]{3,2,1,0:T(8,128)} %collective-permute-done.22.refs_0_, ...), custom_call_target="tpu_custom_call" | custom-call | flops 1 | bytes 1 | tf_op jit(solution)/shard_map/pallas_call | solution.py:49
  131.4 3.1 %collective-permute-start.25 = (f32[4,64,256]{2,1,0:T(8,128)S(1)}, f32[4,64,256]{2,1,0:T(8,128)S(1)}, u32[]{:S(2)}, u32[]{:S(2)}) collective-permute-start(f32[4,64,256]{2,1,0:T(8,128)S(1)} %get-tuple-element.80), channel_id=1, source_target_pairs={{0,64},{1,65},{2,66},{3,67},{4,68},{5,69},{6,70},{7,71},{8,72},{9,... | collective-permute-start | bytes 786440 | tf_op jit(solution)/shard_map/ppermute | solution.py:24
  134.5 5.3 %collective-permute-done.25.other_two = f32[4,64,256]{2,1,0:T(8,128)S(1)} collective-permute-done((f32[4,64,256]{2,1,0:T(8,128)S(1)}, f32[4,64,256]{2,1,0:T(8,128)S(1)}, u32[]{:S(2)}, u32[]{:S(2)}) %collective-permute-start.25) | collective-permute-done | bytes 262176 | tf_op jit(solution)/shard_map/ppermute | solution.py:24
  139.9 0.8 shard_map.41
  (31 shorter events, 0.1 us)
Async XLA Ops:
  0.0 51.6 %copy-start = (f32[4096,256]{1,0:T(8,128)S(1)}, f32[4096,256]{1,0:T(8,128)}, u32[]{:S(2)}) copy-start(f32[4096,256]{1,0:T(8,128)} %value.1) | copy-start | bytes 12582916
  1.4 15.1 %collective-permute-start.2 = (f32[64,1024]{1,0:T(8,128)S(1)}, f32[64,1024]{1,0:T(8,128)S(1)}, u32[]{:S(2)}, u32[]{:S(2)}) collective-permute-start(f32[64,1024]{1,0:T(8,128)S(1)} %get-tuple-element.83), channel_id=1, source_target_pairs={{0,3},{1,2},{2,1},{3,0},{4,7},{5,6},{6,5},{7,4},{8,11},{9,10},{10,... | collective-permute-start | bytes 786440 | tf_op jit(solution)/shard_map/ppermute | solution.py:24
  4.6 11.9 %collective-permute-start.1 = (f32[64,1024]{1,0:T(8,128)S(1)}, f32[64,1024]{1,0:T(8,128)S(1)}, u32[]{:S(2)}, u32[]{:S(2)}) collective-permute-start(f32[64,1024]{1,0:T(8,128)S(1)} %get-tuple-element.84), channel_id=1, source_target_pairs={{0,2},{1,3},{2,0},{3,1},{4,6},{5,7},{6,4},{7,5},{8,10},{9,11},{10,... | collective-permute-start | bytes 786440 | tf_op jit(solution)/shard_map/ppermute | solution.py:24
  5.3 12.0 %collective-permute-start = (f32[64,1024]{1,0:T(8,128)S(1)}, f32[64,1024]{1,0:T(8,128)S(1)}, u32[]{:S(2)}, u32[]{:S(2)}) collective-permute-start(f32[64,1024]{1,0:T(8,128)S(1)} %get-tuple-element.82), channel_id=1, source_target_pairs={{0,1},{1,0},{2,3},{3,2},{4,5},{5,4},{6,7},{7,6},{8,9},{9,8},{10,11... | collective-permute-start | bytes 786440 | tf_op jit(solution)/shard_map/ppermute | solution.py:24
  17.3 26.5 %collective-permute-start.3 = (f32[4,64,1024]{2,1,0:T(8,128)S(1)}, f32[4,64,1024]{2,1,0:T(8,128)S(1)}, u32[]{:S(2)}, u32[]{:S(2)}) collective-permute-start(f32[4,64,1024]{2,1,0:T(8,128)S(1)} %pad_maximum_fusion.refs_0_), channel_id=1, source_target_pairs={{0,18},{1,19},{2,16},{3,17},{4,22},{5,23},{6,20},{7,21},{8,26},{9,... | collective-permute-start | bytes 3145736 | tf_op jit(solution)/shard_map/ppermute | solution.py:24
  21.4 23.6 %collective-permute-start.4 = (f32[4,64,1024]{2,1,0:T(8,128)S(1)}, f32[4,64,1024]{2,1,0:T(8,128)S(1)}, u32[]{:S(2)}, u32[]{:S(2)}) collective-permute-start(f32[4,64,1024]{2,1,0:T(8,128)S(1)} %pad_maximum_fusion.refs_0_), channel_id=1, source_target_pairs={{0,4},{1,5},{2,6},{3,7},{4,0},{5,1},{6,2},{7,3},{8,12},{9,13},{10,... | collective-permute-start | bytes 3145736 | tf_op jit(solution)/shard_map/ppermute | solution.py:24
  23.3 24.4 %collective-permute-start.5 = (f32[4,64,1024]{2,1,0:T(8,128)S(1)}, f32[4,64,1024]{2,1,0:T(8,128)S(1)}, u32[]{:S(2)}, u32[]{:S(2)}) collective-permute-start(f32[4,64,1024]{2,1,0:T(8,128)S(1)} %pad_maximum_fusion.refs_0_), channel_id=1, source_target_pairs={{0,12},{1,13},{2,14},{3,15},{4,8},{5,9},{6,10},{7,11},{8,4},{9,5},... | collective-permute-start | bytes 3145736 | tf_op jit(solution)/shard_map/ppermute | solution.py:24
  43.8 14.6 %copy-start.1 = (f32[4,64,1024]{2,1,0:T(8,128)}, f32[4,64,1024]{2,1,0:T(8,128)S(1)}, u32[]{:S(2)}) copy-start(f32[4,64,1024]{2,1,0:T(8,128)S(1)} %collective-permute-done.3._.refs_0_) | copy-start | bytes 3145732
  45.0 13.4 %copy-start.3 = (f32[4,64,1024]{2,1,0:T(8,128)}, f32[4,64,1024]{2,1,0:T(8,128)S(1)}, u32[]{:S(2)}) copy-start(f32[4,64,1024]{2,1,0:T(8,128)S(1)} %collective-permute-done.4.refs_0_) | copy-start | bytes 3145732
  47.7 1.0 copy-start.5
  48.7 23.1 %collective-permute-start.6 = (f32[4,64,1024]{2,1,0:T(8,128)S(1)}, f32[4,64,1024]{2,1,0:T(8,128)}, u32[]{:S(2)}, u32[]{:S(2)}) collective-permute-start(f32[4,64,1024]{2,1,0:T(8,128)S(1)} %collective-permute-done.3._.refs_0_), channel_id=1, source_target_pairs={{0,4},{1,5},{2,6},{3,7},{4,0},{5,1},{6,2},{7,3},{8,12},{9,13},{10,... | collective-permute-start | bytes 3145736 | tf_op jit(solution)/shard_map/ppermute | solution.py:24
  49.3 23.6 %collective-permute-start.7 = (f32[4,64,1024]{2,1,0:T(8,128)S(1)}, f32[4,64,1024]{2,1,0:T(8,128)}, u32[]{:S(2)}, u32[]{:S(2)}) collective-permute-start(f32[4,64,1024]{2,1,0:T(8,128)S(1)} %collective-permute-done.3._.refs_0_), channel_id=1, source_target_pairs={{0,12},{1,13},{2,14},{3,15},{4,8},{5,9},{6,10},{7,11},{8,4},{9,5},... | collective-permute-start | bytes 3145736 | tf_op jit(solution)/shard_map/ppermute | solution.py:24
  53.4 1.0 copy-start.7
  54.4 22.0 %collective-permute-start.8 = (f32[1024,256]{1,0:T(8,128)}, f32[1024,256]{1,0:T(8,128)}, u32[]{:S(2)}, u32[]{:S(2)}) collective-permute-start(f32[1024,256]{1,0:T(8,128)} %get-tuple-element.48), channel_id=1, source_target_pairs={{0,16},{1,17},{2,18},{3,19},{4,20},{5,21},{6,22},{7,23},{8,24},{9,... | collective-permute-start | bytes 3145736 | tf_op jit(solution)/shard_map/ppermute | solution.py:24
  55.0 22.9 %collective-permute-start.9 = (f32[1024,256]{1,0:T(8,128)}, f32[1024,256]{1,0:T(8,128)}, u32[]{:S(2)}, u32[]{:S(2)}) collective-permute-start(f32[1024,256]{1,0:T(8,128)} %get-tuple-element.51), channel_id=1, source_target_pairs={{0,1},{1,0},{2,3},{3,2},{4,5},{5,4},{6,7},{7,6},{8,9},{9,8},{10,11... | collective-permute-start | bytes 3145736 | tf_op jit(solution)/shard_map/ppermute | solution.py:24
  56.0 23.3 %collective-permute-start.10 = (f32[1024,256]{1,0:T(8,128)}, f32[1024,256]{1,0:T(8,128)}, u32[]{:S(2)}, u32[]{:S(2)}) collective-permute-start(f32[1024,256]{1,0:T(8,128)} %get-tuple-element.54), channel_id=1, source_target_pairs={{0,3},{1,2},{2,1},{3,0},{4,7},{5,6},{6,5},{7,4},{8,11},{9,10},{10,... | collective-permute-start | bytes 3145736 | tf_op jit(solution)/shard_map/ppermute | solution.py:24
  56.9 23.6 %copy-start.6 = (f32[4,64,1024]{2,1,0:T(8,128)S(1)}, f32[4,64,1024]{2,1,0:T(8,128)}, u32[]{:S(2)}) copy-start(f32[4,64,1024]{2,1,0:T(8,128)} %copy-done.5) | copy-start | bytes 3145732
  56.9 1.3 copy-start.8
  71.8 27.8 %collective-permute-start.19 = (f32[4,64,1024]{2,1,0:T(8,128)}, f32[4,64,1024]{2,1,0:T(8,128)S(1)}, u32[]{:S(2)}, u32[]{:S(2)}) collective-permute-start(f32[4,64,1024]{2,1,0:T(8,128)} %copy-done.5), channel_id=1, source_target_pairs={{0,4},{1,5},{2,6},{3,7},{4,0},{5,1},{6,2},{7,3},{8,12},{9,13},{10,... | collective-permute-start | bytes 3145736 | tf_op jit(solution)/shard_map/ppermute | solution.py:24
  72.9 28.1 %collective-permute-start.20 = (f32[4,64,1024]{2,1,0:T(8,128)}, f32[4,64,1024]{2,1,0:T(8,128)S(1)}, u32[]{:S(2)}, u32[]{:S(2)}) collective-permute-start(f32[4,64,1024]{2,1,0:T(8,128)} %collective-permute-done.6.refs_1_), channel_id=1, source_target_pairs={{0,12},{1,13},{2,14},{3,15},{4,8},{5,9},{6,10},{7,11},{8,4},{9,5},... | collective-permute-start | bytes 3145736 | tf_op jit(solution)/shard_map/ppermute | solution.py:24
  80.6 3.4 %copy-start.2 = (f32[4,64,1024]{2,1,0:T(8,128)S(1)}, f32[4,64,1024]{2,1,0:T(8,128)}, u32[]{:S(2)}) copy-start(f32[4,64,1024]{2,1,0:T(8,128)} %copy-done.1) | copy-start | bytes 3145732
  88.7 6.3 %copy-start.4 = (f32[4,64,1024]{2,1,0:T(8,128)S(1)}, f32[4,64,1024]{2,1,0:T(8,128)}, u32[]{:S(2)}) copy-start(f32[4,64,1024]{2,1,0:T(8,128)} %copy-done.3) | copy-start | bytes 3145732
  88.7 2.0 %collective-permute-start.12 = (f32[2,4,64,256]{3,2,1,0:T(8,128)S(1)}, f32[2,4,64,256]{3,2,1,0:T(8,128)S(1)}, u32[]{:S(2)}, u32[]{:S(2)}) collective-permute-start(f32[2,4,64,256]{3,2,1,0:T(8,128)S(1)} %get-tuple-element.64), channel_id=1, source_target_pairs={{0,32},{1,33},{2,34},{3,35},{4,36},{5,37},{6,38},{7,39},{8,40},{9,... | collective-permute-start | bytes 1572872 | tf_op jit(solution)/shard_map/ppermute | solution.py:24
  88.8 2.6 %collective-permute-start.13 = (f32[2,4,64,256]{3,2,1,0:T(8,128)S(1)}, f32[2,4,64,256]{3,2,1,0:T(8,128)S(1)}, u32[]{:S(2)}, u32[]{:S(2)}) collective-permute-start(f32[2,4,64,256]{3,2,1,0:T(8,128)S(1)} %get-tuple-element.65), channel_id=1, source_target_pairs={{0,32},{1,33},{2,34},{3,35},{4,36},{5,37},{6,38},{7,39},{8,40},{9,... | collective-permute-start | bytes 1572872 | tf_op jit(solution)/shard_map/ppermute | solution.py:24
  89.3 2.9 %collective-permute-start.14 = (f32[2,4,64,256]{3,2,1,0:T(8,128)S(1)}, f32[2,4,64,256]{3,2,1,0:T(8,128)S(1)}, u32[]{:S(2)}, u32[]{:S(2)}) collective-permute-start(f32[2,4,64,256]{3,2,1,0:T(8,128)S(1)} %get-tuple-element.66), channel_id=1, source_target_pairs={{0,32},{1,33},{2,34},{3,35},{4,36},{5,37},{6,38},{7,39},{8,40},{9,... | collective-permute-start | bytes 1572872 | tf_op jit(solution)/shard_map/ppermute | solution.py:24
  90.7 21.5 %collective-permute-start.11 = (f32[2,4,64,256]{3,2,1,0:T(8,128)S(1)}, f32[2,4,64,256]{3,2,1,0:T(8,128)S(1)}, u32[]{:S(2)}, u32[]{:S(2)}) collective-permute-start(f32[2,4,64,256]{3,2,1,0:T(8,128)S(1)} %get-tuple-element.63), channel_id=1, source_target_pairs={{0,32},{1,33},{2,34},{3,35},{4,36},{5,37},{6,38},{7,39},{8,40},{9,... | collective-permute-start | bytes 1572872 | tf_op jit(solution)/shard_map/ppermute | solution.py:24
  93.1 19.7 %collective-permute-start.15 = (f32[2,4,64,256]{3,2,1,0:T(8,128)S(1)}, f32[2,4,64,256]{3,2,1,0:T(8,128)S(1)}, u32[]{:S(2)}, u32[]{:S(2)}) collective-permute-start(f32[2,4,64,256]{3,2,1,0:T(8,128)S(1)} %get-tuple-element.67.refs_2_), channel_id=1, source_target_pairs={{0,16},{1,17},{2,18},{3,19},{4,20},{5,21},{6,22},{7,23},{8,24},{9,... | collective-permute-start | bytes 1572872 | tf_op jit(solution)/shard_map/ppermute | solution.py:24
  94.3 19.7 %collective-permute-start.16 = (f32[2,4,64,256]{3,2,1,0:T(8,128)S(1)}, f32[2,4,64,256]{3,2,1,0:T(8,128)S(1)}, u32[]{:S(2)}, u32[]{:S(2)}) collective-permute-start(f32[2,4,64,256]{3,2,1,0:T(8,128)S(1)} %get-tuple-element.68.refs_3_), channel_id=1, source_target_pairs={{0,1},{1,0},{2,3},{3,2},{4,5},{5,4},{6,7},{7,6},{8,9},{9,8},{10,11... | collective-permute-start | bytes 1572872 | tf_op jit(solution)/shard_map/ppermute | solution.py:24
  99.6 17.0 %collective-permute-start.17 = (f32[2,4,64,256]{3,2,1,0:T(8,128)}, f32[2,4,64,256]{3,2,1,0:T(8,128)}, u32[]{:S(2)}, u32[]{:S(2)}) collective-permute-start(f32[2,4,64,256]{3,2,1,0:T(8,128)} %get-tuple-element.69.refs_4_), channel_id=1, source_target_pairs={{0,3},{1,2},{2,1},{3,0},{4,7},{5,6},{6,5},{7,4},{8,11},{9,10},{10,... | collective-permute-start | bytes 1572872 | tf_op jit(solution)/shard_map/ppermute | solution.py:24
  104.5 6.4 %copy-start.11 = (f32[1,2,4,64,256]{4,3,2,1,0:T(8,128)}, f32[1,2,4,64,256]{4,3,2,1,0:T(8,128)S(1)}, u32[]{:S(2)}) copy-start(f32[1,2,4,64,256]{4,3,2,1,0:T(8,128)S(1)} %get-tuple-element.73.keep) | copy-start | bytes 1572868
  104.5 17.8 %collective-permute-start.21 = (f32[2,4,64,256]{3,2,1,0:T(8,128)}, f32[2,4,64,256]{3,2,1,0:T(8,128)}, u32[]{:S(2)}, u32[]{:S(2)}) collective-permute-start(f32[2,4,64,256]{3,2,1,0:T(8,128)} %get-tuple-element.74), channel_id=1, source_target_pairs={{0,32},{1,33},{2,34},{3,35},{4,36},{5,37},{6,38},{7,39},{8,40},{9,... | collective-permute-start | bytes 1572872 | tf_op jit(solution)/shard_map/ppermute | solution.py:24
  112.2 15.1 %collective-permute-start.22 = (f32[2,4,64,256]{3,2,1,0:T(8,128)}, f32[2,4,64,256]{3,2,1,0:T(8,128)}, u32[]{:S(2)}, u32[]{:S(2)}) collective-permute-start(f32[2,4,64,256]{3,2,1,0:T(8,128)} %get-tuple-element.76), channel_id=1, source_target_pairs={{0,16},{1,17},{2,18},{3,19},{4,20},{5,21},{6,22},{7,23},{8,24},{9,... | collective-permute-start | bytes 1572872 | tf_op jit(solution)/shard_map/ppermute | solution.py:24
  112.8 14.5 %collective-permute-start.23 = (f32[2,4,64,256]{3,2,1,0:T(8,128)}, f32[2,4,64,256]{3,2,1,0:T(8,128)}, u32[]{:S(2)}, u32[]{:S(2)}) collective-permute-start(f32[2,4,64,256]{3,2,1,0:T(8,128)} %get-tuple-element.77), channel_id=1, source_target_pairs={{0,1},{1,0},{2,3},{3,2},{4,5},{5,4},{6,7},{7,6},{8,9},{9,8},{10,11... | collective-permute-start | bytes 1572872 | tf_op jit(solution)/shard_map/ppermute | solution.py:24
  114.0 0.8 copy-start.9
  114.8 14.9 %collective-permute-start.24 = (f32[2,4,64,256]{3,2,1,0:T(8,128)}, f32[2,4,64,256]{3,2,1,0:T(8,128)}, u32[]{:S(2)}, u32[]{:S(2)}) collective-permute-start(f32[2,4,64,256]{3,2,1,0:T(8,128)} %get-tuple-element.78), channel_id=1, source_target_pairs={{0,3},{1,2},{2,1},{3,0},{4,7},{5,6},{6,5},{7,4},{8,11},{9,10},{10,... | collective-permute-start | bytes 1572872 | tf_op jit(solution)/shard_map/ppermute | solution.py:24
  116.6 1.0 copy-start.10
  117.7 12.1 %copy-start.12 = (f32[1,2,4,64,256]{4,3,2,1,0:T(8,128)S(1)}, f32[1,2,4,64,256]{4,3,2,1,0:T(8,128)}, u32[]{:S(2)}) copy-start(f32[1,2,4,64,256]{4,3,2,1,0:T(8,128)} %copy-done.11) | copy-start | bytes 1572868
  119.6 14.9 %collective-permute-start.18 = (f32[4,64,256]{2,1,0:T(8,128)}, f32[4,64,256]{2,1,0:T(8,128)S(1)}, u32[]{:S(2)}, u32[]{:S(2)}) collective-permute-start(f32[4,64,256]{2,1,0:T(8,128)} %get-tuple-element.71), channel_id=1, source_target_pairs={{0,64},{1,65},{2,66},{3,67},{4,68},{5,69},{6,70},{7,71},{8,72},{9,... | collective-permute-start | bytes 786440 | tf_op jit(solution)/shard_map/ppermute | solution.py:24
  131.4 8.5 %collective-permute-start.25 = (f32[4,64,256]{2,1,0:T(8,128)S(1)}, f32[4,64,256]{2,1,0:T(8,128)S(1)}, u32[]{:S(2)}, u32[]{:S(2)}) collective-permute-start(f32[4,64,256]{2,1,0:T(8,128)S(1)} %get-tuple-element.80), channel_id=1, source_target_pairs={{0,64},{1,65},{2,66},{3,67},{4,68},{5,69},{6,70},{7,71},{8,72},{9,... | collective-permute-start | bytes 786440 | tf_op jit(solution)/shard_map/ppermute | solution.py:24
